TPU v7x, 32 devices: a whole 2x2x4 slice. The times are simulated.
32 devices in a mesh: groups: 2 (over x), seq: 8 (over z, y), head: 2 (over core).
Axes of the slice: x: 2, y: 2, z: 4, core: 2. Of those that a mesh axis runs over, the one named last changes fastest.
Arguments:
- patches: bfloat16 [2, 320, 4, 1024], P('groups', 'seq'), parts along dimension 0, may hold values from -6 to 6
- keep_list: int32 [2, 64], P('groups'), parts along dimension 0, may hold values from 0 to 319, as said below
- qkv_weight: bfloat16 [1024, 16, 192], P('seq', 'head')
- out_weight: bfloat16 [1024, 1024], P('head', 'seq'), may hold values from -0.1875 to 0.1875
- up_weight: bfloat16 [1024, 4096], P('seq', 'head'), may hold values from -0.1875 to 0.1875
- down_weight: bfloat16 [4096, 1024], P('head', 'seq'), may hold values from -0.09375 to 0.09375
Outputs:
- encoded: bfloat16 [2, 64, 8, 1024], P('groups', None, 'seq', 'head'), parts along dimension 0
There are 2 independent parts, one for each index of `groups`. A program takes and returns all parts, laid end to end along the dimension named above; an argument that names none is the same for every part. Nothing has to cross between parts.
Inputs may be any that keep to these rules, and one draw needn't show every extreme that they name: `keep_list`: each row lists 64 different superpatch indices of one image in increasing order; in every image the first and the last superpatch are listed, and all 40 superpatches of one aligned block (indices b * 40 to b * 40 + 39) are listed.
All inputs are finite; a program needn't handle non-finite values.
Results may differ from a plain program's by a relative error of at most 0.0055.
Values may be sent and summed in bfloat16 or wider, within the bound.
No kernel may reach another device: no remote copies, remote signals or barrier semaphores. Data moves between devices by JAX's collectives and lax.ppermute only.
A program may use at most 64 MiB of HBM per device.

v0:
```python
import math

import jax
import jax.numpy as jnp
from jax import lax
from jax.sharding import PartitionSpec as P


def layer_norm(matrix):
    average = jnp.mean(matrix, axis=-1, keepdims=True)
    power = jnp.mean(matrix * matrix, axis=-1, keepdims=True)
    return (matrix - average) * lax.rsqrt(power - average * average + 1e-06)


def attend(queries, keys, values):
    length = queries.shape[0]
    block = math.gcd(length, 512)
    scale = 1.0 / math.sqrt(queries.shape[1])

    def one_block(query_rows):
        scores = (
            lax.dot_general(
                query_rows, keys, (((1,), (1,)), ((), ())), preferred_element_type=jnp.float32
            )
            * scale
        )
        top = jnp.max(scores, axis=1, keepdims=True)
        powers = jnp.exp(scores - top)
        probs = (powers / jnp.sum(powers, axis=1, keepdims=True)).astype(jnp.bfloat16)
        return jnp.dot(probs, values, preferred_element_type=jnp.float32).astype(jnp.bfloat16)

    blocks = lax.map(one_block, queries.reshape(length // block, block, queries.shape[1]))
    return blocks.reshape(length, values.shape[1])


def local(patches, keep_list, qkv_weight, out_weight, up_weight, down_weight):
    seq_count = lax.axis_size("seq")
    seq_rank = lax.axis_index("seq")
    head_rank = lax.axis_index("head")
    images = patches.shape[0]
    sup_local = patches.shape[1]
    depth = patches.shape[3]
    half_width = depth // lax.axis_size("head")
    head_count = qkv_weight.shape[1]
    seq_length = sup_local * seq_count * 8 // 5
    per_owner = seq_length // seq_count
    capacity = (4 * sup_local + seq_count - 1) // seq_count
    slot_count = 4 * sup_local
    image_index = jnp.arange(images, dtype=jnp.int32)
    bounds = jnp.arange(seq_count + 1, dtype=jnp.int32) * sup_local
    before = jnp.sum((keep_list[:, :, None] < bounds[None, None, :]).astype(jnp.int32), axis=1)
    starts = bounds[None, :seq_count] + 3 * before[:, :seq_count]
    lengths = sup_local + 3 * (before[:, 1:] - before[:, :seq_count])
    my_start = lax.dynamic_index_in_dim(starts, seq_rank, 1, keepdims=False)
    my_length = lax.dynamic_index_in_dim(lengths, seq_rank, 1, keepdims=False)
    local_ids = seq_rank * sup_local + jnp.arange(sup_local, dtype=jnp.int32)
    kept_flag = jnp.any(keep_list[:, None, :] == local_ids[None, :, None], axis=2).astype(jnp.int32)
    offsets = jnp.arange(sup_local, dtype=jnp.int32)[None, :] + 3 * (
        jnp.cumsum(kept_flag, axis=1) - kept_flag
    )
    slot_ids = jnp.arange(slot_count, dtype=jnp.int32)
    owner_patch = (
        jnp.sum((offsets[:, None, :] <= slot_ids[None, :, None]).astype(jnp.int32), axis=2) - 1
    )
    start_of = jnp.take_along_axis(offsets, owner_patch, axis=1)
    sub_index = jnp.minimum(slot_ids[None, :] - start_of, 3)
    kept_of = jnp.take_along_axis(kept_flag, owner_patch, axis=1)
    flat_patches = patches.reshape(images, sup_local * 4, depth)
    fine_rows = flat_patches[
        image_index[:, None], owner_patch * 4 + jnp.where(kept_of == 1, sub_index, 0)
    ]
    mean_rows = jnp.mean(patches.astype(jnp.float32), axis=2).astype(jnp.bfloat16)
    shared_rows = mean_rows[image_index[:, None], owner_patch]
    local_tokens = jnp.where((kept_of == 1)[:, :, None], fine_rows, shared_rows)
    destinations = jnp.arange(seq_count, dtype=jnp.int32)[:, None, None]
    depth_slots = jnp.arange(capacity, dtype=jnp.int32)[None, None, :]
    positions = (destinations - my_start[None, :, None]) % seq_count + depth_slots * seq_count
    valid = positions < my_length[None, :, None]
    outgoing = local_tokens[image_index[None, :, None], jnp.minimum(positions, slot_count - 1)]
    outgoing = jnp.where(valid[:, :, :, None], outgoing, jnp.zeros((), jnp.bfloat16))
    incoming = lax.all_to_all(outgoing, "seq", split_axis=0, concat_axis=0, tiled=True)
    owned = jnp.arange(per_owner, dtype=jnp.int32) * seq_count + seq_rank
    source = jnp.sum((starts[:, None, :] <= owned[None, :, None]).astype(jnp.int32), axis=2) - 1
    first_of = jnp.take_along_axis(starts, source, axis=1)
    depth_of = (owned[None, :] - first_of) // seq_count
    resident = incoming[source, image_index[:, None], depth_of]
    start_rows = resident.reshape(images * per_owner, depth)
    start_float = start_rows.astype(jnp.float32)
    qkv_full, out_full, up_full, down_full = (
        lax.all_gather(qkv_weight, "seq", axis=0, tiled=True),
        lax.all_gather(out_weight, "seq", axis=1, tiled=True),
        lax.all_gather(up_weight, "seq", axis=0, tiled=True),
        lax.all_gather(down_weight, "seq", axis=1, tiled=True),
    )
    normed = layer_norm(start_float).astype(jnp.bfloat16).reshape(images, per_owner, depth)
    projected = jnp.einsum("ipd,dhc->ihpc", normed, qkv_full, preferred_element_type=jnp.float32)
    head_size = qkv_weight.shape[2] // 3
    sending = projected.astype(jnp.bfloat16).reshape(seq_count, per_owner, 3 * head_size)
    gathered = lax.all_to_all(sending, "seq", split_axis=0, concat_axis=0, tiled=True).reshape(
        seq_length, 3 * head_size
    )
    attended = attend(
        gathered[:, :head_size],
        gathered[:, head_size : 2 * head_size],
        gathered[:, 2 * head_size :],
    )
    returned = lax.all_to_all(
        attended.reshape(seq_count, per_owner, head_size),
        "seq",
        split_axis=0,
        concat_axis=0,
        tiled=True,
    )
    returned = returned.reshape(images, head_count, per_owner, head_size)
    partial_sum = jnp.einsum(
        "ihpc,hcd->ipd",
        returned,
        out_full.reshape(head_count, head_size, depth),
        preferred_element_type=jnp.float32,
    ).reshape(images * per_owner, depth)
    attn_total = lax.psum(partial_sum, "head")
    residual = start_float + attn_total
    residual_half = lax.dynamic_slice_in_dim(residual, head_rank * half_width, half_width, 1)
    normed_two = layer_norm(residual).astype(jnp.bfloat16)
    hidden = jax.nn.gelu(
        jnp.dot(normed_two, up_full, preferred_element_type=jnp.float32), approximate=False
    ).astype(jnp.bfloat16)
    mlp_terms = jnp.dot(hidden, down_full, preferred_element_type=jnp.float32)
    mlp_part = lax.psum_scatter(mlp_terms, "head", scatter_dimension=1, tiled=True)
    encoded = (residual_half + mlp_part).astype(jnp.bfloat16)
    return encoded.reshape(images, per_owner, 1, half_width)


def solution(mesh):
    return jax.shard_map(
        local,
        mesh=mesh,
        in_specs=(
            P("groups", "seq", None, None),
            P("groups", None),
            P("seq", "head", None),
            P("head", "seq"),
            P("seq", "head"),
            P("head", "seq"),
        ),
        out_specs=P("groups", None, "seq", "head"),
        check_vma=False,
    )
```

profile of v0, /device:TPU:0, one launch (start us, length us, event | category | flops | bytes accessed | tf_op | source)
XLA Modules:
  0.0 315.5 jit_solution(9587254554680193643)
XLA Ops:
  6.5 0.7 all-gather.5.cloned.1.call-update
  7.3 0.8 compare_reduce_fusion
  8.5 1.6 gather_fusion.5
  10.1 1.6 gather_fusion.4
  11.6 1.1 reshape.781
  12.7 1.0 fusion.61
  13.8 0.7 fusion.111
  14.4 0.6 and_select_fusion.2
  15.3 2.6 gather_fusion
  18.3 2.6 gather_fusion.1
  21.1 2.6 gather_fusion.2
  23.7 0.7 add_compare_fusion
  24.4 0.9 select_bitcast_fusion
  25.3 7.3 %all-to-all-start = ((bf16[8,1,20,1024]{3,2,1,0:T(8,128)(2,1)}), bf16[8,1,20,1024]{3,2,1,0:T(8,128)(2,1)S(1)}, u32[]{:S(2)}, u32[]{:S(2)}) async-start(bf16[8,1,20,1024]{3,2,1,0:T(8,128)(2,1)} %select_bitcast_fusion), calls=%async_computation | async-start | bytes 786432 | tf_op jit(solution)/shard_map/all_to_all | solution.py:81
  32.6 0.7 all-gather.7.cloned.1.call-update
  33.5 5.1 %compare_select_fusion.6 = (s32[1,64,1]{1,2,0:T(1,128)S(1)}, s32[1,64,1]{1,2,0:T(1,128)S(1)}) fusion(s32[64]{0:T(128)S(1)} %convert_reduce_fusion.3, s32[]{:T(128)} %bitcast.38, s32[]{:T(128)} %bitcast.37, s32[]{:T(128)} %bitcast.36, s32[]{:T(128)} %bitcast.35, s32[]{:T(128)} %bitcast.34, s32[]{:T(128)} %bitcast.33, s32[]{:T(128)} %bitcast.32, s32[]{:T(128)} %bitcast.31, ...), kind=kLoop, calls=%fused_computation.110 | loop fusion | flops 2880 | bytes 804 | tf_op jit(solution)/shard_map/select_n | solution.py:86
  38.6 9.5 %all-to-all-done = bf16[8,1,20,1024]{3,2,1,0:T(8,128)(2,1)S(1)} async-done(((bf16[8,1,20,1024]{3,2,1,0:T(8,128)(2,1)}), bf16[8,1,20,1024]{3,2,1,0:T(8,128)(2,1)S(1)}, u32[]{:S(2)}, u32[]{:S(2)}) %all-to-all-start) | async-done | bytes 327712 | tf_op jit(solution)/shard_map/all_to_all | solution.py:81
  48.3 1.1 gather_fusion.3
  49.5 31.6 %all-gather.5.cloned.1.call-done = bf16[1024,8,192]{0,2,1:T(8,128)(2,1)} async-done(((bf16[128,8,192]{0,2,1:T(8,128)(2,1)}), bf16[1024,8,192]{0,2,1:T(8,128)(2,1)}) %all-gather.5.cloned.1.call-update) | async-done | bytes 3145744 | tf_op jit(solution)/shard_map/all_gather | solution.py:90
  81.1 3.0 fusion
  84.2 13.2 %all_to_all.15 = bf16[8,64,192]{2,1,0:T(8,128)(2,1)S(1)} all-to-all(bf16[8,64,192]{2,1,0:T(8,128)(2,1)S(1)} %fusion), channel_id=1, replica_groups=mesh['groups'=2,'seq'=8,'head'=2] {'seq'}, dimensions={0} | all-to-all | bytes 393216 | tf_op jit(solution)/shard_map/all_to_all | solution.py:99
  98.5 10.3 %all_to_all.16 = bf16[8,2,2048]{2,1,0:T(2,128)(2,1)S(1)} all-to-all(bf16[8,2,2048]{2,1,0:T(2,128)(2,1)S(1)} %reshape.923), channel_id=1, replica_groups=mesh['groups'=2,'seq'=8,'head'=2] {'seq'}, dimensions={0} | all-to-all | bytes 131072 | tf_op jit(solution)/shard_map/all_to_all | solution.py:107
  108.9 13.5 %all-gather.7.cloned.1.call-done = bf16[512,1024]{1,0:T(8,128)(2,1)} async-done(((bf16[512,128]{1,0:T(8,128)(2,1)}), bf16[512,1024]{1,0:T(8,128)(2,1)}) %all-gather.7.cloned.1.call-update) | async-done | bytes 1048592 | tf_op jit(solution)/shard_map/all_gather | solution.py:91
  122.4 2.3 convolution_bitcast_fusion
  125.3 0.5 all-gather.9.cloned.1.call-update
  125.9 16.1 %all-reduce.5.cloned.1.call-done = f32[64,1024]{1,0:T(8,128)} async-done(((f32[64,1024]{1,0:T(8,128)}), f32[64,1024]{1,0:T(8,128)}) %all-reduce.5.cloned.1.call-update) | async-done | bytes 262160 | tf_op jit(solution)/shard_map/psum | solution.py:121
  142.0 1.1 fusion.110
  143.1 77.2 %all-gather.11.cloned.1.call-done = bf16[2048,1024]{1,0:T(8,128)(2,1)} async-done(((bf16[2048,128]{1,0:T(8,128)(2,1)}), bf16[2048,1024]{1,0:T(8,128)(2,1)}) %all-gather.11.cloned.1.call-update) | async-done | bytes 4194320 | tf_op jit(solution)/shard_map/all_gather | solution.py:93
  220.3 73.8 %all-gather.9.cloned.1.call-done = bf16[1024,2048]{1,0:T(8,128)(2,1)} async-done(((bf16[128,2048]{1,0:T(8,128)(2,1)}), bf16[1024,2048]{1,0:T(8,128)(2,1)}) %all-gather.9.cloned.1.call-update) | async-done | bytes 4194320 | tf_op jit(solution)/shard_map/all_gather | solution.py:92
  294.1 6.9 %fusion.12 = f32[64,1024]{1,0:T(8,128)} fusion(bf16[2048,1024]{1,0:T(8,128)(2,1)} %all-gather.11.cloned.1.call-done, bf16[1024,2048]{1,0:T(8,128)(2,1)} %all-gather.9.cloned.1.call-done, f32[64,1024]{1,0:T(8,128)S(1)} %get-tuple-element.25, f32[64]{0:T(128)S(1)} %get-tuple-element.29, f32[64]{0:T(128)S(1)} %get-tuple-element.28), kind=kOutput, calls=%fused_computation.40 | convolution fusion | flops 545587200 | bytes 8913408 | tf_op jit(solution)/shard_map/dot_general | solution.py:128
  301.0 6.1 %reduce-scatter.2.cloned.1.call-done = f32[64,512]{1,0:T(8,128)} async-done(((f32[64,1024]{1,0:T(8,128)}), f32[64,512]{1,0:T(8,128)}) %reduce-scatter.2.cloned.1.call-update) | async-done | bytes 131088 | tf_op jit(solution)/shard_map/reduce_scatter | solution.py:129
  307.1 1.6 fusion.60
  (52 shorter events, 3.8 us)
Async XLA Ops:
  6.5 11.3 %copy-start = (bf16[1,40,4,1024]{3,2,1,0:T(4,128)(2,1)S(1)}, bf16[1,40,4,1024]{3,2,1,0:T(4,128)(2,1)}, u32[]{:S(2)}) copy-start(bf16[1,40,4,1024]{3,2,1,0:T(4,128)(2,1)} %param.8) | copy-start | bytes 983044
  6.5 74.6 %all-gather.5.cloned.1.call-start = ((), (), s32[]{:S(2)}) async-start(), calls=%async_computation.4 | async-start | bytes 3538944 | tf_op jit(solution)/shard_map/all_gather | solution.py:90
  25.3 22.8 %all-to-all-start = ((bf16[8,1,20,1024]{3,2,1,0:T(8,128)(2,1)}), bf16[8,1,20,1024]{3,2,1,0:T(8,128)(2,1)S(1)}, u32[]{:S(2)}, u32[]{:S(2)}) async-start(bf16[8,1,20,1024]{3,2,1,0:T(8,128)(2,1)} %select_bitcast_fusion), calls=%async_computation | async-start | bytes 786432 | tf_op jit(solution)/shard_map/all_to_all | solution.py:81
  32.6 89.8 %all-gather.7.cloned.1.call-start = ((), (), s32[]{:S(2)}) async-start(), calls=%async_computation.5 | async-start | bytes 1179648 | tf_op jit(solution)/shard_map/all_gather | solution.py:91
  33.3 108.7 %all-reduce.5.cloned.1.call-start = ((), (), s32[]{:S(2)}) async-start(), calls=%async_computation.6 | async-start | bytes 524288 | tf_op jit(solution)/shard_map/psum | solution.py:121
  124.7 95.6 %all-gather.11.cloned.1.call-start = ((), (), s32[]{:S(2)}) async-start(), calls=%async_computation.8 | async-start | bytes 4718592 | tf_op jit(solution)/shard_map/all_gather | solution.py:93
  125.3 168.9 %all-gather.9.cloned.1.call-start = ((), (), s32[]{:S(2)}) async-start(), calls=%async_computation.7 | async-start | bytes 4718592 | tf_op jit(solution)/shard_map/all_gather | solution.py:92
  125.9 181.2 %reduce-scatter.2.cloned.1.call-start = ((), (), s32[]{:S(2)}) async-start(), calls=%async_computation.9 | async-start | bytes 393216 | tf_op jit(solution)/shard_map/reduce_scatter | solution.py:129
Sparse Core Ops, SparseCore 0:
  9.4 71.6 all-gather.4
  83.1 39.2 all-gather.6
  124.8 17.1 all-reduce.4
  144.1 76.1 all-gather.10
  222.5 71.5 all-gather.8
  301.1 5.9 reduce-scatter.1
where the time goes:
time: 316 us
  waiting for transfers between devices  230 us (73%)
  blocking collectives  23.5 us (7%)
  local copies, waits for them, and re-layouts  14.5 us (5%)
  between operations  13.7 us (4%)
  other arithmetic  13.3 us (4%)
  matrix products  12.8 us (4%)
  starting transfers between devices  7.48 us (2%)
    all_gather x1, waiting for transfers between devices, local(): lax.all_gather(down_weight, 'seq', axis=1, tiled=True)  77.2 us
    all_gather x1, waiting for transfers between devices, local(): lax.all_gather(up_weight, 'seq', axis=0, tiled=True)  73.8 us
    all_gather x1, waiting for transfers between devices, local(): lax.all_gather(qkv_weight, 'seq', axis=0, tiled=True)  31.6 us
    psum x1, waiting for transfers between devices, local(): attn_total = lax.psum(partial_sum, 'head')  16.1 us
    all_gather x1, waiting for transfers between devices, local(): lax.all_gather(out_weight, 'seq', axis=1, tiled=True)  13.5 us
    all_to_all x1, blocking collectives, local(): lax.all_to_all(sending, 'seq', split_axis=0, concat_axis=0, tiled=True)  13.2 us
    all_to_all x1, blocking collectives, local(): lax.all_to_all(attended.reshape(seq_count, per_owner, head_size), 'seq',...  10.3 us
    all_to_all x1, waiting for transfers between devices, local(): lax.all_to_all(outgoing, 'seq', split_axis=0, concat_axis=0, tiled=True)  9.51 us
  transfers between devices with their start and end apart: 7, of which 7 were waited for; matrix products, arithmetic and copies ran while one was open for 9% of the time, Pallas kernels for 0%

commit v1 on v0

--- a/solution.py
+++ b/solution.py
@@ -1,10 +1,18 @@
+import functools
 import math
 
 import jax
 import jax.numpy as jnp
 from jax import lax
+from jax.experimental import pallas as pl
+from jax.experimental.pallas import tpu as pltpu
 from jax.sharding import PartitionSpec as P
 
+F32 = jnp.float32
+BF16 = jnp.bfloat16
+VMEM = pltpu.VMEM
+SLOT = 32
+LIMIT = 48 * 1024 * 1024
 
 def layer_norm(matrix):
     average = jnp.mean(matrix, axis=-1, keepdims=True)
@@ -33,7 +41,7 @@
     return blocks.reshape(length, values.shape[1])
 
 
-def local(patches, keep_list, qkv_weight, out_weight, up_weight, down_weight):
+def local_general(patches, keep_list, qkv_weight, out_weight, up_weight, down_weight):
     seq_count = lax.axis_size("seq")
     seq_rank = lax.axis_index("seq")
     head_rank = lax.axis_index("head")
@@ -131,6 +139,364 @@
     return encoded.reshape(images, per_owner, 1, half_width)
 
 
+def vspec():
+    return pl.BlockSpec(memory_space=VMEM)
+
+
+def aspec():
+    return pl.BlockSpec(memory_space=pl.ANY)
+
+
+def sspec():
+    return pl.BlockSpec(memory_space=pltpu.SMEM)
+
+
+def params():
+    return pltpu.CompilerParams(vmem_limit_bytes=LIMIT)
+
+
+def struct(shape, dtype=BF16):
+    return jax.ShapeDtypeStruct(shape, dtype)
+
+
+def pack_kernel(n, rank_ref, qkv_ref, up_ref, down_ref, *refs):
+    qkv_outs, mlp_outs, sem = refs[:n], refs[n : 2 * n], refs[2 * n]
+    rank = rank_ref[0]
+    rows = up_ref.shape[0]
+    wide = up_ref.shape[1] // n
+    copies = []
+    for j in range(n):
+        dest = rank ^ j
+        copies.append((qkv_ref.at[dest], qkv_outs[j]))
+        for c in range(wide // 128):
+            copies.append(
+                (
+                    up_ref.at[:, pl.ds(pl.multiple_of(dest * wide + c * 128, 128), 128)],
+                    mlp_outs[j].at[pl.ds(c * rows, rows)],
+                )
+            )
+        copies.append(
+            (
+                down_ref.at[pl.ds(pl.multiple_of(dest * wide, 128), wide)],
+                mlp_outs[j].at[pl.ds(rows * wide // 128, wide)],
+            )
+        )
+    started = []
+    for i, (src, dst) in enumerate(copies):
+        copy = pltpu.make_async_copy(src, dst, sem.at[i])
+        copy.start()
+        started.append(copy)
+    for copy in started:
+        copy.wait()
+
+
+def pack(rank, qkv_t, up, down, n):
+    wide = up.shape[1] // n
+    rows = up.shape[0] * wide // 128 + wide
+    copies = n * (2 + wide // 128)
+    outs = pl.pallas_call(
+        functools.partial(pack_kernel, n),
+        in_specs=[sspec(), aspec(), aspec(), aspec()],
+        out_specs=[aspec()] * (2 * n),
+        out_shape=[struct(qkv_t.shape[1:])] * n + [struct((rows, 128))] * n,
+        scratch_shapes=[pltpu.SemaphoreType.DMA((copies,))],
+        compiler_params=params(),
+    )(rank, qkv_t, up, down)
+    return list(outs[:n]), list(outs[n:])
+
+
+def prep_kernel(n, sup, rank_ref, keep_ref, patches_ref, *outs):
+    rank = rank_ref[0]
+    first = rank * sup
+    keep = keep_ref[...]
+    rows = 4 * sup
+    count = keep.shape[0]
+    lane = lax.broadcasted_iota(jnp.int32, (count, rows), 1)
+    ids = first + (lane >> 2)
+    kept = jnp.sum((keep == ids).astype(jnp.int32), axis=0, keepdims=True)
+    below = jnp.sum(
+        jnp.logical_and(keep >= first, keep < ids).astype(jnp.int32), axis=0, keepdims=True
+    )
+    lane_row = lax.broadcasted_iota(jnp.int32, (1, rows), 1)
+    fine_pos = jnp.where(kept == 1, (lane_row >> 2) + 3 * below + (lane_row & 3), -1)
+    lane_s = lax.broadcasted_iota(jnp.int32, (count, sup), 1)
+    ids_s = first + lane_s
+    kept_s = jnp.sum((keep == ids_s).astype(jnp.int32), axis=0, keepdims=True)
+    below_s = jnp.sum(
+        jnp.logical_and(keep >= first, keep < ids_s).astype(jnp.int32), axis=0, keepdims=True
+    )
+    lane_row_s = lax.broadcasted_iota(jnp.int32, (1, sup), 1)
+    mean_pos = jnp.where(kept_s == 1, -1, lane_row_s + 3 * below_s)
+    start = first + 3 * jnp.sum((keep < first).astype(jnp.int32), axis=0, keepdims=True)
+    flat = patches_ref[...]
+    sup_col = lax.broadcasted_iota(jnp.int32, (sup, rows), 0)
+    sup_lane = lax.broadcasted_iota(jnp.int32, (sup, rows), 1) >> 2
+    averaging = jnp.where(sup_col == sup_lane, 0.25, 0.0).astype(BF16)
+    means = jnp.dot(averaging, flat, preferred_element_type=F32).astype(BF16)
+    slot = lax.broadcasted_iota(jnp.int32, (SLOT, 1), 0)
+    for j in range(n):
+        pos = ((rank ^ j) - start) % n + slot * n
+        fine = (pos == fine_pos).astype(F32).astype(BF16)
+        mean = (pos == mean_pos).astype(F32).astype(BF16)
+        outs[j][...] = (
+            jnp.dot(fine, flat, preferred_element_type=F32)
+            + jnp.dot(mean, means, preferred_element_type=F32)
+        ).astype(BF16)
+
+
+def prep(rank, keep_col, flat, half, n, sup):
+    width = flat.shape[1] // 2
+    return pl.pallas_call(
+        functools.partial(prep_kernel_half, n, sup),
+        grid_spec=pltpu.PrefetchScalarGridSpec(
+            num_scalar_prefetch=1,
+            grid=(1,),
+            in_specs=[
+                pl.BlockSpec(keep_col.shape, lambda i, ref: (0, 0)),
+                pl.BlockSpec((flat.shape[0], width), lambda i, ref: (0, ref[1])),
+            ],
+            out_specs=[pl.BlockSpec((SLOT, width), lambda i, ref: (0, 0))] * n,
+        ),
+        out_shape=[struct((SLOT, width))] * n,
+        compiler_params=params(),
+    )(jnp.stack([rank, half]).astype(jnp.int32), keep_col, flat)
+
+
+def prep_kernel_half(n, sup, scalars, keep_ref, patches_ref, *outs):
+    prep_kernel(n, sup, scalars, keep_ref, patches_ref, *outs)
+
+
+def pick_kernel(n, sup, per_owner, rank_ref, keep_ref, *refs):
+    ins, out = refs[:n], refs[n]
+    rank = rank_ref[0]
+    keep = keep_ref[...]
+    count = keep.shape[0]
+    lanes = n * SLOT
+    shift = SLOT.bit_length() - 1
+    source = (lax.broadcasted_iota(jnp.int32, (count, lanes), 1) >> shift) ^ rank
+    low = jnp.sum((keep < source * sup).astype(jnp.int32), axis=0, keepdims=True)
+    high = jnp.sum((keep < source * sup + sup).astype(jnp.int32), axis=0, keepdims=True)
+    lane = lax.broadcasted_iota(jnp.int32, (1, lanes), 1)
+    source_row = (lane >> shift) ^ rank
+    start = source_row * sup + 3 * low
+    stop = source_row * sup + sup + 3 * high
+    token = start + ((rank - start) & (n - 1)) + (lane & (SLOT - 1)) * n
+    row = jnp.where(token < stop, token >> (n.bit_length() - 1), -1)
+    own = lax.broadcasted_iota(jnp.int32, (per_owner, lanes), 0)
+    choose = (own == row).astype(F32).astype(BF16)
+    stacked = jnp.concatenate([ref[...] for ref in ins], axis=0)
+    out[...] = jnp.dot(choose, stacked, preferred_element_type=F32).astype(BF16)
+
+
+def pick(rank, keep_col, pieces, n, sup, per_owner):
+    return pl.pallas_call(
+        functools.partial(pick_kernel, n, sup, per_owner),
+        in_specs=[sspec()] + [vspec()] * (n + 1),
+        out_specs=vspec(),
+        out_shape=struct((per_owner, pieces[0].shape[1])),
+        compiler_params=params(),
+    )(rank, keep_col, *pieces)
+
+
+def norm_rows(x):
+    average = jnp.mean(x, axis=-1, keepdims=True)
+    power = jnp.mean(x * x, axis=-1, keepdims=True)
+    return (x - average) * lax.rsqrt(power - average * average + 1e-06)
+
+
+def attend_kernel(n, rank_ref, mine_ref, other_ref, *refs):
+    weights = refs[:n]
+    tokens_ref, out_ref, weight_ref = refs[n], refs[n + 1], refs[n + 2]
+    rank, half = rank_ref[0], rank_ref[1]
+    rows = mine_ref.shape[1]
+    width = mine_ref.shape[2]
+    depth = weights[0].shape[1]
+    for j in range(n):
+        source = rank ^ j
+        at = pl.ds(pl.multiple_of(source * rows, rows), rows)
+        tokens_ref[at, pl.ds(pl.multiple_of(half * width, width), width)] = mine_ref[j]
+        tokens_ref[at, pl.ds(pl.multiple_of((1 - half) * width, width), width)] = other_ref[j]
+        weight_ref[:, pl.ds(pl.multiple_of(source * depth, depth), depth)] = weights[j][...]
+    normed = norm_rows(tokens_ref[...].astype(F32)).astype(BF16)
+    projected = lax.dot_general(
+        normed, weight_ref[...], (((1,), (1,)), ((), ())), preferred_element_type=F32
+    ).astype(BF16)
+    size = projected.shape[1] // 3
+    queries = projected[:, :size]
+    keys = projected[:, size : 2 * size]
+    values = projected[:, 2 * size :]
+    scores = lax.dot_general(
+        queries, keys, (((1,), (1,)), ((), ())), preferred_element_type=F32
+    ) * (1.0 / math.sqrt(size))
+    powers = jnp.exp(scores - jnp.max(scores, axis=1, keepdims=True))
+    probs = (powers / jnp.sum(powers, axis=1, keepdims=True)).astype(BF16)
+    out_ref[...] = lax.dot_general(
+        values, probs, (((0,), (1,)), ((), ())), preferred_element_type=F32
+    ).astype(BF16)
+
+
+def attend_fast(scalars, mine, other, weights, n):
+    rows = mine.shape[0] * mine.shape[1]
+    size = weights[0].shape[0] // 3
+    return pl.pallas_call(
+        functools.partial(attend_kernel, n),
+        in_specs=[sspec()] + [vspec()] * (n + 2),
+        out_specs=[vspec()] * 2,
+        out_shape=[struct((rows, 2 * mine.shape[2])), struct((size, rows))],
+        scratch_shapes=[VMEM((weights[0].shape[0], n * weights[0].shape[1]), BF16)],
+        compiler_params=params(),
+    )(scalars, mine, other, *weights)
+
+
+def mlp_kernel(n, rank_ref, tokens_ref, mine_ref, other_ref, out_mine_ref, out_other_ref, *refs):
+    weights = refs[:n]
+    residual_ref, keep_ref, send_ref, up_ref, down_ref, row_ref, joined_ref = refs[n:]
+    rank, half = rank_ref[0], rank_ref[1]
+    wide, depth = down_ref.shape
+    block = up_ref.shape[0] // n
+    for j in range(n):
+        source = rank ^ j
+        for c in range(wide // 128):
+            up_ref[pl.ds(pl.multiple_of(source * block, block), block), c * 128 : (c + 1) * 128] = (
+                weights[j][c * block : (c + 1) * block]
+            )
+        down_ref[:, pl.ds(pl.multiple_of(source * 128, 128), 128)] = weights[j][
+            block * wide // 128 :
+        ]
+    size = mine_ref.shape[1]
+    for j in range(n):
+        at = pl.ds(pl.multiple_of((rank ^ j) * size, size), size)
+        joined_ref[0, at] = mine_ref[j]
+        joined_ref[1, at] = other_ref[j]
+    dims = (((0,), (0,)), ((), ()))
+    row_ref[...] = (
+        tokens_ref[...].astype(F32)
+        + lax.dot_general(joined_ref[0], out_mine_ref[...], dims, preferred_element_type=F32)
+        + lax.dot_general(joined_ref[1], out_other_ref[...], dims, preferred_element_type=F32)
+    )
+    part = residual_ref.shape[0]
+    width = residual_ref.shape[1]
+    my_cols = pl.ds(pl.multiple_of(half * width, width), width)
+    other_cols = pl.ds(pl.multiple_of((1 - half) * width, width), width)
+    residual_ref[...] = row_ref[pl.ds(pl.multiple_of(rank * part, part), part), my_cols]
+    normed = norm_rows(row_ref[...]).astype(BF16)
+    raw = jnp.dot(normed, up_ref[...], preferred_element_type=F32)
+    hidden = (0.5 * raw * (1.0 + lax.erf(raw * math.sqrt(0.5)))).astype(BF16)
+    keep_ref[...] = jnp.dot(hidden, down_ref[:, my_cols], preferred_element_type=F32)
+    send_ref[...] = jnp.dot(hidden, down_ref[:, other_cols], preferred_element_type=F32).astype(BF16)
+
+
+def mlp(scalars, tokens, mine, other, out_mine, out_other, weights, n, wide):
+    length, depth = tokens.shape
+    width = depth // 2
+    return pl.pallas_call(
+        functools.partial(mlp_kernel, n),
+        in_specs=[sspec()] + [vspec()] * (n + 5),
+        out_specs=[vspec()] * 3,
+        out_shape=[
+            struct((length // n, width), F32),
+            struct((length, width), F32),
+            struct((length, width)),
+        ],
+        scratch_shapes=[
+            VMEM((depth, wide), BF16),
+            VMEM((wide, depth), BF16),
+            VMEM((length, depth), F32),
+            VMEM((2, mine.shape[0] * mine.shape[1], length), BF16),
+        ],
+        compiler_params=params(),
+    )(scalars, tokens, mine, other, out_mine, out_other, *weights)
+
+
+def join_kernel(n, rank_ref, keep_ref, got_ref, residual_ref, base_ref, *outs):
+    rank = rank_ref[0]
+    part = residual_ref.shape[0]
+    for j in range(n):
+        at = pl.ds(pl.multiple_of((rank ^ j) * part, part), part)
+        total = keep_ref[at] + got_ref[at].astype(F32)
+        if j == 0:
+            base_ref[...] = total + residual_ref[...]
+        else:
+            outs[j - 1][...] = total.astype(BF16)
+
+
+def join(scalars, keep, got, residual, n):
+    part, width = residual.shape
+    outs = pl.pallas_call(
+        functools.partial(join_kernel, n),
+        in_specs=[sspec()] + [vspec()] * 3,
+        out_specs=[vspec()] * n,
+        out_shape=[struct((part, width), F32)] + [struct((part, width))] * (n - 1),
+        compiler_params=params(),
+    )(scalars, keep, got, residual)
+    return outs[0], list(outs[1:])
+
+
+def last_kernel(base_ref, *refs):
+    total = base_ref[...]
+    for ref in refs[:-1]:
+        total = total + ref[...].astype(F32)
+    refs[-1][...] = total.astype(BF16)
+
+
+def last(base, terms):
+    return pl.pallas_call(
+        last_kernel,
+        in_specs=[vspec()] * (1 + len(terms)),
+        out_specs=vspec(),
+        out_shape=struct(base.shape),
+        compiler_params=params(),
+    )(base, *terms)
+
+
+def swap(value, axis, j):
+    n = lax.axis_size(axis)
+    return lax.ppermute(value, axis, [(i, i ^ j) for i in range(n)])
+
+
+def local_fast(patches, keep_list, qkv_weight, out_weight, up_weight, down_weight):
+    n = lax.axis_size("seq")
+    rank = lax.axis_index("seq").astype(jnp.int32)
+    half = lax.axis_index("head").astype(jnp.int32)
+    sup, depth = patches.shape[1], patches.shape[3]
+    length = sup * n * 8 // 5
+    per_owner = length // n
+    wide = up_weight.shape[1] // n
+    scalars = jnp.stack([rank, half])
+    keep_col = keep_list.reshape(-1, 1)
+    flat = patches.reshape(4 * sup, depth)
+    out_mine = lax.all_gather(out_weight, "seq", axis=1, tiled=True)
+    out_other = swap(out_mine, "head", 1)
+    slots = prep(rank, keep_col, flat, half, n, sup)
+    qkv_blocks, mlp_blocks = pack(scalars, qkv_weight.transpose(1, 2, 0), up_weight, down_weight, n)
+    dealt = [slots[0]] + [swap(slots[j], "seq", j) for j in range(1, n)]
+    qkv_got = [qkv_blocks[0]] + [swap(qkv_blocks[j], "seq", j) for j in range(1, n)]
+    owned = pick(scalars, keep_col, dealt, n, sup, per_owner)
+    pieces = jnp.stack([owned] + [swap(owned, "seq", j) for j in range(1, n)])
+    pieces_other = swap(pieces, "head", 1)
+    mlp_got = [mlp_blocks[0]] + [swap(mlp_blocks[j], "seq", j) for j in range(1, n)]
+    tokens, attended = attend_fast(scalars, pieces, pieces_other, qkv_got, n)
+    pair = jnp.stack([attended, swap(attended, "seq", n // 2)])
+    quads = [pair] + [swap(pair, "seq", j) for j in range(1, n // 2)]
+    gathered = jnp.stack([quad[k] for k in range(2) for quad in quads])
+    gathered_other = swap(gathered, "head", 1)
+    residual, keep, send = mlp(
+        scalars, tokens, gathered, gathered_other, out_mine, out_other, mlp_got, n, wide
+    )
+    got = swap(send, "head", 1)
+    base, terms = join(scalars, keep, got, residual, n)
+    terms = [swap(terms[j - 1], "seq", j) for j in range(1, n)]
+    encoded = last(base, terms)
+    return encoded.reshape(1, per_owner, 1, depth // 2)
+
+
+def local(patches, keep_list, qkv_weight, out_weight, up_weight, down_weight):
+    n = lax.axis_size("seq")
+    one_image = patches.shape[0] == 1 and qkv_weight.shape[1] == n and n & (n - 1) == 0
+    plan = local_fast if one_image else local_general
+    return plan(patches, keep_list, qkv_weight, out_weight, up_weight, down_weight)
+
+
 def solution(mesh):
     return jax.shard_map(
         local,

time: 316 us -> 162 us (0.51)
  waiting for transfers between devices: 230 us -> 71.9 us
  starting transfers between devices: 7.48 us -> 59.8 us
  blocking collectives: 23.5 us -> 0 us
  other arithmetic: 13.3 us -> 0.09 us
  matrix products: 12.8 us -> 0 us
  Pallas kernels: 0 us -> 12.2 us
  local copies, waits for them, and re-layouts: 14.5 us -> 4.11 us
    all_gather x4 -> x1, waiting for transfers between devices: 196 us -> 5.84 us  [local_fast(): out_mine = lax.all_gather(out_weight, 'seq', axis=1, tiled=True)]
    ppermute x0 -> x43, waiting for transfers between devices: none -> 66 us  [swap(): return lax.ppermute(value, axis, [(i, i ^ j) for i in range(n)])]
    ppermute x0 -> x43, starting transfers between devices: none -> 59.8 us  [swap(): return lax.ppermute(value, axis, [(i, i ^ j) for i in range(n)])]
    all_to_all x2 -> x0, blocking collectives: 23.5 us -> none  [the longest x1 13.2 us: local(): lax.all_to_all(sending, 'seq', split_axis=0, concat_axis=0, tiled=True)]
    psum x1 -> x0, waiting for transfers between devices: 16.1 us -> none  [local(): attn_total = lax.psum(partial_sum, 'head')]
    dot_general x5 -> x0, matrix products: 12.8 us -> none  [the longest x1 6.86 us: local(): mlp_terms = jnp.dot(hidden, down_full, preferred_element_type=jnp.float32)]
    gather x8 -> x0, local copies, waits for them, and re-layouts: 12.7 us -> none  [the longest x2 2.66 us: local(): local_tokens[image_index[None, :, None], jnp.minimum(positions, slot_coun...]
    pallas_call x0 -> x7, Pallas kernels: none -> 12.2 us  [the longest x1 3.97 us: mlp(): pl.pallas_call(functools.partial(mlp_kernel, n), in_specs=[sspec()] + [vs...]
  transfers between devices with their start and end apart: 7 -> 44, of which waited for: 7 -> 22; matrix products, arithmetic and copies ran while one was open for 9% -> 0% of each run, Pallas kernels for 0% -> 3%
where the time goes in v1:
time: 162 us
  waiting for transfers between devices  71.9 us (44%)
  starting transfers between devices  59.8 us (37%)
  between operations  13.6 us (8%)
  Pallas kernels  12.2 us (8%)
  local copies, waits for them, and re-layouts  4.11 us (3%)
    ppermute x43, waiting for transfers between devices, swap(): return lax.ppermute(value, axis, [(i, i ^ j) for i in range(n)])  66 us
    ppermute x43, starting transfers between devices, swap(): return lax.ppermute(value, axis, [(i, i ^ j) for i in range(n)])  59.8 us
    all_gather x1, waiting for transfers between devices, local_fast(): out_mine = lax.all_gather(out_weight, 'seq', axis=1, tiled=True)  5.84 us
    pallas_call x1, Pallas kernels, mlp(): pl.pallas_call(functools.partial(mlp_kernel, n), in_specs=[sspec()] + [vs...  3.97 us
  transfers between devices with their start and end apart: 44, of which 22 were waited for; matrix products, arithmetic and copies ran while one was open for 0% of the time, Pallas kernels for 3%

profile of v1, /device:TPU:0, one launch (start us, length us, event | category | flops | bytes accessed | tf_op | source)
XLA Modules:
  0.0 161.7 jit_solution(9484447995406451526)
XLA Ops:
  9.5 3.0 %collective-permute-start = (bf16[32,512]{1,0:T(8,128)(2,1)S(1)}, bf16[32,512]{1,0:T(8,128)(2,1)S(1)}, u32[]{:S(2)}, u32[]{:S(2)}) collective-permute-start(bf16[32,512]{1,0:T(8,128)(2,1)S(1)} %get-tuple-element.43), channel_id=1, source_target_pairs={{0,2},{2,0},{4,6},{6,4},{8,10},{10,8},{12,14},{14,12},{1,3},{3,1},... | collective-permute-start | bytes 98312 | tf_op jit(solution)/shard_map/ppermute | solution.py:454
  14.2 3.0 %collective-permute-start.3 = (bf16[32,512]{1,0:T(8,128)(2,1)S(1)}, bf16[32,512]{1,0:T(8,128)(2,1)S(1)}, u32[]{:S(2)}, u32[]{:S(2)}) collective-permute-start(bf16[32,512]{1,0:T(8,128)(2,1)S(1)} %get-tuple-element.46), channel_id=1, source_target_pairs={{0,8},{2,10},{4,12},{6,14},{8,0},{10,2},{12,4},{14,6},{1,9},{3,11}... | collective-permute-start | bytes 98312 | tf_op jit(solution)/shard_map/ppermute | solution.py:454
  18.4 3.6 %collective-permute-start.5 = (bf16[32,512]{1,0:T(8,128)(2,1)S(1)}, bf16[32,512]{1,0:T(8,128)(2,1)S(1)}, u32[]{:S(2)}, u32[]{:S(2)}) collective-permute-start(bf16[32,512]{1,0:T(8,128)(2,1)S(1)} %get-tuple-element.48), channel_id=1, source_target_pairs={{0,12},{2,14},{4,8},{6,10},{8,4},{10,6},{12,0},{14,2},{1,13},{3,15... | collective-permute-start | bytes 98312 | tf_op jit(solution)/shard_map/ppermute | solution.py:454
  24.3 4.5 %collective-permute-done.6.refs_7_ = bf16[32,512]{1,0:T(8,128)(2,1)S(1)} collective-permute-done((bf16[32,512]{1,0:T(8,128)(2,1)S(1)}, bf16[32,512]{1,0:T(8,128)(2,1)S(1)}, u32[]{:S(2)}, u32[]{:S(2)}) %collective-permute-start.6) | collective-permute-done | bytes 32800 | tf_op jit(solution)/shard_map/ppermute | solution.py:454
  29.8 3.4 %collective-permute-start.12 = (bf16[64,512]{1,0:T(8,128)(2,1)S(1)}, bf16[64,512]{1,0:T(8,128)(2,1)S(1)}, u32[]{:S(2)}, u32[]{:S(2)}) collective-permute-start(bf16[64,512]{1,0:T(8,128)(2,1)S(1)} %shard_map.65), channel_id=1, source_target_pairs={{0,12},{2,14},{4,8},{6,10},{8,4},{10,6},{12,0},{14,2},{1,13},{3,15... | collective-permute-start | bytes 196616 | tf_op jit(solution)/shard_map/ppermute | solution.py:454
  33.3 4.0 %collective-permute-start.10 = (bf16[64,512]{1,0:T(8,128)(2,1)S(1)}, bf16[64,512]{1,0:T(8,128)(2,1)S(1)}, u32[]{:S(2)}, u32[]{:S(2)}) collective-permute-start(bf16[64,512]{1,0:T(8,128)(2,1)S(1)} %shard_map.65), channel_id=1, source_target_pairs={{0,8},{2,10},{4,12},{6,14},{8,0},{10,2},{12,4},{14,6},{1,9},{3,11}... | collective-permute-start | bytes 196616 | tf_op jit(solution)/shard_map/ppermute | solution.py:454
  37.7 3.8 %collective-permute-done.7 = bf16[64,512]{1,0:T(8,128)(2,1)S(1)} collective-permute-done((bf16[64,512]{1,0:T(8,128)(2,1)S(1)}, bf16[64,512]{1,0:T(8,128)(2,1)S(1)}, u32[]{:S(2)}, u32[]{:S(2)}) %collective-permute-start.7) | collective-permute-done | bytes 65568 | tf_op jit(solution)/shard_map/ppermute | solution.py:454
  41.5 4.3 %collective-permute-done.8 = bf16[64,512]{1,0:T(8,128)(2,1)S(1)} collective-permute-done((bf16[64,512]{1,0:T(8,128)(2,1)S(1)}, bf16[64,512]{1,0:T(8,128)(2,1)S(1)}, u32[]{:S(2)}, u32[]{:S(2)}) %collective-permute-start.8) | collective-permute-done | bytes 65568 | tf_op jit(solution)/shard_map/ppermute | solution.py:454
  45.9 5.0 %collective-permute-done.9 = bf16[64,512]{1,0:T(8,128)(2,1)S(1)} collective-permute-done((bf16[64,512]{1,0:T(8,128)(2,1)S(1)}, bf16[64,512]{1,0:T(8,128)(2,1)S(1)}, u32[]{:S(2)}, u32[]{:S(2)}) %collective-permute-start.9) | collective-permute-done | bytes 65568 | tf_op jit(solution)/shard_map/ppermute | solution.py:454
  51.2 2.4 %shard_map.66 = (bf16[192,128]{1,0:T(8,128)(2,1)S(1)}, bf16[192,128]{1,0:T(8,128)(2,1)S(1)}, bf16[192,128]{1,0:T(8,128)(2,1)S(1)}, bf16[192,128]{1,0:T(8,128)(2,...) custom-call(s32[2]{0:T(128)S(1)} %pad_add_fusion.scalars.rank_ref, ...), custom_call_target="tpu_custom_call" | custom-call | tf_op jit(solution)/shard_map/pallas_call | solution.py:197
  54.7 2.4 %collective-permute-start.17 = (bf16[192,128]{1,0:T(8,128)(2,1)S(1)}, bf16[192,128]{1,0:T(8,128)(2,1)S(1)}, u32[]{:S(2)}, u32[]{:S(2)}) collective-permute-start(bf16[192,128]{1,0:T(8,128)(2,1)S(1)} %get-tuple-element.53), channel_id=1, source_target_pairs={{0,6},{2,4},{4,2},{6,0},{8,14},{10,12},{12,10},{14,8},{1,7},{3,5},... | collective-permute-start | bytes 147464 | tf_op jit(solution)/shard_map/ppermute | solution.py:454
  57.8 2.8 %collective-permute-start.19 = (bf16[192,128]{1,0:T(8,128)(2,1)S(1)}, bf16[192,128]{1,0:T(8,128)(2,1)S(1)}, u32[]{:S(2)}, u32[]{:S(2)}) collective-permute-start(bf16[192,128]{1,0:T(8,128)(2,1)S(1)} %get-tuple-element.55), channel_id=1, source_target_pairs={{0,10},{2,8},{4,14},{6,12},{8,2},{10,0},{12,6},{14,4},{1,11},{3,9}... | collective-permute-start | bytes 147464 | tf_op jit(solution)/shard_map/ppermute | solution.py:454
  61.2 3.6 %collective-permute-start.21 = (bf16[192,128]{1,0:T(8,128)(2,1)S(1)}, bf16[192,128]{1,0:T(8,128)(2,1)S(1)}, u32[]{:S(2)}, u32[]{:S(2)}) collective-permute-start(bf16[192,128]{1,0:T(8,128)(2,1)S(1)} %get-tuple-element.57), channel_id=1, source_target_pairs={{0,14},{2,12},{4,10},{6,8},{8,6},{10,4},{12,2},{14,0},{1,15},{3,13... | collective-permute-start | bytes 147464 | tf_op jit(solution)/shard_map/ppermute | solution.py:454
  64.8 2.9 %collective-permute-done.18.refs_4_ = bf16[192,128]{1,0:T(8,128)(2,1)S(1)} collective-permute-done((bf16[192,128]{1,0:T(8,128)(2,1)S(1)}, bf16[192,128]{1,0:T(8,128)(2,1)S(1)}, u32[]{:S(2)}, u32[]{:S(2)}) %collective-permute-start.18) | collective-permute-done | bytes 49184 | tf_op jit(solution)/shard_map/ppermute | solution.py:454
  67.7 2.5 %collective-permute-done.19.refs_5_ = bf16[192,128]{1,0:T(8,128)(2,1)S(1)} collective-permute-done((bf16[192,128]{1,0:T(8,128)(2,1)S(1)}, bf16[192,128]{1,0:T(8,128)(2,1)S(1)}, u32[]{:S(2)}, u32[]{:S(2)}) %collective-permute-start.19) | collective-permute-done | bytes 49184 | tf_op jit(solution)/shard_map/ppermute | solution.py:454
  70.2 2.6 %shard_map.67 = (bf16[512,1024]{1,0:T(8,128)(2,1)S(1)}, bf16[64,512]{1,0:T(8,128)(2,1)S(1)}) custom-call(s32[2]{0:T(128)S(1)} %pad_add_fusion.scalars.rank_ref, bf16[8,64,512]{2,1,0:T(8,128)(2,1)S(1)} %bitcast_dynamic-update-slice_fusion.mine_ref, bf16[8,64,512]{2,1,0:T(8,128)(2,1)S(1)} %collective-permute-done.14.other_ref, ...), custom_call_target="tpu_custom_call" | custom-call | tf_op jit(solution)/shard_map/pallas_call | solution.py:341
  72.8 2.2 %collective-permute-start.22 = (bf16[64,512]{1,0:T(8,128)(2,1)S(1)}, bf16[64,512]{1,0:T(8,128)(2,1)S(1)}, u32[]{:S(2)}, u32[]{:S(2)}) collective-permute-start(bf16[64,512]{1,0:T(8,128)(2,1)S(1)} %get-tuple-element.59), channel_id=1, source_target_pairs={{0,8},{2,10},{4,12},{6,14},{8,0},{10,2},{12,4},{14,6},{1,9},{3,11}... | collective-permute-start | bytes 196616 | tf_op jit(solution)/shard_map/ppermute | solution.py:454
  74.9 3.7 %collective-permute-done.22 = bf16[64,512]{1,0:T(8,128)(2,1)S(1)} collective-permute-done((bf16[64,512]{1,0:T(8,128)(2,1)S(1)}, bf16[64,512]{1,0:T(8,128)(2,1)S(1)}, u32[]{:S(2)}, u32[]{:S(2)}) %collective-permute-start.22) | collective-permute-done | bytes 65568 | tf_op jit(solution)/shard_map/ppermute | solution.py:454
  79.3 3.1 %collective-permute-start.25 = (bf16[2,64,512]{2,1,0:T(8,128)(2,1)S(1)}, bf16[2,64,512]{2,1,0:T(8,128)(2,1)S(1)}, u32[]{:S(2)}, u32[]{:S(2)}) collective-permute-start(bf16[2,64,512]{2,1,0:T(8,128)(2,1)S(1)} %pad_maximum_fusion), channel_id=1, source_target_pairs={{0,6},{2,4},{4,2},{6,0},{8,14},{10,12},{12,10},{14,8},{1,7},{3,5},... | collective-permute-start | bytes 393224 | tf_op jit(solution)/shard_map/ppermute | solution.py:454
  82.4 5.8 %collective-permute-done.23 = bf16[2,64,512]{2,1,0:T(8,128)(2,1)S(1)} collective-permute-done((bf16[2,64,512]{2,1,0:T(8,128)(2,1)S(1)}, bf16[2,64,512]{2,1,0:T(8,128)(2,1)S(1)}, u32[]{:S(2)}, u32[]{:S(2)}) %collective-permute-start.23) | collective-permute-done | bytes 131104 | tf_op jit(solution)/shard_map/ppermute | solution.py:454
  88.1 4.4 %collective-permute-done.24 = bf16[2,64,512]{2,1,0:T(8,128)(2,1)S(1)} collective-permute-done((bf16[2,64,512]{2,1,0:T(8,128)(2,1)S(1)}, bf16[2,64,512]{2,1,0:T(8,128)(2,1)S(1)}, u32[]{:S(2)}, u32[]{:S(2)}) %collective-permute-start.24) | collective-permute-done | bytes 131104 | tf_op jit(solution)/shard_map/ppermute | solution.py:454
  92.5 5.8 %all-gather.2.cloned.1.call-done.out_mine_ref = bf16[512,1024]{1,0:T(8,128)(2,1)} async-done(((bf16[512,128]{1,0:T(8,128)(2,1)}), bf16[512,1024]{1,0:T(8,128)(2,1)}) %all-gather.2.cloned.1.call-update) | async-done | bytes 1048592 | tf_op jit(solution)/shard_map/all_gather | solution.py:468
  100.2 2.2 %collective-permute-start.30 = (bf16[512,128]{1,0:T(8,128)(2,1)S(1)}, bf16[512,128]{1,0:T(8,128)(2,1)S(1)}, u32[]{:S(2)}, u32[]{:S(2)}) collective-permute-start(bf16[512,128]{1,0:T(8,128)(2,1)S(1)} %get-tuple-element.63), channel_id=1, source_target_pairs={{0,6},{2,4},{4,2},{6,0},{8,14},{10,12},{12,10},{14,8},{1,7},{3,5},... | collective-permute-start | bytes 393224 | tf_op jit(solution)/shard_map/ppermute | solution.py:454
  102.5 2.0 %collective-permute-done.28.refs_1_ = bf16[512,128]{1,0:T(8,128)(2,1)S(1)} collective-permute-done((bf16[512,128]{1,0:T(8,128)(2,1)S(1)}, bf16[512,128]{1,0:T(8,128)(2,1)S(1)}, u32[]{:S(2)}, u32[]{:S(2)}) %collective-permute-start.28) | collective-permute-done | bytes 131104 | tf_op jit(solution)/shard_map/ppermute | solution.py:454
  109.5 2.0 %collective-permute-start.33 = (bf16[512,128]{1,0:T(8,128)(2,1)S(1)}, bf16[512,128]{1,0:T(8,128)(2,1)S(1)}, u32[]{:S(2)}, u32[]{:S(2)}) collective-permute-start(bf16[512,128]{1,0:T(8,128)(2,1)S(1)} %get-tuple-element.66), channel_id=1, source_target_pairs={{0,12},{2,14},{4,8},{6,10},{8,4},{10,6},{12,0},{14,2},{1,13},{3,15... | collective-permute-start | bytes 393224 | tf_op jit(solution)/shard_map/ppermute | solution.py:454
  111.5 8.1 %collective-permute-done.31.refs_4_ = bf16[512,128]{1,0:T(8,128)(2,1)S(1)} collective-permute-done((bf16[512,128]{1,0:T(8,128)(2,1)S(1)}, bf16[512,128]{1,0:T(8,128)(2,1)S(1)}, u32[]{:S(2)}, u32[]{:S(2)}) %collective-permute-start.31) | collective-permute-done | bytes 131104 | tf_op jit(solution)/shard_map/ppermute | solution.py:454
  122.6 4.7 %collective-permute-done.34.refs_7_ = bf16[512,128]{1,0:T(8,128)(2,1)S(1)} collective-permute-done((bf16[512,128]{1,0:T(8,128)(2,1)S(1)}, bf16[512,128]{1,0:T(8,128)(2,1)S(1)}, u32[]{:S(2)}, u32[]{:S(2)}) %collective-permute-start.34) | collective-permute-done | bytes 131104 | tf_op jit(solution)/shard_map/ppermute | solution.py:454
  129.5 4.0 %shard_map.68 = (f32[64,512]{1,0:T(8,128)S(1)}, f32[512,512]{1,0:T(8,128)S(1)}, bf16[512,512]{1,0:T(8,128)(2,1)S(1)}) custom-call(s32[2]{0:T(128)S(1)} %pad_add_fusion.scalars.rank_ref, bf16[512,1024]{1,0:T(8,128)(2,1)S(1)} %get-tuple-element.58.tokens_ref, bf16[8,64,512]{2,1,0:T(8,128)(2,1)S(1)} %slice_dynamic-update-slice_fusion.mine_ref, ...), custom_call_target="tpu_custom_call" | custom-call | tf_op jit(solution)/shard_map/pallas_call | solution.py:392
  137.0 3.6 %collective-permute-start.37 = (bf16[64,512]{1,0:T(8,128)(2,1)S(1)}, bf16[64,512]{1,0:T(8,128)(2,1)S(1)}, u32[]{:S(2)}, u32[]{:S(2)}) collective-permute-start(bf16[64,512]{1,0:T(8,128)(2,1)S(1)} %get-tuple-element.73), channel_id=1, source_target_pairs={{0,4},{2,6},{4,0},{6,2},{8,12},{10,14},{12,8},{14,10},{1,5},{3,7},... | collective-permute-start | bytes 196616 | tf_op jit(solution)/shard_map/ppermute | solution.py:454
  145.9 2.7 %collective-permute-start.42 = (bf16[64,512]{1,0:T(8,128)(2,1)S(1)}, bf16[64,512]{1,0:T(8,128)(2,1)S(1)}, u32[]{:S(2)}, u32[]{:S(2)}) collective-permute-start(bf16[64,512]{1,0:T(8,128)(2,1)S(1)} %get-tuple-element.78), channel_id=1, source_target_pairs={{0,14},{2,12},{4,10},{6,8},{8,6},{10,4},{12,2},{14,0},{1,15},{3,13... | collective-permute-start | bytes 196616 | tf_op jit(solution)/shard_map/ppermute | solution.py:454
  148.6 2.9 %collective-permute-done.39.refs_3_ = bf16[64,512]{1,0:T(8,128)(2,1)S(1)} collective-permute-done((bf16[64,512]{1,0:T(8,128)(2,1)S(1)}, bf16[64,512]{1,0:T(8,128)(2,1)S(1)}, u32[]{:S(2)}, u32[]{:S(2)}) %collective-permute-start.39) | collective-permute-done | bytes 65568 | tf_op jit(solution)/shard_map/ppermute | solution.py:454
  151.5 2.7 %collective-permute-done.40.refs_4_ = bf16[64,512]{1,0:T(8,128)(2,1)S(1)} collective-permute-done((bf16[64,512]{1,0:T(8,128)(2,1)S(1)}, bf16[64,512]{1,0:T(8,128)(2,1)S(1)}, u32[]{:S(2)}, u32[]{:S(2)}) %collective-permute-start.40) | collective-permute-done | bytes 65568 | tf_op jit(solution)/shard_map/ppermute | solution.py:454
  (96 shorter events, 34.5 us)
Async XLA Ops:
  6.5 91.8 %all-gather.2.cloned.1.call-start = ((), (), s32[]{:S(2)}) async-start(), calls=%async_computation | async-start | bytes 1179648 | tf_op jit(solution)/shard_map/all_gather | solution.py:468
  9.5 8.9 %collective-permute-start = (bf16[32,512]{1,0:T(8,128)(2,1)S(1)}, bf16[32,512]{1,0:T(8,128)(2,1)S(1)}, u32[]{:S(2)}, u32[]{:S(2)}) collective-permute-start(bf16[32,512]{1,0:T(8,128)(2,1)S(1)} %get-tuple-element.43), channel_id=1, source_target_pairs={{0,2},{2,0},{4,6},{6,4},{8,10},{10,8},{12,14},{14,12},{1,3},{3,1},... | collective-permute-start | bytes 98312 | tf_op jit(solution)/shard_map/ppermute | solution.py:454
  12.6 9.5 %collective-permute-start.1 = (bf16[32,512]{1,0:T(8,128)(2,1)S(1)}, bf16[32,512]{1,0:T(8,128)(2,1)S(1)}, u32[]{:S(2)}, u32[]{:S(2)}) collective-permute-start(bf16[32,512]{1,0:T(8,128)(2,1)S(1)} %get-tuple-element.44), channel_id=1, source_target_pairs={{0,4},{2,6},{4,0},{6,2},{8,12},{10,14},{12,8},{14,10},{1,5},{3,7},... | collective-permute-start | bytes 98312 | tf_op jit(solution)/shard_map/ppermute | solution.py:454
  14.1 7.9 %collective-permute-start.2 = (bf16[32,512]{1,0:T(8,128)(2,1)S(1)}, bf16[32,512]{1,0:T(8,128)(2,1)S(1)}, u32[]{:S(2)}, u32[]{:S(2)}) collective-permute-start(bf16[32,512]{1,0:T(8,128)(2,1)S(1)} %get-tuple-element.45), channel_id=1, source_target_pairs={{0,6},{2,4},{4,2},{6,0},{8,14},{10,12},{12,10},{14,8},{1,7},{3,5},... | collective-permute-start | bytes 98312 | tf_op jit(solution)/shard_map/ppermute | solution.py:454
  14.2 7.9 %collective-permute-start.3 = (bf16[32,512]{1,0:T(8,128)(2,1)S(1)}, bf16[32,512]{1,0:T(8,128)(2,1)S(1)}, u32[]{:S(2)}, u32[]{:S(2)}) collective-permute-start(bf16[32,512]{1,0:T(8,128)(2,1)S(1)} %get-tuple-element.46), channel_id=1, source_target_pairs={{0,8},{2,10},{4,12},{6,14},{8,0},{10,2},{12,4},{14,6},{1,9},{3,11}... | collective-permute-start | bytes 98312 | tf_op jit(solution)/shard_map/ppermute | solution.py:454
  22.0 6.7 %collective-permute-start.6 = (bf16[32,512]{1,0:T(8,128)(2,1)S(1)}, bf16[32,512]{1,0:T(8,128)(2,1)S(1)}, u32[]{:S(2)}, u32[]{:S(2)}) collective-permute-start(bf16[32,512]{1,0:T(8,128)(2,1)S(1)} %get-tuple-element.49), channel_id=1, source_target_pairs={{0,14},{2,12},{4,10},{6,8},{8,6},{10,4},{12,2},{14,0},{1,15},{3,13... | collective-permute-start | bytes 98312 | tf_op jit(solution)/shard_map/ppermute | solution.py:454
  29.5 21.5 %collective-permute-start.13 = (bf16[64,512]{1,0:T(8,128)(2,1)S(1)}, bf16[64,512]{1,0:T(8,128)(2,1)S(1)}, u32[]{:S(2)}, u32[]{:S(2)}) collective-permute-start(bf16[64,512]{1,0:T(8,128)(2,1)S(1)} %shard_map.65), channel_id=1, source_target_pairs={{0,14},{2,12},{4,10},{6,8},{8,6},{10,4},{12,2},{14,0},{1,15},{3,13... | collective-permute-start | bytes 196616 | tf_op jit(solution)/shard_map/ppermute | solution.py:454
  29.8 21.2 %collective-permute-start.12 = (bf16[64,512]{1,0:T(8,128)(2,1)S(1)}, bf16[64,512]{1,0:T(8,128)(2,1)S(1)}, u32[]{:S(2)}, u32[]{:S(2)}) collective-permute-start(bf16[64,512]{1,0:T(8,128)(2,1)S(1)} %shard_map.65), channel_id=1, source_target_pairs={{0,12},{2,14},{4,8},{6,10},{8,4},{10,6},{12,0},{14,2},{1,13},{3,15... | collective-permute-start | bytes 196616 | tf_op jit(solution)/shard_map/ppermute | solution.py:454
  33.3 17.7 %collective-permute-start.11 = (bf16[64,512]{1,0:T(8,128)(2,1)S(1)}, bf16[64,512]{1,0:T(8,128)(2,1)S(1)}, u32[]{:S(2)}, u32[]{:S(2)}) collective-permute-start(bf16[64,512]{1,0:T(8,128)(2,1)S(1)} %shard_map.65), channel_id=1, source_target_pairs={{0,10},{2,8},{4,14},{6,12},{8,2},{10,0},{12,6},{14,4},{1,11},{3,9}... | collective-permute-start | bytes 196616 | tf_op jit(solution)/shard_map/ppermute | solution.py:454
  33.3 17.7 %collective-permute-start.10 = (bf16[64,512]{1,0:T(8,128)(2,1)S(1)}, bf16[64,512]{1,0:T(8,128)(2,1)S(1)}, u32[]{:S(2)}, u32[]{:S(2)}) collective-permute-start(bf16[64,512]{1,0:T(8,128)(2,1)S(1)} %shard_map.65), channel_id=1, source_target_pairs={{0,8},{2,10},{4,12},{6,14},{8,0},{10,2},{12,4},{14,6},{1,9},{3,11}... | collective-permute-start | bytes 196616 | tf_op jit(solution)/shard_map/ppermute | solution.py:454
  51.0 19.1 %collective-permute-start.14 = (bf16[8,64,512]{2,1,0:T(8,128)(2,1)S(1)}, bf16[8,64,512]{2,1,0:T(8,128)(2,1)S(1)}, u32[]{:S(2)}, u32[]{:S(2)}) collective-permute-start(bf16[8,64,512]{2,1,0:T(8,128)(2,1)S(1)} %bitcast_dynamic-update-slice_fusion.mine_ref), channel_id=1, source_target_pairs={{0,1},{1,0},{2,3},{3,2},{4,5},{5,4},{6,7},{7,6},{8,9},{9,8},{10,11... | collective-permute-start | bytes 1572872 | tf_op jit(solution)/shard_map/ppermute | solution.py:454
  57.1 10.5 %collective-permute-start.18 = (bf16[192,128]{1,0:T(8,128)(2,1)S(1)}, bf16[192,128]{1,0:T(8,128)(2,1)S(1)}, u32[]{:S(2)}, u32[]{:S(2)}) collective-permute-start(bf16[192,128]{1,0:T(8,128)(2,1)S(1)} %get-tuple-element.54), channel_id=1, source_target_pairs={{0,8},{2,10},{4,12},{6,14},{8,0},{10,2},{12,4},{14,6},{1,9},{3,11}... | collective-permute-start | bytes 147464 | tf_op jit(solution)/shard_map/ppermute | solution.py:454
  57.8 12.4 %collective-permute-start.19 = (bf16[192,128]{1,0:T(8,128)(2,1)S(1)}, bf16[192,128]{1,0:T(8,128)(2,1)S(1)}, u32[]{:S(2)}, u32[]{:S(2)}) collective-permute-start(bf16[192,128]{1,0:T(8,128)(2,1)S(1)} %get-tuple-element.55), channel_id=1, source_target_pairs={{0,10},{2,8},{4,14},{6,12},{8,2},{10,0},{12,6},{14,4},{1,11},{3,9}... | collective-permute-start | bytes 147464 | tf_op jit(solution)/shard_map/ppermute | solution.py:454
  60.6 9.6 %collective-permute-start.20 = (bf16[192,128]{1,0:T(8,128)(2,1)S(1)}, bf16[192,128]{1,0:T(8,128)(2,1)S(1)}, u32[]{:S(2)}, u32[]{:S(2)}) collective-permute-start(bf16[192,128]{1,0:T(8,128)(2,1)S(1)} %get-tuple-element.56), channel_id=1, source_target_pairs={{0,12},{2,14},{4,8},{6,10},{8,4},{10,6},{12,0},{14,2},{1,13},{3,15... | collective-permute-start | bytes 147464 | tf_op jit(solution)/shard_map/ppermute | solution.py:454
  61.2 9.0 %collective-permute-start.21 = (bf16[192,128]{1,0:T(8,128)(2,1)S(1)}, bf16[192,128]{1,0:T(8,128)(2,1)S(1)}, u32[]{:S(2)}, u32[]{:S(2)}) collective-permute-start(bf16[192,128]{1,0:T(8,128)(2,1)S(1)} %get-tuple-element.57), channel_id=1, source_target_pairs={{0,14},{2,12},{4,10},{6,8},{8,6},{10,4},{12,2},{14,0},{1,15},{3,13... | collective-permute-start | bytes 147464 | tf_op jit(solution)/shard_map/ppermute | solution.py:454
  78.7 9.4 %collective-permute-start.23 = (bf16[2,64,512]{2,1,0:T(8,128)(2,1)S(1)}, bf16[2,64,512]{2,1,0:T(8,128)(2,1)S(1)}, u32[]{:S(2)}, u32[]{:S(2)}) collective-permute-start(bf16[2,64,512]{2,1,0:T(8,128)(2,1)S(1)} %pad_maximum_fusion), channel_id=1, source_target_pairs={{0,2},{2,0},{4,6},{6,4},{8,10},{10,8},{12,14},{14,12},{1,3},{3,1},... | collective-permute-start | bytes 393224 | tf_op jit(solution)/shard_map/ppermute | solution.py:454
  79.3 13.2 %collective-permute-start.25 = (bf16[2,64,512]{2,1,0:T(8,128)(2,1)S(1)}, bf16[2,64,512]{2,1,0:T(8,128)(2,1)S(1)}, u32[]{:S(2)}, u32[]{:S(2)}) collective-permute-start(bf16[2,64,512]{2,1,0:T(8,128)(2,1)S(1)} %pad_maximum_fusion), channel_id=1, source_target_pairs={{0,6},{2,4},{4,2},{6,0},{8,14},{10,12},{12,10},{14,8},{1,7},{3,5},... | collective-permute-start | bytes 393224 | tf_op jit(solution)/shard_map/ppermute | solution.py:454
  82.4 10.1 %collective-permute-start.24 = (bf16[2,64,512]{2,1,0:T(8,128)(2,1)S(1)}, bf16[2,64,512]{2,1,0:T(8,128)(2,1)S(1)}, u32[]{:S(2)}, u32[]{:S(2)}) collective-permute-start(bf16[2,64,512]{2,1,0:T(8,128)(2,1)S(1)} %pad_maximum_fusion), channel_id=1, source_target_pairs={{0,4},{2,6},{4,0},{6,2},{8,12},{10,14},{12,8},{14,10},{1,5},{3,7},... | collective-permute-start | bytes 393224 | tf_op jit(solution)/shard_map/ppermute | solution.py:454
  98.4 28.9 %collective-permute-start.27 = (bf16[512,1024]{1,0:T(8,128)(2,1)}, bf16[512,1024]{1,0:T(8,128)(2,1)S(1)}, u32[]{:S(2)}, u32[]{:S(2)}) collective-permute-start(bf16[512,1024]{1,0:T(8,128)(2,1)} %all-gather.2.cloned.1.call-done.out_mine_ref), channel_id=1, source_target_pairs={{0,1},{1,0},{2,3},{3,2},{4,5},{5,4},{6,7},{7,6},{8,9},{9,8},{10,11... | collective-permute-start | bytes 3145736 | tf_op jit(solution)/shard_map/ppermute | solution.py:454
  98.4 28.9 %collective-permute-start.26 = (bf16[8,64,512]{2,1,0:T(8,128)(2,1)S(1)}, bf16[8,64,512]{2,1,0:T(8,128)(2,1)S(1)}, u32[]{:S(2)}, u32[]{:S(2)}) collective-permute-start(bf16[8,64,512]{2,1,0:T(8,128)(2,1)S(1)} %slice_dynamic-update-slice_fusion.mine_ref), channel_id=1, source_target_pairs={{0,1},{1,0},{2,3},{3,2},{4,5},{5,4},{6,7},{7,6},{8,9},{9,8},{10,11... | collective-permute-start | bytes 1572872 | tf_op jit(solution)/shard_map/ppermute | solution.py:454
  100.2 9.2 %collective-permute-start.30 = (bf16[512,128]{1,0:T(8,128)(2,1)S(1)}, bf16[512,128]{1,0:T(8,128)(2,1)S(1)}, u32[]{:S(2)}, u32[]{:S(2)}) collective-permute-start(bf16[512,128]{1,0:T(8,128)(2,1)S(1)} %get-tuple-element.63), channel_id=1, source_target_pairs={{0,6},{2,4},{4,2},{6,0},{8,14},{10,12},{12,10},{14,8},{1,7},{3,5},... | collective-permute-start | bytes 393224 | tf_op jit(solution)/shard_map/ppermute | solution.py:454
  104.5 15.1 %collective-permute-start.31 = (bf16[512,128]{1,0:T(8,128)(2,1)S(1)}, bf16[512,128]{1,0:T(8,128)(2,1)S(1)}, u32[]{:S(2)}, u32[]{:S(2)}) collective-permute-start(bf16[512,128]{1,0:T(8,128)(2,1)S(1)} %get-tuple-element.64), channel_id=1, source_target_pairs={{0,8},{2,10},{4,12},{6,14},{8,0},{10,2},{12,4},{14,6},{1,9},{3,11}... | collective-permute-start | bytes 393224 | tf_op jit(solution)/shard_map/ppermute | solution.py:454
  106.3 16.3 %collective-permute-start.32 = (bf16[512,128]{1,0:T(8,128)(2,1)S(1)}, bf16[512,128]{1,0:T(8,128)(2,1)S(1)}, u32[]{:S(2)}, u32[]{:S(2)}) collective-permute-start(bf16[512,128]{1,0:T(8,128)(2,1)S(1)} %get-tuple-element.65), channel_id=1, source_target_pairs={{0,10},{2,8},{4,14},{6,12},{8,2},{10,0},{12,6},{14,4},{1,11},{3,9}... | collective-permute-start | bytes 393224 | tf_op jit(solution)/shard_map/ppermute | solution.py:454
  109.5 13.1 %collective-permute-start.33 = (bf16[512,128]{1,0:T(8,128)(2,1)S(1)}, bf16[512,128]{1,0:T(8,128)(2,1)S(1)}, u32[]{:S(2)}, u32[]{:S(2)}) collective-permute-start(bf16[512,128]{1,0:T(8,128)(2,1)S(1)} %get-tuple-element.66), channel_id=1, source_target_pairs={{0,12},{2,14},{4,8},{6,10},{8,4},{10,6},{12,0},{14,2},{1,13},{3,15... | collective-permute-start | bytes 393224 | tf_op jit(solution)/shard_map/ppermute | solution.py:454
  119.5 7.8 %collective-permute-start.34 = (bf16[512,128]{1,0:T(8,128)(2,1)S(1)}, bf16[512,128]{1,0:T(8,128)(2,1)S(1)}, u32[]{:S(2)}, u32[]{:S(2)}) collective-permute-start(bf16[512,128]{1,0:T(8,128)(2,1)S(1)} %get-tuple-element.67), channel_id=1, source_target_pairs={{0,14},{2,12},{4,10},{6,8},{8,6},{10,4},{12,2},{14,0},{1,15},{3,13... | collective-permute-start | bytes 393224 | tf_op jit(solution)/shard_map/ppermute | solution.py:454
  136.1 8.3 %collective-permute-start.36 = (bf16[64,512]{1,0:T(8,128)(2,1)S(1)}, bf16[64,512]{1,0:T(8,128)(2,1)S(1)}, u32[]{:S(2)}, u32[]{:S(2)}) collective-permute-start(bf16[64,512]{1,0:T(8,128)(2,1)S(1)} %get-tuple-element.72), channel_id=1, source_target_pairs={{0,2},{2,0},{4,6},{6,4},{8,10},{10,8},{12,14},{14,12},{1,3},{3,1},... | collective-permute-start | bytes 196616 | tf_op jit(solution)/shard_map/ppermute | solution.py:454
  137.0 8.9 %collective-permute-start.37 = (bf16[64,512]{1,0:T(8,128)(2,1)S(1)}, bf16[64,512]{1,0:T(8,128)(2,1)S(1)}, u32[]{:S(2)}, u32[]{:S(2)}) collective-permute-start(bf16[64,512]{1,0:T(8,128)(2,1)S(1)} %get-tuple-element.73), channel_id=1, source_target_pairs={{0,4},{2,6},{4,0},{6,2},{8,12},{10,14},{12,8},{14,10},{1,5},{3,7},... | collective-permute-start | bytes 196616 | tf_op jit(solution)/shard_map/ppermute | solution.py:454
  140.6 8.0 %collective-permute-start.38 = (bf16[64,512]{1,0:T(8,128)(2,1)S(1)}, bf16[64,512]{1,0:T(8,128)(2,1)S(1)}, u32[]{:S(2)}, u32[]{:S(2)}) collective-permute-start(bf16[64,512]{1,0:T(8,128)(2,1)S(1)} %get-tuple-element.74), channel_id=1, source_target_pairs={{0,6},{2,4},{4,2},{6,0},{8,14},{10,12},{12,10},{14,8},{1,7},{3,5},... | collective-permute-start | bytes 196616 | tf_op jit(solution)/shard_map/ppermute | solution.py:454
  141.0 10.6 %collective-permute-start.39 = (bf16[64,512]{1,0:T(8,128)(2,1)S(1)}, bf16[64,512]{1,0:T(8,128)(2,1)S(1)}, u32[]{:S(2)}, u32[]{:S(2)}) collective-permute-start(bf16[64,512]{1,0:T(8,128)(2,1)S(1)} %get-tuple-element.75), channel_id=1, source_target_pairs={{0,8},{2,10},{4,12},{6,14},{8,0},{10,2},{12,4},{14,6},{1,9},{3,11}... | collective-permute-start | bytes 196616 | tf_op jit(solution)/shard_map/ppermute | solution.py:454
  142.5 11.6 %collective-permute-start.40 = (bf16[64,512]{1,0:T(8,128)(2,1)S(1)}, bf16[64,512]{1,0:T(8,128)(2,1)S(1)}, u32[]{:S(2)}, u32[]{:S(2)}) collective-permute-start(bf16[64,512]{1,0:T(8,128)(2,1)S(1)} %get-tuple-element.76), channel_id=1, source_target_pairs={{0,10},{2,8},{4,14},{6,12},{8,2},{10,0},{12,6},{14,4},{1,11},{3,9}... | collective-permute-start | bytes 196616 | tf_op jit(solution)/shard_map/ppermute | solution.py:454
  144.4 9.7 %collective-permute-start.41 = (bf16[64,512]{1,0:T(8,128)(2,1)S(1)}, bf16[64,512]{1,0:T(8,128)(2,1)S(1)}, u32[]{:S(2)}, u32[]{:S(2)}) collective-permute-start(bf16[64,512]{1,0:T(8,128)(2,1)S(1)} %get-tuple-element.77), channel_id=1, source_target_pairs={{0,12},{2,14},{4,8},{6,10},{8,4},{10,6},{12,0},{14,2},{1,13},{3,15... | collective-permute-start | bytes 196616 | tf_op jit(solution)/shard_map/ppermute | solution.py:454
  145.9 8.3 %collective-permute-start.42 = (bf16[64,512]{1,0:T(8,128)(2,1)S(1)}, bf16[64,512]{1,0:T(8,128)(2,1)S(1)}, u32[]{:S(2)}, u32[]{:S(2)}) collective-permute-start(bf16[64,512]{1,0:T(8,128)(2,1)S(1)} %get-tuple-element.78), channel_id=1, source_target_pairs={{0,14},{2,12},{4,10},{6,8},{8,6},{10,4},{12,2},{14,0},{1,15},{3,13... | collective-permute-start | bytes 196616 | tf_op jit(solution)/shard_map/ppermute | solution.py:454
  (18 other events, 114.0 us)
Sparse Core Ops, SparseCore 0:
  51.3 47.0 all-gather.1

commit v2 on v1

--- a/solution.py
+++ b/solution.py
@@ -159,28 +159,17 @@
     return jax.ShapeDtypeStruct(shape, dtype)
 
 
-def pack_kernel(n, rank_ref, qkv_ref, up_ref, down_ref, *refs):
-    qkv_outs, mlp_outs, sem = refs[:n], refs[n : 2 * n], refs[2 * n]
-    rank = rank_ref[0]
+def pack_kernel(n, rank_ref, up_ref, down_ref, out_ref, sem):
+    part = rank_ref[2]
     rows = up_ref.shape[0]
     wide = up_ref.shape[1] // n
+    keep = wide // 2
     copies = []
     for j in range(n):
-        dest = rank ^ j
-        copies.append((qkv_ref.at[dest], qkv_outs[j]))
-        for c in range(wide // 128):
-            copies.append(
-                (
-                    up_ref.at[:, pl.ds(pl.multiple_of(dest * wide + c * 128, 128), 128)],
-                    mlp_outs[j].at[pl.ds(c * rows, rows)],
-                )
-            )
-        copies.append(
-            (
-                down_ref.at[pl.ds(pl.multiple_of(dest * wide, 128), wide)],
-                mlp_outs[j].at[pl.ds(rows * wide // 128, wide)],
-            )
-        )
+        columns = pl.ds(pl.multiple_of(j * wide + part * keep, 128), keep)
+        at = pl.ds(pl.multiple_of(j * wide + part * keep, 128), keep)
+        copies.append((up_ref.at[:, columns], out_ref.at[j, pl.ds(0, rows)]))
+        copies.append((down_ref.at[at], out_ref.at[j, pl.ds(rows, keep)]))
     started = []
     for i, (src, dst) in enumerate(copies):
         copy = pltpu.make_async_copy(src, dst, sem.at[i])
@@ -190,22 +179,19 @@
         copy.wait()
 
 
-def pack(rank, qkv_t, up, down, n):
-    wide = up.shape[1] // n
-    rows = up.shape[0] * wide // 128 + wide
-    copies = n * (2 + wide // 128)
-    outs = pl.pallas_call(
+def pack(scalars, up, down, n):
+    keep = up.shape[1] // n // 2
+    return pl.pallas_call(
         functools.partial(pack_kernel, n),
-        in_specs=[sspec(), aspec(), aspec(), aspec()],
-        out_specs=[aspec()] * (2 * n),
-        out_shape=[struct(qkv_t.shape[1:])] * n + [struct((rows, 128))] * n,
-        scratch_shapes=[pltpu.SemaphoreType.DMA((copies,))],
-        compiler_params=params(),
-    )(rank, qkv_t, up, down)
-    return list(outs[:n]), list(outs[n:])
-
-
-def prep_kernel(n, sup, rank_ref, keep_ref, patches_ref, *outs):
+        in_specs=[sspec(), aspec(), aspec()],
+        out_specs=aspec(),
+        out_shape=struct((n, up.shape[0] + keep, keep)),
+        scratch_shapes=[pltpu.SemaphoreType.DMA((2 * n,))],
+        compiler_params=params(),
+    )(scalars, up, down)
+
+
+def prep_kernel(n, sup, rank_ref, keep_ref, patches_ref, out_ref):
     rank = rank_ref[0]
     first = rank * sup
     keep = keep_ref[...]
@@ -235,19 +221,19 @@
     means = jnp.dot(averaging, flat, preferred_element_type=F32).astype(BF16)
     slot = lax.broadcasted_iota(jnp.int32, (SLOT, 1), 0)
     for j in range(n):
-        pos = ((rank ^ j) - start) % n + slot * n
+        pos = ((j - start) & (n - 1)) + slot * n
         fine = (pos == fine_pos).astype(F32).astype(BF16)
         mean = (pos == mean_pos).astype(F32).astype(BF16)
-        outs[j][...] = (
+        out_ref[j] = (
             jnp.dot(fine, flat, preferred_element_type=F32)
             + jnp.dot(mean, means, preferred_element_type=F32)
         ).astype(BF16)
 
 
-def prep(rank, keep_col, flat, half, n, sup):
+def prep(scalars, keep_col, flat, n, sup):
     width = flat.shape[1] // 2
     return pl.pallas_call(
-        functools.partial(prep_kernel_half, n, sup),
+        functools.partial(prep_kernel, n, sup),
         grid_spec=pltpu.PrefetchScalarGridSpec(
             num_scalar_prefetch=1,
             grid=(1,),
@@ -255,47 +241,44 @@
                 pl.BlockSpec(keep_col.shape, lambda i, ref: (0, 0)),
                 pl.BlockSpec((flat.shape[0], width), lambda i, ref: (0, ref[1])),
             ],
-            out_specs=[pl.BlockSpec((SLOT, width), lambda i, ref: (0, 0))] * n,
+            out_specs=pl.BlockSpec((n, SLOT, width), lambda i, ref: (0, 0, 0)),
         ),
-        out_shape=[struct((SLOT, width))] * n,
-        compiler_params=params(),
-    )(jnp.stack([rank, half]).astype(jnp.int32), keep_col, flat)
-
-
-def prep_kernel_half(n, sup, scalars, keep_ref, patches_ref, *outs):
-    prep_kernel(n, sup, scalars, keep_ref, patches_ref, *outs)
-
-
-def pick_kernel(n, sup, per_owner, rank_ref, keep_ref, *refs):
-    ins, out = refs[:n], refs[n]
+        out_shape=struct((n, SLOT, width)),
+        compiler_params=params(),
+    )(scalars, keep_col, flat)
+
+
+def pick_kernel(n, sup, per_owner, rank_ref, keep_ref, got_ref, out_ref):
     rank = rank_ref[0]
     keep = keep_ref[...]
     count = keep.shape[0]
     lanes = n * SLOT
     shift = SLOT.bit_length() - 1
-    source = (lax.broadcasted_iota(jnp.int32, (count, lanes), 1) >> shift) ^ rank
+    source = (lax.broadcasted_iota(jnp.int32, (count, lanes), 1) >> shift)
     low = jnp.sum((keep < source * sup).astype(jnp.int32), axis=0, keepdims=True)
     high = jnp.sum((keep < source * sup + sup).astype(jnp.int32), axis=0, keepdims=True)
     lane = lax.broadcasted_iota(jnp.int32, (1, lanes), 1)
-    source_row = (lane >> shift) ^ rank
+    source_row = lane >> shift
     start = source_row * sup + 3 * low
     stop = source_row * sup + sup + 3 * high
     token = start + ((rank - start) & (n - 1)) + (lane & (SLOT - 1)) * n
     row = jnp.where(token < stop, token >> (n.bit_length() - 1), -1)
     own = lax.broadcasted_iota(jnp.int32, (per_owner, lanes), 0)
     choose = (own == row).astype(F32).astype(BF16)
-    stacked = jnp.concatenate([ref[...] for ref in ins], axis=0)
-    out[...] = jnp.dot(choose, stacked, preferred_element_type=F32).astype(BF16)
-
-
-def pick(rank, keep_col, pieces, n, sup, per_owner):
+    stacked = got_ref[...].reshape(lanes, got_ref.shape[2])
+    owned = jnp.dot(choose, stacked, preferred_element_type=F32).astype(BF16)
+    for j in range(n):
+        out_ref[j] = owned
+
+
+def pick(scalars, keep_col, got, n, sup, per_owner):
     return pl.pallas_call(
         functools.partial(pick_kernel, n, sup, per_owner),
-        in_specs=[sspec()] + [vspec()] * (n + 1),
+        in_specs=[sspec(), vspec(), vspec()],
         out_specs=vspec(),
-        out_shape=struct((per_owner, pieces[0].shape[1])),
-        compiler_params=params(),
-    )(rank, keep_col, *pieces)
+        out_shape=struct((n, per_owner, got.shape[2])),
+        compiler_params=params(),
+    )(scalars, keep_col, got)
 
 
 def norm_rows(x):
@@ -304,19 +287,14 @@
     return (x - average) * lax.rsqrt(power - average * average + 1e-06)
 
 
-def attend_kernel(n, rank_ref, mine_ref, other_ref, *refs):
-    weights = refs[:n]
-    tokens_ref, out_ref, weight_ref = refs[n], refs[n + 1], refs[n + 2]
-    rank, half = rank_ref[0], rank_ref[1]
-    rows = mine_ref.shape[1]
-    width = mine_ref.shape[2]
-    depth = weights[0].shape[1]
+def attend_kernel(n, rank_ref, mine_ref, other_ref, got_ref, tokens_ref, out_ref, weight_ref):
+    half = rank_ref[1]
+    rows, width = mine_ref.shape
+    depth = got_ref.shape[2]
+    tokens_ref[:, pl.ds(pl.multiple_of(half * width, width), width)] = mine_ref[...]
+    tokens_ref[:, pl.ds(pl.multiple_of((1 - half) * width, width), width)] = other_ref[...]
     for j in range(n):
-        source = rank ^ j
-        at = pl.ds(pl.multiple_of(source * rows, rows), rows)
-        tokens_ref[at, pl.ds(pl.multiple_of(half * width, width), width)] = mine_ref[j]
-        tokens_ref[at, pl.ds(pl.multiple_of((1 - half) * width, width), width)] = other_ref[j]
-        weight_ref[:, pl.ds(pl.multiple_of(source * depth, depth), depth)] = weights[j][...]
+        weight_ref[:, j * depth : (j + 1) * depth] = got_ref[j]
     normed = norm_rows(tokens_ref[...].astype(F32)).astype(BF16)
     projected = lax.dot_general(
         normed, weight_ref[...], (((1,), (1,)), ((), ())), preferred_element_type=F32
@@ -330,49 +308,56 @@
     ) * (1.0 / math.sqrt(size))
     powers = jnp.exp(scores - jnp.max(scores, axis=1, keepdims=True))
     probs = (powers / jnp.sum(powers, axis=1, keepdims=True)).astype(BF16)
-    out_ref[...] = lax.dot_general(
+    attended = lax.dot_general(
         values, probs, (((0,), (1,)), ((), ())), preferred_element_type=F32
     ).astype(BF16)
+    for j in range(n):
+        out_ref[j] = attended
 
 
 def attend_fast(scalars, mine, other, weights, n):
-    rows = mine.shape[0] * mine.shape[1]
-    size = weights[0].shape[0] // 3
+    rows, width = mine.shape
+    size = weights.shape[1] // 3
     return pl.pallas_call(
         functools.partial(attend_kernel, n),
-        in_specs=[sspec()] + [vspec()] * (n + 2),
+        in_specs=[sspec()] + [vspec()] * 3,
         out_specs=[vspec()] * 2,
-        out_shape=[struct((rows, 2 * mine.shape[2])), struct((size, rows))],
-        scratch_shapes=[VMEM((weights[0].shape[0], n * weights[0].shape[1]), BF16)],
-        compiler_params=params(),
-    )(scalars, mine, other, *weights)
-
-
-def mlp_kernel(n, rank_ref, tokens_ref, mine_ref, other_ref, out_mine_ref, out_other_ref, *refs):
-    weights = refs[:n]
-    residual_ref, keep_ref, send_ref, up_ref, down_ref, row_ref, joined_ref = refs[n:]
+        out_shape=[struct((rows, 2 * width)), struct((n, size, rows))],
+        scratch_shapes=[VMEM((weights.shape[1], n * weights.shape[2]), BF16)],
+        compiler_params=params(),
+    )(scalars, mine, other, weights)
+
+
+def mlp_kernel(
+    n,
+    rank_ref,
+    tokens_ref,
+    mine_ref,
+    other_ref,
+    out_mine_ref,
+    out_other_ref,
+    first_ref,
+    second_ref,
+    residual_ref,
+    keep_ref,
+    send_ref,
+    up_ref,
+    down_ref,
+    row_ref,
+):
     rank, half = rank_ref[0], rank_ref[1]
-    wide, depth = down_ref.shape
     block = up_ref.shape[0] // n
+    unit = first_ref.shape[2]
     for j in range(n):
-        source = rank ^ j
-        for c in range(wide // 128):
-            up_ref[pl.ds(pl.multiple_of(source * block, block), block), c * 128 : (c + 1) * 128] = (
-                weights[j][c * block : (c + 1) * block]
-            )
-        down_ref[:, pl.ds(pl.multiple_of(source * 128, 128), 128)] = weights[j][
-            block * wide // 128 :
-        ]
-    size = mine_ref.shape[1]
-    for j in range(n):
-        at = pl.ds(pl.multiple_of((rank ^ j) * size, size), size)
-        joined_ref[0, at] = mine_ref[j]
-        joined_ref[1, at] = other_ref[j]
+        for c, got_ref in enumerate((first_ref, second_ref)):
+            units = pl.ds(c * unit, unit)
+            up_ref[j * block : (j + 1) * block, units] = got_ref[j, :block]
+            down_ref[units, j * 128 : (j + 1) * 128] = got_ref[j, block:]
     dims = (((0,), (0,)), ((), ()))
     row_ref[...] = (
         tokens_ref[...].astype(F32)
-        + lax.dot_general(joined_ref[0], out_mine_ref[...], dims, preferred_element_type=F32)
-        + lax.dot_general(joined_ref[1], out_other_ref[...], dims, preferred_element_type=F32)
+        + lax.dot_general(mine_ref[...], out_mine_ref[...], dims, preferred_element_type=F32)
+        + lax.dot_general(other_ref[...], out_other_ref[...], dims, preferred_element_type=F32)
     )
     part = residual_ref.shape[0]
     width = residual_ref.shape[1]
@@ -386,12 +371,13 @@
     send_ref[...] = jnp.dot(hidden, down_ref[:, other_cols], preferred_element_type=F32).astype(BF16)
 
 
-def mlp(scalars, tokens, mine, other, out_mine, out_other, weights, n, wide):
+def mlp(scalars, tokens, mine, other, out_mine, out_other, first, second, n):
     length, depth = tokens.shape
     width = depth // 2
+    wide = 2 * first.shape[2]
     return pl.pallas_call(
         functools.partial(mlp_kernel, n),
-        in_specs=[sspec()] + [vspec()] * (n + 5),
+        in_specs=[sspec()] + [vspec()] * 7,
         out_specs=[vspec()] * 3,
         out_shape=[
             struct((length // n, width), F32),
@@ -402,51 +388,44 @@
             VMEM((depth, wide), BF16),
             VMEM((wide, depth), BF16),
             VMEM((length, depth), F32),
-            VMEM((2, mine.shape[0] * mine.shape[1], length), BF16),
         ],
         compiler_params=params(),
-    )(scalars, tokens, mine, other, out_mine, out_other, *weights)
-
-
-def join_kernel(n, rank_ref, keep_ref, got_ref, residual_ref, base_ref, *outs):
+    )(scalars, tokens, mine, other, out_mine, out_other, first, second)
+
+
+def join_kernel(rank_ref, keep_ref, got_ref, residual_ref, base_ref, out_ref):
+    part = residual_ref.shape[0]
+    mine = pl.ds(pl.multiple_of(rank_ref[0] * part, part), part)
+    base_ref[...] = keep_ref[mine] + got_ref[mine].astype(F32) + residual_ref[...]
+    out_ref[...] = (keep_ref[...] + got_ref[...].astype(F32)).astype(BF16)
+
+
+def join(scalars, keep, got, residual):
+    return pl.pallas_call(
+        join_kernel,
+        in_specs=[sspec()] + [vspec()] * 3,
+        out_specs=[vspec()] * 2,
+        out_shape=[struct(residual.shape, F32), struct(keep.shape)],
+        compiler_params=params(),
+    )(scalars, keep, got, residual)
+
+
+def last_kernel(n, rank_ref, base_ref, terms_ref, out_ref):
     rank = rank_ref[0]
-    part = residual_ref.shape[0]
-    for j in range(n):
-        at = pl.ds(pl.multiple_of((rank ^ j) * part, part), part)
-        total = keep_ref[at] + got_ref[at].astype(F32)
-        if j == 0:
-            base_ref[...] = total + residual_ref[...]
-        else:
-            outs[j - 1][...] = total.astype(BF16)
-
-
-def join(scalars, keep, got, residual, n):
-    part, width = residual.shape
-    outs = pl.pallas_call(
-        functools.partial(join_kernel, n),
-        in_specs=[sspec()] + [vspec()] * 3,
-        out_specs=[vspec()] * n,
-        out_shape=[struct((part, width), F32)] + [struct((part, width))] * (n - 1),
-        compiler_params=params(),
-    )(scalars, keep, got, residual)
-    return outs[0], list(outs[1:])
-
-
-def last_kernel(base_ref, *refs):
     total = base_ref[...]
-    for ref in refs[:-1]:
-        total = total + ref[...].astype(F32)
-    refs[-1][...] = total.astype(BF16)
-
-
-def last(base, terms):
-    return pl.pallas_call(
-        last_kernel,
-        in_specs=[vspec()] * (1 + len(terms)),
+    for j in range(1, n):
+        total = total + terms_ref[rank ^ j].astype(F32)
+    out_ref[...] = total.astype(BF16)
+
+
+def last(scalars, base, terms):
+    return pl.pallas_call(
+        functools.partial(last_kernel, terms.shape[0]),
+        in_specs=[sspec()] + [vspec()] * 2,
         out_specs=vspec(),
         out_shape=struct(base.shape),
         compiler_params=params(),
-    )(base, *terms)
+    )(scalars, base, terms)
 
 
 def swap(value, axis, j):
@@ -454,45 +433,53 @@
     return lax.ppermute(value, axis, [(i, i ^ j) for i in range(n)])
 
 
+def exchange(value):
+    return lax.all_to_all(value, "seq", split_axis=0, concat_axis=0, tiled=True)
+
+
+def after(value, *others):
+    return lax.optimization_barrier((value, *others))[0]
+
+
 def local_fast(patches, keep_list, qkv_weight, out_weight, up_weight, down_weight):
     n = lax.axis_size("seq")
-    rank = lax.axis_index("seq").astype(jnp.int32)
-    half = lax.axis_index("head").astype(jnp.int32)
+    scalars = jnp.stack(
+        [lax.axis_index(name).astype(jnp.int32) for name in ("seq", "head", "groups")]
+    )
     sup, depth = patches.shape[1], patches.shape[3]
     length = sup * n * 8 // 5
     per_owner = length // n
-    wide = up_weight.shape[1] // n
-    scalars = jnp.stack([rank, half])
+    half_width = depth // 2
     keep_col = keep_list.reshape(-1, 1)
     flat = patches.reshape(4 * sup, depth)
     out_mine = lax.all_gather(out_weight, "seq", axis=1, tiled=True)
     out_other = swap(out_mine, "head", 1)
-    slots = prep(rank, keep_col, flat, half, n, sup)
-    qkv_blocks, mlp_blocks = pack(scalars, qkv_weight.transpose(1, 2, 0), up_weight, down_weight, n)
-    dealt = [slots[0]] + [swap(slots[j], "seq", j) for j in range(1, n)]
-    qkv_got = [qkv_blocks[0]] + [swap(qkv_blocks[j], "seq", j) for j in range(1, n)]
+    slots = prep(scalars, keep_col, flat, n, sup)
+    packed = pack(scalars, up_weight, down_weight, n)
+    dealt = exchange(slots)
+    qkv_got = exchange(after(qkv_weight.transpose(1, 2, 0), slots))
     owned = pick(scalars, keep_col, dealt, n, sup, per_owner)
-    pieces = jnp.stack([owned] + [swap(owned, "seq", j) for j in range(1, n)])
+    pieces = exchange(owned).reshape(length, half_width)
+    first = exchange(after(packed, owned))
     pieces_other = swap(pieces, "head", 1)
-    mlp_got = [mlp_blocks[0]] + [swap(mlp_blocks[j], "seq", j) for j in range(1, n)]
+    second = swap(first, "groups", 1)
     tokens, attended = attend_fast(scalars, pieces, pieces_other, qkv_got, n)
-    pair = jnp.stack([attended, swap(attended, "seq", n // 2)])
-    quads = [pair] + [swap(pair, "seq", j) for j in range(1, n // 2)]
-    gathered = jnp.stack([quad[k] for k in range(2) for quad in quads])
+    gathered = exchange(attended).reshape(half_width, length)
     gathered_other = swap(gathered, "head", 1)
     residual, keep, send = mlp(
-        scalars, tokens, gathered, gathered_other, out_mine, out_other, mlp_got, n, wide
+        scalars, tokens, gathered, gathered_other, out_mine, out_other, first, second, n
     )
     got = swap(send, "head", 1)
-    base, terms = join(scalars, keep, got, residual, n)
-    terms = [swap(terms[j - 1], "seq", j) for j in range(1, n)]
-    encoded = last(base, terms)
-    return encoded.reshape(1, per_owner, 1, depth // 2)
+    base, terms = join(scalars, keep, got, residual)
+    terms = exchange(terms.reshape(n, per_owner, half_width))
+    encoded = last(scalars, base, terms)
+    return encoded.reshape(1, per_owner, 1, half_width)
 
 
 def local(patches, keep_list, qkv_weight, out_weight, up_weight, down_weight):
     n = lax.axis_size("seq")
     one_image = patches.shape[0] == 1 and qkv_weight.shape[1] == n and n & (n - 1) == 0
+    one_image = one_image and lax.axis_size("groups") == 2 and up_weight.shape[1] == n * 256
     plan = local_fast if one_image else local_general
     return plan(patches, keep_list, qkv_weight, out_weight, up_weight, down_weight)
 

time: 162 us -> 149 us (0.920)
  starting transfers between devices: 59.8 us -> 23 us
  blocking collectives: 0 us -> 17.5 us
  waiting for transfers between devices: 71.9 us -> 77.6 us
  Pallas kernels: 12.2 us -> 14.1 us
    ppermute x43 -> x5, starting transfers between devices: 59.8 us -> 1.3 us  [swap(): return lax.ppermute(value, axis, [(i, i ^ j) for i in range(n)])]
    ppermute x43 -> x5, waiting for transfers between devices: 66 us -> 16.8 us  [swap(): return lax.ppermute(value, axis, [(i, i ^ j) for i in range(n)])]
    all_to_all x0 -> x5, waiting for transfers between devices: none -> 41.9 us  [exchange(): return lax.all_to_all(value, 'seq', split_axis=0, concat_axis=0, tiled=True)]
    all_to_all x0 -> x5, starting transfers between devices: none -> 21.6 us  [exchange(): return lax.all_to_all(value, 'seq', split_axis=0, concat_axis=0, tiled=True)]
    all_to_all x0 -> x1, blocking collectives: none -> 17.5 us  [exchange(): return lax.all_to_all(value, 'seq', split_axis=0, concat_axis=0, tiled=True)]
    all_gather x1, waiting for transfers between devices: 5.84 us -> 18.3 us  [local_fast(): out_mine = lax.all_gather(out_weight, 'seq', axis=1, tiled=True)]
  transfers between devices with their start and end apart: 44 -> 11, of which waited for: 22 -> 9; matrix products, arithmetic and copies ran while one was open for 0% -> 0% of each run, Pallas kernels for 3% -> 4%
where the time goes in v2:
time: 149 us
  waiting for transfers between devices  77.6 us (52%)
  starting transfers between devices  23 us (15%)
  blocking collectives  17.5 us (12%)
  Pallas kernels  14.1 us (9%)
  between operations  13.5 us (9%)
  local copies, waits for them, and re-layouts  3.03 us (2%)
    all_to_all x5, waiting for transfers between devices, exchange(): return lax.all_to_all(value, 'seq', split_axis=0, concat_axis=0, tiled=True)  41.9 us
    all_to_all x5, starting transfers between devices, exchange(): return lax.all_to_all(value, 'seq', split_axis=0, concat_axis=0, tiled=True)  21.6 us
    all_gather x1, waiting for transfers between devices, local_fast(): out_mine = lax.all_gather(out_weight, 'seq', axis=1, tiled=True)  18.3 us
    all_to_all x1, blocking collectives, exchange(): return lax.all_to_all(value, 'seq', split_axis=0, concat_axis=0, tiled=True)  17.5 us
    ppermute x5, waiting for transfers between devices, swap(): return lax.ppermute(value, axis, [(i, i ^ j) for i in range(n)])  16.8 us
    pallas_call x1, Pallas kernels, mlp(): pl.pallas_call(functools.partial(mlp_kernel, n), in_specs=[sspec()] + [vs...  3.9 us
    pallas_call x1, Pallas kernels, attend_fast(): pl.pallas_call(functools.partial(attend_kernel, n), in_specs=[sspec()] +...  3.33 us
  transfers between devices with their start and end apart: 11, of which 9 were waited for; matrix products, arithmetic and copies ran while one was open for 0% of the time, Pallas kernels for 4%

profile of v2, /device:TPU:0, one launch (start us, length us, event | category | flops | bytes accessed | tf_op | source)
XLA Modules:
  0.0 148.7 jit_solution(5837287982574383605)
XLA Ops:
  6.5 0.7 copy-done.3
  7.2 0.1 copy.8.keep_ref
  7.3 1.0 reshape.19.patches_ref
  8.3 0.1 pad_add_fusion.rank_ref
  8.4 1.8 %shard_map.64 = bf16[8,32,512]{2,1,0:T(8,128)(2,1)} custom-call(s32[3]{0:T(128)S(1)} %pad_add_fusion.rank_ref, s32[64,1]{1,0:T(8,128)S(1)} %copy.8.keep_ref, bf16[160,1024]{1,0:T(8,128)(2,1)S(1)} %reshape.19.patches_ref), custom_call_target="tpu_custom_call" | custom-call | tf_op jit(solution)/shard_map/pallas_call | solution.py:235
  10.3 7.3 %all-to-all-start = ((bf16[8,32,512]{2,1,0:T(8,128)(2,1)}), bf16[8,32,512]{2,1,0:T(8,128)(2,1)S(1)}, u32[]{:S(2)}, u32[]{:S(2)}) async-start(bf16[8,32,512]{2,1,0:T(8,128)(2,1)} %shard_map.64), calls=%async_computation | async-start | bytes 524288 | tf_op jit(solution)/shard_map/all_to_all | solution.py:437
  17.6 8.9 %all-to-all-done.got_ref = bf16[8,32,512]{2,1,0:T(8,128)(2,1)S(1)} async-done(((bf16[8,32,512]{2,1,0:T(8,128)(2,1)}), bf16[8,32,512]{2,1,0:T(8,128)(2,1)S(1)}, u32[]{:S(2)}, u32[]{:S(2)}) %all-to-all-start) | async-done | bytes 262176 | tf_op jit(solution)/shard_map/all_to_all | solution.py:437
  26.5 3.6 %all-to-all-start.2 = ((bf16[8,192,128]{2,1,0:T(8,128)(2,1)}), bf16[8,192,128]{2,1,0:T(8,128)(2,1)S(1)}, u32[]{:S(2)}, u32[]{:S(2)}) async-start(bf16[8,192,128]{2,1,0:T(8,128)(2,1)} %bitcast.5), calls=%async_computation.2 | async-start | bytes 786432 | tf_op jit(solution)/shard_map/all_to_all | solution.py:437
  30.1 1.6 %shard_map.65 = bf16[8,64,512]{2,1,0:T(8,128)(2,1)} custom-call(s32[3]{0:T(128)S(1)} %pad_add_fusion.rank_ref, s32[64,1]{1,0:T(8,128)S(1)} %copy.8.keep_ref, bf16[8,32,512]{2,1,0:T(8,128)(2,1)S(1)} %all-to-all-done.got_ref), custom_call_target="tpu_custom_call" | custom-call | tf_op jit(solution)/shard_map/pallas_call | solution.py:275
  31.6 9.8 %all-to-all-done.2.got_ref = bf16[8,192,128]{2,1,0:T(8,128)(2,1)S(1)} async-done(((bf16[8,192,128]{2,1,0:T(8,128)(2,1)}), bf16[8,192,128]{2,1,0:T(8,128)(2,1)S(1)}, u32[]{:S(2)}, u32[]{:S(2)}) %all-to-all-start.2) | async-done | bytes 393248 | tf_op jit(solution)/shard_map/all_to_all | solution.py:437
  41.4 3.6 %all-to-all-start.1 = ((bf16[8,64,512]{2,1,0:T(8,128)(2,1)}), bf16[8,64,512]{2,1,0:T(8,128)(2,1)S(1)}, u32[]{:S(2)}, u32[]{:S(2)}) async-start(bf16[8,64,512]{2,1,0:T(8,128)(2,1)} %shard_map.65), calls=%async_computation.1 | async-start | bytes 1048576 | tf_op jit(solution)/shard_map/all_to_all | solution.py:437
  45.1 0.0 all-gather.2.cloned.1.call-start
  45.1 0.7 all-gather.2.cloned.1.call-update
  45.8 1.5 %shard_map.67 = bf16[8,256,128]{2,1,0:T(8,128)(2,1)} custom-call(s32[3]{0:T(128)S(1)} %pad_add_fusion.rank_ref, bf16[128,2048]{1,0:T(8,128)(2,1)S(1)} %copy-done.1, bf16[2048,128]{1,0:T(8,128)(2,1)S(1)} %copy-done.2), custom_call_target="tpu_custom_call" | custom-call | tf_op jit(solution)/shard_map/pallas_call | solution.py:184
  47.3 11.7 %all-to-all-done.1 = bf16[8,64,512]{2,1,0:T(8,128)(2,1)S(1)} async-done(((bf16[8,64,512]{2,1,0:T(8,128)(2,1)}), bf16[8,64,512]{2,1,0:T(8,128)(2,1)S(1)}, u32[]{:S(2)}, u32[]{:S(2)}) %all-to-all-start.1) | async-done | bytes 524320 | tf_op jit(solution)/shard_map/all_to_all | solution.py:437
  59.0 3.6 %all-to-all-start.4 = ((bf16[8,256,128]{2,1,0:T(8,128)(2,1)}), bf16[8,256,128]{2,1,0:T(8,128)(2,1)S(1)}, u32[]{:S(2)}, u32[]{:S(2)}) async-start(bf16[8,256,128]{2,1,0:T(8,128)(2,1)} %shard_map.67), calls=%async_computation.4 | async-start | bytes 1048576 | tf_op jit(solution)/shard_map/all_to_all | solution.py:437
  62.7 1.9 %collective-permute-done.other_ref = bf16[512,512]{1,0:T(8,128)(2,1)S(1)} collective-permute-done((bf16[512,512]{1,0:T(8,128)(2,1)S(1)}, bf16[512,512]{1,0:T(8,128)(2,1)S(1)}, u32[]{:S(2)}, u32[]{:S(2)}) %collective-permute-start) | collective-permute-done | bytes 524320 | tf_op jit(solution)/shard_map/ppermute | solution.py:433
  64.6 3.3 %shard_map.66 = (bf16[512,1024]{1,0:T(8,128)(2,1)S(1)}, bf16[8,64,512]{2,1,0:T(8,128)(2,1)}) custom-call(s32[3]{0:T(128)S(1)} %pad_add_fusion.rank_ref, bf16[512,512]{1,0:T(8,128)(2,1)S(1)} %bitcast.10, bf16[512,512]{1,0:T(8,128)(2,1)S(1)} %collective-permute-done.other_ref, bf16[8,192,128]{2,1,0:T(8,128)(2,1)S(1)} %all-to-all-done.2.got_ref), custom_call_target="tpu_custom_call" | custom-call | tf_op jit(solution)/shard_map/pallas_call | solution.py:321
  67.9 11.4 %all-to-all-done.4.first_ref = bf16[8,256,128]{2,1,0:T(8,128)(2,1)S(1)} async-done(((bf16[8,256,128]{2,1,0:T(8,128)(2,1)}), bf16[8,256,128]{2,1,0:T(8,128)(2,1)S(1)}, u32[]{:S(2)}, u32[]{:S(2)}) %all-to-all-start.4) | async-done | bytes 524320 | tf_op jit(solution)/shard_map/all_to_all | solution.py:437
  79.3 3.5 %all-to-all-start.3 = ((bf16[8,64,512]{2,1,0:T(8,128)(2,1)}), bf16[8,64,512]{2,1,0:T(8,128)(2,1)S(1)}, u32[]{:S(2)}, u32[]{:S(2)}) async-start(bf16[8,64,512]{2,1,0:T(8,128)(2,1)} %get-tuple-element.16), calls=%async_computation.3 | async-start | bytes 1048576 | tf_op jit(solution)/shard_map/all_to_all | solution.py:437
  82.8 18.3 %all-gather.2.cloned.1.call-done.out_mine_ref = bf16[512,1024]{1,0:T(8,128)(2,1)} async-done(((bf16[512,128]{1,0:T(8,128)(2,1)}), bf16[512,1024]{1,0:T(8,128)(2,1)}) %all-gather.2.cloned.1.call-update) | async-done | bytes 1048592 | tf_op jit(solution)/shard_map/all_gather | solution.py:455
  101.0 1.1 collective-permute-start.3
  102.1 0.1 all-to-all-done.3
  102.2 0.2 collective-permute-start.1
  102.3 13.0 %collective-permute-done.3.second_ref = bf16[8,256,128]{2,1,0:T(8,128)(2,1)S(1)} collective-permute-done((bf16[8,256,128]{2,1,0:T(8,128)(2,1)S(1)}, bf16[8,256,128]{2,1,0:T(8,128)(2,1)S(1)}, u32[]{:S(2)}, u32[]{:S(2)}) %collective-permute-start.3) | collective-permute-done | bytes 524320 | tf_op jit(solution)/shard_map/ppermute | solution.py:433
  115.4 1.2 copy-done
  116.6 3.9 %shard_map.68 = (f32[64,512]{1,0:T(8,128)S(1)}, f32[512,512]{1,0:T(8,128)S(1)}, bf16[512,512]{1,0:T(8,128)(2,1)S(1)}) custom-call(s32[3]{0:T(128)S(1)} %pad_add_fusion.rank_ref, bf16[512,1024]{1,0:T(8,128)(2,1)S(1)} %get-tuple-element.15.tokens_ref, bf16[512,512]{1,0:T(8,128)(2,1)S(1)} %bitcast.12, bf16[512,512]{1,0:T(8,128)(2,1)S(1)} %collective-permute-done.1.other_ref, ...), custom_call_target="tpu_custom_call" | custom-call | tf_op jit(solution)/shard_map/pallas_call | solution.py:378
  120.5 0.1 collective-permute-start.4
  120.6 1.9 %collective-permute-done.4.got_ref = bf16[512,512]{1,0:T(8,128)(2,1)S(1)} collective-permute-done((bf16[512,512]{1,0:T(8,128)(2,1)S(1)}, bf16[512,512]{1,0:T(8,128)(2,1)S(1)}, u32[]{:S(2)}, u32[]{:S(2)}) %collective-permute-start.4) | collective-permute-done | bytes 524320 | tf_op jit(solution)/shard_map/ppermute | solution.py:433
  122.5 0.7 shard_map.69
  123.2 17.5 %all_to_all.30.terms_ref = bf16[8,64,512]{2,1,0:T(8,128)(2,1)S(1)} all-to-all(bf16[8,64,512]{2,1,0:T(8,128)(2,1)S(1)} %bitcast.13), channel_id=1, replica_groups=mesh['groups'=2,'seq'=8,'head'=2] {'seq'}, dimensions={0} | all-to-all | bytes 1048576 | tf_op jit(solution)/shard_map/all_to_all | solution.py:437
  140.7 1.2 shard_map.70
  (10 shorter events, 0.0 us)
Async XLA Ops:
  6.5 0.7 copy-start.3
  10.3 16.2 %all-to-all-start = ((bf16[8,32,512]{2,1,0:T(8,128)(2,1)}), bf16[8,32,512]{2,1,0:T(8,128)(2,1)S(1)}, u32[]{:S(2)}, u32[]{:S(2)}) async-start(bf16[8,32,512]{2,1,0:T(8,128)(2,1)} %shard_map.64), calls=%async_computation | async-start | bytes 524288 | tf_op jit(solution)/shard_map/all_to_all | solution.py:437
  26.5 15.0 %all-to-all-start.2 = ((bf16[8,192,128]{2,1,0:T(8,128)(2,1)}), bf16[8,192,128]{2,1,0:T(8,128)(2,1)S(1)}, u32[]{:S(2)}, u32[]{:S(2)}) async-start(bf16[8,192,128]{2,1,0:T(8,128)(2,1)} %bitcast.5), calls=%async_computation.2 | async-start | bytes 786432 | tf_op jit(solution)/shard_map/all_to_all | solution.py:437
  31.6 14.2 %copy-start.1 = (bf16[128,2048]{1,0:T(8,128)(2,1)S(1)}, bf16[128,2048]{1,0:T(8,128)(2,1)}, u32[]{:S(2)}) copy-start(bf16[128,2048]{1,0:T(8,128)(2,1)} %up_ref.1) | copy-start | bytes 1572868
  31.6 14.2 %copy-start.2 = (bf16[2048,128]{1,0:T(8,128)(2,1)S(1)}, bf16[2048,128]{1,0:T(8,128)(2,1)}, u32[]{:S(2)}) copy-start(bf16[2048,128]{1,0:T(8,128)(2,1)} %down_ref.1) | copy-start | bytes 1572868
  41.4 17.6 %all-to-all-start.1 = ((bf16[8,64,512]{2,1,0:T(8,128)(2,1)}), bf16[8,64,512]{2,1,0:T(8,128)(2,1)S(1)}, u32[]{:S(2)}, u32[]{:S(2)}) async-start(bf16[8,64,512]{2,1,0:T(8,128)(2,1)} %shard_map.65), calls=%async_computation.1 | async-start | bytes 1048576 | tf_op jit(solution)/shard_map/all_to_all | solution.py:437
  45.1 56.0 %all-gather.2.cloned.1.call-start = ((), (), s32[]{:S(2)}) async-start(), calls=%async_computation.6 | async-start | bytes 1179648 | tf_op jit(solution)/shard_map/all_gather | solution.py:455
  59.0 20.3 %all-to-all-start.4 = ((bf16[8,256,128]{2,1,0:T(8,128)(2,1)}), bf16[8,256,128]{2,1,0:T(8,128)(2,1)S(1)}, u32[]{:S(2)}, u32[]{:S(2)}) async-start(bf16[8,256,128]{2,1,0:T(8,128)(2,1)} %shard_map.67), calls=%async_computation.4 | async-start | bytes 1048576 | tf_op jit(solution)/shard_map/all_to_all | solution.py:437
  62.7 1.9 %collective-permute-start = (bf16[512,512]{1,0:T(8,128)(2,1)S(1)}, bf16[512,512]{1,0:T(8,128)(2,1)S(1)}, u32[]{:S(2)}, u32[]{:S(2)}) collective-permute-start(bf16[512,512]{1,0:T(8,128)(2,1)S(1)} %bitcast.9), channel_id=1, source_target_pairs={{0,1},{1,0},{2,3},{3,2},{4,5},{5,4},{6,7},{7,6},{8,9},{9,8},{10,11... | collective-permute-start | bytes 1572872 | tf_op jit(solution)/shard_map/ppermute | solution.py:433
  79.3 22.9 %all-to-all-start.3 = ((bf16[8,64,512]{2,1,0:T(8,128)(2,1)}), bf16[8,64,512]{2,1,0:T(8,128)(2,1)S(1)}, u32[]{:S(2)}, u32[]{:S(2)}) async-start(bf16[8,64,512]{2,1,0:T(8,128)(2,1)} %get-tuple-element.16), calls=%async_computation.3 | async-start | bytes 1048576 | tf_op jit(solution)/shard_map/all_to_all | solution.py:437
  101.0 14.3 %collective-permute-start.2 = (bf16[512,1024]{1,0:T(8,128)(2,1)}, bf16[512,1024]{1,0:T(8,128)(2,1)}, u32[]{:S(2)}, u32[]{:S(2)}) collective-permute-start(bf16[512,1024]{1,0:T(8,128)(2,1)} %all-gather.2.cloned.1.call-done.out_mine_ref), channel_id=1, source_target_pairs={{0,1},{1,0},{2,3},{3,2},{4,5},{5,4},{6,7},{7,6},{8,9},{9,8},{10,11... | collective-permute-start | bytes 3145736 | tf_op jit(solution)/shard_map/ppermute | solution.py:433
  101.0 14.3 %collective-permute-start.3 = (bf16[8,256,128]{2,1,0:T(8,128)(2,1)S(1)}, bf16[8,256,128]{2,1,0:T(8,128)(2,1)S(1)}, u32[]{:S(2)}, u32[]{:S(2)}) collective-permute-start(bf16[8,256,128]{2,1,0:T(8,128)(2,1)S(1)} %all-to-all-done.4.first_ref), channel_id=1, source_target_pairs={{0,16},{16,0},{1,17},{17,1},{2,18},{18,2},{3,19},{19,3},{4,20},{20... | collective-permute-start | bytes 1572872 | tf_op jit(solution)/shard_map/ppermute | solution.py:433
  102.2 13.2 %collective-permute-start.1 = (bf16[512,512]{1,0:T(8,128)(2,1)S(1)}, bf16[512,512]{1,0:T(8,128)(2,1)S(1)}, u32[]{:S(2)}, u32[]{:S(2)}) collective-permute-start(bf16[512,512]{1,0:T(8,128)(2,1)S(1)} %bitcast.11), channel_id=1, source_target_pairs={{0,1},{1,0},{2,3},{3,2},{4,5},{5,4},{6,7},{7,6},{8,9},{9,8},{10,11... | collective-permute-start | bytes 1572872 | tf_op jit(solution)/shard_map/ppermute | solution.py:433
  115.4 1.2 copy-start
  120.5 2.0 %collective-permute-start.4 = (bf16[512,512]{1,0:T(8,128)(2,1)S(1)}, bf16[512,512]{1,0:T(8,128)(2,1)S(1)}, u32[]{:S(2)}, u32[]{:S(2)}) collective-permute-start(bf16[512,512]{1,0:T(8,128)(2,1)S(1)} %get-tuple-element.19), channel_id=1, source_target_pairs={{0,1},{1,0},{2,3},{3,2},{4,5},{5,4},{6,7},{7,6},{8,9},{9,8},{10,11... | collective-permute-start | bytes 1572872 | tf_op jit(solution)/shard_map/ppermute | solution.py:433
Sparse Core Ops, SparseCore 0:
  47.9 53.0 all-gather.1

commit v3 on v2

--- a/solution.py
+++ b/solution.py
@@ -12,7 +12,7 @@
 BF16 = jnp.bfloat16
 VMEM = pltpu.VMEM
 SLOT = 32
-LIMIT = 48 * 1024 * 1024
+LIMIT = 32 * 1024 * 1024
 
 def layer_norm(matrix):
     average = jnp.mean(matrix, axis=-1, keepdims=True)
@@ -155,43 +155,15 @@
     return pltpu.CompilerParams(vmem_limit_bytes=LIMIT)
 
 
+def cost(micros):
+    return pl.CostEstimate(flops=micros * 10**9, bytes_accessed=1 << 20, transcendentals=0)
+
+
 def struct(shape, dtype=BF16):
     return jax.ShapeDtypeStruct(shape, dtype)
 
 
-def pack_kernel(n, rank_ref, up_ref, down_ref, out_ref, sem):
-    part = rank_ref[2]
-    rows = up_ref.shape[0]
-    wide = up_ref.shape[1] // n
-    keep = wide // 2
-    copies = []
-    for j in range(n):
-        columns = pl.ds(pl.multiple_of(j * wide + part * keep, 128), keep)
-        at = pl.ds(pl.multiple_of(j * wide + part * keep, 128), keep)
-        copies.append((up_ref.at[:, columns], out_ref.at[j, pl.ds(0, rows)]))
-        copies.append((down_ref.at[at], out_ref.at[j, pl.ds(rows, keep)]))
-    started = []
-    for i, (src, dst) in enumerate(copies):
-        copy = pltpu.make_async_copy(src, dst, sem.at[i])
-        copy.start()
-        started.append(copy)
-    for copy in started:
-        copy.wait()
-
-
-def pack(scalars, up, down, n):
-    keep = up.shape[1] // n // 2
-    return pl.pallas_call(
-        functools.partial(pack_kernel, n),
-        in_specs=[sspec(), aspec(), aspec()],
-        out_specs=aspec(),
-        out_shape=struct((n, up.shape[0] + keep, keep)),
-        scratch_shapes=[pltpu.SemaphoreType.DMA((2 * n,))],
-        compiler_params=params(),
-    )(scalars, up, down)
-
-
-def prep_kernel(n, sup, rank_ref, keep_ref, patches_ref, out_ref):
+def prep_kernel(n, sup, rank_ref, keep_ref, patches_ref, qkv_ref, out_ref):
     rank = rank_ref[0]
     first = rank * sup
     keep = keep_ref[...]
@@ -224,14 +196,19 @@
         pos = ((j - start) & (n - 1)) + slot * n
         fine = (pos == fine_pos).astype(F32).astype(BF16)
         mean = (pos == mean_pos).astype(F32).astype(BF16)
-        out_ref[j] = (
+        dealt = (
             jnp.dot(fine, flat, preferred_element_type=F32)
             + jnp.dot(mean, means, preferred_element_type=F32)
         ).astype(BF16)
-
-
-def prep(scalars, keep_col, flat, n, sup):
+        cuts = dealt.shape[1] // 128
+        for c in range(cuts):
+            out_ref[j, c * SLOT : (c + 1) * SLOT] = dealt[:, c * 128 : (c + 1) * 128]
+        out_ref[j, cuts * SLOT :] = qkv_ref[j]
+
+
+def prep(scalars, keep_col, flat, qkv, n, sup):
     width = flat.shape[1] // 2
+    shape = (n, SLOT * width // 128 + qkv.shape[1], 128)
     return pl.pallas_call(
         functools.partial(prep_kernel, n, sup),
         grid_spec=pltpu.PrefetchScalarGridSpec(
@@ -240,16 +217,31 @@
             in_specs=[
                 pl.BlockSpec(keep_col.shape, lambda i, ref: (0, 0)),
                 pl.BlockSpec((flat.shape[0], width), lambda i, ref: (0, ref[1])),
+                pl.BlockSpec(qkv.shape, lambda i, ref: (0, 0, 0)),
             ],
-            out_specs=pl.BlockSpec((n, SLOT, width), lambda i, ref: (0, 0, 0)),
+            out_specs=pl.BlockSpec(shape, lambda i, ref: (0, 0, 0)),
         ),
-        out_shape=struct((n, SLOT, width)),
+        out_shape=struct(shape),
         compiler_params=params(),
-    )(scalars, keep_col, flat)
-
-
-def pick_kernel(n, sup, per_owner, rank_ref, keep_ref, got_ref, out_ref):
-    rank = rank_ref[0]
+    )(scalars, keep_col, flat, qkv)
+
+
+def pick_kernel(n, sup, per_owner, cuts, rank_ref, keep_ref, got_ref, up_ref, down_ref, out_ref, sem):
+    rank, part = rank_ref[0], rank_ref[2]
+    rows = up_ref.shape[0]
+    wide = up_ref.shape[1] // n
+    units = wide // 2
+    top = cuts * per_owner
+    copies = []
+    for j in range(n):
+        at = pl.ds(pl.multiple_of(j * wide + part * units, 128), units)
+        copies.append((up_ref.at[:, at], out_ref.at[j, pl.ds(top, rows)]))
+        copies.append((down_ref.at[at], out_ref.at[j, pl.ds(top + rows, units)]))
+    started = []
+    for i, (src, dst) in enumerate(copies):
+        copy = pltpu.make_async_copy(src, dst, sem.at[i])
+        copy.start()
+        started.append(copy)
     keep = keep_ref[...]
     count = keep.shape[0]
     lanes = n * SLOT
@@ -265,20 +257,28 @@
     row = jnp.where(token < stop, token >> (n.bit_length() - 1), -1)
     own = lax.broadcasted_iota(jnp.int32, (per_owner, lanes), 0)
     choose = (own == row).astype(F32).astype(BF16)
-    stacked = got_ref[...].reshape(lanes, got_ref.shape[2])
-    owned = jnp.dot(choose, stacked, preferred_element_type=F32).astype(BF16)
-    for j in range(n):
-        out_ref[j] = owned
-
-
-def pick(scalars, keep_col, got, n, sup, per_owner):
+    for c in range(cuts):
+        stacked = jnp.concatenate(
+            [got_ref[j, c * SLOT : (c + 1) * SLOT] for j in range(n)], axis=0
+        )
+        owned = jnp.dot(choose, stacked, preferred_element_type=F32).astype(BF16)
+        for j in range(n):
+            out_ref[j, c * per_owner : (c + 1) * per_owner] = owned
+    for copy in started:
+        copy.wait()
+
+
+def pick(scalars, keep_col, got, up, down, head_rows, n, sup, per_owner):
+    cuts = (got.shape[1] - head_rows) // SLOT
+    rows = cuts * per_owner + up.shape[0] + up.shape[1] // n // 2
     return pl.pallas_call(
-        functools.partial(pick_kernel, n, sup, per_owner),
-        in_specs=[sspec(), vspec(), vspec()],
+        functools.partial(pick_kernel, n, sup, per_owner, cuts),
+        in_specs=[sspec(), vspec(), vspec(), aspec(), aspec()],
         out_specs=vspec(),
-        out_shape=struct((n, per_owner, got.shape[2])),
+        out_shape=struct((n, rows, 128)),
+        scratch_shapes=[pltpu.SemaphoreType.DMA((2 * n,))],
         compiler_params=params(),
-    )(scalars, keep_col, got)
+    )(scalars, keep_col, got, up, down)
 
 
 def norm_rows(x):
@@ -287,14 +287,20 @@
     return (x - average) * lax.rsqrt(power - average * average + 1e-06)
 
 
-def attend_kernel(n, rank_ref, mine_ref, other_ref, got_ref, tokens_ref, out_ref, weight_ref):
+def attend_kernel(n, part, rank_ref, mine_ref, other_ref, got_ref, tokens_ref, out_ref, weight_ref):
     half = rank_ref[1]
-    rows, width = mine_ref.shape
+    cuts = other_ref.shape[1] // part
+    width = cuts * 128
     depth = got_ref.shape[2]
-    tokens_ref[:, pl.ds(pl.multiple_of(half * width, width), width)] = mine_ref[...]
-    tokens_ref[:, pl.ds(pl.multiple_of((1 - half) * width, width), width)] = other_ref[...]
     for j in range(n):
-        weight_ref[:, j * depth : (j + 1) * depth] = got_ref[j]
+        rows = slice(j * part, (j + 1) * part)
+        for c in range(cuts):
+            cut = slice(c * part, (c + 1) * part)
+            at = pl.ds(pl.multiple_of(half * width + c * 128, 128), 128)
+            tokens_ref[rows, at] = mine_ref[j, cut]
+            at = pl.ds(pl.multiple_of((1 - half) * width + c * 128, 128), 128)
+            tokens_ref[rows, at] = other_ref[j, cut]
+        weight_ref[:, j * depth : (j + 1) * depth] = got_ref[j, got_ref.shape[1] - weight_ref.shape[0] :]
     normed = norm_rows(tokens_ref[...].astype(F32)).astype(BF16)
     projected = lax.dot_general(
         normed, weight_ref[...], (((1,), (1,)), ((), ())), preferred_element_type=F32
@@ -315,17 +321,19 @@
         out_ref[j] = attended
 
 
-def attend_fast(scalars, mine, other, weights, n):
-    rows, width = mine.shape
-    size = weights.shape[1] // 3
+def attend_fast(scalars, mine, other, got, head_rows, per_owner, n):
+    length = n * per_owner
+    depth = other.shape[1] // per_owner * 256
+    size = head_rows // 3
     return pl.pallas_call(
-        functools.partial(attend_kernel, n),
+        functools.partial(attend_kernel, n, per_owner),
         in_specs=[sspec()] + [vspec()] * 3,
         out_specs=[vspec()] * 2,
-        out_shape=[struct((rows, 2 * width)), struct((n, size, rows))],
-        scratch_shapes=[VMEM((weights.shape[1], n * weights.shape[2]), BF16)],
+        out_shape=[struct((length, depth)), struct((n, size, length))],
+        scratch_shapes=[VMEM((head_rows, n * 128), BF16)],
         compiler_params=params(),
-    )(scalars, mine, other, weights)
+        cost_estimate=cost(30),
+    )(scalars, mine, other, got)
 
 
 def mlp_kernel(
@@ -344,6 +352,7 @@
     up_ref,
     down_ref,
     row_ref,
+    whole_ref,
 ):
     rank, half = rank_ref[0], rank_ref[1]
     block = up_ref.shape[0] // n
@@ -353,11 +362,15 @@
             units = pl.ds(c * unit, unit)
             up_ref[j * block : (j + 1) * block, units] = got_ref[j, :block]
             down_ref[units, j * 128 : (j + 1) * 128] = got_ref[j, block:]
+    for j in range(n):
+        at = pl.ds(pl.multiple_of((rank ^ j) * 128, 128), 128)
+        whole_ref[0, :, at] = out_mine_ref[j]
+        whole_ref[1, :, at] = out_other_ref[j]
     dims = (((0,), (0,)), ((), ()))
     row_ref[...] = (
         tokens_ref[...].astype(F32)
-        + lax.dot_general(mine_ref[...], out_mine_ref[...], dims, preferred_element_type=F32)
-        + lax.dot_general(other_ref[...], out_other_ref[...], dims, preferred_element_type=F32)
+        + lax.dot_general(mine_ref[...], whole_ref[0], dims, preferred_element_type=F32)
+        + lax.dot_general(other_ref[...], whole_ref[1], dims, preferred_element_type=F32)
     )
     part = residual_ref.shape[0]
     width = residual_ref.shape[1]
@@ -388,6 +401,7 @@
             VMEM((depth, wide), BF16),
             VMEM((wide, depth), BF16),
             VMEM((length, depth), F32),
+            VMEM((2, out_mine.shape[1], depth), BF16),
         ],
         compiler_params=params(),
     )(scalars, tokens, mine, other, out_mine, out_other, first, second)
@@ -450,20 +464,27 @@
     length = sup * n * 8 // 5
     per_owner = length // n
     half_width = depth // 2
+    head_rows = qkv_weight.shape[2]
     keep_col = keep_list.reshape(-1, 1)
     flat = patches.reshape(4 * sup, depth)
-    out_mine = lax.all_gather(out_weight, "seq", axis=1, tiled=True)
+    slots = prep(scalars, keep_col, flat, qkv_weight.transpose(1, 2, 0), n, sup)
+    dealt = exchange(slots)
+    across = swap(after(out_weight, slots), "seq", n // 2)
+    dealt, across = lax.optimization_barrier((dealt, across))
+    sent = pick(scalars, keep_col, dealt, up_weight, down_weight, head_rows, n, sup, per_owner)
+    pair = jnp.stack([out_weight, across])
+    pair = after(pair, sent)
+    got = exchange(sent)
+    quads = [pair] + [swap(pair, "seq", j) for j in range(1, n // 2)]
+    got, *quads = lax.optimization_barrier((got, *quads))
+    top = half_width // 128 * per_owner
+    pieces = got[:, :top]
+    pieces_other = swap(pieces, "head", 1)
+    first = got[:, top:]
+    second = swap(first, "groups", 1)
+    tokens, attended = attend_fast(scalars, pieces, pieces_other, dealt, head_rows, per_owner, n)
+    out_mine = jnp.stack([quad[k] for k in range(2) for quad in quads])
     out_other = swap(out_mine, "head", 1)
-    slots = prep(scalars, keep_col, flat, n, sup)
-    packed = pack(scalars, up_weight, down_weight, n)
-    dealt = exchange(slots)
-    qkv_got = exchange(after(qkv_weight.transpose(1, 2, 0), slots))
-    owned = pick(scalars, keep_col, dealt, n, sup, per_owner)
-    pieces = exchange(owned).reshape(length, half_width)
-    first = exchange(after(packed, owned))
-    pieces_other = swap(pieces, "head", 1)
-    second = swap(first, "groups", 1)
-    tokens, attended = attend_fast(scalars, pieces, pieces_other, qkv_got, n)
     gathered = exchange(attended).reshape(half_width, length)
     gathered_other = swap(gathered, "head", 1)
     residual, keep, send = mlp(

time: 149 us -> 127 us (0.85)
  waiting for transfers between devices: 77.6 us -> 64.2 us
  between operations: 13.5 us -> 0.15 us
  starting transfers between devices: 23 us -> 25.2 us
  blocking collectives: 17.5 us -> 19.4 us
    ppermute x5 -> x9, waiting for transfers between devices: 16.8 us -> 51.9 us  [swap(): return lax.ppermute(value, axis, [(i, i ^ j) for i in range(n)])]
    all_to_all x5 -> x3, waiting for transfers between devices: 41.9 us -> 12.2 us  [exchange(): return lax.all_to_all(value, 'seq', split_axis=0, concat_axis=0, tiled=True)]
    all_gather x1 -> x0, waiting for transfers between devices: 18.3 us -> none  [local_fast(): out_mine = lax.all_gather(out_weight, 'seq', axis=1, tiled=True)]
    ppermute x5 -> x9, starting transfers between devices: 1.3 us -> 8.45 us  [swap(): return lax.ppermute(value, axis, [(i, i ^ j) for i in range(n)])]
    all_to_all x5 -> x3, starting transfers between devices: 21.6 us -> 16.7 us  [exchange(): return lax.all_to_all(value, 'seq', split_axis=0, concat_axis=0, tiled=True)]
    all_to_all x1, blocking collectives: 17.5 us -> 19.4 us  [exchange(): return lax.all_to_all(value, 'seq', split_axis=0, concat_axis=0, tiled=True)]
    pallas_call x3 -> x2, Pallas kernels: 6.41 us -> 5.06 us  [the longest x1 2.65 us: attend_fast(): pl.pallas_call(functools.partial(attend_kernel, n, per_owner), in_specs=[...]
  transfers between devices with their start and end apart: 11 -> 12, of which waited for: 9 -> 8; matrix products, arithmetic and copies ran while one was open for 0% -> 1% of each run, Pallas kernels for 4% -> 0%
where the time goes in v3:
time: 127 us
  waiting for transfers between devices  64.2 us (51%)
  starting transfers between devices  25.2 us (20%)
  blocking collectives  19.4 us (15%)
  Pallas kernels  13.6 us (11%)
  local copies, waits for them, and re-layouts  4.26 us (3%)
    ppermute x9, waiting for transfers between devices, swap(): return lax.ppermute(value, axis, [(i, i ^ j) for i in range(n)])  51.9 us
    all_to_all x1, blocking collectives, exchange(): return lax.all_to_all(value, 'seq', split_axis=0, concat_axis=0, tiled=True)  19.4 us
    all_to_all x3, starting transfers between devices, exchange(): return lax.all_to_all(value, 'seq', split_axis=0, concat_axis=0, tiled=True)  16.7 us
    all_to_all x3, waiting for transfers between devices, exchange(): return lax.all_to_all(value, 'seq', split_axis=0, concat_axis=0, tiled=True)  12.2 us
    ppermute x9, starting transfers between devices, swap(): return lax.ppermute(value, axis, [(i, i ^ j) for i in range(n)])  8.45 us
    pallas_call x1, Pallas kernels, mlp(): pl.pallas_call(functools.partial(mlp_kernel, n), in_specs=[sspec()] + [vs...  4.69 us
    pallas_call x1, Pallas kernels, attend_fast(): pl.pallas_call(functools.partial(attend_kernel, n, per_owner), in_specs=[...  2.65 us
  transfers between devices with their start and end apart: 12, of which 8 were waited for; matrix products, arithmetic and copies ran while one was open for 1% of the time, Pallas kernels for 0%

profile of v3, /device:TPU:0, one launch (start us, length us, event | category | flops | bytes accessed | tf_op | source)
XLA Modules:
  0.0 126.8 jit_solution(14513319050370352276)
XLA Ops:
  0.0 0.8 copy.8.keep_ref
  0.8 1.0 reshape.16.patches_ref
  1.9 0.1 pad_add_fusion.rank_ref
  1.9 2.0 %shard_map.64 = bf16[8,320,128]{2,1,0:T(8,128)(2,1)} custom-call(s32[3]{0:T(128)S(1)} %pad_add_fusion.rank_ref, s32[64,1]{1,0:T(8,128)S(1)} %copy.8.keep_ref, bf16[160,1024]{1,0:T(8,128)(2,1)S(1)} %reshape.16.patches_ref, bf16[8,192,128]{2,1,0:T(8,128)(2,1)S(1)} %bitcast.13), custom_call_target="tpu_custom_call" | custom-call | tf_op jit(solution)/shard_map/pallas_call | solution.py:212
  3.9 7.4 %all-to-all-start = ((bf16[8,320,128]{2,1,0:T(8,128)(2,1)}), bf16[8,320,128]{2,1,0:T(8,128)(2,1)S(1)}, u32[]{:S(2)}, u32[]{:S(2)}) async-start(bf16[8,320,128]{2,1,0:T(8,128)(2,1)} %shard_map.64), calls=%async_computation | async-start | bytes 1310720 | tf_op jit(solution)/shard_map/all_to_all | solution.py:451
  11.4 2.9 %collective-permute-start = (bf16[512,128]{1,0:T(8,128)(2,1)S(1)}, bf16[512,128]{1,0:T(8,128)(2,1)S(1)}, u32[]{:S(2)}, u32[]{:S(2)}) collective-permute-start(bf16[512,128]{1,0:T(8,128)(2,1)S(1)} %copy-done.5), channel_id=1, source_target_pairs={{0,8},{2,10},{4,12},{6,14},{8,0},{10,2},{12,4},{14,6},{1,9},{3,11}... | collective-permute-start | bytes 393224 | tf_op jit(solution)/shard_map/ppermute | solution.py:447
  14.3 20.0 %collective-permute-done = bf16[512,128]{1,0:T(8,128)(2,1)S(1)} collective-permute-done((bf16[512,128]{1,0:T(8,128)(2,1)S(1)}, bf16[512,128]{1,0:T(8,128)(2,1)S(1)}, u32[]{:S(2)}, u32[]{:S(2)}) %collective-permute-start) | collective-permute-done | bytes 131104 | tf_op jit(solution)/shard_map/ppermute | solution.py:447
  34.3 2.4 %shard_map.65 = bf16[8,512,128]{2,1,0:T(8,128)(2,1)} custom-call(s32[3]{0:T(128)S(1)} %pad_add_fusion.rank_ref, s32[64,1]{1,0:T(8,128)S(1)} %copy.8.keep_ref, bf16[8,320,128]{2,1,0:T(8,128)(2,1)S(1)} %all-to-all-done.got_ref, bf16[128,2048]{1,0:T(8,128)(2,1)S(1)} %copy-done.1, bf16[2048,128]{1,0:T(8,128)(2,1)S(1)} %copy-done.2), custom_call_target="tpu_custom_call" | custom-call | tf_op jit(solution)/shard_map/pallas_call | solution.py:274
  36.7 3.6 %all-to-all-start.1 = ((bf16[8,512,128]{2,1,0:T(8,128)(2,1)}), bf16[8,512,128]{2,1,0:T(8,128)(2,1)S(1)}, u32[]{:S(2)}, u32[]{:S(2)}) async-start(bf16[8,512,128]{2,1,0:T(8,128)(2,1)} %shard_map.65), calls=%async_computation.1 | async-start | bytes 2097152 | tf_op jit(solution)/shard_map/all_to_all | solution.py:451
  40.4 3.0 %collective-permute-start.3 = (bf16[2,512,128]{2,1,0:T(8,128)(2,1)S(1)}, bf16[2,512,128]{2,1,0:T(8,128)(2,1)S(1)}, u32[]{:S(2)}, u32[]{:S(2)}) collective-permute-start(bf16[2,512,128]{2,1,0:T(8,128)(2,1)S(1)} %pad_maximum_fusion), channel_id=1, source_target_pairs={{0,6},{2,4},{4,2},{6,0},{8,14},{10,12},{12,10},{14,8},{1,7},{3,5},... | collective-permute-start | bytes 786440 | tf_op jit(solution)/shard_map/ppermute | solution.py:447
  43.4 0.6 collective-permute-start.2
  43.9 0.1 collective-permute-start.1
  44.0 23.3 %collective-permute-done.3 = bf16[2,512,128]{2,1,0:T(8,128)(2,1)S(1)} collective-permute-done((bf16[2,512,128]{2,1,0:T(8,128)(2,1)S(1)}, bf16[2,512,128]{2,1,0:T(8,128)(2,1)S(1)}, u32[]{:S(2)}, u32[]{:S(2)}) %collective-permute-start.3) | collective-permute-done | bytes 262176 | tf_op jit(solution)/shard_map/ppermute | solution.py:447
  67.3 3.7 %collective-permute-done.2 = bf16[2,512,128]{2,1,0:T(8,128)(2,1)S(1)} collective-permute-done((bf16[2,512,128]{2,1,0:T(8,128)(2,1)S(1)}, bf16[2,512,128]{2,1,0:T(8,128)(2,1)S(1)}, u32[]{:S(2)}, u32[]{:S(2)}) %collective-permute-start.2) | collective-permute-done | bytes 262176 | tf_op jit(solution)/shard_map/ppermute | solution.py:447
  71.0 0.1 fusion
  71.2 0.5 copy-done.4
  71.8 1.3 collective-permute-done.4.other_ref
  73.1 2.7 %shard_map.66 = (bf16[512,1024]{1,0:T(8,128)(2,1)S(1)}, bf16[8,64,512]{2,1,0:T(8,128)(2,1)S(1)}) custom-call(s32[3]{0:T(128)S(1)} %pad_add_fusion.rank_ref, bf16[8,256,128]{2,1,0:T(8,128)(2,1)S(1)} %get-tuple-element.38.mine_ref, bf16[8,256,128]{2,1,0:T(8,128)(2,1)S(1)} %collective-permute-done.4.other_ref, bf16[8,320,128]{2,1,0:T(8,128)(2,1)S(1)} %all-to-all-done.got_ref), custom_call_target="tpu_custom_call" | custom-call | flops 30000001024 | bytes 1048576 | tf_op jit(solution)/shard_map/pallas_call | solution.py:328
  75.8 0.8 copy-done
  76.5 5.7 %all-to-all-start.2 = ((bf16[8,64,512]{2,1,0:T(8,128)(2,1)}), bf16[8,64,512]{2,1,0:T(8,128)(2,1)S(1)}, u32[]{:S(2)}, u32[]{:S(2)}) async-start(bf16[8,64,512]{2,1,0:T(8,128)(2,1)} %copy-done), calls=%async_computation.2 | async-start | bytes 1048576 | tf_op jit(solution)/shard_map/all_to_all | solution.py:451
  82.2 0.9 slice_dynamic-update-slice_fusion.1
  83.1 0.1 collective-permute-start.6
  83.2 1.6 %collective-permute-start.7 = (bf16[8,256,128]{2,1,0:T(8,128)(2,1)S(1)}, bf16[8,256,128]{2,1,0:T(8,128)(2,1)}, u32[]{:S(2)}, u32[]{:S(2)}) collective-permute-start(bf16[8,256,128]{2,1,0:T(8,128)(2,1)S(1)} %get-tuple-element.37.first_ref), channel_id=1, source_target_pairs={{0,16},{16,0},{1,17},{17,1},{2,18},{18,2},{3,19},{19,3},{4,20},{20... | collective-permute-start | bytes 1572872 | tf_op jit(solution)/shard_map/ppermute | solution.py:447
  84.8 12.2 %all-to-all-done.2 = bf16[8,64,512]{2,1,0:T(8,128)(2,1)S(1)} async-done(((bf16[8,64,512]{2,1,0:T(8,128)(2,1)}), bf16[8,64,512]{2,1,0:T(8,128)(2,1)S(1)}, u32[]{:S(2)}, u32[]{:S(2)}) %all-to-all-start.2) | async-done | bytes 524320 | tf_op jit(solution)/shard_map/all_to_all | solution.py:451
  97.0 0.7 collective-permute-done.7.second_ref
  97.7 1.2 collective-permute-done.5.other_ref
  98.9 4.7 %shard_map.67 = (f32[64,512]{1,0:T(8,128)S(1)}, f32[512,512]{1,0:T(8,128)S(1)}, bf16[512,512]{1,0:T(8,128)(2,1)S(1)}) custom-call(s32[3]{0:T(128)S(1)} %pad_add_fusion.rank_ref, bf16[512,1024]{1,0:T(8,128)(2,1)S(1)} %get-tuple-element.26.tokens_ref, bf16[512,512]{1,0:T(8,128)(2,1)S(1)} %bitcast.11, bf16[512,512]{1,0:T(8,128)(2,1)S(1)} %collective-permute-done.5.other_ref, ...), custom_call_target="tpu_custom_call" | custom-call | tf_op jit(solution)/shard_map/pallas_call | solution.py:391
  103.6 0.2 collective-permute-start.8
  103.8 1.8 %collective-permute-done.8.got_ref = bf16[512,512]{1,0:T(8,128)(2,1)S(1)} collective-permute-done((bf16[512,512]{1,0:T(8,128)(2,1)S(1)}, bf16[512,512]{1,0:T(8,128)(2,1)S(1)}, u32[]{:S(2)}, u32[]{:S(2)}) %collective-permute-start.8) | collective-permute-done | bytes 524320 | tf_op jit(solution)/shard_map/ppermute | solution.py:447
  105.6 0.6 shard_map.68
  106.2 19.4 %all_to_all.20.terms_ref = bf16[8,64,512]{2,1,0:T(8,128)(2,1)S(1)} all-to-all(bf16[8,64,512]{2,1,0:T(8,128)(2,1)S(1)} %bitcast.12), channel_id=1, replica_groups=mesh['groups'=2,'seq'=8,'head'=2] {'seq'}, dimensions={0} | all-to-all | bytes 1048576 | tf_op jit(solution)/shard_map/all_to_all | solution.py:451
  125.6 1.2 shard_map.69
  (24 shorter events, 0.3 us)
Async XLA Ops:
  0.0 1.9 %copy-start.3 = (bf16[128,8,192]{0,2,1:T(8,128)(2,1)S(1)}, bf16[128,8,192]{0,2,1:T(8,128)(2,1)}, u32[]{:S(2)}) copy-start(bf16[128,8,192]{0,2,1:T(8,128)(2,1)} %param.8) | copy-start | bytes 1179652
  3.9 7.4 %copy-start.5 = (bf16[512,128]{1,0:T(8,128)(2,1)S(1)}, bf16[512,128]{1,0:T(8,128)(2,1)}, u32[]{:S(2)}) copy-start(bf16[512,128]{1,0:T(8,128)(2,1)} %param.9) | copy-start | bytes 393220
  3.9 30.3 %copy-start.1 = (bf16[128,2048]{1,0:T(8,128)(2,1)S(1)}, bf16[128,2048]{1,0:T(8,128)(2,1)}, u32[]{:S(2)}) copy-start(bf16[128,2048]{1,0:T(8,128)(2,1)} %up_ref.1) | copy-start | bytes 1572868
  3.9 30.3 %copy-start.2 = (bf16[2048,128]{1,0:T(8,128)(2,1)S(1)}, bf16[2048,128]{1,0:T(8,128)(2,1)}, u32[]{:S(2)}) copy-start(bf16[2048,128]{1,0:T(8,128)(2,1)} %down_ref.1) | copy-start | bytes 1572868
  3.9 30.3 %all-to-all-start = ((bf16[8,320,128]{2,1,0:T(8,128)(2,1)}), bf16[8,320,128]{2,1,0:T(8,128)(2,1)S(1)}, u32[]{:S(2)}, u32[]{:S(2)}) async-start(bf16[8,320,128]{2,1,0:T(8,128)(2,1)} %shard_map.64), calls=%async_computation | async-start | bytes 1310720 | tf_op jit(solution)/shard_map/all_to_all | solution.py:451
  11.4 22.9 %collective-permute-start = (bf16[512,128]{1,0:T(8,128)(2,1)S(1)}, bf16[512,128]{1,0:T(8,128)(2,1)S(1)}, u32[]{:S(2)}, u32[]{:S(2)}) collective-permute-start(bf16[512,128]{1,0:T(8,128)(2,1)S(1)} %copy-done.5), channel_id=1, source_target_pairs={{0,8},{2,10},{4,12},{6,14},{8,0},{10,2},{12,4},{14,6},{1,9},{3,11}... | collective-permute-start | bytes 393224 | tf_op jit(solution)/shard_map/ppermute | solution.py:447
  36.7 34.3 %all-to-all-start.1 = ((bf16[8,512,128]{2,1,0:T(8,128)(2,1)}), bf16[8,512,128]{2,1,0:T(8,128)(2,1)S(1)}, u32[]{:S(2)}, u32[]{:S(2)}) async-start(bf16[8,512,128]{2,1,0:T(8,128)(2,1)} %shard_map.65), calls=%async_computation.1 | async-start | bytes 2097152 | tf_op jit(solution)/shard_map/all_to_all | solution.py:451
  40.4 26.9 %collective-permute-start.3 = (bf16[2,512,128]{2,1,0:T(8,128)(2,1)S(1)}, bf16[2,512,128]{2,1,0:T(8,128)(2,1)S(1)}, u32[]{:S(2)}, u32[]{:S(2)}) collective-permute-start(bf16[2,512,128]{2,1,0:T(8,128)(2,1)S(1)} %pad_maximum_fusion), channel_id=1, source_target_pairs={{0,6},{2,4},{4,2},{6,0},{8,14},{10,12},{12,10},{14,8},{1,7},{3,5},... | collective-permute-start | bytes 786440 | tf_op jit(solution)/shard_map/ppermute | solution.py:447
  43.4 27.7 %collective-permute-start.2 = (bf16[2,512,128]{2,1,0:T(8,128)(2,1)S(1)}, bf16[2,512,128]{2,1,0:T(8,128)(2,1)S(1)}, u32[]{:S(2)}, u32[]{:S(2)}) collective-permute-start(bf16[2,512,128]{2,1,0:T(8,128)(2,1)S(1)} %pad_maximum_fusion), channel_id=1, source_target_pairs={{0,4},{2,6},{4,0},{6,2},{8,12},{10,14},{12,8},{14,10},{1,5},{3,7},... | collective-permute-start | bytes 786440 | tf_op jit(solution)/shard_map/ppermute | solution.py:447
  43.9 27.1 %collective-permute-start.1 = (bf16[2,512,128]{2,1,0:T(8,128)(2,1)S(1)}, bf16[2,512,128]{2,1,0:T(8,128)(2,1)S(1)}, u32[]{:S(2)}, u32[]{:S(2)}) collective-permute-start(bf16[2,512,128]{2,1,0:T(8,128)(2,1)S(1)} %pad_maximum_fusion), channel_id=1, source_target_pairs={{0,2},{2,0},{4,6},{6,4},{8,10},{10,8},{12,14},{14,12},{1,3},{3,1},... | collective-permute-start | bytes 786440 | tf_op jit(solution)/shard_map/ppermute | solution.py:447
  71.0 0.7 copy-start.4
  71.1 2.0 %collective-permute-start.4 = (bf16[8,256,128]{2,1,0:T(8,128)(2,1)S(1)}, bf16[8,256,128]{2,1,0:T(8,128)(2,1)S(1)}, u32[]{:S(2)}, u32[]{:S(2)}) collective-permute-start(bf16[8,256,128]{2,1,0:T(8,128)(2,1)S(1)} %get-tuple-element.38.mine_ref), channel_id=1, source_target_pairs={{0,1},{1,0},{2,3},{3,2},{4,5},{5,4},{6,7},{7,6},{8,9},{9,8},{10,11... | collective-permute-start | bytes 1572872 | tf_op jit(solution)/shard_map/ppermute | solution.py:447
  75.7 0.8 copy-start
  76.5 20.4 %all-to-all-start.2 = ((bf16[8,64,512]{2,1,0:T(8,128)(2,1)}), bf16[8,64,512]{2,1,0:T(8,128)(2,1)S(1)}, u32[]{:S(2)}, u32[]{:S(2)}) async-start(bf16[8,64,512]{2,1,0:T(8,128)(2,1)} %copy-done), calls=%async_computation.2 | async-start | bytes 1048576 | tf_op jit(solution)/shard_map/all_to_all | solution.py:451
  83.1 14.5 %collective-permute-start.6 = (bf16[8,512,128]{2,1,0:T(8,128)(2,1)S(1)}, bf16[8,512,128]{2,1,0:T(8,128)(2,1)}, u32[]{:S(2)}, u32[]{:S(2)}) collective-permute-start(bf16[8,512,128]{2,1,0:T(8,128)(2,1)S(1)} %slice_dynamic-update-slice_fusion.out_mine_ref), channel_id=1, source_target_pairs={{0,1},{1,0},{2,3},{3,2},{4,5},{5,4},{6,7},{7,6},{8,9},{9,8},{10,11... | collective-permute-start | bytes 3145736 | tf_op jit(solution)/shard_map/ppermute | solution.py:447
  83.2 14.4 %collective-permute-start.7 = (bf16[8,256,128]{2,1,0:T(8,128)(2,1)S(1)}, bf16[8,256,128]{2,1,0:T(8,128)(2,1)}, u32[]{:S(2)}, u32[]{:S(2)}) collective-permute-start(bf16[8,256,128]{2,1,0:T(8,128)(2,1)S(1)} %get-tuple-element.37.first_ref), channel_id=1, source_target_pairs={{0,16},{16,0},{1,17},{17,1},{2,18},{18,2},{3,19},{19,3},{4,20},{20... | collective-permute-start | bytes 1572872 | tf_op jit(solution)/shard_map/ppermute | solution.py:447
  97.0 1.9 %collective-permute-start.5 = (bf16[512,512]{1,0:T(8,128)(2,1)S(1)}, bf16[512,512]{1,0:T(8,128)(2,1)S(1)}, u32[]{:S(2)}, u32[]{:S(2)}) collective-permute-start(bf16[512,512]{1,0:T(8,128)(2,1)S(1)} %bitcast.10), channel_id=1, source_target_pairs={{0,1},{1,0},{2,3},{3,2},{4,5},{5,4},{6,7},{7,6},{8,9},{9,8},{10,11... | collective-permute-start | bytes 1572872 | tf_op jit(solution)/shard_map/ppermute | solution.py:447
  103.6 2.0 %collective-permute-start.8 = (bf16[512,512]{1,0:T(8,128)(2,1)S(1)}, bf16[512,512]{1,0:T(8,128)(2,1)S(1)}, u32[]{:S(2)}, u32[]{:S(2)}) collective-permute-start(bf16[512,512]{1,0:T(8,128)(2,1)S(1)} %get-tuple-element.33), channel_id=1, source_target_pairs={{0,1},{1,0},{2,3},{3,2},{4,5},{5,4},{6,7},{7,6},{8,9},{9,8},{10,11... | collective-permute-start | bytes 1572872 | tf_op jit(solution)/shard_map/ppermute | solution.py:447

commit v4 on v3

--- a/solution.py
+++ b/solution.py
@@ -163,7 +163,7 @@
     return jax.ShapeDtypeStruct(shape, dtype)
 
 
-def prep_kernel(n, sup, rank_ref, keep_ref, patches_ref, qkv_ref, out_ref):
+def prep_kernel(n, sup, rank_ref, keep_ref, patches_ref, out_ref):
     rank = rank_ref[0]
     first = rank * sup
     keep = keep_ref[...]
@@ -203,12 +203,11 @@
         cuts = dealt.shape[1] // 128
         for c in range(cuts):
             out_ref[j, c * SLOT : (c + 1) * SLOT] = dealt[:, c * 128 : (c + 1) * 128]
-        out_ref[j, cuts * SLOT :] = qkv_ref[j]
-
-
-def prep(scalars, keep_col, flat, qkv, n, sup):
+
+
+def prep(scalars, keep_col, flat, n, sup):
     width = flat.shape[1] // 2
-    shape = (n, SLOT * width // 128 + qkv.shape[1], 128)
+    shape = (n, SLOT * width // 128, 128)
     return pl.pallas_call(
         functools.partial(prep_kernel, n, sup),
         grid_spec=pltpu.PrefetchScalarGridSpec(
@@ -217,31 +216,17 @@
             in_specs=[
                 pl.BlockSpec(keep_col.shape, lambda i, ref: (0, 0)),
                 pl.BlockSpec((flat.shape[0], width), lambda i, ref: (0, ref[1])),
-                pl.BlockSpec(qkv.shape, lambda i, ref: (0, 0, 0)),
             ],
             out_specs=pl.BlockSpec(shape, lambda i, ref: (0, 0, 0)),
         ),
         out_shape=struct(shape),
         compiler_params=params(),
-    )(scalars, keep_col, flat, qkv)
-
-
-def pick_kernel(n, sup, per_owner, cuts, rank_ref, keep_ref, got_ref, up_ref, down_ref, out_ref, sem):
-    rank, part = rank_ref[0], rank_ref[2]
-    rows = up_ref.shape[0]
-    wide = up_ref.shape[1] // n
-    units = wide // 2
-    top = cuts * per_owner
-    copies = []
-    for j in range(n):
-        at = pl.ds(pl.multiple_of(j * wide + part * units, 128), units)
-        copies.append((up_ref.at[:, at], out_ref.at[j, pl.ds(top, rows)]))
-        copies.append((down_ref.at[at], out_ref.at[j, pl.ds(top + rows, units)]))
-    started = []
-    for i, (src, dst) in enumerate(copies):
-        copy = pltpu.make_async_copy(src, dst, sem.at[i])
-        copy.start()
-        started.append(copy)
+    )(scalars, keep_col, flat)
+
+
+def pick_kernel(n, sup, per_owner, rank_ref, keep_ref, got_ref, out_ref):
+    rank = rank_ref[0]
+    cuts = got_ref.shape[1] // SLOT
     keep = keep_ref[...]
     count = keep.shape[0]
     lanes = n * SLOT
@@ -262,23 +247,75 @@
             [got_ref[j, c * SLOT : (c + 1) * SLOT] for j in range(n)], axis=0
         )
         owned = jnp.dot(choose, stacked, preferred_element_type=F32).astype(BF16)
-        for j in range(n):
-            out_ref[j, c * per_owner : (c + 1) * per_owner] = owned
+        out_ref[c * per_owner : (c + 1) * per_owner] = owned
+
+
+def pick(scalars, keep_col, got, n, sup, per_owner):
+    return pl.pallas_call(
+        functools.partial(pick_kernel, n, sup, per_owner),
+        in_specs=[sspec(), vspec(), vspec()],
+        out_specs=vspec(),
+        out_shape=struct((got.shape[1] // SLOT * per_owner, 128)),
+        compiler_params=params(),
+    )(scalars, keep_col, got)
+
+
+def pack_kernel(n, rank_ref, up_ref, down_ref, home_ref, away_ref, sem):
+    side, part = rank_ref[0] // (n // 2), rank_ref[2]
+    rows = up_ref.shape[0]
+    wide = up_ref.shape[1] // n
+    units = wide // 2
+    copies = []
+    for k, out_ref in enumerate((home_ref, away_ref)):
+        for d in range(n // 2):
+            dest = (side ^ k) * (n // 2) + d
+            at = pl.ds(pl.multiple_of(dest * wide + part * units, 128), units)
+            copies.append((up_ref.at[:, at], out_ref.at[d, pl.ds(0, rows)]))
+            copies.append((down_ref.at[at], out_ref.at[d, pl.ds(rows, units)]))
+    started = []
+    for i, (src, dst) in enumerate(copies):
+        copy = pltpu.make_async_copy(src, dst, sem.at[i])
+        copy.start()
+        started.append(copy)
     for copy in started:
         copy.wait()
 
 
-def pick(scalars, keep_col, got, up, down, head_rows, n, sup, per_owner):
-    cuts = (got.shape[1] - head_rows) // SLOT
-    rows = cuts * per_owner + up.shape[0] + up.shape[1] // n // 2
-    return pl.pallas_call(
-        functools.partial(pick_kernel, n, sup, per_owner, cuts),
-        in_specs=[sspec(), vspec(), vspec(), aspec(), aspec()],
+def pack(scalars, up, down, n):
+    units = up.shape[1] // n // 2
+    shape = struct((n // 2, up.shape[0] + units, units))
+    return pl.pallas_call(
+        functools.partial(pack_kernel, n),
+        in_specs=[sspec(), aspec(), aspec()],
+        out_specs=[aspec()] * 2,
+        out_shape=[shape, shape],
+        scratch_shapes=[pltpu.SemaphoreType.DMA((2 * n,))],
+        compiler_params=params(),
+    )(scalars, up, down)
+
+
+def fan_kernel(owned_ref, across_ref, home_ref, away_ref, out_ref):
+    rows, depth = owned_ref.shape[0], home_ref.shape[1]
+    for d in range(out_ref.shape[0]):
+        out_ref[d, :rows] = owned_ref[...]
+        out_ref[d, rows : 2 * rows] = across_ref[...]
+        out_ref[d, 2 * rows : 2 * rows + depth] = home_ref[d]
+        out_ref[d, 2 * rows + depth :] = away_ref[d]
+
+
+def fan(owned, across, home, away):
+    shape = struct((home.shape[0], 2 * owned.shape[0] + 2 * home.shape[1], 128))
+    return pl.pallas_call(
+        fan_kernel,
+        in_specs=[vspec()] * 4,
         out_specs=vspec(),
-        out_shape=struct((n, rows, 128)),
-        scratch_shapes=[pltpu.SemaphoreType.DMA((2 * n,))],
-        compiler_params=params(),
-    )(scalars, keep_col, got, up, down)
+        out_shape=shape,
+        compiler_params=params(),
+    )(owned, across, home, away)
+
+
+def source_of(rank, n, q, k):
+    return (rank // (n // 2) ^ k) * (n // 2) + q
 
 
 def norm_rows(x):
@@ -287,20 +324,25 @@
     return (x - average) * lax.rsqrt(power - average * average + 1e-06)
 
 
-def attend_kernel(n, part, rank_ref, mine_ref, other_ref, got_ref, tokens_ref, out_ref, weight_ref):
-    half = rank_ref[1]
-    cuts = other_ref.shape[1] // part
+def attend_kernel(n, part, rank_ref, mine_ref, other_ref, tokens_ref, out_ref, weight_ref):
+    rank, half = rank_ref[0], rank_ref[1]
+    rows = other_ref.shape[1] // 2
+    cuts = rows // part
     width = cuts * 128
-    depth = got_ref.shape[2]
-    for j in range(n):
-        rows = slice(j * part, (j + 1) * part)
-        for c in range(cuts):
-            cut = slice(c * part, (c + 1) * part)
-            at = pl.ds(pl.multiple_of(half * width + c * 128, 128), 128)
-            tokens_ref[rows, at] = mine_ref[j, cut]
-            at = pl.ds(pl.multiple_of((1 - half) * width + c * 128, 128), 128)
-            tokens_ref[rows, at] = other_ref[j, cut]
-        weight_ref[:, j * depth : (j + 1) * depth] = got_ref[j, got_ref.shape[1] - weight_ref.shape[0] :]
+    depth = weight_ref.shape[0]
+    for q in range(n // 2):
+        for k in range(2):
+            source = source_of(rank, n, q, k)
+            at = pl.ds(pl.multiple_of(source * part, part), part)
+            for c in range(cuts):
+                cut = slice(k * rows + c * part, k * rows + (c + 1) * part)
+                to = pl.ds(pl.multiple_of(half * width + c * 128, 128), 128)
+                tokens_ref[at, to] = mine_ref[q, cut]
+                to = pl.ds(pl.multiple_of((1 - half) * width + c * 128, 128), 128)
+                tokens_ref[at, to] = other_ref[q, cut]
+            weight_ref[:, pl.ds(pl.multiple_of(source * 128, 128), 128)] = mine_ref[
+                q, 2 * rows + k * depth : 2 * rows + (k + 1) * depth
+            ]
     normed = norm_rows(tokens_ref[...].astype(F32)).astype(BF16)
     projected = lax.dot_general(
         normed, weight_ref[...], (((1,), (1,)), ((), ())), preferred_element_type=F32
@@ -317,23 +359,22 @@
     attended = lax.dot_general(
         values, probs, (((0,), (1,)), ((), ())), preferred_element_type=F32
     ).astype(BF16)
-    for j in range(n):
-        out_ref[j] = attended
-
-
-def attend_fast(scalars, mine, other, got, head_rows, per_owner, n):
+    out_ref[...] = attended
+
+
+def attend_fast(scalars, mine, other, head_rows, per_owner, n):
     length = n * per_owner
-    depth = other.shape[1] // per_owner * 256
+    depth = other.shape[1] // (2 * per_owner) * 256
     size = head_rows // 3
     return pl.pallas_call(
         functools.partial(attend_kernel, n, per_owner),
-        in_specs=[sspec()] + [vspec()] * 3,
+        in_specs=[sspec()] + [vspec()] * 2,
         out_specs=[vspec()] * 2,
-        out_shape=[struct((length, depth)), struct((n, size, length))],
+        out_shape=[struct((length, depth)), struct((size, length))],
         scratch_shapes=[VMEM((head_rows, n * 128), BF16)],
         compiler_params=params(),
         cost_estimate=cost(30),
-    )(scalars, mine, other, got)
+    )(scalars, mine, other)
 
 
 def mlp_kernel(
@@ -342,8 +383,7 @@
     tokens_ref,
     mine_ref,
     other_ref,
-    out_mine_ref,
-    out_other_ref,
+    out_refs,
     first_ref,
     second_ref,
     residual_ref,
@@ -353,24 +393,37 @@
     down_ref,
     row_ref,
     whole_ref,
+    joined_ref,
 ):
-    rank, half = rank_ref[0], rank_ref[1]
+    rank, half, group = rank_ref[0], rank_ref[1], rank_ref[2]
     block = up_ref.shape[0] // n
     unit = first_ref.shape[2]
-    for j in range(n):
-        for c, got_ref in enumerate((first_ref, second_ref)):
-            units = pl.ds(c * unit, unit)
-            up_ref[j * block : (j + 1) * block, units] = got_ref[j, :block]
-            down_ref[units, j * 128 : (j + 1) * 128] = got_ref[j, block:]
-    for j in range(n):
-        at = pl.ds(pl.multiple_of((rank ^ j) * 128, 128), 128)
-        whole_ref[0, :, at] = out_mine_ref[j]
-        whole_ref[1, :, at] = out_other_ref[j]
+    size = mine_ref.shape[2]
+    rows = out_refs[0][0].shape[1]
+    for q in range(n // 2):
+        for k in range(2):
+            source = source_of(rank, n, q, k)
+            at = pl.ds(pl.multiple_of(source * block, block), block)
+            to = pl.ds(pl.multiple_of(source * 128, 128), 128)
+            for c, got_ref in enumerate((first_ref, second_ref)):
+                units = pl.ds(c * unit, unit)
+                high = k * (block + unit)
+                up_ref[at, units] = got_ref[q, high : high + block]
+                down_ref[units, to] = got_ref[q, high + block : high + block + unit]
+            at = pl.ds(pl.multiple_of(source * size, size), size)
+            joined_ref[0, at] = mine_ref[q, k]
+            joined_ref[1, at] = other_ref[q, k]
+            source = rank ^ (k * (n // 2) + q)
+            to = pl.ds(pl.multiple_of(source * 128, 128), 128)
+            for core in range(2):
+                for c in range(2):
+                    at = pl.ds(pl.multiple_of((group ^ c) * rows, rows), rows)
+                    whole_ref[core, at, to] = out_refs[core][c][q * 2 + k]
     dims = (((0,), (0,)), ((), ()))
     row_ref[...] = (
         tokens_ref[...].astype(F32)
-        + lax.dot_general(mine_ref[...], whole_ref[0], dims, preferred_element_type=F32)
-        + lax.dot_general(other_ref[...], whole_ref[1], dims, preferred_element_type=F32)
+        + lax.dot_general(joined_ref[0], whole_ref[0], dims, preferred_element_type=F32)
+        + lax.dot_general(joined_ref[1], whole_ref[1], dims, preferred_element_type=F32)
     )
     part = residual_ref.shape[0]
     width = residual_ref.shape[1]
@@ -384,13 +437,18 @@
     send_ref[...] = jnp.dot(hidden, down_ref[:, other_cols], preferred_element_type=F32).astype(BF16)
 
 
-def mlp(scalars, tokens, mine, other, out_mine, out_other, first, second, n):
+def mlp(scalars, tokens, mine, other, outs, first, second, n):
     length, depth = tokens.shape
     width = depth // 2
     wide = 2 * first.shape[2]
-    return pl.pallas_call(
-        functools.partial(mlp_kernel, n),
-        in_specs=[sspec()] + [vspec()] * 7,
+    inner = n * mine.shape[2]
+
+    def kernel(scalars, tokens, mine, other, out_a, out_b, out_c, out_d, *refs):
+        mlp_kernel(n, scalars, tokens, mine, other, ((out_a, out_b), (out_c, out_d)), *refs)
+
+    return pl.pallas_call(
+        kernel,
+        in_specs=[sspec()] + [vspec()] * 9,
         out_specs=[vspec()] * 3,
         out_shape=[
             struct((length // n, width), F32),
@@ -401,10 +459,11 @@
             VMEM((depth, wide), BF16),
             VMEM((wide, depth), BF16),
             VMEM((length, depth), F32),
-            VMEM((2, out_mine.shape[1], depth), BF16),
+            VMEM((2, inner, depth), BF16),
+            VMEM((2, inner, length), BF16),
         ],
         compiler_params=params(),
-    )(scalars, tokens, mine, other, out_mine, out_other, first, second)
+    )(scalars, tokens, mine, other, *outs, first, second)
 
 
 def join_kernel(rank_ref, keep_ref, got_ref, residual_ref, base_ref, out_ref):
@@ -451,15 +510,25 @@
     return lax.all_to_all(value, "seq", split_axis=0, concat_axis=0, tiled=True)
 
 
+def exchange_half(value):
+    n = lax.axis_size("seq")
+    groups = [list(range(n // 2)), list(range(n // 2, n))]
+    return lax.all_to_all(
+        value, "seq", split_axis=0, concat_axis=0, axis_index_groups=groups, tiled=True
+    )
+
+
 def after(value, *others):
     return lax.optimization_barrier((value, *others))[0]
 
 
 def local_fast(patches, keep_list, qkv_weight, out_weight, up_weight, down_weight):
     n = lax.axis_size("seq")
-    scalars = jnp.stack(
-        [lax.axis_index(name).astype(jnp.int32) for name in ("seq", "head", "groups")]
-    )
+    rank, half, group = (
+        lax.axis_index(name).astype(jnp.int32) for name in ("seq", "head", "groups")
+    )
+    scalars = jnp.stack([rank, half, group])
+    side = rank // (n // 2)
     sup, depth = patches.shape[1], patches.shape[3]
     length = sup * n * 8 // 5
     per_owner = length // n
@@ -467,28 +536,44 @@
     head_rows = qkv_weight.shape[2]
     keep_col = keep_list.reshape(-1, 1)
     flat = patches.reshape(4 * sup, depth)
-    slots = prep(scalars, keep_col, flat, qkv_weight.transpose(1, 2, 0), n, sup)
+    heads = qkv_weight.transpose(1, 2, 0)
+    qkv_home = lax.dynamic_slice_in_dim(heads, side * (n // 2), n // 2, 0)
+    qkv_away = lax.dynamic_slice_in_dim(heads, (1 - side) * (n // 2), n // 2, 0)
+    out_rows = out_weight.shape[0] // 2
+    out_half = lax.dynamic_slice_in_dim(out_weight, group * out_rows, out_rows, 0)
+
+    slots = prep(scalars, keep_col, flat, n, sup)
     dealt = exchange(slots)
-    across = swap(after(out_weight, slots), "seq", n // 2)
-    dealt, across = lax.optimization_barrier((dealt, across))
-    sent = pick(scalars, keep_col, dealt, up_weight, down_weight, head_rows, n, sup, per_owner)
-    pair = jnp.stack([out_weight, across])
-    pair = after(pair, sent)
-    got = exchange(sent)
-    quads = [pair] + [swap(pair, "seq", j) for j in range(1, n // 2)]
-    got, *quads = lax.optimization_barrier((got, *quads))
-    top = half_width // 128 * per_owner
-    pieces = got[:, :top]
+    qkv_across = swap(qkv_away, "seq", n // 2)
+    out_across = swap(out_half, "seq", n // 2)
+    mlp_home, mlp_away = pack(scalars, up_weight, down_weight, n)
+    dealt, out_across = lax.optimization_barrier((dealt, out_across))
+    owned = pick(scalars, keep_col, dealt, n, sup, per_owner)
+
+    across = swap(owned, "seq", n // 2)
+    out_pair = after(jnp.stack([out_half, out_across]), owned)
+    mlp_across = swap(after(mlp_away, owned), "seq", n // 2)
+    out_mine = jnp.concatenate(
+        [out_pair] + [swap(out_pair, "seq", j) for j in range(1, n // 2)], axis=0
+    )
+
+    got = exchange_half(fan(owned, across, qkv_home, qkv_across))
+    out_second = swap(out_mine, "groups", 1)
+    pieces = got[:, : got.shape[1] - 2 * head_rows]
     pieces_other = swap(pieces, "head", 1)
-    first = got[:, top:]
+    tokens, attended = attend_fast(scalars, got, pieces_other, head_rows, per_owner, n)
+
+    mlp_pair = jnp.concatenate([mlp_home, mlp_across], axis=1)
+    first = exchange_half(mlp_pair)
+    att_across = swap(attended, "seq", n // 2)
+    pair = jnp.stack([attended, att_across])
+    pair, first = lax.optimization_barrier((pair, first))
+    gathered = exchange_half(jnp.broadcast_to(pair[None], (n // 2,) + pair.shape))
     second = swap(first, "groups", 1)
-    tokens, attended = attend_fast(scalars, pieces, pieces_other, dealt, head_rows, per_owner, n)
-    out_mine = jnp.stack([quad[k] for k in range(2) for quad in quads])
-    out_other = swap(out_mine, "head", 1)
-    gathered = exchange(attended).reshape(half_width, length)
+    outs = (out_mine, out_second, swap(out_mine, "head", 1), swap(out_second, "head", 1))
     gathered_other = swap(gathered, "head", 1)
     residual, keep, send = mlp(
-        scalars, tokens, gathered, gathered_other, out_mine, out_other, first, second, n
+        scalars, tokens, gathered, gathered_other, outs, first, second, n
     )
     got = swap(send, "head", 1)
     base, terms = join(scalars, keep, got, residual)

time: 127 us -> 143 us (1.13)
  blocking collectives: 19.4 us -> 33.9 us
    all_to_all x0 -> x1, blocking collectives: none -> 14.1 us  [exchange_half(): lax.all_to_all(value, 'seq', split_axis=0, concat_axis=0, axis_index_grou...]
    all_to_all x3 -> x1, waiting for transfers between devices: 12.2 us -> 0.01 us  [exchange(): return lax.all_to_all(value, 'seq', split_axis=0, concat_axis=0, tiled=True)]
    ppermute x9 -> x15, waiting for transfers between devices: 51.9 us -> 62.4 us  [swap(): return lax.ppermute(value, axis, [(i, i ^ j) for i in range(n)])]
    all_to_all x3 -> x1, starting transfers between devices: 16.7 us -> 7.41 us  [exchange(): return lax.all_to_all(value, 'seq', split_axis=0, concat_axis=0, tiled=True)]
    all_to_all x0 -> x2, starting transfers between devices: none -> 6.94 us  [exchange_half(): lax.all_to_all(value, 'seq', split_axis=0, concat_axis=0, axis_index_grou...]
    ppermute x9 -> x15, starting transfers between devices: 8.45 us -> 11.5 us  [swap(): return lax.ppermute(value, axis, [(i, i ^ j) for i in range(n)])]
    pallas_call x2 -> x4, Pallas kernels: 7.09 us -> 6.88 us  [the longest x1 4.86 us: mlp(): pl.pallas_call(kernel, in_specs=[sspec()] + [vspec()] * 9, out_specs=[vsp...]
  transfers between devices with their start and end apart: 12 -> 18, of which waited for: 8 -> 9; matrix products, arithmetic and copies ran while one was open for 1% -> 2% of each run, Pallas kernels for 0% -> 3%
where the time goes in v4:
time: 143 us; the launch traced here: 142 us
  waiting for transfers between devices  63.2 us (44%)
  blocking collectives  33.9 us (24%)
  starting transfers between devices  25.8 us (18%)
  Pallas kernels  13.3 us (9%)
  local copies, waits for them, and re-layouts  4.84 us (3%)
    ppermute x15, waiting for transfers between devices, swap(): return lax.ppermute(value, axis, [(i, i ^ j) for i in range(n)])  62.4 us
    all_to_all x1, blocking collectives, exchange(): return lax.all_to_all(value, 'seq', split_axis=0, concat_axis=0, tiled=True)  19.7 us
    all_to_all x1, blocking collectives, exchange_half(): lax.all_to_all(value, 'seq', split_axis=0, concat_axis=0, axis_index_grou...  14.1 us
    ppermute x15, starting transfers between devices, swap(): return lax.ppermute(value, axis, [(i, i ^ j) for i in range(n)])  11.5 us
    all_to_all x1, starting transfers between devices, exchange(): return lax.all_to_all(value, 'seq', split_axis=0, concat_axis=0, tiled=True)  7.41 us
    all_to_all x2, starting transfers between devices, exchange_half(): lax.all_to_all(value, 'seq', split_axis=0, concat_axis=0, axis_index_grou...  6.94 us
    pallas_call x1, Pallas kernels, mlp(): pl.pallas_call(kernel, in_specs=[sspec()] + [vspec()] * 9, out_specs=[vsp...  4.86 us
  transfers between devices with their start and end apart: 18, of which 9 were waited for; matrix products, arithmetic and copies ran while one was open for 2% of the time, Pallas kernels for 3%

profile of v4, /device:TPU:0, one launch (start us, length us, event | category | flops | bytes accessed | tf_op | source)
XLA Modules:
  0.0 142.2 jit_solution(15109528856657791226)
XLA Ops:
  0.0 0.7 copy-done.4
  0.8 1.0 reshape.14.patches_ref
  1.9 1.8 %shard_map.64 = bf16[8,128,128]{2,1,0:T(8,128)(2,1)} custom-call(s32[3]{0:T(128)S(1)} %pad_add_fusion.rank_ref.scalars, s32[64,1]{1,0:T(8,128)S(1)} %copy.8.keep_ref, bf16[160,1024]{1,0:T(8,128)(2,1)S(1)} %reshape.14.patches_ref), custom_call_target="tpu_custom_call" | custom-call | tf_op jit(solution)/shard_map/pallas_call | solution.py:211
  3.8 7.4 %all-to-all-start = ((bf16[8,128,128]{2,1,0:T(8,128)(2,1)}), bf16[8,128,128]{2,1,0:T(8,128)(2,1)S(1)}, u32[]{:S(2)}, u32[]{:S(2)}) async-start(bf16[8,128,128]{2,1,0:T(8,128)(2,1)} %shard_map.64), calls=%async_computation | async-start | bytes 524288 | tf_op jit(solution)/shard_map/all_to_all | solution.py:510
  11.2 3.0 %collective-permute-start.2 = (bf16[4,192,128]{2,1,0:T(8,128)(2,1)S(1)}, bf16[4,192,128]{2,1,0:T(8,128)(2,1)S(1)}, u32[]{:S(2)}, u32[]{:S(2)}) collective-permute-start(bf16[4,192,128]{2,1,0:T(8,128)(2,1)S(1)} %get-tuple-element.35), channel_id=1, source_target_pairs={{0,8},{2,10},{4,12},{6,14},{8,0},{10,2},{12,4},{14,6},{1,9},{3,11}... | collective-permute-start | bytes 589832 | tf_op jit(solution)/shard_map/ppermute | solution.py:506
  14.3 17.0 %collective-permute-done = bf16[256,128]{1,0:T(8,128)(2,1)S(1)} collective-permute-done((bf16[256,128]{1,0:T(8,128)(2,1)S(1)}, bf16[256,128]{1,0:T(8,128)(2,1)S(1)}, u32[]{:S(2)}, u32[]{:S(2)}) %collective-permute-start) | collective-permute-done | bytes 65568 | tf_op jit(solution)/shard_map/ppermute | solution.py:506
  31.3 0.8 shard_map.65.owned_ref
  32.2 5.1 %collective-permute-done.1.across_ref = bf16[256,128]{1,0:T(8,128)(2,1)S(1)} collective-permute-done((bf16[256,128]{1,0:T(8,128)(2,1)S(1)}, bf16[256,128]{1,0:T(8,128)(2,1)S(1)}, u32[]{:S(2)}, u32[]{:S(2)}) %collective-permute-start.1) | collective-permute-done | bytes 65568 | tf_op jit(solution)/shard_map/ppermute | solution.py:506
  37.4 14.1 %all_to_all.25.mine_ref = bf16[4,896,128]{2,1,0:T(8,128)(2,1)S(1)} all-to-all(bf16[4,896,128]{2,1,0:T(8,128)(2,1)S(1)} %shard_map.66), channel_id=1, replica_groups={{0,2,4,6},{8,10,12,14},{1,3,5,7},{9,11,13,15},{16,18,20,22},{24,26,28,3..., dimensions={0} | all-to-all | bytes 1835008 | tf_op jit(solution)/shard_map/all_to_all | solution.py:516
  51.7 0.9 copy-done.1
  52.8 1.2 shard_map.68
  53.9 1.3 collective-permute-start.5
  55.3 1.0 collective-permute-start.9
  56.2 1.5 %collective-permute-start.8 = (bf16[2,256,128]{2,1,0:T(8,128)(2,1)S(1)}, bf16[2,256,128]{2,1,0:T(8,128)(2,1)S(1)}, u32[]{:S(2)}, u32[]{:S(2)}) collective-permute-start(bf16[2,256,128]{2,1,0:T(8,128)(2,1)S(1)} %pad_maximum_fusion.2), channel_id=1, source_target_pairs={{0,4},{2,6},{4,0},{6,2},{8,12},{10,14},{12,8},{14,10},{1,5},{3,7},... | collective-permute-start | bytes 393224 | tf_op jit(solution)/shard_map/ppermute | solution.py:506
  57.7 1.1 collective-permute-start.7
  58.8 9.4 %collective-permute-done.5 = bf16[4,256,128]{2,1,0:T(8,128)(2,1)S(1)} collective-permute-done((bf16[4,256,128]{2,1,0:T(8,128)(2,1)S(1)}, bf16[4,256,128]{2,1,0:T(8,128)(2,1)S(1)}, u32[]{:S(2)}, u32[]{:S(2)}) %collective-permute-start.5) | collective-permute-done | bytes 262176 | tf_op jit(solution)/shard_map/ppermute | solution.py:506
  68.2 0.9 pad_maximum_fusion
  69.1 3.5 %all-to-all-start.2 = ((bf16[4,512,128]{2,1,0:T(8,128)(2,1)}), bf16[4,512,128]{2,1,0:T(8,128)(2,1)S(1)}, u32[]{:S(2)}, u32[]{:S(2)}) async-start(bf16[4,512,128]{2,1,0:T(8,128)(2,1)} %pad_maximum_fusion), calls=%async_computation.2 | async-start | bytes 1048576 | tf_op jit(solution)/shard_map/all_to_all | solution.py:516
  72.5 2.7 %shard_map.67 = (bf16[512,1024]{1,0:T(8,128)(2,1)S(1)}, bf16[64,512]{1,0:T(8,128)(2,1)S(1)}) custom-call(s32[3]{0:T(128)S(1)} %pad_add_fusion.rank_ref.scalars, bf16[4,896,128]{2,1,0:T(8,128)(2,1)S(1)} %all_to_all.25.mine_ref, bf16[4,512,128]{2,1,0:T(8,128)(2,1)S(1)} %collective-permute-done.3.other_ref), custom_call_target="tpu_custom_call" | custom-call | flops 30000001024 | bytes 1048576 | tf_op jit(solution)/shard_map/pallas_call | solution.py:369
  75.3 5.8 %collective-permute-done.4 = bf16[64,512]{1,0:T(8,128)(2,1)S(1)} collective-permute-done((bf16[64,512]{1,0:T(8,128)(2,1)S(1)}, bf16[64,512]{1,0:T(8,128)(2,1)S(1)}, u32[]{:S(2)}, u32[]{:S(2)}) %collective-permute-start.4) | collective-permute-done | bytes 65568 | tf_op jit(solution)/shard_map/ppermute | solution.py:506
  81.1 0.8 all-to-all-done.2.refs_0_
  81.9 0.9 broadcast_in_dim.2
  82.8 3.5 %all-to-all-start.3 = ((bf16[4,2,64,512]{3,2,1,0:T(8,128)(2,1)}), bf16[4,2,64,512]{3,2,1,0:T(8,128)(2,1)S(1)}, u32[]{:S(2)}, u32[]{:S(2)}) async-start(bf16[4,2,64,512]{3,2,1,0:T(8,128)(2,1)} %broadcast_in_dim.2), calls=%async_computation.3 | async-start | bytes 1048576 | tf_op jit(solution)/shard_map/all_to_all | solution.py:516
  86.3 0.9 constant_dynamic-update-slice_fusion.2
  87.3 1.6 %collective-permute-start.10 = (bf16[8,256,128]{2,1,0:T(8,128)(2,1)S(1)}, bf16[8,256,128]{2,1,0:T(8,128)(2,1)}, u32[]{:S(2)}, u32[]{:S(2)}) collective-permute-start(bf16[8,256,128]{2,1,0:T(8,128)(2,1)S(1)} %constant_dynamic-update-slice_fusion.out_a), channel_id=1, source_target_pairs={{0,16},{16,0},{1,17},{17,1},{2,18},{18,2},{3,19},{19,3},{4,20},{20... | collective-permute-start | bytes 1572872 | tf_op jit(solution)/shard_map/ppermute | solution.py:506
  88.8 10.4 %collective-permute-done.10.out_b = bf16[8,256,128]{2,1,0:T(8,128)(2,1)} collective-permute-done((bf16[8,256,128]{2,1,0:T(8,128)(2,1)S(1)}, bf16[8,256,128]{2,1,0:T(8,128)(2,1)}, u32[]{:S(2)}, u32[]{:S(2)}) %collective-permute-start.10) | collective-permute-done | bytes 524320 | tf_op jit(solution)/shard_map/ppermute | solution.py:506
  99.3 1.5 %collective-permute-start.13 = (bf16[4,512,128]{2,1,0:T(8,128)(2,1)S(1)}, bf16[4,512,128]{2,1,0:T(8,128)(2,1)}, u32[]{:S(2)}, u32[]{:S(2)}) collective-permute-start(bf16[4,512,128]{2,1,0:T(8,128)(2,1)S(1)} %all-to-all-done.2.refs_0_), channel_id=1, source_target_pairs={{0,16},{16,0},{1,17},{17,1},{2,18},{18,2},{3,19},{19,3},{4,20},{20... | collective-permute-start | bytes 1572872 | tf_op jit(solution)/shard_map/ppermute | solution.py:506
  101.5 12.2 %collective-permute-done.13.refs_1_ = bf16[4,512,128]{2,1,0:T(8,128)(2,1)} collective-permute-done((bf16[4,512,128]{2,1,0:T(8,128)(2,1)S(1)}, bf16[4,512,128]{2,1,0:T(8,128)(2,1)}, u32[]{:S(2)}, u32[]{:S(2)}) %collective-permute-start.13) | collective-permute-done | bytes 524320 | tf_op jit(solution)/shard_map/ppermute | solution.py:506
  113.7 4.9 %shard_map.69 = (f32[64,512]{1,0:T(8,128)S(1)}, f32[512,512]{1,0:T(8,128)S(1)}, bf16[512,512]{1,0:T(8,128)(2,1)S(1)}) custom-call(s32[3]{0:T(128)S(1)} %pad_add_fusion.rank_ref.scalars, bf16[512,1024]{1,0:T(8,128)(2,1)S(1)} %get-tuple-element.21.tokens, bf16[4,2,64,512]{3,2,1,0:T(8,128)(2,1)S(1)} %all-to-all-done.3.mine, ...), custom_call_target="tpu_custom_call" | custom-call | tf_op jit(solution)/shard_map/pallas_call | solution.py:449
  118.7 1.9 %collective-permute-done.14.got_ref = bf16[512,512]{1,0:T(8,128)(2,1)S(1)} collective-permute-done((bf16[512,512]{1,0:T(8,128)(2,1)S(1)}, bf16[512,512]{1,0:T(8,128)(2,1)S(1)}, u32[]{:S(2)}, u32[]{:S(2)}) %collective-permute-start.14) | collective-permute-done | bytes 524320 | tf_op jit(solution)/shard_map/ppermute | solution.py:506
  121.2 19.7 %all_to_all.26.terms_ref = bf16[8,64,512]{2,1,0:T(8,128)(2,1)S(1)} all-to-all(bf16[8,64,512]{2,1,0:T(8,128)(2,1)S(1)} %bitcast.15), channel_id=1, replica_groups=mesh['groups'=2,'seq'=8,'head'=2] {'seq'}, dimensions={0} | all-to-all | bytes 1048576 | tf_op jit(solution)/shard_map/all_to_all | solution.py:510
  141.0 1.2 shard_map.71
  (39 shorter events, 2.4 us)
Async XLA Ops:
  0.0 14.2 %copy-start = (bf16[512,128]{1,0:T(8,128)(2,1)S(1)}, bf16[512,128]{1,0:T(8,128)(2,1)}, u32[]{:S(2)}) copy-start(bf16[512,128]{1,0:T(8,128)(2,1)} %param.9) | copy-start | bytes 393220
  0.0 0.7 copy-start.4
  3.8 7.4 %copy-start.3 = (bf16[128,8,192]{0,2,1:T(8,128)(2,1)S(1)}, bf16[128,8,192]{0,2,1:T(8,128)(2,1)}, u32[]{:S(2)}) copy-start(bf16[128,8,192]{0,2,1:T(8,128)(2,1)} %param.8) | copy-start | bytes 1179652
  3.8 27.6 %all-to-all-start = ((bf16[8,128,128]{2,1,0:T(8,128)(2,1)}), bf16[8,128,128]{2,1,0:T(8,128)(2,1)S(1)}, u32[]{:S(2)}, u32[]{:S(2)}) async-start(bf16[8,128,128]{2,1,0:T(8,128)(2,1)} %shard_map.64), calls=%async_computation | async-start | bytes 524288 | tf_op jit(solution)/shard_map/all_to_all | solution.py:510
  11.2 21.0 %collective-permute-start.2 = (bf16[4,192,128]{2,1,0:T(8,128)(2,1)S(1)}, bf16[4,192,128]{2,1,0:T(8,128)(2,1)S(1)}, u32[]{:S(2)}, u32[]{:S(2)}) collective-permute-start(bf16[4,192,128]{2,1,0:T(8,128)(2,1)S(1)} %get-tuple-element.35), channel_id=1, source_target_pairs={{0,8},{2,10},{4,12},{6,14},{8,0},{10,2},{12,4},{14,6},{1,9},{3,11}... | collective-permute-start | bytes 589832 | tf_op jit(solution)/shard_map/ppermute | solution.py:506
  14.2 17.1 %collective-permute-start = (bf16[256,128]{1,0:T(8,128)(2,1)S(1)}, bf16[256,128]{1,0:T(8,128)(2,1)S(1)}, u32[]{:S(2)}, u32[]{:S(2)}) collective-permute-start(bf16[256,128]{1,0:T(8,128)(2,1)S(1)} %constant_dynamic-slice_fusion), channel_id=1, source_target_pairs={{0,8},{2,10},{4,12},{6,14},{8,0},{10,2},{12,4},{14,6},{1,9},{3,11}... | collective-permute-start | bytes 196616 | tf_op jit(solution)/shard_map/ppermute | solution.py:506
  32.1 5.2 %collective-permute-start.1 = (bf16[256,128]{1,0:T(8,128)(2,1)S(1)}, bf16[256,128]{1,0:T(8,128)(2,1)S(1)}, u32[]{:S(2)}, u32[]{:S(2)}) collective-permute-start(bf16[256,128]{1,0:T(8,128)(2,1)S(1)} %shard_map.65.owned_ref), channel_id=1, source_target_pairs={{0,8},{2,10},{4,12},{6,14},{8,0},{10,2},{12,4},{14,6},{1,9},{3,11}... | collective-permute-start | bytes 196616 | tf_op jit(solution)/shard_map/ppermute | solution.py:506
  51.6 1.0 copy-start.1
  51.6 1.2 copy-start.2
  51.6 20.9 %collective-permute-start.3 = (bf16[4,512,128]{2,1,0:T(8,128)(2,1)S(1)}, bf16[4,512,128]{2,1,0:T(8,128)(2,1)S(1)}, u32[]{:S(2)}, u32[]{:S(2)}) collective-permute-start(bf16[4,512,128]{2,1,0:T(8,128)(2,1)S(1)} %slice.4), channel_id=1, source_target_pairs={{0,1},{1,0},{2,3},{3,2},{4,5},{5,4},{6,7},{7,6},{8,9},{9,8},{10,11... | collective-permute-start | bytes 1572872 | tf_op jit(solution)/shard_map/ppermute | solution.py:506
  53.9 14.3 %collective-permute-start.5 = (bf16[4,256,128]{2,1,0:T(8,128)(2,1)S(1)}, bf16[4,256,128]{2,1,0:T(8,128)(2,1)S(1)}, u32[]{:S(2)}, u32[]{:S(2)}) collective-permute-start(bf16[4,256,128]{2,1,0:T(8,128)(2,1)S(1)} %get-tuple-element.25), channel_id=1, source_target_pairs={{0,8},{2,10},{4,12},{6,14},{8,0},{10,2},{12,4},{14,6},{1,9},{3,11}... | collective-permute-start | bytes 786440 | tf_op jit(solution)/shard_map/ppermute | solution.py:506
  55.3 32.0 %collective-permute-start.9 = (bf16[2,256,128]{2,1,0:T(8,128)(2,1)S(1)}, bf16[2,256,128]{2,1,0:T(8,128)(2,1)S(1)}, u32[]{:S(2)}, u32[]{:S(2)}) collective-permute-start(bf16[2,256,128]{2,1,0:T(8,128)(2,1)S(1)} %pad_maximum_fusion.2), channel_id=1, source_target_pairs={{0,6},{2,4},{4,2},{6,0},{8,14},{10,12},{12,10},{14,8},{1,7},{3,5},... | collective-permute-start | bytes 393224 | tf_op jit(solution)/shard_map/ppermute | solution.py:506
  56.2 31.0 %collective-permute-start.8 = (bf16[2,256,128]{2,1,0:T(8,128)(2,1)S(1)}, bf16[2,256,128]{2,1,0:T(8,128)(2,1)S(1)}, u32[]{:S(2)}, u32[]{:S(2)}) collective-permute-start(bf16[2,256,128]{2,1,0:T(8,128)(2,1)S(1)} %pad_maximum_fusion.2), channel_id=1, source_target_pairs={{0,4},{2,6},{4,0},{6,2},{8,12},{10,14},{12,8},{14,10},{1,5},{3,7},... | collective-permute-start | bytes 393224 | tf_op jit(solution)/shard_map/ppermute | solution.py:506
  57.7 28.6 %collective-permute-start.7 = (bf16[2,256,128]{2,1,0:T(8,128)(2,1)S(1)}, bf16[2,256,128]{2,1,0:T(8,128)(2,1)}, u32[]{:S(2)}, u32[]{:S(2)}) collective-permute-start(bf16[2,256,128]{2,1,0:T(8,128)(2,1)S(1)} %pad_maximum_fusion.2), channel_id=1, source_target_pairs={{0,2},{2,0},{4,6},{6,4},{8,10},{10,8},{12,14},{14,12},{1,3},{3,1},... | collective-permute-start | bytes 393224 | tf_op jit(solution)/shard_map/ppermute | solution.py:506
  69.1 12.9 %all-to-all-start.2 = ((bf16[4,512,128]{2,1,0:T(8,128)(2,1)}), bf16[4,512,128]{2,1,0:T(8,128)(2,1)S(1)}, u32[]{:S(2)}, u32[]{:S(2)}) async-start(bf16[4,512,128]{2,1,0:T(8,128)(2,1)} %pad_maximum_fusion), calls=%async_computation.2 | async-start | bytes 1048576 | tf_op jit(solution)/shard_map/all_to_all | solution.py:516
  75.2 5.9 %collective-permute-start.4 = (bf16[64,512]{1,0:T(8,128)(2,1)S(1)}, bf16[64,512]{1,0:T(8,128)(2,1)S(1)}, u32[]{:S(2)}, u32[]{:S(2)}) collective-permute-start(bf16[64,512]{1,0:T(8,128)(2,1)S(1)} %get-tuple-element.22), channel_id=1, source_target_pairs={{0,8},{2,10},{4,12},{6,14},{8,0},{10,2},{12,4},{14,6},{1,9},{3,11}... | collective-permute-start | bytes 196616 | tf_op jit(solution)/shard_map/ppermute | solution.py:506
  82.8 18.0 %all-to-all-start.3 = ((bf16[4,2,64,512]{3,2,1,0:T(8,128)(2,1)}), bf16[4,2,64,512]{3,2,1,0:T(8,128)(2,1)S(1)}, u32[]{:S(2)}, u32[]{:S(2)}) async-start(bf16[4,2,64,512]{3,2,1,0:T(8,128)(2,1)} %broadcast_in_dim.2), calls=%async_computation.3 | async-start | bytes 1048576 | tf_op jit(solution)/shard_map/all_to_all | solution.py:516
  87.3 12.0 %collective-permute-start.10 = (bf16[8,256,128]{2,1,0:T(8,128)(2,1)S(1)}, bf16[8,256,128]{2,1,0:T(8,128)(2,1)}, u32[]{:S(2)}, u32[]{:S(2)}) collective-permute-start(bf16[8,256,128]{2,1,0:T(8,128)(2,1)S(1)} %constant_dynamic-update-slice_fusion.out_a), channel_id=1, source_target_pairs={{0,16},{16,0},{1,17},{17,1},{2,18},{18,2},{3,19},{19,3},{4,20},{20... | collective-permute-start | bytes 1572872 | tf_op jit(solution)/shard_map/ppermute | solution.py:506
  88.8 12.2 %collective-permute-start.11 = (bf16[8,256,128]{2,1,0:T(8,128)(2,1)S(1)}, bf16[8,256,128]{2,1,0:T(8,128)(2,1)}, u32[]{:S(2)}, u32[]{:S(2)}) collective-permute-start(bf16[8,256,128]{2,1,0:T(8,128)(2,1)S(1)} %constant_dynamic-update-slice_fusion.out_a), channel_id=1, source_target_pairs={{0,1},{1,0},{2,3},{3,2},{4,5},{5,4},{6,7},{7,6},{8,9},{9,8},{10,11... | collective-permute-start | bytes 1572872 | tf_op jit(solution)/shard_map/ppermute | solution.py:506
  99.3 2.3 %collective-permute-start.12 = (bf16[8,256,128]{2,1,0:T(8,128)(2,1)}, bf16[8,256,128]{2,1,0:T(8,128)(2,1)}, u32[]{:S(2)}, u32[]{:S(2)}) collective-permute-start(bf16[8,256,128]{2,1,0:T(8,128)(2,1)} %collective-permute-done.10.out_b), channel_id=1, source_target_pairs={{0,1},{1,0},{2,3},{3,2},{4,5},{5,4},{6,7},{7,6},{8,9},{9,8},{10,11... | collective-permute-start | bytes 1572872 | tf_op jit(solution)/shard_map/ppermute | solution.py:506
  99.3 14.4 %collective-permute-start.13 = (bf16[4,512,128]{2,1,0:T(8,128)(2,1)S(1)}, bf16[4,512,128]{2,1,0:T(8,128)(2,1)}, u32[]{:S(2)}, u32[]{:S(2)}) collective-permute-start(bf16[4,512,128]{2,1,0:T(8,128)(2,1)S(1)} %all-to-all-done.2.refs_0_), channel_id=1, source_target_pairs={{0,16},{16,0},{1,17},{17,1},{2,18},{18,2},{3,19},{19,3},{4,20},{20... | collective-permute-start | bytes 1572872 | tf_op jit(solution)/shard_map/ppermute | solution.py:506
  100.8 12.9 %collective-permute-start.6 = (bf16[4,2,64,512]{3,2,1,0:T(8,128)(2,1)S(1)}, bf16[4,2,64,512]{3,2,1,0:T(8,128)(2,1)S(1)}, u32[]{:S(2)}, u32[]{:S(2)}) collective-permute-start(bf16[4,2,64,512]{3,2,1,0:T(8,128)(2,1)S(1)} %all-to-all-done.3.mine), channel_id=1, source_target_pairs={{0,1},{1,0},{2,3},{3,2},{4,5},{5,4},{6,7},{7,6},{8,9},{9,8},{10,11... | collective-permute-start | bytes 1572872 | tf_op jit(solution)/shard_map/ppermute | solution.py:506
  118.6 2.0 %collective-permute-start.14 = (bf16[512,512]{1,0:T(8,128)(2,1)S(1)}, bf16[512,512]{1,0:T(8,128)(2,1)S(1)}, u32[]{:S(2)}, u32[]{:S(2)}) collective-permute-start(bf16[512,512]{1,0:T(8,128)(2,1)S(1)} %get-tuple-element.31), channel_id=1, source_target_pairs={{0,1},{1,0},{2,3},{3,2},{4,5},{5,4},{6,7},{7,6},{8,9},{9,8},{10,11... | collective-permute-start | bytes 1572872 | tf_op jit(solution)/shard_map/ppermute | solution.py:506

commit v5 on v4

--- a/solution.py
+++ b/solution.py
@@ -11,7 +11,6 @@
 F32 = jnp.float32
 BF16 = jnp.bfloat16
 VMEM = pltpu.VMEM
-SLOT = 32
 LIMIT = 32 * 1024 * 1024
 
 def layer_norm(matrix):
@@ -163,53 +162,65 @@
     return jax.ShapeDtypeStruct(shape, dtype)
 
 
-def prep_kernel(n, sup, rank_ref, keep_ref, patches_ref, out_ref):
+def slot_of(index, n, capacity, cuts):
+    device = sum(((index >= j * cuts * capacity).astype(jnp.int32) for j in range(1, n)), 0 * index)
+    inner = index - device * (cuts * capacity)
+    cut = sum(((inner >= c * capacity).astype(jnp.int32) for c in range(1, cuts)), 0 * index)
+    return device, cut, inner - cut * capacity
+
+
+def one_hot(mask):
+    return mask.astype(F32).astype(BF16)
+
+
+def prep_kernel(n, sup, capacity, rank_ref, keep_ref, patches_ref, out_ref):
     rank = rank_ref[0]
     first = rank * sup
     keep = keep_ref[...]
     rows = 4 * sup
     count = keep.shape[0]
-    lane = lax.broadcasted_iota(jnp.int32, (count, rows), 1)
-    ids = first + (lane >> 2)
-    kept = jnp.sum((keep == ids).astype(jnp.int32), axis=0, keepdims=True)
-    below = jnp.sum(
-        jnp.logical_and(keep >= first, keep < ids).astype(jnp.int32), axis=0, keepdims=True
-    )
-    lane_row = lax.broadcasted_iota(jnp.int32, (1, rows), 1)
-    fine_pos = jnp.where(kept == 1, (lane_row >> 2) + 3 * below + (lane_row & 3), -1)
-    lane_s = lax.broadcasted_iota(jnp.int32, (count, sup), 1)
-    ids_s = first + lane_s
-    kept_s = jnp.sum((keep == ids_s).astype(jnp.int32), axis=0, keepdims=True)
-    below_s = jnp.sum(
-        jnp.logical_and(keep >= first, keep < ids_s).astype(jnp.int32), axis=0, keepdims=True
-    )
-    lane_row_s = lax.broadcasted_iota(jnp.int32, (1, sup), 1)
-    mean_pos = jnp.where(kept_s == 1, -1, lane_row_s + 3 * below_s)
+
+    def places(width, shift):
+        ids = lax.broadcasted_iota(jnp.int32, (count, width), 1) >> shift
+        kept = jnp.sum((keep == first + ids).astype(jnp.int32), axis=0, keepdims=True)
+        below = jnp.sum(
+            jnp.logical_and(keep >= first, keep < first + ids).astype(jnp.int32),
+            axis=0,
+            keepdims=True,
+        )
+        return kept, below, lax.broadcasted_iota(jnp.int32, (1, width), 1)
+
+    kept, below, lane = places(rows, 2)
+    fine_pos = jnp.where(kept == 1, (lane >> 2) + 3 * below + (lane & 3), -1)
+    kept, below, lane = places(sup, 0)
+    mean_pos = jnp.where(kept == 1, -1, lane + 3 * below)
     start = first + 3 * jnp.sum((keep < first).astype(jnp.int32), axis=0, keepdims=True)
     flat = patches_ref[...]
+    cuts = flat.shape[1] // 128
     sup_col = lax.broadcasted_iota(jnp.int32, (sup, rows), 0)
     sup_lane = lax.broadcasted_iota(jnp.int32, (sup, rows), 1) >> 2
     averaging = jnp.where(sup_col == sup_lane, 0.25, 0.0).astype(BF16)
     means = jnp.dot(averaging, flat, preferred_element_type=F32).astype(BF16)
-    slot = lax.broadcasted_iota(jnp.int32, (SLOT, 1), 0)
-    for j in range(n):
-        pos = ((j - start) & (n - 1)) + slot * n
-        fine = (pos == fine_pos).astype(F32).astype(BF16)
-        mean = (pos == mean_pos).astype(F32).astype(BF16)
-        dealt = (
-            jnp.dot(fine, flat, preferred_element_type=F32)
-            + jnp.dot(mean, means, preferred_element_type=F32)
-        ).astype(BF16)
-        cuts = dealt.shape[1] // 128
-        for c in range(cuts):
-            out_ref[j, c * SLOT : (c + 1) * SLOT] = dealt[:, c * 128 : (c + 1) * 128]
-
-
-def prep(scalars, keep_col, flat, n, sup):
+    index = lax.broadcasted_iota(jnp.int32, (n * cuts * capacity, 1), 0)
+    device, cut, slot = slot_of(index, n, capacity, cuts)
+    pos = ((device - start) & (n - 1)) + slot * n
+    total = jnp.zeros((n * cuts * capacity, 128), F32)
+    for c in range(cuts):
+        at = jnp.where(cut == c, pos, -2)
+        features = slice(c * 128, (c + 1) * 128)
+        total = (
+            total
+            + jnp.dot(one_hot(at == fine_pos), flat[:, features], preferred_element_type=F32)
+            + jnp.dot(one_hot(at == mean_pos), means[:, features], preferred_element_type=F32)
+        )
+    out_ref[...] = total.astype(BF16)
+
+
+def prep(scalars, keep_col, flat, n, sup, capacity):
     width = flat.shape[1] // 2
-    shape = (n, SLOT * width // 128, 128)
+    shape = (n * capacity * width // 128, 128)
     return pl.pallas_call(
-        functools.partial(prep_kernel, n, sup),
+        functools.partial(prep_kernel, n, sup, capacity),
         grid_spec=pltpu.PrefetchScalarGridSpec(
             num_scalar_prefetch=1,
             grid=(1,),
@@ -217,61 +228,74 @@
                 pl.BlockSpec(keep_col.shape, lambda i, ref: (0, 0)),
                 pl.BlockSpec((flat.shape[0], width), lambda i, ref: (0, ref[1])),
             ],
-            out_specs=pl.BlockSpec(shape, lambda i, ref: (0, 0, 0)),
+            out_specs=pl.BlockSpec(shape, lambda i, ref: (0, 0)),
         ),
         out_shape=struct(shape),
         compiler_params=params(),
     )(scalars, keep_col, flat)
 
 
-def pick_kernel(n, sup, per_owner, rank_ref, keep_ref, got_ref, out_ref):
+def pick_kernel(n, sup, per_owner, capacity, rank_ref, keep_ref, got_ref, out_ref):
     rank = rank_ref[0]
-    cuts = got_ref.shape[1] // SLOT
     keep = keep_ref[...]
     count = keep.shape[0]
-    lanes = n * SLOT
-    shift = SLOT.bit_length() - 1
-    source = (lax.broadcasted_iota(jnp.int32, (count, lanes), 1) >> shift)
+    lanes = got_ref.shape[0]
+    cuts = lanes // (n * capacity)
+    source, _, _ = slot_of(
+        lax.broadcasted_iota(jnp.int32, (count, lanes), 1), n, capacity, cuts
+    )
     low = jnp.sum((keep < source * sup).astype(jnp.int32), axis=0, keepdims=True)
     high = jnp.sum((keep < source * sup + sup).astype(jnp.int32), axis=0, keepdims=True)
-    lane = lax.broadcasted_iota(jnp.int32, (1, lanes), 1)
-    source_row = lane >> shift
-    start = source_row * sup + 3 * low
-    stop = source_row * sup + sup + 3 * high
-    token = start + ((rank - start) & (n - 1)) + (lane & (SLOT - 1)) * n
+    source, cut, slot = slot_of(
+        lax.broadcasted_iota(jnp.int32, (1, lanes), 1), n, capacity, cuts
+    )
+    start = source * sup + 3 * low
+    stop = source * sup + sup + 3 * high
+    token = start + ((rank - start) & (n - 1)) + slot * n
     row = jnp.where(token < stop, token >> (n.bit_length() - 1), -1)
     own = lax.broadcasted_iota(jnp.int32, (per_owner, lanes), 0)
-    choose = (own == row).astype(F32).astype(BF16)
+    got = got_ref[...]
     for c in range(cuts):
-        stacked = jnp.concatenate(
-            [got_ref[j, c * SLOT : (c + 1) * SLOT] for j in range(n)], axis=0
-        )
-        owned = jnp.dot(choose, stacked, preferred_element_type=F32).astype(BF16)
+        choose = one_hot(own == jnp.where(cut == c, row, -1))
+        owned = jnp.dot(choose, got, preferred_element_type=F32).astype(BF16)
         out_ref[c * per_owner : (c + 1) * per_owner] = owned
 
 
-def pick(scalars, keep_col, got, n, sup, per_owner):
+def pick(scalars, keep_col, got, n, sup, per_owner, capacity):
+    cuts = got.shape[0] // (n * capacity)
     return pl.pallas_call(
-        functools.partial(pick_kernel, n, sup, per_owner),
+        functools.partial(pick_kernel, n, sup, per_owner, capacity),
         in_specs=[sspec(), vspec(), vspec()],
         out_specs=vspec(),
-        out_shape=struct((got.shape[1] // SLOT * per_owner, 128)),
+        out_shape=struct((cuts * per_owner, 128)),
         compiler_params=params(),
     )(scalars, keep_col, got)
 
 
-def pack_kernel(n, rank_ref, up_ref, down_ref, home_ref, away_ref, sem):
-    side, part = rank_ref[0] // (n // 2), rank_ref[2]
+def pack_kernel(n, rank_ref, qkv_ref, out_weight_ref, up_ref, down_ref, *refs):
+    near, away_ref, sem = refs[: n // 2], refs[n // 2], refs[n // 2 + 1]
+    rank, part = rank_ref[0], rank_ref[2]
+    half = n // 2
     rows = up_ref.shape[0]
     wide = up_ref.shape[1] // n
     units = wide // 2
+    long = out_weight_ref.shape[0]
     copies = []
-    for k, out_ref in enumerate((home_ref, away_ref)):
-        for d in range(n // 2):
-            dest = (side ^ k) * (n // 2) + d
-            at = pl.ds(pl.multiple_of(dest * wide + part * units, 128), units)
-            copies.append((up_ref.at[:, at], out_ref.at[d, pl.ds(0, rows)]))
-            copies.append((down_ref.at[at], out_ref.at[d, pl.ds(rows, units)]))
+    for j in range(half):
+        dest = rank ^ j
+        for c in range(2):
+            at = pl.ds(pl.multiple_of(dest * wide + c * units, 128), units)
+            copies.append((up_ref.at[:, at], near[j].at[pl.ds(c * rows, rows)]))
+        at = pl.ds(pl.multiple_of(dest * wide, 128), wide)
+        copies.append((down_ref.at[at], near[j].at[pl.ds(2 * rows, wide)]))
+        copies.append((out_weight_ref, near[j].at[pl.ds(2 * rows + wide, long)]))
+        copies.append(
+            (qkv_ref.at[dest], near[j].at[pl.ds(2 * rows + wide + long, qkv_ref.shape[1])])
+        )
+        dest = (rank // half ^ 1) * half + j
+        at = pl.ds(pl.multiple_of(dest * wide + part * units, 128), units)
+        copies.append((up_ref.at[:, at], away_ref.at[j, pl.ds(0, rows)]))
+        copies.append((down_ref.at[at], away_ref.at[j, pl.ds(rows, units)]))
     started = []
     for i, (src, dst) in enumerate(copies):
         copy = pltpu.make_async_copy(src, dst, sem.at[i])
@@ -281,37 +305,44 @@
         copy.wait()
 
 
-def pack(scalars, up, down, n):
-    units = up.shape[1] // n // 2
-    shape = struct((n // 2, up.shape[0] + units, units))
-    return pl.pallas_call(
+def pack(scalars, qkv, out_weight, up, down, n):
+    wide = up.shape[1] // n
+    near = struct((2 * up.shape[0] + wide + out_weight.shape[0] + qkv.shape[1], 128))
+    away = struct((n // 2, up.shape[0] + wide // 2, 128))
+    outs = pl.pallas_call(
         functools.partial(pack_kernel, n),
-        in_specs=[sspec(), aspec(), aspec()],
-        out_specs=[aspec()] * 2,
-        out_shape=[shape, shape],
-        scratch_shapes=[pltpu.SemaphoreType.DMA((2 * n,))],
-        compiler_params=params(),
-    )(scalars, up, down)
-
-
-def fan_kernel(owned_ref, across_ref, home_ref, away_ref, out_ref):
-    rows, depth = owned_ref.shape[0], home_ref.shape[1]
-    for d in range(out_ref.shape[0]):
+        in_specs=[sspec()] + [aspec()] * 4,
+        out_specs=[aspec()] * (n // 2 + 1),
+        out_shape=[near] * (n // 2) + [away],
+        scratch_shapes=[pltpu.SemaphoreType.DMA((7 * n // 2,))],
+        compiler_params=params(),
+    )(scalars, qkv, out_weight, up, down)
+    return list(outs[:-1]), outs[-1]
+
+
+def fan_kernel(rank_ref, owned_ref, across_ref, mine_ref, other_ref, out_ref):
+    part = rank_ref[2]
+    rows = owned_ref.shape[0]
+    count = out_ref.shape[0]
+    depth = (out_ref.shape[1] - 2 * rows) // 2
+    for d in range(count):
         out_ref[d, :rows] = owned_ref[...]
         out_ref[d, rows : 2 * rows] = across_ref[...]
-        out_ref[d, 2 * rows : 2 * rows + depth] = home_ref[d]
-        out_ref[d, 2 * rows + depth :] = away_ref[d]
-
-
-def fan(owned, across, home, away):
-    shape = struct((home.shape[0], 2 * owned.shape[0] + 2 * home.shape[1], 128))
+        at = pl.ds(pl.multiple_of(2 * rows + part * depth, 32), depth)
+        out_ref[d, at] = mine_ref[d * depth : (d + 1) * depth]
+        at = pl.ds(pl.multiple_of(2 * rows + (1 - part) * depth, 32), depth)
+        out_ref[d, at] = other_ref[d * depth : (d + 1) * depth]
+
+
+def fan(scalars, owned, across, mine, other, head_rows, n):
+    shape = struct((n // 2, 2 * owned.shape[0] + head_rows, 128))
     return pl.pallas_call(
         fan_kernel,
-        in_specs=[vspec()] * 4,
+        in_specs=[sspec()] + [vspec()] * 4,
         out_specs=vspec(),
         out_shape=shape,
         compiler_params=params(),
-    )(owned, across, home, away)
+    )(scalars, owned, across, mine, other)
 
 
 def source_of(rank, n, q, k):
@@ -324,7 +355,8 @@
     return (x - average) * lax.rsqrt(power - average * average + 1e-06)
 
 
-def attend_kernel(n, part, rank_ref, mine_ref, other_ref, tokens_ref, out_ref, weight_ref):
+def attend_kernel(n, part, rank_ref, mine_ref, other_ref, *refs):
+    near, (tokens_ref, out_ref, weight_ref) = refs[: n // 2], refs[n // 2 :]
     rank, half = rank_ref[0], rank_ref[1]
     rows = other_ref.shape[1] // 2
     cuts = rows // part
@@ -340,9 +372,11 @@
                 tokens_ref[at, to] = mine_ref[q, cut]
                 to = pl.ds(pl.multiple_of((1 - half) * width + c * 128, 128), 128)
                 tokens_ref[at, to] = other_ref[q, cut]
-            weight_ref[:, pl.ds(pl.multiple_of(source * 128, 128), 128)] = mine_ref[
-                q, 2 * rows + k * depth : 2 * rows + (k + 1) * depth
-            ]
+        source = source_of(rank, n, q, 1)
+        to = pl.ds(pl.multiple_of(source * 128, 128), 128)
+        weight_ref[:, to] = mine_ref[q, 2 * rows :]
+        to = pl.ds(pl.multiple_of((rank ^ q) * 128, 128), 128)
+        weight_ref[:, to] = near[q][near[q].shape[0] - depth :]
     normed = norm_rows(tokens_ref[...].astype(F32)).astype(BF16)
     projected = lax.dot_general(
         normed, weight_ref[...], (((1,), (1,)), ((), ())), preferred_element_type=F32
@@ -362,30 +396,30 @@
     out_ref[...] = attended
 
 
-def attend_fast(scalars, mine, other, head_rows, per_owner, n):
+def attend_fast(scalars, mine, other, near, head_rows, per_owner, n):
     length = n * per_owner
     depth = other.shape[1] // (2 * per_owner) * 256
     size = head_rows // 3
     return pl.pallas_call(
         functools.partial(attend_kernel, n, per_owner),
-        in_specs=[sspec()] + [vspec()] * 2,
+        in_specs=[sspec()] + [vspec()] * (2 + n // 2),
         out_specs=[vspec()] * 2,
         out_shape=[struct((length, depth)), struct((size, length))],
         scratch_shapes=[VMEM((head_rows, n * 128), BF16)],
         compiler_params=params(),
         cost_estimate=cost(30),
-    )(scalars, mine, other)
+    )(scalars, mine, other, *near)
 
 
 def mlp_kernel(
     n,
     rank_ref,
     tokens_ref,
-    mine_ref,
-    other_ref,
-    out_refs,
-    first_ref,
-    second_ref,
+    pieces,
+    outs_near,
+    outs_far,
+    near,
+    far_ref,
     residual_ref,
     keep_ref,
     send_ref,
@@ -397,28 +431,37 @@
 ):
     rank, half, group = rank_ref[0], rank_ref[1], rank_ref[2]
     block = up_ref.shape[0] // n
-    unit = first_ref.shape[2]
-    size = mine_ref.shape[2]
-    rows = out_refs[0][0].shape[1]
-    for q in range(n // 2):
-        for k in range(2):
-            source = source_of(rank, n, q, k)
-            at = pl.ds(pl.multiple_of(source * block, block), block)
-            to = pl.ds(pl.multiple_of(source * 128, 128), 128)
-            for c, got_ref in enumerate((first_ref, second_ref)):
-                units = pl.ds(c * unit, unit)
-                high = k * (block + unit)
-                up_ref[at, units] = got_ref[q, high : high + block]
-                down_ref[units, to] = got_ref[q, high + block : high + block + unit]
-            at = pl.ds(pl.multiple_of(source * size, size), size)
-            joined_ref[0, at] = mine_ref[q, k]
-            joined_ref[1, at] = other_ref[q, k]
-            source = rank ^ (k * (n // 2) + q)
-            to = pl.ds(pl.multiple_of(source * 128, 128), 128)
-            for core in range(2):
-                for c in range(2):
-                    at = pl.ds(pl.multiple_of((group ^ c) * rows, rows), rows)
-                    whole_ref[core, at, to] = out_refs[core][c][q * 2 + k]
+    wide = down_ref.shape[0]
+    unit = wide // 2
+    size = pieces[0].shape[2]
+    long = outs_near[0].shape[1]
+    rows = long // 2
+    for j in range(n // 2):
+        source = rank ^ j
+        at = pl.ds(pl.multiple_of(source * block, block), block)
+        to = pl.ds(pl.multiple_of(source * 128, 128), 128)
+        for c in range(2):
+            up_ref[at, c * unit : (c + 1) * unit] = near[j][c * block : (c + 1) * block]
+        down_ref[:, to] = near[j][2 * block : 2 * block + wide]
+        for core in range(2):
+            whole_ref[core, :, to] = outs_near[core][j]
+        source = source_of(rank, n, j, 1)
+        at = pl.ds(pl.multiple_of(source * block, block), block)
+        to = pl.ds(pl.multiple_of(source * 128, 128), 128)
+        for c in range(2):
+            units = pl.ds(pl.multiple_of((group ^ c) * unit, unit), unit)
+            high = c * (block + unit)
+            up_ref[at, units] = far_ref[j, high : high + block]
+            down_ref[units, to] = far_ref[j, high + block : high + block + unit]
+        source = rank ^ j ^ (n // 2)
+        to = pl.ds(pl.multiple_of(source * 128, 128), 128)
+        for core in range(2):
+            for c in range(2):
+                at = pl.ds(pl.multiple_of((group ^ c) * rows, rows), rows)
+                whole_ref[core, at, to] = outs_far[core][j, c * rows : (c + 1) * rows]
+            for k in range(2):
+                at = pl.ds(pl.multiple_of((rank ^ j ^ (k * n // 2)) * size, size), size)
+                joined_ref[core, at] = pieces[core][j, k]
     dims = (((0,), (0,)), ((), ()))
     row_ref[...] = (
         tokens_ref[...].astype(F32)
@@ -437,18 +480,19 @@
     send_ref[...] = jnp.dot(hidden, down_ref[:, other_cols], preferred_element_type=F32).astype(BF16)
 
 
-def mlp(scalars, tokens, mine, other, outs, first, second, n):
+def mlp(scalars, tokens, pieces, outs_near, outs_far, near, far, n):
     length, depth = tokens.shape
     width = depth // 2
-    wide = 2 * first.shape[2]
-    inner = n * mine.shape[2]
-
-    def kernel(scalars, tokens, mine, other, out_a, out_b, out_c, out_d, *refs):
-        mlp_kernel(n, scalars, tokens, mine, other, ((out_a, out_b), (out_c, out_d)), *refs)
+    wide = 2 * (far.shape[1] // 2 - depth // n)
+    inner = n * pieces[0].shape[2]
+
+    def kernel(scalars, tokens, a, b, c, d, e, f, *refs):
+        near, (far, *refs) = refs[: n // 2], refs[n // 2 :]
+        mlp_kernel(n, scalars, tokens, (a, b), (c, d), (e, f), near, far, *refs)
 
     return pl.pallas_call(
         kernel,
-        in_specs=[sspec()] + [vspec()] * 9,
+        in_specs=[sspec()] + [vspec()] * (8 + n // 2),
         out_specs=[vspec()] * 3,
         out_shape=[
             struct((length // n, width), F32),
@@ -463,7 +507,7 @@
             VMEM((2, inner, length), BF16),
         ],
         compiler_params=params(),
-    )(scalars, tokens, mine, other, *outs, first, second)
+    )(scalars, tokens, *pieces, *outs_near, *outs_far, *near, far)
 
 
 def join_kernel(rank_ref, keep_ref, got_ref, residual_ref, base_ref, out_ref):
@@ -524,59 +568,71 @@
 
 def local_fast(patches, keep_list, qkv_weight, out_weight, up_weight, down_weight):
     n = lax.axis_size("seq")
-    rank, half, group = (
+    rank, head, group = (
         lax.axis_index(name).astype(jnp.int32) for name in ("seq", "head", "groups")
     )
-    scalars = jnp.stack([rank, half, group])
-    side = rank // (n // 2)
+    scalars = jnp.stack([rank, head, group])
+    half = n // 2
+    side = rank // half
     sup, depth = patches.shape[1], patches.shape[3]
     length = sup * n * 8 // 5
     per_owner = length // n
     half_width = depth // 2
     head_rows = qkv_weight.shape[2]
+    part_rows = head_rows // 2
+    out_rows = out_weight.shape[0] // 2
+    capacity = (4 * sup + n - 1) // n
     keep_col = keep_list.reshape(-1, 1)
     flat = patches.reshape(4 * sup, depth)
     heads = qkv_weight.transpose(1, 2, 0)
-    qkv_home = lax.dynamic_slice_in_dim(heads, side * (n // 2), n // 2, 0)
-    qkv_away = lax.dynamic_slice_in_dim(heads, (1 - side) * (n // 2), n // 2, 0)
-    out_rows = out_weight.shape[0] // 2
-    out_half = lax.dynamic_slice_in_dim(out_weight, group * out_rows, out_rows, 0)
-
-    slots = prep(scalars, keep_col, flat, n, sup)
+
+    qkv_away = lax.dynamic_slice(
+        heads, ((1 - side) * half, group * part_rows, 0), (half, part_rows, 128)
+    ).reshape(half * part_rows, 128)
+    out_away = lax.dynamic_slice_in_dim(out_weight, group * out_rows, out_rows, 0)
+    early = swap(jnp.concatenate([qkv_away, out_away]), "seq", half)
+    slots = prep(scalars, keep_col, flat, n, sup, capacity)
+    slots, early = lax.optimization_barrier((slots, early))
+    near, mlp_away = pack(scalars, heads, out_weight, up_weight, down_weight, n)
     dealt = exchange(slots)
-    qkv_across = swap(qkv_away, "seq", n // 2)
-    out_across = swap(out_half, "seq", n // 2)
-    mlp_home, mlp_away = pack(scalars, up_weight, down_weight, n)
-    dealt, out_across = lax.optimization_barrier((dealt, out_across))
-    owned = pick(scalars, keep_col, dealt, n, sup, per_owner)
-
-    across = swap(owned, "seq", n // 2)
-    out_pair = after(jnp.stack([out_half, out_across]), owned)
-    mlp_across = swap(after(mlp_away, owned), "seq", n // 2)
-    out_mine = jnp.concatenate(
-        [out_pair] + [swap(out_pair, "seq", j) for j in range(1, n // 2)], axis=0
-    )
-
-    got = exchange_half(fan(owned, across, qkv_home, qkv_across))
-    out_second = swap(out_mine, "groups", 1)
-    pieces = got[:, : got.shape[1] - 2 * head_rows]
+    near = [near[0]] + [swap(near[j], "seq", j) for j in range(1, half)]
+    early_other = swap(early, "groups", 1)
+    dealt, early_other, *near = lax.optimization_barrier((dealt, early_other, *near))
+    owned = pick(scalars, keep_col, dealt, n, sup, per_owner, capacity)
+
+    across = swap(owned, "seq", half)
+    mlp_mine = swap(after(mlp_away, across), "seq", half)
+    got = exchange_half(fan(scalars, owned, across, early, early_other, head_rows, n))
+    got, mlp_mine = lax.optimization_barrier((got, mlp_mine))
+
+    pieces = got[:, : got.shape[1] - head_rows]
     pieces_other = swap(pieces, "head", 1)
-    tokens, attended = attend_fast(scalars, got, pieces_other, head_rows, per_owner, n)
-
-    mlp_pair = jnp.concatenate([mlp_home, mlp_across], axis=1)
-    first = exchange_half(mlp_pair)
-    att_across = swap(attended, "seq", n // 2)
+    mlp_other = swap(mlp_mine, "groups", 1)
+    out_far = jnp.concatenate([early[half * part_rows :], early_other[half * part_rows :]])
+    out_far = after(out_far, got)
+    tokens, attended = attend_fast(scalars, got, pieces_other, near, head_rows, per_owner, n)
+
+    outs_far = [out_far] + [swap(out_far, "seq", j) for j in range(1, half)]
+    att_across = swap(attended, "seq", half)
+    mlp_far = exchange_half(jnp.concatenate([mlp_mine, mlp_other], axis=1))
+    att_across, *outs_far = lax.optimization_barrier((att_across, *outs_far))
     pair = jnp.stack([attended, att_across])
-    pair, first = lax.optimization_barrier((pair, first))
-    gathered = exchange_half(jnp.broadcast_to(pair[None], (n // 2,) + pair.shape))
-    second = swap(first, "groups", 1)
-    outs = (out_mine, out_second, swap(out_mine, "head", 1), swap(out_second, "head", 1))
-    gathered_other = swap(gathered, "head", 1)
+    gathered = jnp.stack([pair] + [swap(pair, "seq", j) for j in range(1, half)])
+    outs_far = jnp.stack(outs_far)
+    top = near[0].shape[0] - head_rows - 2 * out_rows
+    outs_near = jnp.stack([block[top : top + 2 * out_rows] for block in near])
     residual, keep, send = mlp(
-        scalars, tokens, gathered, gathered_other, outs, first, second, n
-    )
-    got = swap(send, "head", 1)
-    base, terms = join(scalars, keep, got, residual)
+        scalars,
+        tokens,
+        (gathered, swap(gathered, "head", 1)),
+        (outs_near, swap(outs_near, "head", 1)),
+        (outs_far, swap(outs_far, "head", 1)),
+        near,
+        mlp_far,
+        n,
+    )
+    sent = swap(send, "head", 1)
+    base, terms = join(scalars, keep, sent, residual)
     terms = exchange(terms.reshape(n, per_owner, half_width))
     encoded = last(scalars, base, terms)
     return encoded.reshape(1, per_owner, 1, half_width)

time: 143 us -> 123 us (0.86)
  waiting for transfers between devices: 63.2 us -> 38.2 us
  blocking collectives: 33.9 us -> 17.5 us
  starting transfers between devices: 25.8 us -> 34.6 us
  local copies, waits for them, and re-layouts: 4.84 us -> 12.2 us
  other arithmetic: 0.97 us -> 3.9 us
  Pallas kernels: 13.3 us -> 16 us
    ppermute x15 -> x20, waiting for transfers between devices: 62.4 us -> 34 us  [swap(): return lax.ppermute(value, axis, [(i, i ^ j) for i in range(n)])]
    all_to_all x1 -> x0, blocking collectives: 14.1 us -> none  [exchange_half(): lax.all_to_all(value, 'seq', split_axis=0, concat_axis=0, axis_index_grou...]
    ppermute x15 -> x20, starting transfers between devices: 11.5 us -> 23.8 us  [swap(): return lax.ppermute(value, axis, [(i, i ^ j) for i in range(n)])]
    unnamed x13 -> x40, local copies, waits for them, and re-layouts: 2.73 us -> 7.8 us
    all_to_all x1, starting transfers between devices: 7.41 us -> 3.72 us  [exchange(): return lax.all_to_all(value, 'seq', split_axis=0, concat_axis=0, tiled=True)]
    pallas_call x5, Pallas kernels: 8.72 us -> 11.4 us  [the longest x1 4.51 us: mlp(): pl.pallas_call(kernel, in_specs=[sspec()] + [vspec()] * (8 + n // 2), out...]
    another operation x1 -> x3, local copies, waits for them, and re-layouts: 0.01 us -> 2.33 us  [the longest x2 1.43 us: local_fast(): outs_near = jnp.stack([block[top:top + 2 * out_rows] for block in near])]
    all_to_all x1, blocking collectives: 19.7 us -> 17.5 us  [exchange(): return lax.all_to_all(value, 'seq', split_axis=0, concat_axis=0, tiled=True)]
  transfers between devices with their start and end apart: 18 -> 23, of which waited for: 9 -> 10; matrix products, arithmetic and copies ran while one was open for 2% -> 5% of each run, Pallas kernels for 3% -> 6%
where the time goes in v5:
time: 123 us
  waiting for transfers between devices  38.2 us (31%)
  starting transfers between devices  34.6 us (28%)
  blocking collectives  17.5 us (14%)
  Pallas kernels  16 us (13%)
  local copies, waits for them, and re-layouts  12.2 us (10%)
  other arithmetic  3.9 us (3%)
    ppermute x20, waiting for transfers between devices, swap(): return lax.ppermute(value, axis, [(i, i ^ j) for i in range(n)])  34 us
    ppermute x20, starting transfers between devices, swap(): return lax.ppermute(value, axis, [(i, i ^ j) for i in range(n)])  23.8 us
    all_to_all x1, blocking collectives, exchange(): return lax.all_to_all(value, 'seq', split_axis=0, concat_axis=0, tiled=True)  17.5 us
    unnamed x40, local copies, waits for them, and re-layouts  7.8 us
    all_to_all x2, starting transfers between devices, exchange_half(): lax.all_to_all(value, 'seq', split_axis=0, concat_axis=0, axis_index_grou...  7.09 us
    pallas_call x1, Pallas kernels, mlp(): pl.pallas_call(kernel, in_specs=[sspec()] + [vspec()] * (8 + n // 2), out...  4.51 us
    all_to_all x1, starting transfers between devices, exchange(): return lax.all_to_all(value, 'seq', split_axis=0, concat_axis=0, tiled=True)  3.72 us
    all_to_all x2, waiting for transfers between devices, exchange_half(): lax.all_to_all(value, 'seq', split_axis=0, concat_axis=0, axis_index_grou...  2.89 us
  transfers between devices with their start and end apart: 23, of which 10 were waited for; matrix products, arithmetic and copies ran while one was open for 5% of the time, Pallas kernels for 6%

profile of v5, /device:TPU:0, one launch (start us, length us, event | category | flops | bytes accessed | tf_op | source)
XLA Modules:
  0.0 122.7 jit_solution(11777172534950243807)
XLA Ops:
  1.8 4.1 %collective-permute-start = (bf16[640,128]{1,0:T(8,128)(2,1)S(1)}, bf16[640,128]{1,0:T(8,128)(2,1)S(1)}, u32[]{:S(2)}, u32[]{:S(2)}) collective-permute-start(bf16[640,128]{1,0:T(8,128)(2,1)S(1)} %pad_maximum_fusion.4), channel_id=1, source_target_pairs={{0,8},{2,10},{4,12},{6,14},{8,0},{10,2},{12,4},{14,6},{1,9},{3,11}... | collective-permute-start | bytes 491528 | tf_op jit(solution)/shard_map/ppermute | solution.py:550
  8.1 2.5 %shard_map.65 = (bf16[1216,128]{1,0:T(8,128)(2,1)S(1)}, bf16[1216,128]{1,0:T(8,128)(2,1)S(1)}, bf16[1216,128]{1,0:T(8,128)(2,1)S(1)}, bf16[1216,128]{1,0:T(8,128)(2,1)S(1)}, bf16[4,256,128]{2,1,0:T(8,128)(2,1)S(1)}) custom-call(s32[3]{0:T(128)S(1)} %pad_add_fusion.rank_ref.scalars, bf16[8,192,128]{2,1,0:T(8,128)(2,1)S(1)} %bitcast.32, ...), custom_call_target="tpu_custom_call" | custom-call | tf_op jit(solution)/shard_map/pallas_call | solution.py:312
  11.3 1.5 %collective-permute-start.2 = (bf16[1216,128]{1,0:T(8,128)(2,1)S(1)}, bf16[1216,128]{1,0:T(8,128)(2,1)S(1)}, u32[]{:S(2)}, u32[]{:S(2)}) collective-permute-start(bf16[1216,128]{1,0:T(8,128)(2,1)S(1)} %get-tuple-element.37), channel_id=1, source_target_pairs={{0,2},{2,0},{4,6},{6,4},{8,10},{10,8},{12,14},{14,12},{1,3},{3,1},... | collective-permute-start | bytes 933896 | tf_op jit(solution)/shard_map/ppermute | solution.py:550
  12.8 1.6 %collective-permute-start.3 = (bf16[1216,128]{1,0:T(8,128)(2,1)S(1)}, bf16[1216,128]{1,0:T(8,128)(2,1)S(1)}, u32[]{:S(2)}, u32[]{:S(2)}) collective-permute-start(bf16[1216,128]{1,0:T(8,128)(2,1)S(1)} %get-tuple-element.38), channel_id=1, source_target_pairs={{0,4},{2,6},{4,0},{6,2},{8,12},{10,14},{12,8},{14,10},{1,5},{3,7},... | collective-permute-start | bytes 933896 | tf_op jit(solution)/shard_map/ppermute | solution.py:550
  16.2 2.0 %shard_map.64 = bf16[640,128]{1,0:T(8,128)(2,1)} custom-call(s32[3]{0:T(128)S(1)} %pad_add_fusion.rank_ref.scalars, s32[64,1]{1,0:T(8,128)S(1)} %copy.8.keep_ref, bf16[160,1024]{1,0:T(8,128)(2,1)S(1)} %reshape.18.patches_ref), custom_call_target="tpu_custom_call" | custom-call | tf_op jit(solution)/shard_map/pallas_call | solution.py:222
  18.2 3.7 %all-to-all-start = ((bf16[8,80,128]{2,1,0:T(8,128)(2,1)}), bf16[8,80,128]{2,1,0:T(8,128)(2,1)S(1)}, u32[]{:S(2)}, u32[]{:S(2)}) async-start(bf16[8,80,128]{2,1,0:T(8,128)(2,1)} %bitcast.6), calls=%async_computation | async-start | bytes 327680 | tf_op jit(solution)/shard_map/all_to_all | solution.py:554
  21.9 1.5 %collective-permute-start.1 = (bf16[640,128]{1,0:T(8,128)(2,1)S(1)}, bf16[640,128]{1,0:T(8,128)(2,1)S(1)}, u32[]{:S(2)}, u32[]{:S(2)}) collective-permute-start(bf16[640,128]{1,0:T(8,128)(2,1)S(1)} %collective-permute-done.mine_ref), channel_id=1, source_target_pairs={{0,16},{16,0},{1,17},{17,1},{2,18},{18,2},{3,19},{19,3},{4,20},{20... | collective-permute-start | bytes 491528 | tf_op jit(solution)/shard_map/ppermute | solution.py:550
  23.4 6.4 %collective-permute-done.4.refs_3_ = bf16[1216,128]{1,0:T(8,128)(2,1)S(1)} collective-permute-done((bf16[1216,128]{1,0:T(8,128)(2,1)S(1)}, bf16[1216,128]{1,0:T(8,128)(2,1)S(1)}, u32[]{:S(2)}, u32[]{:S(2)}) %collective-permute-start.4) | collective-permute-done | bytes 311328 | tf_op jit(solution)/shard_map/ppermute | solution.py:550
  29.8 1.3 %all-to-all-done = bf16[8,80,128]{2,1,0:T(8,128)(2,1)S(1)} async-done(((bf16[8,80,128]{2,1,0:T(8,128)(2,1)}), bf16[8,80,128]{2,1,0:T(8,128)(2,1)S(1)}, u32[]{:S(2)}, u32[]{:S(2)}) %all-to-all-start) | async-done | bytes 163872 | tf_op jit(solution)/shard_map/all_to_all | solution.py:554
  32.0 2.4 %collective-permute-start.5 = (bf16[256,128]{1,0:T(8,128)(2,1)S(1)}, bf16[256,128]{1,0:T(8,128)(2,1)S(1)}, u32[]{:S(2)}, u32[]{:S(2)}) collective-permute-start(bf16[256,128]{1,0:T(8,128)(2,1)S(1)} %shard_map.66.owned_ref), channel_id=1, source_target_pairs={{0,8},{2,10},{4,12},{6,14},{8,0},{10,2},{12,4},{14,6},{1,9},{3,11}... | collective-permute-start | bytes 196616 | tf_op jit(solution)/shard_map/ppermute | solution.py:550
  34.4 3.7 %collective-permute-done.5.across_ref = bf16[256,128]{1,0:T(8,128)(2,1)S(1)} collective-permute-done((bf16[256,128]{1,0:T(8,128)(2,1)S(1)}, bf16[256,128]{1,0:T(8,128)(2,1)S(1)}, u32[]{:S(2)}, u32[]{:S(2)}) %collective-permute-start.5) | collective-permute-done | bytes 65568 | tf_op jit(solution)/shard_map/ppermute | solution.py:550
  38.1 1.5 %shard_map.67 = bf16[4,704,128]{2,1,0:T(8,128)(2,1)} custom-call(s32[3]{0:T(128)S(1)} %pad_add_fusion.rank_ref.scalars, bf16[256,128]{1,0:T(8,128)(2,1)S(1)} %shard_map.66.owned_ref, bf16[256,128]{1,0:T(8,128)(2,1)S(1)} %collective-permute-done.5.across_ref, bf16[640,128]{1,0:T(8,128)(2,1)S(1)} %collective-permute-done.mine_ref, ...), custom_call_target="tpu_custom_call" | custom-call | tf_op jit(solution)/shard_map/pallas_call | solution.py:339
  39.6 3.6 %all-to-all-start.1 = ((bf16[4,704,128]{2,1,0:T(8,128)(2,1)}), bf16[4,704,128]{2,1,0:T(8,128)(2,1)S(1)}, u32[]{:S(2)}, u32[]{:S(2)}) async-start(bf16[4,704,128]{2,1,0:T(8,128)(2,1)} %shard_map.67), calls=%async_computation.1 | async-start | bytes 1441792 | tf_op jit(solution)/shard_map/all_to_all | solution.py:560
  43.2 1.6 %collective-permute-start.6 = (bf16[4,256,128]{2,1,0:T(8,128)(2,1)S(1)}, bf16[4,256,128]{2,1,0:T(8,128)(2,1)}, u32[]{:S(2)}, u32[]{:S(2)}) collective-permute-start(bf16[4,256,128]{2,1,0:T(8,128)(2,1)S(1)} %copy-done.14), channel_id=1, source_target_pairs={{0,8},{2,10},{4,12},{6,14},{8,0},{10,2},{12,4},{14,6},{1,9},{3,11}... | collective-permute-start | bytes 786440 | tf_op jit(solution)/shard_map/ppermute | solution.py:550
  44.9 8.8 %collective-permute-done.6 = bf16[4,256,128]{2,1,0:T(8,128)(2,1)} collective-permute-done((bf16[4,256,128]{2,1,0:T(8,128)(2,1)S(1)}, bf16[4,256,128]{2,1,0:T(8,128)(2,1)}, u32[]{:S(2)}, u32[]{:S(2)}) %collective-permute-start.6) | collective-permute-done | bytes 262176 | tf_op jit(solution)/shard_map/ppermute | solution.py:550
  53.7 2.9 %all-to-all-done.1.mine_ref = bf16[4,704,128]{2,1,0:T(8,128)(2,1)S(1)} async-done(((bf16[4,704,128]{2,1,0:T(8,128)(2,1)}), bf16[4,704,128]{2,1,0:T(8,128)(2,1)S(1)}, u32[]{:S(2)}, u32[]{:S(2)}) %all-to-all-start.1) | async-done | bytes 720928 | tf_op jit(solution)/shard_map/all_to_all | solution.py:560
  58.8 2.9 %collective-permute-start.11 = (bf16[512,128]{1,0:T(8,128)(2,1)}, bf16[512,128]{1,0:T(8,128)(2,1)}, u32[]{:S(2)}, u32[]{:S(2)}) collective-permute-start(bf16[512,128]{1,0:T(8,128)(2,1)} %pad_maximum_fusion.5), channel_id=1, source_target_pairs={{0,6},{2,4},{4,2},{6,0},{8,14},{10,12},{12,10},{14,8},{1,7},{3,5},... | collective-permute-start | bytes 393224 | tf_op jit(solution)/shard_map/ppermute | solution.py:550
  61.8 1.3 %collective-permute-start.9 = (bf16[512,128]{1,0:T(8,128)(2,1)}, bf16[512,128]{1,0:T(8,128)(2,1)}, u32[]{:S(2)}, u32[]{:S(2)}) collective-permute-start(bf16[512,128]{1,0:T(8,128)(2,1)} %pad_maximum_fusion.5), channel_id=1, source_target_pairs={{0,2},{2,0},{4,6},{6,4},{8,10},{10,8},{12,14},{14,12},{1,3},{3,1},... | collective-permute-start | bytes 393224 | tf_op jit(solution)/shard_map/ppermute | solution.py:550
  63.0 1.5 %collective-permute-start.18 = (bf16[4,256,128]{2,1,0:T(8,128)(2,1)}, bf16[4,256,128]{2,1,0:T(8,128)(2,1)S(1)}, u32[]{:S(2)}, u32[]{:S(2)}) collective-permute-start(bf16[4,256,128]{2,1,0:T(8,128)(2,1)} %collective-permute-done.6), channel_id=1, source_target_pairs={{0,16},{16,0},{1,17},{17,1},{2,18},{18,2},{3,19},{19,3},{4,20},{20... | collective-permute-start | bytes 786440 | tf_op jit(solution)/shard_map/ppermute | solution.py:550
  64.5 2.7 %shard_map.68 = (bf16[512,1024]{1,0:T(8,128)(2,1)S(1)}, bf16[64,512]{1,0:T(8,128)(2,1)S(1)}) custom-call(s32[3]{0:T(128)S(1)} %pad_add_fusion.rank_ref.scalars, bf16[4,704,128]{2,1,0:T(8,128)(2,1)S(1)} %all-to-all-done.1.mine_ref, bf16[4,512,128]{2,1,0:T(8,128)(2,1)S(1)} %collective-permute-done.7.other_ref, ...), custom_call_target="tpu_custom_call" | custom-call | flops 30000001024 | bytes 1048576 | tf_op jit(solution)/shard_map/pallas_call | solution.py:403
  67.7 3.7 %collective-permute-done.18 = bf16[4,256,128]{2,1,0:T(8,128)(2,1)S(1)} collective-permute-done((bf16[4,256,128]{2,1,0:T(8,128)(2,1)}, bf16[4,256,128]{2,1,0:T(8,128)(2,1)S(1)}, u32[]{:S(2)}, u32[]{:S(2)}) %collective-permute-start.18) | collective-permute-done | bytes 262176 | tf_op jit(solution)/shard_map/ppermute | solution.py:550
  71.4 1.8 %pad_maximum_fusion.3 = bf16[4,512,128]{2,1,0:T(8,128)(2,1)} fusion(bf16[4,256,128]{2,1,0:T(8,128)(2,1)S(1)} %collective-permute-done.18, bf16[4,256,128]{2,1,0:T(8,128)(2,1)} %collective-permute-done.6), kind=kLoop, calls=%fused_computation.3 | loop fusion | flops 1048576 | bytes 1048576 | tf_op jit(solution)/shard_map/concatenate | solution.py:617
  73.2 3.5 %all-to-all-start.2 = ((bf16[4,512,128]{2,1,0:T(8,128)(2,1)}), bf16[4,512,128]{2,1,0:T(8,128)(2,1)S(1)}, u32[]{:S(2)}, u32[]{:S(2)}) async-start(bf16[4,512,128]{2,1,0:T(8,128)(2,1)} %pad_maximum_fusion.3), calls=%async_computation.2 | async-start | bytes 1048576 | tf_op jit(solution)/shard_map/all_to_all | solution.py:560
  76.8 2.0 %collective-permute-start.13 = (bf16[2,64,512]{2,1,0:T(8,128)(2,1)S(1)}, bf16[2,64,512]{2,1,0:T(8,128)(2,1)S(1)}, u32[]{:S(2)}, u32[]{:S(2)}) collective-permute-start(bf16[2,64,512]{2,1,0:T(8,128)(2,1)S(1)} %get-tuple-element.64), channel_id=1, source_target_pairs={{0,4},{2,6},{4,0},{6,2},{8,12},{10,14},{12,8},{14,10},{1,5},{3,7},... | collective-permute-start | bytes 393224 | tf_op jit(solution)/shard_map/ppermute | solution.py:550
  78.8 1.5 %collective-permute-start.12 = (bf16[2,64,512]{2,1,0:T(8,128)(2,1)S(1)}, bf16[2,64,512]{2,1,0:T(8,128)(2,1)S(1)}, u32[]{:S(2)}, u32[]{:S(2)}) collective-permute-start(bf16[2,64,512]{2,1,0:T(8,128)(2,1)S(1)} %get-tuple-element.64), channel_id=1, source_target_pairs={{0,2},{2,0},{4,6},{6,4},{8,10},{10,8},{12,14},{14,12},{1,3},{3,1},... | collective-permute-start | bytes 393224 | tf_op jit(solution)/shard_map/ppermute | solution.py:550
  82.2 6.1 %collective-permute-done.13 = bf16[2,64,512]{2,1,0:T(8,128)(2,1)S(1)} collective-permute-done((bf16[2,64,512]{2,1,0:T(8,128)(2,1)S(1)}, bf16[2,64,512]{2,1,0:T(8,128)(2,1)S(1)}, u32[]{:S(2)}, u32[]{:S(2)}) %collective-permute-start.13) | collective-permute-done | bytes 131104 | tf_op jit(solution)/shard_map/ppermute | solution.py:550
  88.4 2.3 %collective-permute-done.14 = bf16[2,64,512]{2,1,0:T(8,128)(2,1)S(1)} collective-permute-done((bf16[2,64,512]{2,1,0:T(8,128)(2,1)S(1)}, bf16[2,64,512]{2,1,0:T(8,128)(2,1)S(1)}, u32[]{:S(2)}, u32[]{:S(2)}) %collective-permute-start.14) | collective-permute-done | bytes 131104 | tf_op jit(solution)/shard_map/ppermute | solution.py:550
  91.6 1.2 collective-permute-done.15.b
  96.8 4.5 %shard_map.69 = (f32[64,512]{1,0:T(8,128)S(1)}, f32[512,512]{1,0:T(8,128)S(1)}, bf16[512,512]{1,0:T(8,128)(2,1)S(1)}) custom-call(s32[3]{0:T(128)S(1)} %pad_add_fusion.rank_ref.scalars, bf16[512,1024]{1,0:T(8,128)(2,1)S(1)} %get-tuple-element.49.tokens, bf16[4,2,64,512]{3,2,1,0:T(8,128)(2,1)S(1)} %pad_maximum_fusion.a, ...), custom_call_target="tpu_custom_call" | custom-call | tf_op jit(solution)/shard_map/pallas_call | solution.py:493
  101.5 1.8 %collective-permute-done.19.got_ref = bf16[512,512]{1,0:T(8,128)(2,1)S(1)} collective-permute-done((bf16[512,512]{1,0:T(8,128)(2,1)S(1)}, bf16[512,512]{1,0:T(8,128)(2,1)S(1)}, u32[]{:S(2)}, u32[]{:S(2)}) %collective-permute-start.19) | collective-permute-done | bytes 524320 | tf_op jit(solution)/shard_map/ppermute | solution.py:550
  103.9 17.5 %all_to_all.27.terms_ref = bf16[8,64,512]{2,1,0:T(8,128)(2,1)S(1)} all-to-all(bf16[8,64,512]{2,1,0:T(8,128)(2,1)S(1)} %bitcast.33), channel_id=1, replica_groups=mesh['groups'=2,'seq'=8,'head'=2] {'seq'}, dimensions={0} | all-to-all | bytes 1048576 | tf_op jit(solution)/shard_map/all_to_all | solution.py:554
  121.4 1.2 %shard_map.71 = bf16[64,512]{1,0:T(8,128)(2,1)} custom-call(s32[3]{0:T(128)S(1)} %pad_add_fusion.rank_ref.scalars, f32[64,512]{1,0:T(8,128)S(1)} %get-tuple-element.61.base_ref, bf16[8,64,512]{2,1,0:T(8,128)(2,1)S(1)} %all_to_all.27.terms_ref), custom_call_target="tpu_custom_call" | custom-call | tf_op jit(solution)/shard_map/pallas_call | solution.py:539
  (81 shorter events, 17.8 us)
Async XLA Ops:
  0.0 6.0 %copy-start.6 = (bf16[128,8,192]{0,2,1:T(8,128)(2,1)S(1)}, bf16[128,8,192]{0,2,1:T(8,128)(2,1)}, u32[]{:S(2)}) copy-start(bf16[128,8,192]{0,2,1:T(8,128)(2,1)} %param.8) | copy-start | bytes 1179652
  1.8 4.2 %copy-start.12 = (bf16[512,128]{1,0:T(8,128)(2,1)S(1)}, bf16[512,128]{1,0:T(8,128)(2,1)}, u32[]{:S(2)}) copy-start(bf16[512,128]{1,0:T(8,128)(2,1)} %out_weight_ref.1) | copy-start | bytes 393220
  1.8 16.4 %collective-permute-start = (bf16[640,128]{1,0:T(8,128)(2,1)S(1)}, bf16[640,128]{1,0:T(8,128)(2,1)S(1)}, u32[]{:S(2)}, u32[]{:S(2)}) collective-permute-start(bf16[640,128]{1,0:T(8,128)(2,1)S(1)} %pad_maximum_fusion.4), channel_id=1, source_target_pairs={{0,8},{2,10},{4,12},{6,14},{8,0},{10,2},{12,4},{14,6},{1,9},{3,11}... | collective-permute-start | bytes 491528 | tf_op jit(solution)/shard_map/ppermute | solution.py:550
  11.3 12.1 %collective-permute-start.2 = (bf16[1216,128]{1,0:T(8,128)(2,1)S(1)}, bf16[1216,128]{1,0:T(8,128)(2,1)S(1)}, u32[]{:S(2)}, u32[]{:S(2)}) collective-permute-start(bf16[1216,128]{1,0:T(8,128)(2,1)S(1)} %get-tuple-element.37), channel_id=1, source_target_pairs={{0,2},{2,0},{4,6},{6,4},{8,10},{10,8},{12,14},{14,12},{1,3},{3,1},... | collective-permute-start | bytes 933896 | tf_op jit(solution)/shard_map/ppermute | solution.py:550
  12.8 10.6 %collective-permute-start.3 = (bf16[1216,128]{1,0:T(8,128)(2,1)S(1)}, bf16[1216,128]{1,0:T(8,128)(2,1)S(1)}, u32[]{:S(2)}, u32[]{:S(2)}) collective-permute-start(bf16[1216,128]{1,0:T(8,128)(2,1)S(1)} %get-tuple-element.38), channel_id=1, source_target_pairs={{0,4},{2,6},{4,0},{6,2},{8,12},{10,14},{12,8},{14,10},{1,5},{3,7},... | collective-permute-start | bytes 933896 | tf_op jit(solution)/shard_map/ppermute | solution.py:550
  14.4 15.4 %collective-permute-start.4 = (bf16[1216,128]{1,0:T(8,128)(2,1)S(1)}, bf16[1216,128]{1,0:T(8,128)(2,1)S(1)}, u32[]{:S(2)}, u32[]{:S(2)}) collective-permute-start(bf16[1216,128]{1,0:T(8,128)(2,1)S(1)} %get-tuple-element.39), channel_id=1, source_target_pairs={{0,6},{2,4},{4,2},{6,0},{8,14},{10,12},{12,10},{14,8},{1,7},{3,5},... | collective-permute-start | bytes 933896 | tf_op jit(solution)/shard_map/ppermute | solution.py:550
  18.2 12.9 %all-to-all-start = ((bf16[8,80,128]{2,1,0:T(8,128)(2,1)}), bf16[8,80,128]{2,1,0:T(8,128)(2,1)S(1)}, u32[]{:S(2)}, u32[]{:S(2)}) async-start(bf16[8,80,128]{2,1,0:T(8,128)(2,1)} %bitcast.6), calls=%async_computation | async-start | bytes 327680 | tf_op jit(solution)/shard_map/all_to_all | solution.py:554
  21.9 7.9 %collective-permute-start.1 = (bf16[640,128]{1,0:T(8,128)(2,1)S(1)}, bf16[640,128]{1,0:T(8,128)(2,1)S(1)}, u32[]{:S(2)}, u32[]{:S(2)}) collective-permute-start(bf16[640,128]{1,0:T(8,128)(2,1)S(1)} %collective-permute-done.mine_ref), channel_id=1, source_target_pairs={{0,16},{16,0},{1,17},{17,1},{2,18},{18,2},{3,19},{19,3},{4,20},{20... | collective-permute-start | bytes 491528 | tf_op jit(solution)/shard_map/ppermute | solution.py:550
  23.4 41.1 %copy-start = (bf16[1216,128]{1,0:T(8,128)(2,1)}, bf16[1216,128]{1,0:T(8,128)(2,1)S(1)}, u32[]{:S(2)}) copy-start(bf16[1216,128]{1,0:T(8,128)(2,1)S(1)} %collective-permute-done.2.refs_1_) | copy-start | bytes 933892
  23.4 41.1 %copy-start.2 = (bf16[1216,128]{1,0:T(8,128)(2,1)}, bf16[1216,128]{1,0:T(8,128)(2,1)S(1)}, u32[]{:S(2)}) copy-start(bf16[1216,128]{1,0:T(8,128)(2,1)S(1)} %collective-permute-done.3.refs_2_) | copy-start | bytes 933892
  29.8 34.7 %copy-start.4 = (bf16[1216,128]{1,0:T(8,128)(2,1)}, bf16[1216,128]{1,0:T(8,128)(2,1)S(1)}, u32[]{:S(2)}) copy-start(bf16[1216,128]{1,0:T(8,128)(2,1)S(1)} %collective-permute-done.4.refs_3_) | copy-start | bytes 933892
  29.8 15.1 %copy-start.11 = (bf16[640,128]{1,0:T(8,128)(2,1)}, bf16[640,128]{1,0:T(8,128)(2,1)S(1)}, u32[]{:S(2)}) copy-start(bf16[640,128]{1,0:T(8,128)(2,1)S(1)} %collective-permute-done.1.other_ref) | copy-start | bytes 491524
  32.0 6.1 %collective-permute-start.5 = (bf16[256,128]{1,0:T(8,128)(2,1)S(1)}, bf16[256,128]{1,0:T(8,128)(2,1)S(1)}, u32[]{:S(2)}, u32[]{:S(2)}) collective-permute-start(bf16[256,128]{1,0:T(8,128)(2,1)S(1)} %shard_map.66.owned_ref), channel_id=1, source_target_pairs={{0,8},{2,10},{4,12},{6,14},{8,0},{10,2},{12,4},{14,6},{1,9},{3,11}... | collective-permute-start | bytes 196616 | tf_op jit(solution)/shard_map/ppermute | solution.py:550
  39.6 17.0 %all-to-all-start.1 = ((bf16[4,704,128]{2,1,0:T(8,128)(2,1)}), bf16[4,704,128]{2,1,0:T(8,128)(2,1)S(1)}, u32[]{:S(2)}, u32[]{:S(2)}) async-start(bf16[4,704,128]{2,1,0:T(8,128)(2,1)} %shard_map.67), calls=%async_computation.1 | async-start | bytes 1441792 | tf_op jit(solution)/shard_map/all_to_all | solution.py:560
  43.2 10.5 %collective-permute-start.6 = (bf16[4,256,128]{2,1,0:T(8,128)(2,1)S(1)}, bf16[4,256,128]{2,1,0:T(8,128)(2,1)}, u32[]{:S(2)}, u32[]{:S(2)}) collective-permute-start(bf16[4,256,128]{2,1,0:T(8,128)(2,1)S(1)} %copy-done.14), channel_id=1, source_target_pairs={{0,8},{2,10},{4,12},{6,14},{8,0},{10,2},{12,4},{14,6},{1,9},{3,11}... | collective-permute-start | bytes 786440 | tf_op jit(solution)/shard_map/ppermute | solution.py:550
  44.9 11.8 %slice-start = ((bf16[640,128]{1,0:T(8,128)(2,1)}), bf16[256,128]{1,0:T(8,128)(2,1)S(1)}, s32[]{:S(2)}) async-start(bf16[640,128]{1,0:T(8,128)(2,1)} %copy-done.11), calls=%async_computation.4 | async-start | bytes 131072 | tf_op jit(solution)/shard_map/slice | solution.py:611
  56.6 7.9 %collective-permute-start.7 = (bf16[4,512,128]{2,1,0:T(8,128)(2,1)S(1)}, bf16[4,512,128]{2,1,0:T(8,128)(2,1)S(1)}, u32[]{:S(2)}, u32[]{:S(2)}) collective-permute-start(bf16[4,512,128]{2,1,0:T(8,128)(2,1)S(1)} %slice.21), channel_id=1, source_target_pairs={{0,1},{1,0},{2,3},{3,2},{4,5},{5,4},{6,7},{7,6},{8,9},{9,8},{10,11... | collective-permute-start | bytes 1572872 | tf_op jit(solution)/shard_map/ppermute | solution.py:550
  58.8 17.9 %collective-permute-start.11 = (bf16[512,128]{1,0:T(8,128)(2,1)}, bf16[512,128]{1,0:T(8,128)(2,1)}, u32[]{:S(2)}, u32[]{:S(2)}) collective-permute-start(bf16[512,128]{1,0:T(8,128)(2,1)} %pad_maximum_fusion.5), channel_id=1, source_target_pairs={{0,6},{2,4},{4,2},{6,0},{8,14},{10,12},{12,10},{14,8},{1,7},{3,5},... | collective-permute-start | bytes 393224 | tf_op jit(solution)/shard_map/ppermute | solution.py:550
  61.7 14.9 %collective-permute-start.10 = (bf16[512,128]{1,0:T(8,128)(2,1)}, bf16[512,128]{1,0:T(8,128)(2,1)}, u32[]{:S(2)}, u32[]{:S(2)}) collective-permute-start(bf16[512,128]{1,0:T(8,128)(2,1)} %pad_maximum_fusion.5), channel_id=1, source_target_pairs={{0,4},{2,6},{4,0},{6,2},{8,12},{10,14},{12,8},{14,10},{1,5},{3,7},... | collective-permute-start | bytes 393224 | tf_op jit(solution)/shard_map/ppermute | solution.py:550
  61.8 14.9 %collective-permute-start.9 = (bf16[512,128]{1,0:T(8,128)(2,1)}, bf16[512,128]{1,0:T(8,128)(2,1)}, u32[]{:S(2)}, u32[]{:S(2)}) collective-permute-start(bf16[512,128]{1,0:T(8,128)(2,1)} %pad_maximum_fusion.5), channel_id=1, source_target_pairs={{0,2},{2,0},{4,6},{6,4},{8,10},{10,8},{12,14},{14,12},{1,3},{3,1},... | collective-permute-start | bytes 393224 | tf_op jit(solution)/shard_map/ppermute | solution.py:550
  63.0 8.3 %collective-permute-start.18 = (bf16[4,256,128]{2,1,0:T(8,128)(2,1)}, bf16[4,256,128]{2,1,0:T(8,128)(2,1)S(1)}, u32[]{:S(2)}, u32[]{:S(2)}) collective-permute-start(bf16[4,256,128]{2,1,0:T(8,128)(2,1)} %collective-permute-done.6), channel_id=1, source_target_pairs={{0,16},{16,0},{1,17},{17,1},{2,18},{18,2},{3,19},{19,3},{4,20},{20... | collective-permute-start | bytes 786440 | tf_op jit(solution)/shard_map/ppermute | solution.py:550
  67.2 9.5 %collective-permute-start.8 = (bf16[64,512]{1,0:T(8,128)(2,1)S(1)}, bf16[64,512]{1,0:T(8,128)(2,1)S(1)}, u32[]{:S(2)}, u32[]{:S(2)}) collective-permute-start(bf16[64,512]{1,0:T(8,128)(2,1)S(1)} %get-tuple-element.50), channel_id=1, source_target_pairs={{0,8},{2,10},{4,12},{6,14},{8,0},{10,2},{12,4},{14,6},{1,9},{3,11}... | collective-permute-start | bytes 196616 | tf_op jit(solution)/shard_map/ppermute | solution.py:550
  71.4 9.0 %copy-start.18 = (bf16[1,512,128]{2,1,0:T(8,128)(2,1)S(1)}, bf16[1,512,128]{2,1,0:T(8,128)(2,1)}, u32[]{:S(2)}) copy-start(bf16[1,512,128]{2,1,0:T(8,128)(2,1)} %get-tuple-element.66) | copy-start | bytes 393220
  73.2 18.4 %all-to-all-start.2 = ((bf16[4,512,128]{2,1,0:T(8,128)(2,1)}), bf16[4,512,128]{2,1,0:T(8,128)(2,1)S(1)}, u32[]{:S(2)}, u32[]{:S(2)}) async-start(bf16[4,512,128]{2,1,0:T(8,128)(2,1)} %pad_maximum_fusion.3), calls=%async_computation.2 | async-start | bytes 1048576 | tf_op jit(solution)/shard_map/all_to_all | solution.py:560
  76.7 3.6 %copy-start.15 = (bf16[1,512,128]{2,1,0:T(8,128)(2,1)S(1)}, bf16[1,512,128]{2,1,0:T(8,128)(2,1)}, u32[]{:S(2)}) copy-start(bf16[1,512,128]{2,1,0:T(8,128)(2,1)} %get-tuple-element.67) | copy-start | bytes 393220
  76.8 11.6 %collective-permute-start.13 = (bf16[2,64,512]{2,1,0:T(8,128)(2,1)S(1)}, bf16[2,64,512]{2,1,0:T(8,128)(2,1)S(1)}, u32[]{:S(2)}, u32[]{:S(2)}) collective-permute-start(bf16[2,64,512]{2,1,0:T(8,128)(2,1)S(1)} %get-tuple-element.64), channel_id=1, source_target_pairs={{0,4},{2,6},{4,0},{6,2},{8,12},{10,14},{12,8},{14,10},{1,5},{3,7},... | collective-permute-start | bytes 393224 | tf_op jit(solution)/shard_map/ppermute | solution.py:550
  78.8 9.6 %collective-permute-start.12 = (bf16[2,64,512]{2,1,0:T(8,128)(2,1)S(1)}, bf16[2,64,512]{2,1,0:T(8,128)(2,1)S(1)}, u32[]{:S(2)}, u32[]{:S(2)}) collective-permute-start(bf16[2,64,512]{2,1,0:T(8,128)(2,1)S(1)} %get-tuple-element.64), channel_id=1, source_target_pairs={{0,2},{2,0},{4,6},{6,4},{8,10},{10,8},{12,14},{14,12},{1,3},{3,1},... | collective-permute-start | bytes 393224 | tf_op jit(solution)/shard_map/ppermute | solution.py:550
  80.3 10.4 %collective-permute-start.14 = (bf16[2,64,512]{2,1,0:T(8,128)(2,1)S(1)}, bf16[2,64,512]{2,1,0:T(8,128)(2,1)S(1)}, u32[]{:S(2)}, u32[]{:S(2)}) collective-permute-start(bf16[2,64,512]{2,1,0:T(8,128)(2,1)S(1)} %get-tuple-element.64), channel_id=1, source_target_pairs={{0,6},{2,4},{4,2},{6,0},{8,14},{10,12},{12,10},{14,8},{1,7},{3,5},... | collective-permute-start | bytes 393224 | tf_op jit(solution)/shard_map/ppermute | solution.py:550
  80.4 10.4 %collective-permute-start.16 = (bf16[4,512,128]{2,1,0:T(8,128)(2,1)S(1)}, bf16[4,512,128]{2,1,0:T(8,128)(2,1)S(1)}, u32[]{:S(2)}, u32[]{:S(2)}) collective-permute-start(bf16[4,512,128]{2,1,0:T(8,128)(2,1)S(1)} %pad_maximum_fusion.1.c), channel_id=1, source_target_pairs={{0,1},{1,0},{2,3},{3,2},{4,5},{5,4},{6,7},{7,6},{8,9},{9,8},{10,11... | collective-permute-start | bytes 1572872 | tf_op jit(solution)/shard_map/ppermute | solution.py:550
  81.7 10.0 %collective-permute-start.17 = (bf16[4,512,128]{2,1,0:T(8,128)(2,1)S(1)}, bf16[4,512,128]{2,1,0:T(8,128)(2,1)}, u32[]{:S(2)}, u32[]{:S(2)}) collective-permute-start(bf16[4,512,128]{2,1,0:T(8,128)(2,1)S(1)} %pad_maximum_fusion.2.e), channel_id=1, source_target_pairs={{0,1},{1,0},{2,3},{3,2},{4,5},{5,4},{6,7},{7,6},{8,9},{9,8},{10,11... | collective-permute-start | bytes 1572872 | tf_op jit(solution)/shard_map/ppermute | solution.py:550
  90.7 2.1 %collective-permute-start.15 = (bf16[4,2,64,512]{3,2,1,0:T(8,128)(2,1)S(1)}, bf16[4,2,64,512]{3,2,1,0:T(8,128)(2,1)}, u32[]{:S(2)}, u32[]{:S(2)}) collective-permute-start(bf16[4,2,64,512]{3,2,1,0:T(8,128)(2,1)S(1)} %pad_maximum_fusion.a), channel_id=1, source_target_pairs={{0,1},{1,0},{2,3},{3,2},{4,5},{5,4},{6,7},{7,6},{8,9},{9,8},{10,11... | collective-permute-start | bytes 1572872 | tf_op jit(solution)/shard_map/ppermute | solution.py:550
  101.3 2.0 %collective-permute-start.19 = (bf16[512,512]{1,0:T(8,128)(2,1)S(1)}, bf16[512,512]{1,0:T(8,128)(2,1)S(1)}, u32[]{:S(2)}, u32[]{:S(2)}) collective-permute-start(bf16[512,512]{1,0:T(8,128)(2,1)S(1)} %get-tuple-element.59), channel_id=1, source_target_pairs={{0,1},{1,0},{2,3},{3,2},{4,5},{5,4},{6,7},{7,6},{8,9},{9,8},{10,11... | collective-permute-start | bytes 1572872 | tf_op jit(solution)/shard_map/ppermute | solution.py:550
  (12 other events, 19.1 us)

commit v6 on v5

--- a/solution.py
+++ b/solution.py
@@ -11,7 +11,7 @@
 F32 = jnp.float32
 BF16 = jnp.bfloat16
 VMEM = pltpu.VMEM
-LIMIT = 32 * 1024 * 1024
+LIMIT = 24 * 1024 * 1024
 
 def layer_norm(matrix):
     average = jnp.mean(matrix, axis=-1, keepdims=True)
@@ -150,6 +150,24 @@
     return pl.BlockSpec(memory_space=pltpu.SMEM)
 
 
+def hspec():
+    return pl.BlockSpec(memory_space=pltpu.HBM)
+
+
+def run_copies(copies, sem, base=0):
+    started = [
+        pltpu.make_async_copy(src, dst, sem.at[base + i]) for i, (src, dst) in enumerate(copies)
+    ]
+    for copy in started:
+        copy.start()
+
+    def wait():
+        for copy in started:
+            copy.wait()
+
+    return wait
+
+
 def params():
     return pltpu.CompilerParams(vmem_limit_bytes=LIMIT)
 
@@ -296,13 +314,7 @@
         at = pl.ds(pl.multiple_of(dest * wide + part * units, 128), units)
         copies.append((up_ref.at[:, at], away_ref.at[j, pl.ds(0, rows)]))
         copies.append((down_ref.at[at], away_ref.at[j, pl.ds(rows, units)]))
-    started = []
-    for i, (src, dst) in enumerate(copies):
-        copy = pltpu.make_async_copy(src, dst, sem.at[i])
-        copy.start()
-        started.append(copy)
-    for copy in started:
-        copy.wait()
+    run_copies(copies, sem)()
 
 
 def pack(scalars, qkv, out_weight, up, down, n):
@@ -311,13 +323,42 @@
     away = struct((n // 2, up.shape[0] + wide // 2, 128))
     outs = pl.pallas_call(
         functools.partial(pack_kernel, n),
-        in_specs=[sspec()] + [aspec()] * 4,
-        out_specs=[aspec()] * (n // 2 + 1),
+        in_specs=[sspec()] + [hspec()] * 4,
+        out_specs=[hspec()] * (n // 2 + 1),
         out_shape=[near] * (n // 2) + [away],
         scratch_shapes=[pltpu.SemaphoreType.DMA((7 * n // 2,))],
         compiler_params=params(),
     )(scalars, qkv, out_weight, up, down)
     return list(outs[:-1]), outs[-1]
+
+
+def early_kernel(n, rank_ref, qkv_ref, out_weight_ref, heads_ref, rows_ref, sem):
+    rank, part = rank_ref[0], rank_ref[2]
+    half = n // 2
+    depth = heads_ref.shape[0] // half
+    long = rows_ref.shape[0]
+    copies = []
+    for d in range(half):
+        dest = (rank // half ^ 1) * half + d
+        at = pl.ds(pl.multiple_of(part * depth, 32), depth)
+        copies.append((qkv_ref.at[dest, at], heads_ref.at[pl.ds(d * depth, depth)]))
+    at = pl.ds(pl.multiple_of(part * long, 128), long)
+    copies.append((out_weight_ref.at[at], rows_ref))
+    run_copies(copies, sem)()
+
+
+def early_blocks(scalars, qkv, out_weight, n):
+    return pl.pallas_call(
+        functools.partial(early_kernel, n),
+        in_specs=[sspec()] + [hspec()] * 2,
+        out_specs=[aspec()] * 2,
+        out_shape=[
+            struct((n // 2 * qkv.shape[1] // 2, 128)),
+            struct((out_weight.shape[0] // 2, 128)),
+        ],
+        scratch_shapes=[pltpu.SemaphoreType.DMA((n // 2 + 1,))],
+        compiler_params=params(),
+    )(scalars, qkv, out_weight)
 
 
 def fan_kernel(rank_ref, owned_ref, across_ref, mine_ref, other_ref, out_ref):
@@ -356,12 +397,18 @@
 
 
 def attend_kernel(n, part, rank_ref, mine_ref, other_ref, *refs):
-    near, (tokens_ref, out_ref, weight_ref) = refs[: n // 2], refs[n // 2 :]
+    near, (tokens_ref, out_ref, weight_ref, sem) = refs[: n // 2], refs[n // 2 :]
     rank, half = rank_ref[0], rank_ref[1]
+    depth = weight_ref.shape[0]
+    copies = []
+    for j in range(n // 2):
+        to = pl.ds(pl.multiple_of((rank ^ j) * 128, 128), 128)
+        at = pl.ds(near[j].shape[0] - depth, depth)
+        copies.append((near[j].at[at], weight_ref.at[:, to]))
+    wait = run_copies(copies, sem)
     rows = other_ref.shape[1] // 2
     cuts = rows // part
     width = cuts * 128
-    depth = weight_ref.shape[0]
     for q in range(n // 2):
         for k in range(2):
             source = source_of(rank, n, q, k)
@@ -375,9 +422,8 @@
         source = source_of(rank, n, q, 1)
         to = pl.ds(pl.multiple_of(source * 128, 128), 128)
         weight_ref[:, to] = mine_ref[q, 2 * rows :]
-        to = pl.ds(pl.multiple_of((rank ^ q) * 128, 128), 128)
-        weight_ref[:, to] = near[q][near[q].shape[0] - depth :]
     normed = norm_rows(tokens_ref[...].astype(F32)).astype(BF16)
+    wait()
     projected = lax.dot_general(
         normed, weight_ref[...], (((1,), (1,)), ((), ())), preferred_element_type=F32
     ).astype(BF16)
@@ -402,66 +448,60 @@
     size = head_rows // 3
     return pl.pallas_call(
         functools.partial(attend_kernel, n, per_owner),
-        in_specs=[sspec()] + [vspec()] * (2 + n // 2),
+        in_specs=[sspec()] + [vspec()] * 2 + [aspec()] * (n // 2),
         out_specs=[vspec()] * 2,
         out_shape=[struct((length, depth)), struct((size, length))],
-        scratch_shapes=[VMEM((head_rows, n * 128), BF16)],
+        scratch_shapes=[
+            VMEM((head_rows, n * 128), BF16),
+            pltpu.SemaphoreType.DMA((n // 2,)),
+        ],
         compiler_params=params(),
         cost_estimate=cost(30),
     )(scalars, mine, other, *near)
 
 
-def mlp_kernel(
-    n,
-    rank_ref,
-    tokens_ref,
-    pieces,
-    outs_near,
-    outs_far,
-    near,
-    far_ref,
-    residual_ref,
-    keep_ref,
-    send_ref,
-    up_ref,
-    down_ref,
-    row_ref,
-    whole_ref,
-    joined_ref,
-):
+def mlp_kernel(n, rank_ref, tokens_ref, pieces, far, outs_far, near, near_other, outs, scratch):
+    residual_ref, keep_ref, send_ref = outs
+    up_ref, down_ref, row_ref, whole_ref, joined_ref, sem = scratch
     rank, half, group = rank_ref[0], rank_ref[1], rank_ref[2]
     block = up_ref.shape[0] // n
     wide = down_ref.shape[0]
     unit = wide // 2
     size = pieces[0].shape[2]
-    long = outs_near[0].shape[1]
-    rows = long // 2
+    rows = outs_far[0][0].shape[1]
+    first, later = [], []
     for j in range(n // 2):
         source = rank ^ j
         at = pl.ds(pl.multiple_of(source * block, block), block)
         to = pl.ds(pl.multiple_of(source * 128, 128), 128)
         for c in range(2):
-            up_ref[at, c * unit : (c + 1) * unit] = near[j][c * block : (c + 1) * block]
-        down_ref[:, to] = near[j][2 * block : 2 * block + wide]
-        for core in range(2):
-            whole_ref[core, :, to] = outs_near[core][j]
+            later.append(
+                (near[j].at[pl.ds(c * block, block)], up_ref.at[at, pl.ds(c * unit, unit)])
+            )
+        later.append((near[j].at[pl.ds(2 * block, wide)], down_ref.at[:, to]))
+        for core, refs in enumerate((near, near_other)):
+            first.append((refs[j].at[pl.ds(2 * block + wide, 2 * rows)], whole_ref.at[core, :, to]))
         source = source_of(rank, n, j, 1)
         at = pl.ds(pl.multiple_of(source * block, block), block)
         to = pl.ds(pl.multiple_of(source * 128, 128), 128)
         for c in range(2):
             units = pl.ds(pl.multiple_of((group ^ c) * unit, unit), unit)
-            high = c * (block + unit)
-            up_ref[at, units] = far_ref[j, high : high + block]
-            down_ref[units, to] = far_ref[j, high + block : high + block + unit]
+            later.append((far[c].at[j, pl.ds(0, block)], up_ref.at[at, units]))
+            later.append((far[c].at[j, pl.ds(block, unit)], down_ref.at[units, to]))
         source = rank ^ j ^ (n // 2)
         to = pl.ds(pl.multiple_of(source * 128, 128), 128)
         for core in range(2):
             for c in range(2):
                 at = pl.ds(pl.multiple_of((group ^ c) * rows, rows), rows)
-                whole_ref[core, at, to] = outs_far[core][j, c * rows : (c + 1) * rows]
+                first.append((outs_far[core][c].at[j], whole_ref.at[core, at, to]))
+    wait_first = run_copies(first, sem)
+    wait_later = run_copies(later, sem, len(first))
+    for j in range(n // 2):
+        for core in range(2):
             for k in range(2):
                 at = pl.ds(pl.multiple_of((rank ^ j ^ (k * n // 2)) * size, size), size)
                 joined_ref[core, at] = pieces[core][j, k]
+    wait_first()
     dims = (((0,), (0,)), ((), ()))
     row_ref[...] = (
         tokens_ref[...].astype(F32)
@@ -474,25 +514,30 @@
     other_cols = pl.ds(pl.multiple_of((1 - half) * width, width), width)
     residual_ref[...] = row_ref[pl.ds(pl.multiple_of(rank * part, part), part), my_cols]
     normed = norm_rows(row_ref[...]).astype(BF16)
+    wait_later()
     raw = jnp.dot(normed, up_ref[...], preferred_element_type=F32)
     hidden = (0.5 * raw * (1.0 + lax.erf(raw * math.sqrt(0.5)))).astype(BF16)
     keep_ref[...] = jnp.dot(hidden, down_ref[:, my_cols], preferred_element_type=F32)
     send_ref[...] = jnp.dot(hidden, down_ref[:, other_cols], preferred_element_type=F32).astype(BF16)
 
 
-def mlp(scalars, tokens, pieces, outs_near, outs_far, near, far, n):
+def mlp(scalars, tokens, pieces, far, outs_far, near, near_other, n):
     length, depth = tokens.shape
     width = depth // 2
-    wide = 2 * (far.shape[1] // 2 - depth // n)
+    wide = 2 * (far[0].shape[1] - depth // n)
     inner = n * pieces[0].shape[2]
-
-    def kernel(scalars, tokens, a, b, c, d, e, f, *refs):
-        near, (far, *refs) = refs[: n // 2], refs[n // 2 :]
-        mlp_kernel(n, scalars, tokens, (a, b), (c, d), (e, f), near, far, *refs)
+    half = n // 2
+
+    def kernel(scalars, tokens, a, b, c, d, e, f, g, h, *refs):
+        near, near_other = refs[:half], refs[half : 2 * half]
+        outs, scratch = refs[2 * half : 2 * half + 3], refs[2 * half + 3 :]
+        mlp_kernel(
+            n, scalars, tokens, (a, b), (c, d), ((e, f), (g, h)), near, near_other, outs, scratch
+        )
 
     return pl.pallas_call(
         kernel,
-        in_specs=[sspec()] + [vspec()] * (8 + n // 2),
+        in_specs=[sspec()] + [vspec()] * 3 + [aspec()] * (6 + n),
         out_specs=[vspec()] * 3,
         out_shape=[
             struct((length // n, width), F32),
@@ -505,9 +550,10 @@
             VMEM((length, depth), F32),
             VMEM((2, inner, depth), BF16),
             VMEM((2, inner, length), BF16),
+            pltpu.SemaphoreType.DMA((13 * half,)),
         ],
         compiler_params=params(),
-    )(scalars, tokens, *pieces, *outs_near, *outs_far, *near, far)
+    )(scalars, tokens, *pieces, *far, *outs_far[0], *outs_far[1], *near, *near_other)
 
 
 def join_kernel(rank_ref, keep_ref, got_ref, residual_ref, base_ref, out_ref):
@@ -573,62 +619,60 @@
     )
     scalars = jnp.stack([rank, head, group])
     half = n // 2
-    side = rank // half
     sup, depth = patches.shape[1], patches.shape[3]
     length = sup * n * 8 // 5
     per_owner = length // n
     half_width = depth // 2
     head_rows = qkv_weight.shape[2]
-    part_rows = head_rows // 2
-    out_rows = out_weight.shape[0] // 2
     capacity = (4 * sup + n - 1) // n
     keep_col = keep_list.reshape(-1, 1)
     flat = patches.reshape(4 * sup, depth)
     heads = qkv_weight.transpose(1, 2, 0)
 
-    qkv_away = lax.dynamic_slice(
-        heads, ((1 - side) * half, group * part_rows, 0), (half, part_rows, 128)
-    ).reshape(half * part_rows, 128)
-    out_away = lax.dynamic_slice_in_dim(out_weight, group * out_rows, out_rows, 0)
-    early = swap(jnp.concatenate([qkv_away, out_away]), "seq", half)
+    qkv_away, out_away = early_blocks(scalars, heads, out_weight, n)
+    qkv_mine = swap(qkv_away, "seq", half)
     slots = prep(scalars, keep_col, flat, n, sup, capacity)
-    slots, early = lax.optimization_barrier((slots, early))
-    near, mlp_away = pack(scalars, heads, out_weight, up_weight, down_weight, n)
+    slots, qkv_mine = lax.optimization_barrier((slots, qkv_mine))
     dealt = exchange(slots)
+    out_far = swap(after(out_away, slots), "seq", half)
+    qkv_other = swap(qkv_mine, "groups", 1)
+    blocks = lax.optimization_barrier((heads, out_weight, up_weight, down_weight, slots))[:4]
+    near, mlp_away = pack(scalars, *blocks, n)
     near = [near[0]] + [swap(near[j], "seq", j) for j in range(1, half)]
-    early_other = swap(early, "groups", 1)
-    dealt, early_other, *near = lax.optimization_barrier((dealt, early_other, *near))
+    dealt, out_far, qkv_other = lax.optimization_barrier((dealt, out_far, qkv_other))
     owned = pick(scalars, keep_col, dealt, n, sup, per_owner, capacity)
 
     across = swap(owned, "seq", half)
-    mlp_mine = swap(after(mlp_away, across), "seq", half)
-    got = exchange_half(fan(scalars, owned, across, early, early_other, head_rows, n))
-    got, mlp_mine = lax.optimization_barrier((got, mlp_mine))
+    out_far = after(out_far, owned)
+    outs_far = [out_far] + [swap(out_far, "seq", j) for j in range(1, half)]
+    across, *rest = lax.optimization_barrier((across, *outs_far, *near))
+    outs_far, near = rest[:half], rest[half:]
+
+    mlp_far = swap(after(mlp_away, across), "seq", half)
+    got = exchange_half(fan(scalars, owned, across, qkv_mine, qkv_other, head_rows, n))
+    far_mine = jnp.stack(outs_far)
+    far_other = swap(far_mine, "groups", 1)
+    got, mlp_far, far_other = lax.optimization_barrier((got, mlp_far, far_other))
 
     pieces = got[:, : got.shape[1] - head_rows]
     pieces_other = swap(pieces, "head", 1)
-    mlp_other = swap(mlp_mine, "groups", 1)
-    out_far = jnp.concatenate([early[half * part_rows :], early_other[half * part_rows :]])
-    out_far = after(out_far, got)
     tokens, attended = attend_fast(scalars, got, pieces_other, near, head_rows, per_owner, n)
 
-    outs_far = [out_far] + [swap(out_far, "seq", j) for j in range(1, half)]
     att_across = swap(attended, "seq", half)
-    mlp_far = exchange_half(jnp.concatenate([mlp_mine, mlp_other], axis=1))
-    att_across, *outs_far = lax.optimization_barrier((att_across, *outs_far))
+    mlp_mine = exchange_half(after(mlp_far, attended))
     pair = jnp.stack([attended, att_across])
     gathered = jnp.stack([pair] + [swap(pair, "seq", j) for j in range(1, half)])
-    outs_far = jnp.stack(outs_far)
-    top = near[0].shape[0] - head_rows - 2 * out_rows
-    outs_near = jnp.stack([block[top : top + 2 * out_rows] for block in near])
+    mlp_other = swap(mlp_mine, "groups", 1)
+    near_other = [swap(block, "head", 1) for block in after(tuple(near), attended)]
+    far_mine, far_other = after((far_mine, far_other), attended)
     residual, keep, send = mlp(
         scalars,
         tokens,
         (gathered, swap(gathered, "head", 1)),
-        (outs_near, swap(outs_near, "head", 1)),
-        (outs_far, swap(outs_far, "head", 1)),
+        (mlp_mine, mlp_other),
+        ((far_mine, far_other), (swap(far_mine, "head", 1), swap(far_other, "head", 1))),
         near,
-        mlp_far,
+        near_other,
         n,
     )
     sent = swap(send, "head", 1)

time: 123 us -> 128 us (1.041)
  starting transfers between devices: 34.6 us -> 43.7 us
  local copies, waits for them, and re-layouts: 12.2 us -> 8.17 us
  other arithmetic: 3.9 us -> 0.2 us
  Pallas kernels: 16 us -> 18.3 us
    ppermute x20 -> x26, starting transfers between devices: 23.8 us -> 31.5 us  [swap(): return lax.ppermute(value, axis, [(i, i ^ j) for i in range(n)])]
    concatenate x3 -> x0, other arithmetic: 2.5 us -> none  [the longest x1 1.82 us: local_fast(): mlp_far = exchange_half(jnp.concatenate([mlp_mine, mlp_other], axis=1))]
    another operation x3 -> x0, local copies, waits for them, and re-layouts: 2.33 us -> none  [the longest x2 1.43 us: local_fast(): outs_near = jnp.stack([block[top:top + 2 * out_rows] for block in near])]
    ppermute x20 -> x26, waiting for transfers between devices: 34 us -> 36.3 us  [swap(): return lax.ppermute(value, axis, [(i, i ^ j) for i in range(n)])]
    pallas_call x2 -> x3, Pallas kernels: 7.01 us -> 8.59 us  [the longest x1 5.28 us: mlp(): pl.pallas_call(kernel, in_specs=[sspec()] + [vspec()] * 3 + [aspec()] * (...]
    all_to_all x1, waiting for transfers between devices: 1.3 us -> 0.01 us  [exchange(): return lax.all_to_all(value, 'seq', split_axis=0, concat_axis=0, tiled=True)]
    unnamed x40 -> x26, local copies, waits for them, and re-layouts: 7.8 us -> 6.94 us
  transfers between devices with their start and end apart: 23 -> 29, of which waited for: 10 -> 11; matrix products, arithmetic and copies ran while one was open for 5% -> 1% of each run, Pallas kernels for 6% -> 2%
where the time goes in v6:
time: 128 us
  starting transfers between devices  43.7 us (34%)
  waiting for transfers between devices  38.5 us (30%)
  blocking collectives  18.6 us (15%)
  Pallas kernels  18.3 us (14%)
  local copies, waits for them, and re-layouts  8.17 us (6%)
    ppermute x26, waiting for transfers between devices, swap(): return lax.ppermute(value, axis, [(i, i ^ j) for i in range(n)])  36.3 us
    ppermute x26, starting transfers between devices, swap(): return lax.ppermute(value, axis, [(i, i ^ j) for i in range(n)])  31.5 us
    all_to_all x1, blocking collectives, exchange(): return lax.all_to_all(value, 'seq', split_axis=0, concat_axis=0, tiled=True)  18.6 us
    all_to_all x2, starting transfers between devices, exchange_half(): lax.all_to_all(value, 'seq', split_axis=0, concat_axis=0, axis_index_grou...  7.51 us
    unnamed x26, local copies, waits for them, and re-layouts  6.94 us
    pallas_call x1, Pallas kernels, mlp(): pl.pallas_call(kernel, in_specs=[sspec()] + [vspec()] * 3 + [aspec()] * (...  5.28 us
    all_to_all x1, starting transfers between devices, exchange(): return lax.all_to_all(value, 'seq', split_axis=0, concat_axis=0, tiled=True)  4.66 us
    pallas_call x1, Pallas kernels, attend_fast(): pl.pallas_call(functools.partial(attend_kernel, n, per_owner), in_specs=[...  3.4 us
  transfers between devices with their start and end apart: 29, of which 11 were waited for; matrix products, arithmetic and copies ran while one was open for 1% of the time, Pallas kernels for 2%

profile of v6, /device:TPU:0, one launch (start us, length us, event | category | flops | bytes accessed | tf_op | source)
XLA Modules:
  0.0 127.7 jit_solution(5694845608384986014)
XLA Ops:
  2.8 4.1 %collective-permute-start = (bf16[384,128]{1,0:T(8,128)(2,1)S(1)}, bf16[384,128]{1,0:T(8,128)(2,1)S(1)}, u32[]{:S(2)}, u32[]{:S(2)}) collective-permute-start(bf16[384,128]{1,0:T(8,128)(2,1)S(1)} %get-tuple-element.50), channel_id=1, source_target_pairs={{0,8},{2,10},{4,12},{6,14},{8,0},{10,2},{12,4},{14,6},{1,9},{3,11}... | collective-permute-start | bytes 294920 | tf_op jit(solution)/shard_map/ppermute | solution.py:596
  8.2 2.0 %shard_map.64 = bf16[640,128]{1,0:T(8,128)(2,1)} custom-call(s32[3]{0:T(128)S(1)} %pad_add_fusion.rank_ref.scalars, s32[64,1]{1,0:T(8,128)S(1)} %copy.8.keep_ref, bf16[160,1024]{1,0:T(8,128)(2,1)S(1)} %reshape.15.patches_ref), custom_call_target="tpu_custom_call" | custom-call | tf_op jit(solution)/shard_map/pallas_call | solution.py:240
  10.2 1.7 %collective-permute-done.mine_ref = bf16[384,128]{1,0:T(8,128)(2,1)S(1)} collective-permute-done((bf16[384,128]{1,0:T(8,128)(2,1)S(1)}, bf16[384,128]{1,0:T(8,128)(2,1)S(1)}, u32[]{:S(2)}, u32[]{:S(2)}) %collective-permute-start) | collective-permute-done | bytes 98336 | tf_op jit(solution)/shard_map/ppermute | solution.py:596
  11.8 2.5 %shard_map.67 = (bf16[1216,128]{1,0:T(8,128)(2,1)S(1)}, bf16[1216,128]{1,0:T(8,128)(2,1)S(1)}, bf16[1216,128]{1,0:T(8,128)(2,1)S(1)}, bf16[1216,128]{1,0:T(8,128)(2,1)S(1)}, bf16[4,256,128]{2,1,0:T(8,128)(2,1)S(1)}) custom-call(s32[3]{0:T(128)S(1)} %pad_add_fusion.rank_ref.scalars, bf16[8,192,128]{2,1,0:T(8,128)(2,1)S(1)} %bitcast.21, ...), custom_call_target="tpu_custom_call" | custom-call | tf_op jit(solution)/shard_map/pallas_call | solution.py:324
  14.3 1.6 %collective-permute-start.7 = (bf16[1216,128]{1,0:T(8,128)(2,1)S(1)}, bf16[1216,128]{1,0:T(8,128)(2,1)S(1)}, u32[]{:S(2)}, u32[]{:S(2)}) collective-permute-start(bf16[1216,128]{1,0:T(8,128)(2,1)S(1)} %get-tuple-element.63), channel_id=1, source_target_pairs={{0,2},{2,0},{4,6},{6,4},{8,10},{10,8},{12,14},{14,12},{1,3},{3,1},... | collective-permute-start | bytes 933896 | tf_op jit(solution)/shard_map/ppermute | solution.py:596
  16.6 4.7 %all-to-all-start = ((bf16[8,80,128]{2,1,0:T(8,128)(2,1)}), bf16[8,80,128]{2,1,0:T(8,128)(2,1)S(1)}, u32[]{:S(2)}, u32[]{:S(2)}) async-start(bf16[8,80,128]{2,1,0:T(8,128)(2,1)} %bitcast.5), calls=%async_computation | async-start | bytes 327680 | tf_op jit(solution)/shard_map/all_to_all | solution.py:600
  21.3 2.9 %collective-permute-start.9 = (bf16[1216,128]{1,0:T(8,128)(2,1)S(1)}, bf16[1216,128]{1,0:T(8,128)(2,1)}, u32[]{:S(2)}, u32[]{:S(2)}) collective-permute-start(bf16[1216,128]{1,0:T(8,128)(2,1)S(1)} %get-tuple-element.65), channel_id=1, source_target_pairs={{0,6},{2,4},{4,2},{6,0},{8,14},{10,12},{12,10},{14,8},{1,7},{3,5},... | collective-permute-start | bytes 933896 | tf_op jit(solution)/shard_map/ppermute | solution.py:596
  24.2 1.5 %collective-permute-start.2 = (bf16[384,128]{1,0:T(8,128)(2,1)S(1)}, bf16[384,128]{1,0:T(8,128)(2,1)S(1)}, u32[]{:S(2)}, u32[]{:S(2)}) collective-permute-start(bf16[384,128]{1,0:T(8,128)(2,1)S(1)} %collective-permute-done.mine_ref), channel_id=1, source_target_pairs={{0,16},{16,0},{1,17},{17,1},{2,18},{18,2},{3,19},{19,3},{4,20},{20... | collective-permute-start | bytes 294920 | tf_op jit(solution)/shard_map/ppermute | solution.py:596
  25.7 2.4 %collective-permute-start.1 = (bf16[256,128]{1,0:T(8,128)(2,1)S(1)}, bf16[256,128]{1,0:T(8,128)(2,1)S(1)}, u32[]{:S(2)}, u32[]{:S(2)}) collective-permute-start(bf16[256,128]{1,0:T(8,128)(2,1)S(1)} %get-tuple-element.53), channel_id=1, source_target_pairs={{0,8},{2,10},{4,12},{6,14},{8,0},{10,2},{12,4},{14,6},{1,9},{3,11}... | collective-permute-start | bytes 196616 | tf_op jit(solution)/shard_map/ppermute | solution.py:596
  28.1 6.0 %collective-permute-done.1 = bf16[256,128]{1,0:T(8,128)(2,1)S(1)} collective-permute-done((bf16[256,128]{1,0:T(8,128)(2,1)S(1)}, bf16[256,128]{1,0:T(8,128)(2,1)S(1)}, u32[]{:S(2)}, u32[]{:S(2)}) %collective-permute-start.1) | collective-permute-done | bytes 65568 | tf_op jit(solution)/shard_map/ppermute | solution.py:596
  35.0 4.0 %collective-permute-start.6 = (bf16[256,128]{1,0:T(8,128)(2,1)S(1)}, bf16[256,128]{1,0:T(8,128)(2,1)S(1)}, u32[]{:S(2)}, u32[]{:S(2)}) collective-permute-start(bf16[256,128]{1,0:T(8,128)(2,1)S(1)} %collective-permute-done.1), channel_id=1, source_target_pairs={{0,6},{2,4},{4,2},{6,0},{8,14},{10,12},{12,10},{14,8},{1,7},{3,5},... | collective-permute-start | bytes 196616 | tf_op jit(solution)/shard_map/ppermute | solution.py:596
  40.5 1.4 %collective-permute-start.3 = (bf16[256,128]{1,0:T(8,128)(2,1)S(1)}, bf16[256,128]{1,0:T(8,128)(2,1)S(1)}, u32[]{:S(2)}, u32[]{:S(2)}) collective-permute-start(bf16[256,128]{1,0:T(8,128)(2,1)S(1)} %shard_map.66.owned_ref), channel_id=1, source_target_pairs={{0,8},{2,10},{4,12},{6,14},{8,0},{10,2},{12,4},{14,6},{1,9},{3,11}... | collective-permute-start | bytes 196616 | tf_op jit(solution)/shard_map/ppermute | solution.py:596
  41.9 1.8 %collective-permute-done.5 = bf16[256,128]{1,0:T(8,128)(2,1)S(1)} collective-permute-done((bf16[256,128]{1,0:T(8,128)(2,1)S(1)}, bf16[256,128]{1,0:T(8,128)(2,1)S(1)}, u32[]{:S(2)}, u32[]{:S(2)}) %collective-permute-start.5) | collective-permute-done | bytes 65568 | tf_op jit(solution)/shard_map/ppermute | solution.py:596
  43.7 1.9 %collective-permute-done.3.across_ref = bf16[256,128]{1,0:T(8,128)(2,1)S(1)} collective-permute-done((bf16[256,128]{1,0:T(8,128)(2,1)S(1)}, bf16[256,128]{1,0:T(8,128)(2,1)S(1)}, u32[]{:S(2)}, u32[]{:S(2)}) %collective-permute-start.3) | collective-permute-done | bytes 65568 | tf_op jit(solution)/shard_map/ppermute | solution.py:596
  45.6 1.5 %shard_map.68 = bf16[4,704,128]{2,1,0:T(8,128)(2,1)} custom-call(s32[3]{0:T(128)S(1)} %pad_add_fusion.rank_ref.scalars, bf16[256,128]{1,0:T(8,128)(2,1)S(1)} %shard_map.66.owned_ref, bf16[256,128]{1,0:T(8,128)(2,1)S(1)} %collective-permute-done.3.across_ref, bf16[384,128]{1,0:T(8,128)(2,1)S(1)} %collective-permute-done.mine_ref, ...), custom_call_target="tpu_custom_call" | custom-call | tf_op jit(solution)/shard_map/pallas_call | solution.py:380
  47.2 3.5 %all-to-all-start.1 = ((bf16[4,704,128]{2,1,0:T(8,128)(2,1)}), bf16[4,704,128]{2,1,0:T(8,128)(2,1)S(1)}, u32[]{:S(2)}, u32[]{:S(2)}) async-start(bf16[4,704,128]{2,1,0:T(8,128)(2,1)} %shard_map.68), calls=%async_computation.1 | async-start | bytes 1441792 | tf_op jit(solution)/shard_map/all_to_all | solution.py:606
  50.6 1.5 %collective-permute-start.10 = (bf16[4,256,128]{2,1,0:T(8,128)(2,1)S(1)}, bf16[4,256,128]{2,1,0:T(8,128)(2,1)}, u32[]{:S(2)}, u32[]{:S(2)}) collective-permute-start(bf16[4,256,128]{2,1,0:T(8,128)(2,1)S(1)} %get-tuple-element.69), channel_id=1, source_target_pairs={{0,8},{2,10},{4,12},{6,14},{8,0},{10,2},{12,4},{14,6},{1,9},{3,11}... | collective-permute-start | bytes 786440 | tf_op jit(solution)/shard_map/ppermute | solution.py:596
  52.2 1.6 %collective-permute-start.11 = (bf16[4,256,128]{2,1,0:T(8,128)(2,1)S(1)}, bf16[4,256,128]{2,1,0:T(8,128)(2,1)}, u32[]{:S(2)}, u32[]{:S(2)}) collective-permute-start(bf16[4,256,128]{2,1,0:T(8,128)(2,1)S(1)} %pad_maximum_fusion.1.e), channel_id=1, source_target_pairs={{0,16},{16,0},{1,17},{17,1},{2,18},{18,2},{3,19},{19,3},{4,20},{20... | collective-permute-start | bytes 786440 | tf_op jit(solution)/shard_map/ppermute | solution.py:596
  53.8 8.1 %collective-permute-done.10 = bf16[4,256,128]{2,1,0:T(8,128)(2,1)} collective-permute-done((bf16[4,256,128]{2,1,0:T(8,128)(2,1)S(1)}, bf16[4,256,128]{2,1,0:T(8,128)(2,1)}, u32[]{:S(2)}, u32[]{:S(2)}) %collective-permute-start.10) | collective-permute-done | bytes 262176 | tf_op jit(solution)/shard_map/ppermute | solution.py:596
  61.8 2.2 %all-to-all-done.1.mine_ref = bf16[4,704,128]{2,1,0:T(8,128)(2,1)S(1)} async-done(((bf16[4,704,128]{2,1,0:T(8,128)(2,1)}), bf16[4,704,128]{2,1,0:T(8,128)(2,1)S(1)}, u32[]{:S(2)}, u32[]{:S(2)}) %all-to-all-start.1) | async-done | bytes 720928 | tf_op jit(solution)/shard_map/all_to_all | solution.py:606
  64.1 1.9 %collective-permute-done.12.other_ref = bf16[4,512,128]{2,1,0:T(8,128)(2,1)S(1)} collective-permute-done((bf16[4,512,128]{2,1,0:T(8,128)(2,1)S(1)}, bf16[4,512,128]{2,1,0:T(8,128)(2,1)S(1)}, u32[]{:S(2)}, u32[]{:S(2)}) %collective-permute-start.12) | collective-permute-done | bytes 524320 | tf_op jit(solution)/shard_map/ppermute | solution.py:596
  66.0 3.4 %shard_map.69 = (bf16[512,1024]{1,0:T(8,128)(2,1)S(1)}, bf16[64,512]{1,0:T(8,128)(2,1)S(1)}) custom-call(s32[3]{0:T(128)S(1)} %pad_add_fusion.rank_ref.scalars, bf16[4,704,128]{2,1,0:T(8,128)(2,1)S(1)} %all-to-all-done.1.mine_ref, bf16[4,512,128]{2,1,0:T(8,128)(2,1)S(1)} %collective-permute-done.12.other_ref, ...), custom_call_target="tpu_custom_call" | custom-call | flops 30000001024 | bytes 1048576 | tf_op jit(solution)/shard_map/pallas_call | solution.py:449
  70.8 3.8 %collective-permute-done.13 = bf16[64,512]{1,0:T(8,128)(2,1)S(1)} collective-permute-done((bf16[64,512]{1,0:T(8,128)(2,1)S(1)}, bf16[64,512]{1,0:T(8,128)(2,1)S(1)}, u32[]{:S(2)}, u32[]{:S(2)}) %collective-permute-start.13) | collective-permute-done | bytes 65568 | tf_op jit(solution)/shard_map/ppermute | solution.py:596
  74.7 2.1 %collective-permute-start.15 = (bf16[2,64,512]{2,1,0:T(8,128)(2,1)S(1)}, bf16[2,64,512]{2,1,0:T(8,128)(2,1)S(1)}, u32[]{:S(2)}, u32[]{:S(2)}) collective-permute-start(bf16[2,64,512]{2,1,0:T(8,128)(2,1)S(1)} %get-tuple-element.96), channel_id=1, source_target_pairs={{0,4},{2,6},{4,0},{6,2},{8,12},{10,14},{12,8},{14,10},{1,5},{3,7},... | collective-permute-start | bytes 393224 | tf_op jit(solution)/shard_map/ppermute | solution.py:596
  76.8 1.5 %collective-permute-start.14 = (bf16[2,64,512]{2,1,0:T(8,128)(2,1)S(1)}, bf16[2,64,512]{2,1,0:T(8,128)(2,1)S(1)}, u32[]{:S(2)}, u32[]{:S(2)}) collective-permute-start(bf16[2,64,512]{2,1,0:T(8,128)(2,1)S(1)} %get-tuple-element.96), channel_id=1, source_target_pairs={{0,2},{2,0},{4,6},{6,4},{8,10},{10,8},{12,14},{14,12},{1,3},{3,1},... | collective-permute-start | bytes 393224 | tf_op jit(solution)/shard_map/ppermute | solution.py:596
  78.4 4.0 %all-to-all-start.2 = ((bf16[4,256,128]{2,1,0:T(8,128)(2,1)}), bf16[4,256,128]{2,1,0:T(8,128)(2,1)S(1)}, u32[]{:S(2)}, u32[]{:S(2)}) async-start(bf16[4,256,128]{2,1,0:T(8,128)(2,1)} %collective-permute-done.10), calls=%async_computation.2 | async-start | bytes 524288 | tf_op jit(solution)/shard_map/all_to_all | solution.py:606
  82.9 2.4 %collective-permute-done.14 = bf16[2,64,512]{2,1,0:T(8,128)(2,1)S(1)} collective-permute-done((bf16[2,64,512]{2,1,0:T(8,128)(2,1)S(1)}, bf16[2,64,512]{2,1,0:T(8,128)(2,1)S(1)}, u32[]{:S(2)}, u32[]{:S(2)}) %collective-permute-start.14) | collective-permute-done | bytes 131104 | tf_op jit(solution)/shard_map/ppermute | solution.py:596
  88.7 1.5 %collective-permute-start.18 = (bf16[4,256,128]{2,1,0:T(8,128)(2,1)S(1)}, bf16[4,256,128]{2,1,0:T(8,128)(2,1)S(1)}, u32[]{:S(2)}, u32[]{:S(2)}) collective-permute-start(bf16[4,256,128]{2,1,0:T(8,128)(2,1)S(1)} %all-to-all-done.2.c), channel_id=1, source_target_pairs={{0,16},{16,0},{1,17},{17,1},{2,18},{18,2},{3,19},{19,3},{4,20},{20... | collective-permute-start | bytes 786440 | tf_op jit(solution)/shard_map/ppermute | solution.py:596
  90.2 6.8 %collective-permute-done.18.d = bf16[4,256,128]{2,1,0:T(8,128)(2,1)S(1)} collective-permute-done((bf16[4,256,128]{2,1,0:T(8,128)(2,1)S(1)}, bf16[4,256,128]{2,1,0:T(8,128)(2,1)S(1)}, u32[]{:S(2)}, u32[]{:S(2)}) %collective-permute-start.18) | collective-permute-done | bytes 262176 | tf_op jit(solution)/shard_map/ppermute | solution.py:596
  99.9 5.3 %shard_map.70 = (f32[64,512]{1,0:T(8,128)S(1)}, f32[512,512]{1,0:T(8,128)S(1)}, bf16[512,512]{1,0:T(8,128)(2,1)S(1)}) custom-call(s32[3]{0:T(128)S(1)} %pad_add_fusion.rank_ref.scalars, bf16[512,1024]{1,0:T(8,128)(2,1)S(1)} %get-tuple-element.79.tokens, bf16[4,2,64,512]{3,2,1,0:T(8,128)(2,1)S(1)} %pad_maximum_fusion.a, ...), custom_call_target="tpu_custom_call" | custom-call | tf_op jit(solution)/shard_map/pallas_call | solution.py:538
  105.2 1.9 %collective-permute-done.25.got_ref = bf16[512,512]{1,0:T(8,128)(2,1)S(1)} collective-permute-done((bf16[512,512]{1,0:T(8,128)(2,1)S(1)}, bf16[512,512]{1,0:T(8,128)(2,1)S(1)}, u32[]{:S(2)}, u32[]{:S(2)}) %collective-permute-start.25) | collective-permute-done | bytes 524320 | tf_op jit(solution)/shard_map/ppermute | solution.py:596
  107.8 18.6 %all_to_all.27.terms_ref = bf16[8,64,512]{2,1,0:T(8,128)(2,1)S(1)} all-to-all(bf16[8,64,512]{2,1,0:T(8,128)(2,1)S(1)} %bitcast.23), channel_id=1, replica_groups=mesh['groups'=2,'seq'=8,'head'=2] {'seq'}, dimensions={0} | all-to-all | bytes 1048576 | tf_op jit(solution)/shard_map/all_to_all | solution.py:600
  (69 shorter events, 17.5 us)
Async XLA Ops:
  2.0 9.8 %copy-start.5 = (bf16[2048,128]{1,0:T(8,128)(2,1)S(1)}, bf16[2048,128]{1,0:T(8,128)(2,1)}, u32[]{:S(2)}) copy-start(bf16[2048,128]{1,0:T(8,128)(2,1)} %down_ref) | copy-start | bytes 1572868
  2.8 4.1 %copy-start.12 = (s32[1,64]{1,0:T(1,128)S(1)}, s32[1,64]{1,0:T(1,128)}, u32[]{:S(2)}) copy-start(s32[1,64]{1,0:T(1,128)} %param.7) | copy-start | bytes 772
  2.8 9.0 %collective-permute-start = (bf16[384,128]{1,0:T(8,128)(2,1)S(1)}, bf16[384,128]{1,0:T(8,128)(2,1)S(1)}, u32[]{:S(2)}, u32[]{:S(2)}) collective-permute-start(bf16[384,128]{1,0:T(8,128)(2,1)S(1)} %get-tuple-element.50), channel_id=1, source_target_pairs={{0,8},{2,10},{4,12},{6,14},{8,0},{10,2},{12,4},{14,6},{1,9},{3,11}... | collective-permute-start | bytes 294920 | tf_op jit(solution)/shard_map/ppermute | solution.py:596
  7.0 4.8 %copy-start.4 = (bf16[128,2048]{1,0:T(8,128)(2,1)S(1)}, bf16[128,2048]{1,0:T(8,128)(2,1)}, u32[]{:S(2)}) copy-start(bf16[128,2048]{1,0:T(8,128)(2,1)} %up_ref) | copy-start | bytes 1572868
  14.3 24.7 %collective-permute-start.7 = (bf16[1216,128]{1,0:T(8,128)(2,1)S(1)}, bf16[1216,128]{1,0:T(8,128)(2,1)S(1)}, u32[]{:S(2)}, u32[]{:S(2)}) collective-permute-start(bf16[1216,128]{1,0:T(8,128)(2,1)S(1)} %get-tuple-element.63), channel_id=1, source_target_pairs={{0,2},{2,0},{4,6},{6,4},{8,10},{10,8},{12,14},{14,12},{1,3},{3,1},... | collective-permute-start | bytes 933896 | tf_op jit(solution)/shard_map/ppermute | solution.py:596
  16.0 24.5 %collective-permute-start.8 = (bf16[1216,128]{1,0:T(8,128)(2,1)S(1)}, bf16[1216,128]{1,0:T(8,128)(2,1)}, u32[]{:S(2)}, u32[]{:S(2)}) collective-permute-start(bf16[1216,128]{1,0:T(8,128)(2,1)S(1)} %get-tuple-element.64), channel_id=1, source_target_pairs={{0,4},{2,6},{4,0},{6,2},{8,12},{10,14},{12,8},{14,10},{1,5},{3,7},... | collective-permute-start | bytes 933896 | tf_op jit(solution)/shard_map/ppermute | solution.py:596
  16.6 17.4 %all-to-all-start = ((bf16[8,80,128]{2,1,0:T(8,128)(2,1)}), bf16[8,80,128]{2,1,0:T(8,128)(2,1)S(1)}, u32[]{:S(2)}, u32[]{:S(2)}) async-start(bf16[8,80,128]{2,1,0:T(8,128)(2,1)} %bitcast.5), calls=%async_computation | async-start | bytes 327680 | tf_op jit(solution)/shard_map/all_to_all | solution.py:600
  21.3 20.6 %collective-permute-start.9 = (bf16[1216,128]{1,0:T(8,128)(2,1)S(1)}, bf16[1216,128]{1,0:T(8,128)(2,1)}, u32[]{:S(2)}, u32[]{:S(2)}) collective-permute-start(bf16[1216,128]{1,0:T(8,128)(2,1)S(1)} %get-tuple-element.65), channel_id=1, source_target_pairs={{0,6},{2,4},{4,2},{6,0},{8,14},{10,12},{12,10},{14,8},{1,7},{3,5},... | collective-permute-start | bytes 933896 | tf_op jit(solution)/shard_map/ppermute | solution.py:596
  24.2 9.8 %collective-permute-start.2 = (bf16[384,128]{1,0:T(8,128)(2,1)S(1)}, bf16[384,128]{1,0:T(8,128)(2,1)S(1)}, u32[]{:S(2)}, u32[]{:S(2)}) collective-permute-start(bf16[384,128]{1,0:T(8,128)(2,1)S(1)} %collective-permute-done.mine_ref), channel_id=1, source_target_pairs={{0,16},{16,0},{1,17},{17,1},{2,18},{18,2},{3,19},{19,3},{4,20},{20... | collective-permute-start | bytes 294920 | tf_op jit(solution)/shard_map/ppermute | solution.py:596
  25.7 8.3 %collective-permute-start.1 = (bf16[256,128]{1,0:T(8,128)(2,1)S(1)}, bf16[256,128]{1,0:T(8,128)(2,1)S(1)}, u32[]{:S(2)}, u32[]{:S(2)}) collective-permute-start(bf16[256,128]{1,0:T(8,128)(2,1)S(1)} %get-tuple-element.53), channel_id=1, source_target_pairs={{0,8},{2,10},{4,12},{6,14},{8,0},{10,2},{12,4},{14,6},{1,9},{3,11}... | collective-permute-start | bytes 196616 | tf_op jit(solution)/shard_map/ppermute | solution.py:596
  35.0 6.9 %collective-permute-start.6 = (bf16[256,128]{1,0:T(8,128)(2,1)S(1)}, bf16[256,128]{1,0:T(8,128)(2,1)S(1)}, u32[]{:S(2)}, u32[]{:S(2)}) collective-permute-start(bf16[256,128]{1,0:T(8,128)(2,1)S(1)} %collective-permute-done.1), channel_id=1, source_target_pairs={{0,6},{2,4},{4,2},{6,0},{8,14},{10,12},{12,10},{14,8},{1,7},{3,5},... | collective-permute-start | bytes 196616 | tf_op jit(solution)/shard_map/ppermute | solution.py:596
  38.9 4.7 %collective-permute-start.5 = (bf16[256,128]{1,0:T(8,128)(2,1)S(1)}, bf16[256,128]{1,0:T(8,128)(2,1)S(1)}, u32[]{:S(2)}, u32[]{:S(2)}) collective-permute-start(bf16[256,128]{1,0:T(8,128)(2,1)S(1)} %collective-permute-done.1), channel_id=1, source_target_pairs={{0,4},{2,6},{4,0},{6,2},{8,12},{10,14},{12,8},{14,10},{1,5},{3,7},... | collective-permute-start | bytes 196616 | tf_op jit(solution)/shard_map/ppermute | solution.py:596
  39.1 4.6 %collective-permute-start.4 = (bf16[256,128]{1,0:T(8,128)(2,1)S(1)}, bf16[256,128]{1,0:T(8,128)(2,1)S(1)}, u32[]{:S(2)}, u32[]{:S(2)}) collective-permute-start(bf16[256,128]{1,0:T(8,128)(2,1)S(1)} %collective-permute-done.1), channel_id=1, source_target_pairs={{0,2},{2,0},{4,6},{6,4},{8,10},{10,8},{12,14},{14,12},{1,3},{3,1},... | collective-permute-start | bytes 196616 | tf_op jit(solution)/shard_map/ppermute | solution.py:596
  40.5 5.2 %collective-permute-start.3 = (bf16[256,128]{1,0:T(8,128)(2,1)S(1)}, bf16[256,128]{1,0:T(8,128)(2,1)S(1)}, u32[]{:S(2)}, u32[]{:S(2)}) collective-permute-start(bf16[256,128]{1,0:T(8,128)(2,1)S(1)} %shard_map.66.owned_ref), channel_id=1, source_target_pairs={{0,8},{2,10},{4,12},{6,14},{8,0},{10,2},{12,4},{14,6},{1,9},{3,11}... | collective-permute-start | bytes 196616 | tf_op jit(solution)/shard_map/ppermute | solution.py:596
  47.2 16.8 %all-to-all-start.1 = ((bf16[4,704,128]{2,1,0:T(8,128)(2,1)}), bf16[4,704,128]{2,1,0:T(8,128)(2,1)S(1)}, u32[]{:S(2)}, u32[]{:S(2)}) async-start(bf16[4,704,128]{2,1,0:T(8,128)(2,1)} %shard_map.68), calls=%async_computation.1 | async-start | bytes 1441792 | tf_op jit(solution)/shard_map/all_to_all | solution.py:606
  50.6 11.2 %collective-permute-start.10 = (bf16[4,256,128]{2,1,0:T(8,128)(2,1)S(1)}, bf16[4,256,128]{2,1,0:T(8,128)(2,1)}, u32[]{:S(2)}, u32[]{:S(2)}) collective-permute-start(bf16[4,256,128]{2,1,0:T(8,128)(2,1)S(1)} %get-tuple-element.69), channel_id=1, source_target_pairs={{0,8},{2,10},{4,12},{6,14},{8,0},{10,2},{12,4},{14,6},{1,9},{3,11}... | collective-permute-start | bytes 786440 | tf_op jit(solution)/shard_map/ppermute | solution.py:596
  52.2 9.6 %collective-permute-start.11 = (bf16[4,256,128]{2,1,0:T(8,128)(2,1)S(1)}, bf16[4,256,128]{2,1,0:T(8,128)(2,1)}, u32[]{:S(2)}, u32[]{:S(2)}) collective-permute-start(bf16[4,256,128]{2,1,0:T(8,128)(2,1)S(1)} %pad_maximum_fusion.1.e), channel_id=1, source_target_pairs={{0,16},{16,0},{1,17},{17,1},{2,18},{18,2},{3,19},{19,3},{4,20},{20... | collective-permute-start | bytes 786440 | tf_op jit(solution)/shard_map/ppermute | solution.py:596
  64.0 2.0 %collective-permute-start.12 = (bf16[4,512,128]{2,1,0:T(8,128)(2,1)S(1)}, bf16[4,512,128]{2,1,0:T(8,128)(2,1)S(1)}, u32[]{:S(2)}, u32[]{:S(2)}) collective-permute-start(bf16[4,512,128]{2,1,0:T(8,128)(2,1)S(1)} %slice.3), channel_id=1, source_target_pairs={{0,1},{1,0},{2,3},{3,2},{4,5},{5,4},{6,7},{7,6},{8,9},{9,8},{10,11... | collective-permute-start | bytes 1572872 | tf_op jit(solution)/shard_map/ppermute | solution.py:596
  69.4 5.2 %collective-permute-start.13 = (bf16[64,512]{1,0:T(8,128)(2,1)S(1)}, bf16[64,512]{1,0:T(8,128)(2,1)S(1)}, u32[]{:S(2)}, u32[]{:S(2)}) collective-permute-start(bf16[64,512]{1,0:T(8,128)(2,1)S(1)} %get-tuple-element.80), channel_id=1, source_target_pairs={{0,8},{2,10},{4,12},{6,14},{8,0},{10,2},{12,4},{14,6},{1,9},{3,11}... | collective-permute-start | bytes 196616 | tf_op jit(solution)/shard_map/ppermute | solution.py:596
  74.7 8.3 %collective-permute-start.15 = (bf16[2,64,512]{2,1,0:T(8,128)(2,1)S(1)}, bf16[2,64,512]{2,1,0:T(8,128)(2,1)S(1)}, u32[]{:S(2)}, u32[]{:S(2)}) collective-permute-start(bf16[2,64,512]{2,1,0:T(8,128)(2,1)S(1)} %get-tuple-element.96), channel_id=1, source_target_pairs={{0,4},{2,6},{4,0},{6,2},{8,12},{10,14},{12,8},{14,10},{1,5},{3,7},... | collective-permute-start | bytes 393224 | tf_op jit(solution)/shard_map/ppermute | solution.py:596
  76.8 8.6 %collective-permute-start.14 = (bf16[2,64,512]{2,1,0:T(8,128)(2,1)S(1)}, bf16[2,64,512]{2,1,0:T(8,128)(2,1)S(1)}, u32[]{:S(2)}, u32[]{:S(2)}) collective-permute-start(bf16[2,64,512]{2,1,0:T(8,128)(2,1)S(1)} %get-tuple-element.96), channel_id=1, source_target_pairs={{0,2},{2,0},{4,6},{6,4},{8,10},{10,8},{12,14},{14,12},{1,3},{3,1},... | collective-permute-start | bytes 393224 | tf_op jit(solution)/shard_map/ppermute | solution.py:596
  78.2 7.2 %collective-permute-start.16 = (bf16[2,64,512]{2,1,0:T(8,128)(2,1)S(1)}, bf16[2,64,512]{2,1,0:T(8,128)(2,1)S(1)}, u32[]{:S(2)}, u32[]{:S(2)}) collective-permute-start(bf16[2,64,512]{2,1,0:T(8,128)(2,1)S(1)} %get-tuple-element.96), channel_id=1, source_target_pairs={{0,6},{2,4},{4,2},{6,0},{8,14},{10,12},{12,10},{14,8},{1,7},{3,5},... | collective-permute-start | bytes 393224 | tf_op jit(solution)/shard_map/ppermute | solution.py:596
  78.4 10.3 %all-to-all-start.2 = ((bf16[4,256,128]{2,1,0:T(8,128)(2,1)}), bf16[4,256,128]{2,1,0:T(8,128)(2,1)S(1)}, u32[]{:S(2)}, u32[]{:S(2)}) async-start(bf16[4,256,128]{2,1,0:T(8,128)(2,1)} %collective-permute-done.10), calls=%async_computation.2 | async-start | bytes 524288 | tf_op jit(solution)/shard_map/all_to_all | solution.py:606
  82.4 3.6 %collective-permute-start.19 = (bf16[4,256,128]{2,1,0:T(8,128)(2,1)S(1)}, bf16[4,256,128]{2,1,0:T(8,128)(2,1)S(1)}, u32[]{:S(2)}, u32[]{:S(2)}) collective-permute-start(bf16[4,256,128]{2,1,0:T(8,128)(2,1)S(1)} %pad_maximum_fusion.1.e), channel_id=1, source_target_pairs={{0,1},{1,0},{2,3},{3,2},{4,5},{5,4},{6,7},{7,6},{8,9},{9,8},{10,11... | collective-permute-start | bytes 786440 | tf_op jit(solution)/shard_map/ppermute | solution.py:596
  82.4 4.4 %collective-permute-start.20 = (bf16[4,256,128]{2,1,0:T(8,128)(2,1)}, bf16[4,256,128]{2,1,0:T(8,128)(2,1)S(1)}, u32[]{:S(2)}, u32[]{:S(2)}) collective-permute-start(bf16[4,256,128]{2,1,0:T(8,128)(2,1)} %collective-permute-done.11.f), channel_id=1, source_target_pairs={{0,1},{1,0},{2,3},{3,2},{4,5},{5,4},{6,7},{7,6},{8,9},{9,8},{10,11... | collective-permute-start | bytes 786440 | tf_op jit(solution)/shard_map/ppermute | solution.py:596
  82.9 5.0 %collective-permute-start.21 = (bf16[1216,128]{1,0:T(8,128)(2,1)S(1)}, bf16[1216,128]{1,0:T(8,128)(2,1)S(1)}, u32[]{:S(2)}, u32[]{:S(2)}) collective-permute-start(bf16[1216,128]{1,0:T(8,128)(2,1)S(1)} %get-tuple-element.86.refs_0_), channel_id=1, source_target_pairs={{0,1},{1,0},{2,3},{3,2},{4,5},{5,4},{6,7},{7,6},{8,9},{9,8},{10,11... | collective-permute-start | bytes 933896 | tf_op jit(solution)/shard_map/ppermute | solution.py:596
  85.5 11.5 %collective-permute-start.17 = (bf16[4,2,64,512]{3,2,1,0:T(8,128)(2,1)S(1)}, bf16[4,2,64,512]{3,2,1,0:T(8,128)(2,1)S(1)}, u32[]{:S(2)}, u32[]{:S(2)}) collective-permute-start(bf16[4,2,64,512]{3,2,1,0:T(8,128)(2,1)S(1)} %pad_maximum_fusion.a), channel_id=1, source_target_pairs={{0,1},{1,0},{2,3},{3,2},{4,5},{5,4},{6,7},{7,6},{8,9},{9,8},{10,11... | collective-permute-start | bytes 1572872 | tf_op jit(solution)/shard_map/ppermute | solution.py:596
  85.5 4.7 %collective-permute-start.22 = (bf16[1216,128]{1,0:T(8,128)(2,1)S(1)}, bf16[1216,128]{1,0:T(8,128)(2,1)}, u32[]{:S(2)}, u32[]{:S(2)}) collective-permute-start(bf16[1216,128]{1,0:T(8,128)(2,1)S(1)} %collective-permute-done.7.refs_1_), channel_id=1, source_target_pairs={{0,1},{1,0},{2,3},{3,2},{4,5},{5,4},{6,7},{7,6},{8,9},{9,8},{10,11... | collective-permute-start | bytes 933896 | tf_op jit(solution)/shard_map/ppermute | solution.py:596
  86.8 3.4 %collective-permute-start.23 = (bf16[1216,128]{1,0:T(8,128)(2,1)}, bf16[1216,128]{1,0:T(8,128)(2,1)}, u32[]{:S(2)}, u32[]{:S(2)}) collective-permute-start(bf16[1216,128]{1,0:T(8,128)(2,1)} %collective-permute-done.8.refs_2_), channel_id=1, source_target_pairs={{0,1},{1,0},{2,3},{3,2},{4,5},{5,4},{6,7},{7,6},{8,9},{9,8},{10,11... | collective-permute-start | bytes 933896 | tf_op jit(solution)/shard_map/ppermute | solution.py:596
  87.6 2.7 %collective-permute-start.24 = (bf16[1216,128]{1,0:T(8,128)(2,1)}, bf16[1216,128]{1,0:T(8,128)(2,1)}, u32[]{:S(2)}, u32[]{:S(2)}) collective-permute-start(bf16[1216,128]{1,0:T(8,128)(2,1)} %collective-permute-done.9.refs_3_), channel_id=1, source_target_pairs={{0,1},{1,0},{2,3},{3,2},{4,5},{5,4},{6,7},{7,6},{8,9},{9,8},{10,11... | collective-permute-start | bytes 933896 | tf_op jit(solution)/shard_map/ppermute | solution.py:596
  88.7 8.3 %collective-permute-start.18 = (bf16[4,256,128]{2,1,0:T(8,128)(2,1)S(1)}, bf16[4,256,128]{2,1,0:T(8,128)(2,1)S(1)}, u32[]{:S(2)}, u32[]{:S(2)}) collective-permute-start(bf16[4,256,128]{2,1,0:T(8,128)(2,1)S(1)} %all-to-all-done.2.c), channel_id=1, source_target_pairs={{0,16},{16,0},{1,17},{17,1},{2,18},{18,2},{3,19},{19,3},{4,20},{20... | collective-permute-start | bytes 786440 | tf_op jit(solution)/shard_map/ppermute | solution.py:596
  105.2 2.0 %collective-permute-start.25 = (bf16[512,512]{1,0:T(8,128)(2,1)S(1)}, bf16[512,512]{1,0:T(8,128)(2,1)S(1)}, u32[]{:S(2)}, u32[]{:S(2)}) collective-permute-start(bf16[512,512]{1,0:T(8,128)(2,1)S(1)} %get-tuple-element.91), channel_id=1, source_target_pairs={{0,1},{1,0},{2,3},{3,2},{4,5},{5,4},{6,7},{7,6},{8,9},{9,8},{10,11... | collective-permute-start | bytes 1572872 | tf_op jit(solution)/shard_map/ppermute | solution.py:596
  (10 other events, 14.3 us)

commit v7 on v6

--- a/solution.py
+++ b/solution.py
@@ -290,14 +290,13 @@
     )(scalars, keep_col, got)
 
 
-def pack_kernel(n, rank_ref, qkv_ref, out_weight_ref, up_ref, down_ref, *refs):
+def pack_kernel(n, rank_ref, up_ref, down_ref, *refs):
     near, away_ref, sem = refs[: n // 2], refs[n // 2], refs[n // 2 + 1]
     rank, part = rank_ref[0], rank_ref[2]
     half = n // 2
     rows = up_ref.shape[0]
     wide = up_ref.shape[1] // n
     units = wide // 2
-    long = out_weight_ref.shape[0]
     copies = []
     for j in range(half):
         dest = rank ^ j
@@ -306,10 +305,6 @@
             copies.append((up_ref.at[:, at], near[j].at[pl.ds(c * rows, rows)]))
         at = pl.ds(pl.multiple_of(dest * wide, 128), wide)
         copies.append((down_ref.at[at], near[j].at[pl.ds(2 * rows, wide)]))
-        copies.append((out_weight_ref, near[j].at[pl.ds(2 * rows + wide, long)]))
-        copies.append(
-            (qkv_ref.at[dest], near[j].at[pl.ds(2 * rows + wide + long, qkv_ref.shape[1])])
-        )
         dest = (rank // half ^ 1) * half + j
         at = pl.ds(pl.multiple_of(dest * wide + part * units, 128), units)
         copies.append((up_ref.at[:, at], away_ref.at[j, pl.ds(0, rows)]))
@@ -317,22 +312,22 @@
     run_copies(copies, sem)()
 
 
-def pack(scalars, qkv, out_weight, up, down, n):
+def pack(scalars, up, down, n):
     wide = up.shape[1] // n
-    near = struct((2 * up.shape[0] + wide + out_weight.shape[0] + qkv.shape[1], 128))
+    near = struct((2 * up.shape[0] + wide, 128))
     away = struct((n // 2, up.shape[0] + wide // 2, 128))
     outs = pl.pallas_call(
         functools.partial(pack_kernel, n),
-        in_specs=[sspec()] + [hspec()] * 4,
-        out_specs=[hspec()] * (n // 2 + 1),
+        in_specs=[sspec()] + [hspec()] * 2,
+        out_specs=[hspec()] * (n // 2) + [aspec()],
         out_shape=[near] * (n // 2) + [away],
-        scratch_shapes=[pltpu.SemaphoreType.DMA((7 * n // 2,))],
-        compiler_params=params(),
-    )(scalars, qkv, out_weight, up, down)
+        scratch_shapes=[pltpu.SemaphoreType.DMA((5 * n // 2,))],
+        compiler_params=params(),
+    )(scalars, up, down)
     return list(outs[:-1]), outs[-1]
 
 
-def early_kernel(n, rank_ref, qkv_ref, out_weight_ref, heads_ref, rows_ref, sem):
+def early_kernel(n, rank_ref, qkv_ref, out_weight_ref, heads_ref, near_ref, rows_ref, sem):
     rank, part = rank_ref[0], rank_ref[2]
     half = n // 2
     depth = heads_ref.shape[0] // half
@@ -342,6 +337,7 @@
         dest = (rank // half ^ 1) * half + d
         at = pl.ds(pl.multiple_of(part * depth, 32), depth)
         copies.append((qkv_ref.at[dest, at], heads_ref.at[pl.ds(d * depth, depth)]))
+    copies.append((qkv_ref.at[pl.ds(rank // half * half, half)], near_ref))
     at = pl.ds(pl.multiple_of(part * long, 128), long)
     copies.append((out_weight_ref.at[at], rows_ref))
     run_copies(copies, sem)()
@@ -351,39 +347,44 @@
     return pl.pallas_call(
         functools.partial(early_kernel, n),
         in_specs=[sspec()] + [hspec()] * 2,
-        out_specs=[aspec()] * 2,
+        out_specs=[aspec()] * 3,
         out_shape=[
             struct((n // 2 * qkv.shape[1] // 2, 128)),
+            struct((n // 2,) + qkv.shape[1:]),
             struct((out_weight.shape[0] // 2, 128)),
         ],
-        scratch_shapes=[pltpu.SemaphoreType.DMA((n // 2 + 1,))],
+        scratch_shapes=[pltpu.SemaphoreType.DMA((n // 2 + 2,))],
         compiler_params=params(),
     )(scalars, qkv, out_weight)
 
 
-def fan_kernel(rank_ref, owned_ref, across_ref, mine_ref, other_ref, out_ref):
+def fan_kernel(rank_ref, owned_ref, across_ref, mine_ref, other_ref, near_ref, rows_ref, out_ref):
     part = rank_ref[2]
     rows = owned_ref.shape[0]
-    count = out_ref.shape[0]
-    depth = (out_ref.shape[1] - 2 * rows) // 2
+    count, head_rows = near_ref.shape[:2]
+    depth = head_rows // 2
+    top = 2 * rows
     for d in range(count):
         out_ref[d, :rows] = owned_ref[...]
-        out_ref[d, rows : 2 * rows] = across_ref[...]
-        at = pl.ds(pl.multiple_of(2 * rows + part * depth, 32), depth)
+        out_ref[d, rows:top] = across_ref[...]
+        out_ref[d, top : top + head_rows] = near_ref[d]
+        at = pl.ds(pl.multiple_of(top + head_rows + part * depth, 32), depth)
         out_ref[d, at] = mine_ref[d * depth : (d + 1) * depth]
-        at = pl.ds(pl.multiple_of(2 * rows + (1 - part) * depth, 32), depth)
+        at = pl.ds(pl.multiple_of(top + head_rows + (1 - part) * depth, 32), depth)
         out_ref[d, at] = other_ref[d * depth : (d + 1) * depth]
-
-
-def fan(scalars, owned, across, mine, other, head_rows, n):
-    shape = struct((n // 2, 2 * owned.shape[0] + head_rows, 128))
+        out_ref[d, top + 2 * head_rows :] = rows_ref[...]
+
+
+def fan(scalars, owned, across, mine, other, near, rows):
+    count = near.shape[0]
+    shape = struct((count, 2 * owned.shape[0] + 2 * near.shape[1] + rows.shape[0], 128))
     return pl.pallas_call(
         fan_kernel,
-        in_specs=[sspec()] + [vspec()] * 4,
+        in_specs=[sspec()] + [vspec()] * 6,
         out_specs=vspec(),
         out_shape=shape,
         compiler_params=params(),
-    )(scalars, owned, across, mine, other)
+    )(scalars, owned, across, mine, other, near, rows)
 
 
 def source_of(rank, n, q, k):
@@ -396,19 +397,12 @@
     return (x - average) * lax.rsqrt(power - average * average + 1e-06)
 
 
-def attend_kernel(n, part, rank_ref, mine_ref, other_ref, *refs):
-    near, (tokens_ref, out_ref, weight_ref, sem) = refs[: n // 2], refs[n // 2 :]
+def attend_kernel(n, part, rank_ref, mine_ref, other_ref, tokens_ref, out_ref, weight_ref):
     rank, half = rank_ref[0], rank_ref[1]
-    depth = weight_ref.shape[0]
-    copies = []
-    for j in range(n // 2):
-        to = pl.ds(pl.multiple_of((rank ^ j) * 128, 128), 128)
-        at = pl.ds(near[j].shape[0] - depth, depth)
-        copies.append((near[j].at[at], weight_ref.at[:, to]))
-    wait = run_copies(copies, sem)
     rows = other_ref.shape[1] // 2
     cuts = rows // part
     width = cuts * 128
+    depth = weight_ref.shape[0]
     for q in range(n // 2):
         for k in range(2):
             source = source_of(rank, n, q, k)
@@ -419,11 +413,10 @@
                 tokens_ref[at, to] = mine_ref[q, cut]
                 to = pl.ds(pl.multiple_of((1 - half) * width + c * 128, 128), 128)
                 tokens_ref[at, to] = other_ref[q, cut]
-        source = source_of(rank, n, q, 1)
-        to = pl.ds(pl.multiple_of(source * 128, 128), 128)
-        weight_ref[:, to] = mine_ref[q, 2 * rows :]
+            to = pl.ds(pl.multiple_of(source * 128, 128), 128)
+            high = 2 * rows + k * depth
+            weight_ref[:, to] = mine_ref[q, high : high + depth]
     normed = norm_rows(tokens_ref[...].astype(F32)).astype(BF16)
-    wait()
     projected = lax.dot_general(
         normed, weight_ref[...], (((1,), (1,)), ((), ())), preferred_element_type=F32
     ).astype(BF16)
@@ -442,25 +435,22 @@
     out_ref[...] = attended
 
 
-def attend_fast(scalars, mine, other, near, head_rows, per_owner, n):
+def attend_fast(scalars, mine, other, head_rows, per_owner, n):
     length = n * per_owner
     depth = other.shape[1] // (2 * per_owner) * 256
     size = head_rows // 3
     return pl.pallas_call(
         functools.partial(attend_kernel, n, per_owner),
-        in_specs=[sspec()] + [vspec()] * 2 + [aspec()] * (n // 2),
+        in_specs=[sspec()] + [vspec()] * 2,
         out_specs=[vspec()] * 2,
         out_shape=[struct((length, depth)), struct((size, length))],
-        scratch_shapes=[
-            VMEM((head_rows, n * 128), BF16),
-            pltpu.SemaphoreType.DMA((n // 2,)),
-        ],
+        scratch_shapes=[VMEM((head_rows, n * 128), BF16)],
         compiler_params=params(),
         cost_estimate=cost(30),
-    )(scalars, mine, other, *near)
-
-
-def mlp_kernel(n, rank_ref, tokens_ref, pieces, far, outs_far, near, near_other, outs, scratch):
+    )(scalars, mine, other)
+
+
+def mlp_kernel(n, rank_ref, tokens_ref, pieces, far, outs_far, near, outs_near, outs, scratch):
     residual_ref, keep_ref, send_ref = outs
     up_ref, down_ref, row_ref, whole_ref, joined_ref, sem = scratch
     rank, half, group = rank_ref[0], rank_ref[1], rank_ref[2]
@@ -479,8 +469,8 @@
                 (near[j].at[pl.ds(c * block, block)], up_ref.at[at, pl.ds(c * unit, unit)])
             )
         later.append((near[j].at[pl.ds(2 * block, wide)], down_ref.at[:, to]))
-        for core, refs in enumerate((near, near_other)):
-            first.append((refs[j].at[pl.ds(2 * block + wide, 2 * rows)], whole_ref.at[core, :, to]))
+        for core in range(2):
+            first.append((outs_near[core][j], whole_ref.at[core, :, to]))
         source = source_of(rank, n, j, 1)
         at = pl.ds(pl.multiple_of(source * block, block), block)
         to = pl.ds(pl.multiple_of(source * 128, 128), 128)
@@ -488,8 +478,6 @@
             units = pl.ds(pl.multiple_of((group ^ c) * unit, unit), unit)
             later.append((far[c].at[j, pl.ds(0, block)], up_ref.at[at, units]))
             later.append((far[c].at[j, pl.ds(block, unit)], down_ref.at[units, to]))
-        source = rank ^ j ^ (n // 2)
-        to = pl.ds(pl.multiple_of(source * 128, 128), 128)
         for core in range(2):
             for c in range(2):
                 at = pl.ds(pl.multiple_of((group ^ c) * rows, rows), rows)
@@ -521,7 +509,7 @@
     send_ref[...] = jnp.dot(hidden, down_ref[:, other_cols], preferred_element_type=F32).astype(BF16)
 
 
-def mlp(scalars, tokens, pieces, far, outs_far, near, near_other, n):
+def mlp(scalars, tokens, pieces, far, outs_far, near, outs_near, n):
     length, depth = tokens.shape
     width = depth // 2
     wide = 2 * (far[0].shape[1] - depth // n)
@@ -529,15 +517,14 @@
     half = n // 2
 
     def kernel(scalars, tokens, a, b, c, d, e, f, g, h, *refs):
-        near, near_other = refs[:half], refs[half : 2 * half]
-        outs, scratch = refs[2 * half : 2 * half + 3], refs[2 * half + 3 :]
-        mlp_kernel(
-            n, scalars, tokens, (a, b), (c, d), ((e, f), (g, h)), near, near_other, outs, scratch
-        )
+        near, mine, other = refs[:half], refs[half : 2 * half], refs[2 * half : 3 * half]
+        outs, scratch = refs[3 * half : 3 * half + 3], refs[3 * half + 3 :]
+        far, outs_far, outs_near = (c, d), ((e, f), (g, h)), (mine, other)
+        mlp_kernel(n, scalars, tokens, (a, b), far, outs_far, near, outs_near, outs, scratch)
 
     return pl.pallas_call(
         kernel,
-        in_specs=[sspec()] + [vspec()] * 3 + [aspec()] * (6 + n),
+        in_specs=[sspec()] + [vspec()] * 3 + [hspec()] * (6 + 3 * half),
         out_specs=[vspec()] * 3,
         out_shape=[
             struct((length // n, width), F32),
@@ -553,7 +540,7 @@
             pltpu.SemaphoreType.DMA((13 * half,)),
         ],
         compiler_params=params(),
-    )(scalars, tokens, *pieces, *far, *outs_far[0], *outs_far[1], *near, *near_other)
+    )(scalars, tokens, *pieces, *far, *outs_far[0], *outs_far[1], *near, *outs_near[0], *outs_near[1])
 
 
 def join_kernel(rank_ref, keep_ref, got_ref, residual_ref, base_ref, out_ref):
@@ -629,42 +616,47 @@
     flat = patches.reshape(4 * sup, depth)
     heads = qkv_weight.transpose(1, 2, 0)
 
-    qkv_away, out_away = early_blocks(scalars, heads, out_weight, n)
+    qkv_away, qkv_near, out_away = early_blocks(scalars, heads, out_weight, n)
     qkv_mine = swap(qkv_away, "seq", half)
     slots = prep(scalars, keep_col, flat, n, sup, capacity)
     slots, qkv_mine = lax.optimization_barrier((slots, qkv_mine))
     dealt = exchange(slots)
     out_far = swap(after(out_away, slots), "seq", half)
     qkv_other = swap(qkv_mine, "groups", 1)
-    blocks = lax.optimization_barrier((heads, out_weight, up_weight, down_weight, slots))[:4]
-    near, mlp_away = pack(scalars, *blocks, n)
+    own_rows = after(out_weight, slots)
+    outs_near = [out_weight] + [swap(own_rows, "seq", j) for j in range(1, half)]
+    up, down, qkv_other = lax.optimization_barrier((up_weight, down_weight, qkv_other))
+    near, mlp_away = pack(scalars, up, down, n)
+    dealt, qkv_other, mlp_away, *rest = lax.optimization_barrier(
+        (dealt, qkv_other, mlp_away, *near, *outs_near)
+    )
+    near, outs_near = rest[:half], rest[half:]
+    owned = pick(scalars, keep_col, dealt, n, sup, per_owner, capacity)
+
+    across = swap(owned, "seq", half)
+    mlp_far = swap(after(mlp_away, across), "seq", half)
+    got = exchange_half(fan(scalars, owned, across, qkv_mine, qkv_other, qkv_near, out_far))
+    outs_other = [swap(rows, "head", 1) for rows in lax.optimization_barrier((*outs_near, across))[:half]]
+    got, mlp_far, *rest = lax.optimization_barrier((got, mlp_far, *near, *outs_other))
+    near, outs_other = rest[:half], rest[half:]
+
+    top = 2 * owned.shape[0]
+    pieces_other = swap(got[:, :top], "head", 1)
     near = [near[0]] + [swap(near[j], "seq", j) for j in range(1, half)]
-    dealt, out_far, qkv_other = lax.optimization_barrier((dealt, out_far, qkv_other))
-    owned = pick(scalars, keep_col, dealt, n, sup, per_owner, capacity)
-
-    across = swap(owned, "seq", half)
-    out_far = after(out_far, owned)
-    outs_far = [out_far] + [swap(out_far, "seq", j) for j in range(1, half)]
-    across, *rest = lax.optimization_barrier((across, *outs_far, *near))
-    outs_far, near = rest[:half], rest[half:]
-
-    mlp_far = swap(after(mlp_away, across), "seq", half)
-    got = exchange_half(fan(scalars, owned, across, qkv_mine, qkv_other, head_rows, n))
-    far_mine = jnp.stack(outs_far)
+    mlp_mine = exchange_half(mlp_far)
+    tokens, attended = attend_fast(scalars, got, pieces_other, head_rows, per_owner, n)
+
+    att_across = swap(attended, "seq", half)
+    far_mine = got[:, top + 2 * head_rows :]
     far_other = swap(far_mine, "groups", 1)
-    got, mlp_far, far_other = lax.optimization_barrier((got, mlp_far, far_other))
-
-    pieces = got[:, : got.shape[1] - head_rows]
-    pieces_other = swap(pieces, "head", 1)
-    tokens, attended = attend_fast(scalars, got, pieces_other, near, head_rows, per_owner, n)
-
-    att_across = swap(attended, "seq", half)
-    mlp_mine = exchange_half(after(mlp_far, attended))
+    att_across, mlp_mine, far_other, *near = lax.optimization_barrier(
+        (att_across, mlp_mine, far_other, *near)
+    )
     pair = jnp.stack([attended, att_across])
-    gathered = jnp.stack([pair] + [swap(pair, "seq", j) for j in range(1, half)])
     mlp_other = swap(mlp_mine, "groups", 1)
-    near_other = [swap(block, "head", 1) for block in after(tuple(near), attended)]
-    far_mine, far_other = after((far_mine, far_other), attended)
+    pairs = [swap(pair, "seq", j) for j in range(1, half)]
+    mlp_other, *pairs = lax.optimization_barrier((mlp_other, *pairs))
+    gathered = jnp.stack([pair] + pairs)
     residual, keep, send = mlp(
         scalars,
         tokens,
@@ -672,7 +664,7 @@
         (mlp_mine, mlp_other),
         ((far_mine, far_other), (swap(far_mine, "head", 1), swap(far_other, "head", 1))),
         near,
-        near_other,
+        (outs_near, outs_other),
         n,
     )
     sent = swap(send, "head", 1)

time: 128 us -> 122 us (0.953)
  starting transfers between devices: 43.7 us -> 40 us
  waiting for transfers between devices: 38.5 us -> 35.9 us
    ppermute x26, starting transfers between devices: 31.5 us -> 27.3 us  [swap(): return lax.ppermute(value, axis, [(i, i ^ j) for i in range(n)])]
    ppermute x26, waiting for transfers between devices: 36.3 us -> 33.7 us  [swap(): return lax.ppermute(value, axis, [(i, i ^ j) for i in range(n)])]
    unnamed x26 -> x46, local copies, waits for them, and re-layouts: 6.94 us -> 6.41 us
  transfers between devices with their start and end apart: 29 -> 29, of which waited for: 11 -> 18; matrix products, arithmetic and copies ran while one was open for 1% -> 2% of each run, Pallas kernels for 2% -> 7%
where the time goes in v7:
time: 122 us
  starting transfers between devices  40 us (33%)
  waiting for transfers between devices  35.9 us (29%)
  blocking collectives  18 us (15%)
  Pallas kernels  17.5 us (14%)
  local copies, waits for them, and re-layouts  9.07 us (7%)
    ppermute x26, waiting for transfers between devices, swap(): return lax.ppermute(value, axis, [(i, i ^ j) for i in range(n)])  33.7 us
    ppermute x26, starting transfers between devices, swap(): return lax.ppermute(value, axis, [(i, i ^ j) for i in range(n)])  27.3 us
    all_to_all x1, blocking collectives, exchange(): return lax.all_to_all(value, 'seq', split_axis=0, concat_axis=0, tiled=True)  18 us
    all_to_all x2, starting transfers between devices, exchange_half(): lax.all_to_all(value, 'seq', split_axis=0, concat_axis=0, axis_index_grou...  6.94 us
    unnamed x46, local copies, waits for them, and re-layouts  6.41 us
    all_to_all x1, starting transfers between devices, exchange(): return lax.all_to_all(value, 'seq', split_axis=0, concat_axis=0, tiled=True)  5.77 us
    pallas_call x1, Pallas kernels, mlp(): pl.pallas_call(kernel, in_specs=[sspec()] + [vspec()] * 3 + [hspec()] * (...  4.88 us
    pallas_call x1, Pallas kernels, attend_fast(): pl.pallas_call(functools.partial(attend_kernel, n, per_owner), in_specs=[...  3.32 us
  transfers between devices with their start and end apart: 29, of which 18 were waited for; matrix products, arithmetic and copies ran while one was open for 2% of the time, Pallas kernels for 7%

profile of v7, /device:TPU:0, one launch (start us, length us, event | category | flops | bytes accessed | tf_op | source)
XLA Modules:
  0.0 121.6 jit_solution(3625201203545822425)
XLA Ops:
  3.1 4.1 %collective-permute-start = (bf16[384,128]{1,0:T(8,128)(2,1)S(1)}, bf16[384,128]{1,0:T(8,128)(2,1)S(1)}, u32[]{:S(2)}, u32[]{:S(2)}) collective-permute-start(bf16[384,128]{1,0:T(8,128)(2,1)S(1)} %get-tuple-element.64), channel_id=1, source_target_pairs={{0,8},{2,10},{4,12},{6,14},{8,0},{10,2},{12,4},{14,6},{1,9},{3,11}... | collective-permute-start | bytes 294920 | tf_op jit(solution)/shard_map/ppermute | solution.py:583
  9.0 2.0 %shard_map.64 = bf16[640,128]{1,0:T(8,128)(2,1)} custom-call(s32[3]{0:T(128)S(1)} %pad_add_fusion.rank_ref.scalars, s32[64,1]{1,0:T(8,128)S(1)} %copy.8.keep_ref, bf16[160,1024]{1,0:T(8,128)(2,1)S(1)} %reshape.15.patches_ref), custom_call_target="tpu_custom_call" | custom-call | tf_op jit(solution)/shard_map/pallas_call | solution.py:240
  12.1 5.8 %all-to-all-start = ((bf16[8,80,128]{2,1,0:T(8,128)(2,1)}), bf16[8,80,128]{2,1,0:T(8,128)(2,1)S(1)}, u32[]{:S(2)}, u32[]{:S(2)}) async-start(bf16[8,80,128]{2,1,0:T(8,128)(2,1)} %bitcast.5), calls=%async_computation | async-start | bytes 327680 | tf_op jit(solution)/shard_map/all_to_all | solution.py:587
  17.9 2.9 %collective-permute-start.4 = (bf16[512,128]{1,0:T(8,128)(2,1)S(1)}, bf16[512,128]{1,0:T(8,128)(2,1)S(1)}, u32[]{:S(2)}, u32[]{:S(2)}) collective-permute-start(bf16[512,128]{1,0:T(8,128)(2,1)S(1)} %copy-done.1), channel_id=1, source_target_pairs={{0,6},{2,4},{4,2},{6,0},{8,14},{10,12},{12,10},{14,8},{1,7},{3,5},... | collective-permute-start | bytes 393224 | tf_op jit(solution)/shard_map/ppermute | solution.py:583
  21.4 1.5 %collective-permute-start.1 = (bf16[384,128]{1,0:T(8,128)(2,1)S(1)}, bf16[384,128]{1,0:T(8,128)(2,1)S(1)}, u32[]{:S(2)}, u32[]{:S(2)}) collective-permute-start(bf16[384,128]{1,0:T(8,128)(2,1)S(1)} %collective-permute-done.mine_ref), channel_id=1, source_target_pairs={{0,16},{16,0},{1,17},{17,1},{2,18},{18,2},{3,19},{19,3},{4,20},{20... | collective-permute-start | bytes 294920 | tf_op jit(solution)/shard_map/ppermute | solution.py:583
  22.9 2.9 %collective-permute-start.6 = (bf16[256,128]{1,0:T(8,128)(2,1)S(1)}, bf16[256,128]{1,0:T(8,128)(2,1)S(1)}, u32[]{:S(2)}, u32[]{:S(2)}) collective-permute-start(bf16[256,128]{1,0:T(8,128)(2,1)S(1)} %get-tuple-element.80), channel_id=1, source_target_pairs={{0,8},{2,10},{4,12},{6,14},{8,0},{10,2},{12,4},{14,6},{1,9},{3,11}... | collective-permute-start | bytes 196616 | tf_op jit(solution)/shard_map/ppermute | solution.py:583
  26.0 1.7 %shard_map.66 = (bf16[512,128]{1,0:T(8,128)(2,1)S(1)}, bf16[512,128]{1,0:T(8,128)(2,1)}, bf16[512,128]{1,0:T(8,128)(2,1)}, bf16[512,128]{1,0:T(8,128)(2,1)}, bf16[4,256,128]{2,1,0:T(8,128)(2,1)S(1)}) custom-call(s32[3]{0:T(128)S(1)} %pad_add_fusion.rank_ref.scalars, bf16[128,2048]{1,0:T(8,128)(2,1)S(1)} %copy-done.2, bf16[2048,128]{1,0:T(8,128)(2,1)S(1)} %copy-done.3), custom_call_target="tpu_custom_call" | custom-call | tf_op jit(solution)/shard_map/pallas_call | solution.py:319
  28.5 2.1 %collective-permute-done.3.refs_6_ = bf16[512,128]{1,0:T(8,128)(2,1)S(1)} collective-permute-done((bf16[512,128]{1,0:T(8,128)(2,1)S(1)}, bf16[512,128]{1,0:T(8,128)(2,1)S(1)}, u32[]{:S(2)}, u32[]{:S(2)}) %collective-permute-start.3) | collective-permute-done | bytes 131104 | tf_op jit(solution)/shard_map/ppermute | solution.py:583
  31.5 1.2 collective-permute-start.5
  32.7 4.0 %collective-permute-done.5.across_ref = bf16[256,128]{1,0:T(8,128)(2,1)S(1)} collective-permute-done((bf16[256,128]{1,0:T(8,128)(2,1)S(1)}, bf16[256,128]{1,0:T(8,128)(2,1)S(1)}, u32[]{:S(2)}, u32[]{:S(2)}) %collective-permute-start.5) | collective-permute-done | bytes 65568 | tf_op jit(solution)/shard_map/ppermute | solution.py:583
  36.8 1.7 %shard_map.68 = bf16[4,1152,128]{2,1,0:T(8,128)(2,1)} custom-call(s32[3]{0:T(128)S(1)} %pad_add_fusion.rank_ref.scalars, bf16[256,128]{1,0:T(8,128)(2,1)S(1)} %shard_map.67.owned_ref, bf16[256,128]{1,0:T(8,128)(2,1)S(1)} %collective-permute-done.5.across_ref, bf16[384,128]{1,0:T(8,128)(2,1)S(1)} %collective-permute-done.mine_ref, ...), custom_call_target="tpu_custom_call" | custom-call | tf_op jit(solution)/shard_map/pallas_call | solution.py:381
  38.5 3.5 %all-to-all-start.1 = ((bf16[4,1152,128]{2,1,0:T(8,128)(2,1)}), bf16[4,1152,128]{2,1,0:T(8,128)(2,1)S(1)}, u32[]{:S(2)}, u32[]{:S(2)}) async-start(bf16[4,1152,128]{2,1,0:T(8,128)(2,1)} %shard_map.68), calls=%async_computation.1 | async-start | bytes 2359296 | tf_op jit(solution)/shard_map/all_to_all | solution.py:593
  42.0 1.7 %collective-permute-start.7 = (bf16[4,256,128]{2,1,0:T(8,128)(2,1)S(1)}, bf16[4,256,128]{2,1,0:T(8,128)(2,1)}, u32[]{:S(2)}, u32[]{:S(2)}) collective-permute-start(bf16[4,256,128]{2,1,0:T(8,128)(2,1)S(1)} %get-tuple-element.82), channel_id=1, source_target_pairs={{0,8},{2,10},{4,12},{6,14},{8,0},{10,2},{12,4},{14,6},{1,9},{3,11}... | collective-permute-start | bytes 786440 | tf_op jit(solution)/shard_map/ppermute | solution.py:583
  45.8 13.4 %collective-permute-done.7 = bf16[4,256,128]{2,1,0:T(8,128)(2,1)} collective-permute-done((bf16[4,256,128]{2,1,0:T(8,128)(2,1)S(1)}, bf16[4,256,128]{2,1,0:T(8,128)(2,1)}, u32[]{:S(2)}, u32[]{:S(2)}) %collective-permute-start.7) | collective-permute-done | bytes 262176 | tf_op jit(solution)/shard_map/ppermute | solution.py:583
  59.2 2.1 %all-to-all-done.1.mine_ref = bf16[4,1152,128]{2,1,0:T(8,128)(2,1)S(1)} async-done(((bf16[4,1152,128]{2,1,0:T(8,128)(2,1)}), bf16[4,1152,128]{2,1,0:T(8,128)(2,1)S(1)}, u32[]{:S(2)}, u32[]{:S(2)}) %all-to-all-start.1) | async-done | bytes 1179680 | tf_op jit(solution)/shard_map/all_to_all | solution.py:593
  62.2 3.4 %all-to-all-start.2 = ((bf16[4,256,128]{2,1,0:T(8,128)(2,1)}), bf16[4,256,128]{2,1,0:T(8,128)(2,1)S(1)}, u32[]{:S(2)}, u32[]{:S(2)}) async-start(bf16[4,256,128]{2,1,0:T(8,128)(2,1)} %collective-permute-done.7), calls=%async_computation.2 | async-start | bytes 524288 | tf_op jit(solution)/shard_map/all_to_all | solution.py:593
  65.6 2.0 %collective-permute-start.15 = (bf16[512,128]{1,0:T(8,128)(2,1)}, bf16[512,128]{1,0:T(8,128)(2,1)S(1)}, u32[]{:S(2)}, u32[]{:S(2)}) collective-permute-start(bf16[512,128]{1,0:T(8,128)(2,1)} %get-tuple-element.100), channel_id=1, source_target_pairs={{0,2},{2,0},{4,6},{6,4},{8,10},{10,8},{12,14},{14,12},{1,3},{3,1},... | collective-permute-start | bytes 393224 | tf_op jit(solution)/shard_map/ppermute | solution.py:583
  67.6 1.5 %collective-permute-start.16 = (bf16[512,128]{1,0:T(8,128)(2,1)}, bf16[512,128]{1,0:T(8,128)(2,1)S(1)}, u32[]{:S(2)}, u32[]{:S(2)}) collective-permute-start(bf16[512,128]{1,0:T(8,128)(2,1)} %get-tuple-element.101), channel_id=1, source_target_pairs={{0,4},{2,6},{4,0},{6,2},{8,12},{10,14},{12,8},{14,10},{1,5},{3,7},... | collective-permute-start | bytes 393224 | tf_op jit(solution)/shard_map/ppermute | solution.py:583
  69.2 1.5 %collective-permute-start.14 = (bf16[4,256,128]{2,1,0:T(8,128)(2,1)S(1)}, bf16[4,256,128]{2,1,0:T(8,128)(2,1)S(1)}, u32[]{:S(2)}, u32[]{:S(2)}) collective-permute-start(bf16[4,256,128]{2,1,0:T(8,128)(2,1)S(1)} %slice.7.e), channel_id=1, source_target_pairs={{0,16},{16,0},{1,17},{17,1},{2,18},{18,2},{3,19},{19,3},{4,20},{20... | collective-permute-start | bytes 786440 | tf_op jit(solution)/shard_map/ppermute | solution.py:583
  72.5 3.3 %shard_map.69 = (bf16[512,1024]{1,0:T(8,128)(2,1)S(1)}, bf16[64,512]{1,0:T(8,128)(2,1)}) custom-call(s32[3]{0:T(128)S(1)} %pad_add_fusion.rank_ref.scalars, bf16[4,1152,128]{2,1,0:T(8,128)(2,1)S(1)} %all-to-all-done.1.mine_ref, bf16[4,512,128]{2,1,0:T(8,128)(2,1)S(1)} %copy-done.22), custom_call_target="tpu_custom_call" | custom-call | flops 30000001024 | bytes 1048576 | tf_op jit(solution)/shard_map/pallas_call | solution.py:442
  75.9 1.4 %collective-permute-start.13 = (bf16[64,512]{1,0:T(8,128)(2,1)}, bf16[64,512]{1,0:T(8,128)(2,1)S(1)}, u32[]{:S(2)}, u32[]{:S(2)}) collective-permute-start(bf16[64,512]{1,0:T(8,128)(2,1)} %get-tuple-element.97), channel_id=1, source_target_pairs={{0,8},{2,10},{4,12},{6,14},{8,0},{10,2},{12,4},{14,6},{1,9},{3,11}... | collective-permute-start | bytes 196616 | tf_op jit(solution)/shard_map/ppermute | solution.py:583
  79.3 2.2 %collective-permute-done.13 = bf16[64,512]{1,0:T(8,128)(2,1)S(1)} collective-permute-done((bf16[64,512]{1,0:T(8,128)(2,1)}, bf16[64,512]{1,0:T(8,128)(2,1)S(1)}, u32[]{:S(2)}, u32[]{:S(2)}) %collective-permute-start.13) | collective-permute-done | bytes 65568 | tf_op jit(solution)/shard_map/ppermute | solution.py:583
  82.9 1.8 %collective-permute-start.20 = (bf16[2,64,512]{2,1,0:T(8,128)(2,1)S(1)}, bf16[2,64,512]{2,1,0:T(8,128)(2,1)S(1)}, u32[]{:S(2)}, u32[]{:S(2)}) collective-permute-start(bf16[2,64,512]{2,1,0:T(8,128)(2,1)S(1)} %get-tuple-element.124), channel_id=1, source_target_pairs={{0,4},{2,6},{4,0},{6,2},{8,12},{10,14},{12,8},{14,10},{1,5},{3,7},... | collective-permute-start | bytes 393224 | tf_op jit(solution)/shard_map/ppermute | solution.py:583
  84.7 1.5 %collective-permute-start.19 = (bf16[2,64,512]{2,1,0:T(8,128)(2,1)S(1)}, bf16[2,64,512]{2,1,0:T(8,128)(2,1)S(1)}, u32[]{:S(2)}, u32[]{:S(2)}) collective-permute-start(bf16[2,64,512]{2,1,0:T(8,128)(2,1)S(1)} %get-tuple-element.124), channel_id=1, source_target_pairs={{0,2},{2,0},{4,6},{6,4},{8,10},{10,8},{12,14},{14,12},{1,3},{3,1},... | collective-permute-start | bytes 393224 | tf_op jit(solution)/shard_map/ppermute | solution.py:583
  86.5 2.2 %collective-permute-done.20 = bf16[2,64,512]{2,1,0:T(8,128)(2,1)S(1)} collective-permute-done((bf16[2,64,512]{2,1,0:T(8,128)(2,1)S(1)}, bf16[2,64,512]{2,1,0:T(8,128)(2,1)S(1)}, u32[]{:S(2)}, u32[]{:S(2)}) %collective-permute-start.20) | collective-permute-done | bytes 131104 | tf_op jit(solution)/shard_map/ppermute | solution.py:583
  88.7 1.2 collective-permute-done.19
  89.9 2.2 %collective-permute-done.21 = bf16[2,64,512]{2,1,0:T(8,128)(2,1)S(1)} collective-permute-done((bf16[2,64,512]{2,1,0:T(8,128)(2,1)S(1)}, bf16[2,64,512]{2,1,0:T(8,128)(2,1)S(1)}, u32[]{:S(2)}, u32[]{:S(2)}) %collective-permute-start.21) | collective-permute-done | bytes 131104 | tf_op jit(solution)/shard_map/ppermute | solution.py:583
  92.8 1.7 %collective-permute-done.23.g = bf16[4,256,128]{2,1,0:T(8,128)(2,1)S(1)} collective-permute-done((bf16[4,256,128]{2,1,0:T(8,128)(2,1)S(1)}, bf16[4,256,128]{2,1,0:T(8,128)(2,1)S(1)}, u32[]{:S(2)}, u32[]{:S(2)}) %collective-permute-start.23) | collective-permute-done | bytes 262176 | tf_op jit(solution)/shard_map/ppermute | solution.py:583
  94.9 4.9 %shard_map.70 = (f32[64,512]{1,0:T(8,128)S(1)}, f32[512,512]{1,0:T(8,128)S(1)}, bf16[512,512]{1,0:T(8,128)(2,1)S(1)}) custom-call(s32[3]{0:T(128)S(1)} %pad_add_fusion.rank_ref.scalars, bf16[512,1024]{1,0:T(8,128)(2,1)S(1)} %get-tuple-element.96.tokens, bf16[4,2,64,512]{3,2,1,0:T(8,128)(2,1)S(1)} %pad_maximum_fusion.a, ...), custom_call_target="tpu_custom_call" | custom-call | tf_op jit(solution)/shard_map/pallas_call | solution.py:525
  100.0 1.8 %collective-permute-done.25.got_ref = bf16[512,512]{1,0:T(8,128)(2,1)S(1)} collective-permute-done((bf16[512,512]{1,0:T(8,128)(2,1)S(1)}, bf16[512,512]{1,0:T(8,128)(2,1)S(1)}, u32[]{:S(2)}, u32[]{:S(2)}) %collective-permute-start.25) | collective-permute-done | bytes 524320 | tf_op jit(solution)/shard_map/ppermute | solution.py:583
  102.4 18.0 %all_to_all.27.terms_ref = bf16[8,64,512]{2,1,0:T(8,128)(2,1)S(1)} all-to-all(bf16[8,64,512]{2,1,0:T(8,128)(2,1)S(1)} %bitcast.17), channel_id=1, replica_groups=mesh['groups'=2,'seq'=8,'head'=2] {'seq'}, dimensions={0} | all-to-all | bytes 1048576 | tf_op jit(solution)/shard_map/all_to_all | solution.py:587
  120.4 1.2 %shard_map.72 = bf16[64,512]{1,0:T(8,128)(2,1)} custom-call(s32[3]{0:T(128)S(1)} %pad_add_fusion.rank_ref.scalars, f32[64,512]{1,0:T(8,128)S(1)} %get-tuple-element.121.base_ref, bf16[8,64,512]{2,1,0:T(8,128)(2,1)S(1)} %all_to_all.27.terms_ref), custom_call_target="tpu_custom_call" | custom-call | tf_op jit(solution)/shard_map/pallas_call | solution.py:572
  (89 shorter events, 19.1 us)
Async XLA Ops:
  2.0 24.0 %copy-start.3 = (bf16[2048,128]{1,0:T(8,128)(2,1)S(1)}, bf16[2048,128]{1,0:T(8,128)(2,1)}, u32[]{:S(2)}) copy-start(bf16[2048,128]{1,0:T(8,128)(2,1)} %down_ref) | copy-start | bytes 1572868
  3.1 9.0 %collective-permute-start = (bf16[384,128]{1,0:T(8,128)(2,1)S(1)}, bf16[384,128]{1,0:T(8,128)(2,1)S(1)}, u32[]{:S(2)}, u32[]{:S(2)}) collective-permute-start(bf16[384,128]{1,0:T(8,128)(2,1)S(1)} %get-tuple-element.64), channel_id=1, source_target_pairs={{0,8},{2,10},{4,12},{6,14},{8,0},{10,2},{12,4},{14,6},{1,9},{3,11}... | collective-permute-start | bytes 294920 | tf_op jit(solution)/shard_map/ppermute | solution.py:583
  12.1 18.5 %all-to-all-start = ((bf16[8,80,128]{2,1,0:T(8,128)(2,1)}), bf16[8,80,128]{2,1,0:T(8,128)(2,1)S(1)}, u32[]{:S(2)}, u32[]{:S(2)}) async-start(bf16[8,80,128]{2,1,0:T(8,128)(2,1)} %bitcast.5), calls=%async_computation | async-start | bytes 327680 | tf_op jit(solution)/shard_map/all_to_all | solution.py:587
  17.9 10.6 %collective-permute-start.4 = (bf16[512,128]{1,0:T(8,128)(2,1)S(1)}, bf16[512,128]{1,0:T(8,128)(2,1)S(1)}, u32[]{:S(2)}, u32[]{:S(2)}) collective-permute-start(bf16[512,128]{1,0:T(8,128)(2,1)S(1)} %copy-done.1), channel_id=1, source_target_pairs={{0,6},{2,4},{4,2},{6,0},{8,14},{10,12},{12,10},{14,8},{1,7},{3,5},... | collective-permute-start | bytes 393224 | tf_op jit(solution)/shard_map/ppermute | solution.py:583
  20.8 9.8 %collective-permute-start.3 = (bf16[512,128]{1,0:T(8,128)(2,1)S(1)}, bf16[512,128]{1,0:T(8,128)(2,1)S(1)}, u32[]{:S(2)}, u32[]{:S(2)}) collective-permute-start(bf16[512,128]{1,0:T(8,128)(2,1)S(1)} %copy-done.1), channel_id=1, source_target_pairs={{0,4},{2,6},{4,0},{6,2},{8,12},{10,14},{12,8},{14,10},{1,5},{3,7},... | collective-permute-start | bytes 393224 | tf_op jit(solution)/shard_map/ppermute | solution.py:583
  21.3 9.2 %collective-permute-start.2 = (bf16[512,128]{1,0:T(8,128)(2,1)S(1)}, bf16[512,128]{1,0:T(8,128)(2,1)S(1)}, u32[]{:S(2)}, u32[]{:S(2)}) collective-permute-start(bf16[512,128]{1,0:T(8,128)(2,1)S(1)} %copy-done.1), channel_id=1, source_target_pairs={{0,2},{2,0},{4,6},{6,4},{8,10},{10,8},{12,14},{14,12},{1,3},{3,1},... | collective-permute-start | bytes 393224 | tf_op jit(solution)/shard_map/ppermute | solution.py:583
  21.4 4.6 %collective-permute-start.1 = (bf16[384,128]{1,0:T(8,128)(2,1)S(1)}, bf16[384,128]{1,0:T(8,128)(2,1)S(1)}, u32[]{:S(2)}, u32[]{:S(2)}) collective-permute-start(bf16[384,128]{1,0:T(8,128)(2,1)S(1)} %collective-permute-done.mine_ref), channel_id=1, source_target_pairs={{0,16},{16,0},{1,17},{17,1},{2,18},{18,2},{3,19},{19,3},{4,20},{20... | collective-permute-start | bytes 294920 | tf_op jit(solution)/shard_map/ppermute | solution.py:583
  22.9 9.8 %collective-permute-start.6 = (bf16[256,128]{1,0:T(8,128)(2,1)S(1)}, bf16[256,128]{1,0:T(8,128)(2,1)S(1)}, u32[]{:S(2)}, u32[]{:S(2)}) collective-permute-start(bf16[256,128]{1,0:T(8,128)(2,1)S(1)} %get-tuple-element.80), channel_id=1, source_target_pairs={{0,8},{2,10},{4,12},{6,14},{8,0},{10,2},{12,4},{14,6},{1,9},{3,11}... | collective-permute-start | bytes 196616 | tf_op jit(solution)/shard_map/ppermute | solution.py:583
  31.5 5.2 %collective-permute-start.5 = (bf16[256,128]{1,0:T(8,128)(2,1)S(1)}, bf16[256,128]{1,0:T(8,128)(2,1)S(1)}, u32[]{:S(2)}, u32[]{:S(2)}) collective-permute-start(bf16[256,128]{1,0:T(8,128)(2,1)S(1)} %shard_map.67.owned_ref), channel_id=1, source_target_pairs={{0,8},{2,10},{4,12},{6,14},{8,0},{10,2},{12,4},{14,6},{1,9},{3,11}... | collective-permute-start | bytes 196616 | tf_op jit(solution)/shard_map/ppermute | solution.py:583
  38.5 22.8 %all-to-all-start.1 = ((bf16[4,1152,128]{2,1,0:T(8,128)(2,1)}), bf16[4,1152,128]{2,1,0:T(8,128)(2,1)S(1)}, u32[]{:S(2)}, u32[]{:S(2)}) async-start(bf16[4,1152,128]{2,1,0:T(8,128)(2,1)} %shard_map.68), calls=%async_computation.1 | async-start | bytes 2359296 | tf_op jit(solution)/shard_map/all_to_all | solution.py:593
  42.0 17.2 %collective-permute-start.7 = (bf16[4,256,128]{2,1,0:T(8,128)(2,1)S(1)}, bf16[4,256,128]{2,1,0:T(8,128)(2,1)}, u32[]{:S(2)}, u32[]{:S(2)}) collective-permute-start(bf16[4,256,128]{2,1,0:T(8,128)(2,1)S(1)} %get-tuple-element.82), channel_id=1, source_target_pairs={{0,8},{2,10},{4,12},{6,14},{8,0},{10,2},{12,4},{14,6},{1,9},{3,11}... | collective-permute-start | bytes 786440 | tf_op jit(solution)/shard_map/ppermute | solution.py:583
  43.7 1.3 %collective-permute-start.8 = (bf16[512,128]{1,0:T(8,128)(2,1)S(1)}, bf16[512,128]{1,0:T(8,128)(2,1)S(1)}, u32[]{:S(2)}, u32[]{:S(2)}) collective-permute-start(bf16[512,128]{1,0:T(8,128)(2,1)S(1)} %copy-done.1), channel_id=1, source_target_pairs={{0,1},{1,0},{2,3},{3,2},{4,5},{5,4},{6,7},{7,6},{8,9},{9,8},{10,11... | collective-permute-start | bytes 393224 | tf_op jit(solution)/shard_map/ppermute | solution.py:583
  43.7 1.5 %collective-permute-start.9 = (bf16[512,128]{1,0:T(8,128)(2,1)S(1)}, bf16[512,128]{1,0:T(8,128)(2,1)S(1)}, u32[]{:S(2)}, u32[]{:S(2)}) collective-permute-start(bf16[512,128]{1,0:T(8,128)(2,1)S(1)} %collective-permute-done.2.refs_5_), channel_id=1, source_target_pairs={{0,1},{1,0},{2,3},{3,2},{4,5},{5,4},{6,7},{7,6},{8,9},{9,8},{10,11... | collective-permute-start | bytes 393224 | tf_op jit(solution)/shard_map/ppermute | solution.py:583
  44.2 1.3 %collective-permute-start.10 = (bf16[512,128]{1,0:T(8,128)(2,1)S(1)}, bf16[512,128]{1,0:T(8,128)(2,1)S(1)}, u32[]{:S(2)}, u32[]{:S(2)}) collective-permute-start(bf16[512,128]{1,0:T(8,128)(2,1)S(1)} %collective-permute-done.3.refs_6_), channel_id=1, source_target_pairs={{0,1},{1,0},{2,3},{3,2},{4,5},{5,4},{6,7},{7,6},{8,9},{9,8},{10,11... | collective-permute-start | bytes 393224 | tf_op jit(solution)/shard_map/ppermute | solution.py:583
  44.2 1.5 %collective-permute-start.11 = (bf16[512,128]{1,0:T(8,128)(2,1)S(1)}, bf16[512,128]{1,0:T(8,128)(2,1)S(1)}, u32[]{:S(2)}, u32[]{:S(2)}) collective-permute-start(bf16[512,128]{1,0:T(8,128)(2,1)S(1)} %collective-permute-done.4.refs_7_), channel_id=1, source_target_pairs={{0,1},{1,0},{2,3},{3,2},{4,5},{5,4},{6,7},{7,6},{8,9},{9,8},{10,11... | collective-permute-start | bytes 393224 | tf_op jit(solution)/shard_map/ppermute | solution.py:583
  45.6 25.1 %copy-start.11 = (bf16[512,128]{1,0:T(8,128)(2,1)}, bf16[512,128]{1,0:T(8,128)(2,1)S(1)}, u32[]{:S(2)}) copy-start(bf16[512,128]{1,0:T(8,128)(2,1)S(1)} %collective-permute-done.10.refs_10_) | copy-start | bytes 393220
  45.8 24.9 %copy-start.13 = (bf16[512,128]{1,0:T(8,128)(2,1)}, bf16[512,128]{1,0:T(8,128)(2,1)S(1)}, u32[]{:S(2)}) copy-start(bf16[512,128]{1,0:T(8,128)(2,1)S(1)} %collective-permute-done.11.refs_11_) | copy-start | bytes 393220
  62.2 8.5 %collective-permute-start.12 = (bf16[4,512,128]{2,1,0:T(8,128)(2,1)}, bf16[4,512,128]{2,1,0:T(8,128)(2,1)S(1)}, u32[]{:S(2)}, u32[]{:S(2)}) collective-permute-start(bf16[4,512,128]{2,1,0:T(8,128)(2,1)} %slice.6), channel_id=1, source_target_pairs={{0,1},{1,0},{2,3},{3,2},{4,5},{5,4},{6,7},{7,6},{8,9},{9,8},{10,11... | collective-permute-start | bytes 1572872 | tf_op jit(solution)/shard_map/ppermute | solution.py:583
  62.2 17.1 %all-to-all-start.2 = ((bf16[4,256,128]{2,1,0:T(8,128)(2,1)}), bf16[4,256,128]{2,1,0:T(8,128)(2,1)S(1)}, u32[]{:S(2)}, u32[]{:S(2)}) async-start(bf16[4,256,128]{2,1,0:T(8,128)(2,1)} %collective-permute-done.7), calls=%async_computation.2 | async-start | bytes 524288 | tf_op jit(solution)/shard_map/all_to_all | solution.py:593
  65.6 11.7 %collective-permute-start.15 = (bf16[512,128]{1,0:T(8,128)(2,1)}, bf16[512,128]{1,0:T(8,128)(2,1)S(1)}, u32[]{:S(2)}, u32[]{:S(2)}) collective-permute-start(bf16[512,128]{1,0:T(8,128)(2,1)} %get-tuple-element.100), channel_id=1, source_target_pairs={{0,2},{2,0},{4,6},{6,4},{8,10},{10,8},{12,14},{14,12},{1,3},{3,1},... | collective-permute-start | bytes 393224 | tf_op jit(solution)/shard_map/ppermute | solution.py:583
  67.6 10.4 %collective-permute-start.16 = (bf16[512,128]{1,0:T(8,128)(2,1)}, bf16[512,128]{1,0:T(8,128)(2,1)S(1)}, u32[]{:S(2)}, u32[]{:S(2)}) collective-permute-start(bf16[512,128]{1,0:T(8,128)(2,1)} %get-tuple-element.101), channel_id=1, source_target_pairs={{0,4},{2,6},{4,0},{6,2},{8,12},{10,14},{12,8},{14,10},{1,5},{3,7},... | collective-permute-start | bytes 393224 | tf_op jit(solution)/shard_map/ppermute | solution.py:583
  69.1 9.6 %collective-permute-start.17 = (bf16[512,128]{1,0:T(8,128)(2,1)}, bf16[512,128]{1,0:T(8,128)(2,1)S(1)}, u32[]{:S(2)}, u32[]{:S(2)}) collective-permute-start(bf16[512,128]{1,0:T(8,128)(2,1)} %get-tuple-element.102), channel_id=1, source_target_pairs={{0,6},{2,4},{4,2},{6,0},{8,14},{10,12},{12,10},{14,8},{1,7},{3,5},... | collective-permute-start | bytes 393224 | tf_op jit(solution)/shard_map/ppermute | solution.py:583
  69.2 10.1 %collective-permute-start.14 = (bf16[4,256,128]{2,1,0:T(8,128)(2,1)S(1)}, bf16[4,256,128]{2,1,0:T(8,128)(2,1)S(1)}, u32[]{:S(2)}, u32[]{:S(2)}) collective-permute-start(bf16[4,256,128]{2,1,0:T(8,128)(2,1)S(1)} %slice.7.e), channel_id=1, source_target_pairs={{0,16},{16,0},{1,17},{17,1},{2,18},{18,2},{3,19},{19,3},{4,20},{20... | collective-permute-start | bytes 786440 | tf_op jit(solution)/shard_map/ppermute | solution.py:583
  75.9 5.6 %collective-permute-start.13 = (bf16[64,512]{1,0:T(8,128)(2,1)}, bf16[64,512]{1,0:T(8,128)(2,1)S(1)}, u32[]{:S(2)}, u32[]{:S(2)}) collective-permute-start(bf16[64,512]{1,0:T(8,128)(2,1)} %get-tuple-element.97), channel_id=1, source_target_pairs={{0,8},{2,10},{4,12},{6,14},{8,0},{10,2},{12,4},{14,6},{1,9},{3,11}... | collective-permute-start | bytes 196616 | tf_op jit(solution)/shard_map/ppermute | solution.py:583
  81.5 10.5 %collective-permute-start.18 = (bf16[4,256,128]{2,1,0:T(8,128)(2,1)S(1)}, bf16[4,256,128]{2,1,0:T(8,128)(2,1)S(1)}, u32[]{:S(2)}, u32[]{:S(2)}) collective-permute-start(bf16[4,256,128]{2,1,0:T(8,128)(2,1)S(1)} %all-to-all-done.2.c), channel_id=1, source_target_pairs={{0,16},{16,0},{1,17},{17,1},{2,18},{18,2},{3,19},{19,3},{4,20},{20... | collective-permute-start | bytes 786440 | tf_op jit(solution)/shard_map/ppermute | solution.py:583
  82.9 5.8 %collective-permute-start.20 = (bf16[2,64,512]{2,1,0:T(8,128)(2,1)S(1)}, bf16[2,64,512]{2,1,0:T(8,128)(2,1)S(1)}, u32[]{:S(2)}, u32[]{:S(2)}) collective-permute-start(bf16[2,64,512]{2,1,0:T(8,128)(2,1)S(1)} %get-tuple-element.124), channel_id=1, source_target_pairs={{0,4},{2,6},{4,0},{6,2},{8,12},{10,14},{12,8},{14,10},{1,5},{3,7},... | collective-permute-start | bytes 393224 | tf_op jit(solution)/shard_map/ppermute | solution.py:583
  84.7 5.2 %collective-permute-start.19 = (bf16[2,64,512]{2,1,0:T(8,128)(2,1)S(1)}, bf16[2,64,512]{2,1,0:T(8,128)(2,1)S(1)}, u32[]{:S(2)}, u32[]{:S(2)}) collective-permute-start(bf16[2,64,512]{2,1,0:T(8,128)(2,1)S(1)} %get-tuple-element.124), channel_id=1, source_target_pairs={{0,2},{2,0},{4,6},{6,4},{8,10},{10,8},{12,14},{14,12},{1,3},{3,1},... | collective-permute-start | bytes 393224 | tf_op jit(solution)/shard_map/ppermute | solution.py:583
  86.2 5.9 %collective-permute-start.21 = (bf16[2,64,512]{2,1,0:T(8,128)(2,1)S(1)}, bf16[2,64,512]{2,1,0:T(8,128)(2,1)S(1)}, u32[]{:S(2)}, u32[]{:S(2)}) collective-permute-start(bf16[2,64,512]{2,1,0:T(8,128)(2,1)S(1)} %get-tuple-element.124), channel_id=1, source_target_pairs={{0,6},{2,4},{4,2},{6,0},{8,14},{10,12},{12,10},{14,8},{1,7},{3,5},... | collective-permute-start | bytes 393224 | tf_op jit(solution)/shard_map/ppermute | solution.py:583
  92.1 2.7 %collective-permute-start.22 = (bf16[4,2,64,512]{3,2,1,0:T(8,128)(2,1)S(1)}, bf16[4,2,64,512]{3,2,1,0:T(8,128)(2,1)S(1)}, u32[]{:S(2)}, u32[]{:S(2)}) collective-permute-start(bf16[4,2,64,512]{3,2,1,0:T(8,128)(2,1)S(1)} %pad_maximum_fusion.a), channel_id=1, source_target_pairs={{0,1},{1,0},{2,3},{3,2},{4,5},{5,4},{6,7},{7,6},{8,9},{9,8},{10,11... | collective-permute-start | bytes 1572872 | tf_op jit(solution)/shard_map/ppermute | solution.py:583
  92.2 2.3 %collective-permute-start.23 = (bf16[4,256,128]{2,1,0:T(8,128)(2,1)S(1)}, bf16[4,256,128]{2,1,0:T(8,128)(2,1)S(1)}, u32[]{:S(2)}, u32[]{:S(2)}) collective-permute-start(bf16[4,256,128]{2,1,0:T(8,128)(2,1)S(1)} %slice.7.e), channel_id=1, source_target_pairs={{0,1},{1,0},{2,3},{3,2},{4,5},{5,4},{6,7},{7,6},{8,9},{9,8},{10,11... | collective-permute-start | bytes 786440 | tf_op jit(solution)/shard_map/ppermute | solution.py:583
  92.7 2.1 %collective-permute-start.24 = (bf16[4,256,128]{2,1,0:T(8,128)(2,1)S(1)}, bf16[4,256,128]{2,1,0:T(8,128)(2,1)S(1)}, u32[]{:S(2)}, u32[]{:S(2)}) collective-permute-start(bf16[4,256,128]{2,1,0:T(8,128)(2,1)S(1)} %collective-permute-done.14.f), channel_id=1, source_target_pairs={{0,1},{1,0},{2,3},{3,2},{4,5},{5,4},{6,7},{7,6},{8,9},{9,8},{10,11... | collective-permute-start | bytes 786440 | tf_op jit(solution)/shard_map/ppermute | solution.py:583
  99.8 2.0 %collective-permute-start.25 = (bf16[512,512]{1,0:T(8,128)(2,1)S(1)}, bf16[512,512]{1,0:T(8,128)(2,1)S(1)}, u32[]{:S(2)}, u32[]{:S(2)}) collective-permute-start(bf16[512,512]{1,0:T(8,128)(2,1)S(1)} %get-tuple-element.119), channel_id=1, source_target_pairs={{0,1},{1,0},{2,3},{3,2},{4,5},{5,4},{6,7},{7,6},{8,9},{9,8},{10,11... | collective-permute-start | bytes 1572872 | tf_op jit(solution)/shard_map/ppermute | solution.py:583
  (20 other events, 236.5 us)

commit v8 on v7

--- a/solution.py
+++ b/solution.py
@@ -11,7 +11,6 @@
 F32 = jnp.float32
 BF16 = jnp.bfloat16
 VMEM = pltpu.VMEM
-LIMIT = 24 * 1024 * 1024
 
 def layer_norm(matrix):
     average = jnp.mean(matrix, axis=-1, keepdims=True)
@@ -168,8 +167,8 @@
     return wait
 
 
-def params():
-    return pltpu.CompilerParams(vmem_limit_bytes=LIMIT)
+def params(mebibytes=4):
+    return pltpu.CompilerParams(vmem_limit_bytes=mebibytes * 1024 * 1024)
 
 
 def cost(micros):
@@ -290,13 +289,14 @@
     )(scalars, keep_col, got)
 
 
-def pack_kernel(n, rank_ref, up_ref, down_ref, *refs):
+def pack_kernel(n, rank_ref, out_weight_ref, up_ref, down_ref, *refs):
     near, away_ref, sem = refs[: n // 2], refs[n // 2], refs[n // 2 + 1]
     rank, part = rank_ref[0], rank_ref[2]
     half = n // 2
     rows = up_ref.shape[0]
     wide = up_ref.shape[1] // n
     units = wide // 2
+    long = out_weight_ref.shape[0]
     copies = []
     for j in range(half):
         dest = rank ^ j
@@ -305,6 +305,7 @@
             copies.append((up_ref.at[:, at], near[j].at[pl.ds(c * rows, rows)]))
         at = pl.ds(pl.multiple_of(dest * wide, 128), wide)
         copies.append((down_ref.at[at], near[j].at[pl.ds(2 * rows, wide)]))
+        copies.append((out_weight_ref, near[j].at[pl.ds(2 * rows + wide, long)]))
         dest = (rank // half ^ 1) * half + j
         at = pl.ds(pl.multiple_of(dest * wide + part * units, 128), units)
         copies.append((up_ref.at[:, at], away_ref.at[j, pl.ds(0, rows)]))
@@ -312,18 +313,18 @@
     run_copies(copies, sem)()
 
 
-def pack(scalars, up, down, n):
+def pack(scalars, out_weight, up, down, n):
     wide = up.shape[1] // n
-    near = struct((2 * up.shape[0] + wide, 128))
+    near = struct((2 * up.shape[0] + wide + out_weight.shape[0], 128))
     away = struct((n // 2, up.shape[0] + wide // 2, 128))
     outs = pl.pallas_call(
         functools.partial(pack_kernel, n),
-        in_specs=[sspec()] + [hspec()] * 2,
-        out_specs=[hspec()] * (n // 2) + [aspec()],
+        in_specs=[sspec()] + [hspec()] * 3,
+        out_specs=[aspec()] * (n // 2 + 1),
         out_shape=[near] * (n // 2) + [away],
-        scratch_shapes=[pltpu.SemaphoreType.DMA((5 * n // 2,))],
+        scratch_shapes=[pltpu.SemaphoreType.DMA((6 * n // 2,))],
         compiler_params=params(),
-    )(scalars, up, down)
+    )(scalars, out_weight, up, down)
     return list(outs[:-1]), outs[-1]
 
 
@@ -445,7 +446,7 @@
         out_specs=[vspec()] * 2,
         out_shape=[struct((length, depth)), struct((size, length))],
         scratch_shapes=[VMEM((head_rows, n * 128), BF16)],
-        compiler_params=params(),
+        compiler_params=params(12),
         cost_estimate=cost(30),
     )(scalars, mine, other)
 
@@ -470,7 +471,8 @@
             )
         later.append((near[j].at[pl.ds(2 * block, wide)], down_ref.at[:, to]))
         for core in range(2):
-            first.append((outs_near[core][j], whole_ref.at[core, :, to]))
+            rows_from = outs_near[core][j].at[pl.ds(2 * block + wide, 2 * rows)]
+            first.append((rows_from, whole_ref.at[core, :, to]))
         source = source_of(rank, n, j, 1)
         at = pl.ds(pl.multiple_of(source * block, block), block)
         to = pl.ds(pl.multiple_of(source * 128, 128), 128)
@@ -509,7 +511,7 @@
     send_ref[...] = jnp.dot(hidden, down_ref[:, other_cols], preferred_element_type=F32).astype(BF16)
 
 
-def mlp(scalars, tokens, pieces, far, outs_far, near, outs_near, n):
+def mlp(scalars, tokens, pieces, far, outs_far, near, near_other, n):
     length, depth = tokens.shape
     width = depth // 2
     wide = 2 * (far[0].shape[1] - depth // n)
@@ -517,14 +519,14 @@
     half = n // 2
 
     def kernel(scalars, tokens, a, b, c, d, e, f, g, h, *refs):
-        near, mine, other = refs[:half], refs[half : 2 * half], refs[2 * half : 3 * half]
-        outs, scratch = refs[3 * half : 3 * half + 3], refs[3 * half + 3 :]
-        far, outs_far, outs_near = (c, d), ((e, f), (g, h)), (mine, other)
+        near, other = refs[:half], refs[half : 2 * half]
+        outs, scratch = refs[2 * half : 2 * half + 3], refs[2 * half + 3 :]
+        far, outs_far, outs_near = (c, d), ((e, f), (g, h)), (near, other)
         mlp_kernel(n, scalars, tokens, (a, b), far, outs_far, near, outs_near, outs, scratch)
 
     return pl.pallas_call(
         kernel,
-        in_specs=[sspec()] + [vspec()] * 3 + [hspec()] * (6 + 3 * half),
+        in_specs=[sspec()] + [vspec()] * 3 + [aspec()] * (6 + 2 * half),
         out_specs=[vspec()] * 3,
         out_shape=[
             struct((length // n, width), F32),
@@ -539,8 +541,8 @@
             VMEM((2, inner, length), BF16),
             pltpu.SemaphoreType.DMA((13 * half,)),
         ],
-        compiler_params=params(),
-    )(scalars, tokens, *pieces, *far, *outs_far[0], *outs_far[1], *near, *outs_near[0], *outs_near[1])
+        compiler_params=params(20),
+    )(scalars, tokens, *pieces, *far, *outs_far[0], *outs_far[1], *near, *near_other)
 
 
 def join_kernel(rank_ref, keep_ref, got_ref, residual_ref, base_ref, out_ref):
@@ -556,7 +558,7 @@
         in_specs=[sspec()] + [vspec()] * 3,
         out_specs=[vspec()] * 2,
         out_shape=[struct(residual.shape, F32), struct(keep.shape)],
-        compiler_params=params(),
+        compiler_params=params(8),
     )(scalars, keep, got, residual)
 
 
@@ -574,7 +576,7 @@
         in_specs=[sspec()] + [vspec()] * 2,
         out_specs=vspec(),
         out_shape=struct(base.shape),
-        compiler_params=params(),
+        compiler_params=params(8),
     )(scalars, base, terms)
 
 
@@ -616,46 +618,38 @@
     flat = patches.reshape(4 * sup, depth)
     heads = qkv_weight.transpose(1, 2, 0)
 
+    slots = prep(scalars, keep_col, flat, n, sup, capacity)
     qkv_away, qkv_near, out_away = early_blocks(scalars, heads, out_weight, n)
-    qkv_mine = swap(qkv_away, "seq", half)
-    slots = prep(scalars, keep_col, flat, n, sup, capacity)
-    slots, qkv_mine = lax.optimization_barrier((slots, qkv_mine))
     dealt = exchange(slots)
+    qkv_mine = swap(after(qkv_away, slots), "seq", half)
     out_far = swap(after(out_away, slots), "seq", half)
     qkv_other = swap(qkv_mine, "groups", 1)
-    own_rows = after(out_weight, slots)
-    outs_near = [out_weight] + [swap(own_rows, "seq", j) for j in range(1, half)]
-    up, down, qkv_other = lax.optimization_barrier((up_weight, down_weight, qkv_other))
-    near, mlp_away = pack(scalars, up, down, n)
-    dealt, qkv_other, mlp_away, *rest = lax.optimization_barrier(
-        (dealt, qkv_other, mlp_away, *near, *outs_near)
-    )
-    near, outs_near = rest[:half], rest[half:]
+    blocks = lax.optimization_barrier((out_weight, up_weight, down_weight, qkv_mine))[:3]
+    near, mlp_away = pack(scalars, *blocks, n)
+    near = [near[0]] + [swap(near[j], "seq", j) for j in range(1, half)]
     owned = pick(scalars, keep_col, dealt, n, sup, per_owner, capacity)
 
     across = swap(owned, "seq", half)
+    across, out_far, qkv_other = lax.optimization_barrier((across, out_far, qkv_other))
     mlp_far = swap(after(mlp_away, across), "seq", half)
     got = exchange_half(fan(scalars, owned, across, qkv_mine, qkv_other, qkv_near, out_far))
-    outs_other = [swap(rows, "head", 1) for rows in lax.optimization_barrier((*outs_near, across))[:half]]
-    got, mlp_far, *rest = lax.optimization_barrier((got, mlp_far, *near, *outs_other))
-    near, outs_other = rest[:half], rest[half:]
+    near_other = [swap(block, "head", 1) for block in near]
+    got, mlp_far, *near_other = lax.optimization_barrier((got, mlp_far, *near_other))
 
     top = 2 * owned.shape[0]
     pieces_other = swap(got[:, :top], "head", 1)
-    near = [near[0]] + [swap(near[j], "seq", j) for j in range(1, half)]
+    tokens, attended = attend_fast(scalars, got, pieces_other, head_rows, per_owner, n)
+
+    att_across = swap(attended, "seq", half)
+    mlp_far, got = lax.optimization_barrier((mlp_far, got, attended))[:2]
     mlp_mine = exchange_half(mlp_far)
-    tokens, attended = attend_fast(scalars, got, pieces_other, head_rows, per_owner, n)
-
-    att_across = swap(attended, "seq", half)
     far_mine = got[:, top + 2 * head_rows :]
     far_other = swap(far_mine, "groups", 1)
-    att_across, mlp_mine, far_other, *near = lax.optimization_barrier(
-        (att_across, mlp_mine, far_other, *near)
-    )
+    att_across, mlp_mine = lax.optimization_barrier((att_across, mlp_mine))
     pair = jnp.stack([attended, att_across])
     mlp_other = swap(mlp_mine, "groups", 1)
     pairs = [swap(pair, "seq", j) for j in range(1, half)]
-    mlp_other, *pairs = lax.optimization_barrier((mlp_other, *pairs))
+    mlp_other, far_other, *pairs = lax.optimization_barrier((mlp_other, far_other, *pairs))
     gathered = jnp.stack([pair] + pairs)
     residual, keep, send = mlp(
         scalars,
@@ -664,7 +658,7 @@
         (mlp_mine, mlp_other),
         ((far_mine, far_other), (swap(far_mine, "head", 1), swap(far_other, "head", 1))),
         near,
-        (outs_near, outs_other),
+        near_other,
         n,
     )
     sent = swap(send, "head", 1)

time: 122 us -> 130 us (1.066)
  waiting for transfers between devices: 35.9 us -> 50.5 us
  starting transfers between devices: 40 us -> 34.5 us
  local copies, waits for them, and re-layouts: 9.07 us -> 7.08 us
    ppermute x26 -> x23, waiting for transfers between devices: 33.7 us -> 48.9 us  [swap(): return lax.ppermute(value, axis, [(i, i ^ j) for i in range(n)])]
    ppermute x26 -> x23, starting transfers between devices: 27.3 us -> 20 us  [swap(): return lax.ppermute(value, axis, [(i, i ^ j) for i in range(n)])]
    all_to_all x1, starting transfers between devices: 5.77 us -> 7.28 us  [exchange(): return lax.all_to_all(value, 'seq', split_axis=0, concat_axis=0, tiled=True)]
    unnamed x46 -> x34, local copies, waits for them, and re-layouts: 6.41 us -> 5.18 us
  transfers between devices with their start and end apart: 29 -> 26, of which waited for: 18 -> 15; matrix products, arithmetic and copies ran while one was open for 2% -> 1% of each run, Pallas kernels for 7% -> 3%
where the time goes in v8:
time: 130 us; the launch traced here: 129 us
  waiting for transfers between devices  50.5 us (39%)
  starting transfers between devices  34.5 us (27%)
  blocking collectives  18.4 us (14%)
  Pallas kernels  17.3 us (13%)
  local copies, waits for them, and re-layouts  7.08 us (5%)
    ppermute x23, waiting for transfers between devices, swap(): return lax.ppermute(value, axis, [(i, i ^ j) for i in range(n)])  48.9 us
    ppermute x23, starting transfers between devices, swap(): return lax.ppermute(value, axis, [(i, i ^ j) for i in range(n)])  20 us
    all_to_all x1, blocking collectives, exchange(): return lax.all_to_all(value, 'seq', split_axis=0, concat_axis=0, tiled=True)  18.4 us
    all_to_all x1, starting transfers between devices, exchange(): return lax.all_to_all(value, 'seq', split_axis=0, concat_axis=0, tiled=True)  7.28 us
    all_to_all x2, starting transfers between devices, exchange_half(): lax.all_to_all(value, 'seq', split_axis=0, concat_axis=0, axis_index_grou...  7.23 us
    unnamed x34, local copies, waits for them, and re-layouts  5.18 us
    pallas_call x1, Pallas kernels, mlp(): pl.pallas_call(kernel, in_specs=[sspec()] + [vspec()] * 3 + [aspec()] * (...  4.86 us
    pallas_call x1, Pallas kernels, attend_fast(): pl.pallas_call(functools.partial(attend_kernel, n, per_owner), in_specs=[...  2.68 us
  transfers between devices with their start and end apart: 26, of which 15 were waited for; matrix products, arithmetic and copies ran while one was open for 1% of the time, Pallas kernels for 3%

profile of v8, /device:TPU:0, one launch (start us, length us, event | category | flops | bytes accessed | tf_op | source)
XLA Modules:
  0.0 129.0 jit_solution(15464029231819200408)
XLA Ops:
  1.9 2.0 %shard_map.64 = bf16[640,128]{1,0:T(8,128)(2,1)} custom-call(s32[3]{0:T(128)S(1)} %pad_add_fusion.rank_ref.scalars, s32[64,1]{1,0:T(8,128)S(1)} %copy.8.keep_ref, bf16[160,1024]{1,0:T(8,128)(2,1)S(1)} %reshape.15.patches_ref), custom_call_target="tpu_custom_call" | custom-call | tf_op jit(solution)/shard_map/pallas_call | solution.py:239
  3.9 7.3 %all-to-all-start = ((bf16[8,80,128]{2,1,0:T(8,128)(2,1)}), bf16[8,80,128]{2,1,0:T(8,128)(2,1)S(1)}, u32[]{:S(2)}, u32[]{:S(2)}) async-start(bf16[8,80,128]{2,1,0:T(8,128)(2,1)} %bitcast.4), calls=%async_computation | async-start | bytes 327680 | tf_op jit(solution)/shard_map/all_to_all | solution.py:589
  11.2 1.1 shard_map.66
  12.3 3.0 %collective-permute-start.2 = (bf16[384,128]{1,0:T(8,128)(2,1)S(1)}, bf16[384,128]{1,0:T(8,128)(2,1)S(1)}, u32[]{:S(2)}, u32[]{:S(2)}) collective-permute-start(bf16[384,128]{1,0:T(8,128)(2,1)S(1)} %get-tuple-element.47), channel_id=1, source_target_pairs={{0,8},{2,10},{4,12},{6,14},{8,0},{10,2},{12,4},{14,6},{1,9},{3,11}... | collective-permute-start | bytes 294920 | tf_op jit(solution)/shard_map/ppermute | solution.py:585
  15.3 7.0 %collective-permute-done.2.mine_ref = bf16[384,128]{1,0:T(8,128)(2,1)S(1)} collective-permute-done((bf16[384,128]{1,0:T(8,128)(2,1)S(1)}, bf16[384,128]{1,0:T(8,128)(2,1)S(1)}, u32[]{:S(2)}, u32[]{:S(2)}) %collective-permute-start.2) | collective-permute-done | bytes 98336 | tf_op jit(solution)/shard_map/ppermute | solution.py:585
  22.3 1.5 %collective-permute-start.3 = (bf16[384,128]{1,0:T(8,128)(2,1)S(1)}, bf16[384,128]{1,0:T(8,128)(2,1)S(1)}, u32[]{:S(2)}, u32[]{:S(2)}) collective-permute-start(bf16[384,128]{1,0:T(8,128)(2,1)S(1)} %collective-permute-done.2.mine_ref), channel_id=1, source_target_pairs={{0,16},{16,0},{1,17},{17,1},{2,18},{18,2},{3,19},{19,3},{4,20},{20... | collective-permute-start | bytes 294920 | tf_op jit(solution)/shard_map/ppermute | solution.py:585
  24.7 3.0 %collective-permute-start = (bf16[256,128]{1,0:T(8,128)(2,1)S(1)}, bf16[256,128]{1,0:T(8,128)(2,1)S(1)}, u32[]{:S(2)}, u32[]{:S(2)}) collective-permute-start(bf16[256,128]{1,0:T(8,128)(2,1)S(1)} %shard_map.65.owned_ref), channel_id=1, source_target_pairs={{0,8},{2,10},{4,12},{6,14},{8,0},{10,2},{12,4},{14,6},{1,9},{3,11}... | collective-permute-start | bytes 196616 | tf_op jit(solution)/shard_map/ppermute | solution.py:585
  27.7 1.9 %collective-permute-done.1.rows_ref = bf16[256,128]{1,0:T(8,128)(2,1)S(1)} collective-permute-done((bf16[256,128]{1,0:T(8,128)(2,1)S(1)}, bf16[256,128]{1,0:T(8,128)(2,1)S(1)}, u32[]{:S(2)}, u32[]{:S(2)}) %collective-permute-start.1) | collective-permute-done | bytes 65568 | tf_op jit(solution)/shard_map/ppermute | solution.py:585
  30.3 1.7 %shard_map.67 = bf16[4,1152,128]{2,1,0:T(8,128)(2,1)} custom-call(s32[3]{0:T(128)S(1)} %pad_add_fusion.rank_ref.scalars, bf16[256,128]{1,0:T(8,128)(2,1)S(1)} %shard_map.65.owned_ref, bf16[256,128]{1,0:T(8,128)(2,1)S(1)} %collective-permute-done.across_ref, bf16[384,128]{1,0:T(8,128)(2,1)S(1)} %collective-permute-done.2.mine_ref, ...), custom_call_target="tpu_custom_call" | custom-call | tf_op jit(solution)/shard_map/pallas_call | solution.py:382
  32.1 3.8 %all-to-all-start.1 = ((bf16[4,1152,128]{2,1,0:T(8,128)(2,1)}), bf16[4,1152,128]{2,1,0:T(8,128)(2,1)S(1)}, u32[]{:S(2)}, u32[]{:S(2)}) async-start(bf16[4,1152,128]{2,1,0:T(8,128)(2,1)} %shard_map.67), calls=%async_computation.1 | async-start | bytes 2359296 | tf_op jit(solution)/shard_map/all_to_all | solution.py:595
  35.9 2.1 %shard_map.68 = (bf16[1024,128]{1,0:T(8,128)(2,1)S(1)}, bf16[1024,128]{1,0:T(8,128)(2,1)S(1)}, bf16[1024,128]{1,0:T(8,128)(2,1)S(1)}, bf16[1024,128]{1,0:T(8,128)(2,1)S(1)}, bf16[4,256,128]{2,1,0:T(8,128)(2,1)S(1)}) custom-call(s32[3]{0:T(128)S(1)} %pad_add_fusion.rank_ref.scalars, bf16[512,128]{1,0:T(8,128)(2,1)S(1)} %copy-done, ...), custom_call_target="tpu_custom_call" | custom-call | tf_op jit(solution)/shard_map/pallas_call | solution.py:320
  38.1 2.1 %collective-permute-start.6 = (bf16[1024,128]{1,0:T(8,128)(2,1)S(1)}, bf16[1024,128]{1,0:T(8,128)(2,1)S(1)}, u32[]{:S(2)}, u32[]{:S(2)}) collective-permute-start(bf16[1024,128]{1,0:T(8,128)(2,1)S(1)} %get-tuple-element.58), channel_id=1, source_target_pairs={{0,2},{2,0},{4,6},{6,4},{8,10},{10,8},{12,14},{14,12},{1,3},{3,1},... | collective-permute-start | bytes 786440 | tf_op jit(solution)/shard_map/ppermute | solution.py:585
  40.1 1.5 %collective-permute-start.8 = (bf16[1024,128]{1,0:T(8,128)(2,1)S(1)}, bf16[1024,128]{1,0:T(8,128)(2,1)S(1)}, u32[]{:S(2)}, u32[]{:S(2)}) collective-permute-start(bf16[1024,128]{1,0:T(8,128)(2,1)S(1)} %get-tuple-element.59), channel_id=1, source_target_pairs={{0,4},{2,6},{4,0},{6,2},{8,12},{10,14},{12,8},{14,10},{1,5},{3,7},... | collective-permute-start | bytes 786440 | tf_op jit(solution)/shard_map/ppermute | solution.py:585
  41.7 2.3 %collective-permute-start.4 = (bf16[4,256,128]{2,1,0:T(8,128)(2,1)S(1)}, bf16[4,256,128]{2,1,0:T(8,128)(2,1)}, u32[]{:S(2)}, u32[]{:S(2)}) collective-permute-start(bf16[4,256,128]{2,1,0:T(8,128)(2,1)S(1)} %get-tuple-element.56), channel_id=1, source_target_pairs={{0,8},{2,10},{4,12},{6,14},{8,0},{10,2},{12,4},{14,6},{1,9},{3,11}... | collective-permute-start | bytes 786440 | tf_op jit(solution)/shard_map/ppermute | solution.py:585
  44.0 10.8 %collective-permute-done.6.refs_1_ = bf16[1024,128]{1,0:T(8,128)(2,1)S(1)} collective-permute-done((bf16[1024,128]{1,0:T(8,128)(2,1)S(1)}, bf16[1024,128]{1,0:T(8,128)(2,1)S(1)}, u32[]{:S(2)}, u32[]{:S(2)}) %collective-permute-start.6) | collective-permute-done | bytes 262176 | tf_op jit(solution)/shard_map/ppermute | solution.py:585
  54.8 8.5 %collective-permute-done.8.refs_2_ = bf16[1024,128]{1,0:T(8,128)(2,1)S(1)} collective-permute-done((bf16[1024,128]{1,0:T(8,128)(2,1)S(1)}, bf16[1024,128]{1,0:T(8,128)(2,1)S(1)}, u32[]{:S(2)}, u32[]{:S(2)}) %collective-permute-start.8) | collective-permute-done | bytes 262176 | tf_op jit(solution)/shard_map/ppermute | solution.py:585
  63.3 3.7 %collective-permute-done.10.refs_3_ = bf16[1024,128]{1,0:T(8,128)(2,1)S(1)} collective-permute-done((bf16[1024,128]{1,0:T(8,128)(2,1)S(1)}, bf16[1024,128]{1,0:T(8,128)(2,1)S(1)}, u32[]{:S(2)}, u32[]{:S(2)}) %collective-permute-start.10) | collective-permute-done | bytes 262176 | tf_op jit(solution)/shard_map/ppermute | solution.py:585
  67.1 1.5 %collective-permute-done.11.refs_7_ = bf16[1024,128]{1,0:T(8,128)(2,1)S(1)} collective-permute-done((bf16[1024,128]{1,0:T(8,128)(2,1)S(1)}, bf16[1024,128]{1,0:T(8,128)(2,1)S(1)}, u32[]{:S(2)}, u32[]{:S(2)}) %collective-permute-start.11) | collective-permute-done | bytes 262176 | tf_op jit(solution)/shard_map/ppermute | solution.py:585
  69.5 1.8 %collective-permute-done.12.other_ref = bf16[4,512,128]{2,1,0:T(8,128)(2,1)S(1)} collective-permute-done((bf16[4,512,128]{2,1,0:T(8,128)(2,1)S(1)}, bf16[4,512,128]{2,1,0:T(8,128)(2,1)S(1)}, u32[]{:S(2)}, u32[]{:S(2)}) %collective-permute-start.12) | collective-permute-done | bytes 524320 | tf_op jit(solution)/shard_map/ppermute | solution.py:585
  71.3 2.7 %shard_map.69 = (bf16[512,1024]{1,0:T(8,128)(2,1)S(1)}, bf16[64,512]{1,0:T(8,128)(2,1)S(1)}) custom-call(s32[3]{0:T(128)S(1)} %pad_add_fusion.rank_ref.scalars, bf16[4,1152,128]{2,1,0:T(8,128)(2,1)S(1)} %all-to-all-done.1.mine_ref, bf16[4,512,128]{2,1,0:T(8,128)(2,1)S(1)} %collective-permute-done.12.other_ref), custom_call_target="tpu_custom_call" | custom-call | flops 30000001024 | bytes 1048576 | tf_op jit(solution)/shard_map/pallas_call | solution.py:443
  74.6 3.4 %all-to-all-start.2 = ((bf16[4,256,128]{2,1,0:T(8,128)(2,1)}), bf16[4,256,128]{2,1,0:T(8,128)(2,1)S(1)}, u32[]{:S(2)}, u32[]{:S(2)}) async-start(bf16[4,256,128]{2,1,0:T(8,128)(2,1)} %collective-permute-done.4), calls=%async_computation.2 | async-start | bytes 524288 | tf_op jit(solution)/shard_map/all_to_all | solution.py:595
  79.5 4.1 %collective-permute-done.13 = bf16[64,512]{1,0:T(8,128)(2,1)} collective-permute-done((bf16[64,512]{1,0:T(8,128)(2,1)}, bf16[64,512]{1,0:T(8,128)(2,1)}, u32[]{:S(2)}, u32[]{:S(2)}) %collective-permute-start.13) | collective-permute-done | bytes 65568 | tf_op jit(solution)/shard_map/ppermute | solution.py:585
  83.6 1.6 %all-to-all-done.2.c = bf16[4,256,128]{2,1,0:T(8,128)(2,1)S(1)} async-done(((bf16[4,256,128]{2,1,0:T(8,128)(2,1)}), bf16[4,256,128]{2,1,0:T(8,128)(2,1)S(1)}, u32[]{:S(2)}, u32[]{:S(2)}) %all-to-all-start.2) | async-done | bytes 262176 | tf_op jit(solution)/shard_map/all_to_all | solution.py:595
  86.6 1.4 %collective-permute-start.17 = (bf16[2,64,512]{2,1,0:T(8,128)(2,1)S(1)}, bf16[2,64,512]{2,1,0:T(8,128)(2,1)S(1)}, u32[]{:S(2)}, u32[]{:S(2)}) collective-permute-start(bf16[2,64,512]{2,1,0:T(8,128)(2,1)S(1)} %get-tuple-element.84), channel_id=1, source_target_pairs={{0,4},{2,6},{4,0},{6,2},{8,12},{10,14},{12,8},{14,10},{1,5},{3,7},... | collective-permute-start | bytes 393224 | tf_op jit(solution)/shard_map/ppermute | solution.py:585
  88.8 1.3 collective-permute-start.18
  90.1 2.3 %collective-permute-done.17 = bf16[2,64,512]{2,1,0:T(8,128)(2,1)S(1)} collective-permute-done((bf16[2,64,512]{2,1,0:T(8,128)(2,1)S(1)}, bf16[2,64,512]{2,1,0:T(8,128)(2,1)S(1)}, u32[]{:S(2)}, u32[]{:S(2)}) %collective-permute-start.17) | collective-permute-done | bytes 131104 | tf_op jit(solution)/shard_map/ppermute | solution.py:585
  92.5 2.8 %collective-permute-done.16 = bf16[2,64,512]{2,1,0:T(8,128)(2,1)S(1)} collective-permute-done((bf16[2,64,512]{2,1,0:T(8,128)(2,1)S(1)}, bf16[2,64,512]{2,1,0:T(8,128)(2,1)S(1)}, u32[]{:S(2)}, u32[]{:S(2)}) %collective-permute-start.16) | collective-permute-done | bytes 131104 | tf_op jit(solution)/shard_map/ppermute | solution.py:585
  96.0 1.7 %collective-permute-done.20.g = bf16[4,256,128]{2,1,0:T(8,128)(2,1)S(1)} collective-permute-done((bf16[4,256,128]{2,1,0:T(8,128)(2,1)S(1)}, bf16[4,256,128]{2,1,0:T(8,128)(2,1)S(1)}, u32[]{:S(2)}, u32[]{:S(2)}) %collective-permute-start.20) | collective-permute-done | bytes 262176 | tf_op jit(solution)/shard_map/ppermute | solution.py:585
  101.9 4.9 %shard_map.70 = (f32[64,512]{1,0:T(8,128)S(1)}, f32[512,512]{1,0:T(8,128)S(1)}, bf16[512,512]{1,0:T(8,128)(2,1)S(1)}) custom-call(s32[3]{0:T(128)S(1)} %pad_add_fusion.rank_ref.scalars, bf16[512,1024]{1,0:T(8,128)(2,1)S(1)} %get-tuple-element.62.tokens, bf16[4,2,64,512]{3,2,1,0:T(8,128)(2,1)S(1)} %pad_maximum_fusion.a, ...), custom_call_target="tpu_custom_call" | custom-call | tf_op jit(solution)/shard_map/pallas_call | solution.py:527
  106.9 1.8 %collective-permute-done.22.got_ref = bf16[512,512]{1,0:T(8,128)(2,1)S(1)} collective-permute-done((bf16[512,512]{1,0:T(8,128)(2,1)S(1)}, bf16[512,512]{1,0:T(8,128)(2,1)S(1)}, u32[]{:S(2)}, u32[]{:S(2)}) %collective-permute-start.22) | collective-permute-done | bytes 524320 | tf_op jit(solution)/shard_map/ppermute | solution.py:585
  109.4 18.4 %all_to_all.26.terms_ref = bf16[8,64,512]{2,1,0:T(8,128)(2,1)S(1)} all-to-all(bf16[8,64,512]{2,1,0:T(8,128)(2,1)S(1)} %bitcast.17), channel_id=1, replica_groups=mesh['groups'=2,'seq'=8,'head'=2] {'seq'}, dimensions={0} | all-to-all | bytes 1048576 | tf_op jit(solution)/shard_map/all_to_all | solution.py:589
  127.8 1.2 shard_map.72
  (71 shorter events, 14.7 us)
Async XLA Ops:
  0.0 11.2 %copy-start = (bf16[512,128]{1,0:T(8,128)(2,1)S(1)}, bf16[512,128]{1,0:T(8,128)(2,1)}, u32[]{:S(2)}) copy-start(bf16[512,128]{1,0:T(8,128)(2,1)} %out_weight_ref.2) | copy-start | bytes 393220
  0.0 11.2 %copy-start.3 = (bf16[128,8,192]{0,2,1:T(8,128)(2,1)S(1)}, bf16[128,8,192]{0,2,1:T(8,128)(2,1)}, u32[]{:S(2)}) copy-start(bf16[128,8,192]{0,2,1:T(8,128)(2,1)} %param.8) | copy-start | bytes 1179652
  3.9 19.8 %all-to-all-start = ((bf16[8,80,128]{2,1,0:T(8,128)(2,1)}), bf16[8,80,128]{2,1,0:T(8,128)(2,1)S(1)}, u32[]{:S(2)}, u32[]{:S(2)}) async-start(bf16[8,80,128]{2,1,0:T(8,128)(2,1)} %bitcast.4), calls=%async_computation | async-start | bytes 327680 | tf_op jit(solution)/shard_map/all_to_all | solution.py:589
  12.3 10.0 %collective-permute-start.2 = (bf16[384,128]{1,0:T(8,128)(2,1)S(1)}, bf16[384,128]{1,0:T(8,128)(2,1)S(1)}, u32[]{:S(2)}, u32[]{:S(2)}) collective-permute-start(bf16[384,128]{1,0:T(8,128)(2,1)S(1)} %get-tuple-element.47), channel_id=1, source_target_pairs={{0,8},{2,10},{4,12},{6,14},{8,0},{10,2},{12,4},{14,6},{1,9},{3,11}... | collective-permute-start | bytes 294920 | tf_op jit(solution)/shard_map/ppermute | solution.py:585
  22.3 7.4 %collective-permute-start.3 = (bf16[384,128]{1,0:T(8,128)(2,1)S(1)}, bf16[384,128]{1,0:T(8,128)(2,1)S(1)}, u32[]{:S(2)}, u32[]{:S(2)}) collective-permute-start(bf16[384,128]{1,0:T(8,128)(2,1)S(1)} %collective-permute-done.2.mine_ref), channel_id=1, source_target_pairs={{0,16},{16,0},{1,17},{17,1},{2,18},{18,2},{3,19},{19,3},{4,20},{20... | collective-permute-start | bytes 294920 | tf_op jit(solution)/shard_map/ppermute | solution.py:585
  23.8 5.9 %collective-permute-start.1 = (bf16[256,128]{1,0:T(8,128)(2,1)S(1)}, bf16[256,128]{1,0:T(8,128)(2,1)S(1)}, u32[]{:S(2)}, u32[]{:S(2)}) collective-permute-start(bf16[256,128]{1,0:T(8,128)(2,1)S(1)} %get-tuple-element.45), channel_id=1, source_target_pairs={{0,8},{2,10},{4,12},{6,14},{8,0},{10,2},{12,4},{14,6},{1,9},{3,11}... | collective-permute-start | bytes 196616 | tf_op jit(solution)/shard_map/ppermute | solution.py:585
  24.7 5.6 %collective-permute-start = (bf16[256,128]{1,0:T(8,128)(2,1)S(1)}, bf16[256,128]{1,0:T(8,128)(2,1)S(1)}, u32[]{:S(2)}, u32[]{:S(2)}) collective-permute-start(bf16[256,128]{1,0:T(8,128)(2,1)S(1)} %shard_map.65.owned_ref), channel_id=1, source_target_pairs={{0,8},{2,10},{4,12},{6,14},{8,0},{10,2},{12,4},{14,6},{1,9},{3,11}... | collective-permute-start | bytes 196616 | tf_op jit(solution)/shard_map/ppermute | solution.py:585
  32.1 37.1 %all-to-all-start.1 = ((bf16[4,1152,128]{2,1,0:T(8,128)(2,1)}), bf16[4,1152,128]{2,1,0:T(8,128)(2,1)S(1)}, u32[]{:S(2)}, u32[]{:S(2)}) async-start(bf16[4,1152,128]{2,1,0:T(8,128)(2,1)} %shard_map.67), calls=%async_computation.1 | async-start | bytes 2359296 | tf_op jit(solution)/shard_map/all_to_all | solution.py:595
  38.1 16.7 %collective-permute-start.6 = (bf16[1024,128]{1,0:T(8,128)(2,1)S(1)}, bf16[1024,128]{1,0:T(8,128)(2,1)S(1)}, u32[]{:S(2)}, u32[]{:S(2)}) collective-permute-start(bf16[1024,128]{1,0:T(8,128)(2,1)S(1)} %get-tuple-element.58), channel_id=1, source_target_pairs={{0,2},{2,0},{4,6},{6,4},{8,10},{10,8},{12,14},{14,12},{1,3},{3,1},... | collective-permute-start | bytes 786440 | tf_op jit(solution)/shard_map/ppermute | solution.py:585
  40.1 23.1 %collective-permute-start.8 = (bf16[1024,128]{1,0:T(8,128)(2,1)S(1)}, bf16[1024,128]{1,0:T(8,128)(2,1)S(1)}, u32[]{:S(2)}, u32[]{:S(2)}) collective-permute-start(bf16[1024,128]{1,0:T(8,128)(2,1)S(1)} %get-tuple-element.59), channel_id=1, source_target_pairs={{0,4},{2,6},{4,0},{6,2},{8,12},{10,14},{12,8},{14,10},{1,5},{3,7},... | collective-permute-start | bytes 786440 | tf_op jit(solution)/shard_map/ppermute | solution.py:585
  41.6 25.4 %collective-permute-start.10 = (bf16[1024,128]{1,0:T(8,128)(2,1)S(1)}, bf16[1024,128]{1,0:T(8,128)(2,1)S(1)}, u32[]{:S(2)}, u32[]{:S(2)}) collective-permute-start(bf16[1024,128]{1,0:T(8,128)(2,1)S(1)} %get-tuple-element.60), channel_id=1, source_target_pairs={{0,6},{2,4},{4,2},{6,0},{8,14},{10,12},{12,10},{14,8},{1,7},{3,5},... | collective-permute-start | bytes 786440 | tf_op jit(solution)/shard_map/ppermute | solution.py:585
  41.7 25.3 %collective-permute-start.5 = (bf16[1024,128]{1,0:T(8,128)(2,1)S(1)}, bf16[1024,128]{1,0:T(8,128)(2,1)S(1)}, u32[]{:S(2)}, u32[]{:S(2)}) collective-permute-start(bf16[1024,128]{1,0:T(8,128)(2,1)S(1)} %get-tuple-element.57.refs_0_), channel_id=1, source_target_pairs={{0,1},{1,0},{2,3},{3,2},{4,5},{5,4},{6,7},{7,6},{8,9},{9,8},{10,11... | collective-permute-start | bytes 786440 | tf_op jit(solution)/shard_map/ppermute | solution.py:585
  41.7 25.3 %collective-permute-start.4 = (bf16[4,256,128]{2,1,0:T(8,128)(2,1)S(1)}, bf16[4,256,128]{2,1,0:T(8,128)(2,1)}, u32[]{:S(2)}, u32[]{:S(2)}) collective-permute-start(bf16[4,256,128]{2,1,0:T(8,128)(2,1)S(1)} %get-tuple-element.56), channel_id=1, source_target_pairs={{0,8},{2,10},{4,12},{6,14},{8,0},{10,2},{12,4},{14,6},{1,9},{3,11}... | collective-permute-start | bytes 786440 | tf_op jit(solution)/shard_map/ppermute | solution.py:585
  54.8 12.2 %collective-permute-start.7 = (bf16[1024,128]{1,0:T(8,128)(2,1)S(1)}, bf16[1024,128]{1,0:T(8,128)(2,1)S(1)}, u32[]{:S(2)}, u32[]{:S(2)}) collective-permute-start(bf16[1024,128]{1,0:T(8,128)(2,1)S(1)} %collective-permute-done.6.refs_1_), channel_id=1, source_target_pairs={{0,1},{1,0},{2,3},{3,2},{4,5},{5,4},{6,7},{7,6},{8,9},{9,8},{10,11... | collective-permute-start | bytes 786440 | tf_op jit(solution)/shard_map/ppermute | solution.py:585
  63.3 3.8 %collective-permute-start.9 = (bf16[1024,128]{1,0:T(8,128)(2,1)S(1)}, bf16[1024,128]{1,0:T(8,128)(2,1)S(1)}, u32[]{:S(2)}, u32[]{:S(2)}) collective-permute-start(bf16[1024,128]{1,0:T(8,128)(2,1)S(1)} %collective-permute-done.8.refs_2_), channel_id=1, source_target_pairs={{0,1},{1,0},{2,3},{3,2},{4,5},{5,4},{6,7},{7,6},{8,9},{9,8},{10,11... | collective-permute-start | bytes 786440 | tf_op jit(solution)/shard_map/ppermute | solution.py:585
  67.0 7.0 %copy-start.4 = (bf16[1024,128]{1,0:T(8,128)(2,1)}, bf16[1024,128]{1,0:T(8,128)(2,1)S(1)}, u32[]{:S(2)}) copy-start(bf16[1024,128]{1,0:T(8,128)(2,1)S(1)} %collective-permute-done.10.refs_3_) | copy-start | bytes 786436
  67.0 1.5 %collective-permute-start.11 = (bf16[1024,128]{1,0:T(8,128)(2,1)S(1)}, bf16[1024,128]{1,0:T(8,128)(2,1)S(1)}, u32[]{:S(2)}, u32[]{:S(2)}) collective-permute-start(bf16[1024,128]{1,0:T(8,128)(2,1)S(1)} %collective-permute-done.10.refs_3_), channel_id=1, source_target_pairs={{0,1},{1,0},{2,3},{3,2},{4,5},{5,4},{6,7},{7,6},{8,9},{9,8},{10,11... | collective-permute-start | bytes 786440 | tf_op jit(solution)/shard_map/ppermute | solution.py:585
  69.3 2.0 %collective-permute-start.12 = (bf16[4,512,128]{2,1,0:T(8,128)(2,1)S(1)}, bf16[4,512,128]{2,1,0:T(8,128)(2,1)S(1)}, u32[]{:S(2)}, u32[]{:S(2)}) collective-permute-start(bf16[4,512,128]{2,1,0:T(8,128)(2,1)S(1)} %slice.6), channel_id=1, source_target_pairs={{0,1},{1,0},{2,3},{3,2},{4,5},{5,4},{6,7},{7,6},{8,9},{9,8},{10,11... | collective-permute-start | bytes 1572872 | tf_op jit(solution)/shard_map/ppermute | solution.py:585
  74.6 10.5 %all-to-all-start.2 = ((bf16[4,256,128]{2,1,0:T(8,128)(2,1)}), bf16[4,256,128]{2,1,0:T(8,128)(2,1)S(1)}, u32[]{:S(2)}, u32[]{:S(2)}) async-start(bf16[4,256,128]{2,1,0:T(8,128)(2,1)} %collective-permute-done.4), calls=%async_computation.2 | async-start | bytes 524288 | tf_op jit(solution)/shard_map/all_to_all | solution.py:595
  78.0 5.5 %collective-permute-start.13 = (bf16[64,512]{1,0:T(8,128)(2,1)}, bf16[64,512]{1,0:T(8,128)(2,1)}, u32[]{:S(2)}, u32[]{:S(2)}) collective-permute-start(bf16[64,512]{1,0:T(8,128)(2,1)} %copy-done.16), channel_id=1, source_target_pairs={{0,8},{2,10},{4,12},{6,14},{8,0},{10,2},{12,4},{14,6},{1,9},{3,11}... | collective-permute-start | bytes 196616 | tf_op jit(solution)/shard_map/ppermute | solution.py:585
  78.8 19.2 %copy-start.5 = (bf16[1024,128]{1,0:T(8,128)(2,1)S(1)}, bf16[1024,128]{1,0:T(8,128)(2,1)}, u32[]{:S(2)}) copy-start(bf16[1024,128]{1,0:T(8,128)(2,1)} %copy-done.4) | copy-start | bytes 786436
  78.9 19.2 %copy-start.7 = (bf16[1024,128]{1,0:T(8,128)(2,1)S(1)}, bf16[1024,128]{1,0:T(8,128)(2,1)}, u32[]{:S(2)}) copy-start(bf16[1024,128]{1,0:T(8,128)(2,1)} %copy-done.6) | copy-start | bytes 786436
  78.9 11.3 %collective-permute-start.15 = (bf16[4,256,128]{2,1,0:T(8,128)(2,1)S(1)}, bf16[4,256,128]{2,1,0:T(8,128)(2,1)S(1)}, u32[]{:S(2)}, u32[]{:S(2)}) collective-permute-start(bf16[4,256,128]{2,1,0:T(8,128)(2,1)S(1)} %slice.7.e), channel_id=1, source_target_pairs={{0,16},{16,0},{1,17},{17,1},{2,18},{18,2},{3,19},{19,3},{4,20},{20... | collective-permute-start | bytes 786440 | tf_op jit(solution)/shard_map/ppermute | solution.py:585
  85.1 10.1 %collective-permute-start.14 = (bf16[4,256,128]{2,1,0:T(8,128)(2,1)S(1)}, bf16[4,256,128]{2,1,0:T(8,128)(2,1)S(1)}, u32[]{:S(2)}, u32[]{:S(2)}) collective-permute-start(bf16[4,256,128]{2,1,0:T(8,128)(2,1)S(1)} %all-to-all-done.2.c), channel_id=1, source_target_pairs={{0,16},{16,0},{1,17},{17,1},{2,18},{18,2},{3,19},{19,3},{4,20},{20... | collective-permute-start | bytes 786440 | tf_op jit(solution)/shard_map/ppermute | solution.py:585
  86.6 5.9 %collective-permute-start.17 = (bf16[2,64,512]{2,1,0:T(8,128)(2,1)S(1)}, bf16[2,64,512]{2,1,0:T(8,128)(2,1)S(1)}, u32[]{:S(2)}, u32[]{:S(2)}) collective-permute-start(bf16[2,64,512]{2,1,0:T(8,128)(2,1)S(1)} %get-tuple-element.84), channel_id=1, source_target_pairs={{0,4},{2,6},{4,0},{6,2},{8,12},{10,14},{12,8},{14,10},{1,5},{3,7},... | collective-permute-start | bytes 393224 | tf_op jit(solution)/shard_map/ppermute | solution.py:585
  87.9 7.3 %collective-permute-start.16 = (bf16[2,64,512]{2,1,0:T(8,128)(2,1)S(1)}, bf16[2,64,512]{2,1,0:T(8,128)(2,1)S(1)}, u32[]{:S(2)}, u32[]{:S(2)}) collective-permute-start(bf16[2,64,512]{2,1,0:T(8,128)(2,1)S(1)} %get-tuple-element.84), channel_id=1, source_target_pairs={{0,2},{2,0},{4,6},{6,4},{8,10},{10,8},{12,14},{14,12},{1,3},{3,1},... | collective-permute-start | bytes 393224 | tf_op jit(solution)/shard_map/ppermute | solution.py:585
  88.8 6.4 %collective-permute-start.18 = (bf16[2,64,512]{2,1,0:T(8,128)(2,1)S(1)}, bf16[2,64,512]{2,1,0:T(8,128)(2,1)S(1)}, u32[]{:S(2)}, u32[]{:S(2)}) collective-permute-start(bf16[2,64,512]{2,1,0:T(8,128)(2,1)S(1)} %get-tuple-element.84), channel_id=1, source_target_pairs={{0,6},{2,4},{4,2},{6,0},{8,14},{10,12},{12,10},{14,8},{1,7},{3,5},... | collective-permute-start | bytes 393224 | tf_op jit(solution)/shard_map/ppermute | solution.py:585
  90.1 7.9 %copy-start.14 = (bf16[4,256,128]{2,1,0:T(8,128)(2,1)}, bf16[4,256,128]{2,1,0:T(8,128)(2,1)S(1)}, u32[]{:S(2)}) copy-start(bf16[4,256,128]{2,1,0:T(8,128)(2,1)S(1)} %collective-permute-done.15.f) | copy-start | bytes 786436
  95.3 2.7 %collective-permute-start.19 = (bf16[4,2,64,512]{3,2,1,0:T(8,128)(2,1)S(1)}, bf16[4,2,64,512]{3,2,1,0:T(8,128)(2,1)S(1)}, u32[]{:S(2)}, u32[]{:S(2)}) collective-permute-start(bf16[4,2,64,512]{3,2,1,0:T(8,128)(2,1)S(1)} %pad_maximum_fusion.a), channel_id=1, source_target_pairs={{0,1},{1,0},{2,3},{3,2},{4,5},{5,4},{6,7},{7,6},{8,9},{9,8},{10,11... | collective-permute-start | bytes 1572872 | tf_op jit(solution)/shard_map/ppermute | solution.py:585
  95.4 2.3 %collective-permute-start.20 = (bf16[4,256,128]{2,1,0:T(8,128)(2,1)S(1)}, bf16[4,256,128]{2,1,0:T(8,128)(2,1)S(1)}, u32[]{:S(2)}, u32[]{:S(2)}) collective-permute-start(bf16[4,256,128]{2,1,0:T(8,128)(2,1)S(1)} %slice.7.e), channel_id=1, source_target_pairs={{0,1},{1,0},{2,3},{3,2},{4,5},{5,4},{6,7},{7,6},{8,9},{9,8},{10,11... | collective-permute-start | bytes 786440 | tf_op jit(solution)/shard_map/ppermute | solution.py:585
  95.9 2.1 %collective-permute-start.21 = (bf16[4,256,128]{2,1,0:T(8,128)(2,1)S(1)}, bf16[4,256,128]{2,1,0:T(8,128)(2,1)S(1)}, u32[]{:S(2)}, u32[]{:S(2)}) collective-permute-start(bf16[4,256,128]{2,1,0:T(8,128)(2,1)S(1)} %collective-permute-done.15.f), channel_id=1, source_target_pairs={{0,1},{1,0},{2,3},{3,2},{4,5},{5,4},{6,7},{7,6},{8,9},{9,8},{10,11... | collective-permute-start | bytes 786440 | tf_op jit(solution)/shard_map/ppermute | solution.py:585
  106.7 2.0 %collective-permute-start.22 = (bf16[512,512]{1,0:T(8,128)(2,1)S(1)}, bf16[512,512]{1,0:T(8,128)(2,1)S(1)}, u32[]{:S(2)}, u32[]{:S(2)}) collective-permute-start(bf16[512,512]{1,0:T(8,128)(2,1)S(1)} %get-tuple-element.79), channel_id=1, source_target_pairs={{0,1},{1,0},{2,3},{3,2},{4,5},{5,4},{6,7},{7,6},{8,9},{9,8},{10,11... | collective-permute-start | bytes 1572872 | tf_op jit(solution)/shard_map/ppermute | solution.py:585
  (11 other events, 24.7 us)

commit v9 on v8

--- a/solution.py
+++ b/solution.py
@@ -289,15 +289,28 @@
     )(scalars, keep_col, got)
 
 
-def pack_kernel(n, rank_ref, out_weight_ref, up_ref, down_ref, *refs):
-    near, away_ref, sem = refs[: n // 2], refs[n // 2], refs[n // 2 + 1]
+def pack_kernel(n, rank_ref, qkv_ref, out_weight_ref, up_ref, down_ref, *refs):
+    near, (heads_ref, away_ref, sem) = refs[: n // 2], refs[n // 2 :]
     rank, part = rank_ref[0], rank_ref[2]
     half = n // 2
     rows = up_ref.shape[0]
     wide = up_ref.shape[1] // n
     units = wide // 2
     long = out_weight_ref.shape[0]
+    depth = qkv_ref.shape[1] // 2
+    each = depth + rows + units
     copies = []
+    for d in range(half):
+        dest = (rank // half ^ 1) * half + d
+        low = d * each
+        at = pl.ds(pl.multiple_of(part * depth, 32), depth)
+        copies.append((qkv_ref.at[dest, at], away_ref.at[pl.ds(low, depth)]))
+        at = pl.ds(pl.multiple_of(dest * wide + part * units, 128), units)
+        copies.append((up_ref.at[:, at], away_ref.at[pl.ds(low + depth, rows)]))
+        copies.append((down_ref.at[at], away_ref.at[pl.ds(low + depth + rows, units)]))
+    at = pl.ds(pl.multiple_of(part * (long // 2), 128), long // 2)
+    copies.append((out_weight_ref.at[at], away_ref.at[pl.ds(half * each, long // 2)]))
+    copies.append((qkv_ref.at[pl.ds(rank // half * half, half)], heads_ref))
     for j in range(half):
         dest = rank ^ j
         for c in range(2):
@@ -306,86 +319,51 @@
         at = pl.ds(pl.multiple_of(dest * wide, 128), wide)
         copies.append((down_ref.at[at], near[j].at[pl.ds(2 * rows, wide)]))
         copies.append((out_weight_ref, near[j].at[pl.ds(2 * rows + wide, long)]))
-        dest = (rank // half ^ 1) * half + j
-        at = pl.ds(pl.multiple_of(dest * wide + part * units, 128), units)
-        copies.append((up_ref.at[:, at], away_ref.at[j, pl.ds(0, rows)]))
-        copies.append((down_ref.at[at], away_ref.at[j, pl.ds(rows, units)]))
     run_copies(copies, sem)()
 
 
-def pack(scalars, out_weight, up, down, n):
+def pack(scalars, qkv, out_weight, up, down, n):
+    half = n // 2
     wide = up.shape[1] // n
     near = struct((2 * up.shape[0] + wide + out_weight.shape[0], 128))
-    away = struct((n // 2, up.shape[0] + wide // 2, 128))
+    each = qkv.shape[1] // 2 + up.shape[0] + wide // 2
+    away = struct((half * each + out_weight.shape[0] // 2, 128))
     outs = pl.pallas_call(
         functools.partial(pack_kernel, n),
-        in_specs=[sspec()] + [hspec()] * 3,
-        out_specs=[aspec()] * (n // 2 + 1),
-        out_shape=[near] * (n // 2) + [away],
-        scratch_shapes=[pltpu.SemaphoreType.DMA((6 * n // 2,))],
+        in_specs=[sspec()] + [hspec()] * 4,
+        out_specs=[aspec()] * (half + 2),
+        out_shape=[near] * half + [struct((half,) + qkv.shape[1:]), away],
+        scratch_shapes=[pltpu.SemaphoreType.DMA((7 * half + 2,))],
         compiler_params=params(),
-    )(scalars, out_weight, up, down)
-    return list(outs[:-1]), outs[-1]
-
-
-def early_kernel(n, rank_ref, qkv_ref, out_weight_ref, heads_ref, near_ref, rows_ref, sem):
-    rank, part = rank_ref[0], rank_ref[2]
-    half = n // 2
-    depth = heads_ref.shape[0] // half
-    long = rows_ref.shape[0]
-    copies = []
-    for d in range(half):
-        dest = (rank // half ^ 1) * half + d
-        at = pl.ds(pl.multiple_of(part * depth, 32), depth)
-        copies.append((qkv_ref.at[dest, at], heads_ref.at[pl.ds(d * depth, depth)]))
-    copies.append((qkv_ref.at[pl.ds(rank // half * half, half)], near_ref))
-    at = pl.ds(pl.multiple_of(part * long, 128), long)
-    copies.append((out_weight_ref.at[at], rows_ref))
-    run_copies(copies, sem)()
-
-
-def early_blocks(scalars, qkv, out_weight, n):
-    return pl.pallas_call(
-        functools.partial(early_kernel, n),
-        in_specs=[sspec()] + [hspec()] * 2,
-        out_specs=[aspec()] * 3,
-        out_shape=[
-            struct((n // 2 * qkv.shape[1] // 2, 128)),
-            struct((n // 2,) + qkv.shape[1:]),
-            struct((out_weight.shape[0] // 2, 128)),
-        ],
-        scratch_shapes=[pltpu.SemaphoreType.DMA((n // 2 + 2,))],
-        compiler_params=params(),
-    )(scalars, qkv, out_weight)
-
-
-def fan_kernel(rank_ref, owned_ref, across_ref, mine_ref, other_ref, near_ref, rows_ref, out_ref):
-    part = rank_ref[2]
+    )(scalars, qkv, out_weight, up, down)
+    return list(outs[:half]), outs[half], outs[half + 1]
+
+
+def fan_kernel(owned_ref, across_ref, heads_ref, far_ref, out_ref):
     rows = owned_ref.shape[0]
-    count, head_rows = near_ref.shape[:2]
-    depth = head_rows // 2
-    top = 2 * rows
+    count, head_rows = heads_ref.shape[:2]
+    top = 2 * rows + head_rows
+    rest = out_ref.shape[1] - top
+    each = (far_ref.shape[0] - rest) // (count - 1)
     for d in range(count):
         out_ref[d, :rows] = owned_ref[...]
-        out_ref[d, rows:top] = across_ref[...]
-        out_ref[d, top : top + head_rows] = near_ref[d]
-        at = pl.ds(pl.multiple_of(top + head_rows + part * depth, 32), depth)
-        out_ref[d, at] = mine_ref[d * depth : (d + 1) * depth]
-        at = pl.ds(pl.multiple_of(top + head_rows + (1 - part) * depth, 32), depth)
-        out_ref[d, at] = other_ref[d * depth : (d + 1) * depth]
-        out_ref[d, top + 2 * head_rows :] = rows_ref[...]
-
-
-def fan(scalars, owned, across, mine, other, near, rows):
-    count = near.shape[0]
-    shape = struct((count, 2 * owned.shape[0] + 2 * near.shape[1] + rows.shape[0], 128))
+        out_ref[d, rows : 2 * rows] = across_ref[...]
+        out_ref[d, 2 * rows : top] = heads_ref[d]
+        out_ref[d, top : top + each] = far_ref[d * each : (d + 1) * each]
+        out_ref[d, top + each :] = far_ref[count * each :]
+
+
+def fan(owned, across, heads, far, out_rows):
+    count = heads.shape[0]
+    each = (far.shape[0] - out_rows) // count
+    shape = struct((count, 2 * owned.shape[0] + heads.shape[1] + each + out_rows, 128))
     return pl.pallas_call(
         fan_kernel,
-        in_specs=[sspec()] + [vspec()] * 6,
+        in_specs=[vspec()] * 4,
         out_specs=vspec(),
         out_shape=shape,
-        compiler_params=params(),
-    )(scalars, owned, across, mine, other, near, rows)
+        compiler_params=params(8),
+    )(owned, across, heads, far)
 
 
 def source_of(rank, n, q, k):
@@ -398,12 +376,13 @@
     return (x - average) * lax.rsqrt(power - average * average + 1e-06)
 
 
-def attend_kernel(n, part, rank_ref, mine_ref, other_ref, tokens_ref, out_ref, weight_ref):
-    rank, half = rank_ref[0], rank_ref[1]
+def attend_kernel(n, part, rank_ref, mine_ref, other_ref, far_ref, tokens_ref, out_ref, weight_ref):
+    rank, half, group = rank_ref[0], rank_ref[1], rank_ref[2]
     rows = other_ref.shape[1] // 2
     cuts = rows // part
     width = cuts * 128
     depth = weight_ref.shape[0]
+    piece = far_ref.shape[1]
     for q in range(n // 2):
         for k in range(2):
             source = source_of(rank, n, q, k)
@@ -414,9 +393,13 @@
                 tokens_ref[at, to] = mine_ref[q, cut]
                 to = pl.ds(pl.multiple_of((1 - half) * width + c * 128, 128), 128)
                 tokens_ref[at, to] = other_ref[q, cut]
-            to = pl.ds(pl.multiple_of(source * 128, 128), 128)
-            high = 2 * rows + k * depth
-            weight_ref[:, to] = mine_ref[q, high : high + depth]
+        to = pl.ds(pl.multiple_of(source_of(rank, n, q, 0) * 128, 128), 128)
+        weight_ref[:, to] = mine_ref[q, 2 * rows : 2 * rows + depth]
+        to = pl.ds(pl.multiple_of(source_of(rank, n, q, 1) * 128, 128), 128)
+        at = pl.ds(pl.multiple_of(group * piece, 32), piece)
+        weight_ref[at, to] = mine_ref[q, 2 * rows + depth : 2 * rows + depth + piece]
+        at = pl.ds(pl.multiple_of((1 - group) * piece, 32), piece)
+        weight_ref[at, to] = far_ref[q]
     normed = norm_rows(tokens_ref[...].astype(F32)).astype(BF16)
     projected = lax.dot_general(
         normed, weight_ref[...], (((1,), (1,)), ((), ())), preferred_element_type=F32
@@ -436,19 +419,19 @@
     out_ref[...] = attended
 
 
-def attend_fast(scalars, mine, other, head_rows, per_owner, n):
+def attend_fast(scalars, mine, other, far, head_rows, per_owner, n):
     length = n * per_owner
     depth = other.shape[1] // (2 * per_owner) * 256
     size = head_rows // 3
     return pl.pallas_call(
         functools.partial(attend_kernel, n, per_owner),
-        in_specs=[sspec()] + [vspec()] * 2,
+        in_specs=[sspec()] + [vspec()] * 3,
         out_specs=[vspec()] * 2,
         out_shape=[struct((length, depth)), struct((size, length))],
         scratch_shapes=[VMEM((head_rows, n * 128), BF16)],
         compiler_params=params(12),
         cost_estimate=cost(30),
-    )(scalars, mine, other)
+    )(scalars, mine, other, far)
 
 
 def mlp_kernel(n, rank_ref, tokens_ref, pieces, far, outs_far, near, outs_near, outs, scratch):
@@ -618,36 +601,36 @@
     flat = patches.reshape(4 * sup, depth)
     heads = qkv_weight.transpose(1, 2, 0)
 
-    slots = prep(scalars, keep_col, flat, n, sup, capacity)
-    qkv_away, qkv_near, out_away = early_blocks(scalars, heads, out_weight, n)
+    near, qkv_near, away = pack(scalars, heads, out_weight, up_weight, down_weight, n)
+    far = swap(away, "seq", half)
+    slots = prep(scalars, keep_col, after(flat, away), n, sup, capacity)
     dealt = exchange(slots)
-    qkv_mine = swap(after(qkv_away, slots), "seq", half)
-    out_far = swap(after(out_away, slots), "seq", half)
-    qkv_other = swap(qkv_mine, "groups", 1)
-    blocks = lax.optimization_barrier((out_weight, up_weight, down_weight, qkv_mine))[:3]
-    near, mlp_away = pack(scalars, *blocks, n)
+    near = lax.optimization_barrier((*near, slots))[:half]
     near = [near[0]] + [swap(near[j], "seq", j) for j in range(1, half)]
     owned = pick(scalars, keep_col, dealt, n, sup, per_owner, capacity)
-
     across = swap(owned, "seq", half)
-    across, out_far, qkv_other = lax.optimization_barrier((across, out_far, qkv_other))
-    mlp_far = swap(after(mlp_away, across), "seq", half)
-    got = exchange_half(fan(scalars, owned, across, qkv_mine, qkv_other, qkv_near, out_far))
+    across, far, *near = lax.optimization_barrier((across, far, *near))
+
+    out_rows = out_weight.shape[0] // 2
+    got = exchange_half(fan(owned, across, qkv_near, far, out_rows))
     near_other = [swap(block, "head", 1) for block in near]
-    got, mlp_far, *near_other = lax.optimization_barrier((got, mlp_far, *near_other))
+    got, *near_other = lax.optimization_barrier((got, *near_other))
 
     top = 2 * owned.shape[0]
     pieces_other = swap(got[:, :top], "head", 1)
-    tokens, attended = attend_fast(scalars, got, pieces_other, head_rows, per_owner, n)
+    top = top + head_rows
+    qkv_far = swap(got[:, top : top + head_rows // 2], "groups", 1)
+    tokens, attended = attend_fast(
+        scalars, got, pieces_other, qkv_far, head_rows, per_owner, n
+    )
 
     att_across = swap(attended, "seq", half)
-    mlp_far, got = lax.optimization_barrier((mlp_far, got, attended))[:2]
-    mlp_mine = exchange_half(mlp_far)
-    far_mine = got[:, top + 2 * head_rows :]
+    got = after(got, attended)
+    mlp_mine = got[:, top + head_rows // 2 : got.shape[1] - out_rows]
+    far_mine = got[:, got.shape[1] - out_rows :]
     far_other = swap(far_mine, "groups", 1)
-    att_across, mlp_mine = lax.optimization_barrier((att_across, mlp_mine))
+    mlp_other = swap(mlp_mine, "groups", 1)
     pair = jnp.stack([attended, att_across])
-    mlp_other = swap(mlp_mine, "groups", 1)
     pairs = [swap(pair, "seq", j) for j in range(1, half)]
     mlp_other, far_other, *pairs = lax.optimization_barrier((mlp_other, far_other, *pairs))
     gathered = jnp.stack([pair] + pairs)

time: 130 us -> 118 us (0.908)
  starting transfers between devices: 34.5 us -> 30.9 us
  local copies, waits for them, and re-layouts: 7.08 us -> 4.24 us
  waiting for transfers between devices: 50.5 us -> 48.3 us
    ppermute x23 -> x21, waiting for transfers between devices: 48.9 us -> 21.8 us  [swap(): return lax.ppermute(value, axis, [(i, i ^ j) for i in range(n)])]
    all_to_all x1, waiting for transfers between devices: 0.01 us -> 13.4 us  [exchange(): return lax.all_to_all(value, 'seq', split_axis=0, concat_axis=0, tiled=True)]
    all_to_all x2 -> x1, waiting for transfers between devices: 1.58 us -> 13 us  [exchange_half(): lax.all_to_all(value, 'seq', split_axis=0, concat_axis=0, axis_index_grou...]
    all_to_all x2 -> x1, starting transfers between devices: 7.23 us -> 3.54 us  [exchange_half(): lax.all_to_all(value, 'seq', split_axis=0, concat_axis=0, axis_index_grou...]
    ppermute x23 -> x21, starting transfers between devices: 20 us -> 23.5 us  [swap(): return lax.ppermute(value, axis, [(i, i ^ j) for i in range(n)])]
    all_to_all x1, starting transfers between devices: 7.28 us -> 3.81 us  [exchange(): return lax.all_to_all(value, 'seq', split_axis=0, concat_axis=0, tiled=True)]
    pallas_call x2 -> x1, Pallas kernels: 2.82 us -> 1.22 us  [fan(): pl.pallas_call(fan_kernel, in_specs=[vspec()] * 4, out_specs=vspec(), out...]
    unnamed x34 -> x12, local copies, waits for them, and re-layouts: 5.18 us -> 3.99 us
  transfers between devices with their start and end apart: 26 -> 23, of which waited for: 15 -> 15; matrix products, arithmetic and copies ran while one was open for 1% -> 0% of each run, Pallas kernels for 3% -> 2%
where the time goes in v9:
time: 118 us
  waiting for transfers between devices  48.3 us (41%)
  starting transfers between devices  30.9 us (26%)
  blocking collectives  17.5 us (15%)
  Pallas kernels  16.5 us (14%)
  local copies, waits for them, and re-layouts  4.24 us (4%)
    ppermute x21, starting transfers between devices, swap(): return lax.ppermute(value, axis, [(i, i ^ j) for i in range(n)])  23.5 us
    ppermute x21, waiting for transfers between devices, swap(): return lax.ppermute(value, axis, [(i, i ^ j) for i in range(n)])  21.8 us
    all_to_all x1, blocking collectives, exchange(): return lax.all_to_all(value, 'seq', split_axis=0, concat_axis=0, tiled=True)  17.5 us
    all_to_all x1, waiting for transfers between devices, exchange(): return lax.all_to_all(value, 'seq', split_axis=0, concat_axis=0, tiled=True)  13.4 us
    all_to_all x1, waiting for transfers between devices, exchange_half(): lax.all_to_all(value, 'seq', split_axis=0, concat_axis=0, axis_index_grou...  13 us
    pallas_call x1, Pallas kernels, mlp(): pl.pallas_call(kernel, in_specs=[sspec()] + [vspec()] * 3 + [aspec()] * (...  4.86 us
    unnamed x12, local copies, waits for them, and re-layouts  3.99 us
    all_to_all x1, starting transfers between devices, exchange(): return lax.all_to_all(value, 'seq', split_axis=0, concat_axis=0, tiled=True)  3.81 us
  transfers between devices with their start and end apart: 23, of which 15 were waited for; matrix products, arithmetic and copies ran while one was open for 0% of the time, Pallas kernels for 2%

profile of v9, /device:TPU:0, one launch (start us, length us, event | category | flops | bytes accessed | tf_op | source)
XLA Modules:
  0.0 117.6 jit_solution(18219946455040871389)
XLA Ops:
  0.1 1.0 copy-done
  1.1 1.0 copy-done.1
  2.2 1.0 copy-done.2
  3.2 0.9 copy-done.3
  4.1 2.9 %shard_map.64 = (bf16[1024,128]{1,0:T(8,128)(2,1)S(1)}, bf16[1024,128]{1,0:T(8,128)(2,1)S(1)}, bf16[1024,128]{1,0:T(8,128)(2,1)S(1)}, bf16[1024,128]{1,0:T(8,128...) custom-call(s32[3]{0:T(128)S(1)} %pad_add_fusion.rank_ref.scalars, ...), custom_call_target="tpu_custom_call" | custom-call | tf_op jit(solution)/shard_map/pallas_call | solution.py:331
  6.9 4.1 %collective-permute-start.1 = (bf16[1664,128]{1,0:T(8,128)(2,1)S(1)}, bf16[1664,128]{1,0:T(8,128)(2,1)S(1)}, u32[]{:S(2)}, u32[]{:S(2)}) collective-permute-start(bf16[1664,128]{1,0:T(8,128)(2,1)S(1)} %get-tuple-element.40), channel_id=1, source_target_pairs={{0,8},{2,10},{4,12},{6,14},{8,0},{10,2},{12,4},{14,6},{1,9},{3,11}... | collective-permute-start | bytes 1277960 | tf_op jit(solution)/shard_map/ppermute | solution.py:568
  11.2 2.0 %shard_map.65 = bf16[640,128]{1,0:T(8,128)(2,1)} custom-call(s32[3]{0:T(128)S(1)} %pad_add_fusion.rank_ref.scalars, s32[64,1]{1,0:T(8,128)S(1)} %copy.8.keep_ref, bf16[160,1024]{1,0:T(8,128)(2,1)S(1)} %reshape.15.patches_ref), custom_call_target="tpu_custom_call" | custom-call | tf_op jit(solution)/shard_map/pallas_call | solution.py:239
  13.2 3.8 %all-to-all-start = ((bf16[8,80,128]{2,1,0:T(8,128)(2,1)}), bf16[8,80,128]{2,1,0:T(8,128)(2,1)S(1)}, u32[]{:S(2)}, u32[]{:S(2)}) async-start(bf16[8,80,128]{2,1,0:T(8,128)(2,1)} %bitcast.5), calls=%async_computation | async-start | bytes 327680 | tf_op jit(solution)/shard_map/all_to_all | solution.py:572
  17.0 2.0 %collective-permute-start.2 = (bf16[1024,128]{1,0:T(8,128)(2,1)S(1)}, bf16[1024,128]{1,0:T(8,128)(2,1)S(1)}, u32[]{:S(2)}, u32[]{:S(2)}) collective-permute-start(bf16[1024,128]{1,0:T(8,128)(2,1)S(1)} %get-tuple-element.47), channel_id=1, source_target_pairs={{0,2},{2,0},{4,6},{6,4},{8,10},{10,8},{12,14},{14,12},{1,3},{3,1},... | collective-permute-start | bytes 786440 | tf_op jit(solution)/shard_map/ppermute | solution.py:568
  19.1 1.5 %collective-permute-start.3 = (bf16[1024,128]{1,0:T(8,128)(2,1)S(1)}, bf16[1024,128]{1,0:T(8,128)(2,1)S(1)}, u32[]{:S(2)}, u32[]{:S(2)}) collective-permute-start(bf16[1024,128]{1,0:T(8,128)(2,1)S(1)} %get-tuple-element.48), channel_id=1, source_target_pairs={{0,4},{2,6},{4,0},{6,2},{8,12},{10,14},{12,8},{14,10},{1,5},{3,7},... | collective-permute-start | bytes 786440 | tf_op jit(solution)/shard_map/ppermute | solution.py:568
  20.6 13.4 %all-to-all-done = bf16[8,80,128]{2,1,0:T(8,128)(2,1)S(1)} async-done(((bf16[8,80,128]{2,1,0:T(8,128)(2,1)}), bf16[8,80,128]{2,1,0:T(8,128)(2,1)S(1)}, u32[]{:S(2)}, u32[]{:S(2)}) %all-to-all-start) | async-done | bytes 163872 | tf_op jit(solution)/shard_map/all_to_all | solution.py:572
  34.0 0.9 shard_map.66.owned_ref
  34.9 3.4 %collective-permute-start = (bf16[256,128]{1,0:T(8,128)(2,1)S(1)}, bf16[256,128]{1,0:T(8,128)(2,1)S(1)}, u32[]{:S(2)}, u32[]{:S(2)}) collective-permute-start(bf16[256,128]{1,0:T(8,128)(2,1)S(1)} %shard_map.66.owned_ref), channel_id=1, source_target_pairs={{0,8},{2,10},{4,12},{6,14},{8,0},{10,2},{12,4},{14,6},{1,9},{3,11}... | collective-permute-start | bytes 196616 | tf_op jit(solution)/shard_map/ppermute | solution.py:568
  38.2 5.1 %collective-permute-done.4.refs_3_ = bf16[1024,128]{1,0:T(8,128)(2,1)S(1)} collective-permute-done((bf16[1024,128]{1,0:T(8,128)(2,1)S(1)}, bf16[1024,128]{1,0:T(8,128)(2,1)S(1)}, u32[]{:S(2)}, u32[]{:S(2)}) %collective-permute-start.4) | collective-permute-done | bytes 262176 | tf_op jit(solution)/shard_map/ppermute | solution.py:568
  43.3 1.2 %shard_map.67 = bf16[4,1312,128]{2,1,0:T(8,128)(2,1)} custom-call(bf16[256,128]{1,0:T(8,128)(2,1)S(1)} %shard_map.66.owned_ref, bf16[256,128]{1,0:T(8,128)(2,1)S(1)} %collective-permute-done.across_ref, bf16[4,192,128]{2,1,0:T(8,128)(2,1)S(1)} %get-tuple-element.51.heads_ref, bf16[1664,128]{1,0:T(8,128)(2,1)S(1)} %collective-permute-done.1.far_ref), custom_call_target="tpu_custom_call" | custom-call | tf_op jit(solution)/shard_map/pallas_call | solution.py:360
  44.5 3.5 %all-to-all-start.1 = ((bf16[4,1312,128]{2,1,0:T(8,128)(2,1)}), bf16[4,1312,128]{2,1,0:T(8,128)(2,1)S(1)}, u32[]{:S(2)}, u32[]{:S(2)}) async-start(bf16[4,1312,128]{2,1,0:T(8,128)(2,1)} %shard_map.67), calls=%async_computation.1 | async-start | bytes 2686976 | tf_op jit(solution)/shard_map/all_to_all | solution.py:578
  50.8 13.0 %all-to-all-done.1.mine_ref = bf16[4,1312,128]{2,1,0:T(8,128)(2,1)S(1)} async-done(((bf16[4,1312,128]{2,1,0:T(8,128)(2,1)}), bf16[4,1312,128]{2,1,0:T(8,128)(2,1)S(1)}, u32[]{:S(2)}, u32[]{:S(2)}) %all-to-all-start.1) | async-done | bytes 1343520 | tf_op jit(solution)/shard_map/all_to_all | solution.py:578
  64.0 1.6 %collective-permute-start.10 = (bf16[4,96,128]{2,1,0:T(8,128)(2,1)S(1)}, bf16[4,96,128]{2,1,0:T(8,128)(2,1)S(1)}, u32[]{:S(2)}, u32[]{:S(2)}) collective-permute-start(bf16[4,96,128]{2,1,0:T(8,128)(2,1)S(1)} %slice.13), channel_id=1, source_target_pairs={{0,16},{16,0},{1,17},{17,1},{2,18},{18,2},{3,19},{19,3},{4,20},{20... | collective-permute-start | bytes 294920 | tf_op jit(solution)/shard_map/ppermute | solution.py:568
  65.6 3.6 %collective-permute-done.10.far_ref = bf16[4,96,128]{2,1,0:T(8,128)(2,1)S(1)} collective-permute-done((bf16[4,96,128]{2,1,0:T(8,128)(2,1)S(1)}, bf16[4,96,128]{2,1,0:T(8,128)(2,1)S(1)}, u32[]{:S(2)}, u32[]{:S(2)}) %collective-permute-start.10) | collective-permute-done | bytes 98336 | tf_op jit(solution)/shard_map/ppermute | solution.py:568
  69.2 2.7 %shard_map.68 = (bf16[512,1024]{1,0:T(8,128)(2,1)S(1)}, bf16[64,512]{1,0:T(8,128)(2,1)S(1)}) custom-call(s32[3]{0:T(128)S(1)} %pad_add_fusion.rank_ref.scalars, bf16[4,1312,128]{2,1,0:T(8,128)(2,1)S(1)} %all-to-all-done.1.mine_ref, bf16[4,512,128]{2,1,0:T(8,128)(2,1)S(1)} %collective-permute-done.9.other_ref, ...), custom_call_target="tpu_custom_call" | custom-call | flops 30000001024 | bytes 1048576 | tf_op jit(solution)/shard_map/pallas_call | solution.py:426
  71.9 3.3 %collective-permute-start.11 = (bf16[64,512]{1,0:T(8,128)(2,1)S(1)}, bf16[64,512]{1,0:T(8,128)(2,1)S(1)}, u32[]{:S(2)}, u32[]{:S(2)}) collective-permute-start(bf16[64,512]{1,0:T(8,128)(2,1)S(1)} %get-tuple-element.59), channel_id=1, source_target_pairs={{0,8},{2,10},{4,12},{6,14},{8,0},{10,2},{12,4},{14,6},{1,9},{3,11}... | collective-permute-start | bytes 196616 | tf_op jit(solution)/shard_map/ppermute | solution.py:568
  75.3 1.6 %collective-permute-start.12 = (bf16[4,256,128]{2,1,0:T(8,128)(2,1)S(1)}, bf16[4,256,128]{2,1,0:T(8,128)(2,1)S(1)}, u32[]{:S(2)}, u32[]{:S(2)}) collective-permute-start(bf16[4,256,128]{2,1,0:T(8,128)(2,1)S(1)} %get-tuple-element.76.c), channel_id=1, source_target_pairs={{0,16},{16,0},{1,17},{17,1},{2,18},{18,2},{3,19},{19,3},{4,20},{20... | collective-permute-start | bytes 786440 | tf_op jit(solution)/shard_map/ppermute | solution.py:568
  77.4 1.2 %collective-permute-done.11 = bf16[64,512]{1,0:T(8,128)(2,1)S(1)} collective-permute-done((bf16[64,512]{1,0:T(8,128)(2,1)S(1)}, bf16[64,512]{1,0:T(8,128)(2,1)S(1)}, u32[]{:S(2)}, u32[]{:S(2)}) %collective-permute-start.11) | collective-permute-done | bytes 65568 | tf_op jit(solution)/shard_map/ppermute | solution.py:568
  79.8 2.3 %collective-permute-start.16 = (bf16[2,64,512]{2,1,0:T(8,128)(2,1)S(1)}, bf16[2,64,512]{2,1,0:T(8,128)(2,1)S(1)}, u32[]{:S(2)}, u32[]{:S(2)}) collective-permute-start(bf16[2,64,512]{2,1,0:T(8,128)(2,1)S(1)} %get-tuple-element.78), channel_id=1, source_target_pairs={{0,6},{2,4},{4,2},{6,0},{8,14},{10,12},{12,10},{14,8},{1,7},{3,5},... | collective-permute-start | bytes 393224 | tf_op jit(solution)/shard_map/ppermute | solution.py:568
  82.2 2.9 %collective-permute-done.15 = bf16[2,64,512]{2,1,0:T(8,128)(2,1)S(1)} collective-permute-done((bf16[2,64,512]{2,1,0:T(8,128)(2,1)S(1)}, bf16[2,64,512]{2,1,0:T(8,128)(2,1)S(1)}, u32[]{:S(2)}, u32[]{:S(2)}) %collective-permute-start.15) | collective-permute-done | bytes 131104 | tf_op jit(solution)/shard_map/ppermute | solution.py:568
  85.1 2.2 %collective-permute-done.16 = bf16[2,64,512]{2,1,0:T(8,128)(2,1)S(1)} collective-permute-done((bf16[2,64,512]{2,1,0:T(8,128)(2,1)S(1)}, bf16[2,64,512]{2,1,0:T(8,128)(2,1)S(1)}, u32[]{:S(2)}, u32[]{:S(2)}) %collective-permute-start.16) | collective-permute-done | bytes 131104 | tf_op jit(solution)/shard_map/ppermute | solution.py:568
  87.2 1.4 %collective-permute-done.13.f = bf16[4,256,128]{2,1,0:T(8,128)(2,1)S(1)} collective-permute-done((bf16[4,256,128]{2,1,0:T(8,128)(2,1)S(1)}, bf16[4,256,128]{2,1,0:T(8,128)(2,1)S(1)}, u32[]{:S(2)}, u32[]{:S(2)}) %collective-permute-start.13) | collective-permute-done | bytes 262176 | tf_op jit(solution)/shard_map/ppermute | solution.py:568
  89.3 1.7 %collective-permute-done.18.g = bf16[4,256,128]{2,1,0:T(8,128)(2,1)S(1)} collective-permute-done((bf16[4,256,128]{2,1,0:T(8,128)(2,1)S(1)}, bf16[4,256,128]{2,1,0:T(8,128)(2,1)S(1)}, u32[]{:S(2)}, u32[]{:S(2)}) %collective-permute-start.18) | collective-permute-done | bytes 262176 | tf_op jit(solution)/shard_map/ppermute | solution.py:568
  91.4 4.9 %shard_map.69 = (f32[64,512]{1,0:T(8,128)S(1)}, f32[512,512]{1,0:T(8,128)S(1)}, bf16[512,512]{1,0:T(8,128)(2,1)S(1)}) custom-call(s32[3]{0:T(128)S(1)} %pad_add_fusion.rank_ref.scalars, bf16[512,1024]{1,0:T(8,128)(2,1)S(1)} %get-tuple-element.58.tokens, bf16[4,2,64,512]{3,2,1,0:T(8,128)(2,1)S(1)} %pad_maximum_fusion.a, ...), custom_call_target="tpu_custom_call" | custom-call | tf_op jit(solution)/shard_map/pallas_call | solution.py:510
  96.5 1.8 %collective-permute-done.20.got_ref = bf16[512,512]{1,0:T(8,128)(2,1)S(1)} collective-permute-done((bf16[512,512]{1,0:T(8,128)(2,1)S(1)}, bf16[512,512]{1,0:T(8,128)(2,1)S(1)}, u32[]{:S(2)}, u32[]{:S(2)}) %collective-permute-start.20) | collective-permute-done | bytes 524320 | tf_op jit(solution)/shard_map/ppermute | solution.py:568
  98.9 17.5 %all_to_all.21.terms_ref = bf16[8,64,512]{2,1,0:T(8,128)(2,1)S(1)} all-to-all(bf16[8,64,512]{2,1,0:T(8,128)(2,1)S(1)} %bitcast.17), channel_id=1, replica_groups=mesh['groups'=2,'seq'=8,'head'=2] {'seq'}, dimensions={0} | all-to-all | bytes 1048576 | tf_op jit(solution)/shard_map/all_to_all | solution.py:572
  116.4 1.2 %shard_map.71 = bf16[64,512]{1,0:T(8,128)(2,1)} custom-call(s32[3]{0:T(128)S(1)} %pad_add_fusion.rank_ref.scalars, f32[64,512]{1,0:T(8,128)S(1)} %get-tuple-element.73.base_ref, bf16[8,64,512]{2,1,0:T(8,128)(2,1)S(1)} %all_to_all.21.terms_ref), custom_call_target="tpu_custom_call" | custom-call | tf_op jit(solution)/shard_map/pallas_call | solution.py:557
  (43 shorter events, 6.9 us)
Async XLA Ops:
  0.0 11.0 %copy-start.5 = (s32[1,64]{1,0:T(1,128)S(1)}, s32[1,64]{1,0:T(1,128)}, u32[]{:S(2)}) copy-start(s32[1,64]{1,0:T(1,128)} %param.7) | copy-start | bytes 772
  0.1 1.0 copy-start
  1.1 1.0 copy-start.1
  2.2 1.0 copy-start.2
  3.2 0.9 copy-start.3
  4.1 7.1 %copy-start.4 = (bf16[1,40,4,1024]{3,2,1,0:T(4,128)(2,1)S(1)}, bf16[1,40,4,1024]{3,2,1,0:T(4,128)(2,1)}, u32[]{:S(2)}) copy-start(bf16[1,40,4,1024]{3,2,1,0:T(4,128)(2,1)} %param.6) | copy-start | bytes 983044
  6.9 36.4 %collective-permute-start.1 = (bf16[1664,128]{1,0:T(8,128)(2,1)S(1)}, bf16[1664,128]{1,0:T(8,128)(2,1)S(1)}, u32[]{:S(2)}, u32[]{:S(2)}) collective-permute-start(bf16[1664,128]{1,0:T(8,128)(2,1)S(1)} %get-tuple-element.40), channel_id=1, source_target_pairs={{0,8},{2,10},{4,12},{6,14},{8,0},{10,2},{12,4},{14,6},{1,9},{3,11}... | collective-permute-start | bytes 1277960 | tf_op jit(solution)/shard_map/ppermute | solution.py:568
  13.2 20.7 %all-to-all-start = ((bf16[8,80,128]{2,1,0:T(8,128)(2,1)}), bf16[8,80,128]{2,1,0:T(8,128)(2,1)S(1)}, u32[]{:S(2)}, u32[]{:S(2)}) async-start(bf16[8,80,128]{2,1,0:T(8,128)(2,1)} %bitcast.5), calls=%async_computation | async-start | bytes 327680 | tf_op jit(solution)/shard_map/all_to_all | solution.py:572
  17.0 21.2 %collective-permute-start.2 = (bf16[1024,128]{1,0:T(8,128)(2,1)S(1)}, bf16[1024,128]{1,0:T(8,128)(2,1)S(1)}, u32[]{:S(2)}, u32[]{:S(2)}) collective-permute-start(bf16[1024,128]{1,0:T(8,128)(2,1)S(1)} %get-tuple-element.47), channel_id=1, source_target_pairs={{0,2},{2,0},{4,6},{6,4},{8,10},{10,8},{12,14},{14,12},{1,3},{3,1},... | collective-permute-start | bytes 786440 | tf_op jit(solution)/shard_map/ppermute | solution.py:568
  19.1 19.2 %collective-permute-start.3 = (bf16[1024,128]{1,0:T(8,128)(2,1)S(1)}, bf16[1024,128]{1,0:T(8,128)(2,1)S(1)}, u32[]{:S(2)}, u32[]{:S(2)}) collective-permute-start(bf16[1024,128]{1,0:T(8,128)(2,1)S(1)} %get-tuple-element.48), channel_id=1, source_target_pairs={{0,4},{2,6},{4,0},{6,2},{8,12},{10,14},{12,8},{14,10},{1,5},{3,7},... | collective-permute-start | bytes 786440 | tf_op jit(solution)/shard_map/ppermute | solution.py:568
  20.5 22.8 %collective-permute-start.4 = (bf16[1024,128]{1,0:T(8,128)(2,1)S(1)}, bf16[1024,128]{1,0:T(8,128)(2,1)S(1)}, u32[]{:S(2)}, u32[]{:S(2)}) collective-permute-start(bf16[1024,128]{1,0:T(8,128)(2,1)S(1)} %get-tuple-element.49), channel_id=1, source_target_pairs={{0,6},{2,4},{4,2},{6,0},{8,14},{10,12},{12,10},{14,8},{1,7},{3,5},... | collective-permute-start | bytes 786440 | tf_op jit(solution)/shard_map/ppermute | solution.py:568
  34.9 8.4 %collective-permute-start = (bf16[256,128]{1,0:T(8,128)(2,1)S(1)}, bf16[256,128]{1,0:T(8,128)(2,1)S(1)}, u32[]{:S(2)}, u32[]{:S(2)}) collective-permute-start(bf16[256,128]{1,0:T(8,128)(2,1)S(1)} %shard_map.66.owned_ref), channel_id=1, source_target_pairs={{0,8},{2,10},{4,12},{6,14},{8,0},{10,2},{12,4},{14,6},{1,9},{3,11}... | collective-permute-start | bytes 196616 | tf_op jit(solution)/shard_map/ppermute | solution.py:568
  44.5 19.3 %all-to-all-start.1 = ((bf16[4,1312,128]{2,1,0:T(8,128)(2,1)}), bf16[4,1312,128]{2,1,0:T(8,128)(2,1)S(1)}, u32[]{:S(2)}, u32[]{:S(2)}) async-start(bf16[4,1312,128]{2,1,0:T(8,128)(2,1)} %shard_map.67), calls=%async_computation.1 | async-start | bytes 2686976 | tf_op jit(solution)/shard_map/all_to_all | solution.py:578
  48.1 1.6 %collective-permute-start.5 = (bf16[1024,128]{1,0:T(8,128)(2,1)S(1)}, bf16[1024,128]{1,0:T(8,128)(2,1)S(1)}, u32[]{:S(2)}, u32[]{:S(2)}) collective-permute-start(bf16[1024,128]{1,0:T(8,128)(2,1)S(1)} %get-tuple-element.53.refs_0_), channel_id=1, source_target_pairs={{0,1},{1,0},{2,3},{3,2},{4,5},{5,4},{6,7},{7,6},{8,9},{9,8},{10,11... | collective-permute-start | bytes 786440 | tf_op jit(solution)/shard_map/ppermute | solution.py:568
  48.2 1.9 %collective-permute-start.6 = (bf16[1024,128]{1,0:T(8,128)(2,1)S(1)}, bf16[1024,128]{1,0:T(8,128)(2,1)S(1)}, u32[]{:S(2)}, u32[]{:S(2)}) collective-permute-start(bf16[1024,128]{1,0:T(8,128)(2,1)S(1)} %collective-permute-done.2.refs_1_), channel_id=1, source_target_pairs={{0,1},{1,0},{2,3},{3,2},{4,5},{5,4},{6,7},{7,6},{8,9},{9,8},{10,11... | collective-permute-start | bytes 786440 | tf_op jit(solution)/shard_map/ppermute | solution.py:568
  48.7 1.8 %collective-permute-start.7 = (bf16[1024,128]{1,0:T(8,128)(2,1)S(1)}, bf16[1024,128]{1,0:T(8,128)(2,1)S(1)}, u32[]{:S(2)}, u32[]{:S(2)}) collective-permute-start(bf16[1024,128]{1,0:T(8,128)(2,1)S(1)} %collective-permute-done.3.refs_2_), channel_id=1, source_target_pairs={{0,1},{1,0},{2,3},{3,2},{4,5},{5,4},{6,7},{7,6},{8,9},{9,8},{10,11... | collective-permute-start | bytes 786440 | tf_op jit(solution)/shard_map/ppermute | solution.py:568
  48.7 2.1 %collective-permute-start.8 = (bf16[1024,128]{1,0:T(8,128)(2,1)S(1)}, bf16[1024,128]{1,0:T(8,128)(2,1)S(1)}, u32[]{:S(2)}, u32[]{:S(2)}) collective-permute-start(bf16[1024,128]{1,0:T(8,128)(2,1)S(1)} %collective-permute-done.4.refs_3_), channel_id=1, source_target_pairs={{0,1},{1,0},{2,3},{3,2},{4,5},{5,4},{6,7},{7,6},{8,9},{9,8},{10,11... | collective-permute-start | bytes 786440 | tf_op jit(solution)/shard_map/ppermute | solution.py:568
  63.9 5.3 %collective-permute-start.9 = (bf16[4,512,128]{2,1,0:T(8,128)(2,1)S(1)}, bf16[4,512,128]{2,1,0:T(8,128)(2,1)S(1)}, u32[]{:S(2)}, u32[]{:S(2)}) collective-permute-start(bf16[4,512,128]{2,1,0:T(8,128)(2,1)S(1)} %slice.12), channel_id=1, source_target_pairs={{0,1},{1,0},{2,3},{3,2},{4,5},{5,4},{6,7},{7,6},{8,9},{9,8},{10,11... | collective-permute-start | bytes 1572872 | tf_op jit(solution)/shard_map/ppermute | solution.py:568
  64.0 5.2 %collective-permute-start.10 = (bf16[4,96,128]{2,1,0:T(8,128)(2,1)S(1)}, bf16[4,96,128]{2,1,0:T(8,128)(2,1)S(1)}, u32[]{:S(2)}, u32[]{:S(2)}) collective-permute-start(bf16[4,96,128]{2,1,0:T(8,128)(2,1)S(1)} %slice.13), channel_id=1, source_target_pairs={{0,16},{16,0},{1,17},{17,1},{2,18},{18,2},{3,19},{19,3},{4,20},{20... | collective-permute-start | bytes 294920 | tf_op jit(solution)/shard_map/ppermute | solution.py:568
  71.9 6.7 %collective-permute-start.11 = (bf16[64,512]{1,0:T(8,128)(2,1)S(1)}, bf16[64,512]{1,0:T(8,128)(2,1)S(1)}, u32[]{:S(2)}, u32[]{:S(2)}) collective-permute-start(bf16[64,512]{1,0:T(8,128)(2,1)S(1)} %get-tuple-element.59), channel_id=1, source_target_pairs={{0,8},{2,10},{4,12},{6,14},{8,0},{10,2},{12,4},{14,6},{1,9},{3,11}... | collective-permute-start | bytes 196616 | tf_op jit(solution)/shard_map/ppermute | solution.py:568
  75.3 12.0 %collective-permute-start.12 = (bf16[4,256,128]{2,1,0:T(8,128)(2,1)S(1)}, bf16[4,256,128]{2,1,0:T(8,128)(2,1)S(1)}, u32[]{:S(2)}, u32[]{:S(2)}) collective-permute-start(bf16[4,256,128]{2,1,0:T(8,128)(2,1)S(1)} %get-tuple-element.76.c), channel_id=1, source_target_pairs={{0,16},{16,0},{1,17},{17,1},{2,18},{18,2},{3,19},{19,3},{4,20},{20... | collective-permute-start | bytes 786440 | tf_op jit(solution)/shard_map/ppermute | solution.py:568
  76.8 11.8 %collective-permute-start.13 = (bf16[4,256,128]{2,1,0:T(8,128)(2,1)S(1)}, bf16[4,256,128]{2,1,0:T(8,128)(2,1)S(1)}, u32[]{:S(2)}, u32[]{:S(2)}) collective-permute-start(bf16[4,256,128]{2,1,0:T(8,128)(2,1)S(1)} %get-tuple-element.75.e), channel_id=1, source_target_pairs={{0,16},{16,0},{1,17},{17,1},{2,18},{18,2},{3,19},{19,3},{4,20},{20... | collective-permute-start | bytes 786440 | tf_op jit(solution)/shard_map/ppermute | solution.py:568
  78.6 6.4 %collective-permute-start.15 = (bf16[2,64,512]{2,1,0:T(8,128)(2,1)S(1)}, bf16[2,64,512]{2,1,0:T(8,128)(2,1)S(1)}, u32[]{:S(2)}, u32[]{:S(2)}) collective-permute-start(bf16[2,64,512]{2,1,0:T(8,128)(2,1)S(1)} %get-tuple-element.78), channel_id=1, source_target_pairs={{0,4},{2,6},{4,0},{6,2},{8,12},{10,14},{12,8},{14,10},{1,5},{3,7},... | collective-permute-start | bytes 393224 | tf_op jit(solution)/shard_map/ppermute | solution.py:568
  79.0 6.1 %collective-permute-start.14 = (bf16[2,64,512]{2,1,0:T(8,128)(2,1)S(1)}, bf16[2,64,512]{2,1,0:T(8,128)(2,1)S(1)}, u32[]{:S(2)}, u32[]{:S(2)}) collective-permute-start(bf16[2,64,512]{2,1,0:T(8,128)(2,1)S(1)} %get-tuple-element.78), channel_id=1, source_target_pairs={{0,2},{2,0},{4,6},{6,4},{8,10},{10,8},{12,14},{14,12},{1,3},{3,1},... | collective-permute-start | bytes 393224 | tf_op jit(solution)/shard_map/ppermute | solution.py:568
  79.8 7.4 %collective-permute-start.16 = (bf16[2,64,512]{2,1,0:T(8,128)(2,1)S(1)}, bf16[2,64,512]{2,1,0:T(8,128)(2,1)S(1)}, u32[]{:S(2)}, u32[]{:S(2)}) collective-permute-start(bf16[2,64,512]{2,1,0:T(8,128)(2,1)S(1)} %get-tuple-element.78), channel_id=1, source_target_pairs={{0,6},{2,4},{4,2},{6,0},{8,14},{10,12},{12,10},{14,8},{1,7},{3,5},... | collective-permute-start | bytes 393224 | tf_op jit(solution)/shard_map/ppermute | solution.py:568
  88.7 2.7 %collective-permute-start.17 = (bf16[4,2,64,512]{3,2,1,0:T(8,128)(2,1)S(1)}, bf16[4,2,64,512]{3,2,1,0:T(8,128)(2,1)S(1)}, u32[]{:S(2)}, u32[]{:S(2)}) collective-permute-start(bf16[4,2,64,512]{3,2,1,0:T(8,128)(2,1)S(1)} %pad_maximum_fusion.a), channel_id=1, source_target_pairs={{0,1},{1,0},{2,3},{3,2},{4,5},{5,4},{6,7},{7,6},{8,9},{9,8},{10,11... | collective-permute-start | bytes 1572872 | tf_op jit(solution)/shard_map/ppermute | solution.py:568
  88.7 2.3 %collective-permute-start.18 = (bf16[4,256,128]{2,1,0:T(8,128)(2,1)S(1)}, bf16[4,256,128]{2,1,0:T(8,128)(2,1)S(1)}, u32[]{:S(2)}, u32[]{:S(2)}) collective-permute-start(bf16[4,256,128]{2,1,0:T(8,128)(2,1)S(1)} %get-tuple-element.75.e), channel_id=1, source_target_pairs={{0,1},{1,0},{2,3},{3,2},{4,5},{5,4},{6,7},{7,6},{8,9},{9,8},{10,11... | collective-permute-start | bytes 786440 | tf_op jit(solution)/shard_map/ppermute | solution.py:568
  89.2 2.1 %collective-permute-start.19 = (bf16[4,256,128]{2,1,0:T(8,128)(2,1)S(1)}, bf16[4,256,128]{2,1,0:T(8,128)(2,1)S(1)}, u32[]{:S(2)}, u32[]{:S(2)}) collective-permute-start(bf16[4,256,128]{2,1,0:T(8,128)(2,1)S(1)} %collective-permute-done.13.f), channel_id=1, source_target_pairs={{0,1},{1,0},{2,3},{3,2},{4,5},{5,4},{6,7},{7,6},{8,9},{9,8},{10,11... | collective-permute-start | bytes 786440 | tf_op jit(solution)/shard_map/ppermute | solution.py:568
  96.3 2.0 %collective-permute-start.20 = (bf16[512,512]{1,0:T(8,128)(2,1)S(1)}, bf16[512,512]{1,0:T(8,128)(2,1)S(1)}, u32[]{:S(2)}, u32[]{:S(2)}) collective-permute-start(bf16[512,512]{1,0:T(8,128)(2,1)S(1)} %get-tuple-element.71), channel_id=1, source_target_pairs={{0,1},{1,0},{2,3},{3,2},{4,5},{5,4},{6,7},{7,6},{8,9},{9,8},{10,11... | collective-permute-start | bytes 1572872 | tf_op jit(solution)/shard_map/ppermute | solution.py:568

commit v10 on v9

--- a/solution.py
+++ b/solution.py
@@ -290,7 +290,7 @@
 
 
 def pack_kernel(n, rank_ref, qkv_ref, out_weight_ref, up_ref, down_ref, *refs):
-    near, (heads_ref, away_ref, sem) = refs[: n // 2], refs[n // 2 :]
+    near, (heads_ref, away_ref, blocks_ref, sem) = refs[: n // 2], refs[n // 2 :]
     rank, part = rank_ref[0], rank_ref[2]
     half = n // 2
     rows = up_ref.shape[0]
@@ -298,18 +298,16 @@
     units = wide // 2
     long = out_weight_ref.shape[0]
     depth = qkv_ref.shape[1] // 2
-    each = depth + rows + units
     copies = []
     for d in range(half):
         dest = (rank // half ^ 1) * half + d
-        low = d * each
         at = pl.ds(pl.multiple_of(part * depth, 32), depth)
-        copies.append((qkv_ref.at[dest, at], away_ref.at[pl.ds(low, depth)]))
+        copies.append((qkv_ref.at[dest, at], away_ref.at[pl.ds(d * depth, depth)]))
         at = pl.ds(pl.multiple_of(dest * wide + part * units, 128), units)
-        copies.append((up_ref.at[:, at], away_ref.at[pl.ds(low + depth, rows)]))
-        copies.append((down_ref.at[at], away_ref.at[pl.ds(low + depth + rows, units)]))
+        copies.append((up_ref.at[:, at], blocks_ref.at[d, pl.ds(0, rows)]))
+        copies.append((down_ref.at[at], blocks_ref.at[d, pl.ds(rows, units)]))
     at = pl.ds(pl.multiple_of(part * (long // 2), 128), long // 2)
-    copies.append((out_weight_ref.at[at], away_ref.at[pl.ds(half * each, long // 2)]))
+    copies.append((out_weight_ref.at[at], away_ref.at[pl.ds(half * depth, long // 2)]))
     copies.append((qkv_ref.at[pl.ds(rank // half * half, half)], heads_ref))
     for j in range(half):
         dest = rank ^ j
@@ -326,44 +324,50 @@
     half = n // 2
     wide = up.shape[1] // n
     near = struct((2 * up.shape[0] + wide + out_weight.shape[0], 128))
-    each = qkv.shape[1] // 2 + up.shape[0] + wide // 2
-    away = struct((half * each + out_weight.shape[0] // 2, 128))
+    away = struct((half * qkv.shape[1] // 2 + out_weight.shape[0] // 2, 128))
+    blocks = struct((half, up.shape[0] + wide // 2, 128))
     outs = pl.pallas_call(
         functools.partial(pack_kernel, n),
         in_specs=[sspec()] + [hspec()] * 4,
-        out_specs=[aspec()] * (half + 2),
-        out_shape=[near] * half + [struct((half,) + qkv.shape[1:]), away],
+        out_specs=[aspec()] * (half + 3),
+        out_shape=[near] * half + [struct((half,) + qkv.shape[1:]), away, blocks],
         scratch_shapes=[pltpu.SemaphoreType.DMA((7 * half + 2,))],
-        compiler_params=params(),
+        compiler_params=params(48),
     )(scalars, qkv, out_weight, up, down)
-    return list(outs[:half]), outs[half], outs[half + 1]
-
-
-def fan_kernel(owned_ref, across_ref, heads_ref, far_ref, out_ref):
+    return list(outs[:half]), *outs[half:]
+
+
+def fan_kernel(owned_ref, across_ref, heads_ref, far_ref, blocks_ref, out_ref):
     rows = owned_ref.shape[0]
     count, head_rows = heads_ref.shape[:2]
-    top = 2 * rows + head_rows
-    rest = out_ref.shape[1] - top
-    each = (far_ref.shape[0] - rest) // (count - 1)
+    piece = head_rows // 2
+    units = blocks_ref.shape[1]
     for d in range(count):
-        out_ref[d, :rows] = owned_ref[...]
-        out_ref[d, rows : 2 * rows] = across_ref[...]
-        out_ref[d, 2 * rows : top] = heads_ref[d]
-        out_ref[d, top : top + each] = far_ref[d * each : (d + 1) * each]
-        out_ref[d, top + each :] = far_ref[count * each :]
-
-
-def fan(owned, across, heads, far, out_rows):
+        parts = (
+            owned_ref[...],
+            across_ref[...],
+            heads_ref[d],
+            far_ref[d * piece : (d + 1) * piece],
+            blocks_ref[d],
+            far_ref[count * piece :],
+        )
+        low = 0
+        for part in parts:
+            out_ref[d, low : low + part.shape[0]] = part
+            low += part.shape[0]
+
+
+def fan(owned, across, heads, far, blocks):
     count = heads.shape[0]
-    each = (far.shape[0] - out_rows) // count
-    shape = struct((count, 2 * owned.shape[0] + heads.shape[1] + each + out_rows, 128))
+    out_rows = far.shape[0] - count * heads.shape[1] // 2
+    rows = 2 * owned.shape[0] + 3 * heads.shape[1] // 2 + blocks.shape[1] + out_rows
     return pl.pallas_call(
         fan_kernel,
-        in_specs=[vspec()] * 4,
+        in_specs=[vspec()] * 5,
         out_specs=vspec(),
-        out_shape=shape,
+        out_shape=struct((count, rows, 128)),
         compiler_params=params(8),
-    )(owned, across, heads, far)
+    )(owned, across, heads, far, blocks)
 
 
 def source_of(rank, n, q, k):
@@ -601,18 +605,19 @@
     flat = patches.reshape(4 * sup, depth)
     heads = qkv_weight.transpose(1, 2, 0)
 
-    near, qkv_near, away = pack(scalars, heads, out_weight, up_weight, down_weight, n)
+    near, qkv_near, away, blocks = pack(scalars, heads, out_weight, up_weight, down_weight, n)
     far = swap(away, "seq", half)
     slots = prep(scalars, keep_col, after(flat, away), n, sup, capacity)
     dealt = exchange(slots)
-    near = lax.optimization_barrier((*near, slots))[:half]
+    blocks, *near = lax.optimization_barrier((blocks, *near, slots))[:-1]
+    mlp_far = swap(blocks, "seq", half)
     near = [near[0]] + [swap(near[j], "seq", j) for j in range(1, half)]
     owned = pick(scalars, keep_col, dealt, n, sup, per_owner, capacity)
     across = swap(owned, "seq", half)
-    across, far, *near = lax.optimization_barrier((across, far, *near))
+    across, far, mlp_far, *near = lax.optimization_barrier((across, far, mlp_far, *near))
 
     out_rows = out_weight.shape[0] // 2
-    got = exchange_half(fan(owned, across, qkv_near, far, out_rows))
+    got = exchange_half(fan(owned, across, qkv_near, far, mlp_far))
     near_other = [swap(block, "head", 1) for block in near]
     got, *near_other = lax.optimization_barrier((got, *near_other))
 

time: 118 us -> 122 us (1.034)
  starting transfers between devices: 30.9 us -> 33.7 us
  local copies, waits for them, and re-layouts: 4.24 us -> 5.85 us
  waiting for transfers between devices: 48.3 us -> 46.9 us
    all_to_all x1, waiting for transfers between devices: 13.4 us -> 6.98 us  [exchange(): return lax.all_to_all(value, 'seq', split_axis=0, concat_axis=0, tiled=True)]
    ppermute x21 -> x22, waiting for transfers between devices: 21.8 us -> 28.2 us  [swap(): return lax.ppermute(value, axis, [(i, i ^ j) for i in range(n)])]
    all_to_all x1, starting transfers between devices: 3.81 us -> 7.28 us  [exchange(): return lax.all_to_all(value, 'seq', split_axis=0, concat_axis=0, tiled=True)]
    ppermute x21 -> x22, starting transfers between devices: 23.5 us -> 20.1 us  [swap(): return lax.ppermute(value, axis, [(i, i ^ j) for i in range(n)])]
    all_to_all x1, starting transfers between devices: 3.54 us -> 6.29 us  [exchange_half(): lax.all_to_all(value, 'seq', split_axis=0, concat_axis=0, axis_index_grou...]
    all_to_all x1, waiting for transfers between devices: 13 us -> 11.8 us  [exchange_half(): lax.all_to_all(value, 'seq', split_axis=0, concat_axis=0, axis_index_grou...]
    unnamed x12 -> x8, local copies, waits for them, and re-layouts: 3.99 us -> 3.98 us
  transfers between devices with their start and end apart: 23 -> 24, of which waited for: 15 -> 17; matrix products, arithmetic and copies ran while one was open for 0% -> 0% of each run, Pallas kernels for 2% -> 1%
where the time goes in v10:
time: 122 us; the launch traced here: 121 us
  waiting for transfers between devices  46.9 us (38%)
  starting transfers between devices  33.7 us (28%)
  blocking collectives  18.3 us (15%)
  Pallas kernels  16.4 us (13%)
  local copies, waits for them, and re-layouts  5.85 us (5%)
    ppermute x22, waiting for transfers between devices, swap(): return lax.ppermute(value, axis, [(i, i ^ j) for i in range(n)])  28.2 us
    ppermute x22, starting transfers between devices, swap(): return lax.ppermute(value, axis, [(i, i ^ j) for i in range(n)])  20.1 us
    all_to_all x1, blocking collectives, exchange(): return lax.all_to_all(value, 'seq', split_axis=0, concat_axis=0, tiled=True)  18.3 us
    all_to_all x1, waiting for transfers between devices, exchange_half(): lax.all_to_all(value, 'seq', split_axis=0, concat_axis=0, axis_index_grou...  11.8 us
    all_to_all x1, starting transfers between devices, exchange(): return lax.all_to_all(value, 'seq', split_axis=0, concat_axis=0, tiled=True)  7.28 us
    all_to_all x1, waiting for transfers between devices, exchange(): return lax.all_to_all(value, 'seq', split_axis=0, concat_axis=0, tiled=True)  6.98 us
    all_to_all x1, starting transfers between devices, exchange_half(): lax.all_to_all(value, 'seq', split_axis=0, concat_axis=0, axis_index_grou...  6.29 us
    pallas_call x1, Pallas kernels, mlp(): pl.pallas_call(kernel, in_specs=[sspec()] + [vspec()] * 3 + [aspec()] * (...  4.86 us
  transfers between devices with their start and end apart: 24, of which 17 were waited for; matrix products, arithmetic and copies ran while one was open for 0% of the time, Pallas kernels for 1%

profile of v10, /device:TPU:0, one launch (start us, length us, event | category | flops | bytes accessed | tf_op | source)
XLA Modules:
  0.0 121.5 jit_solution(12981757573727196462)
XLA Ops:
  0.7 1.0 reshape.15.patches_ref
  1.9 1.0 copy-done
  2.9 1.0 copy-done.1
  4.0 1.0 copy-done.2
  5.9 2.9 %shard_map.64 = (bf16[1024,128]{1,0:T(8,128)(2,1)S(1)}, bf16[1024,128]{1,0:T(8,128)(2,1)S(1)}, bf16[1024,128]{1,0:T(8,128)(2,1)S(1)}, bf16[1024,128]{1,0:T(8,128...) custom-call(s32[3]{0:T(128)S(1)} %pad_add_fusion.rank_ref.scalars, ...), custom_call_target="tpu_custom_call" | custom-call | tf_op jit(solution)/shard_map/pallas_call | solution.py:329
  8.7 2.0 %shard_map.65 = bf16[640,128]{1,0:T(8,128)(2,1)} custom-call(s32[3]{0:T(128)S(1)} %pad_add_fusion.rank_ref.scalars, s32[64,1]{1,0:T(8,128)S(1)} %copy.8.keep_ref, bf16[160,1024]{1,0:T(8,128)(2,1)S(1)} %reshape.15.patches_ref), custom_call_target="tpu_custom_call" | custom-call | tf_op jit(solution)/shard_map/pallas_call | solution.py:239
  10.7 7.3 %all-to-all-start = ((bf16[8,80,128]{2,1,0:T(8,128)(2,1)}), bf16[8,80,128]{2,1,0:T(8,128)(2,1)S(1)}, u32[]{:S(2)}, u32[]{:S(2)}) async-start(bf16[8,80,128]{2,1,0:T(8,128)(2,1)} %bitcast.5), calls=%async_computation | async-start | bytes 327680 | tf_op jit(solution)/shard_map/all_to_all | solution.py:576
  18.0 2.9 %collective-permute-start.2 = (bf16[4,256,128]{2,1,0:T(8,128)(2,1)S(1)}, bf16[4,256,128]{2,1,0:T(8,128)(2,1)S(1)}, u32[]{:S(2)}, u32[]{:S(2)}) collective-permute-start(bf16[4,256,128]{2,1,0:T(8,128)(2,1)S(1)} %get-tuple-element.50), channel_id=1, source_target_pairs={{0,8},{2,10},{4,12},{6,14},{8,0},{10,2},{12,4},{14,6},{1,9},{3,11}... | collective-permute-start | bytes 786440 | tf_op jit(solution)/shard_map/ppermute | solution.py:572
  20.9 1.5 %collective-permute-start.3 = (bf16[1024,128]{1,0:T(8,128)(2,1)S(1)}, bf16[1024,128]{1,0:T(8,128)(2,1)S(1)}, u32[]{:S(2)}, u32[]{:S(2)}) collective-permute-start(bf16[1024,128]{1,0:T(8,128)(2,1)S(1)} %get-tuple-element.52), channel_id=1, source_target_pairs={{0,2},{2,0},{4,6},{6,4},{8,10},{10,8},{12,14},{14,12},{1,3},{3,1},... | collective-permute-start | bytes 786440 | tf_op jit(solution)/shard_map/ppermute | solution.py:572
  22.4 1.5 %collective-permute-start.4 = (bf16[1024,128]{1,0:T(8,128)(2,1)S(1)}, bf16[1024,128]{1,0:T(8,128)(2,1)S(1)}, u32[]{:S(2)}, u32[]{:S(2)}) collective-permute-start(bf16[1024,128]{1,0:T(8,128)(2,1)S(1)} %get-tuple-element.53), channel_id=1, source_target_pairs={{0,4},{2,6},{4,0},{6,2},{8,12},{10,14},{12,8},{14,10},{1,5},{3,7},... | collective-permute-start | bytes 786440 | tf_op jit(solution)/shard_map/ppermute | solution.py:572
  24.5 7.0 %all-to-all-done = bf16[8,80,128]{2,1,0:T(8,128)(2,1)S(1)} async-done(((bf16[8,80,128]{2,1,0:T(8,128)(2,1)}), bf16[8,80,128]{2,1,0:T(8,128)(2,1)S(1)}, u32[]{:S(2)}, u32[]{:S(2)}) %all-to-all-start) | async-done | bytes 163872 | tf_op jit(solution)/shard_map/all_to_all | solution.py:576
  31.4 0.9 shard_map.66.owned_ref
  32.4 8.8 %collective-permute-done.1.far_ref = bf16[640,128]{1,0:T(8,128)(2,1)S(1)} collective-permute-done((bf16[640,128]{1,0:T(8,128)(2,1)S(1)}, bf16[640,128]{1,0:T(8,128)(2,1)S(1)}, u32[]{:S(2)}, u32[]{:S(2)}) %collective-permute-start.1) | collective-permute-done | bytes 163872 | tf_op jit(solution)/shard_map/ppermute | solution.py:572
  41.2 3.4 %collective-permute-start = (bf16[256,128]{1,0:T(8,128)(2,1)S(1)}, bf16[256,128]{1,0:T(8,128)(2,1)S(1)}, u32[]{:S(2)}, u32[]{:S(2)}) collective-permute-start(bf16[256,128]{1,0:T(8,128)(2,1)S(1)} %shard_map.66.owned_ref), channel_id=1, source_target_pairs={{0,8},{2,10},{4,12},{6,14},{8,0},{10,2},{12,4},{14,6},{1,9},{3,11}... | collective-permute-start | bytes 196616 | tf_op jit(solution)/shard_map/ppermute | solution.py:572
  45.0 1.8 %collective-permute-done.across_ref = bf16[256,128]{1,0:T(8,128)(2,1)S(1)} collective-permute-done((bf16[256,128]{1,0:T(8,128)(2,1)S(1)}, bf16[256,128]{1,0:T(8,128)(2,1)S(1)}, u32[]{:S(2)}, u32[]{:S(2)}) %collective-permute-start) | collective-permute-done | bytes 65568 | tf_op jit(solution)/shard_map/ppermute | solution.py:572
  46.8 1.2 %shard_map.67 = bf16[4,1312,128]{2,1,0:T(8,128)(2,1)} custom-call(bf16[256,128]{1,0:T(8,128)(2,1)S(1)} %shard_map.66.owned_ref, bf16[256,128]{1,0:T(8,128)(2,1)S(1)} %collective-permute-done.across_ref, bf16[4,192,128]{2,1,0:T(8,128)(2,1)S(1)} %get-tuple-element.56.heads_ref, bf16[640,128]{1,0:T(8,128)(2,1)S(1)} %collective-permute-done.1.far_ref, ...), custom_call_target="tpu_custom_call" | custom-call | tf_op jit(solution)/shard_map/pallas_call | solution.py:364
  48.0 6.3 %all-to-all-start.1 = ((bf16[4,1312,128]{2,1,0:T(8,128)(2,1)}), bf16[4,1312,128]{2,1,0:T(8,128)(2,1)S(1)}, u32[]{:S(2)}, u32[]{:S(2)}) async-start(bf16[4,1312,128]{2,1,0:T(8,128)(2,1)} %shard_map.67), calls=%async_computation.1 | async-start | bytes 2686976 | tf_op jit(solution)/shard_map/all_to_all | solution.py:582
  57.0 11.8 %all-to-all-done.1.mine_ref = bf16[4,1312,128]{2,1,0:T(8,128)(2,1)S(1)} async-done(((bf16[4,1312,128]{2,1,0:T(8,128)(2,1)}), bf16[4,1312,128]{2,1,0:T(8,128)(2,1)S(1)}, u32[]{:S(2)}, u32[]{:S(2)}) %all-to-all-start.1) | async-done | bytes 1343520 | tf_op jit(solution)/shard_map/all_to_all | solution.py:582
  68.9 1.6 %collective-permute-start.11 = (bf16[4,96,128]{2,1,0:T(8,128)(2,1)S(1)}, bf16[4,96,128]{2,1,0:T(8,128)(2,1)S(1)}, u32[]{:S(2)}, u32[]{:S(2)}) collective-permute-start(bf16[4,96,128]{2,1,0:T(8,128)(2,1)S(1)} %slice.13), channel_id=1, source_target_pairs={{0,16},{16,0},{1,17},{17,1},{2,18},{18,2},{3,19},{19,3},{4,20},{20... | collective-permute-start | bytes 294920 | tf_op jit(solution)/shard_map/ppermute | solution.py:572
  70.4 3.7 %collective-permute-done.11.far_ref = bf16[4,96,128]{2,1,0:T(8,128)(2,1)S(1)} collective-permute-done((bf16[4,96,128]{2,1,0:T(8,128)(2,1)S(1)}, bf16[4,96,128]{2,1,0:T(8,128)(2,1)S(1)}, u32[]{:S(2)}, u32[]{:S(2)}) %collective-permute-start.11) | collective-permute-done | bytes 98336 | tf_op jit(solution)/shard_map/ppermute | solution.py:572
  74.1 2.7 %shard_map.68 = (bf16[512,1024]{1,0:T(8,128)(2,1)S(1)}, bf16[64,512]{1,0:T(8,128)(2,1)S(1)}) custom-call(s32[3]{0:T(128)S(1)} %pad_add_fusion.rank_ref.scalars, bf16[4,1312,128]{2,1,0:T(8,128)(2,1)S(1)} %all-to-all-done.1.mine_ref, bf16[4,512,128]{2,1,0:T(8,128)(2,1)S(1)} %collective-permute-done.10.other_ref, ...), custom_call_target="tpu_custom_call" | custom-call | flops 30000001024 | bytes 1048576 | tf_op jit(solution)/shard_map/pallas_call | solution.py:430
  76.8 1.1 collective-permute-start.12
  78.0 1.6 %collective-permute-start.13 = (bf16[4,256,128]{2,1,0:T(8,128)(2,1)S(1)}, bf16[4,256,128]{2,1,0:T(8,128)(2,1)S(1)}, u32[]{:S(2)}, u32[]{:S(2)}) collective-permute-start(bf16[4,256,128]{2,1,0:T(8,128)(2,1)S(1)} %get-tuple-element.82.c), channel_id=1, source_target_pairs={{0,16},{16,0},{1,17},{17,1},{2,18},{18,2},{3,19},{19,3},{4,20},{20... | collective-permute-start | bytes 786440 | tf_op jit(solution)/shard_map/ppermute | solution.py:572
  80.1 3.0 %collective-permute-done.12 = bf16[64,512]{1,0:T(8,128)(2,1)S(1)} collective-permute-done((bf16[64,512]{1,0:T(8,128)(2,1)S(1)}, bf16[64,512]{1,0:T(8,128)(2,1)S(1)}, u32[]{:S(2)}, u32[]{:S(2)}) %collective-permute-start.12) | collective-permute-done | bytes 65568 | tf_op jit(solution)/shard_map/ppermute | solution.py:572
  84.5 2.1 %collective-permute-start.17 = (bf16[2,64,512]{2,1,0:T(8,128)(2,1)S(1)}, bf16[2,64,512]{2,1,0:T(8,128)(2,1)S(1)}, u32[]{:S(2)}, u32[]{:S(2)}) collective-permute-start(bf16[2,64,512]{2,1,0:T(8,128)(2,1)S(1)} %get-tuple-element.84), channel_id=1, source_target_pairs={{0,6},{2,4},{4,2},{6,0},{8,14},{10,12},{12,10},{14,8},{1,7},{3,5},... | collective-permute-start | bytes 393224 | tf_op jit(solution)/shard_map/ppermute | solution.py:572
  86.6 2.5 %collective-permute-done.16 = bf16[2,64,512]{2,1,0:T(8,128)(2,1)S(1)} collective-permute-done((bf16[2,64,512]{2,1,0:T(8,128)(2,1)S(1)}, bf16[2,64,512]{2,1,0:T(8,128)(2,1)S(1)}, u32[]{:S(2)}, u32[]{:S(2)}) %collective-permute-start.16) | collective-permute-done | bytes 131104 | tf_op jit(solution)/shard_map/ppermute | solution.py:572
  90.0 1.6 %collective-permute-done.17 = bf16[2,64,512]{2,1,0:T(8,128)(2,1)S(1)} collective-permute-done((bf16[2,64,512]{2,1,0:T(8,128)(2,1)S(1)}, bf16[2,64,512]{2,1,0:T(8,128)(2,1)S(1)}, u32[]{:S(2)}, u32[]{:S(2)}) %collective-permute-start.17) | collective-permute-done | bytes 131104 | tf_op jit(solution)/shard_map/ppermute | solution.py:572
  92.3 1.7 %collective-permute-done.19.g = bf16[4,256,128]{2,1,0:T(8,128)(2,1)S(1)} collective-permute-done((bf16[4,256,128]{2,1,0:T(8,128)(2,1)S(1)}, bf16[4,256,128]{2,1,0:T(8,128)(2,1)S(1)}, u32[]{:S(2)}, u32[]{:S(2)}) %collective-permute-start.19) | collective-permute-done | bytes 262176 | tf_op jit(solution)/shard_map/ppermute | solution.py:572
  94.4 4.9 %shard_map.69 = (f32[64,512]{1,0:T(8,128)S(1)}, f32[512,512]{1,0:T(8,128)S(1)}, bf16[512,512]{1,0:T(8,128)(2,1)S(1)}) custom-call(s32[3]{0:T(128)S(1)} %pad_add_fusion.rank_ref.scalars, bf16[512,1024]{1,0:T(8,128)(2,1)S(1)} %get-tuple-element.64.tokens, bf16[4,2,64,512]{3,2,1,0:T(8,128)(2,1)S(1)} %pad_maximum_fusion.a, ...), custom_call_target="tpu_custom_call" | custom-call | tf_op jit(solution)/shard_map/pallas_call | solution.py:514
  99.5 1.8 %collective-permute-done.21.got_ref = bf16[512,512]{1,0:T(8,128)(2,1)S(1)} collective-permute-done((bf16[512,512]{1,0:T(8,128)(2,1)S(1)}, bf16[512,512]{1,0:T(8,128)(2,1)S(1)}, u32[]{:S(2)}, u32[]{:S(2)}) %collective-permute-start.21) | collective-permute-done | bytes 524320 | tf_op jit(solution)/shard_map/ppermute | solution.py:572
  101.9 18.3 %all_to_all.21.terms_ref = bf16[8,64,512]{2,1,0:T(8,128)(2,1)S(1)} all-to-all(bf16[8,64,512]{2,1,0:T(8,128)(2,1)S(1)} %bitcast.17), channel_id=1, replica_groups=mesh['groups'=2,'seq'=8,'head'=2] {'seq'}, dimensions={0} | all-to-all | bytes 1048576 | tf_op jit(solution)/shard_map/all_to_all | solution.py:576
  120.2 1.2 %shard_map.71 = bf16[64,512]{1,0:T(8,128)(2,1)} custom-call(s32[3]{0:T(128)S(1)} %pad_add_fusion.rank_ref.scalars, f32[64,512]{1,0:T(8,128)S(1)} %get-tuple-element.79.base_ref, bf16[8,64,512]{2,1,0:T(8,128)(2,1)S(1)} %all_to_all.21.terms_ref), custom_call_target="tpu_custom_call" | custom-call | tf_op jit(solution)/shard_map/pallas_call | solution.py:561
  (41 shorter events, 10.4 us)
Async XLA Ops:
  1.9 1.0 copy-start
  2.9 1.0 copy-start.1
  4.0 1.0 copy-start.2
  5.0 0.9 copy-start.3
  10.7 20.7 %all-to-all-start = ((bf16[8,80,128]{2,1,0:T(8,128)(2,1)}), bf16[8,80,128]{2,1,0:T(8,128)(2,1)S(1)}, u32[]{:S(2)}, u32[]{:S(2)}) async-start(bf16[8,80,128]{2,1,0:T(8,128)(2,1)} %bitcast.5), calls=%async_computation | async-start | bytes 327680 | tf_op jit(solution)/shard_map/all_to_all | solution.py:576
  18.0 26.5 %collective-permute-start.2 = (bf16[4,256,128]{2,1,0:T(8,128)(2,1)S(1)}, bf16[4,256,128]{2,1,0:T(8,128)(2,1)S(1)}, u32[]{:S(2)}, u32[]{:S(2)}) collective-permute-start(bf16[4,256,128]{2,1,0:T(8,128)(2,1)S(1)} %get-tuple-element.50), channel_id=1, source_target_pairs={{0,8},{2,10},{4,12},{6,14},{8,0},{10,2},{12,4},{14,6},{1,9},{3,11}... | collective-permute-start | bytes 786440 | tf_op jit(solution)/shard_map/ppermute | solution.py:572
  20.9 23.6 %collective-permute-start.3 = (bf16[1024,128]{1,0:T(8,128)(2,1)S(1)}, bf16[1024,128]{1,0:T(8,128)(2,1)S(1)}, u32[]{:S(2)}, u32[]{:S(2)}) collective-permute-start(bf16[1024,128]{1,0:T(8,128)(2,1)S(1)} %get-tuple-element.52), channel_id=1, source_target_pairs={{0,2},{2,0},{4,6},{6,4},{8,10},{10,8},{12,14},{14,12},{1,3},{3,1},... | collective-permute-start | bytes 786440 | tf_op jit(solution)/shard_map/ppermute | solution.py:572
  22.4 22.2 %collective-permute-start.4 = (bf16[1024,128]{1,0:T(8,128)(2,1)S(1)}, bf16[1024,128]{1,0:T(8,128)(2,1)S(1)}, u32[]{:S(2)}, u32[]{:S(2)}) collective-permute-start(bf16[1024,128]{1,0:T(8,128)(2,1)S(1)} %get-tuple-element.53), channel_id=1, source_target_pairs={{0,4},{2,6},{4,0},{6,2},{8,12},{10,14},{12,8},{14,10},{1,5},{3,7},... | collective-permute-start | bytes 786440 | tf_op jit(solution)/shard_map/ppermute | solution.py:572
  23.9 21.2 %collective-permute-start.5 = (bf16[1024,128]{1,0:T(8,128)(2,1)S(1)}, bf16[1024,128]{1,0:T(8,128)(2,1)S(1)}, u32[]{:S(2)}, u32[]{:S(2)}) collective-permute-start(bf16[1024,128]{1,0:T(8,128)(2,1)S(1)} %get-tuple-element.54), channel_id=1, source_target_pairs={{0,6},{2,4},{4,2},{6,0},{8,14},{10,12},{12,10},{14,8},{1,7},{3,5},... | collective-permute-start | bytes 786440 | tf_op jit(solution)/shard_map/ppermute | solution.py:572
  24.4 16.7 %collective-permute-start.1 = (bf16[640,128]{1,0:T(8,128)(2,1)S(1)}, bf16[640,128]{1,0:T(8,128)(2,1)S(1)}, u32[]{:S(2)}, u32[]{:S(2)}) collective-permute-start(bf16[640,128]{1,0:T(8,128)(2,1)S(1)} %get-tuple-element.43), channel_id=1, source_target_pairs={{0,8},{2,10},{4,12},{6,14},{8,0},{10,2},{12,4},{14,6},{1,9},{3,11}... | collective-permute-start | bytes 491528 | tf_op jit(solution)/shard_map/ppermute | solution.py:572
  41.2 5.6 %collective-permute-start = (bf16[256,128]{1,0:T(8,128)(2,1)S(1)}, bf16[256,128]{1,0:T(8,128)(2,1)S(1)}, u32[]{:S(2)}, u32[]{:S(2)}) collective-permute-start(bf16[256,128]{1,0:T(8,128)(2,1)S(1)} %shard_map.66.owned_ref), channel_id=1, source_target_pairs={{0,8},{2,10},{4,12},{6,14},{8,0},{10,2},{12,4},{14,6},{1,9},{3,11}... | collective-permute-start | bytes 196616 | tf_op jit(solution)/shard_map/ppermute | solution.py:572
  48.0 20.7 %all-to-all-start.1 = ((bf16[4,1312,128]{2,1,0:T(8,128)(2,1)}), bf16[4,1312,128]{2,1,0:T(8,128)(2,1)S(1)}, u32[]{:S(2)}, u32[]{:S(2)}) async-start(bf16[4,1312,128]{2,1,0:T(8,128)(2,1)} %shard_map.67), calls=%async_computation.1 | async-start | bytes 2686976 | tf_op jit(solution)/shard_map/all_to_all | solution.py:582
  54.3 1.5 %collective-permute-start.6 = (bf16[1024,128]{1,0:T(8,128)(2,1)S(1)}, bf16[1024,128]{1,0:T(8,128)(2,1)S(1)}, u32[]{:S(2)}, u32[]{:S(2)}) collective-permute-start(bf16[1024,128]{1,0:T(8,128)(2,1)S(1)} %get-tuple-element.59.refs_0_), channel_id=1, source_target_pairs={{0,1},{1,0},{2,3},{3,2},{4,5},{5,4},{6,7},{7,6},{8,9},{9,8},{10,11... | collective-permute-start | bytes 786440 | tf_op jit(solution)/shard_map/ppermute | solution.py:572
  54.3 1.9 %collective-permute-start.7 = (bf16[1024,128]{1,0:T(8,128)(2,1)S(1)}, bf16[1024,128]{1,0:T(8,128)(2,1)S(1)}, u32[]{:S(2)}, u32[]{:S(2)}) collective-permute-start(bf16[1024,128]{1,0:T(8,128)(2,1)S(1)} %collective-permute-done.3.refs_1_), channel_id=1, source_target_pairs={{0,1},{1,0},{2,3},{3,2},{4,5},{5,4},{6,7},{7,6},{8,9},{9,8},{10,11... | collective-permute-start | bytes 786440 | tf_op jit(solution)/shard_map/ppermute | solution.py:572
  54.8 1.8 %collective-permute-start.8 = (bf16[1024,128]{1,0:T(8,128)(2,1)S(1)}, bf16[1024,128]{1,0:T(8,128)(2,1)S(1)}, u32[]{:S(2)}, u32[]{:S(2)}) collective-permute-start(bf16[1024,128]{1,0:T(8,128)(2,1)S(1)} %collective-permute-done.4.refs_2_), channel_id=1, source_target_pairs={{0,1},{1,0},{2,3},{3,2},{4,5},{5,4},{6,7},{7,6},{8,9},{9,8},{10,11... | collective-permute-start | bytes 786440 | tf_op jit(solution)/shard_map/ppermute | solution.py:572
  54.8 2.1 %collective-permute-start.9 = (bf16[1024,128]{1,0:T(8,128)(2,1)S(1)}, bf16[1024,128]{1,0:T(8,128)(2,1)S(1)}, u32[]{:S(2)}, u32[]{:S(2)}) collective-permute-start(bf16[1024,128]{1,0:T(8,128)(2,1)S(1)} %collective-permute-done.5.refs_3_), channel_id=1, source_target_pairs={{0,1},{1,0},{2,3},{3,2},{4,5},{5,4},{6,7},{7,6},{8,9},{9,8},{10,11... | collective-permute-start | bytes 786440 | tf_op jit(solution)/shard_map/ppermute | solution.py:572
  68.8 5.3 %collective-permute-start.10 = (bf16[4,512,128]{2,1,0:T(8,128)(2,1)S(1)}, bf16[4,512,128]{2,1,0:T(8,128)(2,1)S(1)}, u32[]{:S(2)}, u32[]{:S(2)}) collective-permute-start(bf16[4,512,128]{2,1,0:T(8,128)(2,1)S(1)} %slice.12), channel_id=1, source_target_pairs={{0,1},{1,0},{2,3},{3,2},{4,5},{5,4},{6,7},{7,6},{8,9},{9,8},{10,11... | collective-permute-start | bytes 1572872 | tf_op jit(solution)/shard_map/ppermute | solution.py:572
  68.9 5.2 %collective-permute-start.11 = (bf16[4,96,128]{2,1,0:T(8,128)(2,1)S(1)}, bf16[4,96,128]{2,1,0:T(8,128)(2,1)S(1)}, u32[]{:S(2)}, u32[]{:S(2)}) collective-permute-start(bf16[4,96,128]{2,1,0:T(8,128)(2,1)S(1)} %slice.13), channel_id=1, source_target_pairs={{0,16},{16,0},{1,17},{17,1},{2,18},{18,2},{3,19},{19,3},{4,20},{20... | collective-permute-start | bytes 294920 | tf_op jit(solution)/shard_map/ppermute | solution.py:572
  76.8 6.2 %collective-permute-start.12 = (bf16[64,512]{1,0:T(8,128)(2,1)S(1)}, bf16[64,512]{1,0:T(8,128)(2,1)S(1)}, u32[]{:S(2)}, u32[]{:S(2)}) collective-permute-start(bf16[64,512]{1,0:T(8,128)(2,1)S(1)} %get-tuple-element.65), channel_id=1, source_target_pairs={{0,8},{2,10},{4,12},{6,14},{8,0},{10,2},{12,4},{14,6},{1,9},{3,11}... | collective-permute-start | bytes 196616 | tf_op jit(solution)/shard_map/ppermute | solution.py:572
  78.0 13.6 %collective-permute-start.13 = (bf16[4,256,128]{2,1,0:T(8,128)(2,1)S(1)}, bf16[4,256,128]{2,1,0:T(8,128)(2,1)S(1)}, u32[]{:S(2)}, u32[]{:S(2)}) collective-permute-start(bf16[4,256,128]{2,1,0:T(8,128)(2,1)S(1)} %get-tuple-element.82.c), channel_id=1, source_target_pairs={{0,16},{16,0},{1,17},{17,1},{2,18},{18,2},{3,19},{19,3},{4,20},{20... | collective-permute-start | bytes 786440 | tf_op jit(solution)/shard_map/ppermute | solution.py:572
  79.5 12.1 %collective-permute-start.14 = (bf16[4,256,128]{2,1,0:T(8,128)(2,1)S(1)}, bf16[4,256,128]{2,1,0:T(8,128)(2,1)S(1)}, u32[]{:S(2)}, u32[]{:S(2)}) collective-permute-start(bf16[4,256,128]{2,1,0:T(8,128)(2,1)S(1)} %get-tuple-element.81.e), channel_id=1, source_target_pairs={{0,16},{16,0},{1,17},{17,1},{2,18},{18,2},{3,19},{19,3},{4,20},{20... | collective-permute-start | bytes 786440 | tf_op jit(solution)/shard_map/ppermute | solution.py:572
  83.1 6.0 %collective-permute-start.16 = (bf16[2,64,512]{2,1,0:T(8,128)(2,1)S(1)}, bf16[2,64,512]{2,1,0:T(8,128)(2,1)S(1)}, u32[]{:S(2)}, u32[]{:S(2)}) collective-permute-start(bf16[2,64,512]{2,1,0:T(8,128)(2,1)S(1)} %get-tuple-element.84), channel_id=1, source_target_pairs={{0,4},{2,6},{4,0},{6,2},{8,12},{10,14},{12,8},{14,10},{1,5},{3,7},... | collective-permute-start | bytes 393224 | tf_op jit(solution)/shard_map/ppermute | solution.py:572
  83.7 6.3 %collective-permute-start.15 = (bf16[2,64,512]{2,1,0:T(8,128)(2,1)S(1)}, bf16[2,64,512]{2,1,0:T(8,128)(2,1)S(1)}, u32[]{:S(2)}, u32[]{:S(2)}) collective-permute-start(bf16[2,64,512]{2,1,0:T(8,128)(2,1)S(1)} %get-tuple-element.84), channel_id=1, source_target_pairs={{0,2},{2,0},{4,6},{6,4},{8,10},{10,8},{12,14},{14,12},{1,3},{3,1},... | collective-permute-start | bytes 393224 | tf_op jit(solution)/shard_map/ppermute | solution.py:572
  84.5 7.1 %collective-permute-start.17 = (bf16[2,64,512]{2,1,0:T(8,128)(2,1)S(1)}, bf16[2,64,512]{2,1,0:T(8,128)(2,1)S(1)}, u32[]{:S(2)}, u32[]{:S(2)}) collective-permute-start(bf16[2,64,512]{2,1,0:T(8,128)(2,1)S(1)} %get-tuple-element.84), channel_id=1, source_target_pairs={{0,6},{2,4},{4,2},{6,0},{8,14},{10,12},{12,10},{14,8},{1,7},{3,5},... | collective-permute-start | bytes 393224 | tf_op jit(solution)/shard_map/ppermute | solution.py:572
  91.7 2.7 %collective-permute-start.18 = (bf16[4,2,64,512]{3,2,1,0:T(8,128)(2,1)S(1)}, bf16[4,2,64,512]{3,2,1,0:T(8,128)(2,1)S(1)}, u32[]{:S(2)}, u32[]{:S(2)}) collective-permute-start(bf16[4,2,64,512]{3,2,1,0:T(8,128)(2,1)S(1)} %pad_maximum_fusion.a), channel_id=1, source_target_pairs={{0,1},{1,0},{2,3},{3,2},{4,5},{5,4},{6,7},{7,6},{8,9},{9,8},{10,11... | collective-permute-start | bytes 1572872 | tf_op jit(solution)/shard_map/ppermute | solution.py:572
  91.8 2.3 %collective-permute-start.19 = (bf16[4,256,128]{2,1,0:T(8,128)(2,1)S(1)}, bf16[4,256,128]{2,1,0:T(8,128)(2,1)S(1)}, u32[]{:S(2)}, u32[]{:S(2)}) collective-permute-start(bf16[4,256,128]{2,1,0:T(8,128)(2,1)S(1)} %get-tuple-element.81.e), channel_id=1, source_target_pairs={{0,1},{1,0},{2,3},{3,2},{4,5},{5,4},{6,7},{7,6},{8,9},{9,8},{10,11... | collective-permute-start | bytes 786440 | tf_op jit(solution)/shard_map/ppermute | solution.py:572
  92.2 2.1 %collective-permute-start.20 = (bf16[4,256,128]{2,1,0:T(8,128)(2,1)S(1)}, bf16[4,256,128]{2,1,0:T(8,128)(2,1)S(1)}, u32[]{:S(2)}, u32[]{:S(2)}) collective-permute-start(bf16[4,256,128]{2,1,0:T(8,128)(2,1)S(1)} %collective-permute-done.14.f), channel_id=1, source_target_pairs={{0,1},{1,0},{2,3},{3,2},{4,5},{5,4},{6,7},{7,6},{8,9},{9,8},{10,11... | collective-permute-start | bytes 786440 | tf_op jit(solution)/shard_map/ppermute | solution.py:572
  99.3 2.0 %collective-permute-start.21 = (bf16[512,512]{1,0:T(8,128)(2,1)S(1)}, bf16[512,512]{1,0:T(8,128)(2,1)S(1)}, u32[]{:S(2)}, u32[]{:S(2)}) collective-permute-start(bf16[512,512]{1,0:T(8,128)(2,1)S(1)} %get-tuple-element.77), channel_id=1, source_target_pairs={{0,1},{1,0},{2,3},{3,2},{4,5},{5,4},{6,7},{7,6},{8,9},{9,8},{10,11... | collective-permute-start | bytes 1572872 | tf_op jit(solution)/shard_map/ppermute | solution.py:572

commit v11 on v9

--- a/solution.py
+++ b/solution.py
@@ -186,6 +186,14 @@
     return device, cut, inner - cut * capacity
 
 
+def as_column(row):
+    count = row.shape[1]
+    same = lax.broadcasted_iota(jnp.int32, (count, count), 0) == lax.broadcasted_iota(
+        jnp.int32, (count, count), 1
+    )
+    return jnp.sum(jnp.where(same, row, 0), axis=1, keepdims=True)
+
+
 def one_hot(mask):
     return mask.astype(F32).astype(BF16)
 
@@ -193,7 +201,7 @@
 def prep_kernel(n, sup, capacity, rank_ref, keep_ref, patches_ref, out_ref):
     rank = rank_ref[0]
     first = rank * sup
-    keep = keep_ref[...]
+    keep = as_column(keep_ref[...])
     rows = 4 * sup
     count = keep.shape[0]
 
@@ -233,7 +241,7 @@
     out_ref[...] = total.astype(BF16)
 
 
-def prep(scalars, keep_col, flat, n, sup, capacity):
+def prep(scalars, keep_list, flat, n, sup, capacity):
     width = flat.shape[1] // 2
     shape = (n * capacity * width // 128, 128)
     return pl.pallas_call(
@@ -242,19 +250,19 @@
             num_scalar_prefetch=1,
             grid=(1,),
             in_specs=[
-                pl.BlockSpec(keep_col.shape, lambda i, ref: (0, 0)),
+                pl.BlockSpec(keep_list.shape, lambda i, ref: (0, 0)),
                 pl.BlockSpec((flat.shape[0], width), lambda i, ref: (0, ref[1])),
             ],
             out_specs=pl.BlockSpec(shape, lambda i, ref: (0, 0)),
         ),
         out_shape=struct(shape),
         compiler_params=params(),
-    )(scalars, keep_col, flat)
+    )(scalars, keep_list, flat)
 
 
 def pick_kernel(n, sup, per_owner, capacity, rank_ref, keep_ref, got_ref, out_ref):
     rank = rank_ref[0]
-    keep = keep_ref[...]
+    keep = as_column(keep_ref[...])
     count = keep.shape[0]
     lanes = got_ref.shape[0]
     cuts = lanes // (n * capacity)
@@ -278,7 +286,7 @@
         out_ref[c * per_owner : (c + 1) * per_owner] = owned
 
 
-def pick(scalars, keep_col, got, n, sup, per_owner, capacity):
+def pick(scalars, keep_list, got, n, sup, per_owner, capacity):
     cuts = got.shape[0] // (n * capacity)
     return pl.pallas_call(
         functools.partial(pick_kernel, n, sup, per_owner, capacity),
@@ -286,7 +294,7 @@
         out_specs=vspec(),
         out_shape=struct((cuts * per_owner, 128)),
         compiler_params=params(),
-    )(scalars, keep_col, got)
+    )(scalars, keep_list, got)
 
 
 def pack_kernel(n, rank_ref, qkv_ref, out_weight_ref, up_ref, down_ref, *refs):
@@ -434,12 +442,12 @@
     )(scalars, mine, other, far)
 
 
-def mlp_kernel(n, rank_ref, tokens_ref, pieces, far, outs_far, near, outs_near, outs, scratch):
-    residual_ref, keep_ref, send_ref = outs
+def mlp_kernel(n, rank_ref, tokens_ref, pieces, far, outs_far, near, outs, scratch):
+    base_ref, terms_ref = outs
     up_ref, down_ref, row_ref, whole_ref, joined_ref, sem = scratch
     rank, half, group = rank_ref[0], rank_ref[1], rank_ref[2]
     block = up_ref.shape[0] // n
-    wide = down_ref.shape[0]
+    wide = down_ref.shape[0] // 2
     unit = wide // 2
     size = pieces[0].shape[2]
     rows = outs_far[0][0].shape[1]
@@ -448,25 +456,25 @@
         source = rank ^ j
         at = pl.ds(pl.multiple_of(source * block, block), block)
         to = pl.ds(pl.multiple_of(source * 128, 128), 128)
-        for c in range(2):
-            later.append(
-                (near[j].at[pl.ds(c * block, block)], up_ref.at[at, pl.ds(c * unit, unit)])
-            )
-        later.append((near[j].at[pl.ds(2 * block, wide)], down_ref.at[:, to]))
         for core in range(2):
-            rows_from = outs_near[core][j].at[pl.ds(2 * block + wide, 2 * rows)]
+            ref = near[core][j]
+            for c in range(2):
+                units = pl.ds(core * wide + c * unit, unit)
+                later.append((ref.at[pl.ds(c * block, block)], up_ref.at[at, units]))
+            units = pl.ds(core * wide, wide)
+            later.append((ref.at[pl.ds(2 * block, wide)], down_ref.at[units, to]))
+            rows_from = ref.at[pl.ds(2 * block + wide, 2 * rows)]
             first.append((rows_from, whole_ref.at[core, :, to]))
         source = source_of(rank, n, j, 1)
         at = pl.ds(pl.multiple_of(source * block, block), block)
         to = pl.ds(pl.multiple_of(source * 128, 128), 128)
-        for c in range(2):
-            units = pl.ds(pl.multiple_of((group ^ c) * unit, unit), unit)
-            later.append((far[c].at[j, pl.ds(0, block)], up_ref.at[at, units]))
-            later.append((far[c].at[j, pl.ds(block, unit)], down_ref.at[units, to]))
         for core in range(2):
             for c in range(2):
-                at = pl.ds(pl.multiple_of((group ^ c) * rows, rows), rows)
-                first.append((outs_far[core][c].at[j], whole_ref.at[core, at, to]))
+                units = pl.ds(pl.multiple_of(core * wide + (group ^ c) * unit, unit), unit)
+                later.append((far[core][c].at[j, pl.ds(0, block)], up_ref.at[at, units]))
+                later.append((far[core][c].at[j, pl.ds(block, unit)], down_ref.at[units, to]))
+                rows_to = pl.ds(pl.multiple_of((group ^ c) * rows, rows), rows)
+                first.append((outs_far[core][c].at[j], whole_ref.at[core, rows_to, to]))
     wait_first = run_copies(first, sem)
     wait_later = run_copies(later, sem, len(first))
     for j in range(n // 2):
@@ -481,68 +489,47 @@
         + lax.dot_general(joined_ref[0], whole_ref[0], dims, preferred_element_type=F32)
         + lax.dot_general(joined_ref[1], whole_ref[1], dims, preferred_element_type=F32)
     )
-    part = residual_ref.shape[0]
-    width = residual_ref.shape[1]
+    part, width = base_ref.shape
     my_cols = pl.ds(pl.multiple_of(half * width, width), width)
-    other_cols = pl.ds(pl.multiple_of((1 - half) * width, width), width)
-    residual_ref[...] = row_ref[pl.ds(pl.multiple_of(rank * part, part), part), my_cols]
+    my_rows = pl.ds(pl.multiple_of(rank * part, part), part)
     normed = norm_rows(row_ref[...]).astype(BF16)
+    base_ref[...] = row_ref[my_rows, my_cols]
     wait_later()
     raw = jnp.dot(normed, up_ref[...], preferred_element_type=F32)
     hidden = (0.5 * raw * (1.0 + lax.erf(raw * math.sqrt(0.5)))).astype(BF16)
-    keep_ref[...] = jnp.dot(hidden, down_ref[:, my_cols], preferred_element_type=F32)
-    send_ref[...] = jnp.dot(hidden, down_ref[:, other_cols], preferred_element_type=F32).astype(BF16)
-
-
-def mlp(scalars, tokens, pieces, far, outs_far, near, near_other, n):
+    row_ref[:, :width] = jnp.dot(hidden, down_ref[:, my_cols], preferred_element_type=F32)
+    base_ref[...] = base_ref[...] + row_ref[my_rows, :width]
+    terms_ref[...] = row_ref[:, :width].astype(BF16)
+
+
+def mlp(scalars, tokens, pieces, far, outs_far, near, n):
     length, depth = tokens.shape
     width = depth // 2
-    wide = 2 * (far[0].shape[1] - depth // n)
+    wide = 2 * (far[0][0].shape[1] - depth // n)
     inner = n * pieces[0].shape[2]
     half = n // 2
 
-    def kernel(scalars, tokens, a, b, c, d, e, f, g, h, *refs):
-        near, other = refs[:half], refs[half : 2 * half]
-        outs, scratch = refs[2 * half : 2 * half + 3], refs[2 * half + 3 :]
-        far, outs_far, outs_near = (c, d), ((e, f), (g, h)), (near, other)
-        mlp_kernel(n, scalars, tokens, (a, b), far, outs_far, near, outs_near, outs, scratch)
+    def kernel(scalars, tokens, a, b, *refs):
+        far, refs = (refs[:2], refs[2:4]), refs[4:]
+        outs_far, refs = (refs[:2], refs[2:4]), refs[4:]
+        near, refs = (refs[:half], refs[half:n]), refs[n:]
+        mlp_kernel(n, scalars, tokens, (a, b), far, outs_far, near, refs[:2], refs[2:])
 
     return pl.pallas_call(
         kernel,
-        in_specs=[sspec()] + [vspec()] * 3 + [aspec()] * (6 + 2 * half),
-        out_specs=[vspec()] * 3,
-        out_shape=[
-            struct((length // n, width), F32),
-            struct((length, width), F32),
-            struct((length, width)),
-        ],
+        in_specs=[sspec()] + [vspec()] * 3 + [aspec()] * (8 + n),
+        out_specs=[vspec()] * 2,
+        out_shape=[struct((length // n, width), F32), struct((length, width))],
         scratch_shapes=[
-            VMEM((depth, wide), BF16),
-            VMEM((wide, depth), BF16),
+            VMEM((depth, 2 * wide), BF16),
+            VMEM((2 * wide, depth), BF16),
             VMEM((length, depth), F32),
             VMEM((2, inner, depth), BF16),
             VMEM((2, inner, length), BF16),
-            pltpu.SemaphoreType.DMA((13 * half,)),
+            pltpu.SemaphoreType.DMA((20 * half,)),
         ],
-        compiler_params=params(20),
-    )(scalars, tokens, *pieces, *far, *outs_far[0], *outs_far[1], *near, *near_other)
-
-
-def join_kernel(rank_ref, keep_ref, got_ref, residual_ref, base_ref, out_ref):
-    part = residual_ref.shape[0]
-    mine = pl.ds(pl.multiple_of(rank_ref[0] * part, part), part)
-    base_ref[...] = keep_ref[mine] + got_ref[mine].astype(F32) + residual_ref[...]
-    out_ref[...] = (keep_ref[...] + got_ref[...].astype(F32)).astype(BF16)
-
-
-def join(scalars, keep, got, residual):
-    return pl.pallas_call(
-        join_kernel,
-        in_specs=[sspec()] + [vspec()] * 3,
-        out_specs=[vspec()] * 2,
-        out_shape=[struct(residual.shape, F32), struct(keep.shape)],
-        compiler_params=params(8),
-    )(scalars, keep, got, residual)
+        compiler_params=params(24),
+    )(scalars, tokens, *pieces, *far[0], *far[1], *outs_far[0], *outs_far[1], *near[0], *near[1])
 
 
 def last_kernel(n, rank_ref, base_ref, terms_ref, out_ref):
@@ -597,17 +584,16 @@
     half_width = depth // 2
     head_rows = qkv_weight.shape[2]
     capacity = (4 * sup + n - 1) // n
-    keep_col = keep_list.reshape(-1, 1)
     flat = patches.reshape(4 * sup, depth)
     heads = qkv_weight.transpose(1, 2, 0)
 
     near, qkv_near, away = pack(scalars, heads, out_weight, up_weight, down_weight, n)
+    slots = prep(scalars, keep_list, flat, n, sup, capacity)
+    dealt = exchange(slots)
+    away, *near = lax.optimization_barrier((away, *near, slots))[:-1]
     far = swap(away, "seq", half)
-    slots = prep(scalars, keep_col, after(flat, away), n, sup, capacity)
-    dealt = exchange(slots)
-    near = lax.optimization_barrier((*near, slots))[:half]
     near = [near[0]] + [swap(near[j], "seq", j) for j in range(1, half)]
-    owned = pick(scalars, keep_col, dealt, n, sup, per_owner, capacity)
+    owned = pick(scalars, keep_list, dealt, n, sup, per_owner, capacity)
     across = swap(owned, "seq", half)
     across, far, *near = lax.optimization_barrier((across, far, *near))
 
@@ -634,18 +620,17 @@
     pairs = [swap(pair, "seq", j) for j in range(1, half)]
     mlp_other, far_other, *pairs = lax.optimization_barrier((mlp_other, far_other, *pairs))
     gathered = jnp.stack([pair] + pairs)
-    residual, keep, send = mlp(
+    mlp_pair = (mlp_mine, mlp_other)
+    far_pair = (far_mine, far_other)
+    base, terms = mlp(
         scalars,
         tokens,
         (gathered, swap(gathered, "head", 1)),
-        (mlp_mine, mlp_other),
-        ((far_mine, far_other), (swap(far_mine, "head", 1), swap(far_other, "head", 1))),
-        near,
-        near_other,
+        (mlp_pair, tuple(swap(value, "head", 1) for value in mlp_pair)),
+        (far_pair, tuple(swap(value, "head", 1) for value in far_pair)),
+        (near, near_other),
         n,
     )
-    sent = swap(send, "head", 1)
-    base, terms = join(scalars, keep, sent, residual)
     terms = exchange(terms.reshape(n, per_owner, half_width))
     encoded = last(scalars, base, terms)
     return encoded.reshape(1, per_owner, 1, half_width)

time: 118 us -> 116 us (0.983)
  starting transfers between devices: 30.9 us -> 29.3 us
    ppermute x21 -> x22, waiting for transfers between devices: 21.8 us -> 18.5 us  [swap(): return lax.ppermute(value, axis, [(i, i ^ j) for i in range(n)])]
    all_to_all x1, waiting for transfers between devices: 13.4 us -> 15.5 us  [exchange(): return lax.all_to_all(value, 'seq', split_axis=0, concat_axis=0, tiled=True)]
    ppermute x21 -> x22, starting transfers between devices: 23.5 us -> 22 us  [swap(): return lax.ppermute(value, axis, [(i, i ^ j) for i in range(n)])]
    unnamed x12, local copies, waits for them, and re-layouts: 3.99 us -> 2.57 us
  transfers between devices with their start and end apart: 23 -> 24, of which waited for: 15 -> 17; matrix products, arithmetic and copies ran while one was open for 0% -> 0% of each run, Pallas kernels for 2% -> 1%
where the time goes in v11:
time: 116 us
  waiting for transfers between devices  48.1 us (41%)
  starting transfers between devices  29.3 us (25%)
  blocking collectives  18.3 us (16%)
  Pallas kernels  15.9 us (14%)
  local copies, waits for them, and re-layouts  3.78 us (3%)
    ppermute x22, starting transfers between devices, swap(): return lax.ppermute(value, axis, [(i, i ^ j) for i in range(n)])  22 us
    ppermute x22, waiting for transfers between devices, swap(): return lax.ppermute(value, axis, [(i, i ^ j) for i in range(n)])  18.5 us
    all_to_all x1, blocking collectives, exchange(): return lax.all_to_all(value, 'seq', split_axis=0, concat_axis=0, tiled=True)  18.3 us
    all_to_all x1, waiting for transfers between devices, exchange(): return lax.all_to_all(value, 'seq', split_axis=0, concat_axis=0, tiled=True)  15.5 us
    all_to_all x1, waiting for transfers between devices, exchange_half(): lax.all_to_all(value, 'seq', split_axis=0, concat_axis=0, axis_index_grou...  14.1 us
    pallas_call x1, Pallas kernels, mlp(): pl.pallas_call(kernel, in_specs=[sspec()] + [vspec()] * 3 + [aspec()] * (...  5.24 us
    all_to_all x1, starting transfers between devices, exchange(): return lax.all_to_all(value, 'seq', split_axis=0, concat_axis=0, tiled=True)  3.81 us
    all_to_all x1, starting transfers between devices, exchange_half(): lax.all_to_all(value, 'seq', split_axis=0, concat_axis=0, axis_index_grou...  3.54 us
  transfers between devices with their start and end apart: 24, of which 17 were waited for; matrix products, arithmetic and copies ran while one was open for 0% of the time, Pallas kernels for 1%

profile of v11, /device:TPU:0, one launch (start us, length us, event | category | flops | bytes accessed | tf_op | source)
XLA Modules:
  0.0 115.7 jit_solution(15927743923121782145)
XLA Ops:
  0.0 1.1 reshape.11.patches_ref
  1.9 2.0 %shard_map.64 = bf16[640,128]{1,0:T(8,128)(2,1)} custom-call(s32[3]{0:T(128)S(1)} %pad_add_fusion.rank_ref.scalars, s32[1,64]{1,0:T(1,128)S(1)} %copy-done.4, bf16[160,1024]{1,0:T(8,128)(2,1)S(1)} %reshape.11.patches_ref), custom_call_target="tpu_custom_call" | custom-call | tf_op jit(solution)/shard_map/pallas_call | solution.py:247
  3.9 1.0 copy-done.2
  4.9 0.9 copy-done.3
  5.8 2.6 %shard_map.66 = (bf16[1024,128]{1,0:T(8,128)(2,1)S(1)}, bf16[1024,128]{1,0:T(8,128)(2,1)}, bf16[1024,128]{1,0:T(8,128)(2,1)}, bf16[1024,128]{1,0:T(8,128)(2,1)S(...) custom-call(s32[3]{0:T(128)S(1)} %pad_add_fusion.rank_ref.scalars, ...), custom_call_target="tpu_custom_call" | custom-call | tf_op jit(solution)/shard_map/pallas_call | solution.py:339
  8.4 4.1 %collective-permute-start.1 = (bf16[1664,128]{1,0:T(8,128)(2,1)S(1)}, bf16[1664,128]{1,0:T(8,128)(2,1)S(1)}, u32[]{:S(2)}, u32[]{:S(2)}) collective-permute-start(bf16[1664,128]{1,0:T(8,128)(2,1)S(1)} %get-tuple-element.42), channel_id=1, source_target_pairs={{0,8},{2,10},{4,12},{6,14},{8,0},{10,2},{12,4},{14,6},{1,9},{3,11}... | collective-permute-start | bytes 1277960 | tf_op jit(solution)/shard_map/ppermute | solution.py:555
  12.5 3.8 %all-to-all-start = ((bf16[8,80,128]{2,1,0:T(8,128)(2,1)}), bf16[8,80,128]{2,1,0:T(8,128)(2,1)S(1)}, u32[]{:S(2)}, u32[]{:S(2)}) async-start(bf16[8,80,128]{2,1,0:T(8,128)(2,1)} %bitcast.3), calls=%async_computation | async-start | bytes 327680 | tf_op jit(solution)/shard_map/all_to_all | solution.py:559
  16.3 2.0 %collective-permute-start.2 = (bf16[1024,128]{1,0:T(8,128)(2,1)}, bf16[1024,128]{1,0:T(8,128)(2,1)S(1)}, u32[]{:S(2)}, u32[]{:S(2)}) collective-permute-start(bf16[1024,128]{1,0:T(8,128)(2,1)} %get-tuple-element.44), channel_id=1, source_target_pairs={{0,2},{2,0},{4,6},{6,4},{8,10},{10,8},{12,14},{14,12},{1,3},{3,1},... | collective-permute-start | bytes 786440 | tf_op jit(solution)/shard_map/ppermute | solution.py:555
  18.4 1.5 %collective-permute-start.3 = (bf16[1024,128]{1,0:T(8,128)(2,1)}, bf16[1024,128]{1,0:T(8,128)(2,1)S(1)}, u32[]{:S(2)}, u32[]{:S(2)}) collective-permute-start(bf16[1024,128]{1,0:T(8,128)(2,1)} %get-tuple-element.45), channel_id=1, source_target_pairs={{0,4},{2,6},{4,0},{6,2},{8,12},{10,14},{12,8},{14,10},{1,5},{3,7},... | collective-permute-start | bytes 786440 | tf_op jit(solution)/shard_map/ppermute | solution.py:555
  19.9 15.5 %all-to-all-done = bf16[8,80,128]{2,1,0:T(8,128)(2,1)S(1)} async-done(((bf16[8,80,128]{2,1,0:T(8,128)(2,1)}), bf16[8,80,128]{2,1,0:T(8,128)(2,1)S(1)}, u32[]{:S(2)}, u32[]{:S(2)}) %all-to-all-start) | async-done | bytes 163872 | tf_op jit(solution)/shard_map/all_to_all | solution.py:559
  35.4 0.9 shard_map.65.owned_ref
  36.3 3.4 %collective-permute-start = (bf16[256,128]{1,0:T(8,128)(2,1)S(1)}, bf16[256,128]{1,0:T(8,128)(2,1)S(1)}, u32[]{:S(2)}, u32[]{:S(2)}) collective-permute-start(bf16[256,128]{1,0:T(8,128)(2,1)S(1)} %shard_map.65.owned_ref), channel_id=1, source_target_pairs={{0,8},{2,10},{4,12},{6,14},{8,0},{10,2},{12,4},{14,6},{1,9},{3,11}... | collective-permute-start | bytes 196616 | tf_op jit(solution)/shard_map/ppermute | solution.py:555
  39.7 2.2 %collective-permute-done.4.refs_11_ = bf16[1024,128]{1,0:T(8,128)(2,1)S(1)} collective-permute-done((bf16[1024,128]{1,0:T(8,128)(2,1)S(1)}, bf16[1024,128]{1,0:T(8,128)(2,1)S(1)}, u32[]{:S(2)}, u32[]{:S(2)}) %collective-permute-start.4) | collective-permute-done | bytes 262176 | tf_op jit(solution)/shard_map/ppermute | solution.py:555
  42.0 0.9 collective-permute-done.across_ref
  42.9 1.2 %shard_map.67 = bf16[4,1312,128]{2,1,0:T(8,128)(2,1)} custom-call(bf16[256,128]{1,0:T(8,128)(2,1)S(1)} %shard_map.65.owned_ref, bf16[256,128]{1,0:T(8,128)(2,1)S(1)} %collective-permute-done.across_ref, bf16[4,192,128]{2,1,0:T(8,128)(2,1)S(1)} %get-tuple-element.48.heads_ref, bf16[1664,128]{1,0:T(8,128)(2,1)S(1)} %collective-permute-done.1.far_ref), custom_call_target="tpu_custom_call" | custom-call | tf_op jit(solution)/shard_map/pallas_call | solution.py:368
  44.1 3.5 %all-to-all-start.1 = ((bf16[4,1312,128]{2,1,0:T(8,128)(2,1)}), bf16[4,1312,128]{2,1,0:T(8,128)(2,1)S(1)}, u32[]{:S(2)}, u32[]{:S(2)}) async-start(bf16[4,1312,128]{2,1,0:T(8,128)(2,1)} %shard_map.67), calls=%async_computation.1 | async-start | bytes 2686976 | tf_op jit(solution)/shard_map/all_to_all | solution.py:565
  50.4 14.1 %all-to-all-done.1.mine_ref = bf16[4,1312,128]{2,1,0:T(8,128)(2,1)S(1)} async-done(((bf16[4,1312,128]{2,1,0:T(8,128)(2,1)}), bf16[4,1312,128]{2,1,0:T(8,128)(2,1)S(1)}, u32[]{:S(2)}, u32[]{:S(2)}) %all-to-all-start.1) | async-done | bytes 1343520 | tf_op jit(solution)/shard_map/all_to_all | solution.py:565
  64.6 1.6 %collective-permute-start.10 = (bf16[4,96,128]{2,1,0:T(8,128)(2,1)S(1)}, bf16[4,96,128]{2,1,0:T(8,128)(2,1)S(1)}, u32[]{:S(2)}, u32[]{:S(2)}) collective-permute-start(bf16[4,96,128]{2,1,0:T(8,128)(2,1)S(1)} %slice.13), channel_id=1, source_target_pairs={{0,16},{16,0},{1,17},{17,1},{2,18},{18,2},{3,19},{19,3},{4,20},{20... | collective-permute-start | bytes 294920 | tf_op jit(solution)/shard_map/ppermute | solution.py:555
  66.2 3.7 %collective-permute-done.10.far_ref = bf16[4,96,128]{2,1,0:T(8,128)(2,1)S(1)} collective-permute-done((bf16[4,96,128]{2,1,0:T(8,128)(2,1)S(1)}, bf16[4,96,128]{2,1,0:T(8,128)(2,1)S(1)}, u32[]{:S(2)}, u32[]{:S(2)}) %collective-permute-start.10) | collective-permute-done | bytes 98336 | tf_op jit(solution)/shard_map/ppermute | solution.py:555
  69.9 2.7 %shard_map.68 = (bf16[512,1024]{1,0:T(8,128)(2,1)S(1)}, bf16[64,512]{1,0:T(8,128)(2,1)S(1)}) custom-call(s32[3]{0:T(128)S(1)} %pad_add_fusion.rank_ref.scalars, bf16[4,1312,128]{2,1,0:T(8,128)(2,1)S(1)} %all-to-all-done.1.mine_ref, bf16[4,512,128]{2,1,0:T(8,128)(2,1)S(1)} %collective-permute-done.9.other_ref, ...), custom_call_target="tpu_custom_call" | custom-call | flops 30000001024 | bytes 1048576 | tf_op jit(solution)/shard_map/pallas_call | solution.py:434
  72.6 1.5 %collective-permute-start.11 = (bf16[64,512]{1,0:T(8,128)(2,1)S(1)}, bf16[64,512]{1,0:T(8,128)(2,1)S(1)}, u32[]{:S(2)}, u32[]{:S(2)}) collective-permute-start(bf16[64,512]{1,0:T(8,128)(2,1)S(1)} %get-tuple-element.56), channel_id=1, source_target_pairs={{0,8},{2,10},{4,12},{6,14},{8,0},{10,2},{12,4},{14,6},{1,9},{3,11}... | collective-permute-start | bytes 196616 | tf_op jit(solution)/shard_map/ppermute | solution.py:555
  74.1 1.6 %collective-permute-start.13 = (bf16[4,256,128]{2,1,0:T(8,128)(2,1)S(1)}, bf16[4,256,128]{2,1,0:T(8,128)(2,1)S(1)}, u32[]{:S(2)}, u32[]{:S(2)}) collective-permute-start(bf16[4,256,128]{2,1,0:T(8,128)(2,1)S(1)} %get-tuple-element.69.refs_4_), channel_id=1, source_target_pairs={{0,16},{16,0},{1,17},{17,1},{2,18},{18,2},{3,19},{19,3},{4,20},{20... | collective-permute-start | bytes 786440 | tf_op jit(solution)/shard_map/ppermute | solution.py:555
  76.2 2.6 %collective-permute-done.11 = bf16[64,512]{1,0:T(8,128)(2,1)S(1)} collective-permute-done((bf16[64,512]{1,0:T(8,128)(2,1)S(1)}, bf16[64,512]{1,0:T(8,128)(2,1)S(1)}, u32[]{:S(2)}, u32[]{:S(2)}) %collective-permute-start.11) | collective-permute-done | bytes 65568 | tf_op jit(solution)/shard_map/ppermute | solution.py:555
  79.4 0.9 collective-permute-start.14
  80.3 2.1 %collective-permute-start.16 = (bf16[2,64,512]{2,1,0:T(8,128)(2,1)S(1)}, bf16[2,64,512]{2,1,0:T(8,128)(2,1)S(1)}, u32[]{:S(2)}, u32[]{:S(2)}) collective-permute-start(bf16[2,64,512]{2,1,0:T(8,128)(2,1)S(1)} %get-tuple-element.72), channel_id=1, source_target_pairs={{0,6},{2,4},{4,2},{6,0},{8,14},{10,12},{12,10},{14,8},{1,7},{3,5},... | collective-permute-start | bytes 393224 | tf_op jit(solution)/shard_map/ppermute | solution.py:555
  82.4 2.5 %collective-permute-done.15 = bf16[2,64,512]{2,1,0:T(8,128)(2,1)S(1)} collective-permute-done((bf16[2,64,512]{2,1,0:T(8,128)(2,1)S(1)}, bf16[2,64,512]{2,1,0:T(8,128)(2,1)S(1)}, u32[]{:S(2)}, u32[]{:S(2)}) %collective-permute-start.15) | collective-permute-done | bytes 131104 | tf_op jit(solution)/shard_map/ppermute | solution.py:555
  84.8 0.9 collective-permute-done.14
  85.7 1.6 %collective-permute-done.16 = bf16[2,64,512]{2,1,0:T(8,128)(2,1)S(1)} collective-permute-done((bf16[2,64,512]{2,1,0:T(8,128)(2,1)S(1)}, bf16[2,64,512]{2,1,0:T(8,128)(2,1)S(1)}, u32[]{:S(2)}, u32[]{:S(2)}) %collective-permute-start.16) | collective-permute-done | bytes 131104 | tf_op jit(solution)/shard_map/ppermute | solution.py:555
  88.6 1.2 %collective-permute-done.20.refs_6_ = bf16[4,256,128]{2,1,0:T(8,128)(2,1)S(1)} collective-permute-done((bf16[4,256,128]{2,1,0:T(8,128)(2,1)S(1)}, bf16[4,256,128]{2,1,0:T(8,128)(2,1)S(1)}, u32[]{:S(2)}, u32[]{:S(2)}) %collective-permute-start.20) | collective-permute-done | bytes 262176 | tf_op jit(solution)/shard_map/ppermute | solution.py:555
  91.0 5.2 %shard_map.69 = (f32[64,512]{1,0:T(8,128)S(1)}, bf16[512,512]{1,0:T(8,128)(2,1)S(1)}) custom-call(s32[3]{0:T(128)S(1)} %pad_add_fusion.rank_ref.scalars, bf16[512,1024]{1,0:T(8,128)(2,1)S(1)} %get-tuple-element.55.tokens, bf16[4,2,64,512]{3,2,1,0:T(8,128)(2,1)S(1)} %pad_maximum_fusion.a, bf16[4,2,64,512]{3,2,1,0:T(8,128)(2,1)S(1)} %collective-permute-done.17.b, ...), custom_call_target="tpu_custom_call" | custom-call | tf_op jit(solution)/shard_map/pallas_call | solution.py:518
  96.2 18.3 %all_to_all.21.terms_ref = bf16[8,64,512]{2,1,0:T(8,128)(2,1)S(1)} all-to-all(bf16[8,64,512]{2,1,0:T(8,128)(2,1)S(1)} %bitcast.16), channel_id=1, replica_groups=mesh['groups'=2,'seq'=8,'head'=2] {'seq'}, dimensions={0} | all-to-all | bytes 1048576 | tf_op jit(solution)/shard_map/all_to_all | solution.py:559
  114.5 1.2 %shard_map.70 = bf16[64,512]{1,0:T(8,128)(2,1)} custom-call(s32[3]{0:T(128)S(1)} %pad_add_fusion.rank_ref.scalars, f32[64,512]{1,0:T(8,128)S(1)} %get-tuple-element.67.base_ref, bf16[8,64,512]{2,1,0:T(8,128)(2,1)S(1)} %all_to_all.21.terms_ref), custom_call_target="tpu_custom_call" | custom-call | tf_op jit(solution)/shard_map/pallas_call | solution.py:544
  (43 shorter events, 7.2 us)
Async XLA Ops:
  0.0 3.9 %copy-start.1 = (bf16[2048,128]{1,0:T(8,128)(2,1)S(1)}, bf16[2048,128]{1,0:T(8,128)(2,1)}, u32[]{:S(2)}) copy-start(bf16[2048,128]{1,0:T(8,128)(2,1)} %down_ref.1) | copy-start | bytes 1572868
  0.0 3.9 %copy-start = (bf16[128,2048]{1,0:T(8,128)(2,1)S(1)}, bf16[128,2048]{1,0:T(8,128)(2,1)}, u32[]{:S(2)}) copy-start(bf16[128,2048]{1,0:T(8,128)(2,1)} %up_ref.1) | copy-start | bytes 1572868
  1.2 0.7 copy-start.4
  1.9 33.5 %copy-start.5 = (s32[1,64]{1,0:T(1,128)S(1)}, s32[1,64]{1,0:T(1,128)}, u32[]{:S(2)}) copy-start(s32[1,64]{1,0:T(1,128)} %keep_ref.3) | copy-start | bytes 772
  3.9 1.0 copy-start.2
  4.9 0.9 copy-start.3
  8.4 34.5 %collective-permute-start.1 = (bf16[1664,128]{1,0:T(8,128)(2,1)S(1)}, bf16[1664,128]{1,0:T(8,128)(2,1)S(1)}, u32[]{:S(2)}, u32[]{:S(2)}) collective-permute-start(bf16[1664,128]{1,0:T(8,128)(2,1)S(1)} %get-tuple-element.42), channel_id=1, source_target_pairs={{0,8},{2,10},{4,12},{6,14},{8,0},{10,2},{12,4},{14,6},{1,9},{3,11}... | collective-permute-start | bytes 1277960 | tf_op jit(solution)/shard_map/ppermute | solution.py:555
  12.5 22.9 %all-to-all-start = ((bf16[8,80,128]{2,1,0:T(8,128)(2,1)}), bf16[8,80,128]{2,1,0:T(8,128)(2,1)S(1)}, u32[]{:S(2)}, u32[]{:S(2)}) async-start(bf16[8,80,128]{2,1,0:T(8,128)(2,1)} %bitcast.3), calls=%async_computation | async-start | bytes 327680 | tf_op jit(solution)/shard_map/all_to_all | solution.py:559
  16.3 23.4 %collective-permute-start.2 = (bf16[1024,128]{1,0:T(8,128)(2,1)}, bf16[1024,128]{1,0:T(8,128)(2,1)S(1)}, u32[]{:S(2)}, u32[]{:S(2)}) collective-permute-start(bf16[1024,128]{1,0:T(8,128)(2,1)} %get-tuple-element.44), channel_id=1, source_target_pairs={{0,2},{2,0},{4,6},{6,4},{8,10},{10,8},{12,14},{14,12},{1,3},{3,1},... | collective-permute-start | bytes 786440 | tf_op jit(solution)/shard_map/ppermute | solution.py:555
  18.4 21.3 %collective-permute-start.3 = (bf16[1024,128]{1,0:T(8,128)(2,1)}, bf16[1024,128]{1,0:T(8,128)(2,1)S(1)}, u32[]{:S(2)}, u32[]{:S(2)}) collective-permute-start(bf16[1024,128]{1,0:T(8,128)(2,1)} %get-tuple-element.45), channel_id=1, source_target_pairs={{0,4},{2,6},{4,0},{6,2},{8,12},{10,14},{12,8},{14,10},{1,5},{3,7},... | collective-permute-start | bytes 786440 | tf_op jit(solution)/shard_map/ppermute | solution.py:555
  19.8 22.1 %collective-permute-start.4 = (bf16[1024,128]{1,0:T(8,128)(2,1)S(1)}, bf16[1024,128]{1,0:T(8,128)(2,1)S(1)}, u32[]{:S(2)}, u32[]{:S(2)}) collective-permute-start(bf16[1024,128]{1,0:T(8,128)(2,1)S(1)} %get-tuple-element.46), channel_id=1, source_target_pairs={{0,6},{2,4},{4,2},{6,0},{8,14},{10,12},{12,10},{14,8},{1,7},{3,5},... | collective-permute-start | bytes 786440 | tf_op jit(solution)/shard_map/ppermute | solution.py:555
  36.3 6.6 %collective-permute-start = (bf16[256,128]{1,0:T(8,128)(2,1)S(1)}, bf16[256,128]{1,0:T(8,128)(2,1)S(1)}, u32[]{:S(2)}, u32[]{:S(2)}) collective-permute-start(bf16[256,128]{1,0:T(8,128)(2,1)S(1)} %shard_map.65.owned_ref), channel_id=1, source_target_pairs={{0,8},{2,10},{4,12},{6,14},{8,0},{10,2},{12,4},{14,6},{1,9},{3,11}... | collective-permute-start | bytes 196616 | tf_op jit(solution)/shard_map/ppermute | solution.py:555
  44.1 20.4 %all-to-all-start.1 = ((bf16[4,1312,128]{2,1,0:T(8,128)(2,1)}), bf16[4,1312,128]{2,1,0:T(8,128)(2,1)S(1)}, u32[]{:S(2)}, u32[]{:S(2)}) async-start(bf16[4,1312,128]{2,1,0:T(8,128)(2,1)} %shard_map.67), calls=%async_computation.1 | async-start | bytes 2686976 | tf_op jit(solution)/shard_map/all_to_all | solution.py:565
  47.7 1.6 %collective-permute-start.5 = (bf16[1024,128]{1,0:T(8,128)(2,1)S(1)}, bf16[1024,128]{1,0:T(8,128)(2,1)S(1)}, u32[]{:S(2)}, u32[]{:S(2)}) collective-permute-start(bf16[1024,128]{1,0:T(8,128)(2,1)S(1)} %get-tuple-element.50.refs_8_), channel_id=1, source_target_pairs={{0,1},{1,0},{2,3},{3,2},{4,5},{5,4},{6,7},{7,6},{8,9},{9,8},{10,11... | collective-permute-start | bytes 786440 | tf_op jit(solution)/shard_map/ppermute | solution.py:555
  47.7 1.9 %collective-permute-start.6 = (bf16[1024,128]{1,0:T(8,128)(2,1)S(1)}, bf16[1024,128]{1,0:T(8,128)(2,1)S(1)}, u32[]{:S(2)}, u32[]{:S(2)}) collective-permute-start(bf16[1024,128]{1,0:T(8,128)(2,1)S(1)} %collective-permute-done.2.refs_9_), channel_id=1, source_target_pairs={{0,1},{1,0},{2,3},{3,2},{4,5},{5,4},{6,7},{7,6},{8,9},{9,8},{10,11... | collective-permute-start | bytes 786440 | tf_op jit(solution)/shard_map/ppermute | solution.py:555
  48.2 1.8 %collective-permute-start.7 = (bf16[1024,128]{1,0:T(8,128)(2,1)S(1)}, bf16[1024,128]{1,0:T(8,128)(2,1)S(1)}, u32[]{:S(2)}, u32[]{:S(2)}) collective-permute-start(bf16[1024,128]{1,0:T(8,128)(2,1)S(1)} %collective-permute-done.3.refs_10_), channel_id=1, source_target_pairs={{0,1},{1,0},{2,3},{3,2},{4,5},{5,4},{6,7},{7,6},{8,9},{9,8},{10,11... | collective-permute-start | bytes 786440 | tf_op jit(solution)/shard_map/ppermute | solution.py:555
  48.3 2.1 %collective-permute-start.8 = (bf16[1024,128]{1,0:T(8,128)(2,1)S(1)}, bf16[1024,128]{1,0:T(8,128)(2,1)S(1)}, u32[]{:S(2)}, u32[]{:S(2)}) collective-permute-start(bf16[1024,128]{1,0:T(8,128)(2,1)S(1)} %collective-permute-done.4.refs_11_), channel_id=1, source_target_pairs={{0,1},{1,0},{2,3},{3,2},{4,5},{5,4},{6,7},{7,6},{8,9},{9,8},{10,11... | collective-permute-start | bytes 786440 | tf_op jit(solution)/shard_map/ppermute | solution.py:555
  64.5 5.3 %collective-permute-start.9 = (bf16[4,512,128]{2,1,0:T(8,128)(2,1)S(1)}, bf16[4,512,128]{2,1,0:T(8,128)(2,1)S(1)}, u32[]{:S(2)}, u32[]{:S(2)}) collective-permute-start(bf16[4,512,128]{2,1,0:T(8,128)(2,1)S(1)} %slice.12), channel_id=1, source_target_pairs={{0,1},{1,0},{2,3},{3,2},{4,5},{5,4},{6,7},{7,6},{8,9},{9,8},{10,11... | collective-permute-start | bytes 1572872 | tf_op jit(solution)/shard_map/ppermute | solution.py:555
  64.6 5.2 %collective-permute-start.10 = (bf16[4,96,128]{2,1,0:T(8,128)(2,1)S(1)}, bf16[4,96,128]{2,1,0:T(8,128)(2,1)S(1)}, u32[]{:S(2)}, u32[]{:S(2)}) collective-permute-start(bf16[4,96,128]{2,1,0:T(8,128)(2,1)S(1)} %slice.13), channel_id=1, source_target_pairs={{0,16},{16,0},{1,17},{17,1},{2,18},{18,2},{3,19},{19,3},{4,20},{20... | collective-permute-start | bytes 294920 | tf_op jit(solution)/shard_map/ppermute | solution.py:555
  72.6 6.2 %collective-permute-start.11 = (bf16[64,512]{1,0:T(8,128)(2,1)S(1)}, bf16[64,512]{1,0:T(8,128)(2,1)S(1)}, u32[]{:S(2)}, u32[]{:S(2)}) collective-permute-start(bf16[64,512]{1,0:T(8,128)(2,1)S(1)} %get-tuple-element.56), channel_id=1, source_target_pairs={{0,8},{2,10},{4,12},{6,14},{8,0},{10,2},{12,4},{14,6},{1,9},{3,11}... | collective-permute-start | bytes 196616 | tf_op jit(solution)/shard_map/ppermute | solution.py:555
  74.1 13.3 %collective-permute-start.13 = (bf16[4,256,128]{2,1,0:T(8,128)(2,1)S(1)}, bf16[4,256,128]{2,1,0:T(8,128)(2,1)S(1)}, u32[]{:S(2)}, u32[]{:S(2)}) collective-permute-start(bf16[4,256,128]{2,1,0:T(8,128)(2,1)S(1)} %get-tuple-element.69.refs_4_), channel_id=1, source_target_pairs={{0,16},{16,0},{1,17},{17,1},{2,18},{18,2},{3,19},{19,3},{4,20},{20... | collective-permute-start | bytes 786440 | tf_op jit(solution)/shard_map/ppermute | solution.py:555
  75.6 11.8 %collective-permute-start.12 = (bf16[4,256,128]{2,1,0:T(8,128)(2,1)S(1)}, bf16[4,256,128]{2,1,0:T(8,128)(2,1)S(1)}, u32[]{:S(2)}, u32[]{:S(2)}) collective-permute-start(bf16[4,256,128]{2,1,0:T(8,128)(2,1)S(1)} %get-tuple-element.70.refs_0_), channel_id=1, source_target_pairs={{0,16},{16,0},{1,17},{17,1},{2,18},{18,2},{3,19},{19,3},{4,20},{20... | collective-permute-start | bytes 786440 | tf_op jit(solution)/shard_map/ppermute | solution.py:555
  78.8 6.0 %collective-permute-start.15 = (bf16[2,64,512]{2,1,0:T(8,128)(2,1)S(1)}, bf16[2,64,512]{2,1,0:T(8,128)(2,1)S(1)}, u32[]{:S(2)}, u32[]{:S(2)}) collective-permute-start(bf16[2,64,512]{2,1,0:T(8,128)(2,1)S(1)} %get-tuple-element.72), channel_id=1, source_target_pairs={{0,4},{2,6},{4,0},{6,2},{8,12},{10,14},{12,8},{14,10},{1,5},{3,7},... | collective-permute-start | bytes 393224 | tf_op jit(solution)/shard_map/ppermute | solution.py:555
  79.4 6.3 %collective-permute-start.14 = (bf16[2,64,512]{2,1,0:T(8,128)(2,1)S(1)}, bf16[2,64,512]{2,1,0:T(8,128)(2,1)S(1)}, u32[]{:S(2)}, u32[]{:S(2)}) collective-permute-start(bf16[2,64,512]{2,1,0:T(8,128)(2,1)S(1)} %get-tuple-element.72), channel_id=1, source_target_pairs={{0,2},{2,0},{4,6},{6,4},{8,10},{10,8},{12,14},{14,12},{1,3},{3,1},... | collective-permute-start | bytes 393224 | tf_op jit(solution)/shard_map/ppermute | solution.py:555
  80.3 7.1 %collective-permute-start.16 = (bf16[2,64,512]{2,1,0:T(8,128)(2,1)S(1)}, bf16[2,64,512]{2,1,0:T(8,128)(2,1)S(1)}, u32[]{:S(2)}, u32[]{:S(2)}) collective-permute-start(bf16[2,64,512]{2,1,0:T(8,128)(2,1)S(1)} %get-tuple-element.72), channel_id=1, source_target_pairs={{0,6},{2,4},{4,2},{6,0},{8,14},{10,12},{12,10},{14,8},{1,7},{3,5},... | collective-permute-start | bytes 393224 | tf_op jit(solution)/shard_map/ppermute | solution.py:555
  87.5 3.5 %collective-permute-start.17 = (bf16[4,2,64,512]{3,2,1,0:T(8,128)(2,1)S(1)}, bf16[4,2,64,512]{3,2,1,0:T(8,128)(2,1)S(1)}, u32[]{:S(2)}, u32[]{:S(2)}) collective-permute-start(bf16[4,2,64,512]{3,2,1,0:T(8,128)(2,1)S(1)} %pad_maximum_fusion.a), channel_id=1, source_target_pairs={{0,1},{1,0},{2,3},{3,2},{4,5},{5,4},{6,7},{7,6},{8,9},{9,8},{10,11... | collective-permute-start | bytes 1572872 | tf_op jit(solution)/shard_map/ppermute | solution.py:555
  87.6 2.3 %collective-permute-start.20 = (bf16[4,256,128]{2,1,0:T(8,128)(2,1)S(1)}, bf16[4,256,128]{2,1,0:T(8,128)(2,1)S(1)}, u32[]{:S(2)}, u32[]{:S(2)}) collective-permute-start(bf16[4,256,128]{2,1,0:T(8,128)(2,1)S(1)} %get-tuple-element.69.refs_4_), channel_id=1, source_target_pairs={{0,1},{1,0},{2,3},{3,2},{4,5},{5,4},{6,7},{7,6},{8,9},{9,8},{10,11... | collective-permute-start | bytes 786440 | tf_op jit(solution)/shard_map/ppermute | solution.py:555
  88.1 2.1 %collective-permute-start.18 = (bf16[4,256,128]{2,1,0:T(8,128)(2,1)S(1)}, bf16[4,256,128]{2,1,0:T(8,128)(2,1)S(1)}, u32[]{:S(2)}, u32[]{:S(2)}) collective-permute-start(bf16[4,256,128]{2,1,0:T(8,128)(2,1)S(1)} %get-tuple-element.70.refs_0_), channel_id=1, source_target_pairs={{0,1},{1,0},{2,3},{3,2},{4,5},{5,4},{6,7},{7,6},{8,9},{9,8},{10,11... | collective-permute-start | bytes 786440 | tf_op jit(solution)/shard_map/ppermute | solution.py:555
  88.1 2.4 %collective-permute-start.19 = (bf16[4,256,128]{2,1,0:T(8,128)(2,1)S(1)}, bf16[4,256,128]{2,1,0:T(8,128)(2,1)S(1)}, u32[]{:S(2)}, u32[]{:S(2)}) collective-permute-start(bf16[4,256,128]{2,1,0:T(8,128)(2,1)S(1)} %collective-permute-done.12.refs_1_), channel_id=1, source_target_pairs={{0,1},{1,0},{2,3},{3,2},{4,5},{5,4},{6,7},{7,6},{8,9},{9,8},{10,11... | collective-permute-start | bytes 786440 | tf_op jit(solution)/shard_map/ppermute | solution.py:555
  88.6 2.4 %collective-permute-start.21 = (bf16[4,256,128]{2,1,0:T(8,128)(2,1)S(1)}, bf16[4,256,128]{2,1,0:T(8,128)(2,1)S(1)}, u32[]{:S(2)}, u32[]{:S(2)}) collective-permute-start(bf16[4,256,128]{2,1,0:T(8,128)(2,1)S(1)} %collective-permute-done.13.refs_5_), channel_id=1, source_target_pairs={{0,1},{1,0},{2,3},{3,2},{4,5},{5,4},{6,7},{7,6},{8,9},{9,8},{10,11... | collective-permute-start | bytes 786440 | tf_op jit(solution)/shard_map/ppermute | solution.py:555

commit v12 on v11

--- a/solution.py
+++ b/solution.py
@@ -297,14 +297,13 @@
     )(scalars, keep_list, got)
 
 
-def pack_kernel(n, rank_ref, qkv_ref, out_weight_ref, up_ref, down_ref, *refs):
-    near, (heads_ref, away_ref, sem) = refs[: n // 2], refs[n // 2 :]
+def far_kernel(n, rank_ref, qkv_ref, out_weight_ref, up_ref, down_ref, away_ref, sem):
     rank, part = rank_ref[0], rank_ref[2]
     half = n // 2
     rows = up_ref.shape[0]
     wide = up_ref.shape[1] // n
     units = wide // 2
-    long = out_weight_ref.shape[0]
+    long = out_weight_ref.shape[0] // 2
     depth = qkv_ref.shape[1] // 2
     each = depth + rows + units
     copies = []
@@ -316,9 +315,20 @@
         at = pl.ds(pl.multiple_of(dest * wide + part * units, 128), units)
         copies.append((up_ref.at[:, at], away_ref.at[pl.ds(low + depth, rows)]))
         copies.append((down_ref.at[at], away_ref.at[pl.ds(low + depth + rows, units)]))
-    at = pl.ds(pl.multiple_of(part * (long // 2), 128), long // 2)
-    copies.append((out_weight_ref.at[at], away_ref.at[pl.ds(half * each, long // 2)]))
-    copies.append((qkv_ref.at[pl.ds(rank // half * half, half)], heads_ref))
+    at = pl.ds(pl.multiple_of(part * long, 128), long)
+    copies.append((out_weight_ref.at[at], away_ref.at[pl.ds(half * each, long)]))
+    run_copies(copies, sem)()
+
+
+def near_kernel(n, rank_ref, qkv_ref, out_weight_ref, up_ref, down_ref, *refs):
+    near, (heads_ref, sem) = refs[: n // 2], refs[n // 2 :]
+    rank = rank_ref[0]
+    half = n // 2
+    rows = up_ref.shape[0]
+    wide = up_ref.shape[1] // n
+    units = wide // 2
+    long = out_weight_ref.shape[0]
+    copies = [(qkv_ref.at[pl.ds(rank // half * half, half)], heads_ref)]
     for j in range(half):
         dest = rank ^ j
         for c in range(2):
@@ -330,21 +340,31 @@
     run_copies(copies, sem)()
 
 
-def pack(scalars, qkv, out_weight, up, down, n):
+def pack(kernel, shapes, count, scalars, *weights):
+    return pl.pallas_call(
+        kernel,
+        in_specs=[sspec()] + [hspec()] * 4,
+        out_specs=[aspec()] * len(shapes),
+        out_shape=[struct(shape) for shape in shapes],
+        scratch_shapes=[pltpu.SemaphoreType.DMA((count,))],
+    )(scalars, *weights)
+
+
+def pack_far(scalars, qkv, out_weight, up, down, n):
     half = n // 2
-    wide = up.shape[1] // n
-    near = struct((2 * up.shape[0] + wide + out_weight.shape[0], 128))
-    each = qkv.shape[1] // 2 + up.shape[0] + wide // 2
-    away = struct((half * each + out_weight.shape[0] // 2, 128))
-    outs = pl.pallas_call(
-        functools.partial(pack_kernel, n),
-        in_specs=[sspec()] + [hspec()] * 4,
-        out_specs=[aspec()] * (half + 2),
-        out_shape=[near] * half + [struct((half,) + qkv.shape[1:]), away],
-        scratch_shapes=[pltpu.SemaphoreType.DMA((7 * half + 2,))],
-        compiler_params=params(),
-    )(scalars, qkv, out_weight, up, down)
-    return list(outs[:half]), outs[half], outs[half + 1]
+    each = qkv.shape[1] // 2 + up.shape[0] + up.shape[1] // n // 2
+    shapes = [(half * each + out_weight.shape[0] // 2, 128)]
+    kernel = functools.partial(far_kernel, n)
+    return pack(kernel, shapes, 3 * half + 1, scalars, qkv, out_weight, up, down)[0]
+
+
+def pack_near(scalars, qkv, out_weight, up, down, n):
+    half = n // 2
+    near = (2 * up.shape[0] + up.shape[1] // n + out_weight.shape[0], 128)
+    shapes = [near] * half + [(half,) + qkv.shape[1:]]
+    kernel = functools.partial(near_kernel, n)
+    outs = pack(kernel, shapes, 4 * half + 1, scalars, qkv, out_weight, up, down)
+    return list(outs[:half]), outs[half]
 
 
 def fan_kernel(owned_ref, across_ref, heads_ref, far_ref, out_ref):
@@ -443,7 +463,7 @@
 
 
 def mlp_kernel(n, rank_ref, tokens_ref, pieces, far, outs_far, near, outs, scratch):
-    base_ref, terms_ref = outs
+    base_ref, away_ref, sends = outs[0], outs[1], outs[2:]
     up_ref, down_ref, row_ref, whole_ref, joined_ref, sem = scratch
     rank, half, group = rank_ref[0], rank_ref[1], rank_ref[2]
     block = up_ref.shape[0] // n
@@ -499,7 +519,14 @@
     hidden = (0.5 * raw * (1.0 + lax.erf(raw * math.sqrt(0.5)))).astype(BF16)
     row_ref[:, :width] = jnp.dot(hidden, down_ref[:, my_cols], preferred_element_type=F32)
     base_ref[...] = base_ref[...] + row_ref[my_rows, :width]
-    terms_ref[...] = row_ref[:, :width].astype(BF16)
+    for j in range(n // 2):
+        for k in range(2):
+            owner = rank ^ j ^ (k * n // 2)
+            term = row_ref[pl.ds(pl.multiple_of(owner * part, part), part), :width]
+            if j > 0:
+                sends[j - 1][k] = term.astype(BF16)
+            elif k == 1:
+                away_ref[...] = term
 
 
 def mlp(scalars, tokens, pieces, far, outs_far, near, n):
@@ -513,13 +540,14 @@
         far, refs = (refs[:2], refs[2:4]), refs[4:]
         outs_far, refs = (refs[:2], refs[2:4]), refs[4:]
         near, refs = (refs[:half], refs[half:n]), refs[n:]
-        mlp_kernel(n, scalars, tokens, (a, b), far, outs_far, near, refs[:2], refs[2:])
+        mlp_kernel(n, scalars, tokens, (a, b), far, outs_far, near, refs[: half + 1], refs[half + 1 :])
 
     return pl.pallas_call(
         kernel,
         in_specs=[sspec()] + [vspec()] * 3 + [aspec()] * (8 + n),
-        out_specs=[vspec()] * 2,
-        out_shape=[struct((length // n, width), F32), struct((length, width))],
+        out_specs=[vspec()] * (half + 1),
+        out_shape=[struct((length // n, width), F32)] * 2
+        + [struct((2, length // n, width))] * (half - 1),
         scratch_shapes=[
             VMEM((depth, 2 * wide), BF16),
             VMEM((2 * wide, depth), BF16),
@@ -532,22 +560,38 @@
     )(scalars, tokens, *pieces, *far[0], *far[1], *outs_far[0], *outs_far[1], *near[0], *near[1])
 
 
-def last_kernel(n, rank_ref, base_ref, terms_ref, out_ref):
-    rank = rank_ref[0]
-    total = base_ref[...]
-    for j in range(1, n):
-        total = total + terms_ref[rank ^ j].astype(F32)
-    out_ref[...] = total.astype(BF16)
-
-
-def last(scalars, base, terms):
+def sum_kernel(base_ref, away_ref, *refs):
+    terms, (base_out, away_out) = refs[:-2], refs[-2:]
+    base, away = base_ref[...], away_ref[...]
+    for ref in terms:
+        base = base + ref[0].astype(F32)
+        away = away + ref[1].astype(F32)
+    base_out[...] = base
+    away_out[...] = away.astype(BF16)
+
+
+def sum_terms(base, away, terms):
     return pl.pallas_call(
-        functools.partial(last_kernel, terms.shape[0]),
-        in_specs=[sspec()] + [vspec()] * 2,
+        sum_kernel,
+        in_specs=[vspec()] * (2 + len(terms)),
+        out_specs=[vspec()] * 2,
+        out_shape=[struct(base.shape, F32), struct(away.shape)],
+        compiler_params=params(),
+    )(base, away, *terms)
+
+
+def last_kernel(base_ref, across_ref, out_ref):
+    out_ref[...] = (base_ref[...] + across_ref[...].astype(F32)).astype(BF16)
+
+
+def last(base, across):
+    return pl.pallas_call(
+        last_kernel,
+        in_specs=[vspec()] * 2,
         out_specs=vspec(),
         out_shape=struct(base.shape),
-        compiler_params=params(8),
-    )(scalars, base, terms)
+        compiler_params=params(),
+    )(base, across)
 
 
 def swap(value, axis, j):
@@ -587,11 +631,13 @@
     flat = patches.reshape(4 * sup, depth)
     heads = qkv_weight.transpose(1, 2, 0)
 
-    near, qkv_near, away = pack(scalars, heads, out_weight, up_weight, down_weight, n)
-    slots = prep(scalars, keep_list, flat, n, sup, capacity)
+    weights = (heads, out_weight, up_weight, down_weight)
+    away = pack_far(scalars, *weights, n)
+    far = swap(away, "seq", half)
+    slots = prep(scalars, keep_list, after(flat, away), n, sup, capacity)
     dealt = exchange(slots)
-    away, *near = lax.optimization_barrier((away, *near, slots))[:-1]
-    far = swap(away, "seq", half)
+    weights = lax.optimization_barrier((*weights, slots))[:4]
+    near, qkv_near = pack_near(scalars, *weights, n)
     near = [near[0]] + [swap(near[j], "seq", j) for j in range(1, half)]
     owned = pick(scalars, keep_list, dealt, n, sup, per_owner, capacity)
     across = swap(owned, "seq", half)
@@ -622,7 +668,7 @@
     gathered = jnp.stack([pair] + pairs)
     mlp_pair = (mlp_mine, mlp_other)
     far_pair = (far_mine, far_other)
-    base, terms = mlp(
+    base, term_away, *terms = mlp(
         scalars,
         tokens,
         (gathered, swap(gathered, "head", 1)),
@@ -631,8 +677,9 @@
         (near, near_other),
         n,
     )
-    terms = exchange(terms.reshape(n, per_owner, half_width))
-    encoded = last(scalars, base, terms)
+    terms = [swap(terms[j - 1], "seq", j) for j in range(1, half)]
+    base, term_away = sum_terms(base, term_away, terms)
+    encoded = last(base, swap(term_away, "seq", half))
     return encoded.reshape(1, per_owner, 1, half_width)
 
 

time: 116 us -> 151 us (1.30)
  Pallas kernels: 15.9 us -> 67.4 us
  blocking collectives: 18.3 us -> 0 us
  starting transfers between devices: 29.3 us -> 34.9 us
  local copies, waits for them, and re-layouts: 3.78 us -> 1.1 us
  waiting for transfers between devices: 48.1 us -> 46.3 us
    pallas_call x2 -> x4, Pallas kernels: 3.88 us -> 55.3 us  [the longest x2 54.6 us: pack(): pl.pallas_call(kernel, in_specs=[sspec()] + [hspec()] * 4, out_specs=[asp...]
    all_to_all x1 -> x0, blocking collectives: 18.3 us -> none  [exchange(): return lax.all_to_all(value, 'seq', split_axis=0, concat_axis=0, tiled=True)]
    all_to_all x1, waiting for transfers between devices: 15.5 us -> 0.01 us  [exchange(): return lax.all_to_all(value, 'seq', split_axis=0, concat_axis=0, tiled=True)]
    ppermute x22 -> x26, waiting for transfers between devices: 18.5 us -> 33.5 us  [swap(): return lax.ppermute(value, axis, [(i, i ^ j) for i in range(n)])]
    ppermute x22 -> x26, starting transfers between devices: 22 us -> 27.1 us  [swap(): return lax.ppermute(value, axis, [(i, i ^ j) for i in range(n)])]
    unnamed x12, local copies, waits for them, and re-layouts: 2.57 us -> 0.95 us
  transfers between devices with their start and end apart: 24 -> 28, of which waited for: 17 -> 22; matrix products, arithmetic and copies ran while one was open for 0% -> 0% of each run, Pallas kernels for 1% -> 28%
where the time goes in v12:
time: 151 us
  Pallas kernels  67.4 us (45%)
  waiting for transfers between devices  46.3 us (31%)
  starting transfers between devices  34.9 us (23%)
    pallas_call x2, Pallas kernels, pack(): pl.pallas_call(kernel, in_specs=[sspec()] + [hspec()] * 4, out_specs=[asp...  54.6 us
    ppermute x26, waiting for transfers between devices, swap(): return lax.ppermute(value, axis, [(i, i ^ j) for i in range(n)])  33.5 us
    ppermute x26, starting transfers between devices, swap(): return lax.ppermute(value, axis, [(i, i ^ j) for i in range(n)])  27.1 us
    all_to_all x1, waiting for transfers between devices, exchange_half(): lax.all_to_all(value, 'seq', split_axis=0, concat_axis=0, axis_index_grou...  12.9 us
    pallas_call x1, Pallas kernels, mlp(): pl.pallas_call(kernel, in_specs=[sspec()] + [vspec()] * 3 + [aspec()] * (...  5.28 us
    all_to_all x1, starting transfers between devices, exchange_half(): lax.all_to_all(value, 'seq', split_axis=0, concat_axis=0, axis_index_grou...  3.97 us
    all_to_all x1, starting transfers between devices, exchange(): return lax.all_to_all(value, 'seq', split_axis=0, concat_axis=0, tiled=True)  3.81 us
  transfers between devices with their start and end apart: 28, of which 22 were waited for; matrix products, arithmetic and copies ran while one was open for 0% of the time, Pallas kernels for 28%

profile of v12, /device:TPU:0, one launch (start us, length us, event | category | flops | bytes accessed | tf_op | source)
XLA Modules:
  0.0 150.6 jit_solution(8036122181880182306)
XLA Ops:
  0.7 14.9 %shard_map.64 = bf16[1664,128]{1,0:T(8,128)(2,1)} custom-call(s32[3]{0:T(128)} %pad_add_fusion.rank_ref.scalars, bf16[8,192,128]{2,1,0:T(8,128)(2,1)} %bitcast.16, bf16[512,128]{1,0:T(8,128)(2,1)} %out_weight_ref.2, bf16[128,2048]{1,0:T(8,128)(2,1)} %up_ref.2, bf16[2048,128]{1,0:T(8,128)(2,1)} %down_ref.2), custom_call_target="tpu_custom_call" | custom-call | tf_op jit(solution)/shard_map/pallas_call | solution.py:344
  15.6 4.1 %collective-permute-start.1 = (bf16[1664,128]{1,0:T(8,128)(2,1)}, bf16[1664,128]{1,0:T(8,128)(2,1)S(1)}, u32[]{:S(2)}, u32[]{:S(2)}) collective-permute-start(bf16[1664,128]{1,0:T(8,128)(2,1)} %shard_map.64), channel_id=1, source_target_pairs={{0,8},{2,10},{4,12},{6,14},{8,0},{10,2},{12,4},{14,6},{1,9},{3,11}... | collective-permute-start | bytes 1277960 | tf_op jit(solution)/shard_map/ppermute | solution.py:599
  19.8 2.0 %shard_map.65 = bf16[640,128]{1,0:T(8,128)(2,1)} custom-call(s32[3]{0:T(128)S(1)} %copy-done.2, s32[1,64]{1,0:T(1,128)S(1)} %copy-done.4, bf16[160,1024]{1,0:T(8,128)(2,1)S(1)} %reshape.8.patches_ref), custom_call_target="tpu_custom_call" | custom-call | tf_op jit(solution)/shard_map/pallas_call | solution.py:247
  21.8 3.8 %all-to-all-start = ((bf16[8,80,128]{2,1,0:T(8,128)(2,1)}), bf16[8,80,128]{2,1,0:T(8,128)(2,1)S(1)}, u32[]{:S(2)}, u32[]{:S(2)}) async-start(bf16[8,80,128]{2,1,0:T(8,128)(2,1)} %bitcast.4), calls=%async_computation | async-start | bytes 327680 | tf_op jit(solution)/shard_map/all_to_all | solution.py:603
  25.6 39.6 %shard_map.67 = (bf16[1024,128]{1,0:T(8,128)(2,1)}, bf16[1024,128]{1,0:T(8,128)(2,1)}, bf16[1024,128]{1,0:T(8,128)(2,1)}, bf16[1024,128]{1,0:T(8,128)(2,1)}, bf16[4,192,128]{2,1,0:T(8,128)(2,1)}) custom-call(s32[3]{0:T(128)} %pad_add_fusion.rank_ref.scalars, bf16[8,192,128]{2,1,0:T(8,128)(2,1)} %bitcast.17, bf16[512,128]{1,0:T(8,128)(2,1)} %out_weight_ref.2, ...), custom_call_target="tpu_custom_call" | custom-call | tf_op jit(solution)/shard_map/pallas_call | solution.py:344
  65.3 2.1 %collective-permute-start.2 = (bf16[1024,128]{1,0:T(8,128)(2,1)}, bf16[1024,128]{1,0:T(8,128)(2,1)S(1)}, u32[]{:S(2)}, u32[]{:S(2)}) collective-permute-start(bf16[1024,128]{1,0:T(8,128)(2,1)} %get-tuple-element.47), channel_id=1, source_target_pairs={{0,2},{2,0},{4,6},{6,4},{8,10},{10,8},{12,14},{14,12},{1,3},{3,1},... | collective-permute-start | bytes 786440 | tf_op jit(solution)/shard_map/ppermute | solution.py:599
  67.4 1.5 collective-permute-start.3
  69.8 2.9 %collective-permute-start = (bf16[256,128]{1,0:T(8,128)(2,1)S(1)}, bf16[256,128]{1,0:T(8,128)(2,1)S(1)}, u32[]{:S(2)}, u32[]{:S(2)}) collective-permute-start(bf16[256,128]{1,0:T(8,128)(2,1)S(1)} %shard_map.66.owned_ref), channel_id=1, source_target_pairs={{0,8},{2,10},{4,12},{6,14},{8,0},{10,2},{12,4},{14,6},{1,9},{3,11}... | collective-permute-start | bytes 196616 | tf_op jit(solution)/shard_map/ppermute | solution.py:599
  73.4 4.8 %collective-permute-done.3.refs_10_ = bf16[1024,128]{1,0:T(8,128)(2,1)S(1)} collective-permute-done((bf16[1024,128]{1,0:T(8,128)(2,1)}, bf16[1024,128]{1,0:T(8,128)(2,1)S(1)}, u32[]{:S(2)}, u32[]{:S(2)}) %collective-permute-start.3) | collective-permute-done | bytes 262176 | tf_op jit(solution)/shard_map/ppermute | solution.py:599
  78.2 3.1 %collective-permute-done.4.refs_11_ = bf16[1024,128]{1,0:T(8,128)(2,1)S(1)} collective-permute-done((bf16[1024,128]{1,0:T(8,128)(2,1)}, bf16[1024,128]{1,0:T(8,128)(2,1)S(1)}, u32[]{:S(2)}, u32[]{:S(2)}) %collective-permute-start.4) | collective-permute-done | bytes 262176 | tf_op jit(solution)/shard_map/ppermute | solution.py:599
  81.3 0.9 copy-done.1
  82.3 1.2 shard_map.68
  83.5 4.0 %all-to-all-start.1 = ((bf16[4,1312,128]{2,1,0:T(8,128)(2,1)}), bf16[4,1312,128]{2,1,0:T(8,128)(2,1)S(1)}, u32[]{:S(2)}, u32[]{:S(2)}) async-start(bf16[4,1312,128]{2,1,0:T(8,128)(2,1)} %shard_map.68), calls=%async_computation.1 | async-start | bytes 2686976 | tf_op jit(solution)/shard_map/all_to_all | solution.py:609
  90.1 12.9 %all-to-all-done.1.mine_ref = bf16[4,1312,128]{2,1,0:T(8,128)(2,1)S(1)} async-done(((bf16[4,1312,128]{2,1,0:T(8,128)(2,1)}), bf16[4,1312,128]{2,1,0:T(8,128)(2,1)S(1)}, u32[]{:S(2)}, u32[]{:S(2)}) %all-to-all-start.1) | async-done | bytes 1343520 | tf_op jit(solution)/shard_map/all_to_all | solution.py:609
  103.2 1.6 %collective-permute-start.10 = (bf16[4,96,128]{2,1,0:T(8,128)(2,1)S(1)}, bf16[4,96,128]{2,1,0:T(8,128)(2,1)S(1)}, u32[]{:S(2)}, u32[]{:S(2)}) collective-permute-start(bf16[4,96,128]{2,1,0:T(8,128)(2,1)S(1)} %slice.13), channel_id=1, source_target_pairs={{0,16},{16,0},{1,17},{17,1},{2,18},{18,2},{3,19},{19,3},{4,20},{20... | collective-permute-start | bytes 294920 | tf_op jit(solution)/shard_map/ppermute | solution.py:599
  104.7 3.7 %collective-permute-done.10.far_ref = bf16[4,96,128]{2,1,0:T(8,128)(2,1)S(1)} collective-permute-done((bf16[4,96,128]{2,1,0:T(8,128)(2,1)S(1)}, bf16[4,96,128]{2,1,0:T(8,128)(2,1)S(1)}, u32[]{:S(2)}, u32[]{:S(2)}) %collective-permute-start.10) | collective-permute-done | bytes 98336 | tf_op jit(solution)/shard_map/ppermute | solution.py:599
  108.4 2.7 %shard_map.69 = (bf16[512,1024]{1,0:T(8,128)(2,1)S(1)}, bf16[64,512]{1,0:T(8,128)(2,1)S(1)}) custom-call(s32[3]{0:T(128)S(1)} %copy-done.3, bf16[4,1312,128]{2,1,0:T(8,128)(2,1)S(1)} %all-to-all-done.1.mine_ref, bf16[4,512,128]{2,1,0:T(8,128)(2,1)S(1)} %collective-permute-done.9.other_ref, bf16[4,96,128]{2,1,0:T(8,128)(2,1)S(1)} %collective-permute-done.10.far_ref), custom_call_target="tpu_custom_call" | custom-call | flops 30000001024 | bytes 1048576 | tf_op jit(solution)/shard_map/pallas_call | solution.py:454
  111.1 1.8 %collective-permute-start.11 = (bf16[64,512]{1,0:T(8,128)(2,1)S(1)}, bf16[64,512]{1,0:T(8,128)(2,1)S(1)}, u32[]{:S(2)}, u32[]{:S(2)}) collective-permute-start(bf16[64,512]{1,0:T(8,128)(2,1)S(1)} %get-tuple-element.59), channel_id=1, source_target_pairs={{0,8},{2,10},{4,12},{6,14},{8,0},{10,2},{12,4},{14,6},{1,9},{3,11}... | collective-permute-start | bytes 196616 | tf_op jit(solution)/shard_map/ppermute | solution.py:599
  112.9 1.6 %collective-permute-start.13 = (bf16[4,256,128]{2,1,0:T(8,128)(2,1)S(1)}, bf16[4,256,128]{2,1,0:T(8,128)(2,1)S(1)}, u32[]{:S(2)}, u32[]{:S(2)}) collective-permute-start(bf16[4,256,128]{2,1,0:T(8,128)(2,1)S(1)} %get-tuple-element.77.refs_4_), channel_id=1, source_target_pairs={{0,16},{16,0},{1,17},{17,1},{2,18},{18,2},{3,19},{19,3},{4,20},{20... | collective-permute-start | bytes 786440 | tf_op jit(solution)/shard_map/ppermute | solution.py:599
  115.0 2.1 %collective-permute-done.11 = bf16[64,512]{1,0:T(8,128)(2,1)S(1)} collective-permute-done((bf16[64,512]{1,0:T(8,128)(2,1)S(1)}, bf16[64,512]{1,0:T(8,128)(2,1)S(1)}, u32[]{:S(2)}, u32[]{:S(2)}) %collective-permute-start.11) | collective-permute-done | bytes 65568 | tf_op jit(solution)/shard_map/ppermute | solution.py:599
  118.2 2.5 %collective-permute-start.16 = (bf16[2,64,512]{2,1,0:T(8,128)(2,1)S(1)}, bf16[2,64,512]{2,1,0:T(8,128)(2,1)S(1)}, u32[]{:S(2)}, u32[]{:S(2)}) collective-permute-start(bf16[2,64,512]{2,1,0:T(8,128)(2,1)S(1)} %get-tuple-element.80), channel_id=1, source_target_pairs={{0,6},{2,4},{4,2},{6,0},{8,14},{10,12},{12,10},{14,8},{1,7},{3,5},... | collective-permute-start | bytes 393224 | tf_op jit(solution)/shard_map/ppermute | solution.py:599
  120.8 2.1 %collective-permute-done.15 = bf16[2,64,512]{2,1,0:T(8,128)(2,1)S(1)} collective-permute-done((bf16[2,64,512]{2,1,0:T(8,128)(2,1)S(1)}, bf16[2,64,512]{2,1,0:T(8,128)(2,1)S(1)}, u32[]{:S(2)}, u32[]{:S(2)}) %collective-permute-start.15) | collective-permute-done | bytes 131104 | tf_op jit(solution)/shard_map/ppermute | solution.py:599
  123.7 1.6 %collective-permute-done.16 = bf16[2,64,512]{2,1,0:T(8,128)(2,1)S(1)} collective-permute-done((bf16[2,64,512]{2,1,0:T(8,128)(2,1)S(1)}, bf16[2,64,512]{2,1,0:T(8,128)(2,1)S(1)}, u32[]{:S(2)}, u32[]{:S(2)}) %collective-permute-start.16) | collective-permute-done | bytes 131104 | tf_op jit(solution)/shard_map/ppermute | solution.py:599
  127.5 1.2 collective-permute-done.20.refs_6_
  129.8 5.3 %shard_map.70 = (f32[64,512]{1,0:T(8,128)S(1)}, f32[64,512]{1,0:T(8,128)S(1)}, bf16[2,64,512]{2,1,0:T(8,128)(2,1)S(1)}, bf16[2,64,512]{2,1,0:T(8,128)(2,1)S(1)}, bf16[2,64,512]{2,1,0:T(8,128)(2,1)S(1)}) custom-call(s32[3]{0:T(128)S(1)} %copy-done.3, bf16[512,1024]{1,0:T(8,128)(2,1)S(1)} %get-tuple-element.58.tokens, ...), custom_call_target="tpu_custom_call" | custom-call | tf_op jit(solution)/shard_map/pallas_call | solution.py:545
  135.1 1.5 %collective-permute-start.22 = (bf16[2,64,512]{2,1,0:T(8,128)(2,1)S(1)}, bf16[2,64,512]{2,1,0:T(8,128)(2,1)S(1)}, u32[]{:S(2)}, u32[]{:S(2)}) collective-permute-start(bf16[2,64,512]{2,1,0:T(8,128)(2,1)S(1)} %get-tuple-element.72), channel_id=1, source_target_pairs={{0,2},{2,0},{4,6},{6,4},{8,10},{10,8},{12,14},{14,12},{1,3},{3,1},... | collective-permute-start | bytes 393224 | tf_op jit(solution)/shard_map/ppermute | solution.py:599
  137.2 1.5 collective-permute-start.24
  138.6 2.1 %collective-permute-done.22.refs_0_ = bf16[2,64,512]{2,1,0:T(8,128)(2,1)S(1)} collective-permute-done((bf16[2,64,512]{2,1,0:T(8,128)(2,1)S(1)}, bf16[2,64,512]{2,1,0:T(8,128)(2,1)S(1)}, u32[]{:S(2)}, u32[]{:S(2)}) %collective-permute-start.22) | collective-permute-done | bytes 131104 | tf_op jit(solution)/shard_map/ppermute | solution.py:599
  140.7 2.3 %collective-permute-done.23.refs_1_ = bf16[2,64,512]{2,1,0:T(8,128)(2,1)S(1)} collective-permute-done((bf16[2,64,512]{2,1,0:T(8,128)(2,1)S(1)}, bf16[2,64,512]{2,1,0:T(8,128)(2,1)S(1)}, u32[]{:S(2)}, u32[]{:S(2)}) %collective-permute-start.23) | collective-permute-done | bytes 131104 | tf_op jit(solution)/shard_map/ppermute | solution.py:599
  143.0 1.7 %collective-permute-done.24.refs_2_ = bf16[2,64,512]{2,1,0:T(8,128)(2,1)S(1)} collective-permute-done((bf16[2,64,512]{2,1,0:T(8,128)(2,1)S(1)}, bf16[2,64,512]{2,1,0:T(8,128)(2,1)S(1)}, u32[]{:S(2)}, u32[]{:S(2)}) %collective-permute-start.24) | collective-permute-done | bytes 131104 | tf_op jit(solution)/shard_map/ppermute | solution.py:599
  144.8 1.7 %collective-permute-start.25 = (bf16[64,512]{1,0:T(8,128)(2,1)S(1)}, bf16[64,512]{1,0:T(8,128)(2,1)S(1)}, u32[]{:S(2)}, u32[]{:S(2)}) collective-permute-start(bf16[64,512]{1,0:T(8,128)(2,1)S(1)} %get-tuple-element.76), channel_id=1, source_target_pairs={{0,8},{2,10},{4,12},{6,14},{8,0},{10,2},{12,4},{14,6},{1,9},{3,11}... | collective-permute-start | bytes 196616 | tf_op jit(solution)/shard_map/ppermute | solution.py:599
  146.4 3.5 %collective-permute-done.25.across_ref = bf16[64,512]{1,0:T(8,128)(2,1)S(1)} collective-permute-done((bf16[64,512]{1,0:T(8,128)(2,1)S(1)}, bf16[64,512]{1,0:T(8,128)(2,1)S(1)}, u32[]{:S(2)}, u32[]{:S(2)}) %collective-permute-start.25) | collective-permute-done | bytes 65568 | tf_op jit(solution)/shard_map/ppermute | solution.py:599
  (52 shorter events, 12.2 us)
Async XLA Ops:
  0.0 19.7 %copy-start.5 = (bf16[1,40,4,1024]{3,2,1,0:T(4,128)(2,1)S(1)}, bf16[1,40,4,1024]{3,2,1,0:T(4,128)(2,1)}, u32[]{:S(2)}) copy-start(bf16[1,40,4,1024]{3,2,1,0:T(4,128)(2,1)} %param.6) | copy-start | bytes 983044
  0.0 19.8 %copy-start.4 = (s32[1,64]{1,0:T(1,128)S(1)}, s32[1,64]{1,0:T(1,128)}, u32[]{:S(2)}) copy-start(s32[1,64]{1,0:T(1,128)} %keep_ref.3) | copy-start | bytes 772
  0.7 19.1 %copy-start.2 = (s32[3]{0:T(128)S(1)}, s32[3]{0:T(128)}, u32[]{:S(2)}) copy-start(s32[3]{0:T(128)} %pad_add_fusion.rank_ref.scalars) | copy-start | bytes 40
  15.6 65.7 %collective-permute-start.1 = (bf16[1664,128]{1,0:T(8,128)(2,1)}, bf16[1664,128]{1,0:T(8,128)(2,1)S(1)}, u32[]{:S(2)}, u32[]{:S(2)}) collective-permute-start(bf16[1664,128]{1,0:T(8,128)(2,1)} %shard_map.64), channel_id=1, source_target_pairs={{0,8},{2,10},{4,12},{6,14},{8,0},{10,2},{12,4},{14,6},{1,9},{3,11}... | collective-permute-start | bytes 1277960 | tf_op jit(solution)/shard_map/ppermute | solution.py:599
  19.8 49.1 %copy-start.3 = (s32[3]{0:T(128)S(1)}, s32[3]{0:T(128)}, u32[]{:S(2)}) copy-start(s32[3]{0:T(128)} %pad_add_fusion.rank_ref.scalars) | copy-start | bytes 40
  21.8 47.1 %all-to-all-start = ((bf16[8,80,128]{2,1,0:T(8,128)(2,1)}), bf16[8,80,128]{2,1,0:T(8,128)(2,1)S(1)}, u32[]{:S(2)}, u32[]{:S(2)}) async-start(bf16[8,80,128]{2,1,0:T(8,128)(2,1)} %bitcast.4), calls=%async_computation | async-start | bytes 327680 | tf_op jit(solution)/shard_map/all_to_all | solution.py:603
  65.3 8.1 %collective-permute-start.2 = (bf16[1024,128]{1,0:T(8,128)(2,1)}, bf16[1024,128]{1,0:T(8,128)(2,1)S(1)}, u32[]{:S(2)}, u32[]{:S(2)}) collective-permute-start(bf16[1024,128]{1,0:T(8,128)(2,1)} %get-tuple-element.47), channel_id=1, source_target_pairs={{0,2},{2,0},{4,6},{6,4},{8,10},{10,8},{12,14},{14,12},{1,3},{3,1},... | collective-permute-start | bytes 786440 | tf_op jit(solution)/shard_map/ppermute | solution.py:599
  67.4 10.9 %collective-permute-start.3 = (bf16[1024,128]{1,0:T(8,128)(2,1)}, bf16[1024,128]{1,0:T(8,128)(2,1)S(1)}, u32[]{:S(2)}, u32[]{:S(2)}) collective-permute-start(bf16[1024,128]{1,0:T(8,128)(2,1)} %get-tuple-element.48), channel_id=1, source_target_pairs={{0,4},{2,6},{4,0},{6,2},{8,12},{10,14},{12,8},{14,10},{1,5},{3,7},... | collective-permute-start | bytes 786440 | tf_op jit(solution)/shard_map/ppermute | solution.py:599
  68.8 12.5 %collective-permute-start.4 = (bf16[1024,128]{1,0:T(8,128)(2,1)}, bf16[1024,128]{1,0:T(8,128)(2,1)S(1)}, u32[]{:S(2)}, u32[]{:S(2)}) collective-permute-start(bf16[1024,128]{1,0:T(8,128)(2,1)} %get-tuple-element.49), channel_id=1, source_target_pairs={{0,6},{2,4},{4,2},{6,0},{8,14},{10,12},{12,10},{14,8},{1,7},{3,5},... | collective-permute-start | bytes 786440 | tf_op jit(solution)/shard_map/ppermute | solution.py:599
  69.8 11.5 %collective-permute-start = (bf16[256,128]{1,0:T(8,128)(2,1)S(1)}, bf16[256,128]{1,0:T(8,128)(2,1)S(1)}, u32[]{:S(2)}, u32[]{:S(2)}) collective-permute-start(bf16[256,128]{1,0:T(8,128)(2,1)S(1)} %shard_map.66.owned_ref), channel_id=1, source_target_pairs={{0,8},{2,10},{4,12},{6,14},{8,0},{10,2},{12,4},{14,6},{1,9},{3,11}... | collective-permute-start | bytes 196616 | tf_op jit(solution)/shard_map/ppermute | solution.py:599
  83.5 19.5 %all-to-all-start.1 = ((bf16[4,1312,128]{2,1,0:T(8,128)(2,1)}), bf16[4,1312,128]{2,1,0:T(8,128)(2,1)S(1)}, u32[]{:S(2)}, u32[]{:S(2)}) async-start(bf16[4,1312,128]{2,1,0:T(8,128)(2,1)} %shard_map.68), calls=%async_computation.1 | async-start | bytes 2686976 | tf_op jit(solution)/shard_map/all_to_all | solution.py:609
  87.5 1.5 %collective-permute-start.5 = (bf16[1024,128]{1,0:T(8,128)(2,1)S(1)}, bf16[1024,128]{1,0:T(8,128)(2,1)S(1)}, u32[]{:S(2)}, u32[]{:S(2)}) collective-permute-start(bf16[1024,128]{1,0:T(8,128)(2,1)S(1)} %copy-done), channel_id=1, source_target_pairs={{0,1},{1,0},{2,3},{3,2},{4,5},{5,4},{6,7},{7,6},{8,9},{9,8},{10,11... | collective-permute-start | bytes 786440 | tf_op jit(solution)/shard_map/ppermute | solution.py:599
  87.5 1.9 %collective-permute-start.6 = (bf16[1024,128]{1,0:T(8,128)(2,1)S(1)}, bf16[1024,128]{1,0:T(8,128)(2,1)S(1)}, u32[]{:S(2)}, u32[]{:S(2)}) collective-permute-start(bf16[1024,128]{1,0:T(8,128)(2,1)S(1)} %collective-permute-done.2.refs_9_), channel_id=1, source_target_pairs={{0,1},{1,0},{2,3},{3,2},{4,5},{5,4},{6,7},{7,6},{8,9},{9,8},{10,11... | collective-permute-start | bytes 786440 | tf_op jit(solution)/shard_map/ppermute | solution.py:599
  88.0 1.8 %collective-permute-start.7 = (bf16[1024,128]{1,0:T(8,128)(2,1)S(1)}, bf16[1024,128]{1,0:T(8,128)(2,1)S(1)}, u32[]{:S(2)}, u32[]{:S(2)}) collective-permute-start(bf16[1024,128]{1,0:T(8,128)(2,1)S(1)} %collective-permute-done.3.refs_10_), channel_id=1, source_target_pairs={{0,1},{1,0},{2,3},{3,2},{4,5},{5,4},{6,7},{7,6},{8,9},{9,8},{10,11... | collective-permute-start | bytes 786440 | tf_op jit(solution)/shard_map/ppermute | solution.py:599
  88.1 2.1 %collective-permute-start.8 = (bf16[1024,128]{1,0:T(8,128)(2,1)S(1)}, bf16[1024,128]{1,0:T(8,128)(2,1)S(1)}, u32[]{:S(2)}, u32[]{:S(2)}) collective-permute-start(bf16[1024,128]{1,0:T(8,128)(2,1)S(1)} %collective-permute-done.4.refs_11_), channel_id=1, source_target_pairs={{0,1},{1,0},{2,3},{3,2},{4,5},{5,4},{6,7},{7,6},{8,9},{9,8},{10,11... | collective-permute-start | bytes 786440 | tf_op jit(solution)/shard_map/ppermute | solution.py:599
  103.1 5.3 %collective-permute-start.9 = (bf16[4,512,128]{2,1,0:T(8,128)(2,1)S(1)}, bf16[4,512,128]{2,1,0:T(8,128)(2,1)S(1)}, u32[]{:S(2)}, u32[]{:S(2)}) collective-permute-start(bf16[4,512,128]{2,1,0:T(8,128)(2,1)S(1)} %slice.12), channel_id=1, source_target_pairs={{0,1},{1,0},{2,3},{3,2},{4,5},{5,4},{6,7},{7,6},{8,9},{9,8},{10,11... | collective-permute-start | bytes 1572872 | tf_op jit(solution)/shard_map/ppermute | solution.py:599
  103.2 5.2 %collective-permute-start.10 = (bf16[4,96,128]{2,1,0:T(8,128)(2,1)S(1)}, bf16[4,96,128]{2,1,0:T(8,128)(2,1)S(1)}, u32[]{:S(2)}, u32[]{:S(2)}) collective-permute-start(bf16[4,96,128]{2,1,0:T(8,128)(2,1)S(1)} %slice.13), channel_id=1, source_target_pairs={{0,16},{16,0},{1,17},{17,1},{2,18},{18,2},{3,19},{19,3},{4,20},{20... | collective-permute-start | bytes 294920 | tf_op jit(solution)/shard_map/ppermute | solution.py:599
  111.1 6.1 %collective-permute-start.11 = (bf16[64,512]{1,0:T(8,128)(2,1)S(1)}, bf16[64,512]{1,0:T(8,128)(2,1)S(1)}, u32[]{:S(2)}, u32[]{:S(2)}) collective-permute-start(bf16[64,512]{1,0:T(8,128)(2,1)S(1)} %get-tuple-element.59), channel_id=1, source_target_pairs={{0,8},{2,10},{4,12},{6,14},{8,0},{10,2},{12,4},{14,6},{1,9},{3,11}... | collective-permute-start | bytes 196616 | tf_op jit(solution)/shard_map/ppermute | solution.py:599
  112.9 12.4 %collective-permute-start.13 = (bf16[4,256,128]{2,1,0:T(8,128)(2,1)S(1)}, bf16[4,256,128]{2,1,0:T(8,128)(2,1)S(1)}, u32[]{:S(2)}, u32[]{:S(2)}) collective-permute-start(bf16[4,256,128]{2,1,0:T(8,128)(2,1)S(1)} %get-tuple-element.77.refs_4_), channel_id=1, source_target_pairs={{0,16},{16,0},{1,17},{17,1},{2,18},{18,2},{3,19},{19,3},{4,20},{20... | collective-permute-start | bytes 786440 | tf_op jit(solution)/shard_map/ppermute | solution.py:599
  114.5 11.8 %collective-permute-start.12 = (bf16[4,256,128]{2,1,0:T(8,128)(2,1)S(1)}, bf16[4,256,128]{2,1,0:T(8,128)(2,1)S(1)}, u32[]{:S(2)}, u32[]{:S(2)}) collective-permute-start(bf16[4,256,128]{2,1,0:T(8,128)(2,1)S(1)} %get-tuple-element.78.refs_0_), channel_id=1, source_target_pairs={{0,16},{16,0},{1,17},{17,1},{2,18},{18,2},{3,19},{19,3},{4,20},{20... | collective-permute-start | bytes 786440 | tf_op jit(solution)/shard_map/ppermute | solution.py:599
  117.2 5.7 %collective-permute-start.15 = (bf16[2,64,512]{2,1,0:T(8,128)(2,1)S(1)}, bf16[2,64,512]{2,1,0:T(8,128)(2,1)S(1)}, u32[]{:S(2)}, u32[]{:S(2)}) collective-permute-start(bf16[2,64,512]{2,1,0:T(8,128)(2,1)S(1)} %get-tuple-element.80), channel_id=1, source_target_pairs={{0,4},{2,6},{4,0},{6,2},{8,12},{10,14},{12,8},{14,10},{1,5},{3,7},... | collective-permute-start | bytes 393224 | tf_op jit(solution)/shard_map/ppermute | solution.py:599
  117.4 6.3 %collective-permute-start.14 = (bf16[2,64,512]{2,1,0:T(8,128)(2,1)S(1)}, bf16[2,64,512]{2,1,0:T(8,128)(2,1)S(1)}, u32[]{:S(2)}, u32[]{:S(2)}) collective-permute-start(bf16[2,64,512]{2,1,0:T(8,128)(2,1)S(1)} %get-tuple-element.80), channel_id=1, source_target_pairs={{0,2},{2,0},{4,6},{6,4},{8,10},{10,8},{12,14},{14,12},{1,3},{3,1},... | collective-permute-start | bytes 393224 | tf_op jit(solution)/shard_map/ppermute | solution.py:599
  118.2 7.1 %collective-permute-start.16 = (bf16[2,64,512]{2,1,0:T(8,128)(2,1)S(1)}, bf16[2,64,512]{2,1,0:T(8,128)(2,1)S(1)}, u32[]{:S(2)}, u32[]{:S(2)}) collective-permute-start(bf16[2,64,512]{2,1,0:T(8,128)(2,1)S(1)} %get-tuple-element.80), channel_id=1, source_target_pairs={{0,6},{2,4},{4,2},{6,0},{8,14},{10,12},{12,10},{14,8},{1,7},{3,5},... | collective-permute-start | bytes 393224 | tf_op jit(solution)/shard_map/ppermute | solution.py:599
  126.3 3.5 %collective-permute-start.17 = (bf16[4,2,64,512]{3,2,1,0:T(8,128)(2,1)S(1)}, bf16[4,2,64,512]{3,2,1,0:T(8,128)(2,1)S(1)}, u32[]{:S(2)}, u32[]{:S(2)}) collective-permute-start(bf16[4,2,64,512]{3,2,1,0:T(8,128)(2,1)S(1)} %pad_maximum_fusion.a), channel_id=1, source_target_pairs={{0,1},{1,0},{2,3},{3,2},{4,5},{5,4},{6,7},{7,6},{8,9},{9,8},{10,11... | collective-permute-start | bytes 1572872 | tf_op jit(solution)/shard_map/ppermute | solution.py:599
  126.4 2.3 %collective-permute-start.20 = (bf16[4,256,128]{2,1,0:T(8,128)(2,1)S(1)}, bf16[4,256,128]{2,1,0:T(8,128)(2,1)S(1)}, u32[]{:S(2)}, u32[]{:S(2)}) collective-permute-start(bf16[4,256,128]{2,1,0:T(8,128)(2,1)S(1)} %get-tuple-element.77.refs_4_), channel_id=1, source_target_pairs={{0,1},{1,0},{2,3},{3,2},{4,5},{5,4},{6,7},{7,6},{8,9},{9,8},{10,11... | collective-permute-start | bytes 786440 | tf_op jit(solution)/shard_map/ppermute | solution.py:599
  126.9 2.1 %collective-permute-start.18 = (bf16[4,256,128]{2,1,0:T(8,128)(2,1)S(1)}, bf16[4,256,128]{2,1,0:T(8,128)(2,1)S(1)}, u32[]{:S(2)}, u32[]{:S(2)}) collective-permute-start(bf16[4,256,128]{2,1,0:T(8,128)(2,1)S(1)} %get-tuple-element.78.refs_0_), channel_id=1, source_target_pairs={{0,1},{1,0},{2,3},{3,2},{4,5},{5,4},{6,7},{7,6},{8,9},{9,8},{10,11... | collective-permute-start | bytes 786440 | tf_op jit(solution)/shard_map/ppermute | solution.py:599
  127.0 2.4 %collective-permute-start.19 = (bf16[4,256,128]{2,1,0:T(8,128)(2,1)S(1)}, bf16[4,256,128]{2,1,0:T(8,128)(2,1)S(1)}, u32[]{:S(2)}, u32[]{:S(2)}) collective-permute-start(bf16[4,256,128]{2,1,0:T(8,128)(2,1)S(1)} %collective-permute-done.12.refs_1_), channel_id=1, source_target_pairs={{0,1},{1,0},{2,3},{3,2},{4,5},{5,4},{6,7},{7,6},{8,9},{9,8},{10,11... | collective-permute-start | bytes 786440 | tf_op jit(solution)/shard_map/ppermute | solution.py:599
  127.4 2.4 %collective-permute-start.21 = (bf16[4,256,128]{2,1,0:T(8,128)(2,1)S(1)}, bf16[4,256,128]{2,1,0:T(8,128)(2,1)S(1)}, u32[]{:S(2)}, u32[]{:S(2)}) collective-permute-start(bf16[4,256,128]{2,1,0:T(8,128)(2,1)S(1)} %collective-permute-done.13.refs_5_), channel_id=1, source_target_pairs={{0,1},{1,0},{2,3},{3,2},{4,5},{5,4},{6,7},{7,6},{8,9},{9,8},{10,11... | collective-permute-start | bytes 786440 | tf_op jit(solution)/shard_map/ppermute | solution.py:599
  135.1 5.6 %collective-permute-start.22 = (bf16[2,64,512]{2,1,0:T(8,128)(2,1)S(1)}, bf16[2,64,512]{2,1,0:T(8,128)(2,1)S(1)}, u32[]{:S(2)}, u32[]{:S(2)}) collective-permute-start(bf16[2,64,512]{2,1,0:T(8,128)(2,1)S(1)} %get-tuple-element.72), channel_id=1, source_target_pairs={{0,2},{2,0},{4,6},{6,4},{8,10},{10,8},{12,14},{14,12},{1,3},{3,1},... | collective-permute-start | bytes 393224 | tf_op jit(solution)/shard_map/ppermute | solution.py:599
  136.6 6.4 %collective-permute-start.23 = (bf16[2,64,512]{2,1,0:T(8,128)(2,1)S(1)}, bf16[2,64,512]{2,1,0:T(8,128)(2,1)S(1)}, u32[]{:S(2)}, u32[]{:S(2)}) collective-permute-start(bf16[2,64,512]{2,1,0:T(8,128)(2,1)S(1)} %get-tuple-element.73), channel_id=1, source_target_pairs={{0,4},{2,6},{4,0},{6,2},{8,12},{10,14},{12,8},{14,10},{1,5},{3,7},... | collective-permute-start | bytes 393224 | tf_op jit(solution)/shard_map/ppermute | solution.py:599
  137.2 7.5 %collective-permute-start.24 = (bf16[2,64,512]{2,1,0:T(8,128)(2,1)S(1)}, bf16[2,64,512]{2,1,0:T(8,128)(2,1)S(1)}, u32[]{:S(2)}, u32[]{:S(2)}) collective-permute-start(bf16[2,64,512]{2,1,0:T(8,128)(2,1)S(1)} %get-tuple-element.74), channel_id=1, source_target_pairs={{0,6},{2,4},{4,2},{6,0},{8,14},{10,12},{12,10},{14,8},{1,7},{3,5},... | collective-permute-start | bytes 393224 | tf_op jit(solution)/shard_map/ppermute | solution.py:599
  144.8 5.2 %collective-permute-start.25 = (bf16[64,512]{1,0:T(8,128)(2,1)S(1)}, bf16[64,512]{1,0:T(8,128)(2,1)S(1)}, u32[]{:S(2)}, u32[]{:S(2)}) collective-permute-start(bf16[64,512]{1,0:T(8,128)(2,1)S(1)} %get-tuple-element.76), channel_id=1, source_target_pairs={{0,8},{2,10},{4,12},{6,14},{8,0},{10,2},{12,4},{14,6},{1,9},{3,11}... | collective-permute-start | bytes 196616 | tf_op jit(solution)/shard_map/ppermute | solution.py:599
  (2 other events, 4.9 us)

commit v13 on v12

--- a/solution.py
+++ b/solution.py
@@ -344,7 +344,7 @@
     return pl.pallas_call(
         kernel,
         in_specs=[sspec()] + [hspec()] * 4,
-        out_specs=[aspec()] * len(shapes),
+        out_specs=[vspec()] * len(shapes),
         out_shape=[struct(shape) for shape in shapes],
         scratch_shapes=[pltpu.SemaphoreType.DMA((count,))],
     )(scalars, *weights)

time: 151 us -> 115 us (0.76)
  Pallas kernels: 67.4 us -> 18.8 us
  waiting for transfers between devices: 46.3 us -> 57.9 us
    pallas_call x2, Pallas kernels: 54.6 us -> 5.96 us  [pack(): pl.pallas_call(kernel, in_specs=[sspec()] + [hspec()] * 4, out_specs=[vsp...]
    all_to_all x1, waiting for transfers between devices: 0.01 us -> 10.2 us  [exchange(): return lax.all_to_all(value, 'seq', split_axis=0, concat_axis=0, tiled=True)]
  transfers between devices with their start and end apart: 28 -> 28, of which waited for: 22 -> 21; matrix products, arithmetic and copies ran while one was open for 0% -> 0% of each run, Pallas kernels for 28% -> 5%
where the time goes in v13:
time: 115 us; the launch traced here: 114 us
  waiting for transfers between devices  57.9 us (50%)
  starting transfers between devices  35.7 us (31%)
  Pallas kernels  18.8 us (16%)
    ppermute x26, waiting for transfers between devices, swap(): return lax.ppermute(value, axis, [(i, i ^ j) for i in range(n)])  34 us
    ppermute x26, starting transfers between devices, swap(): return lax.ppermute(value, axis, [(i, i ^ j) for i in range(n)])  28.2 us
    all_to_all x1, waiting for transfers between devices, exchange_half(): lax.all_to_all(value, 'seq', split_axis=0, concat_axis=0, axis_index_grou...  13.7 us
    all_to_all x1, waiting for transfers between devices, exchange(): return lax.all_to_all(value, 'seq', split_axis=0, concat_axis=0, tiled=True)  10.2 us
    pallas_call x2, Pallas kernels, pack(): pl.pallas_call(kernel, in_specs=[sspec()] + [hspec()] * 4, out_specs=[vsp...  5.96 us
    pallas_call x1, Pallas kernels, mlp(): pl.pallas_call(kernel, in_specs=[sspec()] + [vspec()] * 3 + [aspec()] * (...  5.28 us
    all_to_all x1, starting transfers between devices, exchange(): return lax.all_to_all(value, 'seq', split_axis=0, concat_axis=0, tiled=True)  3.81 us
    all_to_all x1, starting transfers between devices, exchange_half(): lax.all_to_all(value, 'seq', split_axis=0, concat_axis=0, axis_index_grou...  3.67 us
  transfers between devices with their start and end apart: 28, of which 21 were waited for; matrix products, arithmetic and copies ran while one was open for 0% of the time, Pallas kernels for 5%

profile of v13, /device:TPU:0, one launch (start us, length us, event | category | flops | bytes accessed | tf_op | source)
XLA Modules:
  0.0 114.5 jit_solution(1921127543415207513)
XLA Ops:
  0.7 2.7 %shard_map.64 = bf16[1664,128]{1,0:T(8,128)(2,1)} custom-call(s32[3]{0:T(128)} %pad_add_fusion.rank_ref.scalars, bf16[8,192,128]{2,1,0:T(8,128)(2,1)} %bitcast.16, bf16[512,128]{1,0:T(8,128)(2,1)} %out_weight_ref.2, bf16[128,2048]{1,0:T(8,128)(2,1)} %up_ref.2, bf16[2048,128]{1,0:T(8,128)(2,1)} %down_ref.2), custom_call_target="tpu_custom_call" | custom-call | tf_op jit(solution)/shard_map/pallas_call | solution.py:344
  3.4 4.1 %collective-permute-start.1 = (bf16[1664,128]{1,0:T(8,128)(2,1)}, bf16[1664,128]{1,0:T(8,128)(2,1)S(1)}, u32[]{:S(2)}, u32[]{:S(2)}) collective-permute-start(bf16[1664,128]{1,0:T(8,128)(2,1)} %shard_map.64), channel_id=1, source_target_pairs={{0,8},{2,10},{4,12},{6,14},{8,0},{10,2},{12,4},{14,6},{1,9},{3,11}... | collective-permute-start | bytes 1277960 | tf_op jit(solution)/shard_map/ppermute | solution.py:599
  7.6 2.0 %shard_map.65 = bf16[640,128]{1,0:T(8,128)(2,1)} custom-call(s32[3]{0:T(128)S(1)} %copy-done.2, s32[1,64]{1,0:T(1,128)S(1)} %copy-done.4, bf16[160,1024]{1,0:T(8,128)(2,1)S(1)} %reshape.8.patches_ref), custom_call_target="tpu_custom_call" | custom-call | tf_op jit(solution)/shard_map/pallas_call | solution.py:247
  9.6 3.8 %all-to-all-start = ((bf16[8,80,128]{2,1,0:T(8,128)(2,1)}), bf16[8,80,128]{2,1,0:T(8,128)(2,1)S(1)}, u32[]{:S(2)}, u32[]{:S(2)}) async-start(bf16[8,80,128]{2,1,0:T(8,128)(2,1)} %bitcast.4), calls=%async_computation | async-start | bytes 327680 | tf_op jit(solution)/shard_map/all_to_all | solution.py:603
  13.4 3.3 %shard_map.67 = (bf16[1024,128]{1,0:T(8,128)(2,1)}, bf16[1024,128]{1,0:T(8,128)(2,1)}, bf16[1024,128]{1,0:T(8,128)(2,1)}, bf16[1024,128]{1,0:T(8,128)(2,1)}, bf16[4,192,128]{2,1,0:T(8,128)(2,1)}) custom-call(s32[3]{0:T(128)} %pad_add_fusion.rank_ref.scalars, bf16[8,192,128]{2,1,0:T(8,128)(2,1)} %bitcast.17, bf16[512,128]{1,0:T(8,128)(2,1)} %out_weight_ref.2, ...), custom_call_target="tpu_custom_call" | custom-call | tf_op jit(solution)/shard_map/pallas_call | solution.py:344
  16.7 2.1 %collective-permute-start.2 = (bf16[1024,128]{1,0:T(8,128)(2,1)}, bf16[1024,128]{1,0:T(8,128)(2,1)S(1)}, u32[]{:S(2)}, u32[]{:S(2)}) collective-permute-start(bf16[1024,128]{1,0:T(8,128)(2,1)} %get-tuple-element.47), channel_id=1, source_target_pairs={{0,2},{2,0},{4,6},{6,4},{8,10},{10,8},{12,14},{14,12},{1,3},{3,1},... | collective-permute-start | bytes 786440 | tf_op jit(solution)/shard_map/ppermute | solution.py:599
  18.8 1.5 %collective-permute-start.3 = (bf16[1024,128]{1,0:T(8,128)(2,1)}, bf16[1024,128]{1,0:T(8,128)(2,1)S(1)}, u32[]{:S(2)}, u32[]{:S(2)}) collective-permute-start(bf16[1024,128]{1,0:T(8,128)(2,1)} %get-tuple-element.48), channel_id=1, source_target_pairs={{0,4},{2,6},{4,0},{6,2},{8,12},{10,14},{12,8},{14,10},{1,5},{3,7},... | collective-permute-start | bytes 786440 | tf_op jit(solution)/shard_map/ppermute | solution.py:599
  20.3 10.2 %all-to-all-done = bf16[8,80,128]{2,1,0:T(8,128)(2,1)S(1)} async-done(((bf16[8,80,128]{2,1,0:T(8,128)(2,1)}), bf16[8,80,128]{2,1,0:T(8,128)(2,1)S(1)}, u32[]{:S(2)}, u32[]{:S(2)}) %all-to-all-start) | async-done | bytes 163872 | tf_op jit(solution)/shard_map/all_to_all | solution.py:603
  30.6 0.9 shard_map.66.owned_ref
  31.5 3.4 %collective-permute-start = (bf16[256,128]{1,0:T(8,128)(2,1)S(1)}, bf16[256,128]{1,0:T(8,128)(2,1)S(1)}, u32[]{:S(2)}, u32[]{:S(2)}) collective-permute-start(bf16[256,128]{1,0:T(8,128)(2,1)S(1)} %shard_map.66.owned_ref), channel_id=1, source_target_pairs={{0,8},{2,10},{4,12},{6,14},{8,0},{10,2},{12,4},{14,6},{1,9},{3,11}... | collective-permute-start | bytes 196616 | tf_op jit(solution)/shard_map/ppermute | solution.py:599
  35.0 7.0 %collective-permute-done.4.refs_11_ = bf16[1024,128]{1,0:T(8,128)(2,1)S(1)} collective-permute-done((bf16[1024,128]{1,0:T(8,128)(2,1)}, bf16[1024,128]{1,0:T(8,128)(2,1)S(1)}, u32[]{:S(2)}, u32[]{:S(2)}) %collective-permute-start.4) | collective-permute-done | bytes 262176 | tf_op jit(solution)/shard_map/ppermute | solution.py:599
  42.0 0.9 copy-done.1
  42.9 1.2 %shard_map.68 = bf16[4,1312,128]{2,1,0:T(8,128)(2,1)} custom-call(bf16[256,128]{1,0:T(8,128)(2,1)S(1)} %shard_map.66.owned_ref, bf16[256,128]{1,0:T(8,128)(2,1)S(1)} %collective-permute-done.across_ref, bf16[4,192,128]{2,1,0:T(8,128)(2,1)S(1)} %copy-done.1, bf16[1664,128]{1,0:T(8,128)(2,1)S(1)} %collective-permute-done.1.far_ref), custom_call_target="tpu_custom_call" | custom-call | tf_op jit(solution)/shard_map/pallas_call | solution.py:388
  44.1 3.7 %all-to-all-start.1 = ((bf16[4,1312,128]{2,1,0:T(8,128)(2,1)}), bf16[4,1312,128]{2,1,0:T(8,128)(2,1)S(1)}, u32[]{:S(2)}, u32[]{:S(2)}) async-start(bf16[4,1312,128]{2,1,0:T(8,128)(2,1)} %shard_map.68), calls=%async_computation.1 | async-start | bytes 2686976 | tf_op jit(solution)/shard_map/all_to_all | solution.py:609
  50.6 13.7 %all-to-all-done.1.mine_ref = bf16[4,1312,128]{2,1,0:T(8,128)(2,1)S(1)} async-done(((bf16[4,1312,128]{2,1,0:T(8,128)(2,1)}), bf16[4,1312,128]{2,1,0:T(8,128)(2,1)S(1)}, u32[]{:S(2)}, u32[]{:S(2)}) %all-to-all-start.1) | async-done | bytes 1343520 | tf_op jit(solution)/shard_map/all_to_all | solution.py:609
  64.4 1.6 %collective-permute-start.10 = (bf16[4,96,128]{2,1,0:T(8,128)(2,1)S(1)}, bf16[4,96,128]{2,1,0:T(8,128)(2,1)S(1)}, u32[]{:S(2)}, u32[]{:S(2)}) collective-permute-start(bf16[4,96,128]{2,1,0:T(8,128)(2,1)S(1)} %slice.13), channel_id=1, source_target_pairs={{0,16},{16,0},{1,17},{17,1},{2,18},{18,2},{3,19},{19,3},{4,20},{20... | collective-permute-start | bytes 294920 | tf_op jit(solution)/shard_map/ppermute | solution.py:599
  65.9 3.7 %collective-permute-done.10.far_ref = bf16[4,96,128]{2,1,0:T(8,128)(2,1)S(1)} collective-permute-done((bf16[4,96,128]{2,1,0:T(8,128)(2,1)S(1)}, bf16[4,96,128]{2,1,0:T(8,128)(2,1)S(1)}, u32[]{:S(2)}, u32[]{:S(2)}) %collective-permute-start.10) | collective-permute-done | bytes 98336 | tf_op jit(solution)/shard_map/ppermute | solution.py:599
  69.6 2.7 %shard_map.69 = (bf16[512,1024]{1,0:T(8,128)(2,1)S(1)}, bf16[64,512]{1,0:T(8,128)(2,1)S(1)}) custom-call(s32[3]{0:T(128)S(1)} %copy-done.3, bf16[4,1312,128]{2,1,0:T(8,128)(2,1)S(1)} %all-to-all-done.1.mine_ref, bf16[4,512,128]{2,1,0:T(8,128)(2,1)S(1)} %collective-permute-done.9.other_ref, bf16[4,96,128]{2,1,0:T(8,128)(2,1)S(1)} %collective-permute-done.10.far_ref), custom_call_target="tpu_custom_call" | custom-call | flops 30000001024 | bytes 1048576 | tf_op jit(solution)/shard_map/pallas_call | solution.py:454
  72.3 3.7 %collective-permute-start.11 = (bf16[64,512]{1,0:T(8,128)(2,1)S(1)}, bf16[64,512]{1,0:T(8,128)(2,1)S(1)}, u32[]{:S(2)}, u32[]{:S(2)}) collective-permute-start(bf16[64,512]{1,0:T(8,128)(2,1)S(1)} %get-tuple-element.59), channel_id=1, source_target_pairs={{0,8},{2,10},{4,12},{6,14},{8,0},{10,2},{12,4},{14,6},{1,9},{3,11}... | collective-permute-start | bytes 196616 | tf_op jit(solution)/shard_map/ppermute | solution.py:599
  76.1 1.6 %collective-permute-start.13 = (bf16[4,256,128]{2,1,0:T(8,128)(2,1)S(1)}, bf16[4,256,128]{2,1,0:T(8,128)(2,1)S(1)}, u32[]{:S(2)}, u32[]{:S(2)}) collective-permute-start(bf16[4,256,128]{2,1,0:T(8,128)(2,1)S(1)} %get-tuple-element.77.refs_4_), channel_id=1, source_target_pairs={{0,16},{16,0},{1,17},{17,1},{2,18},{18,2},{3,19},{19,3},{4,20},{20... | collective-permute-start | bytes 786440 | tf_op jit(solution)/shard_map/ppermute | solution.py:599
  78.2 1.2 %collective-permute-done.11 = bf16[64,512]{1,0:T(8,128)(2,1)S(1)} collective-permute-done((bf16[64,512]{1,0:T(8,128)(2,1)S(1)}, bf16[64,512]{1,0:T(8,128)(2,1)S(1)}, u32[]{:S(2)}, u32[]{:S(2)}) %collective-permute-start.11) | collective-permute-done | bytes 65568 | tf_op jit(solution)/shard_map/ppermute | solution.py:599
  80.3 2.7 %collective-permute-start.16 = (bf16[2,64,512]{2,1,0:T(8,128)(2,1)S(1)}, bf16[2,64,512]{2,1,0:T(8,128)(2,1)S(1)}, u32[]{:S(2)}, u32[]{:S(2)}) collective-permute-start(bf16[2,64,512]{2,1,0:T(8,128)(2,1)S(1)} %get-tuple-element.80), channel_id=1, source_target_pairs={{0,6},{2,4},{4,2},{6,0},{8,14},{10,12},{12,10},{14,8},{1,7},{3,5},... | collective-permute-start | bytes 393224 | tf_op jit(solution)/shard_map/ppermute | solution.py:599
  83.0 2.9 %collective-permute-done.15 = bf16[2,64,512]{2,1,0:T(8,128)(2,1)S(1)} collective-permute-done((bf16[2,64,512]{2,1,0:T(8,128)(2,1)S(1)}, bf16[2,64,512]{2,1,0:T(8,128)(2,1)S(1)}, u32[]{:S(2)}, u32[]{:S(2)}) %collective-permute-start.15) | collective-permute-done | bytes 131104 | tf_op jit(solution)/shard_map/ppermute | solution.py:599
  85.9 1.8 %collective-permute-done.16 = bf16[2,64,512]{2,1,0:T(8,128)(2,1)S(1)} collective-permute-done((bf16[2,64,512]{2,1,0:T(8,128)(2,1)S(1)}, bf16[2,64,512]{2,1,0:T(8,128)(2,1)S(1)}, u32[]{:S(2)}, u32[]{:S(2)}) %collective-permute-start.16) | collective-permute-done | bytes 131104 | tf_op jit(solution)/shard_map/ppermute | solution.py:599
  87.7 1.7 %collective-permute-done.12.refs_1_ = bf16[4,256,128]{2,1,0:T(8,128)(2,1)S(1)} collective-permute-done((bf16[4,256,128]{2,1,0:T(8,128)(2,1)S(1)}, bf16[4,256,128]{2,1,0:T(8,128)(2,1)S(1)}, u32[]{:S(2)}, u32[]{:S(2)}) %collective-permute-start.12) | collective-permute-done | bytes 262176 | tf_op jit(solution)/shard_map/ppermute | solution.py:599
  90.6 1.2 %collective-permute-done.20.refs_6_ = bf16[4,256,128]{2,1,0:T(8,128)(2,1)S(1)} collective-permute-done((bf16[4,256,128]{2,1,0:T(8,128)(2,1)S(1)}, bf16[4,256,128]{2,1,0:T(8,128)(2,1)S(1)}, u32[]{:S(2)}, u32[]{:S(2)}) %collective-permute-start.20) | collective-permute-done | bytes 262176 | tf_op jit(solution)/shard_map/ppermute | solution.py:599
  92.9 5.3 %shard_map.70 = (f32[64,512]{1,0:T(8,128)S(1)}, f32[64,512]{1,0:T(8,128)S(1)}, bf16[2,64,512]{2,1,0:T(8,128)(2,1)S(1)}, bf16[2,64,512]{2,1,0:T(8,128)(2,1)S(1)}, bf16[2,64,512]{2,1,0:T(8,128)(2,1)S(1)}) custom-call(s32[3]{0:T(128)S(1)} %copy-done.3, bf16[512,1024]{1,0:T(8,128)(2,1)S(1)} %get-tuple-element.58.tokens, ...), custom_call_target="tpu_custom_call" | custom-call | tf_op jit(solution)/shard_map/pallas_call | solution.py:545
  99.6 2.2 %collective-permute-start.24 = (bf16[2,64,512]{2,1,0:T(8,128)(2,1)S(1)}, bf16[2,64,512]{2,1,0:T(8,128)(2,1)S(1)}, u32[]{:S(2)}, u32[]{:S(2)}) collective-permute-start(bf16[2,64,512]{2,1,0:T(8,128)(2,1)S(1)} %get-tuple-element.74), channel_id=1, source_target_pairs={{0,6},{2,4},{4,2},{6,0},{8,14},{10,12},{12,10},{14,8},{1,7},{3,5},... | collective-permute-start | bytes 393224 | tf_op jit(solution)/shard_map/ppermute | solution.py:599
  101.8 2.1 %collective-permute-done.22.refs_0_ = bf16[2,64,512]{2,1,0:T(8,128)(2,1)S(1)} collective-permute-done((bf16[2,64,512]{2,1,0:T(8,128)(2,1)S(1)}, bf16[2,64,512]{2,1,0:T(8,128)(2,1)S(1)}, u32[]{:S(2)}, u32[]{:S(2)}) %collective-permute-start.22) | collective-permute-done | bytes 131104 | tf_op jit(solution)/shard_map/ppermute | solution.py:599
  103.8 1.6 %collective-permute-done.23.refs_1_ = bf16[2,64,512]{2,1,0:T(8,128)(2,1)S(1)} collective-permute-done((bf16[2,64,512]{2,1,0:T(8,128)(2,1)S(1)}, bf16[2,64,512]{2,1,0:T(8,128)(2,1)S(1)}, u32[]{:S(2)}, u32[]{:S(2)}) %collective-permute-start.23) | collective-permute-done | bytes 131104 | tf_op jit(solution)/shard_map/ppermute | solution.py:599
  105.4 2.4 %collective-permute-done.24.refs_2_ = bf16[2,64,512]{2,1,0:T(8,128)(2,1)S(1)} collective-permute-done((bf16[2,64,512]{2,1,0:T(8,128)(2,1)S(1)}, bf16[2,64,512]{2,1,0:T(8,128)(2,1)S(1)}, u32[]{:S(2)}, u32[]{:S(2)}) %collective-permute-start.24) | collective-permute-done | bytes 131104 | tf_op jit(solution)/shard_map/ppermute | solution.py:599
  108.3 5.6 %collective-permute-done.25.across_ref = bf16[64,512]{1,0:T(8,128)(2,1)S(1)} collective-permute-done((bf16[64,512]{1,0:T(8,128)(2,1)S(1)}, bf16[64,512]{1,0:T(8,128)(2,1)S(1)}, u32[]{:S(2)}, u32[]{:S(2)}) %collective-permute-start.25) | collective-permute-done | bytes 65568 | tf_op jit(solution)/shard_map/ppermute | solution.py:599
  (52 shorter events, 10.1 us)
Async XLA Ops:
  0.0 7.5 %copy-start.5 = (bf16[1,40,4,1024]{3,2,1,0:T(4,128)(2,1)S(1)}, bf16[1,40,4,1024]{3,2,1,0:T(4,128)(2,1)}, u32[]{:S(2)}) copy-start(bf16[1,40,4,1024]{3,2,1,0:T(4,128)(2,1)} %param.6) | copy-start | bytes 983044
  0.0 7.6 %copy-start.4 = (s32[1,64]{1,0:T(1,128)S(1)}, s32[1,64]{1,0:T(1,128)}, u32[]{:S(2)}) copy-start(s32[1,64]{1,0:T(1,128)} %keep_ref.3) | copy-start | bytes 772
  0.7 6.9 %copy-start.2 = (s32[3]{0:T(128)S(1)}, s32[3]{0:T(128)}, u32[]{:S(2)}) copy-start(s32[3]{0:T(128)} %pad_add_fusion.rank_ref.scalars) | copy-start | bytes 40
  3.4 38.6 %collective-permute-start.1 = (bf16[1664,128]{1,0:T(8,128)(2,1)}, bf16[1664,128]{1,0:T(8,128)(2,1)S(1)}, u32[]{:S(2)}, u32[]{:S(2)}) collective-permute-start(bf16[1664,128]{1,0:T(8,128)(2,1)} %shard_map.64), channel_id=1, source_target_pairs={{0,8},{2,10},{4,12},{6,14},{8,0},{10,2},{12,4},{14,6},{1,9},{3,11}... | collective-permute-start | bytes 1277960 | tf_op jit(solution)/shard_map/ppermute | solution.py:599
  7.6 23.0 %copy-start.3 = (s32[3]{0:T(128)S(1)}, s32[3]{0:T(128)}, u32[]{:S(2)}) copy-start(s32[3]{0:T(128)} %pad_add_fusion.rank_ref.scalars) | copy-start | bytes 40
  9.6 20.9 %all-to-all-start = ((bf16[8,80,128]{2,1,0:T(8,128)(2,1)}), bf16[8,80,128]{2,1,0:T(8,128)(2,1)S(1)}, u32[]{:S(2)}, u32[]{:S(2)}) async-start(bf16[8,80,128]{2,1,0:T(8,128)(2,1)} %bitcast.4), calls=%async_computation | async-start | bytes 327680 | tf_op jit(solution)/shard_map/all_to_all | solution.py:603
  16.7 18.2 %collective-permute-start.2 = (bf16[1024,128]{1,0:T(8,128)(2,1)}, bf16[1024,128]{1,0:T(8,128)(2,1)S(1)}, u32[]{:S(2)}, u32[]{:S(2)}) collective-permute-start(bf16[1024,128]{1,0:T(8,128)(2,1)} %get-tuple-element.47), channel_id=1, source_target_pairs={{0,2},{2,0},{4,6},{6,4},{8,10},{10,8},{12,14},{14,12},{1,3},{3,1},... | collective-permute-start | bytes 786440 | tf_op jit(solution)/shard_map/ppermute | solution.py:599
  18.8 16.2 %collective-permute-start.3 = (bf16[1024,128]{1,0:T(8,128)(2,1)}, bf16[1024,128]{1,0:T(8,128)(2,1)S(1)}, u32[]{:S(2)}, u32[]{:S(2)}) collective-permute-start(bf16[1024,128]{1,0:T(8,128)(2,1)} %get-tuple-element.48), channel_id=1, source_target_pairs={{0,4},{2,6},{4,0},{6,2},{8,12},{10,14},{12,8},{14,10},{1,5},{3,7},... | collective-permute-start | bytes 786440 | tf_op jit(solution)/shard_map/ppermute | solution.py:599
  20.2 21.7 %collective-permute-start.4 = (bf16[1024,128]{1,0:T(8,128)(2,1)}, bf16[1024,128]{1,0:T(8,128)(2,1)S(1)}, u32[]{:S(2)}, u32[]{:S(2)}) collective-permute-start(bf16[1024,128]{1,0:T(8,128)(2,1)} %get-tuple-element.49), channel_id=1, source_target_pairs={{0,6},{2,4},{4,2},{6,0},{8,14},{10,12},{12,10},{14,8},{1,7},{3,5},... | collective-permute-start | bytes 786440 | tf_op jit(solution)/shard_map/ppermute | solution.py:599
  31.5 10.5 %collective-permute-start = (bf16[256,128]{1,0:T(8,128)(2,1)S(1)}, bf16[256,128]{1,0:T(8,128)(2,1)S(1)}, u32[]{:S(2)}, u32[]{:S(2)}) collective-permute-start(bf16[256,128]{1,0:T(8,128)(2,1)S(1)} %shard_map.66.owned_ref), channel_id=1, source_target_pairs={{0,8},{2,10},{4,12},{6,14},{8,0},{10,2},{12,4},{14,6},{1,9},{3,11}... | collective-permute-start | bytes 196616 | tf_op jit(solution)/shard_map/ppermute | solution.py:599
  44.1 20.1 %all-to-all-start.1 = ((bf16[4,1312,128]{2,1,0:T(8,128)(2,1)}), bf16[4,1312,128]{2,1,0:T(8,128)(2,1)S(1)}, u32[]{:S(2)}, u32[]{:S(2)}) async-start(bf16[4,1312,128]{2,1,0:T(8,128)(2,1)} %shard_map.68), calls=%async_computation.1 | async-start | bytes 2686976 | tf_op jit(solution)/shard_map/all_to_all | solution.py:609
  47.8 1.6 %collective-permute-start.5 = (bf16[1024,128]{1,0:T(8,128)(2,1)S(1)}, bf16[1024,128]{1,0:T(8,128)(2,1)S(1)}, u32[]{:S(2)}, u32[]{:S(2)}) collective-permute-start(bf16[1024,128]{1,0:T(8,128)(2,1)S(1)} %copy-done), channel_id=1, source_target_pairs={{0,1},{1,0},{2,3},{3,2},{4,5},{5,4},{6,7},{7,6},{8,9},{9,8},{10,11... | collective-permute-start | bytes 786440 | tf_op jit(solution)/shard_map/ppermute | solution.py:599
  47.9 1.9 %collective-permute-start.6 = (bf16[1024,128]{1,0:T(8,128)(2,1)S(1)}, bf16[1024,128]{1,0:T(8,128)(2,1)S(1)}, u32[]{:S(2)}, u32[]{:S(2)}) collective-permute-start(bf16[1024,128]{1,0:T(8,128)(2,1)S(1)} %collective-permute-done.2.refs_9_), channel_id=1, source_target_pairs={{0,1},{1,0},{2,3},{3,2},{4,5},{5,4},{6,7},{7,6},{8,9},{9,8},{10,11... | collective-permute-start | bytes 786440 | tf_op jit(solution)/shard_map/ppermute | solution.py:599
  48.4 1.8 %collective-permute-start.7 = (bf16[1024,128]{1,0:T(8,128)(2,1)S(1)}, bf16[1024,128]{1,0:T(8,128)(2,1)S(1)}, u32[]{:S(2)}, u32[]{:S(2)}) collective-permute-start(bf16[1024,128]{1,0:T(8,128)(2,1)S(1)} %collective-permute-done.3.refs_10_), channel_id=1, source_target_pairs={{0,1},{1,0},{2,3},{3,2},{4,5},{5,4},{6,7},{7,6},{8,9},{9,8},{10,11... | collective-permute-start | bytes 786440 | tf_op jit(solution)/shard_map/ppermute | solution.py:599
  48.5 2.1 %collective-permute-start.8 = (bf16[1024,128]{1,0:T(8,128)(2,1)S(1)}, bf16[1024,128]{1,0:T(8,128)(2,1)S(1)}, u32[]{:S(2)}, u32[]{:S(2)}) collective-permute-start(bf16[1024,128]{1,0:T(8,128)(2,1)S(1)} %collective-permute-done.4.refs_11_), channel_id=1, source_target_pairs={{0,1},{1,0},{2,3},{3,2},{4,5},{5,4},{6,7},{7,6},{8,9},{9,8},{10,11... | collective-permute-start | bytes 786440 | tf_op jit(solution)/shard_map/ppermute | solution.py:599
  64.3 5.3 %collective-permute-start.9 = (bf16[4,512,128]{2,1,0:T(8,128)(2,1)S(1)}, bf16[4,512,128]{2,1,0:T(8,128)(2,1)S(1)}, u32[]{:S(2)}, u32[]{:S(2)}) collective-permute-start(bf16[4,512,128]{2,1,0:T(8,128)(2,1)S(1)} %slice.12), channel_id=1, source_target_pairs={{0,1},{1,0},{2,3},{3,2},{4,5},{5,4},{6,7},{7,6},{8,9},{9,8},{10,11... | collective-permute-start | bytes 1572872 | tf_op jit(solution)/shard_map/ppermute | solution.py:599
  64.4 5.2 %collective-permute-start.10 = (bf16[4,96,128]{2,1,0:T(8,128)(2,1)S(1)}, bf16[4,96,128]{2,1,0:T(8,128)(2,1)S(1)}, u32[]{:S(2)}, u32[]{:S(2)}) collective-permute-start(bf16[4,96,128]{2,1,0:T(8,128)(2,1)S(1)} %slice.13), channel_id=1, source_target_pairs={{0,16},{16,0},{1,17},{17,1},{2,18},{18,2},{3,19},{19,3},{4,20},{20... | collective-permute-start | bytes 294920 | tf_op jit(solution)/shard_map/ppermute | solution.py:599
  72.3 7.1 %collective-permute-start.11 = (bf16[64,512]{1,0:T(8,128)(2,1)S(1)}, bf16[64,512]{1,0:T(8,128)(2,1)S(1)}, u32[]{:S(2)}, u32[]{:S(2)}) collective-permute-start(bf16[64,512]{1,0:T(8,128)(2,1)S(1)} %get-tuple-element.59), channel_id=1, source_target_pairs={{0,8},{2,10},{4,12},{6,14},{8,0},{10,2},{12,4},{14,6},{1,9},{3,11}... | collective-permute-start | bytes 196616 | tf_op jit(solution)/shard_map/ppermute | solution.py:599
  76.1 11.6 %collective-permute-start.13 = (bf16[4,256,128]{2,1,0:T(8,128)(2,1)S(1)}, bf16[4,256,128]{2,1,0:T(8,128)(2,1)S(1)}, u32[]{:S(2)}, u32[]{:S(2)}) collective-permute-start(bf16[4,256,128]{2,1,0:T(8,128)(2,1)S(1)} %get-tuple-element.77.refs_4_), channel_id=1, source_target_pairs={{0,16},{16,0},{1,17},{17,1},{2,18},{18,2},{3,19},{19,3},{4,20},{20... | collective-permute-start | bytes 786440 | tf_op jit(solution)/shard_map/ppermute | solution.py:599
  77.6 11.8 %collective-permute-start.12 = (bf16[4,256,128]{2,1,0:T(8,128)(2,1)S(1)}, bf16[4,256,128]{2,1,0:T(8,128)(2,1)S(1)}, u32[]{:S(2)}, u32[]{:S(2)}) collective-permute-start(bf16[4,256,128]{2,1,0:T(8,128)(2,1)S(1)} %get-tuple-element.78.refs_0_), channel_id=1, source_target_pairs={{0,16},{16,0},{1,17},{17,1},{2,18},{18,2},{3,19},{19,3},{4,20},{20... | collective-permute-start | bytes 786440 | tf_op jit(solution)/shard_map/ppermute | solution.py:599
  79.4 6.4 %collective-permute-start.15 = (bf16[2,64,512]{2,1,0:T(8,128)(2,1)S(1)}, bf16[2,64,512]{2,1,0:T(8,128)(2,1)S(1)}, u32[]{:S(2)}, u32[]{:S(2)}) collective-permute-start(bf16[2,64,512]{2,1,0:T(8,128)(2,1)S(1)} %get-tuple-element.80), channel_id=1, source_target_pairs={{0,4},{2,6},{4,0},{6,2},{8,12},{10,14},{12,8},{14,10},{1,5},{3,7},... | collective-permute-start | bytes 393224 | tf_op jit(solution)/shard_map/ppermute | solution.py:599
  79.5 6.4 %collective-permute-start.14 = (bf16[2,64,512]{2,1,0:T(8,128)(2,1)S(1)}, bf16[2,64,512]{2,1,0:T(8,128)(2,1)S(1)}, u32[]{:S(2)}, u32[]{:S(2)}) collective-permute-start(bf16[2,64,512]{2,1,0:T(8,128)(2,1)S(1)} %get-tuple-element.80), channel_id=1, source_target_pairs={{0,2},{2,0},{4,6},{6,4},{8,10},{10,8},{12,14},{14,12},{1,3},{3,1},... | collective-permute-start | bytes 393224 | tf_op jit(solution)/shard_map/ppermute | solution.py:599
  80.3 7.4 %collective-permute-start.16 = (bf16[2,64,512]{2,1,0:T(8,128)(2,1)S(1)}, bf16[2,64,512]{2,1,0:T(8,128)(2,1)S(1)}, u32[]{:S(2)}, u32[]{:S(2)}) collective-permute-start(bf16[2,64,512]{2,1,0:T(8,128)(2,1)S(1)} %get-tuple-element.80), channel_id=1, source_target_pairs={{0,6},{2,4},{4,2},{6,0},{8,14},{10,12},{12,10},{14,8},{1,7},{3,5},... | collective-permute-start | bytes 393224 | tf_op jit(solution)/shard_map/ppermute | solution.py:599
  89.5 3.5 %collective-permute-start.17 = (bf16[4,2,64,512]{3,2,1,0:T(8,128)(2,1)S(1)}, bf16[4,2,64,512]{3,2,1,0:T(8,128)(2,1)S(1)}, u32[]{:S(2)}, u32[]{:S(2)}) collective-permute-start(bf16[4,2,64,512]{3,2,1,0:T(8,128)(2,1)S(1)} %pad_maximum_fusion.a), channel_id=1, source_target_pairs={{0,1},{1,0},{2,3},{3,2},{4,5},{5,4},{6,7},{7,6},{8,9},{9,8},{10,11... | collective-permute-start | bytes 1572872 | tf_op jit(solution)/shard_map/ppermute | solution.py:599
  89.5 2.3 %collective-permute-start.20 = (bf16[4,256,128]{2,1,0:T(8,128)(2,1)S(1)}, bf16[4,256,128]{2,1,0:T(8,128)(2,1)S(1)}, u32[]{:S(2)}, u32[]{:S(2)}) collective-permute-start(bf16[4,256,128]{2,1,0:T(8,128)(2,1)S(1)} %get-tuple-element.77.refs_4_), channel_id=1, source_target_pairs={{0,1},{1,0},{2,3},{3,2},{4,5},{5,4},{6,7},{7,6},{8,9},{9,8},{10,11... | collective-permute-start | bytes 786440 | tf_op jit(solution)/shard_map/ppermute | solution.py:599
  90.0 2.1 %collective-permute-start.18 = (bf16[4,256,128]{2,1,0:T(8,128)(2,1)S(1)}, bf16[4,256,128]{2,1,0:T(8,128)(2,1)S(1)}, u32[]{:S(2)}, u32[]{:S(2)}) collective-permute-start(bf16[4,256,128]{2,1,0:T(8,128)(2,1)S(1)} %get-tuple-element.78.refs_0_), channel_id=1, source_target_pairs={{0,1},{1,0},{2,3},{3,2},{4,5},{5,4},{6,7},{7,6},{8,9},{9,8},{10,11... | collective-permute-start | bytes 786440 | tf_op jit(solution)/shard_map/ppermute | solution.py:599
  90.1 2.4 %collective-permute-start.19 = (bf16[4,256,128]{2,1,0:T(8,128)(2,1)S(1)}, bf16[4,256,128]{2,1,0:T(8,128)(2,1)S(1)}, u32[]{:S(2)}, u32[]{:S(2)}) collective-permute-start(bf16[4,256,128]{2,1,0:T(8,128)(2,1)S(1)} %collective-permute-done.12.refs_1_), channel_id=1, source_target_pairs={{0,1},{1,0},{2,3},{3,2},{4,5},{5,4},{6,7},{7,6},{8,9},{9,8},{10,11... | collective-permute-start | bytes 786440 | tf_op jit(solution)/shard_map/ppermute | solution.py:599
  90.6 2.4 %collective-permute-start.21 = (bf16[4,256,128]{2,1,0:T(8,128)(2,1)S(1)}, bf16[4,256,128]{2,1,0:T(8,128)(2,1)S(1)}, u32[]{:S(2)}, u32[]{:S(2)}) collective-permute-start(bf16[4,256,128]{2,1,0:T(8,128)(2,1)S(1)} %collective-permute-done.13.refs_5_), channel_id=1, source_target_pairs={{0,1},{1,0},{2,3},{3,2},{4,5},{5,4},{6,7},{7,6},{8,9},{9,8},{10,11... | collective-permute-start | bytes 786440 | tf_op jit(solution)/shard_map/ppermute | solution.py:599
  98.2 5.6 %collective-permute-start.22 = (bf16[2,64,512]{2,1,0:T(8,128)(2,1)S(1)}, bf16[2,64,512]{2,1,0:T(8,128)(2,1)S(1)}, u32[]{:S(2)}, u32[]{:S(2)}) collective-permute-start(bf16[2,64,512]{2,1,0:T(8,128)(2,1)S(1)} %get-tuple-element.72), channel_id=1, source_target_pairs={{0,2},{2,0},{4,6},{6,4},{8,10},{10,8},{12,14},{14,12},{1,3},{3,1},... | collective-permute-start | bytes 393224 | tf_op jit(solution)/shard_map/ppermute | solution.py:599
  99.0 6.4 %collective-permute-start.23 = (bf16[2,64,512]{2,1,0:T(8,128)(2,1)S(1)}, bf16[2,64,512]{2,1,0:T(8,128)(2,1)S(1)}, u32[]{:S(2)}, u32[]{:S(2)}) collective-permute-start(bf16[2,64,512]{2,1,0:T(8,128)(2,1)S(1)} %get-tuple-element.73), channel_id=1, source_target_pairs={{0,4},{2,6},{4,0},{6,2},{8,12},{10,14},{12,8},{14,10},{1,5},{3,7},... | collective-permute-start | bytes 393224 | tf_op jit(solution)/shard_map/ppermute | solution.py:599
  99.6 8.2 %collective-permute-start.24 = (bf16[2,64,512]{2,1,0:T(8,128)(2,1)S(1)}, bf16[2,64,512]{2,1,0:T(8,128)(2,1)S(1)}, u32[]{:S(2)}, u32[]{:S(2)}) collective-permute-start(bf16[2,64,512]{2,1,0:T(8,128)(2,1)S(1)} %get-tuple-element.74), channel_id=1, source_target_pairs={{0,6},{2,4},{4,2},{6,0},{8,14},{10,12},{12,10},{14,8},{1,7},{3,5},... | collective-permute-start | bytes 393224 | tf_op jit(solution)/shard_map/ppermute | solution.py:599
  107.9 5.9 %collective-permute-start.25 = (bf16[64,512]{1,0:T(8,128)(2,1)S(1)}, bf16[64,512]{1,0:T(8,128)(2,1)S(1)}, u32[]{:S(2)}, u32[]{:S(2)}) collective-permute-start(bf16[64,512]{1,0:T(8,128)(2,1)S(1)} %get-tuple-element.76), channel_id=1, source_target_pairs={{0,8},{2,10},{4,12},{6,14},{8,0},{10,2},{12,4},{14,6},{1,9},{3,11}... | collective-permute-start | bytes 196616 | tf_op jit(solution)/shard_map/ppermute | solution.py:599
  (2 other events, 4.6 us)

commit v14 on v13

--- a/solution.py
+++ b/solution.py
@@ -321,22 +321,22 @@
 
 
 def near_kernel(n, rank_ref, qkv_ref, out_weight_ref, up_ref, down_ref, *refs):
-    near, (heads_ref, sem) = refs[: n // 2], refs[n // 2 :]
-    rank = rank_ref[0]
-    half = n // 2
+    near, sem = refs[: n // 2], refs[n // 2]
+    rank, part = rank_ref[0], rank_ref[2]
     rows = up_ref.shape[0]
     wide = up_ref.shape[1] // n
     units = wide // 2
-    long = out_weight_ref.shape[0]
-    copies = [(qkv_ref.at[pl.ds(rank // half * half, half)], heads_ref)]
-    for j in range(half):
+    long = out_weight_ref.shape[0] // 2
+    copies = []
+    for j in range(n // 2):
         dest = rank ^ j
-        for c in range(2):
-            at = pl.ds(pl.multiple_of(dest * wide + c * units, 128), units)
-            copies.append((up_ref.at[:, at], near[j].at[pl.ds(c * rows, rows)]))
-        at = pl.ds(pl.multiple_of(dest * wide, 128), wide)
-        copies.append((down_ref.at[at], near[j].at[pl.ds(2 * rows, wide)]))
-        copies.append((out_weight_ref, near[j].at[pl.ds(2 * rows + wide, long)]))
+        at = pl.ds(pl.multiple_of(dest * wide + part * units, 128), units)
+        copies.append((up_ref.at[:, at], near[j].at[pl.ds(0, rows)]))
+        copies.append((down_ref.at[at], near[j].at[pl.ds(rows, units)]))
+        at = pl.ds(pl.multiple_of(part * long, 128), long)
+        copies.append((out_weight_ref.at[at], near[j].at[pl.ds(rows + units, long)]))
+        low = rows + units + long
+        copies.append((qkv_ref.at[dest], near[j].at[pl.ds(low, qkv_ref.shape[1])]))
     run_copies(copies, sem)()
 
 
@@ -360,38 +360,34 @@
 
 def pack_near(scalars, qkv, out_weight, up, down, n):
     half = n // 2
-    near = (2 * up.shape[0] + up.shape[1] // n + out_weight.shape[0], 128)
-    shapes = [near] * half + [(half,) + qkv.shape[1:]]
+    rows = up.shape[0] + up.shape[1] // n // 2 + out_weight.shape[0] // 2 + qkv.shape[1]
     kernel = functools.partial(near_kernel, n)
-    outs = pack(kernel, shapes, 4 * half + 1, scalars, qkv, out_weight, up, down)
-    return list(outs[:half]), outs[half]
-
-
-def fan_kernel(owned_ref, across_ref, heads_ref, far_ref, out_ref):
+    return pack(kernel, [(rows, 128)] * half, 4 * half, scalars, qkv, out_weight, up, down)
+
+
+def fan_kernel(owned_ref, across_ref, far_ref, out_ref):
     rows = owned_ref.shape[0]
-    count, head_rows = heads_ref.shape[:2]
-    top = 2 * rows + head_rows
+    count = out_ref.shape[0]
+    top = 2 * rows
     rest = out_ref.shape[1] - top
     each = (far_ref.shape[0] - rest) // (count - 1)
     for d in range(count):
         out_ref[d, :rows] = owned_ref[...]
-        out_ref[d, rows : 2 * rows] = across_ref[...]
-        out_ref[d, 2 * rows : top] = heads_ref[d]
+        out_ref[d, rows:top] = across_ref[...]
         out_ref[d, top : top + each] = far_ref[d * each : (d + 1) * each]
         out_ref[d, top + each :] = far_ref[count * each :]
 
 
-def fan(owned, across, heads, far, out_rows):
-    count = heads.shape[0]
+def fan(owned, across, far, out_rows, count):
     each = (far.shape[0] - out_rows) // count
-    shape = struct((count, 2 * owned.shape[0] + heads.shape[1] + each + out_rows, 128))
+    shape = struct((count, 2 * owned.shape[0] + each + out_rows, 128))
     return pl.pallas_call(
         fan_kernel,
-        in_specs=[vspec()] * 4,
+        in_specs=[vspec()] * 3,
         out_specs=vspec(),
         out_shape=shape,
         compiler_params=params(8),
-    )(owned, across, heads, far)
+    )(owned, across, far)
 
 
 def source_of(rank, n, q, k):
@@ -404,7 +400,9 @@
     return (x - average) * lax.rsqrt(power - average * average + 1e-06)
 
 
-def attend_kernel(n, part, rank_ref, mine_ref, other_ref, far_ref, tokens_ref, out_ref, weight_ref):
+def attend_kernel(
+    n, part, rank_ref, mine_ref, other_ref, near_ref, far_ref, tokens_ref, out_ref, weight_ref
+):
     rank, half, group = rank_ref[0], rank_ref[1], rank_ref[2]
     rows = other_ref.shape[1] // 2
     cuts = rows // part
@@ -421,11 +419,11 @@
                 tokens_ref[at, to] = mine_ref[q, cut]
                 to = pl.ds(pl.multiple_of((1 - half) * width + c * 128, 128), 128)
                 tokens_ref[at, to] = other_ref[q, cut]
-        to = pl.ds(pl.multiple_of(source_of(rank, n, q, 0) * 128, 128), 128)
-        weight_ref[:, to] = mine_ref[q, 2 * rows : 2 * rows + depth]
+        to = pl.ds(pl.multiple_of((rank ^ q) * 128, 128), 128)
+        weight_ref[:, to] = near_ref[q]
         to = pl.ds(pl.multiple_of(source_of(rank, n, q, 1) * 128, 128), 128)
         at = pl.ds(pl.multiple_of(group * piece, 32), piece)
-        weight_ref[at, to] = mine_ref[q, 2 * rows + depth : 2 * rows + depth + piece]
+        weight_ref[at, to] = mine_ref[q, 2 * rows : 2 * rows + piece]
         at = pl.ds(pl.multiple_of((1 - group) * piece, 32), piece)
         weight_ref[at, to] = far_ref[q]
     normed = norm_rows(tokens_ref[...].astype(F32)).astype(BF16)
@@ -447,19 +445,19 @@
     out_ref[...] = attended
 
 
-def attend_fast(scalars, mine, other, far, head_rows, per_owner, n):
+def attend_fast(scalars, mine, other, near, far, head_rows, per_owner, n):
     length = n * per_owner
     depth = other.shape[1] // (2 * per_owner) * 256
     size = head_rows // 3
     return pl.pallas_call(
         functools.partial(attend_kernel, n, per_owner),
-        in_specs=[sspec()] + [vspec()] * 3,
+        in_specs=[sspec()] + [vspec()] * 4,
         out_specs=[vspec()] * 2,
         out_shape=[struct((length, depth)), struct((size, length))],
         scratch_shapes=[VMEM((head_rows, n * 128), BF16)],
         compiler_params=params(12),
         cost_estimate=cost(30),
-    )(scalars, mine, other, far)
+    )(scalars, mine, other, near, far)
 
 
 def mlp_kernel(n, rank_ref, tokens_ref, pieces, far, outs_far, near, outs, scratch):
@@ -477,14 +475,14 @@
         at = pl.ds(pl.multiple_of(source * block, block), block)
         to = pl.ds(pl.multiple_of(source * 128, 128), 128)
         for core in range(2):
-            ref = near[core][j]
             for c in range(2):
-                units = pl.ds(core * wide + c * unit, unit)
-                later.append((ref.at[pl.ds(c * block, block)], up_ref.at[at, units]))
-            units = pl.ds(core * wide, wide)
-            later.append((ref.at[pl.ds(2 * block, wide)], down_ref.at[units, to]))
-            rows_from = ref.at[pl.ds(2 * block + wide, 2 * rows)]
-            first.append((rows_from, whole_ref.at[core, :, to]))
+                ref = near[core][c]
+                units = pl.ds(pl.multiple_of(core * wide + (group ^ c) * unit, unit), unit)
+                later.append((ref.at[j, pl.ds(0, block)], up_ref.at[at, units]))
+                later.append((ref.at[j, pl.ds(block, unit)], down_ref.at[units, to]))
+                rows_to = pl.ds(pl.multiple_of((group ^ c) * rows, rows), rows)
+                rows_from = ref.at[j, pl.ds(block + unit, rows)]
+                first.append((rows_from, whole_ref.at[core, rows_to, to]))
         source = source_of(rank, n, j, 1)
         at = pl.ds(pl.multiple_of(source * block, block), block)
         to = pl.ds(pl.multiple_of(source * 128, 128), 128)
@@ -539,12 +537,12 @@
     def kernel(scalars, tokens, a, b, *refs):
         far, refs = (refs[:2], refs[2:4]), refs[4:]
         outs_far, refs = (refs[:2], refs[2:4]), refs[4:]
-        near, refs = (refs[:half], refs[half:n]), refs[n:]
+        near, refs = (refs[:2], refs[2:4]), refs[4:]
         mlp_kernel(n, scalars, tokens, (a, b), far, outs_far, near, refs[: half + 1], refs[half + 1 :])
 
     return pl.pallas_call(
         kernel,
-        in_specs=[sspec()] + [vspec()] * 3 + [aspec()] * (8 + n),
+        in_specs=[sspec()] + [vspec()] * 3 + [aspec()] * 12,
         out_specs=[vspec()] * (half + 1),
         out_shape=[struct((length // n, width), F32)] * 2
         + [struct((2, length // n, width))] * (half - 1),
@@ -554,7 +552,7 @@
             VMEM((length, depth), F32),
             VMEM((2, inner, depth), BF16),
             VMEM((2, inner, length), BF16),
-            pltpu.SemaphoreType.DMA((20 * half,)),
+            pltpu.SemaphoreType.DMA((24 * half,)),
         ],
         compiler_params=params(24),
     )(scalars, tokens, *pieces, *far[0], *far[1], *outs_far[0], *outs_far[1], *near[0], *near[1])
@@ -637,26 +635,31 @@
     slots = prep(scalars, keep_list, after(flat, away), n, sup, capacity)
     dealt = exchange(slots)
     weights = lax.optimization_barrier((*weights, slots))[:4]
-    near, qkv_near = pack_near(scalars, *weights, n)
+    near = pack_near(scalars, *weights, n)
     near = [near[0]] + [swap(near[j], "seq", j) for j in range(1, half)]
     owned = pick(scalars, keep_list, dealt, n, sup, per_owner, capacity)
     across = swap(owned, "seq", half)
     across, far, *near = lax.optimization_barrier((across, far, *near))
 
     out_rows = out_weight.shape[0] // 2
-    got = exchange_half(fan(owned, across, qkv_near, far, out_rows))
-    near_other = [swap(block, "head", 1) for block in near]
-    got, *near_other = lax.optimization_barrier((got, *near_other))
+    got = exchange_half(fan(owned, across, far, out_rows, half))
+    near_qkv = jnp.stack([block[block.shape[0] - head_rows :] for block in near])
+    near_mine = jnp.stack([block[: block.shape[0] - head_rows] for block in near])
+    near_other = swap(near_mine, "groups", 1)
+    near_pair = swap(near_mine, "head", 1)
+    got, near_qkv, near_other, near_pair = lax.optimization_barrier(
+        (got, near_qkv, near_other, near_pair)
+    )
 
     top = 2 * owned.shape[0]
     pieces_other = swap(got[:, :top], "head", 1)
-    top = top + head_rows
     qkv_far = swap(got[:, top : top + head_rows // 2], "groups", 1)
     tokens, attended = attend_fast(
-        scalars, got, pieces_other, qkv_far, head_rows, per_owner, n
+        scalars, got, pieces_other, near_qkv, qkv_far, head_rows, per_owner, n
     )
 
     att_across = swap(attended, "seq", half)
+    att_across, near_last = lax.optimization_barrier((att_across, swap(near_other, "head", 1)))
     got = after(got, attended)
     mlp_mine = got[:, top + head_rows // 2 : got.shape[1] - out_rows]
     far_mine = got[:, got.shape[1] - out_rows :]
@@ -674,7 +677,7 @@
         (gathered, swap(gathered, "head", 1)),
         (mlp_pair, tuple(swap(value, "head", 1) for value in mlp_pair)),
         (far_pair, tuple(swap(value, "head", 1) for value in far_pair)),
-        (near, near_other),
+        ((near_mine, near_other), (near_pair, near_last)),
         n,
     )
     terms = [swap(terms[j - 1], "seq", j) for j in range(1, half)]

time: 115 us -> 107 us (0.930)
  waiting for transfers between devices: 57.9 us -> 49.9 us
  starting transfers between devices: 35.7 us -> 36.9 us
    all_to_all x1, waiting for transfers between devices: 13.7 us -> 0.23 us  [exchange_half(): lax.all_to_all(value, 'seq', split_axis=0, concat_axis=0, axis_index_grou...]
    ppermute x26 -> x25, waiting for transfers between devices: 34 us -> 39 us  [swap(): return lax.ppermute(value, axis, [(i, i ^ j) for i in range(n)])]
    ppermute x26 -> x25, starting transfers between devices: 28.2 us -> 29.4 us  [swap(): return lax.ppermute(value, axis, [(i, i ^ j) for i in range(n)])]
  transfers between devices with their start and end apart: 28 -> 27, of which waited for: 21 -> 20; matrix products, arithmetic and copies ran while one was open for 0% -> 0% of each run, Pallas kernels for 5% -> 8%
where the time goes in v14:
time: 107 us; the launch traced here: 106 us
  waiting for transfers between devices  49.9 us (47%)
  starting transfers between devices  36.9 us (34%)
  Pallas kernels  18.4 us (17%)
    ppermute x25, waiting for transfers between devices, swap(): return lax.ppermute(value, axis, [(i, i ^ j) for i in range(n)])  39 us
    ppermute x25, starting transfers between devices, swap(): return lax.ppermute(value, axis, [(i, i ^ j) for i in range(n)])  29.4 us
    all_to_all x1, waiting for transfers between devices, exchange(): return lax.all_to_all(value, 'seq', split_axis=0, concat_axis=0, tiled=True)  10.7 us
    pallas_call x2, Pallas kernels, pack(): pl.pallas_call(kernel, in_specs=[sspec()] + [hspec()] * 4, out_specs=[vsp...  5.53 us
    pallas_call x1, Pallas kernels, mlp(): pl.pallas_call(kernel, in_specs=[sspec()] + [vspec()] * 3 + [aspec()] * 1...  5.45 us
    all_to_all x1, starting transfers between devices, exchange(): return lax.all_to_all(value, 'seq', split_axis=0, concat_axis=0, tiled=True)  3.81 us
    all_to_all x1, starting transfers between devices, exchange_half(): lax.all_to_all(value, 'seq', split_axis=0, concat_axis=0, axis_index_grou...  3.66 us
    pallas_call x1, Pallas kernels, attend_fast(): pl.pallas_call(functools.partial(attend_kernel, n, per_owner), in_specs=[...  2.68 us
  transfers between devices with their start and end apart: 27, of which 20 were waited for; matrix products, arithmetic and copies ran while one was open for 0% of the time, Pallas kernels for 8%

profile of v14, /device:TPU:0, one launch (start us, length us, event | category | flops | bytes accessed | tf_op | source)
XLA Modules:
  0.0 106.5 jit_solution(3629347329376377559)
XLA Ops:
  0.7 2.7 %shard_map.64 = bf16[1664,128]{1,0:T(8,128)(2,1)} custom-call(s32[3]{0:T(128)} %pad_add_fusion.rank_ref.scalars, bf16[8,192,128]{2,1,0:T(8,128)(2,1)} %bitcast.32, bf16[512,128]{1,0:T(8,128)(2,1)} %out_weight_ref.2, bf16[128,2048]{1,0:T(8,128)(2,1)} %up_ref.2, bf16[2048,128]{1,0:T(8,128)(2,1)} %down_ref.2), custom_call_target="tpu_custom_call" | custom-call | tf_op jit(solution)/shard_map/pallas_call | solution.py:344
  3.4 4.1 %collective-permute-start.1 = (bf16[1664,128]{1,0:T(8,128)(2,1)}, bf16[1664,128]{1,0:T(8,128)(2,1)S(1)}, u32[]{:S(2)}, u32[]{:S(2)}) collective-permute-start(bf16[1664,128]{1,0:T(8,128)(2,1)} %shard_map.64), channel_id=1, source_target_pairs={{0,8},{2,10},{4,12},{6,14},{8,0},{10,2},{12,4},{14,6},{1,9},{3,11}... | collective-permute-start | bytes 1277960 | tf_op jit(solution)/shard_map/ppermute | solution.py:597
  7.6 2.0 %shard_map.65 = bf16[640,128]{1,0:T(8,128)(2,1)} custom-call(s32[3]{0:T(128)S(1)} %copy-done, s32[1,64]{1,0:T(1,128)S(1)} %copy-done.2, bf16[160,1024]{1,0:T(8,128)(2,1)S(1)} %reshape.8.patches_ref), custom_call_target="tpu_custom_call" | custom-call | tf_op jit(solution)/shard_map/pallas_call | solution.py:247
  9.6 3.8 %all-to-all-start = ((bf16[8,80,128]{2,1,0:T(8,128)(2,1)}), bf16[8,80,128]{2,1,0:T(8,128)(2,1)S(1)}, u32[]{:S(2)}, u32[]{:S(2)}) async-start(bf16[8,80,128]{2,1,0:T(8,128)(2,1)} %bitcast.4), calls=%async_computation | async-start | bytes 327680 | tf_op jit(solution)/shard_map/all_to_all | solution.py:601
  13.4 2.8 %shard_map.67 = (bf16[704,128]{1,0:T(8,128)(2,1)}, bf16[704,128]{1,0:T(8,128)(2,1)}, bf16[704,128]{1,0:T(8,128)(2,1)}, bf16[704,128]{1,0:T(8,128)(2,1)}) custom-call(s32[3]{0:T(128)} %pad_add_fusion.rank_ref.scalars, bf16[8,192,128]{2,1,0:T(8,128)(2,1)} %bitcast.33, bf16[512,128]{1,0:T(8,128)(2,1)} %out_weight_ref.2, bf16[128,2048]{1,0:T(8,128)(2,1)} %up_ref.2, ...), custom_call_target="tpu_custom_call" | custom-call | tf_op jit(solution)/shard_map/pallas_call | solution.py:344
  16.2 2.1 %collective-permute-start.2 = (bf16[704,128]{1,0:T(8,128)(2,1)}, bf16[704,128]{1,0:T(8,128)(2,1)S(1)}, u32[]{:S(2)}, u32[]{:S(2)}) collective-permute-start(bf16[704,128]{1,0:T(8,128)(2,1)} %get-tuple-element.47), channel_id=1, source_target_pairs={{0,2},{2,0},{4,6},{6,4},{8,10},{10,8},{12,14},{14,12},{1,3},{3,1},... | collective-permute-start | bytes 540680 | tf_op jit(solution)/shard_map/ppermute | solution.py:597
  18.3 1.5 %collective-permute-start.3 = (bf16[704,128]{1,0:T(8,128)(2,1)}, bf16[704,128]{1,0:T(8,128)(2,1)S(1)}, u32[]{:S(2)}, u32[]{:S(2)}) collective-permute-start(bf16[704,128]{1,0:T(8,128)(2,1)} %get-tuple-element.48), channel_id=1, source_target_pairs={{0,4},{2,6},{4,0},{6,2},{8,12},{10,14},{12,8},{14,10},{1,5},{3,7},... | collective-permute-start | bytes 540680 | tf_op jit(solution)/shard_map/ppermute | solution.py:597
  19.9 10.7 %all-to-all-done = bf16[8,80,128]{2,1,0:T(8,128)(2,1)S(1)} async-done(((bf16[8,80,128]{2,1,0:T(8,128)(2,1)}), bf16[8,80,128]{2,1,0:T(8,128)(2,1)S(1)}, u32[]{:S(2)}, u32[]{:S(2)}) %all-to-all-start) | async-done | bytes 163872 | tf_op jit(solution)/shard_map/all_to_all | solution.py:601
  31.5 2.9 %collective-permute-start = (bf16[256,128]{1,0:T(8,128)(2,1)S(1)}, bf16[256,128]{1,0:T(8,128)(2,1)S(1)}, u32[]{:S(2)}, u32[]{:S(2)}) collective-permute-start(bf16[256,128]{1,0:T(8,128)(2,1)S(1)} %shard_map.66.owned_ref), channel_id=1, source_target_pairs={{0,8},{2,10},{4,12},{6,14},{8,0},{10,2},{12,4},{14,6},{1,9},{3,11}... | collective-permute-start | bytes 196616 | tf_op jit(solution)/shard_map/ppermute | solution.py:597
  34.4 3.2 %collective-permute-done.4 = bf16[704,128]{1,0:T(8,128)(2,1)S(1)} collective-permute-done((bf16[704,128]{1,0:T(8,128)(2,1)}, bf16[704,128]{1,0:T(8,128)(2,1)S(1)}, u32[]{:S(2)}, u32[]{:S(2)}) %collective-permute-start.4) | collective-permute-done | bytes 180256 | tf_op jit(solution)/shard_map/ppermute | solution.py:597
  39.2 3.7 %all-to-all-start.1 = ((bf16[4,1120,128]{2,1,0:T(8,128)(2,1)}), bf16[4,1120,128]{2,1,0:T(8,128)(2,1)S(1)}, u32[]{:S(2)}, u32[]{:S(2)}) async-start(bf16[4,1120,128]{2,1,0:T(8,128)(2,1)} %shard_map.68), calls=%async_computation.1 | async-start | bytes 2293760 | tf_op jit(solution)/shard_map/all_to_all | solution.py:607
  43.1 1.6 %collective-permute-start.5 = (bf16[4,512,128]{2,1,0:T(8,128)(2,1)S(1)}, bf16[4,512,128]{2,1,0:T(8,128)(2,1)S(1)}, u32[]{:S(2)}, u32[]{:S(2)}) collective-permute-start(bf16[4,512,128]{2,1,0:T(8,128)(2,1)S(1)} %pad_maximum_fusion.refs_8_), channel_id=1, source_target_pairs={{0,16},{16,0},{1,17},{17,1},{2,18},{18,2},{3,19},{19,3},{4,20},{20... | collective-permute-start | bytes 1572872 | tf_op jit(solution)/shard_map/ppermute | solution.py:597
  45.0 12.4 %collective-permute-done.5.refs_9_ = bf16[4,512,128]{2,1,0:T(8,128)(2,1)S(1)} collective-permute-done((bf16[4,512,128]{2,1,0:T(8,128)(2,1)S(1)}, bf16[4,512,128]{2,1,0:T(8,128)(2,1)S(1)}, u32[]{:S(2)}, u32[]{:S(2)}) %collective-permute-start.5) | collective-permute-done | bytes 524320 | tf_op jit(solution)/shard_map/ppermute | solution.py:597
  57.8 1.6 %collective-permute-start.8 = (bf16[4,96,128]{2,1,0:T(8,128)(2,1)S(1)}, bf16[4,96,128]{2,1,0:T(8,128)(2,1)S(1)}, u32[]{:S(2)}, u32[]{:S(2)}) collective-permute-start(bf16[4,96,128]{2,1,0:T(8,128)(2,1)S(1)} %slice.45), channel_id=1, source_target_pairs={{0,16},{16,0},{1,17},{17,1},{2,18},{18,2},{3,19},{19,3},{4,20},{20... | collective-permute-start | bytes 294920 | tf_op jit(solution)/shard_map/ppermute | solution.py:597
  59.5 3.5 %collective-permute-done.8.far_ref = bf16[4,96,128]{2,1,0:T(8,128)(2,1)S(1)} collective-permute-done((bf16[4,96,128]{2,1,0:T(8,128)(2,1)S(1)}, bf16[4,96,128]{2,1,0:T(8,128)(2,1)S(1)}, u32[]{:S(2)}, u32[]{:S(2)}) %collective-permute-start.8) | collective-permute-done | bytes 98336 | tf_op jit(solution)/shard_map/ppermute | solution.py:597
  63.0 2.7 %shard_map.69 = (bf16[512,1024]{1,0:T(8,128)(2,1)S(1)}, bf16[64,512]{1,0:T(8,128)(2,1)S(1)}) custom-call(s32[3]{0:T(128)S(1)} %copy-done.1, bf16[4,1120,128]{2,1,0:T(8,128)(2,1)S(1)} %all-to-all-done.1.mine_ref, bf16[4,512,128]{2,1,0:T(8,128)(2,1)S(1)} %collective-permute-done.7.other_ref, bf16[4,192,128]{2,1,0:T(8,128)(2,1)S(1)} %pad_maximum_fusion.2.near_ref, ...), custom_call_target="tpu_custom_call" | custom-call | flops 30000001024 | bytes 1048576 | tf_op jit(solution)/shard_map/pallas_call | solution.py:452
  65.7 2.9 %collective-permute-start.9 = (bf16[64,512]{1,0:T(8,128)(2,1)S(1)}, bf16[64,512]{1,0:T(8,128)(2,1)S(1)}, u32[]{:S(2)}, u32[]{:S(2)}) collective-permute-start(bf16[64,512]{1,0:T(8,128)(2,1)S(1)} %get-tuple-element.59), channel_id=1, source_target_pairs={{0,8},{2,10},{4,12},{6,14},{8,0},{10,2},{12,4},{14,6},{1,9},{3,11}... | collective-permute-start | bytes 196616 | tf_op jit(solution)/shard_map/ppermute | solution.py:597
  68.6 1.6 %collective-permute-start.12 = (bf16[4,256,128]{2,1,0:T(8,128)(2,1)S(1)}, bf16[4,256,128]{2,1,0:T(8,128)(2,1)S(1)}, u32[]{:S(2)}, u32[]{:S(2)}) collective-permute-start(bf16[4,256,128]{2,1,0:T(8,128)(2,1)S(1)} %get-tuple-element.77.refs_4_), channel_id=1, source_target_pairs={{0,16},{16,0},{1,17},{17,1},{2,18},{18,2},{3,19},{19,3},{4,20},{20... | collective-permute-start | bytes 786440 | tf_op jit(solution)/shard_map/ppermute | solution.py:597
  70.7 1.6 %collective-permute-done.9 = bf16[64,512]{1,0:T(8,128)(2,1)S(1)} collective-permute-done((bf16[64,512]{1,0:T(8,128)(2,1)S(1)}, bf16[64,512]{1,0:T(8,128)(2,1)S(1)}, u32[]{:S(2)}, u32[]{:S(2)}) %collective-permute-start.9) | collective-permute-done | bytes 65568 | tf_op jit(solution)/shard_map/ppermute | solution.py:597
  72.8 1.7 %collective-permute-start.13 = (bf16[2,64,512]{2,1,0:T(8,128)(2,1)S(1)}, bf16[2,64,512]{2,1,0:T(8,128)(2,1)S(1)}, u32[]{:S(2)}, u32[]{:S(2)}) collective-permute-start(bf16[2,64,512]{2,1,0:T(8,128)(2,1)S(1)} %get-tuple-element.80), channel_id=1, source_target_pairs={{0,2},{2,0},{4,6},{6,4},{8,10},{10,8},{12,14},{14,12},{1,3},{3,1},... | collective-permute-start | bytes 393224 | tf_op jit(solution)/shard_map/ppermute | solution.py:597
  74.4 1.5 %collective-permute-start.15 = (bf16[2,64,512]{2,1,0:T(8,128)(2,1)S(1)}, bf16[2,64,512]{2,1,0:T(8,128)(2,1)S(1)}, u32[]{:S(2)}, u32[]{:S(2)}) collective-permute-start(bf16[2,64,512]{2,1,0:T(8,128)(2,1)S(1)} %get-tuple-element.80), channel_id=1, source_target_pairs={{0,6},{2,4},{4,2},{6,0},{8,14},{10,12},{12,10},{14,8},{1,7},{3,5},... | collective-permute-start | bytes 393224 | tf_op jit(solution)/shard_map/ppermute | solution.py:597
  75.9 2.0 %collective-permute-done.14 = bf16[2,64,512]{2,1,0:T(8,128)(2,1)S(1)} collective-permute-done((bf16[2,64,512]{2,1,0:T(8,128)(2,1)S(1)}, bf16[2,64,512]{2,1,0:T(8,128)(2,1)S(1)}, u32[]{:S(2)}, u32[]{:S(2)}) %collective-permute-start.14) | collective-permute-done | bytes 131104 | tf_op jit(solution)/shard_map/ppermute | solution.py:597
  78.9 1.4 %collective-permute-done.15 = bf16[2,64,512]{2,1,0:T(8,128)(2,1)S(1)} collective-permute-done((bf16[2,64,512]{2,1,0:T(8,128)(2,1)S(1)}, bf16[2,64,512]{2,1,0:T(8,128)(2,1)S(1)}, u32[]{:S(2)}, u32[]{:S(2)}) %collective-permute-start.15) | collective-permute-done | bytes 131104 | tf_op jit(solution)/shard_map/ppermute | solution.py:597
  80.3 1.6 %collective-permute-done.11.refs_1_ = bf16[4,256,128]{2,1,0:T(8,128)(2,1)S(1)} collective-permute-done((bf16[4,256,128]{2,1,0:T(8,128)(2,1)S(1)}, bf16[4,256,128]{2,1,0:T(8,128)(2,1)S(1)}, u32[]{:S(2)}, u32[]{:S(2)}) %collective-permute-start.11) | collective-permute-done | bytes 262176 | tf_op jit(solution)/shard_map/ppermute | solution.py:597
  85.5 5.5 %shard_map.70 = (f32[64,512]{1,0:T(8,128)S(1)}, f32[64,512]{1,0:T(8,128)S(1)}, bf16[2,64,512]{2,1,0:T(8,128)(2,1)S(1)}, bf16[2,64,512]{2,1,0:T(8,128)(2,1)S(1)}, bf16[2,64,512]{2,1,0:T(8,128)(2,1)S(1)}) custom-call(s32[3]{0:T(128)S(1)} %copy-done.1, bf16[512,1024]{1,0:T(8,128)(2,1)S(1)} %get-tuple-element.58.tokens, ...), custom_call_target="tpu_custom_call" | custom-call | tf_op jit(solution)/shard_map/pallas_call | solution.py:543
  91.0 1.7 %collective-permute-start.21 = (bf16[2,64,512]{2,1,0:T(8,128)(2,1)S(1)}, bf16[2,64,512]{2,1,0:T(8,128)(2,1)S(1)}, u32[]{:S(2)}, u32[]{:S(2)}) collective-permute-start(bf16[2,64,512]{2,1,0:T(8,128)(2,1)S(1)} %get-tuple-element.72), channel_id=1, source_target_pairs={{0,2},{2,0},{4,6},{6,4},{8,10},{10,8},{12,14},{14,12},{1,3},{3,1},... | collective-permute-start | bytes 393224 | tf_op jit(solution)/shard_map/ppermute | solution.py:597
  92.7 1.5 %collective-permute-start.22 = (bf16[2,64,512]{2,1,0:T(8,128)(2,1)S(1)}, bf16[2,64,512]{2,1,0:T(8,128)(2,1)S(1)}, u32[]{:S(2)}, u32[]{:S(2)}) collective-permute-start(bf16[2,64,512]{2,1,0:T(8,128)(2,1)S(1)} %get-tuple-element.73), channel_id=1, source_target_pairs={{0,4},{2,6},{4,0},{6,2},{8,12},{10,14},{12,8},{14,10},{1,5},{3,7},... | collective-permute-start | bytes 393224 | tf_op jit(solution)/shard_map/ppermute | solution.py:597
  94.5 2.1 %collective-permute-done.21.refs_0_ = bf16[2,64,512]{2,1,0:T(8,128)(2,1)S(1)} collective-permute-done((bf16[2,64,512]{2,1,0:T(8,128)(2,1)S(1)}, bf16[2,64,512]{2,1,0:T(8,128)(2,1)S(1)}, u32[]{:S(2)}, u32[]{:S(2)}) %collective-permute-start.21) | collective-permute-done | bytes 131104 | tf_op jit(solution)/shard_map/ppermute | solution.py:597
  96.6 2.5 %collective-permute-done.22.refs_1_ = bf16[2,64,512]{2,1,0:T(8,128)(2,1)S(1)} collective-permute-done((bf16[2,64,512]{2,1,0:T(8,128)(2,1)S(1)}, bf16[2,64,512]{2,1,0:T(8,128)(2,1)S(1)}, u32[]{:S(2)}, u32[]{:S(2)}) %collective-permute-start.22) | collective-permute-done | bytes 131104 | tf_op jit(solution)/shard_map/ppermute | solution.py:597
  99.1 1.5 %collective-permute-done.23.refs_2_ = bf16[2,64,512]{2,1,0:T(8,128)(2,1)S(1)} collective-permute-done((bf16[2,64,512]{2,1,0:T(8,128)(2,1)S(1)}, bf16[2,64,512]{2,1,0:T(8,128)(2,1)S(1)}, u32[]{:S(2)}, u32[]{:S(2)}) %collective-permute-start.23) | collective-permute-done | bytes 131104 | tf_op jit(solution)/shard_map/ppermute | solution.py:597
  100.6 2.1 %collective-permute-start.24 = (bf16[64,512]{1,0:T(8,128)(2,1)S(1)}, bf16[64,512]{1,0:T(8,128)(2,1)S(1)}, u32[]{:S(2)}, u32[]{:S(2)}) collective-permute-start(bf16[64,512]{1,0:T(8,128)(2,1)S(1)} %get-tuple-element.76), channel_id=1, source_target_pairs={{0,8},{2,10},{4,12},{6,14},{8,0},{10,2},{12,4},{14,6},{1,9},{3,11}... | collective-permute-start | bytes 196616 | tf_op jit(solution)/shard_map/ppermute | solution.py:597
  102.7 3.2 %collective-permute-done.24.across_ref = bf16[64,512]{1,0:T(8,128)(2,1)S(1)} collective-permute-done((bf16[64,512]{1,0:T(8,128)(2,1)S(1)}, bf16[64,512]{1,0:T(8,128)(2,1)S(1)}, u32[]{:S(2)}, u32[]{:S(2)}) %collective-permute-start.24) | collective-permute-done | bytes 65568 | tf_op jit(solution)/shard_map/ppermute | solution.py:597
  (54 shorter events, 10.9 us)
Async XLA Ops:
  0.0 7.5 %copy-start.3 = (bf16[1,40,4,1024]{3,2,1,0:T(4,128)(2,1)S(1)}, bf16[1,40,4,1024]{3,2,1,0:T(4,128)(2,1)}, u32[]{:S(2)}) copy-start(bf16[1,40,4,1024]{3,2,1,0:T(4,128)(2,1)} %param.6) | copy-start | bytes 983044
  0.7 6.9 %copy-start = (s32[3]{0:T(128)S(1)}, s32[3]{0:T(128)}, u32[]{:S(2)}) copy-start(s32[3]{0:T(128)} %pad_add_fusion.rank_ref.scalars) | copy-start | bytes 40
  0.7 6.9 %copy-start.2 = (s32[1,64]{1,0:T(1,128)S(1)}, s32[1,64]{1,0:T(1,128)}, u32[]{:S(2)}) copy-start(s32[1,64]{1,0:T(1,128)} %keep_ref.3) | copy-start | bytes 772
  3.4 34.6 %collective-permute-start.1 = (bf16[1664,128]{1,0:T(8,128)(2,1)}, bf16[1664,128]{1,0:T(8,128)(2,1)S(1)}, u32[]{:S(2)}, u32[]{:S(2)}) collective-permute-start(bf16[1664,128]{1,0:T(8,128)(2,1)} %shard_map.64), channel_id=1, source_target_pairs={{0,8},{2,10},{4,12},{6,14},{8,0},{10,2},{12,4},{14,6},{1,9},{3,11}... | collective-permute-start | bytes 1277960 | tf_op jit(solution)/shard_map/ppermute | solution.py:597
  7.6 23.0 %copy-start.1 = (s32[3]{0:T(128)S(1)}, s32[3]{0:T(128)}, u32[]{:S(2)}) copy-start(s32[3]{0:T(128)} %pad_add_fusion.rank_ref.scalars) | copy-start | bytes 40
  9.6 21.0 %all-to-all-start = ((bf16[8,80,128]{2,1,0:T(8,128)(2,1)}), bf16[8,80,128]{2,1,0:T(8,128)(2,1)S(1)}, u32[]{:S(2)}, u32[]{:S(2)}) async-start(bf16[8,80,128]{2,1,0:T(8,128)(2,1)} %bitcast.4), calls=%async_computation | async-start | bytes 327680 | tf_op jit(solution)/shard_map/all_to_all | solution.py:601
  16.2 18.2 %collective-permute-start.2 = (bf16[704,128]{1,0:T(8,128)(2,1)}, bf16[704,128]{1,0:T(8,128)(2,1)S(1)}, u32[]{:S(2)}, u32[]{:S(2)}) collective-permute-start(bf16[704,128]{1,0:T(8,128)(2,1)} %get-tuple-element.47), channel_id=1, source_target_pairs={{0,2},{2,0},{4,6},{6,4},{8,10},{10,8},{12,14},{14,12},{1,3},{3,1},... | collective-permute-start | bytes 540680 | tf_op jit(solution)/shard_map/ppermute | solution.py:597
  18.3 16.1 %collective-permute-start.3 = (bf16[704,128]{1,0:T(8,128)(2,1)}, bf16[704,128]{1,0:T(8,128)(2,1)S(1)}, u32[]{:S(2)}, u32[]{:S(2)}) collective-permute-start(bf16[704,128]{1,0:T(8,128)(2,1)} %get-tuple-element.48), channel_id=1, source_target_pairs={{0,4},{2,6},{4,0},{6,2},{8,12},{10,14},{12,8},{14,10},{1,5},{3,7},... | collective-permute-start | bytes 540680 | tf_op jit(solution)/shard_map/ppermute | solution.py:597
  19.8 17.8 %collective-permute-start.4 = (bf16[704,128]{1,0:T(8,128)(2,1)}, bf16[704,128]{1,0:T(8,128)(2,1)S(1)}, u32[]{:S(2)}, u32[]{:S(2)}) collective-permute-start(bf16[704,128]{1,0:T(8,128)(2,1)} %get-tuple-element.49), channel_id=1, source_target_pairs={{0,6},{2,4},{4,2},{6,0},{8,14},{10,12},{12,10},{14,8},{1,7},{3,5},... | collective-permute-start | bytes 540680 | tf_op jit(solution)/shard_map/ppermute | solution.py:597
  31.5 6.5 %collective-permute-start = (bf16[256,128]{1,0:T(8,128)(2,1)S(1)}, bf16[256,128]{1,0:T(8,128)(2,1)S(1)}, u32[]{:S(2)}, u32[]{:S(2)}) collective-permute-start(bf16[256,128]{1,0:T(8,128)(2,1)S(1)} %shard_map.66.owned_ref), channel_id=1, source_target_pairs={{0,8},{2,10},{4,12},{6,14},{8,0},{10,2},{12,4},{14,6},{1,9},{3,11}... | collective-permute-start | bytes 196616 | tf_op jit(solution)/shard_map/ppermute | solution.py:597
  39.2 3.7 %copy-start.4 = (bf16[704,128]{1,0:T(8,128)(2,1)S(1)}, bf16[704,128]{1,0:T(8,128)(2,1)}, u32[]{:S(2)}) copy-start(bf16[704,128]{1,0:T(8,128)(2,1)} %get-tuple-element.52) | copy-start | bytes 540676
  39.2 18.5 %all-to-all-start.1 = ((bf16[4,1120,128]{2,1,0:T(8,128)(2,1)}), bf16[4,1120,128]{2,1,0:T(8,128)(2,1)S(1)}, u32[]{:S(2)}, u32[]{:S(2)}) async-start(bf16[4,1120,128]{2,1,0:T(8,128)(2,1)} %shard_map.68), calls=%async_computation.1 | async-start | bytes 2293760 | tf_op jit(solution)/shard_map/all_to_all | solution.py:607
  43.0 2.0 %collective-permute-start.6 = (bf16[4,512,128]{2,1,0:T(8,128)(2,1)S(1)}, bf16[4,512,128]{2,1,0:T(8,128)(2,1)S(1)}, u32[]{:S(2)}, u32[]{:S(2)}) collective-permute-start(bf16[4,512,128]{2,1,0:T(8,128)(2,1)S(1)} %pad_maximum_fusion.refs_8_), channel_id=1, source_target_pairs={{0,1},{1,0},{2,3},{3,2},{4,5},{5,4},{6,7},{7,6},{8,9},{9,8},{10,11... | collective-permute-start | bytes 1572872 | tf_op jit(solution)/shard_map/ppermute | solution.py:597
  43.1 14.3 %collective-permute-start.5 = (bf16[4,512,128]{2,1,0:T(8,128)(2,1)S(1)}, bf16[4,512,128]{2,1,0:T(8,128)(2,1)S(1)}, u32[]{:S(2)}, u32[]{:S(2)}) collective-permute-start(bf16[4,512,128]{2,1,0:T(8,128)(2,1)S(1)} %pad_maximum_fusion.refs_8_), channel_id=1, source_target_pairs={{0,16},{16,0},{1,17},{17,1},{2,18},{18,2},{3,19},{19,3},{4,20},{20... | collective-permute-start | bytes 1572872 | tf_op jit(solution)/shard_map/ppermute | solution.py:597
  57.7 5.3 %collective-permute-start.7 = (bf16[4,512,128]{2,1,0:T(8,128)(2,1)S(1)}, bf16[4,512,128]{2,1,0:T(8,128)(2,1)S(1)}, u32[]{:S(2)}, u32[]{:S(2)}) collective-permute-start(bf16[4,512,128]{2,1,0:T(8,128)(2,1)S(1)} %slice.44), channel_id=1, source_target_pairs={{0,1},{1,0},{2,3},{3,2},{4,5},{5,4},{6,7},{7,6},{8,9},{9,8},{10,11... | collective-permute-start | bytes 1572872 | tf_op jit(solution)/shard_map/ppermute | solution.py:597
  57.8 5.2 %collective-permute-start.8 = (bf16[4,96,128]{2,1,0:T(8,128)(2,1)S(1)}, bf16[4,96,128]{2,1,0:T(8,128)(2,1)S(1)}, u32[]{:S(2)}, u32[]{:S(2)}) collective-permute-start(bf16[4,96,128]{2,1,0:T(8,128)(2,1)S(1)} %slice.45), channel_id=1, source_target_pairs={{0,16},{16,0},{1,17},{17,1},{2,18},{18,2},{3,19},{19,3},{4,20},{20... | collective-permute-start | bytes 294920 | tf_op jit(solution)/shard_map/ppermute | solution.py:597
  59.3 11.4 %collective-permute-start.10 = (bf16[4,512,128]{2,1,0:T(8,128)(2,1)S(1)}, bf16[4,512,128]{2,1,0:T(8,128)(2,1)S(1)}, u32[]{:S(2)}, u32[]{:S(2)}) collective-permute-start(bf16[4,512,128]{2,1,0:T(8,128)(2,1)S(1)} %collective-permute-done.5.refs_9_), channel_id=1, source_target_pairs={{0,1},{1,0},{2,3},{3,2},{4,5},{5,4},{6,7},{7,6},{8,9},{9,8},{10,11... | collective-permute-start | bytes 1572872 | tf_op jit(solution)/shard_map/ppermute | solution.py:597
  65.7 6.6 %collective-permute-start.9 = (bf16[64,512]{1,0:T(8,128)(2,1)S(1)}, bf16[64,512]{1,0:T(8,128)(2,1)S(1)}, u32[]{:S(2)}, u32[]{:S(2)}) collective-permute-start(bf16[64,512]{1,0:T(8,128)(2,1)S(1)} %get-tuple-element.59), channel_id=1, source_target_pairs={{0,8},{2,10},{4,12},{6,14},{8,0},{10,2},{12,4},{14,6},{1,9},{3,11}... | collective-permute-start | bytes 196616 | tf_op jit(solution)/shard_map/ppermute | solution.py:597
  68.6 11.7 %collective-permute-start.12 = (bf16[4,256,128]{2,1,0:T(8,128)(2,1)S(1)}, bf16[4,256,128]{2,1,0:T(8,128)(2,1)S(1)}, u32[]{:S(2)}, u32[]{:S(2)}) collective-permute-start(bf16[4,256,128]{2,1,0:T(8,128)(2,1)S(1)} %get-tuple-element.77.refs_4_), channel_id=1, source_target_pairs={{0,16},{16,0},{1,17},{17,1},{2,18},{18,2},{3,19},{19,3},{4,20},{20... | collective-permute-start | bytes 786440 | tf_op jit(solution)/shard_map/ppermute | solution.py:597
  70.2 11.8 %collective-permute-start.11 = (bf16[4,256,128]{2,1,0:T(8,128)(2,1)S(1)}, bf16[4,256,128]{2,1,0:T(8,128)(2,1)S(1)}, u32[]{:S(2)}, u32[]{:S(2)}) collective-permute-start(bf16[4,256,128]{2,1,0:T(8,128)(2,1)S(1)} %get-tuple-element.78.refs_0_), channel_id=1, source_target_pairs={{0,16},{16,0},{1,17},{17,1},{2,18},{18,2},{3,19},{19,3},{4,20},{20... | collective-permute-start | bytes 786440 | tf_op jit(solution)/shard_map/ppermute | solution.py:597
  72.4 5.5 %collective-permute-start.14 = (bf16[2,64,512]{2,1,0:T(8,128)(2,1)S(1)}, bf16[2,64,512]{2,1,0:T(8,128)(2,1)S(1)}, u32[]{:S(2)}, u32[]{:S(2)}) collective-permute-start(bf16[2,64,512]{2,1,0:T(8,128)(2,1)S(1)} %get-tuple-element.80), channel_id=1, source_target_pairs={{0,4},{2,6},{4,0},{6,2},{8,12},{10,14},{12,8},{14,10},{1,5},{3,7},... | collective-permute-start | bytes 393224 | tf_op jit(solution)/shard_map/ppermute | solution.py:597
  72.8 6.1 %collective-permute-start.13 = (bf16[2,64,512]{2,1,0:T(8,128)(2,1)S(1)}, bf16[2,64,512]{2,1,0:T(8,128)(2,1)S(1)}, u32[]{:S(2)}, u32[]{:S(2)}) collective-permute-start(bf16[2,64,512]{2,1,0:T(8,128)(2,1)S(1)} %get-tuple-element.80), channel_id=1, source_target_pairs={{0,2},{2,0},{4,6},{6,4},{8,10},{10,8},{12,14},{14,12},{1,3},{3,1},... | collective-permute-start | bytes 393224 | tf_op jit(solution)/shard_map/ppermute | solution.py:597
  74.4 5.9 %collective-permute-start.15 = (bf16[2,64,512]{2,1,0:T(8,128)(2,1)S(1)}, bf16[2,64,512]{2,1,0:T(8,128)(2,1)S(1)}, u32[]{:S(2)}, u32[]{:S(2)}) collective-permute-start(bf16[2,64,512]{2,1,0:T(8,128)(2,1)S(1)} %get-tuple-element.80), channel_id=1, source_target_pairs={{0,6},{2,4},{4,2},{6,0},{8,14},{10,12},{12,10},{14,8},{1,7},{3,5},... | collective-permute-start | bytes 393224 | tf_op jit(solution)/shard_map/ppermute | solution.py:597
  82.0 3.5 %collective-permute-start.16 = (bf16[4,2,64,512]{3,2,1,0:T(8,128)(2,1)S(1)}, bf16[4,2,64,512]{3,2,1,0:T(8,128)(2,1)S(1)}, u32[]{:S(2)}, u32[]{:S(2)}) collective-permute-start(bf16[4,2,64,512]{3,2,1,0:T(8,128)(2,1)S(1)} %pad_maximum_fusion.1.a), channel_id=1, source_target_pairs={{0,1},{1,0},{2,3},{3,2},{4,5},{5,4},{6,7},{7,6},{8,9},{9,8},{10,11... | collective-permute-start | bytes 1572872 | tf_op jit(solution)/shard_map/ppermute | solution.py:597
  82.1 2.3 %collective-permute-start.19 = (bf16[4,256,128]{2,1,0:T(8,128)(2,1)S(1)}, bf16[4,256,128]{2,1,0:T(8,128)(2,1)S(1)}, u32[]{:S(2)}, u32[]{:S(2)}) collective-permute-start(bf16[4,256,128]{2,1,0:T(8,128)(2,1)S(1)} %get-tuple-element.77.refs_4_), channel_id=1, source_target_pairs={{0,1},{1,0},{2,3},{3,2},{4,5},{5,4},{6,7},{7,6},{8,9},{9,8},{10,11... | collective-permute-start | bytes 786440 | tf_op jit(solution)/shard_map/ppermute | solution.py:597
  82.6 2.1 %collective-permute-start.17 = (bf16[4,256,128]{2,1,0:T(8,128)(2,1)S(1)}, bf16[4,256,128]{2,1,0:T(8,128)(2,1)S(1)}, u32[]{:S(2)}, u32[]{:S(2)}) collective-permute-start(bf16[4,256,128]{2,1,0:T(8,128)(2,1)S(1)} %get-tuple-element.78.refs_0_), channel_id=1, source_target_pairs={{0,1},{1,0},{2,3},{3,2},{4,5},{5,4},{6,7},{7,6},{8,9},{9,8},{10,11... | collective-permute-start | bytes 786440 | tf_op jit(solution)/shard_map/ppermute | solution.py:597
  82.7 2.4 %collective-permute-start.18 = (bf16[4,256,128]{2,1,0:T(8,128)(2,1)S(1)}, bf16[4,256,128]{2,1,0:T(8,128)(2,1)S(1)}, u32[]{:S(2)}, u32[]{:S(2)}) collective-permute-start(bf16[4,256,128]{2,1,0:T(8,128)(2,1)S(1)} %collective-permute-done.11.refs_1_), channel_id=1, source_target_pairs={{0,1},{1,0},{2,3},{3,2},{4,5},{5,4},{6,7},{7,6},{8,9},{9,8},{10,11... | collective-permute-start | bytes 786440 | tf_op jit(solution)/shard_map/ppermute | solution.py:597
  83.1 2.4 %collective-permute-start.20 = (bf16[4,256,128]{2,1,0:T(8,128)(2,1)S(1)}, bf16[4,256,128]{2,1,0:T(8,128)(2,1)S(1)}, u32[]{:S(2)}, u32[]{:S(2)}) collective-permute-start(bf16[4,256,128]{2,1,0:T(8,128)(2,1)S(1)} %collective-permute-done.12.refs_5_), channel_id=1, source_target_pairs={{0,1},{1,0},{2,3},{3,2},{4,5},{5,4},{6,7},{7,6},{8,9},{9,8},{10,11... | collective-permute-start | bytes 786440 | tf_op jit(solution)/shard_map/ppermute | solution.py:597
  91.0 5.6 %collective-permute-start.21 = (bf16[2,64,512]{2,1,0:T(8,128)(2,1)S(1)}, bf16[2,64,512]{2,1,0:T(8,128)(2,1)S(1)}, u32[]{:S(2)}, u32[]{:S(2)}) collective-permute-start(bf16[2,64,512]{2,1,0:T(8,128)(2,1)S(1)} %get-tuple-element.72), channel_id=1, source_target_pairs={{0,2},{2,0},{4,6},{6,4},{8,10},{10,8},{12,14},{14,12},{1,3},{3,1},... | collective-permute-start | bytes 393224 | tf_op jit(solution)/shard_map/ppermute | solution.py:597
  92.7 6.4 %collective-permute-start.22 = (bf16[2,64,512]{2,1,0:T(8,128)(2,1)S(1)}, bf16[2,64,512]{2,1,0:T(8,128)(2,1)S(1)}, u32[]{:S(2)}, u32[]{:S(2)}) collective-permute-start(bf16[2,64,512]{2,1,0:T(8,128)(2,1)S(1)} %get-tuple-element.73), channel_id=1, source_target_pairs={{0,4},{2,6},{4,0},{6,2},{8,12},{10,14},{12,8},{14,10},{1,5},{3,7},... | collective-permute-start | bytes 393224 | tf_op jit(solution)/shard_map/ppermute | solution.py:597
  94.2 6.4 %collective-permute-start.23 = (bf16[2,64,512]{2,1,0:T(8,128)(2,1)S(1)}, bf16[2,64,512]{2,1,0:T(8,128)(2,1)S(1)}, u32[]{:S(2)}, u32[]{:S(2)}) collective-permute-start(bf16[2,64,512]{2,1,0:T(8,128)(2,1)S(1)} %get-tuple-element.74), channel_id=1, source_target_pairs={{0,6},{2,4},{4,2},{6,0},{8,14},{10,12},{12,10},{14,8},{1,7},{3,5},... | collective-permute-start | bytes 393224 | tf_op jit(solution)/shard_map/ppermute | solution.py:597
  100.6 5.2 %collective-permute-start.24 = (bf16[64,512]{1,0:T(8,128)(2,1)S(1)}, bf16[64,512]{1,0:T(8,128)(2,1)S(1)}, u32[]{:S(2)}, u32[]{:S(2)}) collective-permute-start(bf16[64,512]{1,0:T(8,128)(2,1)S(1)} %get-tuple-element.76), channel_id=1, source_target_pairs={{0,8},{2,10},{4,12},{6,14},{8,0},{10,2},{12,4},{14,6},{1,9},{3,11}... | collective-permute-start | bytes 196616 | tf_op jit(solution)/shard_map/ppermute | solution.py:597

commit v15 on v14

--- a/solution.py
+++ b/solution.py
@@ -297,7 +297,7 @@
     )(scalars, keep_list, got)
 
 
-def far_kernel(n, rank_ref, qkv_ref, out_weight_ref, up_ref, down_ref, away_ref, sem):
+def far_kernel(n, rank_ref, qkv_ref, out_weight_ref, up_ref, down_ref, away_ref, blocks_ref, sem):
     rank, part = rank_ref[0], rank_ref[2]
     half = n // 2
     rows = up_ref.shape[0]
@@ -305,18 +305,16 @@
     units = wide // 2
     long = out_weight_ref.shape[0] // 2
     depth = qkv_ref.shape[1] // 2
-    each = depth + rows + units
     copies = []
     for d in range(half):
         dest = (rank // half ^ 1) * half + d
-        low = d * each
         at = pl.ds(pl.multiple_of(part * depth, 32), depth)
-        copies.append((qkv_ref.at[dest, at], away_ref.at[pl.ds(low, depth)]))
+        copies.append((qkv_ref.at[dest, at], away_ref.at[pl.ds(d * depth, depth)]))
         at = pl.ds(pl.multiple_of(dest * wide + part * units, 128), units)
-        copies.append((up_ref.at[:, at], away_ref.at[pl.ds(low + depth, rows)]))
-        copies.append((down_ref.at[at], away_ref.at[pl.ds(low + depth + rows, units)]))
+        copies.append((up_ref.at[:, at], blocks_ref.at[d, pl.ds(0, rows)]))
+        copies.append((down_ref.at[at], blocks_ref.at[d, pl.ds(rows, units)]))
     at = pl.ds(pl.multiple_of(part * long, 128), long)
-    copies.append((out_weight_ref.at[at], away_ref.at[pl.ds(half * each, long)]))
+    copies.append((out_weight_ref.at[at], away_ref.at[pl.ds(half * depth, long)]))
     run_copies(copies, sem)()
 
 
@@ -352,10 +350,10 @@
 
 def pack_far(scalars, qkv, out_weight, up, down, n):
     half = n // 2
-    each = qkv.shape[1] // 2 + up.shape[0] + up.shape[1] // n // 2
-    shapes = [(half * each + out_weight.shape[0] // 2, 128)]
+    away = (half * qkv.shape[1] // 2 + out_weight.shape[0] // 2, 128)
+    blocks = (half, up.shape[0] + up.shape[1] // n // 2, 128)
     kernel = functools.partial(far_kernel, n)
-    return pack(kernel, shapes, 3 * half + 1, scalars, qkv, out_weight, up, down)[0]
+    return pack(kernel, [away, blocks], 3 * half + 1, scalars, qkv, out_weight, up, down)
 
 
 def pack_near(scalars, qkv, out_weight, up, down, n):
@@ -630,7 +628,7 @@
     heads = qkv_weight.transpose(1, 2, 0)
 
     weights = (heads, out_weight, up_weight, down_weight)
-    away = pack_far(scalars, *weights, n)
+    away, blocks = pack_far(scalars, *weights, n)
     far = swap(away, "seq", half)
     slots = prep(scalars, keep_list, after(flat, away), n, sup, capacity)
     dealt = exchange(slots)
@@ -642,26 +640,29 @@
     across, far, *near = lax.optimization_barrier((across, far, *near))
 
     out_rows = out_weight.shape[0] // 2
+    mlp_far = swap(after(blocks, across), "seq", half)
     got = exchange_half(fan(owned, across, far, out_rows, half))
     near_qkv = jnp.stack([block[block.shape[0] - head_rows :] for block in near])
     near_mine = jnp.stack([block[: block.shape[0] - head_rows] for block in near])
     near_other = swap(near_mine, "groups", 1)
     near_pair = swap(near_mine, "head", 1)
-    got, near_qkv, near_other, near_pair = lax.optimization_barrier(
-        (got, near_qkv, near_other, near_pair)
+    got, mlp_far, near_qkv, near_other, near_pair = lax.optimization_barrier(
+        (got, mlp_far, near_qkv, near_other, near_pair)
     )
 
     top = 2 * owned.shape[0]
     pieces_other = swap(got[:, :top], "head", 1)
     qkv_far = swap(got[:, top : top + head_rows // 2], "groups", 1)
+    mlp_mine = exchange_half(mlp_far)
     tokens, attended = attend_fast(
         scalars, got, pieces_other, near_qkv, qkv_far, head_rows, per_owner, n
     )
 
     att_across = swap(attended, "seq", half)
-    att_across, near_last = lax.optimization_barrier((att_across, swap(near_other, "head", 1)))
+    att_across, near_last, mlp_mine = lax.optimization_barrier(
+        (att_across, swap(near_other, "head", 1), mlp_mine)
+    )
     got = after(got, attended)
-    mlp_mine = got[:, top + head_rows // 2 : got.shape[1] - out_rows]
     far_mine = got[:, got.shape[1] - out_rows :]
     far_other = swap(far_mine, "groups", 1)
     mlp_other = swap(mlp_mine, "groups", 1)

time: 107 us -> 112 us (1.047)
  waiting for transfers between devices: 49.9 us -> 40.9 us
  starting transfers between devices: 36.9 us -> 43.3 us
  local copies, waits for them, and re-layouts: 0.23 us -> 6.01 us
    all_to_all x1, waiting for transfers between devices: 10.7 us -> 0.01 us  [exchange(): return lax.all_to_all(value, 'seq', split_axis=0, concat_axis=0, tiled=True)]
    unnamed x10 -> x20, local copies, waits for them, and re-layouts: 0.02 us -> 4.04 us
    all_to_all x1, starting transfers between devices: 3.81 us -> 7.28 us  [exchange(): return lax.all_to_all(value, 'seq', split_axis=0, concat_axis=0, tiled=True)]
    all_to_all x1 -> x2, starting transfers between devices: 3.66 us -> 7.04 us  [exchange_half(): lax.all_to_all(value, 'seq', split_axis=0, concat_axis=0, axis_index_grou...]
    all_to_all x1 -> x2, waiting for transfers between devices: 0.23 us -> 2.13 us  [exchange_half(): lax.all_to_all(value, 'seq', split_axis=0, concat_axis=0, axis_index_grou...]
    ppermute x25 -> x26, starting transfers between devices: 29.4 us -> 28.9 us  [swap(): return lax.ppermute(value, axis, [(i, i ^ j) for i in range(n)])]
    ppermute x25 -> x26, waiting for transfers between devices: 39 us -> 38.8 us  [swap(): return lax.ppermute(value, axis, [(i, i ^ j) for i in range(n)])]
  transfers between devices with their start and end apart: 27 -> 29, of which waited for: 20 -> 16; matrix products, arithmetic and copies ran while one was open for 0% -> 1% of each run, Pallas kernels for 8% -> 6%
where the time goes in v15:
time: 112 us; the launch traced here: 111 us
  starting transfers between devices  43.3 us (39%)
  waiting for transfers between devices  40.9 us (37%)
  Pallas kernels  19 us (17%)
  local copies, waits for them, and re-layouts  6.01 us (5%)
  other arithmetic  1.62 us (1%)
    ppermute x26, waiting for transfers between devices, swap(): return lax.ppermute(value, axis, [(i, i ^ j) for i in range(n)])  38.8 us
    ppermute x26, starting transfers between devices, swap(): return lax.ppermute(value, axis, [(i, i ^ j) for i in range(n)])  28.9 us
    all_to_all x1, starting transfers between devices, exchange(): return lax.all_to_all(value, 'seq', split_axis=0, concat_axis=0, tiled=True)  7.28 us
    all_to_all x2, starting transfers between devices, exchange_half(): lax.all_to_all(value, 'seq', split_axis=0, concat_axis=0, axis_index_grou...  7.04 us
    pallas_call x2, Pallas kernels, pack(): pl.pallas_call(kernel, in_specs=[sspec()] + [hspec()] * 4, out_specs=[vsp...  5.55 us
    pallas_call x1, Pallas kernels, mlp(): pl.pallas_call(kernel, in_specs=[sspec()] + [vspec()] * 3 + [aspec()] * 1...  5.49 us
    unnamed x20, local copies, waits for them, and re-layouts  4.04 us
    pallas_call x1, Pallas kernels, attend_fast(): pl.pallas_call(functools.partial(attend_kernel, n, per_owner), in_specs=[...  3.31 us
  transfers between devices with their start and end apart: 29, of which 16 were waited for; matrix products, arithmetic and copies ran while one was open for 1% of the time, Pallas kernels for 6%

profile of v15, /device:TPU:0, one launch (start us, length us, event | category | flops | bytes accessed | tf_op | source)
XLA Modules:
  0.0 111.0 jit_solution(1108739396815454798)
XLA Ops:
  1.6 2.6 %shard_map.64 = (bf16[640,128]{1,0:T(8,128)(2,1)}, bf16[4,256,128]{2,1,0:T(8,128)(2,1)}) custom-call(s32[3]{0:T(128)} %pad_add_fusion.rank_ref.scalars, bf16[8,192,128]{2,1,0:T(8,128)(2,1)} %bitcast.31, bf16[512,128]{1,0:T(8,128)(2,1)} %out_weight_ref.2, bf16[128,2048]{1,0:T(8,128)(2,1)} %up_ref.2, bf16[2048,128]{1,0:T(8,128)(2,1)} %down_ref.2), custom_call_target="tpu_custom_call" | custom-call | tf_op jit(solution)/shard_map/pallas_call | solution.py:342
  4.9 2.0 %shard_map.65 = bf16[640,128]{1,0:T(8,128)(2,1)} custom-call(s32[3]{0:T(128)S(1)} %copy-done, s32[1,64]{1,0:T(1,128)S(1)} %copy-done.2, bf16[160,1024]{1,0:T(8,128)(2,1)S(1)} %reshape.8.patches_ref), custom_call_target="tpu_custom_call" | custom-call | tf_op jit(solution)/shard_map/pallas_call | solution.py:247
  6.9 7.3 %all-to-all-start = ((bf16[8,80,128]{2,1,0:T(8,128)(2,1)}), bf16[8,80,128]{2,1,0:T(8,128)(2,1)S(1)}, u32[]{:S(2)}, u32[]{:S(2)}) async-start(bf16[8,80,128]{2,1,0:T(8,128)(2,1)} %bitcast.4), calls=%async_computation | async-start | bytes 327680 | tf_op jit(solution)/shard_map/all_to_all | solution.py:599
  14.2 3.0 %shard_map.67 = (bf16[704,128]{1,0:T(8,128)(2,1)}, bf16[704,128]{1,0:T(8,128)(2,1)}, bf16[704,128]{1,0:T(8,128)(2,1)}, bf16[704,128]{1,0:T(8,128)(2,1)}) custom-call(s32[3]{0:T(128)} %pad_add_fusion.rank_ref.scalars, bf16[8,192,128]{2,1,0:T(8,128)(2,1)} %bitcast.32, bf16[512,128]{1,0:T(8,128)(2,1)} %out_weight_ref.2, bf16[128,2048]{1,0:T(8,128)(2,1)} %up_ref.2, ...), custom_call_target="tpu_custom_call" | custom-call | tf_op jit(solution)/shard_map/pallas_call | solution.py:342
  17.1 2.1 %collective-permute-start.2 = (bf16[704,128]{1,0:T(8,128)(2,1)}, bf16[704,128]{1,0:T(8,128)(2,1)S(1)}, u32[]{:S(2)}, u32[]{:S(2)}) collective-permute-start(bf16[704,128]{1,0:T(8,128)(2,1)} %get-tuple-element.53), channel_id=1, source_target_pairs={{0,2},{2,0},{4,6},{6,4},{8,10},{10,8},{12,14},{14,12},{1,3},{3,1},... | collective-permute-start | bytes 540680 | tf_op jit(solution)/shard_map/ppermute | solution.py:595
  19.2 1.5 %collective-permute-start.3 = (bf16[704,128]{1,0:T(8,128)(2,1)}, bf16[704,128]{1,0:T(8,128)(2,1)S(1)}, u32[]{:S(2)}, u32[]{:S(2)}) collective-permute-start(bf16[704,128]{1,0:T(8,128)(2,1)} %get-tuple-element.54), channel_id=1, source_target_pairs={{0,4},{2,6},{4,0},{6,2},{8,12},{10,14},{12,8},{14,10},{1,5},{3,7},... | collective-permute-start | bytes 540680 | tf_op jit(solution)/shard_map/ppermute | solution.py:595
  20.8 2.8 %collective-permute-start.1 = (bf16[640,128]{1,0:T(8,128)(2,1)S(1)}, bf16[640,128]{1,0:T(8,128)(2,1)S(1)}, u32[]{:S(2)}, u32[]{:S(2)}) collective-permute-start(bf16[640,128]{1,0:T(8,128)(2,1)S(1)} %copy-done.9), channel_id=1, source_target_pairs={{0,8},{2,10},{4,12},{6,14},{8,0},{10,2},{12,4},{14,6},{1,9},{3,11}... | collective-permute-start | bytes 491528 | tf_op jit(solution)/shard_map/ppermute | solution.py:595
  24.7 7.3 %collective-permute-done.1.far_ref = bf16[640,128]{1,0:T(8,128)(2,1)S(1)} collective-permute-done((bf16[640,128]{1,0:T(8,128)(2,1)S(1)}, bf16[640,128]{1,0:T(8,128)(2,1)S(1)}, u32[]{:S(2)}, u32[]{:S(2)}) %collective-permute-start.1) | collective-permute-done | bytes 163872 | tf_op jit(solution)/shard_map/ppermute | solution.py:595
  31.9 2.2 %collective-permute-done.4 = bf16[704,128]{1,0:T(8,128)(2,1)S(1)} collective-permute-done((bf16[704,128]{1,0:T(8,128)(2,1)}, bf16[704,128]{1,0:T(8,128)(2,1)S(1)}, u32[]{:S(2)}, u32[]{:S(2)}) %collective-permute-start.4) | collective-permute-done | bytes 180256 | tf_op jit(solution)/shard_map/ppermute | solution.py:595
  35.1 3.6 %all-to-all-start.1 = ((bf16[4,864,128]{2,1,0:T(8,128)(2,1)}), bf16[4,864,128]{2,1,0:T(8,128)(2,1)S(1)}, u32[]{:S(2)}, u32[]{:S(2)}) async-start(bf16[4,864,128]{2,1,0:T(8,128)(2,1)} %shard_map.68), calls=%async_computation.1 | async-start | bytes 1769472 | tf_op jit(solution)/shard_map/all_to_all | solution.py:605
  39.0 1.6 %collective-permute-start.6 = (bf16[4,512,128]{2,1,0:T(8,128)(2,1)S(1)}, bf16[4,512,128]{2,1,0:T(8,128)(2,1)}, u32[]{:S(2)}, u32[]{:S(2)}) collective-permute-start(bf16[4,512,128]{2,1,0:T(8,128)(2,1)S(1)} %pad_maximum_fusion.refs_8_), channel_id=1, source_target_pairs={{0,16},{16,0},{1,17},{17,1},{2,18},{18,2},{3,19},{19,3},{4,20},{20... | collective-permute-start | bytes 1572872 | tf_op jit(solution)/shard_map/ppermute | solution.py:595
  40.6 2.0 %collective-permute-start.5 = (bf16[4,256,128]{2,1,0:T(8,128)(2,1)S(1)}, bf16[4,256,128]{2,1,0:T(8,128)(2,1)}, u32[]{:S(2)}, u32[]{:S(2)}) collective-permute-start(bf16[4,256,128]{2,1,0:T(8,128)(2,1)S(1)} %copy-done.8), channel_id=1, source_target_pairs={{0,8},{2,10},{4,12},{6,14},{8,0},{10,2},{12,4},{14,6},{1,9},{3,11}... | collective-permute-start | bytes 786440 | tf_op jit(solution)/shard_map/ppermute | solution.py:595
  42.6 10.9 %collective-permute-done.5 = bf16[4,256,128]{2,1,0:T(8,128)(2,1)} collective-permute-done((bf16[4,256,128]{2,1,0:T(8,128)(2,1)S(1)}, bf16[4,256,128]{2,1,0:T(8,128)(2,1)}, u32[]{:S(2)}, u32[]{:S(2)}) %collective-permute-start.5) | collective-permute-done | bytes 262176 | tf_op jit(solution)/shard_map/ppermute | solution.py:595
  53.6 2.1 %all-to-all-done.1.mine_ref = bf16[4,864,128]{2,1,0:T(8,128)(2,1)S(1)} async-done(((bf16[4,864,128]{2,1,0:T(8,128)(2,1)}), bf16[4,864,128]{2,1,0:T(8,128)(2,1)S(1)}, u32[]{:S(2)}, u32[]{:S(2)}) %all-to-all-start.1) | async-done | bytes 884768 | tf_op jit(solution)/shard_map/all_to_all | solution.py:605
  56.5 1.6 %collective-permute-start.9 = (bf16[4,96,128]{2,1,0:T(8,128)(2,1)S(1)}, bf16[4,96,128]{2,1,0:T(8,128)(2,1)S(1)}, u32[]{:S(2)}, u32[]{:S(2)}) collective-permute-start(bf16[4,96,128]{2,1,0:T(8,128)(2,1)S(1)} %slice.42), channel_id=1, source_target_pairs={{0,16},{16,0},{1,17},{17,1},{2,18},{18,2},{3,19},{19,3},{4,20},{20... | collective-permute-start | bytes 294920 | tf_op jit(solution)/shard_map/ppermute | solution.py:595
  58.1 3.4 %all-to-all-start.2 = ((bf16[4,256,128]{2,1,0:T(8,128)(2,1)}), bf16[4,256,128]{2,1,0:T(8,128)(2,1)S(1)}, u32[]{:S(2)}, u32[]{:S(2)}) async-start(bf16[4,256,128]{2,1,0:T(8,128)(2,1)} %collective-permute-done.5), calls=%async_computation.2 | async-start | bytes 524288 | tf_op jit(solution)/shard_map/all_to_all | solution.py:605
  65.2 3.3 %shard_map.69 = (bf16[512,1024]{1,0:T(8,128)(2,1)S(1)}, bf16[64,512]{1,0:T(8,128)(2,1)}) custom-call(s32[3]{0:T(128)S(1)} %copy-done.1, bf16[4,864,128]{2,1,0:T(8,128)(2,1)S(1)} %all-to-all-done.1.mine_ref, bf16[4,512,128]{2,1,0:T(8,128)(2,1)S(1)} %copy-done.4, bf16[4,192,128]{2,1,0:T(8,128)(2,1)S(1)} %pad_maximum_fusion.2.near_ref, ...), custom_call_target="tpu_custom_call" | custom-call | flops 30000001024 | bytes 1048576 | tf_op jit(solution)/shard_map/pallas_call | solution.py:450
  68.5 1.4 %collective-permute-start.10 = (bf16[64,512]{1,0:T(8,128)(2,1)}, bf16[64,512]{1,0:T(8,128)(2,1)}, u32[]{:S(2)}, u32[]{:S(2)}) collective-permute-start(bf16[64,512]{1,0:T(8,128)(2,1)} %get-tuple-element.67), channel_id=1, source_target_pairs={{0,8},{2,10},{4,12},{6,14},{8,0},{10,2},{12,4},{14,6},{1,9},{3,11}... | collective-permute-start | bytes 196616 | tf_op jit(solution)/shard_map/ppermute | solution.py:595
  69.9 1.6 %collective-permute-start.13 = (bf16[4,256,128]{2,1,0:T(8,128)(2,1)S(1)}, bf16[4,256,128]{2,1,0:T(8,128)(2,1)S(1)}, u32[]{:S(2)}, u32[]{:S(2)}) collective-permute-start(bf16[4,256,128]{2,1,0:T(8,128)(2,1)S(1)} %slice.43.refs_4_), channel_id=1, source_target_pairs={{0,16},{16,0},{1,17},{17,1},{2,18},{18,2},{3,19},{19,3},{4,20},{20... | collective-permute-start | bytes 786440 | tf_op jit(solution)/shard_map/ppermute | solution.py:595
  71.6 2.4 %collective-permute-done.10 = bf16[64,512]{1,0:T(8,128)(2,1)} collective-permute-done((bf16[64,512]{1,0:T(8,128)(2,1)}, bf16[64,512]{1,0:T(8,128)(2,1)}, u32[]{:S(2)}, u32[]{:S(2)}) %collective-permute-start.10) | collective-permute-done | bytes 65568 | tf_op jit(solution)/shard_map/ppermute | solution.py:595
  74.0 2.7 %collective-permute-start.12 = (bf16[4,256,128]{2,1,0:T(8,128)(2,1)S(1)}, bf16[4,256,128]{2,1,0:T(8,128)(2,1)S(1)}, u32[]{:S(2)}, u32[]{:S(2)}) collective-permute-start(bf16[4,256,128]{2,1,0:T(8,128)(2,1)S(1)} %all-to-all-done.2.refs_0_), channel_id=1, source_target_pairs={{0,16},{16,0},{1,17},{17,1},{2,18},{18,2},{3,19},{19,3},{4,20},{20... | collective-permute-start | bytes 786440 | tf_op jit(solution)/shard_map/ppermute | solution.py:595
  77.7 2.0 %collective-permute-start.14 = (bf16[2,64,512]{2,1,0:T(8,128)(2,1)S(1)}, bf16[2,64,512]{2,1,0:T(8,128)(2,1)S(1)}, u32[]{:S(2)}, u32[]{:S(2)}) collective-permute-start(bf16[2,64,512]{2,1,0:T(8,128)(2,1)S(1)} %get-tuple-element.88), channel_id=1, source_target_pairs={{0,2},{2,0},{4,6},{6,4},{8,10},{10,8},{12,14},{14,12},{1,3},{3,1},... | collective-permute-start | bytes 393224 | tf_op jit(solution)/shard_map/ppermute | solution.py:595
  79.7 1.5 %collective-permute-start.16 = (bf16[2,64,512]{2,1,0:T(8,128)(2,1)S(1)}, bf16[2,64,512]{2,1,0:T(8,128)(2,1)S(1)}, u32[]{:S(2)}, u32[]{:S(2)}) collective-permute-start(bf16[2,64,512]{2,1,0:T(8,128)(2,1)S(1)} %get-tuple-element.88), channel_id=1, source_target_pairs={{0,6},{2,4},{4,2},{6,0},{8,14},{10,12},{12,10},{14,8},{1,7},{3,5},... | collective-permute-start | bytes 393224 | tf_op jit(solution)/shard_map/ppermute | solution.py:595
  81.2 2.9 %collective-permute-done.15 = bf16[2,64,512]{2,1,0:T(8,128)(2,1)S(1)} collective-permute-done((bf16[2,64,512]{2,1,0:T(8,128)(2,1)S(1)}, bf16[2,64,512]{2,1,0:T(8,128)(2,1)S(1)}, u32[]{:S(2)}, u32[]{:S(2)}) %collective-permute-start.15) | collective-permute-done | bytes 131104 | tf_op jit(solution)/shard_map/ppermute | solution.py:595
  84.9 1.4 %collective-permute-done.16 = bf16[2,64,512]{2,1,0:T(8,128)(2,1)S(1)} collective-permute-done((bf16[2,64,512]{2,1,0:T(8,128)(2,1)S(1)}, bf16[2,64,512]{2,1,0:T(8,128)(2,1)S(1)}, u32[]{:S(2)}, u32[]{:S(2)}) %collective-permute-start.16) | collective-permute-done | bytes 131104 | tf_op jit(solution)/shard_map/ppermute | solution.py:595
  89.9 5.5 %shard_map.70 = (f32[64,512]{1,0:T(8,128)S(1)}, f32[64,512]{1,0:T(8,128)S(1)}, bf16[2,64,512]{2,1,0:T(8,128)(2,1)S(1)}, bf16[2,64,512]{2,1,0:T(8,128)(2,1)S(1)}, bf16[2,64,512]{2,1,0:T(8,128)(2,1)S(1)}) custom-call(s32[3]{0:T(128)S(1)} %copy-done.1, bf16[512,1024]{1,0:T(8,128)(2,1)S(1)} %get-tuple-element.66.tokens, ...), custom_call_target="tpu_custom_call" | custom-call | tf_op jit(solution)/shard_map/pallas_call | solution.py:541
  97.3 1.7 %collective-permute-start.24 = (bf16[2,64,512]{2,1,0:T(8,128)(2,1)S(1)}, bf16[2,64,512]{2,1,0:T(8,128)(2,1)S(1)}, u32[]{:S(2)}, u32[]{:S(2)}) collective-permute-start(bf16[2,64,512]{2,1,0:T(8,128)(2,1)S(1)} %get-tuple-element.84), channel_id=1, source_target_pairs={{0,6},{2,4},{4,2},{6,0},{8,14},{10,12},{12,10},{14,8},{1,7},{3,5},... | collective-permute-start | bytes 393224 | tf_op jit(solution)/shard_map/ppermute | solution.py:595
  99.0 2.1 %collective-permute-done.22.refs_0_ = bf16[2,64,512]{2,1,0:T(8,128)(2,1)S(1)} collective-permute-done((bf16[2,64,512]{2,1,0:T(8,128)(2,1)S(1)}, bf16[2,64,512]{2,1,0:T(8,128)(2,1)S(1)}, u32[]{:S(2)}, u32[]{:S(2)}) %collective-permute-start.22) | collective-permute-done | bytes 131104 | tf_op jit(solution)/shard_map/ppermute | solution.py:595
  101.0 1.9 %collective-permute-done.23.refs_1_ = bf16[2,64,512]{2,1,0:T(8,128)(2,1)S(1)} collective-permute-done((bf16[2,64,512]{2,1,0:T(8,128)(2,1)S(1)}, bf16[2,64,512]{2,1,0:T(8,128)(2,1)S(1)}, u32[]{:S(2)}, u32[]{:S(2)}) %collective-permute-start.23) | collective-permute-done | bytes 131104 | tf_op jit(solution)/shard_map/ppermute | solution.py:595
  102.9 2.1 %collective-permute-done.24.refs_2_ = bf16[2,64,512]{2,1,0:T(8,128)(2,1)S(1)} collective-permute-done((bf16[2,64,512]{2,1,0:T(8,128)(2,1)S(1)}, bf16[2,64,512]{2,1,0:T(8,128)(2,1)S(1)}, u32[]{:S(2)}, u32[]{:S(2)}) %collective-permute-start.24) | collective-permute-done | bytes 131104 | tf_op jit(solution)/shard_map/ppermute | solution.py:595
  105.1 2.8 %collective-permute-start.25 = (bf16[64,512]{1,0:T(8,128)(2,1)S(1)}, bf16[64,512]{1,0:T(8,128)(2,1)S(1)}, u32[]{:S(2)}, u32[]{:S(2)}) collective-permute-start(bf16[64,512]{1,0:T(8,128)(2,1)S(1)} %get-tuple-element.86), channel_id=1, source_target_pairs={{0,8},{2,10},{4,12},{6,14},{8,0},{10,2},{12,4},{14,6},{1,9},{3,11}... | collective-permute-start | bytes 196616 | tf_op jit(solution)/shard_map/ppermute | solution.py:595
  107.9 2.4 %collective-permute-done.25.across_ref = bf16[64,512]{1,0:T(8,128)(2,1)S(1)} collective-permute-done((bf16[64,512]{1,0:T(8,128)(2,1)S(1)}, bf16[64,512]{1,0:T(8,128)(2,1)S(1)}, u32[]{:S(2)}, u32[]{:S(2)}) %collective-permute-start.25) | collective-permute-done | bytes 65568 | tf_op jit(solution)/shard_map/ppermute | solution.py:595
  (68 shorter events, 17.2 us)
Async XLA Ops:
  6.9 16.8 %all-to-all-start = ((bf16[8,80,128]{2,1,0:T(8,128)(2,1)}), bf16[8,80,128]{2,1,0:T(8,128)(2,1)S(1)}, u32[]{:S(2)}, u32[]{:S(2)}) async-start(bf16[8,80,128]{2,1,0:T(8,128)(2,1)} %bitcast.4), calls=%async_computation | async-start | bytes 327680 | tf_op jit(solution)/shard_map/all_to_all | solution.py:599
  14.2 6.6 %copy-start.9 = (bf16[640,128]{1,0:T(8,128)(2,1)S(1)}, bf16[640,128]{1,0:T(8,128)(2,1)}, u32[]{:S(2)}) copy-start(bf16[640,128]{1,0:T(8,128)(2,1)} %get-tuple-element.46) | copy-start | bytes 491524
  17.1 14.8 %collective-permute-start.2 = (bf16[704,128]{1,0:T(8,128)(2,1)}, bf16[704,128]{1,0:T(8,128)(2,1)S(1)}, u32[]{:S(2)}, u32[]{:S(2)}) collective-permute-start(bf16[704,128]{1,0:T(8,128)(2,1)} %get-tuple-element.53), channel_id=1, source_target_pairs={{0,2},{2,0},{4,6},{6,4},{8,10},{10,8},{12,14},{14,12},{1,3},{3,1},... | collective-permute-start | bytes 540680 | tf_op jit(solution)/shard_map/ppermute | solution.py:595
  19.2 12.7 %collective-permute-start.3 = (bf16[704,128]{1,0:T(8,128)(2,1)}, bf16[704,128]{1,0:T(8,128)(2,1)S(1)}, u32[]{:S(2)}, u32[]{:S(2)}) collective-permute-start(bf16[704,128]{1,0:T(8,128)(2,1)} %get-tuple-element.54), channel_id=1, source_target_pairs={{0,4},{2,6},{4,0},{6,2},{8,12},{10,14},{12,8},{14,10},{1,5},{3,7},... | collective-permute-start | bytes 540680 | tf_op jit(solution)/shard_map/ppermute | solution.py:595
  20.7 2.9 %copy-start.1 = (s32[3]{0:T(128)S(1)}, s32[3]{0:T(128)}, u32[]{:S(2)}) copy-start(s32[3]{0:T(128)} %pad_add_fusion.rank_ref.scalars) | copy-start | bytes 40
  20.7 13.4 %collective-permute-start.4 = (bf16[704,128]{1,0:T(8,128)(2,1)}, bf16[704,128]{1,0:T(8,128)(2,1)S(1)}, u32[]{:S(2)}, u32[]{:S(2)}) collective-permute-start(bf16[704,128]{1,0:T(8,128)(2,1)} %get-tuple-element.55), channel_id=1, source_target_pairs={{0,6},{2,4},{4,2},{6,0},{8,14},{10,12},{12,10},{14,8},{1,7},{3,5},... | collective-permute-start | bytes 540680 | tf_op jit(solution)/shard_map/ppermute | solution.py:595
  20.8 11.2 %collective-permute-start.1 = (bf16[640,128]{1,0:T(8,128)(2,1)S(1)}, bf16[640,128]{1,0:T(8,128)(2,1)S(1)}, u32[]{:S(2)}, u32[]{:S(2)}) collective-permute-start(bf16[640,128]{1,0:T(8,128)(2,1)S(1)} %copy-done.9), channel_id=1, source_target_pairs={{0,8},{2,10},{4,12},{6,14},{8,0},{10,2},{12,4},{14,6},{1,9},{3,11}... | collective-permute-start | bytes 491528 | tf_op jit(solution)/shard_map/ppermute | solution.py:595
  24.5 9.6 %collective-permute-start = (bf16[256,128]{1,0:T(8,128)(2,1)S(1)}, bf16[256,128]{1,0:T(8,128)(2,1)S(1)}, u32[]{:S(2)}, u32[]{:S(2)}) collective-permute-start(bf16[256,128]{1,0:T(8,128)(2,1)S(1)} %shard_map.66.owned_ref), channel_id=1, source_target_pairs={{0,8},{2,10},{4,12},{6,14},{8,0},{10,2},{12,4},{14,6},{1,9},{3,11}... | collective-permute-start | bytes 196616 | tf_op jit(solution)/shard_map/ppermute | solution.py:595
  35.1 3.6 %copy-start.7 = (bf16[704,128]{1,0:T(8,128)(2,1)S(1)}, bf16[704,128]{1,0:T(8,128)(2,1)}, u32[]{:S(2)}) copy-start(bf16[704,128]{1,0:T(8,128)(2,1)} %get-tuple-element.60) | copy-start | bytes 540676
  35.1 20.6 %all-to-all-start.1 = ((bf16[4,864,128]{2,1,0:T(8,128)(2,1)}), bf16[4,864,128]{2,1,0:T(8,128)(2,1)S(1)}, u32[]{:S(2)}, u32[]{:S(2)}) async-start(bf16[4,864,128]{2,1,0:T(8,128)(2,1)} %shard_map.68), calls=%async_computation.1 | async-start | bytes 1769472 | tf_op jit(solution)/shard_map/all_to_all | solution.py:605
  38.9 14.6 %collective-permute-start.7 = (bf16[4,512,128]{2,1,0:T(8,128)(2,1)S(1)}, bf16[4,512,128]{2,1,0:T(8,128)(2,1)S(1)}, u32[]{:S(2)}, u32[]{:S(2)}) collective-permute-start(bf16[4,512,128]{2,1,0:T(8,128)(2,1)S(1)} %pad_maximum_fusion.refs_8_), channel_id=1, source_target_pairs={{0,1},{1,0},{2,3},{3,2},{4,5},{5,4},{6,7},{7,6},{8,9},{9,8},{10,11... | collective-permute-start | bytes 1572872 | tf_op jit(solution)/shard_map/ppermute | solution.py:595
  39.0 14.6 %collective-permute-start.6 = (bf16[4,512,128]{2,1,0:T(8,128)(2,1)S(1)}, bf16[4,512,128]{2,1,0:T(8,128)(2,1)}, u32[]{:S(2)}, u32[]{:S(2)}) collective-permute-start(bf16[4,512,128]{2,1,0:T(8,128)(2,1)S(1)} %pad_maximum_fusion.refs_8_), channel_id=1, source_target_pairs={{0,16},{16,0},{1,17},{17,1},{2,18},{18,2},{3,19},{19,3},{4,20},{20... | collective-permute-start | bytes 1572872 | tf_op jit(solution)/shard_map/ppermute | solution.py:595
  40.6 13.0 %collective-permute-start.5 = (bf16[4,256,128]{2,1,0:T(8,128)(2,1)S(1)}, bf16[4,256,128]{2,1,0:T(8,128)(2,1)}, u32[]{:S(2)}, u32[]{:S(2)}) collective-permute-start(bf16[4,256,128]{2,1,0:T(8,128)(2,1)S(1)} %copy-done.8), channel_id=1, source_target_pairs={{0,8},{2,10},{4,12},{6,14},{8,0},{10,2},{12,4},{14,6},{1,9},{3,11}... | collective-permute-start | bytes 786440 | tf_op jit(solution)/shard_map/ppermute | solution.py:595
  56.5 5.9 %collective-permute-start.8 = (bf16[4,512,128]{2,1,0:T(8,128)(2,1)}, bf16[4,512,128]{2,1,0:T(8,128)(2,1)S(1)}, u32[]{:S(2)}, u32[]{:S(2)}) collective-permute-start(bf16[4,512,128]{2,1,0:T(8,128)(2,1)} %slice.41), channel_id=1, source_target_pairs={{0,1},{1,0},{2,3},{3,2},{4,5},{5,4},{6,7},{7,6},{8,9},{9,8},{10,11... | collective-permute-start | bytes 1572872 | tf_op jit(solution)/shard_map/ppermute | solution.py:595
  56.5 5.3 %collective-permute-start.9 = (bf16[4,96,128]{2,1,0:T(8,128)(2,1)S(1)}, bf16[4,96,128]{2,1,0:T(8,128)(2,1)S(1)}, u32[]{:S(2)}, u32[]{:S(2)}) collective-permute-start(bf16[4,96,128]{2,1,0:T(8,128)(2,1)S(1)} %slice.42), channel_id=1, source_target_pairs={{0,16},{16,0},{1,17},{17,1},{2,18},{18,2},{3,19},{19,3},{4,20},{20... | collective-permute-start | bytes 294920 | tf_op jit(solution)/shard_map/ppermute | solution.py:595
  58.1 13.5 %all-to-all-start.2 = ((bf16[4,256,128]{2,1,0:T(8,128)(2,1)}), bf16[4,256,128]{2,1,0:T(8,128)(2,1)S(1)}, u32[]{:S(2)}, u32[]{:S(2)}) async-start(bf16[4,256,128]{2,1,0:T(8,128)(2,1)} %collective-permute-done.5), calls=%async_computation.2 | async-start | bytes 524288 | tf_op jit(solution)/shard_map/all_to_all | solution.py:605
  61.5 10.1 %collective-permute-start.11 = (bf16[4,512,128]{2,1,0:T(8,128)(2,1)}, bf16[4,512,128]{2,1,0:T(8,128)(2,1)}, u32[]{:S(2)}, u32[]{:S(2)}) collective-permute-start(bf16[4,512,128]{2,1,0:T(8,128)(2,1)} %collective-permute-done.6.refs_9_), channel_id=1, source_target_pairs={{0,1},{1,0},{2,3},{3,2},{4,5},{5,4},{6,7},{7,6},{8,9},{9,8},{10,11... | collective-permute-start | bytes 1572872 | tf_op jit(solution)/shard_map/ppermute | solution.py:595
  68.5 5.5 %collective-permute-start.10 = (bf16[64,512]{1,0:T(8,128)(2,1)}, bf16[64,512]{1,0:T(8,128)(2,1)}, u32[]{:S(2)}, u32[]{:S(2)}) collective-permute-start(bf16[64,512]{1,0:T(8,128)(2,1)} %get-tuple-element.67), channel_id=1, source_target_pairs={{0,8},{2,10},{4,12},{6,14},{8,0},{10,2},{12,4},{14,6},{1,9},{3,11}... | collective-permute-start | bytes 196616 | tf_op jit(solution)/shard_map/ppermute | solution.py:595
  69.9 16.4 %collective-permute-start.13 = (bf16[4,256,128]{2,1,0:T(8,128)(2,1)S(1)}, bf16[4,256,128]{2,1,0:T(8,128)(2,1)S(1)}, u32[]{:S(2)}, u32[]{:S(2)}) collective-permute-start(bf16[4,256,128]{2,1,0:T(8,128)(2,1)S(1)} %slice.43.refs_4_), channel_id=1, source_target_pairs={{0,16},{16,0},{1,17},{17,1},{2,18},{18,2},{3,19},{19,3},{4,20},{20... | collective-permute-start | bytes 786440 | tf_op jit(solution)/shard_map/ppermute | solution.py:595
  74.0 12.4 %collective-permute-start.12 = (bf16[4,256,128]{2,1,0:T(8,128)(2,1)S(1)}, bf16[4,256,128]{2,1,0:T(8,128)(2,1)S(1)}, u32[]{:S(2)}, u32[]{:S(2)}) collective-permute-start(bf16[4,256,128]{2,1,0:T(8,128)(2,1)S(1)} %all-to-all-done.2.refs_0_), channel_id=1, source_target_pairs={{0,16},{16,0},{1,17},{17,1},{2,18},{18,2},{3,19},{19,3},{4,20},{20... | collective-permute-start | bytes 786440 | tf_op jit(solution)/shard_map/ppermute | solution.py:595
  77.6 6.4 %collective-permute-start.15 = (bf16[2,64,512]{2,1,0:T(8,128)(2,1)S(1)}, bf16[2,64,512]{2,1,0:T(8,128)(2,1)S(1)}, u32[]{:S(2)}, u32[]{:S(2)}) collective-permute-start(bf16[2,64,512]{2,1,0:T(8,128)(2,1)S(1)} %get-tuple-element.88), channel_id=1, source_target_pairs={{0,4},{2,6},{4,0},{6,2},{8,12},{10,14},{12,8},{14,10},{1,5},{3,7},... | collective-permute-start | bytes 393224 | tf_op jit(solution)/shard_map/ppermute | solution.py:595
  77.7 7.2 %collective-permute-start.14 = (bf16[2,64,512]{2,1,0:T(8,128)(2,1)S(1)}, bf16[2,64,512]{2,1,0:T(8,128)(2,1)S(1)}, u32[]{:S(2)}, u32[]{:S(2)}) collective-permute-start(bf16[2,64,512]{2,1,0:T(8,128)(2,1)S(1)} %get-tuple-element.88), channel_id=1, source_target_pairs={{0,2},{2,0},{4,6},{6,4},{8,10},{10,8},{12,14},{14,12},{1,3},{3,1},... | collective-permute-start | bytes 393224 | tf_op jit(solution)/shard_map/ppermute | solution.py:595
  79.7 6.7 %collective-permute-start.16 = (bf16[2,64,512]{2,1,0:T(8,128)(2,1)S(1)}, bf16[2,64,512]{2,1,0:T(8,128)(2,1)S(1)}, u32[]{:S(2)}, u32[]{:S(2)}) collective-permute-start(bf16[2,64,512]{2,1,0:T(8,128)(2,1)S(1)} %get-tuple-element.88), channel_id=1, source_target_pairs={{0,6},{2,4},{4,2},{6,0},{8,14},{10,12},{12,10},{14,8},{1,7},{3,5},... | collective-permute-start | bytes 393224 | tf_op jit(solution)/shard_map/ppermute | solution.py:595
  86.4 3.5 %collective-permute-start.17 = (bf16[4,2,64,512]{3,2,1,0:T(8,128)(2,1)S(1)}, bf16[4,2,64,512]{3,2,1,0:T(8,128)(2,1)S(1)}, u32[]{:S(2)}, u32[]{:S(2)}) collective-permute-start(bf16[4,2,64,512]{3,2,1,0:T(8,128)(2,1)S(1)} %pad_maximum_fusion.1.a), channel_id=1, source_target_pairs={{0,1},{1,0},{2,3},{3,2},{4,5},{5,4},{6,7},{7,6},{8,9},{9,8},{10,11... | collective-permute-start | bytes 1572872 | tf_op jit(solution)/shard_map/ppermute | solution.py:595
  86.5 2.3 %collective-permute-start.20 = (bf16[4,256,128]{2,1,0:T(8,128)(2,1)S(1)}, bf16[4,256,128]{2,1,0:T(8,128)(2,1)S(1)}, u32[]{:S(2)}, u32[]{:S(2)}) collective-permute-start(bf16[4,256,128]{2,1,0:T(8,128)(2,1)S(1)} %slice.43.refs_4_), channel_id=1, source_target_pairs={{0,1},{1,0},{2,3},{3,2},{4,5},{5,4},{6,7},{7,6},{8,9},{9,8},{10,11... | collective-permute-start | bytes 786440 | tf_op jit(solution)/shard_map/ppermute | solution.py:595
  87.0 2.1 %collective-permute-start.18 = (bf16[4,256,128]{2,1,0:T(8,128)(2,1)S(1)}, bf16[4,256,128]{2,1,0:T(8,128)(2,1)S(1)}, u32[]{:S(2)}, u32[]{:S(2)}) collective-permute-start(bf16[4,256,128]{2,1,0:T(8,128)(2,1)S(1)} %all-to-all-done.2.refs_0_), channel_id=1, source_target_pairs={{0,1},{1,0},{2,3},{3,2},{4,5},{5,4},{6,7},{7,6},{8,9},{9,8},{10,11... | collective-permute-start | bytes 786440 | tf_op jit(solution)/shard_map/ppermute | solution.py:595
  87.1 2.4 %collective-permute-start.19 = (bf16[4,256,128]{2,1,0:T(8,128)(2,1)S(1)}, bf16[4,256,128]{2,1,0:T(8,128)(2,1)S(1)}, u32[]{:S(2)}, u32[]{:S(2)}) collective-permute-start(bf16[4,256,128]{2,1,0:T(8,128)(2,1)S(1)} %collective-permute-done.12.refs_1_), channel_id=1, source_target_pairs={{0,1},{1,0},{2,3},{3,2},{4,5},{5,4},{6,7},{7,6},{8,9},{9,8},{10,11... | collective-permute-start | bytes 786440 | tf_op jit(solution)/shard_map/ppermute | solution.py:595
  87.5 2.4 %collective-permute-start.21 = (bf16[4,256,128]{2,1,0:T(8,128)(2,1)S(1)}, bf16[4,256,128]{2,1,0:T(8,128)(2,1)S(1)}, u32[]{:S(2)}, u32[]{:S(2)}) collective-permute-start(bf16[4,256,128]{2,1,0:T(8,128)(2,1)S(1)} %collective-permute-done.13.refs_5_), channel_id=1, source_target_pairs={{0,1},{1,0},{2,3},{3,2},{4,5},{5,4},{6,7},{7,6},{8,9},{9,8},{10,11... | collective-permute-start | bytes 786440 | tf_op jit(solution)/shard_map/ppermute | solution.py:595
  95.4 5.6 %collective-permute-start.22 = (bf16[2,64,512]{2,1,0:T(8,128)(2,1)S(1)}, bf16[2,64,512]{2,1,0:T(8,128)(2,1)S(1)}, u32[]{:S(2)}, u32[]{:S(2)}) collective-permute-start(bf16[2,64,512]{2,1,0:T(8,128)(2,1)S(1)} %get-tuple-element.82), channel_id=1, source_target_pairs={{0,2},{2,0},{4,6},{6,4},{8,10},{10,8},{12,14},{14,12},{1,3},{3,1},... | collective-permute-start | bytes 393224 | tf_op jit(solution)/shard_map/ppermute | solution.py:595
  96.5 6.4 %collective-permute-start.23 = (bf16[2,64,512]{2,1,0:T(8,128)(2,1)S(1)}, bf16[2,64,512]{2,1,0:T(8,128)(2,1)S(1)}, u32[]{:S(2)}, u32[]{:S(2)}) collective-permute-start(bf16[2,64,512]{2,1,0:T(8,128)(2,1)S(1)} %get-tuple-element.83), channel_id=1, source_target_pairs={{0,4},{2,6},{4,0},{6,2},{8,12},{10,14},{12,8},{14,10},{1,5},{3,7},... | collective-permute-start | bytes 393224 | tf_op jit(solution)/shard_map/ppermute | solution.py:595
  97.3 7.7 %collective-permute-start.24 = (bf16[2,64,512]{2,1,0:T(8,128)(2,1)S(1)}, bf16[2,64,512]{2,1,0:T(8,128)(2,1)S(1)}, u32[]{:S(2)}, u32[]{:S(2)}) collective-permute-start(bf16[2,64,512]{2,1,0:T(8,128)(2,1)S(1)} %get-tuple-element.84), channel_id=1, source_target_pairs={{0,6},{2,4},{4,2},{6,0},{8,14},{10,12},{12,10},{14,8},{1,7},{3,5},... | collective-permute-start | bytes 393224 | tf_op jit(solution)/shard_map/ppermute | solution.py:595
  105.1 5.2 %collective-permute-start.25 = (bf16[64,512]{1,0:T(8,128)(2,1)S(1)}, bf16[64,512]{1,0:T(8,128)(2,1)S(1)}, u32[]{:S(2)}, u32[]{:S(2)}) collective-permute-start(bf16[64,512]{1,0:T(8,128)(2,1)S(1)} %get-tuple-element.86), channel_id=1, source_target_pairs={{0,8},{2,10},{4,12},{6,14},{8,0},{10,2},{12,4},{14,6},{1,9},{3,11}... | collective-permute-start | bytes 196616 | tf_op jit(solution)/shard_map/ppermute | solution.py:595
  (7 other events, 6.3 us)

commit v16 on v15

--- a/solution.py
+++ b/solution.py
@@ -453,7 +453,7 @@
         out_specs=[vspec()] * 2,
         out_shape=[struct((length, depth)), struct((size, length))],
         scratch_shapes=[VMEM((head_rows, n * 128), BF16)],
-        compiler_params=params(12),
+        compiler_params=params(8),
         cost_estimate=cost(30),
     )(scalars, mine, other, near, far)
 
@@ -552,7 +552,7 @@
             VMEM((2, inner, length), BF16),
             pltpu.SemaphoreType.DMA((24 * half,)),
         ],
-        compiler_params=params(24),
+        compiler_params=params(16),
     )(scalars, tokens, *pieces, *far[0], *far[1], *outs_far[0], *outs_far[1], *near[0], *near[1])
 
 
@@ -631,6 +631,7 @@
     away, blocks = pack_far(scalars, *weights, n)
     far = swap(away, "seq", half)
     slots = prep(scalars, keep_list, after(flat, away), n, sup, capacity)
+    slots, far = lax.optimization_barrier((slots, far))
     dealt = exchange(slots)
     weights = lax.optimization_barrier((*weights, slots))[:4]
     near = pack_near(scalars, *weights, n)
@@ -659,8 +660,9 @@
     )
 
     att_across = swap(attended, "seq", half)
-    att_across, near_last, mlp_mine = lax.optimization_barrier(
-        (att_across, swap(near_other, "head", 1), mlp_mine)
+    far_pair = swap(got[:, got.shape[1] - out_rows :], "head", 1)
+    att_across, near_last, mlp_mine, far_pair = lax.optimization_barrier(
+        (att_across, swap(near_other, "head", 1), mlp_mine, far_pair)
     )
     got = after(got, attended)
     far_mine = got[:, got.shape[1] - out_rows :]
@@ -671,13 +673,12 @@
     mlp_other, far_other, *pairs = lax.optimization_barrier((mlp_other, far_other, *pairs))
     gathered = jnp.stack([pair] + pairs)
     mlp_pair = (mlp_mine, mlp_other)
-    far_pair = (far_mine, far_other)
     base, term_away, *terms = mlp(
         scalars,
         tokens,
         (gathered, swap(gathered, "head", 1)),
         (mlp_pair, tuple(swap(value, "head", 1) for value in mlp_pair)),
-        (far_pair, tuple(swap(value, "head", 1) for value in far_pair)),
+        ((far_mine, far_other), (far_pair, swap(far_other, "head", 1))),
         ((near_mine, near_other), (near_pair, near_last)),
         n,
     )

time: 112 us -> 116 us (1.036)
  waiting for transfers between devices: 40.9 us -> 46.5 us
    ppermute x26, waiting for transfers between devices: 38.8 us -> 43.1 us  [swap(): return lax.ppermute(value, axis, [(i, i ^ j) for i in range(n)])]
    all_to_all x1, starting transfers between devices: 7.28 us -> 5.77 us  [exchange(): return lax.all_to_all(value, 'seq', split_axis=0, concat_axis=0, tiled=True)]
    all_to_all x1, waiting for transfers between devices: 0.01 us -> 1.34 us  [exchange(): return lax.all_to_all(value, 'seq', split_axis=0, concat_axis=0, tiled=True)]
    unnamed x20 -> x24, local copies, waits for them, and re-layouts: 4.04 us -> 4.09 us
  transfers between devices with their start and end apart: 29 -> 29, of which waited for: 16 -> 17; matrix products, arithmetic and copies ran while one was open for 1% -> 2% of each run, Pallas kernels for 6% -> 8%
where the time goes in v16:
time: 116 us
  waiting for transfers between devices  46.5 us (40%)
  starting transfers between devices  42.3 us (36%)
  Pallas kernels  19 us (16%)
  local copies, waits for them, and re-layouts  5.79 us (5%)
  other arithmetic  1.64 us (1%)
    ppermute x26, waiting for transfers between devices, swap(): return lax.ppermute(value, axis, [(i, i ^ j) for i in range(n)])  43.1 us
    ppermute x26, starting transfers between devices, swap(): return lax.ppermute(value, axis, [(i, i ^ j) for i in range(n)])  29.5 us
    all_to_all x2, starting transfers between devices, exchange_half(): lax.all_to_all(value, 'seq', split_axis=0, concat_axis=0, axis_index_grou...  7.04 us
    all_to_all x1, starting transfers between devices, exchange(): return lax.all_to_all(value, 'seq', split_axis=0, concat_axis=0, tiled=True)  5.77 us
    pallas_call x1, Pallas kernels, mlp(): pl.pallas_call(kernel, in_specs=[sspec()] + [vspec()] * 3 + [aspec()] * 1...  5.5 us
    pallas_call x2, Pallas kernels, pack(): pl.pallas_call(kernel, in_specs=[sspec()] + [hspec()] * 4, out_specs=[vsp...  5.5 us
    unnamed x24, local copies, waits for them, and re-layouts  4.09 us
    pallas_call x1, Pallas kernels, attend_fast(): pl.pallas_call(functools.partial(attend_kernel, n, per_owner), in_specs=[...  3.31 us
  transfers between devices with their start and end apart: 29, of which 17 were waited for; matrix products, arithmetic and copies ran while one was open for 2% of the time, Pallas kernels for 8%

profile of v16, /device:TPU:0, one launch (start us, length us, event | category | flops | bytes accessed | tf_op | source)
XLA Modules:
  0.0 115.5 jit_solution(16507796609103874338)
XLA Ops:
  0.6 2.7 %shard_map.64 = (bf16[640,128]{1,0:T(8,128)(2,1)}, bf16[4,256,128]{2,1,0:T(8,128)(2,1)}) custom-call(s32[3]{0:T(128)} %pad_add_fusion.rank_ref.scalars, bf16[8,192,128]{2,1,0:T(8,128)(2,1)} %bitcast.31, bf16[512,128]{1,0:T(8,128)(2,1)} %out_weight_ref.2, bf16[128,2048]{1,0:T(8,128)(2,1)} %up_ref.2, bf16[2048,128]{1,0:T(8,128)(2,1)} %down_ref.2), custom_call_target="tpu_custom_call" | custom-call | tf_op jit(solution)/shard_map/pallas_call | solution.py:342
  3.3 4.1 %collective-permute-start = (bf16[640,128]{1,0:T(8,128)(2,1)}, bf16[640,128]{1,0:T(8,128)(2,1)S(1)}, u32[]{:S(2)}, u32[]{:S(2)}) collective-permute-start(bf16[640,128]{1,0:T(8,128)(2,1)} %get-tuple-element.49), channel_id=1, source_target_pairs={{0,8},{2,10},{4,12},{6,14},{8,0},{10,2},{12,4},{14,6},{1,9},{3,11}... | collective-permute-start | bytes 491528 | tf_op jit(solution)/shard_map/ppermute | solution.py:595
  7.5 2.0 %shard_map.65 = bf16[640,128]{1,0:T(8,128)(2,1)} custom-call(s32[3]{0:T(128)S(1)} %copy-done.2, s32[1,64]{1,0:T(1,128)S(1)} %copy-done.4, bf16[160,1024]{1,0:T(8,128)(2,1)S(1)} %reshape.8.patches_ref), custom_call_target="tpu_custom_call" | custom-call | tf_op jit(solution)/shard_map/pallas_call | solution.py:247
  9.5 5.8 %collective-permute-done.far_ref = bf16[640,128]{1,0:T(8,128)(2,1)S(1)} collective-permute-done((bf16[640,128]{1,0:T(8,128)(2,1)}, bf16[640,128]{1,0:T(8,128)(2,1)S(1)}, u32[]{:S(2)}, u32[]{:S(2)}) %collective-permute-start) | collective-permute-done | bytes 163872 | tf_op jit(solution)/shard_map/ppermute | solution.py:595
  15.3 5.8 %all-to-all-start = ((bf16[8,80,128]{2,1,0:T(8,128)(2,1)}), bf16[8,80,128]{2,1,0:T(8,128)(2,1)S(1)}, u32[]{:S(2)}, u32[]{:S(2)}) async-start(bf16[8,80,128]{2,1,0:T(8,128)(2,1)} %bitcast.4), calls=%async_computation | async-start | bytes 327680 | tf_op jit(solution)/shard_map/all_to_all | solution.py:599
  21.1 2.8 %shard_map.67 = (bf16[704,128]{1,0:T(8,128)(2,1)}, bf16[704,128]{1,0:T(8,128)(2,1)}, bf16[704,128]{1,0:T(8,128)(2,1)}, bf16[704,128]{1,0:T(8,128)(2,1)}) custom-call(s32[3]{0:T(128)} %pad_add_fusion.rank_ref.scalars, bf16[8,192,128]{2,1,0:T(8,128)(2,1)} %bitcast.32, bf16[512,128]{1,0:T(8,128)(2,1)} %out_weight_ref.2, bf16[128,2048]{1,0:T(8,128)(2,1)} %up_ref.2, ...), custom_call_target="tpu_custom_call" | custom-call | tf_op jit(solution)/shard_map/pallas_call | solution.py:342
  23.9 2.1 %collective-permute-start.2 = (bf16[704,128]{1,0:T(8,128)(2,1)}, bf16[704,128]{1,0:T(8,128)(2,1)S(1)}, u32[]{:S(2)}, u32[]{:S(2)}) collective-permute-start(bf16[704,128]{1,0:T(8,128)(2,1)} %get-tuple-element.58), channel_id=1, source_target_pairs={{0,2},{2,0},{4,6},{6,4},{8,10},{10,8},{12,14},{14,12},{1,3},{3,1},... | collective-permute-start | bytes 540680 | tf_op jit(solution)/shard_map/ppermute | solution.py:595
  26.0 1.5 %collective-permute-start.3 = (bf16[704,128]{1,0:T(8,128)(2,1)}, bf16[704,128]{1,0:T(8,128)(2,1)S(1)}, u32[]{:S(2)}, u32[]{:S(2)}) collective-permute-start(bf16[704,128]{1,0:T(8,128)(2,1)} %get-tuple-element.59), channel_id=1, source_target_pairs={{0,4},{2,6},{4,0},{6,2},{8,12},{10,14},{12,8},{14,10},{1,5},{3,7},... | collective-permute-start | bytes 540680 | tf_op jit(solution)/shard_map/ppermute | solution.py:595
  29.8 1.6 %collective-permute-start.1 = (bf16[256,128]{1,0:T(8,128)(2,1)S(1)}, bf16[256,128]{1,0:T(8,128)(2,1)S(1)}, u32[]{:S(2)}, u32[]{:S(2)}) collective-permute-start(bf16[256,128]{1,0:T(8,128)(2,1)S(1)} %shard_map.66.owned_ref), channel_id=1, source_target_pairs={{0,8},{2,10},{4,12},{6,14},{8,0},{10,2},{12,4},{14,6},{1,9},{3,11}... | collective-permute-start | bytes 196616 | tf_op jit(solution)/shard_map/ppermute | solution.py:595
  31.4 3.0 %collective-permute-done.3 = bf16[704,128]{1,0:T(8,128)(2,1)S(1)} collective-permute-done((bf16[704,128]{1,0:T(8,128)(2,1)}, bf16[704,128]{1,0:T(8,128)(2,1)S(1)}, u32[]{:S(2)}, u32[]{:S(2)}) %collective-permute-start.3) | collective-permute-done | bytes 180256 | tf_op jit(solution)/shard_map/ppermute | solution.py:595
  34.4 3.2 %collective-permute-done.4 = bf16[704,128]{1,0:T(8,128)(2,1)S(1)} collective-permute-done((bf16[704,128]{1,0:T(8,128)(2,1)}, bf16[704,128]{1,0:T(8,128)(2,1)S(1)}, u32[]{:S(2)}, u32[]{:S(2)}) %collective-permute-start.4) | collective-permute-done | bytes 180256 | tf_op jit(solution)/shard_map/ppermute | solution.py:595
  38.6 3.6 %all-to-all-start.1 = ((bf16[4,864,128]{2,1,0:T(8,128)(2,1)}), bf16[4,864,128]{2,1,0:T(8,128)(2,1)S(1)}, u32[]{:S(2)}, u32[]{:S(2)}) async-start(bf16[4,864,128]{2,1,0:T(8,128)(2,1)} %shard_map.68), calls=%async_computation.1 | async-start | bytes 1769472 | tf_op jit(solution)/shard_map/all_to_all | solution.py:605
  42.5 1.6 %collective-permute-start.6 = (bf16[4,512,128]{2,1,0:T(8,128)(2,1)S(1)}, bf16[4,512,128]{2,1,0:T(8,128)(2,1)}, u32[]{:S(2)}, u32[]{:S(2)}) collective-permute-start(bf16[4,512,128]{2,1,0:T(8,128)(2,1)S(1)} %pad_maximum_fusion.refs_8_), channel_id=1, source_target_pairs={{0,16},{16,0},{1,17},{17,1},{2,18},{18,2},{3,19},{19,3},{4,20},{20... | collective-permute-start | bytes 1572872 | tf_op jit(solution)/shard_map/ppermute | solution.py:595
  44.1 2.0 %collective-permute-start.5 = (bf16[4,256,128]{2,1,0:T(8,128)(2,1)S(1)}, bf16[4,256,128]{2,1,0:T(8,128)(2,1)}, u32[]{:S(2)}, u32[]{:S(2)}) collective-permute-start(bf16[4,256,128]{2,1,0:T(8,128)(2,1)S(1)} %copy-done.11), channel_id=1, source_target_pairs={{0,8},{2,10},{4,12},{6,14},{8,0},{10,2},{12,4},{14,6},{1,9},{3,11}... | collective-permute-start | bytes 786440 | tf_op jit(solution)/shard_map/ppermute | solution.py:595
  46.1 11.1 %collective-permute-done.5 = bf16[4,256,128]{2,1,0:T(8,128)(2,1)} collective-permute-done((bf16[4,256,128]{2,1,0:T(8,128)(2,1)S(1)}, bf16[4,256,128]{2,1,0:T(8,128)(2,1)}, u32[]{:S(2)}, u32[]{:S(2)}) %collective-permute-start.5) | collective-permute-done | bytes 262176 | tf_op jit(solution)/shard_map/ppermute | solution.py:595
  57.2 2.1 %all-to-all-done.1.mine_ref = bf16[4,864,128]{2,1,0:T(8,128)(2,1)S(1)} async-done(((bf16[4,864,128]{2,1,0:T(8,128)(2,1)}), bf16[4,864,128]{2,1,0:T(8,128)(2,1)S(1)}, u32[]{:S(2)}, u32[]{:S(2)}) %all-to-all-start.1) | async-done | bytes 884768 | tf_op jit(solution)/shard_map/all_to_all | solution.py:605
  60.2 1.6 %collective-permute-start.9 = (bf16[4,96,128]{2,1,0:T(8,128)(2,1)S(1)}, bf16[4,96,128]{2,1,0:T(8,128)(2,1)S(1)}, u32[]{:S(2)}, u32[]{:S(2)}) collective-permute-start(bf16[4,96,128]{2,1,0:T(8,128)(2,1)S(1)} %slice.45), channel_id=1, source_target_pairs={{0,16},{16,0},{1,17},{17,1},{2,18},{18,2},{3,19},{19,3},{4,20},{20... | collective-permute-start | bytes 294920 | tf_op jit(solution)/shard_map/ppermute | solution.py:595
  62.5 3.4 %all-to-all-start.2 = ((bf16[4,256,128]{2,1,0:T(8,128)(2,1)}), bf16[4,256,128]{2,1,0:T(8,128)(2,1)S(1)}, u32[]{:S(2)}, u32[]{:S(2)}) async-start(bf16[4,256,128]{2,1,0:T(8,128)(2,1)} %collective-permute-done.5), calls=%async_computation.2 | async-start | bytes 524288 | tf_op jit(solution)/shard_map/all_to_all | solution.py:605
  69.8 3.3 %shard_map.69 = (bf16[512,1024]{1,0:T(8,128)(2,1)S(1)}, bf16[64,512]{1,0:T(8,128)(2,1)}) custom-call(s32[3]{0:T(128)S(1)} %copy-done.3, bf16[4,864,128]{2,1,0:T(8,128)(2,1)S(1)} %all-to-all-done.1.mine_ref, bf16[4,512,128]{2,1,0:T(8,128)(2,1)S(1)} %copy-done.6, bf16[4,192,128]{2,1,0:T(8,128)(2,1)S(1)} %pad_maximum_fusion.2.near_ref, ...), custom_call_target="tpu_custom_call" | custom-call | flops 30000001024 | bytes 1048576 | tf_op jit(solution)/shard_map/pallas_call | solution.py:450
  73.2 1.4 %collective-permute-start.10 = (bf16[64,512]{1,0:T(8,128)(2,1)}, bf16[64,512]{1,0:T(8,128)(2,1)}, u32[]{:S(2)}, u32[]{:S(2)}) collective-permute-start(bf16[64,512]{1,0:T(8,128)(2,1)} %get-tuple-element.72), channel_id=1, source_target_pairs={{0,8},{2,10},{4,12},{6,14},{8,0},{10,2},{12,4},{14,6},{1,9},{3,11}... | collective-permute-start | bytes 196616 | tf_op jit(solution)/shard_map/ppermute | solution.py:595
  74.5 1.7 %collective-permute-start.14 = (bf16[4,256,128]{2,1,0:T(8,128)(2,1)S(1)}, bf16[4,256,128]{2,1,0:T(8,128)(2,1)S(1)}, u32[]{:S(2)}, u32[]{:S(2)}) collective-permute-start(bf16[4,256,128]{2,1,0:T(8,128)(2,1)S(1)} %slice.47.refs_4_), channel_id=1, source_target_pairs={{0,16},{16,0},{1,17},{17,1},{2,18},{18,2},{3,19},{19,3},{4,20},{20... | collective-permute-start | bytes 786440 | tf_op jit(solution)/shard_map/ppermute | solution.py:595
  77.0 3.1 %collective-permute-done.10 = bf16[64,512]{1,0:T(8,128)(2,1)} collective-permute-done((bf16[64,512]{1,0:T(8,128)(2,1)}, bf16[64,512]{1,0:T(8,128)(2,1)}, u32[]{:S(2)}, u32[]{:S(2)}) %collective-permute-start.10) | collective-permute-done | bytes 65568 | tf_op jit(solution)/shard_map/ppermute | solution.py:595
  82.0 1.8 %collective-permute-start.15 = (bf16[2,64,512]{2,1,0:T(8,128)(2,1)S(1)}, bf16[2,64,512]{2,1,0:T(8,128)(2,1)S(1)}, u32[]{:S(2)}, u32[]{:S(2)}) collective-permute-start(bf16[2,64,512]{2,1,0:T(8,128)(2,1)S(1)} %get-tuple-element.94), channel_id=1, source_target_pairs={{0,2},{2,0},{4,6},{6,4},{8,10},{10,8},{12,14},{14,12},{1,3},{3,1},... | collective-permute-start | bytes 393224 | tf_op jit(solution)/shard_map/ppermute | solution.py:595
  85.0 2.8 %collective-permute-done.16 = bf16[2,64,512]{2,1,0:T(8,128)(2,1)S(1)} collective-permute-done((bf16[2,64,512]{2,1,0:T(8,128)(2,1)S(1)}, bf16[2,64,512]{2,1,0:T(8,128)(2,1)S(1)}, u32[]{:S(2)}, u32[]{:S(2)}) %collective-permute-start.16) | collective-permute-done | bytes 131104 | tf_op jit(solution)/shard_map/ppermute | solution.py:595
  88.9 1.7 %collective-permute-done.17 = bf16[2,64,512]{2,1,0:T(8,128)(2,1)S(1)} collective-permute-done((bf16[2,64,512]{2,1,0:T(8,128)(2,1)S(1)}, bf16[2,64,512]{2,1,0:T(8,128)(2,1)S(1)}, u32[]{:S(2)}, u32[]{:S(2)}) %collective-permute-start.17) | collective-permute-done | bytes 131104 | tf_op jit(solution)/shard_map/ppermute | solution.py:595
  93.8 5.5 %shard_map.70 = (f32[64,512]{1,0:T(8,128)S(1)}, f32[64,512]{1,0:T(8,128)S(1)}, bf16[2,64,512]{2,1,0:T(8,128)(2,1)S(1)}, bf16[2,64,512]{2,1,0:T(8,128)(2,1)S(1)}, bf16[2,64,512]{2,1,0:T(8,128)(2,1)S(1)}) custom-call(s32[3]{0:T(128)S(1)} %copy-done.3, bf16[512,1024]{1,0:T(8,128)(2,1)S(1)} %get-tuple-element.71.tokens, ...), custom_call_target="tpu_custom_call" | custom-call | tf_op jit(solution)/shard_map/pallas_call | solution.py:541
  101.1 1.8 %collective-permute-start.24 = (bf16[2,64,512]{2,1,0:T(8,128)(2,1)S(1)}, bf16[2,64,512]{2,1,0:T(8,128)(2,1)S(1)}, u32[]{:S(2)}, u32[]{:S(2)}) collective-permute-start(bf16[2,64,512]{2,1,0:T(8,128)(2,1)S(1)} %get-tuple-element.90), channel_id=1, source_target_pairs={{0,6},{2,4},{4,2},{6,0},{8,14},{10,12},{12,10},{14,8},{1,7},{3,5},... | collective-permute-start | bytes 393224 | tf_op jit(solution)/shard_map/ppermute | solution.py:595
  102.8 2.0 %collective-permute-done.22.refs_0_ = bf16[2,64,512]{2,1,0:T(8,128)(2,1)S(1)} collective-permute-done((bf16[2,64,512]{2,1,0:T(8,128)(2,1)S(1)}, bf16[2,64,512]{2,1,0:T(8,128)(2,1)S(1)}, u32[]{:S(2)}, u32[]{:S(2)}) %collective-permute-start.22) | collective-permute-done | bytes 131104 | tf_op jit(solution)/shard_map/ppermute | solution.py:595
  104.9 1.6 %collective-permute-done.23.refs_1_ = bf16[2,64,512]{2,1,0:T(8,128)(2,1)S(1)} collective-permute-done((bf16[2,64,512]{2,1,0:T(8,128)(2,1)S(1)}, bf16[2,64,512]{2,1,0:T(8,128)(2,1)S(1)}, u32[]{:S(2)}, u32[]{:S(2)}) %collective-permute-start.23) | collective-permute-done | bytes 131104 | tf_op jit(solution)/shard_map/ppermute | solution.py:595
  106.5 2.4 %collective-permute-done.24.refs_2_ = bf16[2,64,512]{2,1,0:T(8,128)(2,1)S(1)} collective-permute-done((bf16[2,64,512]{2,1,0:T(8,128)(2,1)S(1)}, bf16[2,64,512]{2,1,0:T(8,128)(2,1)S(1)}, u32[]{:S(2)}, u32[]{:S(2)}) %collective-permute-start.24) | collective-permute-done | bytes 131104 | tf_op jit(solution)/shard_map/ppermute | solution.py:595
  108.9 2.6 %collective-permute-start.25 = (bf16[64,512]{1,0:T(8,128)(2,1)S(1)}, bf16[64,512]{1,0:T(8,128)(2,1)S(1)}, u32[]{:S(2)}, u32[]{:S(2)}) collective-permute-start(bf16[64,512]{1,0:T(8,128)(2,1)S(1)} %get-tuple-element.92), channel_id=1, source_target_pairs={{0,8},{2,10},{4,12},{6,14},{8,0},{10,2},{12,4},{14,6},{1,9},{3,11}... | collective-permute-start | bytes 196616 | tf_op jit(solution)/shard_map/ppermute | solution.py:595
  111.5 3.3 %collective-permute-done.25.across_ref = bf16[64,512]{1,0:T(8,128)(2,1)S(1)} collective-permute-done((bf16[64,512]{1,0:T(8,128)(2,1)S(1)}, bf16[64,512]{1,0:T(8,128)(2,1)S(1)}, u32[]{:S(2)}, u32[]{:S(2)}) %collective-permute-start.25) | collective-permute-done | bytes 65568 | tf_op jit(solution)/shard_map/ppermute | solution.py:595
  (73 shorter events, 20.4 us)
Async XLA Ops:
  0.6 6.8 %copy-start.9 = (bf16[1,40,4,1024]{3,2,1,0:T(4,128)(2,1)S(1)}, bf16[1,40,4,1024]{3,2,1,0:T(4,128)(2,1)}, u32[]{:S(2)}) copy-start(bf16[1,40,4,1024]{3,2,1,0:T(4,128)(2,1)} %param.6) | copy-start | bytes 983044
  3.3 4.2 %copy-start.2 = (s32[3]{0:T(128)S(1)}, s32[3]{0:T(128)}, u32[]{:S(2)}) copy-start(s32[3]{0:T(128)} %pad_add_fusion.rank_ref.scalars) | copy-start | bytes 40
  3.3 4.2 %copy-start.4 = (s32[1,64]{1,0:T(1,128)S(1)}, s32[1,64]{1,0:T(1,128)}, u32[]{:S(2)}) copy-start(s32[1,64]{1,0:T(1,128)} %keep_ref.3) | copy-start | bytes 772
  3.3 12.0 %collective-permute-start = (bf16[640,128]{1,0:T(8,128)(2,1)}, bf16[640,128]{1,0:T(8,128)(2,1)S(1)}, u32[]{:S(2)}, u32[]{:S(2)}) collective-permute-start(bf16[640,128]{1,0:T(8,128)(2,1)} %get-tuple-element.49), channel_id=1, source_target_pairs={{0,8},{2,10},{4,12},{6,14},{8,0},{10,2},{12,4},{14,6},{1,9},{3,11}... | collective-permute-start | bytes 491528 | tf_op jit(solution)/shard_map/ppermute | solution.py:595
  15.3 13.5 %all-to-all-start = ((bf16[8,80,128]{2,1,0:T(8,128)(2,1)}), bf16[8,80,128]{2,1,0:T(8,128)(2,1)S(1)}, u32[]{:S(2)}, u32[]{:S(2)}) async-start(bf16[8,80,128]{2,1,0:T(8,128)(2,1)} %bitcast.4), calls=%async_computation | async-start | bytes 327680 | tf_op jit(solution)/shard_map/all_to_all | solution.py:599
  23.9 7.5 %collective-permute-start.2 = (bf16[704,128]{1,0:T(8,128)(2,1)}, bf16[704,128]{1,0:T(8,128)(2,1)S(1)}, u32[]{:S(2)}, u32[]{:S(2)}) collective-permute-start(bf16[704,128]{1,0:T(8,128)(2,1)} %get-tuple-element.58), channel_id=1, source_target_pairs={{0,2},{2,0},{4,6},{6,4},{8,10},{10,8},{12,14},{14,12},{1,3},{3,1},... | collective-permute-start | bytes 540680 | tf_op jit(solution)/shard_map/ppermute | solution.py:595
  26.0 8.4 %collective-permute-start.3 = (bf16[704,128]{1,0:T(8,128)(2,1)}, bf16[704,128]{1,0:T(8,128)(2,1)S(1)}, u32[]{:S(2)}, u32[]{:S(2)}) collective-permute-start(bf16[704,128]{1,0:T(8,128)(2,1)} %get-tuple-element.59), channel_id=1, source_target_pairs={{0,4},{2,6},{4,0},{6,2},{8,12},{10,14},{12,8},{14,10},{1,5},{3,7},... | collective-permute-start | bytes 540680 | tf_op jit(solution)/shard_map/ppermute | solution.py:595
  27.5 10.1 %collective-permute-start.4 = (bf16[704,128]{1,0:T(8,128)(2,1)}, bf16[704,128]{1,0:T(8,128)(2,1)S(1)}, u32[]{:S(2)}, u32[]{:S(2)}) collective-permute-start(bf16[704,128]{1,0:T(8,128)(2,1)} %get-tuple-element.60), channel_id=1, source_target_pairs={{0,6},{2,4},{4,2},{6,0},{8,14},{10,12},{12,10},{14,8},{1,7},{3,5},... | collective-permute-start | bytes 540680 | tf_op jit(solution)/shard_map/ppermute | solution.py:595
  29.8 7.8 %collective-permute-start.1 = (bf16[256,128]{1,0:T(8,128)(2,1)S(1)}, bf16[256,128]{1,0:T(8,128)(2,1)S(1)}, u32[]{:S(2)}, u32[]{:S(2)}) collective-permute-start(bf16[256,128]{1,0:T(8,128)(2,1)S(1)} %shard_map.66.owned_ref), channel_id=1, source_target_pairs={{0,8},{2,10},{4,12},{6,14},{8,0},{10,2},{12,4},{14,6},{1,9},{3,11}... | collective-permute-start | bytes 196616 | tf_op jit(solution)/shard_map/ppermute | solution.py:595
  38.6 20.7 %all-to-all-start.1 = ((bf16[4,864,128]{2,1,0:T(8,128)(2,1)}), bf16[4,864,128]{2,1,0:T(8,128)(2,1)S(1)}, u32[]{:S(2)}, u32[]{:S(2)}) async-start(bf16[4,864,128]{2,1,0:T(8,128)(2,1)} %shard_map.68), calls=%async_computation.1 | async-start | bytes 1769472 | tf_op jit(solution)/shard_map/all_to_all | solution.py:605
  42.4 14.8 %collective-permute-start.7 = (bf16[4,512,128]{2,1,0:T(8,128)(2,1)S(1)}, bf16[4,512,128]{2,1,0:T(8,128)(2,1)S(1)}, u32[]{:S(2)}, u32[]{:S(2)}) collective-permute-start(bf16[4,512,128]{2,1,0:T(8,128)(2,1)S(1)} %pad_maximum_fusion.refs_8_), channel_id=1, source_target_pairs={{0,1},{1,0},{2,3},{3,2},{4,5},{5,4},{6,7},{7,6},{8,9},{9,8},{10,11... | collective-permute-start | bytes 1572872 | tf_op jit(solution)/shard_map/ppermute | solution.py:595
  42.5 14.7 %collective-permute-start.6 = (bf16[4,512,128]{2,1,0:T(8,128)(2,1)S(1)}, bf16[4,512,128]{2,1,0:T(8,128)(2,1)}, u32[]{:S(2)}, u32[]{:S(2)}) collective-permute-start(bf16[4,512,128]{2,1,0:T(8,128)(2,1)S(1)} %pad_maximum_fusion.refs_8_), channel_id=1, source_target_pairs={{0,16},{16,0},{1,17},{17,1},{2,18},{18,2},{3,19},{19,3},{4,20},{20... | collective-permute-start | bytes 1572872 | tf_op jit(solution)/shard_map/ppermute | solution.py:595
  44.1 13.2 %collective-permute-start.5 = (bf16[4,256,128]{2,1,0:T(8,128)(2,1)S(1)}, bf16[4,256,128]{2,1,0:T(8,128)(2,1)}, u32[]{:S(2)}, u32[]{:S(2)}) collective-permute-start(bf16[4,256,128]{2,1,0:T(8,128)(2,1)S(1)} %copy-done.11), channel_id=1, source_target_pairs={{0,8},{2,10},{4,12},{6,14},{8,0},{10,2},{12,4},{14,6},{1,9},{3,11}... | collective-permute-start | bytes 786440 | tf_op jit(solution)/shard_map/ppermute | solution.py:595
  60.2 6.9 %collective-permute-start.8 = (bf16[4,512,128]{2,1,0:T(8,128)(2,1)}, bf16[4,512,128]{2,1,0:T(8,128)(2,1)S(1)}, u32[]{:S(2)}, u32[]{:S(2)}) collective-permute-start(bf16[4,512,128]{2,1,0:T(8,128)(2,1)} %slice.44), channel_id=1, source_target_pairs={{0,1},{1,0},{2,3},{3,2},{4,5},{5,4},{6,7},{7,6},{8,9},{9,8},{10,11... | collective-permute-start | bytes 1572872 | tf_op jit(solution)/shard_map/ppermute | solution.py:595
  60.2 6.3 %collective-permute-start.9 = (bf16[4,96,128]{2,1,0:T(8,128)(2,1)S(1)}, bf16[4,96,128]{2,1,0:T(8,128)(2,1)S(1)}, u32[]{:S(2)}, u32[]{:S(2)}) collective-permute-start(bf16[4,96,128]{2,1,0:T(8,128)(2,1)S(1)} %slice.45), channel_id=1, source_target_pairs={{0,16},{16,0},{1,17},{17,1},{2,18},{18,2},{3,19},{19,3},{4,20},{20... | collective-permute-start | bytes 294920 | tf_op jit(solution)/shard_map/ppermute | solution.py:595
  62.5 14.5 %all-to-all-start.2 = ((bf16[4,256,128]{2,1,0:T(8,128)(2,1)}), bf16[4,256,128]{2,1,0:T(8,128)(2,1)S(1)}, u32[]{:S(2)}, u32[]{:S(2)}) async-start(bf16[4,256,128]{2,1,0:T(8,128)(2,1)} %collective-permute-done.5), calls=%async_computation.2 | async-start | bytes 524288 | tf_op jit(solution)/shard_map/all_to_all | solution.py:605
  65.9 10.4 %collective-permute-start.12 = (bf16[4,256,128]{2,1,0:T(8,128)(2,1)}, bf16[4,256,128]{2,1,0:T(8,128)(2,1)S(1)}, u32[]{:S(2)}, u32[]{:S(2)}) collective-permute-start(bf16[4,256,128]{2,1,0:T(8,128)(2,1)} %slice.46), channel_id=1, source_target_pairs={{0,1},{1,0},{2,3},{3,2},{4,5},{5,4},{6,7},{7,6},{8,9},{9,8},{10,11... | collective-permute-start | bytes 786440 | tf_op jit(solution)/shard_map/ppermute | solution.py:595
  66.2 10.8 %collective-permute-start.11 = (bf16[4,512,128]{2,1,0:T(8,128)(2,1)}, bf16[4,512,128]{2,1,0:T(8,128)(2,1)}, u32[]{:S(2)}, u32[]{:S(2)}) collective-permute-start(bf16[4,512,128]{2,1,0:T(8,128)(2,1)} %collective-permute-done.6.refs_9_), channel_id=1, source_target_pairs={{0,1},{1,0},{2,3},{3,2},{4,5},{5,4},{6,7},{7,6},{8,9},{9,8},{10,11... | collective-permute-start | bytes 1572872 | tf_op jit(solution)/shard_map/ppermute | solution.py:595
  73.2 6.9 %collective-permute-start.10 = (bf16[64,512]{1,0:T(8,128)(2,1)}, bf16[64,512]{1,0:T(8,128)(2,1)}, u32[]{:S(2)}, u32[]{:S(2)}) collective-permute-start(bf16[64,512]{1,0:T(8,128)(2,1)} %get-tuple-element.72), channel_id=1, source_target_pairs={{0,8},{2,10},{4,12},{6,14},{8,0},{10,2},{12,4},{14,6},{1,9},{3,11}... | collective-permute-start | bytes 196616 | tf_op jit(solution)/shard_map/ppermute | solution.py:595
  74.5 16.0 %collective-permute-start.14 = (bf16[4,256,128]{2,1,0:T(8,128)(2,1)S(1)}, bf16[4,256,128]{2,1,0:T(8,128)(2,1)S(1)}, u32[]{:S(2)}, u32[]{:S(2)}) collective-permute-start(bf16[4,256,128]{2,1,0:T(8,128)(2,1)S(1)} %slice.47.refs_4_), channel_id=1, source_target_pairs={{0,16},{16,0},{1,17},{17,1},{2,18},{18,2},{3,19},{19,3},{4,20},{20... | collective-permute-start | bytes 786440 | tf_op jit(solution)/shard_map/ppermute | solution.py:595
  80.0 10.5 %collective-permute-start.13 = (bf16[4,256,128]{2,1,0:T(8,128)(2,1)S(1)}, bf16[4,256,128]{2,1,0:T(8,128)(2,1)S(1)}, u32[]{:S(2)}, u32[]{:S(2)}) collective-permute-start(bf16[4,256,128]{2,1,0:T(8,128)(2,1)S(1)} %all-to-all-done.2.refs_0_), channel_id=1, source_target_pairs={{0,16},{16,0},{1,17},{17,1},{2,18},{18,2},{3,19},{19,3},{4,20},{20... | collective-permute-start | bytes 786440 | tf_op jit(solution)/shard_map/ppermute | solution.py:595
  81.4 6.3 %collective-permute-start.16 = (bf16[2,64,512]{2,1,0:T(8,128)(2,1)S(1)}, bf16[2,64,512]{2,1,0:T(8,128)(2,1)S(1)}, u32[]{:S(2)}, u32[]{:S(2)}) collective-permute-start(bf16[2,64,512]{2,1,0:T(8,128)(2,1)S(1)} %get-tuple-element.94), channel_id=1, source_target_pairs={{0,4},{2,6},{4,0},{6,2},{8,12},{10,14},{12,8},{14,10},{1,5},{3,7},... | collective-permute-start | bytes 393224 | tf_op jit(solution)/shard_map/ppermute | solution.py:595
  82.0 6.9 %collective-permute-start.15 = (bf16[2,64,512]{2,1,0:T(8,128)(2,1)S(1)}, bf16[2,64,512]{2,1,0:T(8,128)(2,1)S(1)}, u32[]{:S(2)}, u32[]{:S(2)}) collective-permute-start(bf16[2,64,512]{2,1,0:T(8,128)(2,1)S(1)} %get-tuple-element.94), channel_id=1, source_target_pairs={{0,2},{2,0},{4,6},{6,4},{8,10},{10,8},{12,14},{14,12},{1,3},{3,1},... | collective-permute-start | bytes 393224 | tf_op jit(solution)/shard_map/ppermute | solution.py:595
  83.9 6.7 %collective-permute-start.17 = (bf16[2,64,512]{2,1,0:T(8,128)(2,1)S(1)}, bf16[2,64,512]{2,1,0:T(8,128)(2,1)S(1)}, u32[]{:S(2)}, u32[]{:S(2)}) collective-permute-start(bf16[2,64,512]{2,1,0:T(8,128)(2,1)S(1)} %get-tuple-element.94), channel_id=1, source_target_pairs={{0,6},{2,4},{4,2},{6,0},{8,14},{10,12},{12,10},{14,8},{1,7},{3,5},... | collective-permute-start | bytes 393224 | tf_op jit(solution)/shard_map/ppermute | solution.py:595
  90.7 3.1 %collective-permute-start.18 = (bf16[4,2,64,512]{3,2,1,0:T(8,128)(2,1)S(1)}, bf16[4,2,64,512]{3,2,1,0:T(8,128)(2,1)S(1)}, u32[]{:S(2)}, u32[]{:S(2)}) collective-permute-start(bf16[4,2,64,512]{3,2,1,0:T(8,128)(2,1)S(1)} %pad_maximum_fusion.1.a), channel_id=1, source_target_pairs={{0,1},{1,0},{2,3},{3,2},{4,5},{5,4},{6,7},{7,6},{8,9},{9,8},{10,11... | collective-permute-start | bytes 1572872 | tf_op jit(solution)/shard_map/ppermute | solution.py:595
  90.7 2.3 %collective-permute-start.19 = (bf16[4,256,128]{2,1,0:T(8,128)(2,1)S(1)}, bf16[4,256,128]{2,1,0:T(8,128)(2,1)S(1)}, u32[]{:S(2)}, u32[]{:S(2)}) collective-permute-start(bf16[4,256,128]{2,1,0:T(8,128)(2,1)S(1)} %all-to-all-done.2.refs_0_), channel_id=1, source_target_pairs={{0,1},{1,0},{2,3},{3,2},{4,5},{5,4},{6,7},{7,6},{8,9},{9,8},{10,11... | collective-permute-start | bytes 786440 | tf_op jit(solution)/shard_map/ppermute | solution.py:595
  91.2 2.1 %collective-permute-start.20 = (bf16[4,256,128]{2,1,0:T(8,128)(2,1)S(1)}, bf16[4,256,128]{2,1,0:T(8,128)(2,1)S(1)}, u32[]{:S(2)}, u32[]{:S(2)}) collective-permute-start(bf16[4,256,128]{2,1,0:T(8,128)(2,1)S(1)} %collective-permute-done.13.refs_1_), channel_id=1, source_target_pairs={{0,1},{1,0},{2,3},{3,2},{4,5},{5,4},{6,7},{7,6},{8,9},{9,8},{10,11... | collective-permute-start | bytes 786440 | tf_op jit(solution)/shard_map/ppermute | solution.py:595
  91.3 2.4 %collective-permute-start.21 = (bf16[4,256,128]{2,1,0:T(8,128)(2,1)S(1)}, bf16[4,256,128]{2,1,0:T(8,128)(2,1)S(1)}, u32[]{:S(2)}, u32[]{:S(2)}) collective-permute-start(bf16[4,256,128]{2,1,0:T(8,128)(2,1)S(1)} %collective-permute-done.14.refs_5_), channel_id=1, source_target_pairs={{0,1},{1,0},{2,3},{3,2},{4,5},{5,4},{6,7},{7,6},{8,9},{9,8},{10,11... | collective-permute-start | bytes 786440 | tf_op jit(solution)/shard_map/ppermute | solution.py:595
  99.3 5.6 %collective-permute-start.22 = (bf16[2,64,512]{2,1,0:T(8,128)(2,1)S(1)}, bf16[2,64,512]{2,1,0:T(8,128)(2,1)S(1)}, u32[]{:S(2)}, u32[]{:S(2)}) collective-permute-start(bf16[2,64,512]{2,1,0:T(8,128)(2,1)S(1)} %get-tuple-element.88), channel_id=1, source_target_pairs={{0,2},{2,0},{4,6},{6,4},{8,10},{10,8},{12,14},{14,12},{1,3},{3,1},... | collective-permute-start | bytes 393224 | tf_op jit(solution)/shard_map/ppermute | solution.py:595
  100.1 6.4 %collective-permute-start.23 = (bf16[2,64,512]{2,1,0:T(8,128)(2,1)S(1)}, bf16[2,64,512]{2,1,0:T(8,128)(2,1)S(1)}, u32[]{:S(2)}, u32[]{:S(2)}) collective-permute-start(bf16[2,64,512]{2,1,0:T(8,128)(2,1)S(1)} %get-tuple-element.89), channel_id=1, source_target_pairs={{0,4},{2,6},{4,0},{6,2},{8,12},{10,14},{12,8},{14,10},{1,5},{3,7},... | collective-permute-start | bytes 393224 | tf_op jit(solution)/shard_map/ppermute | solution.py:595
  101.1 7.8 %collective-permute-start.24 = (bf16[2,64,512]{2,1,0:T(8,128)(2,1)S(1)}, bf16[2,64,512]{2,1,0:T(8,128)(2,1)S(1)}, u32[]{:S(2)}, u32[]{:S(2)}) collective-permute-start(bf16[2,64,512]{2,1,0:T(8,128)(2,1)S(1)} %get-tuple-element.90), channel_id=1, source_target_pairs={{0,6},{2,4},{4,2},{6,0},{8,14},{10,12},{12,10},{14,8},{1,7},{3,5},... | collective-permute-start | bytes 393224 | tf_op jit(solution)/shard_map/ppermute | solution.py:595
  108.9 5.9 %collective-permute-start.25 = (bf16[64,512]{1,0:T(8,128)(2,1)S(1)}, bf16[64,512]{1,0:T(8,128)(2,1)S(1)}, u32[]{:S(2)}, u32[]{:S(2)}) collective-permute-start(bf16[64,512]{1,0:T(8,128)(2,1)S(1)} %get-tuple-element.92), channel_id=1, source_target_pairs={{0,8},{2,10},{4,12},{6,14},{8,0},{10,2},{12,4},{14,6},{1,9},{3,11}... | collective-permute-start | bytes 196616 | tf_op jit(solution)/shard_map/ppermute | solution.py:595
  (9 other events, 14.1 us)

commit v17 on v14

--- a/solution.py
+++ b/solution.py
@@ -659,7 +659,11 @@
     )
 
     att_across = swap(attended, "seq", half)
-    att_across, near_last = lax.optimization_barrier((att_across, swap(near_other, "head", 1)))
+    far_last = swap(got[:, top + head_rows // 2 :], "head", 1)
+    att_across, near_last, far_last = lax.optimization_barrier(
+        (att_across, swap(near_other, "head", 1), far_last)
+    )
+    units = far_last.shape[1] - out_rows
     got = after(got, attended)
     mlp_mine = got[:, top + head_rows // 2 : got.shape[1] - out_rows]
     far_mine = got[:, got.shape[1] - out_rows :]
@@ -675,8 +679,8 @@
         scalars,
         tokens,
         (gathered, swap(gathered, "head", 1)),
-        (mlp_pair, tuple(swap(value, "head", 1) for value in mlp_pair)),
-        (far_pair, tuple(swap(value, "head", 1) for value in far_pair)),
+        (mlp_pair, (far_last[:, :units], swap(mlp_other, "head", 1))),
+        (far_pair, (far_last[:, units:], swap(far_other, "head", 1))),
         ((near_mine, near_other), (near_pair, near_last)),
         n,
     )

time: 107 us -> 106 us (level)
    ppermute x25 -> x24, waiting for transfers between devices: 39 us -> 38.4 us  [swap(): return lax.ppermute(value, axis, [(i, i ^ j) for i in range(n)])]
    ppermute x25 -> x24, starting transfers between devices: 29.4 us -> 29.2 us  [swap(): return lax.ppermute(value, axis, [(i, i ^ j) for i in range(n)])]
  transfers between devices with their start and end apart: 27 -> 26, of which waited for: 20 -> 18; matrix products, arithmetic and copies ran while one was open for 0% -> 0% of each run, Pallas kernels for 8% -> 8%
where the time goes in v17:
time: 106 us
  waiting for transfers between devices  49.3 us (47%)
  starting transfers between devices  36.7 us (35%)
  Pallas kernels  18.5 us (17%)
    ppermute x24, waiting for transfers between devices, swap(): return lax.ppermute(value, axis, [(i, i ^ j) for i in range(n)])  38.4 us
    ppermute x24, starting transfers between devices, swap(): return lax.ppermute(value, axis, [(i, i ^ j) for i in range(n)])  29.2 us
    all_to_all x1, waiting for transfers between devices, exchange(): return lax.all_to_all(value, 'seq', split_axis=0, concat_axis=0, tiled=True)  10.7 us
    pallas_call x2, Pallas kernels, pack(): pl.pallas_call(kernel, in_specs=[sspec()] + [hspec()] * 4, out_specs=[vsp...  5.57 us
    pallas_call x1, Pallas kernels, mlp(): pl.pallas_call(kernel, in_specs=[sspec()] + [vspec()] * 3 + [aspec()] * 1...  5.45 us
    all_to_all x1, starting transfers between devices, exchange(): return lax.all_to_all(value, 'seq', split_axis=0, concat_axis=0, tiled=True)  3.81 us
    all_to_all x1, starting transfers between devices, exchange_half(): lax.all_to_all(value, 'seq', split_axis=0, concat_axis=0, axis_index_grou...  3.66 us
    pallas_call x1, Pallas kernels, attend_fast(): pl.pallas_call(functools.partial(attend_kernel, n, per_owner), in_specs=[...  2.68 us
  transfers between devices with their start and end apart: 26, of which 18 were waited for; matrix products, arithmetic and copies ran while one was open for 0% of the time, Pallas kernels for 8%

profile of v17, /device:TPU:0, one launch (start us, length us, event | category | flops | bytes accessed | tf_op | source)
XLA Modules:
  0.0 105.8 jit_solution(1331091675822237259)
XLA Ops:
  0.7 2.7 %shard_map.64 = bf16[1664,128]{1,0:T(8,128)(2,1)} custom-call(s32[3]{0:T(128)} %pad_add_fusion.rank_ref.scalars, bf16[8,192,128]{2,1,0:T(8,128)(2,1)} %bitcast.32, bf16[512,128]{1,0:T(8,128)(2,1)} %out_weight_ref.2, bf16[128,2048]{1,0:T(8,128)(2,1)} %up_ref.2, bf16[2048,128]{1,0:T(8,128)(2,1)} %down_ref.2), custom_call_target="tpu_custom_call" | custom-call | tf_op jit(solution)/shard_map/pallas_call | solution.py:344
  3.4 4.1 %collective-permute-start.1 = (bf16[1664,128]{1,0:T(8,128)(2,1)}, bf16[1664,128]{1,0:T(8,128)(2,1)S(1)}, u32[]{:S(2)}, u32[]{:S(2)}) collective-permute-start(bf16[1664,128]{1,0:T(8,128)(2,1)} %shard_map.64), channel_id=1, source_target_pairs={{0,8},{2,10},{4,12},{6,14},{8,0},{10,2},{12,4},{14,6},{1,9},{3,11}... | collective-permute-start | bytes 1277960 | tf_op jit(solution)/shard_map/ppermute | solution.py:597
  7.6 2.0 %shard_map.65 = bf16[640,128]{1,0:T(8,128)(2,1)} custom-call(s32[3]{0:T(128)S(1)} %copy-done, s32[1,64]{1,0:T(1,128)S(1)} %copy-done.2, bf16[160,1024]{1,0:T(8,128)(2,1)S(1)} %reshape.8.patches_ref), custom_call_target="tpu_custom_call" | custom-call | tf_op jit(solution)/shard_map/pallas_call | solution.py:247
  9.6 3.8 %all-to-all-start = ((bf16[8,80,128]{2,1,0:T(8,128)(2,1)}), bf16[8,80,128]{2,1,0:T(8,128)(2,1)S(1)}, u32[]{:S(2)}, u32[]{:S(2)}) async-start(bf16[8,80,128]{2,1,0:T(8,128)(2,1)} %bitcast.4), calls=%async_computation | async-start | bytes 327680 | tf_op jit(solution)/shard_map/all_to_all | solution.py:601
  13.4 2.9 %shard_map.67 = (bf16[704,128]{1,0:T(8,128)(2,1)}, bf16[704,128]{1,0:T(8,128)(2,1)}, bf16[704,128]{1,0:T(8,128)(2,1)}, bf16[704,128]{1,0:T(8,128)(2,1)}) custom-call(s32[3]{0:T(128)} %pad_add_fusion.rank_ref.scalars, bf16[8,192,128]{2,1,0:T(8,128)(2,1)} %bitcast.33, bf16[512,128]{1,0:T(8,128)(2,1)} %out_weight_ref.2, bf16[128,2048]{1,0:T(8,128)(2,1)} %up_ref.2, ...), custom_call_target="tpu_custom_call" | custom-call | tf_op jit(solution)/shard_map/pallas_call | solution.py:344
  16.3 2.1 %collective-permute-start.2 = (bf16[704,128]{1,0:T(8,128)(2,1)}, bf16[704,128]{1,0:T(8,128)(2,1)S(1)}, u32[]{:S(2)}, u32[]{:S(2)}) collective-permute-start(bf16[704,128]{1,0:T(8,128)(2,1)} %get-tuple-element.48), channel_id=1, source_target_pairs={{0,2},{2,0},{4,6},{6,4},{8,10},{10,8},{12,14},{14,12},{1,3},{3,1},... | collective-permute-start | bytes 540680 | tf_op jit(solution)/shard_map/ppermute | solution.py:597
  18.4 1.5 %collective-permute-start.3 = (bf16[704,128]{1,0:T(8,128)(2,1)}, bf16[704,128]{1,0:T(8,128)(2,1)S(1)}, u32[]{:S(2)}, u32[]{:S(2)}) collective-permute-start(bf16[704,128]{1,0:T(8,128)(2,1)} %get-tuple-element.49), channel_id=1, source_target_pairs={{0,4},{2,6},{4,0},{6,2},{8,12},{10,14},{12,8},{14,10},{1,5},{3,7},... | collective-permute-start | bytes 540680 | tf_op jit(solution)/shard_map/ppermute | solution.py:597
  19.9 10.7 %all-to-all-done = bf16[8,80,128]{2,1,0:T(8,128)(2,1)S(1)} async-done(((bf16[8,80,128]{2,1,0:T(8,128)(2,1)}), bf16[8,80,128]{2,1,0:T(8,128)(2,1)S(1)}, u32[]{:S(2)}, u32[]{:S(2)}) %all-to-all-start) | async-done | bytes 163872 | tf_op jit(solution)/shard_map/all_to_all | solution.py:601
  31.5 2.9 %collective-permute-start = (bf16[256,128]{1,0:T(8,128)(2,1)S(1)}, bf16[256,128]{1,0:T(8,128)(2,1)S(1)}, u32[]{:S(2)}, u32[]{:S(2)}) collective-permute-start(bf16[256,128]{1,0:T(8,128)(2,1)S(1)} %shard_map.66.owned_ref), channel_id=1, source_target_pairs={{0,8},{2,10},{4,12},{6,14},{8,0},{10,2},{12,4},{14,6},{1,9},{3,11}... | collective-permute-start | bytes 196616 | tf_op jit(solution)/shard_map/ppermute | solution.py:597
  34.4 3.2 %collective-permute-done.4 = bf16[704,128]{1,0:T(8,128)(2,1)S(1)} collective-permute-done((bf16[704,128]{1,0:T(8,128)(2,1)}, bf16[704,128]{1,0:T(8,128)(2,1)S(1)}, u32[]{:S(2)}, u32[]{:S(2)}) %collective-permute-start.4) | collective-permute-done | bytes 180256 | tf_op jit(solution)/shard_map/ppermute | solution.py:597
  39.2 3.7 %all-to-all-start.1 = ((bf16[4,1120,128]{2,1,0:T(8,128)(2,1)}), bf16[4,1120,128]{2,1,0:T(8,128)(2,1)S(1)}, u32[]{:S(2)}, u32[]{:S(2)}) async-start(bf16[4,1120,128]{2,1,0:T(8,128)(2,1)} %shard_map.68), calls=%async_computation.1 | async-start | bytes 2293760 | tf_op jit(solution)/shard_map/all_to_all | solution.py:607
  43.1 1.6 %collective-permute-start.5 = (bf16[4,512,128]{2,1,0:T(8,128)(2,1)S(1)}, bf16[4,512,128]{2,1,0:T(8,128)(2,1)S(1)}, u32[]{:S(2)}, u32[]{:S(2)}) collective-permute-start(bf16[4,512,128]{2,1,0:T(8,128)(2,1)S(1)} %pad_maximum_fusion.refs_8_), channel_id=1, source_target_pairs={{0,16},{16,0},{1,17},{17,1},{2,18},{18,2},{3,19},{19,3},{4,20},{20... | collective-permute-start | bytes 1572872 | tf_op jit(solution)/shard_map/ppermute | solution.py:597
  45.0 12.4 %collective-permute-done.5.refs_9_ = bf16[4,512,128]{2,1,0:T(8,128)(2,1)S(1)} collective-permute-done((bf16[4,512,128]{2,1,0:T(8,128)(2,1)S(1)}, bf16[4,512,128]{2,1,0:T(8,128)(2,1)S(1)}, u32[]{:S(2)}, u32[]{:S(2)}) %collective-permute-start.5) | collective-permute-done | bytes 524320 | tf_op jit(solution)/shard_map/ppermute | solution.py:597
  57.8 1.6 %collective-permute-start.8 = (bf16[4,96,128]{2,1,0:T(8,128)(2,1)S(1)}, bf16[4,96,128]{2,1,0:T(8,128)(2,1)S(1)}, u32[]{:S(2)}, u32[]{:S(2)}) collective-permute-start(bf16[4,96,128]{2,1,0:T(8,128)(2,1)S(1)} %slice.54), channel_id=1, source_target_pairs={{0,16},{16,0},{1,17},{17,1},{2,18},{18,2},{3,19},{19,3},{4,20},{20... | collective-permute-start | bytes 294920 | tf_op jit(solution)/shard_map/ppermute | solution.py:597
  59.9 3.2 %collective-permute-done.8.far_ref = bf16[4,96,128]{2,1,0:T(8,128)(2,1)S(1)} collective-permute-done((bf16[4,96,128]{2,1,0:T(8,128)(2,1)S(1)}, bf16[4,96,128]{2,1,0:T(8,128)(2,1)S(1)}, u32[]{:S(2)}, u32[]{:S(2)}) %collective-permute-start.8) | collective-permute-done | bytes 98336 | tf_op jit(solution)/shard_map/ppermute | solution.py:597
  63.1 2.7 %shard_map.69 = (bf16[512,1024]{1,0:T(8,128)(2,1)S(1)}, bf16[64,512]{1,0:T(8,128)(2,1)S(1)}) custom-call(s32[3]{0:T(128)S(1)} %copy-done.1, bf16[4,1120,128]{2,1,0:T(8,128)(2,1)S(1)} %all-to-all-done.1.mine_ref, bf16[4,512,128]{2,1,0:T(8,128)(2,1)S(1)} %collective-permute-done.7.other_ref, bf16[4,192,128]{2,1,0:T(8,128)(2,1)S(1)} %pad_maximum_fusion.2.near_ref, ...), custom_call_target="tpu_custom_call" | custom-call | flops 30000001024 | bytes 1048576 | tf_op jit(solution)/shard_map/pallas_call | solution.py:452
  65.8 2.9 %collective-permute-start.9 = (bf16[64,512]{1,0:T(8,128)(2,1)S(1)}, bf16[64,512]{1,0:T(8,128)(2,1)S(1)}, u32[]{:S(2)}, u32[]{:S(2)}) collective-permute-start(bf16[64,512]{1,0:T(8,128)(2,1)S(1)} %get-tuple-element.60), channel_id=1, source_target_pairs={{0,8},{2,10},{4,12},{6,14},{8,0},{10,2},{12,4},{14,6},{1,9},{3,11}... | collective-permute-start | bytes 196616 | tf_op jit(solution)/shard_map/ppermute | solution.py:597
  68.7 1.6 %collective-permute-start.13 = (bf16[4,256,128]{2,1,0:T(8,128)(2,1)S(1)}, bf16[4,256,128]{2,1,0:T(8,128)(2,1)S(1)}, u32[]{:S(2)}, u32[]{:S(2)}) collective-permute-start(bf16[4,256,128]{2,1,0:T(8,128)(2,1)S(1)} %get-tuple-element.81.refs_4_), channel_id=1, source_target_pairs={{0,16},{16,0},{1,17},{17,1},{2,18},{18,2},{3,19},{19,3},{4,20},{20... | collective-permute-start | bytes 786440 | tf_op jit(solution)/shard_map/ppermute | solution.py:597
  70.8 1.6 %collective-permute-done.9 = bf16[64,512]{1,0:T(8,128)(2,1)S(1)} collective-permute-done((bf16[64,512]{1,0:T(8,128)(2,1)S(1)}, bf16[64,512]{1,0:T(8,128)(2,1)S(1)}, u32[]{:S(2)}, u32[]{:S(2)}) %collective-permute-start.9) | collective-permute-done | bytes 65568 | tf_op jit(solution)/shard_map/ppermute | solution.py:597
  72.9 1.6 %collective-permute-start.14 = (bf16[2,64,512]{2,1,0:T(8,128)(2,1)S(1)}, bf16[2,64,512]{2,1,0:T(8,128)(2,1)S(1)}, u32[]{:S(2)}, u32[]{:S(2)}) collective-permute-start(bf16[2,64,512]{2,1,0:T(8,128)(2,1)S(1)} %get-tuple-element.86), channel_id=1, source_target_pairs={{0,2},{2,0},{4,6},{6,4},{8,10},{10,8},{12,14},{14,12},{1,3},{3,1},... | collective-permute-start | bytes 393224 | tf_op jit(solution)/shard_map/ppermute | solution.py:597
  74.5 1.5 %collective-permute-start.16 = (bf16[2,64,512]{2,1,0:T(8,128)(2,1)S(1)}, bf16[2,64,512]{2,1,0:T(8,128)(2,1)S(1)}, u32[]{:S(2)}, u32[]{:S(2)}) collective-permute-start(bf16[2,64,512]{2,1,0:T(8,128)(2,1)S(1)} %get-tuple-element.86), channel_id=1, source_target_pairs={{0,6},{2,4},{4,2},{6,0},{8,14},{10,12},{12,10},{14,8},{1,7},{3,5},... | collective-permute-start | bytes 393224 | tf_op jit(solution)/shard_map/ppermute | solution.py:597
  76.0 2.0 %collective-permute-done.15 = bf16[2,64,512]{2,1,0:T(8,128)(2,1)S(1)} collective-permute-done((bf16[2,64,512]{2,1,0:T(8,128)(2,1)S(1)}, bf16[2,64,512]{2,1,0:T(8,128)(2,1)S(1)}, u32[]{:S(2)}, u32[]{:S(2)}) %collective-permute-start.15) | collective-permute-done | bytes 131104 | tf_op jit(solution)/shard_map/ppermute | solution.py:597
  80.3 1.7 %collective-permute-done.12.refs_1_ = bf16[4,256,128]{2,1,0:T(8,128)(2,1)S(1)} collective-permute-done((bf16[4,256,128]{2,1,0:T(8,128)(2,1)S(1)}, bf16[4,256,128]{2,1,0:T(8,128)(2,1)S(1)}, u32[]{:S(2)}, u32[]{:S(2)}) %collective-permute-start.12) | collective-permute-done | bytes 262176 | tf_op jit(solution)/shard_map/ppermute | solution.py:597
  82.8 1.7 %collective-permute-done.18.refs_3_ = bf16[4,256,128]{2,1,0:T(8,128)(2,1)S(1)} collective-permute-done((bf16[4,256,128]{2,1,0:T(8,128)(2,1)S(1)}, bf16[4,256,128]{2,1,0:T(8,128)(2,1)S(1)}, u32[]{:S(2)}, u32[]{:S(2)}) %collective-permute-start.18) | collective-permute-done | bytes 262176 | tf_op jit(solution)/shard_map/ppermute | solution.py:597
  84.8 5.5 %shard_map.70 = (f32[64,512]{1,0:T(8,128)S(1)}, f32[64,512]{1,0:T(8,128)S(1)}, bf16[2,64,512]{2,1,0:T(8,128)(2,1)S(1)}, bf16[2,64,512]{2,1,0:T(8,128)(2,1)S(1)}, bf16[2,64,512]{2,1,0:T(8,128)(2,1)S(1)}) custom-call(s32[3]{0:T(128)S(1)} %copy-done.1, bf16[512,1024]{1,0:T(8,128)(2,1)S(1)} %get-tuple-element.59.tokens, ...), custom_call_target="tpu_custom_call" | custom-call | tf_op jit(solution)/shard_map/pallas_call | solution.py:543
  90.3 1.7 %collective-permute-start.20 = (bf16[2,64,512]{2,1,0:T(8,128)(2,1)S(1)}, bf16[2,64,512]{2,1,0:T(8,128)(2,1)S(1)}, u32[]{:S(2)}, u32[]{:S(2)}) collective-permute-start(bf16[2,64,512]{2,1,0:T(8,128)(2,1)S(1)} %get-tuple-element.74), channel_id=1, source_target_pairs={{0,2},{2,0},{4,6},{6,4},{8,10},{10,8},{12,14},{14,12},{1,3},{3,1},... | collective-permute-start | bytes 393224 | tf_op jit(solution)/shard_map/ppermute | solution.py:597
  92.0 1.5 %collective-permute-start.21 = (bf16[2,64,512]{2,1,0:T(8,128)(2,1)S(1)}, bf16[2,64,512]{2,1,0:T(8,128)(2,1)S(1)}, u32[]{:S(2)}, u32[]{:S(2)}) collective-permute-start(bf16[2,64,512]{2,1,0:T(8,128)(2,1)S(1)} %get-tuple-element.75), channel_id=1, source_target_pairs={{0,4},{2,6},{4,0},{6,2},{8,12},{10,14},{12,8},{14,10},{1,5},{3,7},... | collective-permute-start | bytes 393224 | tf_op jit(solution)/shard_map/ppermute | solution.py:597
  93.9 2.1 %collective-permute-done.20.refs_0_ = bf16[2,64,512]{2,1,0:T(8,128)(2,1)S(1)} collective-permute-done((bf16[2,64,512]{2,1,0:T(8,128)(2,1)S(1)}, bf16[2,64,512]{2,1,0:T(8,128)(2,1)S(1)}, u32[]{:S(2)}, u32[]{:S(2)}) %collective-permute-start.20) | collective-permute-done | bytes 131104 | tf_op jit(solution)/shard_map/ppermute | solution.py:597
  95.9 2.4 %collective-permute-done.21.refs_1_ = bf16[2,64,512]{2,1,0:T(8,128)(2,1)S(1)} collective-permute-done((bf16[2,64,512]{2,1,0:T(8,128)(2,1)S(1)}, bf16[2,64,512]{2,1,0:T(8,128)(2,1)S(1)}, u32[]{:S(2)}, u32[]{:S(2)}) %collective-permute-start.21) | collective-permute-done | bytes 131104 | tf_op jit(solution)/shard_map/ppermute | solution.py:597
  98.4 1.6 %collective-permute-done.22.refs_2_ = bf16[2,64,512]{2,1,0:T(8,128)(2,1)S(1)} collective-permute-done((bf16[2,64,512]{2,1,0:T(8,128)(2,1)S(1)}, bf16[2,64,512]{2,1,0:T(8,128)(2,1)S(1)}, u32[]{:S(2)}, u32[]{:S(2)}) %collective-permute-start.22) | collective-permute-done | bytes 131104 | tf_op jit(solution)/shard_map/ppermute | solution.py:597
  100.0 2.1 %collective-permute-start.23 = (bf16[64,512]{1,0:T(8,128)(2,1)S(1)}, bf16[64,512]{1,0:T(8,128)(2,1)S(1)}, u32[]{:S(2)}, u32[]{:S(2)}) collective-permute-start(bf16[64,512]{1,0:T(8,128)(2,1)S(1)} %get-tuple-element.78), channel_id=1, source_target_pairs={{0,8},{2,10},{4,12},{6,14},{8,0},{10,2},{12,4},{14,6},{1,9},{3,11}... | collective-permute-start | bytes 196616 | tf_op jit(solution)/shard_map/ppermute | solution.py:597
  102.0 3.2 %collective-permute-done.23.across_ref = bf16[64,512]{1,0:T(8,128)(2,1)S(1)} collective-permute-done((bf16[64,512]{1,0:T(8,128)(2,1)S(1)}, bf16[64,512]{1,0:T(8,128)(2,1)S(1)}, u32[]{:S(2)}, u32[]{:S(2)}) %collective-permute-start.23) | collective-permute-done | bytes 65568 | tf_op jit(solution)/shard_map/ppermute | solution.py:597
  (53 shorter events, 10.3 us)
Async XLA Ops:
  0.0 7.5 %copy-start.3 = (bf16[1,40,4,1024]{3,2,1,0:T(4,128)(2,1)S(1)}, bf16[1,40,4,1024]{3,2,1,0:T(4,128)(2,1)}, u32[]{:S(2)}) copy-start(bf16[1,40,4,1024]{3,2,1,0:T(4,128)(2,1)} %param.6) | copy-start | bytes 983044
  0.7 6.9 %copy-start = (s32[3]{0:T(128)S(1)}, s32[3]{0:T(128)}, u32[]{:S(2)}) copy-start(s32[3]{0:T(128)} %pad_add_fusion.rank_ref.scalars) | copy-start | bytes 40
  0.7 6.9 %copy-start.2 = (s32[1,64]{1,0:T(1,128)S(1)}, s32[1,64]{1,0:T(1,128)}, u32[]{:S(2)}) copy-start(s32[1,64]{1,0:T(1,128)} %keep_ref.3) | copy-start | bytes 772
  3.4 34.6 %collective-permute-start.1 = (bf16[1664,128]{1,0:T(8,128)(2,1)}, bf16[1664,128]{1,0:T(8,128)(2,1)S(1)}, u32[]{:S(2)}, u32[]{:S(2)}) collective-permute-start(bf16[1664,128]{1,0:T(8,128)(2,1)} %shard_map.64), channel_id=1, source_target_pairs={{0,8},{2,10},{4,12},{6,14},{8,0},{10,2},{12,4},{14,6},{1,9},{3,11}... | collective-permute-start | bytes 1277960 | tf_op jit(solution)/shard_map/ppermute | solution.py:597
  7.6 23.0 %copy-start.1 = (s32[3]{0:T(128)S(1)}, s32[3]{0:T(128)}, u32[]{:S(2)}) copy-start(s32[3]{0:T(128)} %pad_add_fusion.rank_ref.scalars) | copy-start | bytes 40
  9.6 21.0 %all-to-all-start = ((bf16[8,80,128]{2,1,0:T(8,128)(2,1)}), bf16[8,80,128]{2,1,0:T(8,128)(2,1)S(1)}, u32[]{:S(2)}, u32[]{:S(2)}) async-start(bf16[8,80,128]{2,1,0:T(8,128)(2,1)} %bitcast.4), calls=%async_computation | async-start | bytes 327680 | tf_op jit(solution)/shard_map/all_to_all | solution.py:601
  16.3 18.2 %collective-permute-start.2 = (bf16[704,128]{1,0:T(8,128)(2,1)}, bf16[704,128]{1,0:T(8,128)(2,1)S(1)}, u32[]{:S(2)}, u32[]{:S(2)}) collective-permute-start(bf16[704,128]{1,0:T(8,128)(2,1)} %get-tuple-element.48), channel_id=1, source_target_pairs={{0,2},{2,0},{4,6},{6,4},{8,10},{10,8},{12,14},{14,12},{1,3},{3,1},... | collective-permute-start | bytes 540680 | tf_op jit(solution)/shard_map/ppermute | solution.py:597
  18.4 16.1 %collective-permute-start.3 = (bf16[704,128]{1,0:T(8,128)(2,1)}, bf16[704,128]{1,0:T(8,128)(2,1)S(1)}, u32[]{:S(2)}, u32[]{:S(2)}) collective-permute-start(bf16[704,128]{1,0:T(8,128)(2,1)} %get-tuple-element.49), channel_id=1, source_target_pairs={{0,4},{2,6},{4,0},{6,2},{8,12},{10,14},{12,8},{14,10},{1,5},{3,7},... | collective-permute-start | bytes 540680 | tf_op jit(solution)/shard_map/ppermute | solution.py:597
  19.8 17.8 %collective-permute-start.4 = (bf16[704,128]{1,0:T(8,128)(2,1)}, bf16[704,128]{1,0:T(8,128)(2,1)S(1)}, u32[]{:S(2)}, u32[]{:S(2)}) collective-permute-start(bf16[704,128]{1,0:T(8,128)(2,1)} %get-tuple-element.50), channel_id=1, source_target_pairs={{0,6},{2,4},{4,2},{6,0},{8,14},{10,12},{12,10},{14,8},{1,7},{3,5},... | collective-permute-start | bytes 540680 | tf_op jit(solution)/shard_map/ppermute | solution.py:597
  31.5 6.5 %collective-permute-start = (bf16[256,128]{1,0:T(8,128)(2,1)S(1)}, bf16[256,128]{1,0:T(8,128)(2,1)S(1)}, u32[]{:S(2)}, u32[]{:S(2)}) collective-permute-start(bf16[256,128]{1,0:T(8,128)(2,1)S(1)} %shard_map.66.owned_ref), channel_id=1, source_target_pairs={{0,8},{2,10},{4,12},{6,14},{8,0},{10,2},{12,4},{14,6},{1,9},{3,11}... | collective-permute-start | bytes 196616 | tf_op jit(solution)/shard_map/ppermute | solution.py:597
  39.2 3.7 %copy-start.4 = (bf16[704,128]{1,0:T(8,128)(2,1)S(1)}, bf16[704,128]{1,0:T(8,128)(2,1)}, u32[]{:S(2)}) copy-start(bf16[704,128]{1,0:T(8,128)(2,1)} %get-tuple-element.53) | copy-start | bytes 540676
  39.2 18.5 %all-to-all-start.1 = ((bf16[4,1120,128]{2,1,0:T(8,128)(2,1)}), bf16[4,1120,128]{2,1,0:T(8,128)(2,1)S(1)}, u32[]{:S(2)}, u32[]{:S(2)}) async-start(bf16[4,1120,128]{2,1,0:T(8,128)(2,1)} %shard_map.68), calls=%async_computation.1 | async-start | bytes 2293760 | tf_op jit(solution)/shard_map/all_to_all | solution.py:607
  43.0 2.0 %collective-permute-start.6 = (bf16[4,512,128]{2,1,0:T(8,128)(2,1)S(1)}, bf16[4,512,128]{2,1,0:T(8,128)(2,1)S(1)}, u32[]{:S(2)}, u32[]{:S(2)}) collective-permute-start(bf16[4,512,128]{2,1,0:T(8,128)(2,1)S(1)} %pad_maximum_fusion.refs_8_), channel_id=1, source_target_pairs={{0,1},{1,0},{2,3},{3,2},{4,5},{5,4},{6,7},{7,6},{8,9},{9,8},{10,11... | collective-permute-start | bytes 1572872 | tf_op jit(solution)/shard_map/ppermute | solution.py:597
  43.1 14.3 %collective-permute-start.5 = (bf16[4,512,128]{2,1,0:T(8,128)(2,1)S(1)}, bf16[4,512,128]{2,1,0:T(8,128)(2,1)S(1)}, u32[]{:S(2)}, u32[]{:S(2)}) collective-permute-start(bf16[4,512,128]{2,1,0:T(8,128)(2,1)S(1)} %pad_maximum_fusion.refs_8_), channel_id=1, source_target_pairs={{0,16},{16,0},{1,17},{17,1},{2,18},{18,2},{3,19},{19,3},{4,20},{20... | collective-permute-start | bytes 1572872 | tf_op jit(solution)/shard_map/ppermute | solution.py:597
  57.7 5.3 %collective-permute-start.7 = (bf16[4,512,128]{2,1,0:T(8,128)(2,1)S(1)}, bf16[4,512,128]{2,1,0:T(8,128)(2,1)S(1)}, u32[]{:S(2)}, u32[]{:S(2)}) collective-permute-start(bf16[4,512,128]{2,1,0:T(8,128)(2,1)S(1)} %get-tuple-element.80), channel_id=1, source_target_pairs={{0,1},{1,0},{2,3},{3,2},{4,5},{5,4},{6,7},{7,6},{8,9},{9,8},{10,11... | collective-permute-start | bytes 1572872 | tf_op jit(solution)/shard_map/ppermute | solution.py:597
  57.8 5.2 %collective-permute-start.8 = (bf16[4,96,128]{2,1,0:T(8,128)(2,1)S(1)}, bf16[4,96,128]{2,1,0:T(8,128)(2,1)S(1)}, u32[]{:S(2)}, u32[]{:S(2)}) collective-permute-start(bf16[4,96,128]{2,1,0:T(8,128)(2,1)S(1)} %slice.54), channel_id=1, source_target_pairs={{0,16},{16,0},{1,17},{17,1},{2,18},{18,2},{3,19},{19,3},{4,20},{20... | collective-permute-start | bytes 294920 | tf_op jit(solution)/shard_map/ppermute | solution.py:597
  59.4 11.5 %collective-permute-start.10 = (bf16[4,512,128]{2,1,0:T(8,128)(2,1)S(1)}, bf16[4,512,128]{2,1,0:T(8,128)(2,1)S(1)}, u32[]{:S(2)}, u32[]{:S(2)}) collective-permute-start(bf16[4,512,128]{2,1,0:T(8,128)(2,1)S(1)} %collective-permute-done.5.refs_9_), channel_id=1, source_target_pairs={{0,1},{1,0},{2,3},{3,2},{4,5},{5,4},{6,7},{7,6},{8,9},{9,8},{10,11... | collective-permute-start | bytes 1572872 | tf_op jit(solution)/shard_map/ppermute | solution.py:597
  59.6 11.2 %collective-permute-start.11 = (bf16[4,512,128]{2,1,0:T(8,128)(2,1)S(1)}, bf16[4,512,128]{2,1,0:T(8,128)(2,1)S(1)}, u32[]{:S(2)}, u32[]{:S(2)}) collective-permute-start(bf16[4,512,128]{2,1,0:T(8,128)(2,1)S(1)} %get-tuple-element.79), channel_id=1, source_target_pairs={{0,1},{1,0},{2,3},{3,2},{4,5},{5,4},{6,7},{7,6},{8,9},{9,8},{10,11... | collective-permute-start | bytes 1572872 | tf_op jit(solution)/shard_map/ppermute | solution.py:597
  65.8 6.6 %collective-permute-start.9 = (bf16[64,512]{1,0:T(8,128)(2,1)S(1)}, bf16[64,512]{1,0:T(8,128)(2,1)S(1)}, u32[]{:S(2)}, u32[]{:S(2)}) collective-permute-start(bf16[64,512]{1,0:T(8,128)(2,1)S(1)} %get-tuple-element.60), channel_id=1, source_target_pairs={{0,8},{2,10},{4,12},{6,14},{8,0},{10,2},{12,4},{14,6},{1,9},{3,11}... | collective-permute-start | bytes 196616 | tf_op jit(solution)/shard_map/ppermute | solution.py:597
  68.7 11.6 %collective-permute-start.13 = (bf16[4,256,128]{2,1,0:T(8,128)(2,1)S(1)}, bf16[4,256,128]{2,1,0:T(8,128)(2,1)S(1)}, u32[]{:S(2)}, u32[]{:S(2)}) collective-permute-start(bf16[4,256,128]{2,1,0:T(8,128)(2,1)S(1)} %get-tuple-element.81.refs_4_), channel_id=1, source_target_pairs={{0,16},{16,0},{1,17},{17,1},{2,18},{18,2},{3,19},{19,3},{4,20},{20... | collective-permute-start | bytes 786440 | tf_op jit(solution)/shard_map/ppermute | solution.py:597
  70.3 11.8 %collective-permute-start.12 = (bf16[4,256,128]{2,1,0:T(8,128)(2,1)S(1)}, bf16[4,256,128]{2,1,0:T(8,128)(2,1)S(1)}, u32[]{:S(2)}, u32[]{:S(2)}) collective-permute-start(bf16[4,256,128]{2,1,0:T(8,128)(2,1)S(1)} %get-tuple-element.82.refs_0_), channel_id=1, source_target_pairs={{0,16},{16,0},{1,17},{17,1},{2,18},{18,2},{3,19},{19,3},{4,20},{20... | collective-permute-start | bytes 786440 | tf_op jit(solution)/shard_map/ppermute | solution.py:597
  72.4 5.5 %collective-permute-start.15 = (bf16[2,64,512]{2,1,0:T(8,128)(2,1)S(1)}, bf16[2,64,512]{2,1,0:T(8,128)(2,1)S(1)}, u32[]{:S(2)}, u32[]{:S(2)}) collective-permute-start(bf16[2,64,512]{2,1,0:T(8,128)(2,1)S(1)} %get-tuple-element.86), channel_id=1, source_target_pairs={{0,4},{2,6},{4,0},{6,2},{8,12},{10,14},{12,8},{14,10},{1,5},{3,7},... | collective-permute-start | bytes 393224 | tf_op jit(solution)/shard_map/ppermute | solution.py:597
  72.9 6.1 %collective-permute-start.14 = (bf16[2,64,512]{2,1,0:T(8,128)(2,1)S(1)}, bf16[2,64,512]{2,1,0:T(8,128)(2,1)S(1)}, u32[]{:S(2)}, u32[]{:S(2)}) collective-permute-start(bf16[2,64,512]{2,1,0:T(8,128)(2,1)S(1)} %get-tuple-element.86), channel_id=1, source_target_pairs={{0,2},{2,0},{4,6},{6,4},{8,10},{10,8},{12,14},{14,12},{1,3},{3,1},... | collective-permute-start | bytes 393224 | tf_op jit(solution)/shard_map/ppermute | solution.py:597
  74.5 5.9 %collective-permute-start.16 = (bf16[2,64,512]{2,1,0:T(8,128)(2,1)S(1)}, bf16[2,64,512]{2,1,0:T(8,128)(2,1)S(1)}, u32[]{:S(2)}, u32[]{:S(2)}) collective-permute-start(bf16[2,64,512]{2,1,0:T(8,128)(2,1)S(1)} %get-tuple-element.86), channel_id=1, source_target_pairs={{0,6},{2,4},{4,2},{6,0},{8,14},{10,12},{12,10},{14,8},{1,7},{3,5},... | collective-permute-start | bytes 393224 | tf_op jit(solution)/shard_map/ppermute | solution.py:597
  82.1 2.7 %collective-permute-start.17 = (bf16[4,2,64,512]{3,2,1,0:T(8,128)(2,1)S(1)}, bf16[4,2,64,512]{3,2,1,0:T(8,128)(2,1)S(1)}, u32[]{:S(2)}, u32[]{:S(2)}) collective-permute-start(bf16[4,2,64,512]{3,2,1,0:T(8,128)(2,1)S(1)} %pad_maximum_fusion.1.a), channel_id=1, source_target_pairs={{0,1},{1,0},{2,3},{3,2},{4,5},{5,4},{6,7},{7,6},{8,9},{9,8},{10,11... | collective-permute-start | bytes 1572872 | tf_op jit(solution)/shard_map/ppermute | solution.py:597
  82.2 2.3 %collective-permute-start.18 = (bf16[4,256,128]{2,1,0:T(8,128)(2,1)S(1)}, bf16[4,256,128]{2,1,0:T(8,128)(2,1)S(1)}, u32[]{:S(2)}, u32[]{:S(2)}) collective-permute-start(bf16[4,256,128]{2,1,0:T(8,128)(2,1)S(1)} %collective-permute-done.12.refs_1_), channel_id=1, source_target_pairs={{0,1},{1,0},{2,3},{3,2},{4,5},{5,4},{6,7},{7,6},{8,9},{9,8},{10,11... | collective-permute-start | bytes 786440 | tf_op jit(solution)/shard_map/ppermute | solution.py:597
  82.7 2.1 %collective-permute-start.19 = (bf16[4,256,128]{2,1,0:T(8,128)(2,1)S(1)}, bf16[4,256,128]{2,1,0:T(8,128)(2,1)S(1)}, u32[]{:S(2)}, u32[]{:S(2)}) collective-permute-start(bf16[4,256,128]{2,1,0:T(8,128)(2,1)S(1)} %collective-permute-done.13.refs_5_), channel_id=1, source_target_pairs={{0,1},{1,0},{2,3},{3,2},{4,5},{5,4},{6,7},{7,6},{8,9},{9,8},{10,11... | collective-permute-start | bytes 786440 | tf_op jit(solution)/shard_map/ppermute | solution.py:597
  90.3 5.6 %collective-permute-start.20 = (bf16[2,64,512]{2,1,0:T(8,128)(2,1)S(1)}, bf16[2,64,512]{2,1,0:T(8,128)(2,1)S(1)}, u32[]{:S(2)}, u32[]{:S(2)}) collective-permute-start(bf16[2,64,512]{2,1,0:T(8,128)(2,1)S(1)} %get-tuple-element.74), channel_id=1, source_target_pairs={{0,2},{2,0},{4,6},{6,4},{8,10},{10,8},{12,14},{14,12},{1,3},{3,1},... | collective-permute-start | bytes 393224 | tf_op jit(solution)/shard_map/ppermute | solution.py:597
  92.0 6.4 %collective-permute-start.21 = (bf16[2,64,512]{2,1,0:T(8,128)(2,1)S(1)}, bf16[2,64,512]{2,1,0:T(8,128)(2,1)S(1)}, u32[]{:S(2)}, u32[]{:S(2)}) collective-permute-start(bf16[2,64,512]{2,1,0:T(8,128)(2,1)S(1)} %get-tuple-element.75), channel_id=1, source_target_pairs={{0,4},{2,6},{4,0},{6,2},{8,12},{10,14},{12,8},{14,10},{1,5},{3,7},... | collective-permute-start | bytes 393224 | tf_op jit(solution)/shard_map/ppermute | solution.py:597
  93.4 6.5 %collective-permute-start.22 = (bf16[2,64,512]{2,1,0:T(8,128)(2,1)S(1)}, bf16[2,64,512]{2,1,0:T(8,128)(2,1)S(1)}, u32[]{:S(2)}, u32[]{:S(2)}) collective-permute-start(bf16[2,64,512]{2,1,0:T(8,128)(2,1)S(1)} %get-tuple-element.76), channel_id=1, source_target_pairs={{0,6},{2,4},{4,2},{6,0},{8,14},{10,12},{12,10},{14,8},{1,7},{3,5},... | collective-permute-start | bytes 393224 | tf_op jit(solution)/shard_map/ppermute | solution.py:597
  100.0 5.2 %collective-permute-start.23 = (bf16[64,512]{1,0:T(8,128)(2,1)S(1)}, bf16[64,512]{1,0:T(8,128)(2,1)S(1)}, u32[]{:S(2)}, u32[]{:S(2)}) collective-permute-start(bf16[64,512]{1,0:T(8,128)(2,1)S(1)} %get-tuple-element.78), channel_id=1, source_target_pairs={{0,8},{2,10},{4,12},{6,14},{8,0},{10,2},{12,4},{14,6},{1,9},{3,11}... | collective-permute-start | bytes 196616 | tf_op jit(solution)/shard_map/ppermute | solution.py:597
